TPU v7x, 32 devices: a whole 2x2x4 slice. The times are simulated.
32 devices in a mesh: parts: 2 (over y), chan: 4 (over z), lad: 2 (over x), sub: 2 (over core).
Axes of the slice: x: 2, y: 2, z: 4, core: 2. Of those that a mesh axis runs over, the one named last changes fastest.
Arguments:
- amplitudes: bfloat16 [8, 3072, 512], P(('parts', 'chan'), ('lad', 'sub')), parts along dimension 0, may hold values from -6 to 6
- driving: bfloat16 [8, 3072, 512], P(('parts', 'chan'), ('lad', 'sub')), parts along dimension 0, may hold values from -6 to 6
- route: int32 [4, 3072, 1], P('chan', ('lad', 'sub')), may hold values from 0 to 3; in each aligned block of 768 rows (0 to 767, 768 to 1535, ..., all dimensions but the last counted through in order) at most 384 rows name the same one
- ladder_weight: bfloat16 [4, 3072, 3072], P('chan', None, ('lad', 'sub')), may hold values from -0.15625 to 0.15625
- ph_weight: bfloat16 [4, 4, 1536, 1536], P('chan', ('lad', 'sub')), may hold values from -0.15625 to 0.15625
- recouple: bfloat16 [4, 4, 12, 128, 128], P('chan', ('lad', 'sub')), may hold values from -1 to 2, as said below
- gap_part: float32 [8, 3072], P(('parts', 'chan'), ('lad', 'sub')), parts along dimension 0, may hold values from 1 to 4
- gap_hole: float32 [1024], P('parts'), parts along dimension 0, may hold values from 1 to 4
Outputs:
- updated: bfloat16 [8, 3072, 512], P(('parts', 'chan'), ('lad', 'sub')), parts along dimension 0
There are 2 independent parts, one for each index of `parts`. A program takes and returns all parts, laid end to end along the dimension named above; an argument that names none is the same for every part. Nothing has to cross between parts.
Inputs may be any that keep to these rules, and one draw needn't show every extreme that they name: `route`: in each aligned block of 768 rows (the rows of one device), at most 384 rows name one cycle block, and some cycle block is named by exactly 384 rows in some blocks. `recouple`: each mixing matrix is the identity plus independent coefficients.
All inputs are finite; a program needn't handle non-finite values.
Results may differ from a plain program's by a relative error of at most 0.007.
Values may be sent and summed in bfloat16 or wider, within the bound.
No kernel may reach another device: no remote copies, remote signals or barrier semaphores. Data moves between devices by JAX's collectives and lax.ppermute only.
A program may use at most 64 MiB of HBM per device.

v0:
```python
import jax
import jax.numpy as jnp
from jax import lax
from jax.sharding import PartitionSpec as P


def body(amplitudes, driving, route, ladder_weight, ph_weight, recouple, gap_part, gap_hole):
    local_amps = amplitudes[0]
    row_count = local_amps.shape[0]
    hole_count = local_amps.shape[1]
    chan_count = lax.axis_size("chan")
    capacity = ph_weight.shape[2]
    send_slots = capacity // chan_count
    owners = route[0, :, 0]
    one_hot = (owners[:, None] == jnp.arange(chan_count, dtype=jnp.int32)[None, :]).astype(
        jnp.int32
    )
    earlier = jnp.cumsum(one_hot, axis=0) - one_hot
    slot_index = jnp.sum(earlier * one_hot, axis=1)
    target = owners * send_slots + slot_index
    outgoing = jnp.zeros((capacity, hole_count), jnp.bfloat16).at[target].set(local_amps)
    outgoing = outgoing.reshape(chan_count, send_slots, hole_count)
    mixing = recouple[0, 0]
    cycle_weight = ph_weight[0, 0]
    groups = mixing.shape[0]
    group_size = mixing.shape[1]
    block = lax.all_to_all(outgoing, "chan", split_axis=0, concat_axis=0, tiled=True)
    col_count = block.shape[2]
    grouped = block.reshape(groups, group_size, col_count)
    recoupled = jnp.einsum("gab,gbk->gak", mixing, grouped, preferred_element_type=jnp.float32)
    recoupled = recoupled.astype(jnp.bfloat16).reshape(capacity, col_count)
    cycle_part = jnp.dot(cycle_weight, recoupled, preferred_element_type=jnp.float32).astype(
        jnp.bfloat16
    )
    cycle_back = jnp.einsum(
        "gba,gbk->gak",
        mixing,
        cycle_part.reshape(groups, group_size, col_count),
        preferred_element_type=jnp.float32,
    ).astype(jnp.bfloat16)
    arrived = lax.all_to_all(
        cycle_back.reshape(chan_count, send_slots, col_count),
        "chan",
        split_axis=0,
        concat_axis=0,
        tiled=True,
    )
    returned = arrived.reshape(capacity, hole_count)[target]
    local_weight = ladder_weight[0]
    row_weight = lax.all_to_all(
        local_weight, ("lad", "sub"), split_axis=0, concat_axis=1, tiled=True
    )
    piece = lax.all_gather(local_amps, ("lad", "sub"), axis=0, tiled=True)
    piece_rows = piece.shape[0]
    shards = piece_rows // row_count
    terms = jnp.einsum(
        "okr,krh->koh",
        row_weight.reshape(row_count, shards, row_count),
        piece.reshape(shards, row_count, hole_count),
        preferred_element_type=jnp.float32,
    ).astype(jnp.bfloat16)
    terms = lax.optimization_barrier(terms)
    ladder = jnp.sum(terms.astype(jnp.float32), axis=0)
    gap_sum = gap_part[0][:, None] + gap_hole[None, :]
    total = driving[0].astype(jnp.float32) + ladder + returned.astype(jnp.float32)
    return (total / gap_sum).astype(jnp.bfloat16)[None]


def solution(mesh):
    placed = (
        P(("parts", "chan"), ("lad", "sub"), None),
        P(("parts", "chan"), ("lad", "sub"), None),
        P("chan", ("lad", "sub"), None),
        P("chan", None, ("lad", "sub")),
        P("chan", ("lad", "sub"), None, None),
        P("chan", ("lad", "sub"), None, None, None),
        P(("parts", "chan"), ("lad", "sub")),
        P("parts"),
    )
    return jax.shard_map(
        body,
        mesh=mesh,
        in_specs=placed,
        out_specs=P(("parts", "chan"), ("lad", "sub"), None),
        check_vma=False,
    )
```

profile of v0, /device:TPU:0, one launch (start us, length us, event | category | flops | bytes accessed | tf_op | source)
XLA Modules:
  0.0 188.5 jit_solution(3378371008392806517)
XLA Ops:
  6.5 0.0 copy-start
  6.5 0.7 reduce
  7.3 1.1 reduce-window.6
  8.4 0.2 slice_reduce_fusion
  8.7 0.2 reduce-window.9
  8.8 0.1 add_bitcast_fusion
  9.0 0.7 fusion.24
  9.7 6.5 %scatter_custom_fusion = bf16[1536,512]{1,0:T(8,128)(2,1)S(1)} fusion(s32[768]{0:T(1024)S(1)} %fusion.24, bf16[1,768,512]{2,1,0:T(8,128)(2,1)} %param.8, bf16[]{:T(256)} %constant.6.clone.1), kind=kCustom, calls=%fused_computation.16 | custom fusion | bytes 2359298 | tf_op jit(solution)/shard_map/scatter | solution.py:21
  16.2 43.1 %all_to_all.26 = bf16[4,384,512]{2,1,0:T(8,128)(2,1)S(1)} all-to-all(bf16[4,384,512]{2,1,0:T(8,128)(2,1)S(1)} %bitcast.71), channel_id=1, replica_groups=mesh['parts'=2,'chan'=4,'lad'=2,'sub'=2] {'chan'}, dimensions={0} | all-to-all | bytes 3145728 | tf_op jit(solution)/shard_map/all_to_all | solution.py:27
  59.3 4.9 %all-to-all-start = ((bf16[4,768,768]{2,1,0:T(8,128)(2,1)}), bf16[4,768,768]{2,1,0:T(8,128)(2,1)}, u32[]{:S(2)}, u32[]{:S(2)}) async-start(bf16[4,768,768]{2,1,0:T(8,128)(2,1)} %bitcast.73), calls=%async_computation | async-start | bytes 9437184 | tf_op jit(solution)/shard_map/all_to_all | solution.py:50
  64.2 0.0 all-gather.3.cloned.1.call-start
  64.2 0.7 all-gather.3.cloned.1.call-update
  64.9 0.0 copy-done
  64.9 0.6 convolution_convert_fusion
  65.5 5.0 %fusion.7 = bf16[1536,512]{0,1:T(8,128)(2,1)S(1)} fusion(bf16[1536,512]{1,0:T(8,128)(2,1)S(1)} %bitcast.74, bf16[1,1,1536,1536]{3,2,1,0:T(8,128)(2,1)} %param.12), kind=kOutput, calls=%fused_computation.8 | convolution fusion | flops 2416705536 | bytes 7864320 | tf_op jit(solution)/shard_map/dot_general | solution.py:32
  70.5 0.7 copy.11
  71.3 1.9 convolution_convert_fusion.1
  73.1 61.8 %all-to-all-done = bf16[4,768,768]{2,1,0:T(8,128)(2,1)} async-done(((bf16[4,768,768]{2,1,0:T(8,128)(2,1)}), bf16[4,768,768]{2,1,0:T(8,128)(2,1)}, u32[]{:S(2)}, u32[]{:S(2)}) %all-to-all-start) | async-done | bytes 4718624 | tf_op jit(solution)/shard_map/all_to_all | solution.py:50
  134.9 0.0 copy-start.1
  134.9 3.7 %all-to-all-start.2 = ((bf16[4,384,512]{2,1,0:T(8,128)(2,1)}), bf16[4,384,512]{2,1,0:T(8,128)(2,1)S(1)}, u32[]{:S(2)}, u32[]{:S(2)}) async-start(bf16[4,384,512]{2,1,0:T(8,128)(2,1)} %bitcast.16), calls=%async_computation.2 | async-start | bytes 3145728 | tf_op jit(solution)/shard_map/all_to_all | solution.py:41
  138.6 0.0 copy-done.1
  138.6 0.0 all-gather.3.cloned.1.call-done
  138.7 5.9 %fusion.10 = bf16[4,768,512]{2,1,0:T(8,128)(2,1)S(1)} fusion(bf16[4,768,512]{2,1,0:T(8,128)(2,1)} %bitcast.77, bf16[4,768,768]{2,1,0:T(8,128)(2,1)} %all-to-all-done), kind=kOutput, calls=%fused_computation.9 | convolution fusion | flops 2417491968 | bytes 11010048 | tf_op jit(solution)/shard_map/okr,krh->koh/dot_general | solution.py:56
  144.6 0.5 convert_reduce_fusion
  145.1 30.5 %all-to-all-done.2 = bf16[4,384,512]{2,1,0:T(8,128)(2,1)S(1)} async-done(((bf16[4,384,512]{2,1,0:T(8,128)(2,1)}), bf16[4,384,512]{2,1,0:T(8,128)(2,1)S(1)}, u32[]{:S(2)}, u32[]{:S(2)}) %all-to-all-start.2) | async-done | bytes 1572896 | tf_op jit(solution)/shard_map/all_to_all | solution.py:41
  175.6 0.0 copy-start.2
  175.6 3.3 %gather_fusion = bf16[768,512]{1,0:T(8,128)(2,1)} fusion(bf16[1536,512]{1,0:T(8,128)(2,1)S(1)} %bitcast.69, s32[1024]{0:T(1024)S(1)} %pad_clamp_fusion), kind=kCustom, calls=%fused_computation | custom fusion | bytes 1575936 | tf_op jit(solution)/shard_map/gather | solution.py:48
  178.9 0.0 copy-done.2
  178.9 2.7 %fusion.14 = bf16[1,768,512]{2,1,0:T(8,128)(2,1)} fusion(f32[768,512]{1,0:T(8,128)S(1)} %convert_reduce_fusion, bf16[1,768,512]{2,1,0:T(8,128)(2,1)} %param.9, bf16[768,512]{1,0:T(8,128)(2,1)} %gather_fusion, f32[512]{0:T(512)S(1)} %copy-done.2, f32[768]{0:T(1024)S(1)} %reduce.4), kind=kLoop, calls=%fused_computation.14 | loop fusion | flops 2752512 | bytes 3937280 | tf_op jit(solution)/shard_map/convert_element_type | solution.py:66
  (4 shorter events, 0.0 us)
Async XLA Ops:
  6.5 58.4 %copy-start = (bf16[1,1,12,128,128]{4,3,2,1,0:T(8,128)(2,1)S(1)}, bf16[1,1,12,128,128]{4,3,2,1,0:T(8,128)(2,1)}, u32[]{:S(2)}) copy-start(bf16[1,1,12,128,128]{4,3,2,1,0:T(8,128)(2,1)} %param.13) | copy-start | bytes 1179652
  59.3 75.6 %all-to-all-start = ((bf16[4,768,768]{2,1,0:T(8,128)(2,1)}), bf16[4,768,768]{2,1,0:T(8,128)(2,1)}, u32[]{:S(2)}, u32[]{:S(2)}) async-start(bf16[4,768,768]{2,1,0:T(8,128)(2,1)} %bitcast.73), calls=%async_computation | async-start | bytes 9437184 | tf_op jit(solution)/shard_map/all_to_all | solution.py:50
  64.2 74.5 %all-gather.3.cloned.1.call-start = ((), (), s32[]{:S(2)}) async-start(), calls=%async_computation.3 | async-start | bytes 3932160 | tf_op jit(solution)/shard_map/all_gather | solution.py:53
  134.9 3.7 %copy-start.1 = (f32[1,768]{1,0:T(1,128)S(1)}, f32[1,768]{1,0:T(1,128)}, u32[]{:S(2)}) copy-start(f32[1,768]{1,0:T(1,128)} %param.14) | copy-start | bytes 9220
  134.9 40.7 %all-to-all-start.2 = ((bf16[4,384,512]{2,1,0:T(8,128)(2,1)}), bf16[4,384,512]{2,1,0:T(8,128)(2,1)S(1)}, u32[]{:S(2)}, u32[]{:S(2)}) async-start(bf16[4,384,512]{2,1,0:T(8,128)(2,1)} %bitcast.16), calls=%async_computation.2 | async-start | bytes 3145728 | tf_op jit(solution)/shard_map/all_to_all | solution.py:41
  175.6 3.3 %copy-start.2 = (f32[512]{0:T(512)S(1)}, f32[512]{0:T(512)}, u32[]{:S(2)}) copy-start(f32[512]{0:T(512)} %param.15) | copy-start | bytes 6148
Sparse Core Ops, SparseCore 0:
  66.6 45.0 all-gather.2
where the time goes:
time: 189 us; the launch traced here: 188 us
  waiting for transfers between devices  93 us (49%)
  blocking collectives  43.1 us (23%)
  between operations  13.5 us (7%)
  matrix products  13.4 us (7%)
  local copies, waits for them, and re-layouts  10.8 us (6%)
  starting transfers between devices  8.67 us (5%)
  other arithmetic  6.08 us (3%)
    all_to_all x1, waiting for transfers between devices, body(): lax.all_to_all(local_weight, ('lad', 'sub'), split_axis=0, concat_axis=1,...  61.8 us
    all_to_all x1, blocking collectives, body(): lax.all_to_all(outgoing, 'chan', split_axis=0, concat_axis=0, tiled=True)  43.1 us
    all_to_all x1, waiting for transfers between devices, body(): lax.all_to_all(cycle_back.reshape(chan_count, send_slots, col_count), 'ch...  30.5 us
    scatter x1, local copies, waits for them, and re-layouts, body(): jnp.zeros((capacity, hole_count), jnp.bfloat16).at[target].set(local_amps)  6.5 us
    dot_general x1, matrix products, body(): jnp.einsum('okr,krh->koh', row_weight.reshape(row_count, shards, row_coun...  5.92 us
    dot_general x1, matrix products, body(): jnp.dot(cycle_weight, recoupled, preferred_element_type=jnp.float32)  5.03 us
    all_to_all x1, starting transfers between devices, body(): lax.all_to_all(local_weight, ('lad', 'sub'), split_axis=0, concat_axis=1,...  4.93 us
  transfers between devices with their start and end apart: 3, of which 2 were waited for; matrix products, arithmetic and copies ran while one was open for 8% of the time, Pallas kernels for 0%

commit v1 on v0

v1 whole, which is shorter than its diff:
```python
import functools

import jax
import jax.numpy as jnp
from jax import lax
from jax.experimental import pallas as pl
from jax.experimental.pallas import tpu as pltpu
from jax.sharding import PartitionSpec as P

VMEM_LIMIT = 48 * 1024 * 1024
F32 = jnp.float32
BF16 = jnp.bfloat16


def params():
    return pltpu.CompilerParams(vmem_limit_bytes=VMEM_LIMIT)


def whole(memory=pltpu.VMEM):
    return pl.BlockSpec(memory_space=memory)


def selection(match):
    return jnp.where(match, 1.0, 0.0).astype(BF16)


def pack_kernel(chan_count, send, off_ref, route_ref, amps_ref, *out_refs):
    target_ref, block_refs = out_refs[0], out_refs[1:]
    owners = route_ref[...]
    rows = owners.shape[1]
    lanes = max(16, chan_count)
    hot = lax.broadcasted_iota(jnp.int32, (lanes, rows), 0) == owners
    before = selection(
        lax.broadcasted_iota(jnp.int32, (rows, rows), 0)
        < lax.broadcasted_iota(jnp.int32, (rows, rows), 1)
    )
    earlier = jnp.dot(selection(hot), before, preferred_element_type=F32)
    slot = jnp.sum(jnp.where(hot, earlier, 0.0), axis=0, keepdims=True)
    target = owners * send + slot.astype(jnp.int32)
    target_ref[...] = target
    place_rows(off_ref, target, amps_ref, block_refs)


def place_rows(off_ref, target, amps_ref, block_refs):
    for k, block_ref in enumerate(block_refs):
        slots = lax.broadcasted_iota(jnp.int32, (block_ref.shape[0], target.shape[1]), 0)
        pick = selection(slots == target - off_ref[k])
        block_ref[...] = jnp.dot(pick, amps_ref[...], preferred_element_type=F32).astype(BF16)


def more_kernel(off_ref, target_ref, amps_ref, *block_refs):
    place_rows(off_ref, target_ref[...], amps_ref, block_refs)


def pack(offsets, route_row, amps, chan_count, send, block_rows):
    rows, holes = amps.shape
    block = jax.ShapeDtypeStruct((block_rows, holes), BF16)
    count = offsets.shape[0]
    first = (count + 1) // 2
    outs = pl.pallas_call(
        functools.partial(pack_kernel, chan_count, send),
        out_shape=[jax.ShapeDtypeStruct((1, rows), jnp.int32)] + [block] * first,
        in_specs=[whole(pltpu.SMEM), whole(), whole()],
        out_specs=[whole()] * (1 + first),
        compiler_params=params(),
        name="pack_far",
    )(offsets[count - first :], route_row, amps)
    target, far = outs[0], list(outs[1:])
    near = []
    if count > first:
        near = pl.pallas_call(
            more_kernel,
            out_shape=[block] * (count - first),
            in_specs=[whole(pltpu.SMEM), whole(), whole()],
            out_specs=[whole()] * (count - first),
            compiler_params=params(),
            name="pack_near",
        )(offsets[: count - first], target, amps)
    return target, list(near) + far


def ladder_kernel(share_ref, weight_ref, amps_ref, out_ref):
    out_ref[...] = jnp.dot(weight_ref[...], amps_ref[...], preferred_element_type=F32).astype(BF16)[None]


def ladder_share(share, weight, amps, lad_count, sub_count):
    rows, holes = amps.shape
    return pl.pallas_call(
        ladder_kernel,
        out_shape=jax.ShapeDtypeStruct((lad_count, rows, holes), BF16),
        grid_spec=pltpu.PrefetchScalarGridSpec(
            num_scalar_prefetch=1,
            grid=(lad_count,),
            in_specs=[
                pl.BlockSpec((rows, rows), lambda i, share: (i * sub_count + share[0], 0)),
                pl.BlockSpec((rows, holes), lambda i, share: (0, 0)),
            ],
            out_specs=pl.BlockSpec((1, rows, holes), lambda i, share: (i, 0, 0)),
        ),
        compiler_params=params(),
        cost_estimate=pl.CostEstimate(
            flops=2 * lad_count * rows * rows * holes,
            bytes_accessed=2 * lad_count * rows * (rows + holes),
            transcendentals=0,
        ),
        name="ladder_share",
    )(share, weight, amps)


def operator_kernel(group, block_index, weight_ref, mixing_ref, out_ref, half_ref):
    k = pl.program_id(0)
    block_rows, capacity = weight_ref.shape
    per_block = block_rows // group
    for a in range(per_block):
        mix = mixing_ref[block_index[k] * per_block + a]
        half_ref[pl.ds(a * group, group), :] = lax.dot_general(
            mix,
            weight_ref[pl.ds(a * group, group), :],
            (((0,), (0,)), ((), ())),
            preferred_element_type=F32,
        ).astype(BF16)
    for j in range(capacity // block_rows):
        for b in range(per_block):
            at = block_index[j] * per_block + b
            columns = pl.ds(pl.multiple_of(at * group, group), group)
            out_ref[:, pl.ds(j * block_rows + b * group, group)] = jnp.dot(
                half_ref[:, columns], mixing_ref[at], preferred_element_type=F32
            ).astype(BF16)


def cycle_operator(block_index, weight, mixing, block_rows):
    capacity = weight.shape[0]
    group = mixing.shape[1]
    return pl.pallas_call(
        functools.partial(operator_kernel, group),
        out_shape=jax.ShapeDtypeStruct((capacity, capacity), BF16),
        grid_spec=pltpu.PrefetchScalarGridSpec(
            num_scalar_prefetch=1,
            grid=(capacity // block_rows,),
            in_specs=[
                pl.BlockSpec((block_rows, capacity), lambda k, index: (index[k], 0)),
                pl.BlockSpec(mixing.shape, lambda k, index: (0, 0, 0)),
            ],
            out_specs=pl.BlockSpec((block_rows, capacity), lambda k, index: (k, 0)),
            scratch_shapes=[pltpu.VMEM((block_rows, capacity), BF16)],
        ),
        compiler_params=params(),
        cost_estimate=pl.CostEstimate(
            flops=4 * capacity * capacity * group, bytes_accessed=4 * capacity * capacity, transcendentals=0
        ),
        name="cycle_operator",
    )(block_index, weight, mixing)


def cycle_kernel(operator_ref, *refs):
    count = len(refs) // 2
    in_refs, out_refs = refs[:count], refs[count:]
    block_rows = in_refs[0].shape[0]
    for k in reversed(range(count)):
        total = None
        for j in range(count):
            part = jnp.dot(
                operator_ref[pl.ds(k * block_rows, block_rows), pl.ds(j * block_rows, block_rows)],
                in_refs[j][...],
                preferred_element_type=F32,
            )
            total = part if total is None else total + part
        out_refs[k][...] = total.astype(BF16)


def apply_cycle(operator, blocks):
    return pl.pallas_call(
        cycle_kernel,
        out_shape=[jax.ShapeDtypeStruct(b.shape, BF16) for b in blocks],
        in_specs=[whole()] * (1 + len(blocks)),
        out_specs=[whole()] * len(blocks),
        compiler_params=params(),
        name="apply_cycle",
    )(operator, *blocks)


def finish_kernel(off_ref, target_ref, base_ref, part_ref, hole_ref, *refs):
    block_refs, out_ref = refs[:-1], refs[-1]
    total = base_ref[...]
    target = target_ref[...]
    for k, block_ref in enumerate(block_refs):
        slots = lax.broadcasted_iota(jnp.int32, (target.shape[0], block_ref.shape[0]), 1)
        pick = selection(slots == target - off_ref[k])
        total = total + jnp.dot(pick, block_ref[...], preferred_element_type=F32)
    out_ref[...] = (total / (part_ref[...] + hole_ref[...])).astype(BF16)


def finish(offsets, target_column, base, part_column, hole_row, blocks):
    rows, holes = base.shape
    tile = 128 if rows % 128 == 0 else rows
    row_spec = lambda width: pl.BlockSpec((tile, width), lambda i: (i, 0))
    return pl.pallas_call(
        finish_kernel,
        out_shape=jax.ShapeDtypeStruct((rows, holes), BF16),
        grid=(rows // tile,),
        in_specs=[whole(pltpu.SMEM), row_spec(1), row_spec(holes), row_spec(1), pl.BlockSpec((1, holes), lambda i: (0, 0))]
        + [pl.BlockSpec(b.shape, lambda i: (0, 0)) for b in blocks],
        out_specs=row_spec(holes),
        compiler_params=params(),
        name="finish",
    )(offsets, target_column, base, part_column, hole_row, *blocks)


def body(amplitudes, driving, route, ladder_weight, ph_weight, recouple, gap_part, gap_hole):
    amps = amplitudes[0]
    rows, holes = amps.shape
    chan_count = lax.axis_size("chan")
    lad_count = lax.axis_size("lad")
    sub_count = lax.axis_size("sub")
    chan, lad, sub = lax.axis_index("chan"), lax.axis_index("lad"), lax.axis_index("sub")
    weight, mixing = ph_weight[0, 0], recouple[0, 0]
    capacity = weight.shape[0]
    send = capacity // chan_count
    paired = send % mixing.shape[1] == 0 and chan_count & (chan_count - 1) == 0
    if paired:
        block_rows = send
        block_index = jnp.stack([chan ^ k for k in range(chan_count)]).astype(jnp.int32)
    else:
        block_rows = capacity
        block_index = jnp.zeros((1,), jnp.int32)
    offsets = block_index * block_rows

    def exchange(blocks):
        if not paired:
            whole_block = blocks[0].reshape(chan_count, send, holes)
            whole_block = lax.all_to_all(whole_block, "chan", split_axis=0, concat_axis=0, tiled=True)
            return [whole_block.reshape(capacity, holes)]
        arrived = [blocks[0]]
        for k in range(1, chan_count):
            pairs = [(i, i ^ k) for i in range(chan_count)]
            arrived.append(lax.ppermute(blocks[k], "chan", pairs))
        return arrived

    target, outgoing = pack(offsets, route[0].reshape(1, rows), amps, chan_count, send, block_rows)
    blocks = exchange(outgoing)

    kept = None
    for step in reversed(range(sub_count)):
        share = lax.rem(sub + step, sub_count).astype(jnp.int32).reshape(1)
        part = ladder_share(share, ladder_weight[0], amps, lad_count, sub_count)
        if step:
            pairs = [(i, (i + step) % sub_count) for i in range(sub_count)]
            part = lax.ppermute(part, "sub", pairs)
        kept = [part] if kept is None else kept + [part]

    def chip_sum(position):
        picked = [lax.dynamic_index_in_dim(p, position, 0, keepdims=False) for p in kept]
        return sum(p.astype(F32) for p in picked)

    base = driving[0].astype(F32) + chip_sum(lad)
    for step in range(1, lad_count):
        pairs = [(i, (i + step) % lad_count) for i in range(lad_count)]
        term = chip_sum(lax.rem(lad + step, lad_count)).astype(BF16)
        base = base + lax.ppermute(term, "lad", pairs).astype(F32)

    operator = cycle_operator(block_index, weight, mixing, block_rows)
    returned = exchange(apply_cycle(operator, blocks))
    updated = finish(
        offsets,
        target.reshape(rows, 1),
        base,
        gap_part[0].reshape(rows, 1),
        gap_hole.reshape(1, holes),
        returned,
    )
    return updated[None]


def solution(mesh):
    placed = (
        P(("parts", "chan"), ("lad", "sub"), None),
        P(("parts", "chan"), ("lad", "sub"), None),
        P("chan", ("lad", "sub"), None),
        P("chan", None, ("lad", "sub")),
        P("chan", ("lad", "sub"), None, None),
        P("chan", ("lad", "sub"), None, None, None),
        P(("parts", "chan"), ("lad", "sub")),
        P("parts"),
    )
    return jax.shard_map(
        body,
        mesh=mesh,
        in_specs=placed,
        out_specs=P(("parts", "chan"), ("lad", "sub"), None),
        check_vma=False,
    )
```

time: 189 us -> 101 us (0.53)
  the two profiles are of different devices: /device:TPU:0 before, /device:TPU:16 now
where the time goes in v1:
time: 101 us; the launch traced here: 100 us
  waiting for transfers between devices  57.2 us (57%)
  Pallas kernels  26.3 us (26%)
  starting transfers between devices  8.59 us (9%)
  other arithmetic  4.3 us (4%)
  local copies, waits for them, and re-layouts  3.71 us (4%)
    ppermute x6, waiting for transfers between devices, exchange(): arrived.append(lax.ppermute(blocks[k], 'chan', pairs))  56.3 us
    ppermute x6, starting transfers between devices, exchange(): arrived.append(lax.ppermute(blocks[k], 'chan', pairs))  7.1 us
    pallas_call x2, Pallas kernels, ladder_share(): pl.pallas_call(ladder_kernel, out_shape=jax.ShapeDtypeStruct((lad_count,...  6.66 us
    pallas_call x1, Pallas kernels, cycle_operator(): pl.pallas_call(functools.partial(operator_kernel, group), out_shape=jax.S...  6.07 us
    pallas_call x1, Pallas kernels, apply_cycle(): pl.pallas_call(cycle_kernel, out_shape=[jax.ShapeDtypeStruct(b.shape, BF1...  5.76 us
    pallas_call x1, Pallas kernels, finish(): pl.pallas_call(finish_kernel, out_shape=jax.ShapeDtypeStruct((rows, holes...  4.99 us
    unnamed x14, local copies, waits for them, and re-layouts  3.27 us
    convert_element_type x1, other arithmetic, body(): term = chip_sum(lax.rem(lad + step, lad_count)).astype(BF16)  2.22 us
  transfers between devices with their start and end apart: 8, of which 7 were waited for; matrix products, arithmetic and copies ran while one was open for 3% of the time, Pallas kernels for 17%

profile of v1, /device:TPU:16, one launch (start us, length us, event | category | flops | bytes accessed | tf_op | source)
XLA Modules:
  0.0 100.3 jit_solution(4817334316830215308)
XLA Ops:
  0.0 0.0 copy-start.1
  0.0 1.1 %copy-done.1 = bf16[1,768,512]{2,1,0:T(8,128)(2,1)S(1)} copy-done((bf16[1,768,512]{2,1,0:T(8,128)(2,1)S(1)}, bf16[1,768,512]{2,1,0:T(8,128)(2,1)}, u32[]{:S(2)}) %copy-start.1) | copy-done | bytes 786456
  1.1 0.0 copy-start.2
  1.1 3.8 %ladder_share.2 = bf16[2,768,512]{2,1,0:T(8,128)(2,1)} custom-call(s32[1]{0:T(128)} %bitcast.7.share_ref, bf16[3072,768]{1,0:T(8,128)(2,1)} %bitcast.27, bf16[768,512]{1,0:T(8,128)(2,1)S(1)} %bitcast.19), custom_call_target="tpu_custom_call" | custom-call | flops 1207959552 | bytes 3932160 | tf_op jit(solution)/shard_map/ladder_share/pallas_call | solution.py:88
  5.0 0.0 collective-permute-start
  5.0 0.0 copy-done.2
  5.0 2.8 %ladder_share.3 = bf16[2,768,512]{2,1,0:T(8,128)(2,1)S(1)} custom-call(s32[1]{0:T(128)} %bitcast.9.share_ref, bf16[3072,768]{1,0:T(8,128)(2,1)} %bitcast.28, bf16[768,512]{1,0:T(8,128)(2,1)S(1)} %bitcast.20), custom_call_target="tpu_custom_call" | custom-call | flops 1207959552 | bytes 3932160 | tf_op jit(solution)/shard_map/ladder_share/pallas_call | solution.py:88
  7.8 0.0 copy-start.4
  7.8 0.0 copy-start.3
  7.8 0.9 collective-permute-done
  8.7 2.2 %fusion = bf16[768,512]{1,0:T(8,128)(2,1)} fusion(bf16[2,768,512]{2,1,0:T(8,128)(2,1)S(1)} %ladder_share.3, s32[]{:T(128)S(6)} %select_n.10, bf16[2,768,512]{2,1,0:T(8,128)(2,1)} %collective-permute-done), kind=kLoop, calls=%fused_computation.2 | loop fusion | flops 1572864 | bytes 2359300 | tf_op jit(solution)/shard_map/convert_element_type | solution.py:258
  10.9 1.5 %collective-permute-start.1 = (bf16[768,512]{1,0:T(8,128)(2,1)}, bf16[768,512]{1,0:T(8,128)(2,1)}, u32[]{:S(2)}, u32[]{:S(2)}) collective-permute-start(bf16[768,512]{1,0:T(8,128)(2,1)} %fusion), channel_id=1, source_target_pairs={{0,2},{2,0},{1,3},{3,1},{4,6},{6,4},{5,7},{7,5},{8,10},{10,8},{9,1... | collective-permute-start | bytes 2359304 | tf_op jit(solution)/shard_map/ppermute | solution.py:259
  12.4 0.1 broadcast_multiply_fusion
  12.5 0.1 fusion.1
  12.6 0.0 copy-done.4
  12.6 1.5 %pack_far.1 = (s32[1,768]{1,0:T(1,128)S(1)}, bf16[384,512]{1,0:T(8,128)(2,1)S(1)}, bf16[384,512]{1,0:T(8,128)(2,1)S(1)}) custom-call(s32[2]{0:T(128)S(1)} %get-tuple-element.26.off_ref, s32[1,768]{1,0:T(1,128)S(1)} %bitcast.25, bf16[768,512]{1,0:T(8,128)(2,1)S(1)} %bitcast.21), custom_call_target="tpu_custom_call" | custom-call | tf_op jit(solution)/shard_map/pack_far/pallas_call | solution.py:60
  14.1 1.3 %pack_near.1 = (bf16[384,512]{1,0:T(8,128)(2,1)S(1)}, bf16[384,512]{1,0:T(8,128)(2,1)S(1)}) custom-call(s32[2]{0:T(128)S(1)} %get-tuple-element.25.off_ref, s32[1,768]{1,0:T(1,128)S(1)} %get-tuple-element.14.target_ref, bf16[768,512]{1,0:T(8,128)(2,1)S(1)} %bitcast.22), custom_call_target="tpu_custom_call" | custom-call | tf_op jit(solution)/shard_map/pack_near/pallas_call | solution.py:71
  15.4 1.6 %collective-permute-start.2 = (bf16[384,512]{1,0:T(8,128)(2,1)S(1)}, bf16[384,512]{1,0:T(8,128)(2,1)S(1)}, u32[]{:S(2)}, u32[]{:S(2)}) collective-permute-start(bf16[384,512]{1,0:T(8,128)(2,1)S(1)} %get-tuple-element.16), channel_id=1, source_target_pairs={{0,4},{4,0},{8,12},{12,8},{1,5},{5,1},{9,13},{13,9},{2,6},{6,2},{1... | collective-permute-start | bytes 1179656 | tf_op jit(solution)/shard_map/ppermute | solution.py:236
  17.1 0.3 collective-permute-start.3
  17.4 1.6 %collective-permute-start.4 = (bf16[384,512]{1,0:T(8,128)(2,1)S(1)}, bf16[384,512]{1,0:T(8,128)(2,1)S(1)}, u32[]{:S(2)}, u32[]{:S(2)}) collective-permute-start(bf16[384,512]{1,0:T(8,128)(2,1)S(1)} %get-tuple-element.18), channel_id=1, source_target_pairs={{0,12},{4,8},{8,4},{12,0},{1,13},{5,9},{9,5},{13,1},{2,14},{6,10},... | collective-permute-start | bytes 1179656 | tf_op jit(solution)/shard_map/ppermute | solution.py:236
  19.0 0.0 copy-done.3
  19.0 6.1 %cycle_operator.1.operator_ref = bf16[1536,1536]{1,0:T(8,128)(2,1)S(1)} custom-call(s32[4]{0:T(128)S(1)} %get-tuple-element.24.block_index, bf16[1536,1536]{1,0:T(8,128)(2,1)} %bitcast.29, bf16[12,128,128]{2,1,0:T(8,128)(2,1)S(1)} %bitcast.23), custom_call_target="tpu_custom_call" | custom-call | flops 1207959552 | bytes 9437184 | tf_op jit(solution)/shard_map/cycle_operator/pallas_call | solution.py:134
  25.1 0.0 copy-start
  25.1 2.1 %copy-done = bf16[1536,1536]{1,0:T(8,128)(2,1)} copy-done((bf16[1536,1536]{1,0:T(8,128)(2,1)}, bf16[1536,1536]{1,0:T(8,128)(2,1)S(1)}, u32[]{:S(2)}) %copy-start) | copy-done | bytes 4718616
  27.2 5.4 %collective-permute-done.2.refs_1_ = bf16[384,512]{1,0:T(8,128)(2,1)S(1)} collective-permute-done((bf16[384,512]{1,0:T(8,128)(2,1)S(1)}, bf16[384,512]{1,0:T(8,128)(2,1)S(1)}, u32[]{:S(2)}, u32[]{:S(2)}) %collective-permute-start.2) | collective-permute-done | bytes 393248 | tf_op jit(solution)/shard_map/ppermute | solution.py:236
  32.6 11.2 %collective-permute-done.3.refs_2_ = bf16[384,512]{1,0:T(8,128)(2,1)S(1)} collective-permute-done((bf16[384,512]{1,0:T(8,128)(2,1)S(1)}, bf16[384,512]{1,0:T(8,128)(2,1)S(1)}, u32[]{:S(2)}, u32[]{:S(2)}) %collective-permute-start.3) | collective-permute-done | bytes 393248 | tf_op jit(solution)/shard_map/ppermute | solution.py:236
  43.8 9.1 %collective-permute-done.4.refs_3_ = bf16[384,512]{1,0:T(8,128)(2,1)S(1)} collective-permute-done((bf16[384,512]{1,0:T(8,128)(2,1)S(1)}, bf16[384,512]{1,0:T(8,128)(2,1)S(1)}, u32[]{:S(2)}, u32[]{:S(2)}) %collective-permute-start.4) | collective-permute-done | bytes 393248 | tf_op jit(solution)/shard_map/ppermute | solution.py:236
  52.9 0.0 copy-start.6
  52.9 5.8 %apply_cycle.1 = (bf16[384,512]{1,0:T(8,128)(2,1)S(1)}, bf16[384,512]{1,0:T(8,128)(2,1)}, bf16[384,512]{1,0:T(8,128)(2,1)}, bf16[384,512]{1,0:T(8,128)(2,1)}) custom-call(bf16[1536,1536]{1,0:T(8,128)(2,1)} %copy-done, bf16[384,512]{1,0:T(8,128)(2,1)S(1)} %get-tuple-element.15.refs_0_, bf16[384,512]{1,0:T(8,128)(2,1)S(1)} %collective-permute-done.2.refs_1_, ...), custom_call_target="tpu_custom_call" | custom-call | tf_op jit(solution)/shard_map/apply_cycle/pallas_call | solution.py:172
  58.6 0.1 collective-permute-start.5
  58.7 1.9 %collective-permute-start.6 = (bf16[384,512]{1,0:T(8,128)(2,1)}, bf16[384,512]{1,0:T(8,128)(2,1)S(1)}, u32[]{:S(2)}, u32[]{:S(2)}) collective-permute-start(bf16[384,512]{1,0:T(8,128)(2,1)} %get-tuple-element.21), channel_id=1, source_target_pairs={{0,8},{4,12},{8,0},{12,4},{1,9},{5,13},{9,1},{13,5},{2,10},{6,14},... | collective-permute-start | bytes 1179656 | tf_op jit(solution)/shard_map/ppermute | solution.py:236
  60.6 1.6 %collective-permute-start.7 = (bf16[384,512]{1,0:T(8,128)(2,1)}, bf16[384,512]{1,0:T(8,128)(2,1)}, u32[]{:S(2)}, u32[]{:S(2)}) collective-permute-start(bf16[384,512]{1,0:T(8,128)(2,1)} %get-tuple-element.22), channel_id=1, source_target_pairs={{0,12},{4,8},{8,4},{12,0},{1,13},{5,9},{9,5},{13,1},{2,14},{6,10},... | collective-permute-start | bytes 1179656 | tf_op jit(solution)/shard_map/ppermute | solution.py:236
  62.2 0.2 copy.9.target_ref
  62.4 0.0 copy-done.6
  62.4 0.2 copy.10.part_ref
  62.6 0.0 copy-start.5
  62.6 0.0 collective-permute-done.1
  62.6 2.0 %bitcast_add_fusion.base_ref = f32[768,512]{1,0:T(8,128)S(1)} fusion(bf16[768,512]{1,0:T(8,128)(2,1)} %collective-permute-done.1, bf16[1,768,512]{2,1,0:T(8,128)(2,1)} %param.9, bf16[2,768,512]{2,1,0:T(8,128)(2,1)S(1)} %ladder_share.3, s32[]{:T(128)S(6)} %select_n.9, bf16[2,768,512]{2,1,0:T(8,128)(2,1)} %collective-permute-done), kind=kLoop, calls=%fused_computation | loop fusion | flops 2752512 | bytes 4718596 | tf_op jit(solution)/shard_map/add | solution.py:259
  64.6 8.5 %collective-permute-done.5.refs_1_ = bf16[384,512]{1,0:T(8,128)(2,1)S(1)} collective-permute-done((bf16[384,512]{1,0:T(8,128)(2,1)}, bf16[384,512]{1,0:T(8,128)(2,1)S(1)}, u32[]{:S(2)}, u32[]{:S(2)}) %collective-permute-start.5) | collective-permute-done | bytes 393248 | tf_op jit(solution)/shard_map/ppermute | solution.py:236
  73.1 14.3 %collective-permute-done.6.refs_2_ = bf16[384,512]{1,0:T(8,128)(2,1)S(1)} collective-permute-done((bf16[384,512]{1,0:T(8,128)(2,1)}, bf16[384,512]{1,0:T(8,128)(2,1)S(1)}, u32[]{:S(2)}, u32[]{:S(2)}) %collective-permute-start.6) | collective-permute-done | bytes 393248 | tf_op jit(solution)/shard_map/ppermute | solution.py:236
  87.4 7.9 %collective-permute-done.7.refs_3_ = bf16[384,512]{1,0:T(8,128)(2,1)} collective-permute-done((bf16[384,512]{1,0:T(8,128)(2,1)}, bf16[384,512]{1,0:T(8,128)(2,1)}, u32[]{:S(2)}, u32[]{:S(2)}) %collective-permute-start.7) | collective-permute-done | bytes 393248 | tf_op jit(solution)/shard_map/ppermute | solution.py:236
  95.3 0.0 copy-done.5
  95.3 5.0 %finish.1 = bf16[768,512]{1,0:T(8,128)(2,1)} custom-call(s32[4]{0:T(128)S(1)} %get-tuple-element.23.off_ref, s32[768,1]{1,0:T(8,128)S(1)} %copy.9.target_ref, f32[768,512]{1,0:T(8,128)S(1)} %bitcast_add_fusion.base_ref, f32[768,1]{1,0:T(8,128)S(1)} %copy.10.part_ref, f32[1,512]{1,0:T(1,128)S(1)} %bitcast.26, bf16[384,512]{1,0:T(8,128)(2,1)S(1)} %get-tuple-element.19.refs_0_, ...), custom_call_target="tpu_custom_call" | custom-call | tf_op jit(solution)/shard_map/finish/pallas_call | solution.py:197
Async XLA Ops:
  0.0 1.1 %copy-start.1 = (bf16[1,768,512]{2,1,0:T(8,128)(2,1)S(1)}, bf16[1,768,512]{2,1,0:T(8,128)(2,1)}, u32[]{:S(2)}) copy-start(bf16[1,768,512]{2,1,0:T(8,128)(2,1)} %param.8) | copy-start | bytes 2359300
  1.1 3.8 %copy-start.2 = (bf16[1,768,512]{2,1,0:T(8,128)(2,1)S(1)}, bf16[1,768,512]{2,1,0:T(8,128)(2,1)}, u32[]{:S(2)}) copy-start(bf16[1,768,512]{2,1,0:T(8,128)(2,1)} %param.8) | copy-start | bytes 2359300
  5.0 3.8 %collective-permute-start = (bf16[2,768,512]{2,1,0:T(8,128)(2,1)}, bf16[2,768,512]{2,1,0:T(8,128)(2,1)}, u32[]{:S(2)}, u32[]{:S(2)}) collective-permute-start(bf16[2,768,512]{2,1,0:T(8,128)(2,1)} %ladder_share.2), channel_id=1, source_target_pairs={{0,1},{1,0},{2,3},{3,2},{4,5},{5,4},{6,7},{7,6},{8,9},{9,8},{10,11... | collective-permute-start | bytes 4718600 | tf_op jit(solution)/shard_map/ppermute | solution.py:248
  7.8 4.8 %copy-start.4 = (s32[1,768,1]{1,2,0:T(1,128)S(1)}, s32[1,768,1]{1,2,0:T(1,128)}, u32[]{:S(2)}) copy-start(s32[1,768,1]{1,2,0:T(1,128)} %param.10) | copy-start | bytes 9220
  7.8 11.2 %copy-start.3 = (bf16[1,1,12,128,128]{4,3,2,1,0:T(8,128)(2,1)S(1)}, bf16[1,1,12,128,128]{4,3,2,1,0:T(8,128)(2,1)}, u32[]{:S(2)}) copy-start(bf16[1,1,12,128,128]{4,3,2,1,0:T(8,128)(2,1)} %param.13) | copy-start | bytes 1179652
  10.9 51.7 %collective-permute-start.1 = (bf16[768,512]{1,0:T(8,128)(2,1)}, bf16[768,512]{1,0:T(8,128)(2,1)}, u32[]{:S(2)}, u32[]{:S(2)}) collective-permute-start(bf16[768,512]{1,0:T(8,128)(2,1)} %fusion), channel_id=1, source_target_pairs={{0,2},{2,0},{1,3},{3,1},{4,6},{6,4},{5,7},{7,5},{8,10},{10,8},{9,1... | collective-permute-start | bytes 2359304 | tf_op jit(solution)/shard_map/ppermute | solution.py:259
  15.4 17.1 %collective-permute-start.2 = (bf16[384,512]{1,0:T(8,128)(2,1)S(1)}, bf16[384,512]{1,0:T(8,128)(2,1)S(1)}, u32[]{:S(2)}, u32[]{:S(2)}) collective-permute-start(bf16[384,512]{1,0:T(8,128)(2,1)S(1)} %get-tuple-element.16), channel_id=1, source_target_pairs={{0,4},{4,0},{8,12},{12,8},{1,5},{5,1},{9,13},{13,9},{2,6},{6,2},{1... | collective-permute-start | bytes 1179656 | tf_op jit(solution)/shard_map/ppermute | solution.py:236
  17.1 26.7 %collective-permute-start.3 = (bf16[384,512]{1,0:T(8,128)(2,1)S(1)}, bf16[384,512]{1,0:T(8,128)(2,1)S(1)}, u32[]{:S(2)}, u32[]{:S(2)}) collective-permute-start(bf16[384,512]{1,0:T(8,128)(2,1)S(1)} %get-tuple-element.17), channel_id=1, source_target_pairs={{0,8},{4,12},{8,0},{12,4},{1,9},{5,13},{9,1},{13,5},{2,10},{6,14},... | collective-permute-start | bytes 1179656 | tf_op jit(solution)/shard_map/ppermute | solution.py:236
  17.4 35.5 %collective-permute-start.4 = (bf16[384,512]{1,0:T(8,128)(2,1)S(1)}, bf16[384,512]{1,0:T(8,128)(2,1)S(1)}, u32[]{:S(2)}, u32[]{:S(2)}) collective-permute-start(bf16[384,512]{1,0:T(8,128)(2,1)S(1)} %get-tuple-element.18), channel_id=1, source_target_pairs={{0,12},{4,8},{8,4},{12,0},{1,13},{5,9},{9,5},{13,1},{2,14},{6,10},... | collective-permute-start | bytes 1179656 | tf_op jit(solution)/shard_map/ppermute | solution.py:236
  25.1 2.1 %copy-start = (bf16[1536,1536]{1,0:T(8,128)(2,1)}, bf16[1536,1536]{1,0:T(8,128)(2,1)S(1)}, u32[]{:S(2)}) copy-start(bf16[1536,1536]{1,0:T(8,128)(2,1)S(1)} %cycle_operator.1.operator_ref) | copy-start | bytes 14155780
  52.9 9.5 %copy-start.6 = (f32[1,768]{1,0:T(1,128)S(1)}, f32[1,768]{1,0:T(1,128)}, u32[]{:S(2)}) copy-start(f32[1,768]{1,0:T(1,128)} %param.14) | copy-start | bytes 9220
  58.6 14.4 %collective-permute-start.5 = (bf16[384,512]{1,0:T(8,128)(2,1)}, bf16[384,512]{1,0:T(8,128)(2,1)S(1)}, u32[]{:S(2)}, u32[]{:S(2)}) collective-permute-start(bf16[384,512]{1,0:T(8,128)(2,1)} %get-tuple-element.20), channel_id=1, source_target_pairs={{0,4},{4,0},{8,12},{12,8},{1,5},{5,1},{9,13},{13,9},{2,6},{6,2},{1... | collective-permute-start | bytes 1179656 | tf_op jit(solution)/shard_map/ppermute | solution.py:236
  58.7 28.6 %collective-permute-start.6 = (bf16[384,512]{1,0:T(8,128)(2,1)}, bf16[384,512]{1,0:T(8,128)(2,1)S(1)}, u32[]{:S(2)}, u32[]{:S(2)}) collective-permute-start(bf16[384,512]{1,0:T(8,128)(2,1)} %get-tuple-element.21), channel_id=1, source_target_pairs={{0,8},{4,12},{8,0},{12,4},{1,9},{5,13},{9,1},{13,5},{2,10},{6,14},... | collective-permute-start | bytes 1179656 | tf_op jit(solution)/shard_map/ppermute | solution.py:236
  60.6 34.6 %collective-permute-start.7 = (bf16[384,512]{1,0:T(8,128)(2,1)}, bf16[384,512]{1,0:T(8,128)(2,1)}, u32[]{:S(2)}, u32[]{:S(2)}) collective-permute-start(bf16[384,512]{1,0:T(8,128)(2,1)} %get-tuple-element.22), channel_id=1, source_target_pairs={{0,12},{4,8},{8,4},{12,0},{1,13},{5,9},{9,5},{13,1},{2,14},{6,10},... | collective-permute-start | bytes 1179656 | tf_op jit(solution)/shard_map/ppermute | solution.py:236
  62.6 32.7 %copy-start.5 = (f32[512]{0:T(512)S(1)}, f32[512]{0:T(512)}, u32[]{:S(2)}) copy-start(f32[512]{0:T(512)} %param.15) | copy-start | bytes 6148

commit v2 on v1

--- a/solution.py
+++ b/solution.py
@@ -7,9 +7,12 @@
 from jax.experimental.pallas import tpu as pltpu
 from jax.sharding import PartitionSpec as P
 
-VMEM_LIMIT = 48 * 1024 * 1024
+VMEM_LIMIT = 20 * 1024 * 1024
+HALVES = 2
 F32 = jnp.float32
 BF16 = jnp.bfloat16
+CHEAP = pl.CostEstimate(flops=0, bytes_accessed=0, transcendentals=0)
+DEAR = pl.CostEstimate(flops=3 * 10**10, bytes_accessed=10**6, transcendentals=0)
 
 
 def params():
@@ -24,8 +27,14 @@
     return jnp.where(match, 1.0, 0.0).astype(BF16)
 
 
-def pack_kernel(chan_count, send, off_ref, route_ref, amps_ref, *out_refs):
-    target_ref, block_refs = out_refs[0], out_refs[1:]
+def place_rows(offset, target, amps, block_refs):
+    slots = lax.broadcasted_iota(jnp.int32, (block_refs[0].shape[0], target.shape[1]), 0)
+    pick = selection(slots == target - offset)
+    for block_ref, columns in zip(block_refs, amps):
+        block_ref[...] = jnp.dot(pick, columns, preferred_element_type=F32).astype(BF16)
+
+
+def first_kernel(chan_count, send, off_ref, route_ref, amps_ref, target_ref, *block_refs):
     owners = route_ref[...]
     rows = owners.shape[1]
     lanes = max(16, chan_count)
@@ -38,45 +47,78 @@
     slot = jnp.sum(jnp.where(hot, earlier, 0.0), axis=0, keepdims=True)
     target = owners * send + slot.astype(jnp.int32)
     target_ref[...] = target
-    place_rows(off_ref, target, amps_ref, block_refs)
-
-
-def place_rows(off_ref, target, amps_ref, block_refs):
-    for k, block_ref in enumerate(block_refs):
-        slots = lax.broadcasted_iota(jnp.int32, (block_ref.shape[0], target.shape[1]), 0)
-        pick = selection(slots == target - off_ref[k])
-        block_ref[...] = jnp.dot(pick, amps_ref[...], preferred_element_type=F32).astype(BF16)
-
-
-def more_kernel(off_ref, target_ref, amps_ref, *block_refs):
-    place_rows(off_ref, target_ref[...], amps_ref, block_refs)
+    first = off_ref.shape[0] - len(block_refs)
+    for i, block_ref in enumerate(block_refs):
+        place_rows(off_ref[first + i], target, [amps_ref[:, : block_ref.shape[1]]], [block_ref])
+
+
+def rest_kernel(parts, skipped, off_ref, target_ref, amps_ref, *block_refs):
+    target = target_ref[...]
+    width = amps_ref.shape[1] // parts
+    columns = [amps_ref[:, pl.ds(h * width, width)] for h in range(parts)]
+    left = list(block_refs)
+    for k in range(off_ref.shape[0]):
+        wanted = columns if k < skipped else columns[1:]
+        refs, left = left[: len(wanted)], left[len(wanted) :]
+        place_rows(off_ref[k], target, wanted, refs)
 
 
 def pack(offsets, route_row, amps, chan_count, send, block_rows):
     rows, holes = amps.shape
-    block = jax.ShapeDtypeStruct((block_rows, holes), BF16)
     count = offsets.shape[0]
-    first = (count + 1) // 2
+    far = count // 2 if count > 1 else 1
+    near = count - far
+    block = jax.ShapeDtypeStruct((block_rows, holes // HALVES), BF16)
     outs = pl.pallas_call(
-        functools.partial(pack_kernel, chan_count, send),
-        out_shape=[jax.ShapeDtypeStruct((1, rows), jnp.int32)] + [block] * first,
+        functools.partial(first_kernel, chan_count, send),
+        out_shape=[jax.ShapeDtypeStruct((1, rows), jnp.int32)] + [block] * far,
         in_specs=[whole(pltpu.SMEM), whole(), whole()],
-        out_specs=[whole()] * (1 + first),
-        compiler_params=params(),
-        name="pack_far",
-    )(offsets[count - first :], route_row, amps)
-    target, far = outs[0], list(outs[1:])
-    near = []
-    if count > first:
-        near = pl.pallas_call(
-            more_kernel,
-            out_shape=[block] * (count - first),
+        out_specs=[whole()] * (1 + far),
+        compiler_params=params(),
+        cost_estimate=CHEAP,
+        name="pack_first",
+    )(offsets, route_row, amps)
+    target, early = outs[0], list(outs[1:])
+    number = near * HALVES + far * (HALVES - 1)
+    late = list(
+        pl.pallas_call(
+            functools.partial(rest_kernel, HALVES, near),
+            out_shape=[block] * number,
             in_specs=[whole(pltpu.SMEM), whole(), whole()],
-            out_specs=[whole()] * (count - first),
+            out_specs=[whole()] * number,
             compiler_params=params(),
-            name="pack_near",
-        )(offsets[: count - first], target, amps)
-    return target, list(near) + far
+            name="pack_rest",
+        )(offsets, target, amps)
+    )
+    blocks = [[None] * count for _ in range(HALVES)]
+    for k in range(count):
+        if k >= near:
+            blocks[0][k] = early[k - near]
+        for h in range(0 if k < near else 1, HALVES):
+            blocks[h][k] = late.pop(0)
+    return target, blocks
+
+
+def unpack_kernel(off_ref, target_ref, out_ref):
+    count = off_ref.shape[0]
+    rows, capacity = out_ref.shape
+    block_rows = capacity // count
+    target = target_ref[...]
+    slots = lax.broadcasted_iota(jnp.int32, (rows, block_rows), 1)
+    for k in range(count):
+        out_ref[:, pl.ds(k * block_rows, block_rows)] = selection(slots == target - off_ref[k])
+
+
+def unpack_matrix(offsets, target_column, capacity):
+    return pl.pallas_call(
+        unpack_kernel,
+        out_shape=jax.ShapeDtypeStruct((target_column.shape[0], capacity), BF16),
+        in_specs=[whole(pltpu.SMEM), whole()],
+        out_specs=whole(),
+        compiler_params=params(),
+        cost_estimate=CHEAP,
+        name="unpack_matrix",
+    )(offsets, target_column)
 
 
 def ladder_kernel(share_ref, weight_ref, amps_ref, out_ref):
@@ -98,11 +140,7 @@
             out_specs=pl.BlockSpec((1, rows, holes), lambda i, share: (i, 0, 0)),
         ),
         compiler_params=params(),
-        cost_estimate=pl.CostEstimate(
-            flops=2 * lad_count * rows * rows * holes,
-            bytes_accessed=2 * lad_count * rows * (rows + holes),
-            transcendentals=0,
-        ),
+        cost_estimate=CHEAP,
         name="ladder_share",
     )(share, weight, amps)
 
@@ -145,27 +183,21 @@
             scratch_shapes=[pltpu.VMEM((block_rows, capacity), BF16)],
         ),
         compiler_params=params(),
-        cost_estimate=pl.CostEstimate(
-            flops=4 * capacity * capacity * group, bytes_accessed=4 * capacity * capacity, transcendentals=0
-        ),
+        cost_estimate=CHEAP,
         name="cycle_operator",
     )(block_index, weight, mixing)
 
 
 def cycle_kernel(operator_ref, *refs):
     count = len(refs) // 2
-    in_refs, out_refs = refs[:count], refs[count:]
+    in_refs, out_refs, block_ref = refs[:count], refs[count : 2 * count], refs[2 * count]
     block_rows = in_refs[0].shape[0]
+    for j in range(count):
+        block_ref[pl.ds(j * block_rows, block_rows), :] = in_refs[j][...]
     for k in reversed(range(count)):
-        total = None
-        for j in range(count):
-            part = jnp.dot(
-                operator_ref[pl.ds(k * block_rows, block_rows), pl.ds(j * block_rows, block_rows)],
-                in_refs[j][...],
-                preferred_element_type=F32,
-            )
-            total = part if total is None else total + part
-        out_refs[k][...] = total.astype(BF16)
+        out_refs[k][...] = jnp.dot(
+            operator_ref[pl.ds(k * block_rows, block_rows), :], block_ref[...], preferred_element_type=F32
+        ).astype(BF16)
 
 
 def apply_cycle(operator, blocks):
@@ -174,36 +206,52 @@
         out_shape=[jax.ShapeDtypeStruct(b.shape, BF16) for b in blocks],
         in_specs=[whole()] * (1 + len(blocks)),
         out_specs=[whole()] * len(blocks),
-        compiler_params=params(),
+        scratch_shapes=[pltpu.VMEM((operator.shape[0], blocks[0].shape[1]), BF16)],
+        compiler_params=params(),
+        cost_estimate=DEAR,
         name="apply_cycle",
     )(operator, *blocks)
 
 
-def finish_kernel(off_ref, target_ref, base_ref, part_ref, hole_ref, *refs):
-    block_refs, out_ref = refs[:-1], refs[-1]
+def finish_kernel(pick_ref, base_ref, part_ref, hole_ref, *refs):
+    out_ref = refs[-1]
+    count = (pick_ref.shape[1]) // refs[0].shape[0]
+    block_rows = refs[0].shape[0]
     total = base_ref[...]
-    target = target_ref[...]
-    for k, block_ref in enumerate(block_refs):
-        slots = lax.broadcasted_iota(jnp.int32, (target.shape[0], block_ref.shape[0]), 1)
-        pick = selection(slots == target - off_ref[k])
-        total = total + jnp.dot(pick, block_ref[...], preferred_element_type=F32)
+    for k in range(count):
+        total = total + jnp.dot(
+            pick_ref[:, pl.ds(k * block_rows, block_rows)], refs[k][...], preferred_element_type=F32
+        )
     out_ref[...] = (total / (part_ref[...] + hole_ref[...])).astype(BF16)
 
 
-def finish(offsets, target_column, base, part_column, hole_row, blocks):
+def finish(half, pick, base, part_column, hole_row, blocks, earlier):
     rows, holes = base.shape
-    tile = 128 if rows % 128 == 0 else rows
-    row_spec = lambda width: pl.BlockSpec((tile, width), lambda i: (i, 0))
+    tile = rows // 2
+    width = holes // HALVES
+    in_specs = [
+        pl.BlockSpec((tile, pick.shape[1]), lambda i: (i, 0)),
+        pl.BlockSpec((tile, width), lambda i: (i, half)),
+        pl.BlockSpec((tile, 1), lambda i: (i, 0)),
+        pl.BlockSpec((1, width), lambda i: (0, half)),
+    ] + [pl.BlockSpec(b.shape, lambda i: (0, 0)) for b in blocks]
+    operands = [pick, base, part_column, hole_row, *blocks]
+    aliases = {}
+    if earlier is not None:
+        aliases = {len(operands): 0}
+        operands.append(earlier)
+        in_specs.append(pl.BlockSpec(memory_space=pl.ANY))
     return pl.pallas_call(
         finish_kernel,
         out_shape=jax.ShapeDtypeStruct((rows, holes), BF16),
         grid=(rows // tile,),
-        in_specs=[whole(pltpu.SMEM), row_spec(1), row_spec(holes), row_spec(1), pl.BlockSpec((1, holes), lambda i: (0, 0))]
-        + [pl.BlockSpec(b.shape, lambda i: (0, 0)) for b in blocks],
-        out_specs=row_spec(holes),
-        compiler_params=params(),
+        in_specs=in_specs,
+        out_specs=pl.BlockSpec((tile, width), lambda i: (i, half)),
+        input_output_aliases=aliases,
+        compiler_params=params(),
+        cost_estimate=CHEAP,
         name="finish",
-    )(offsets, target_column, base, part_column, hole_row, *blocks)
+    )(*operands)
 
 
 def body(amplitudes, driving, route, ladder_weight, ph_weight, recouple, gap_part, gap_hole):
@@ -227,17 +275,19 @@
 
     def exchange(blocks):
         if not paired:
-            whole_block = blocks[0].reshape(chan_count, send, holes)
-            whole_block = lax.all_to_all(whole_block, "chan", split_axis=0, concat_axis=0, tiled=True)
-            return [whole_block.reshape(capacity, holes)]
-        arrived = [blocks[0]]
-        for k in range(1, chan_count):
+            split = blocks[0].reshape(chan_count, send, -1)
+            split = lax.all_to_all(split, "chan", split_axis=0, concat_axis=0, tiled=True)
+            return [split.reshape(capacity, -1)]
+        arrived = [blocks[0]] + [None] * (chan_count - 1)
+        for k in reversed(range(1, chan_count)):
             pairs = [(i, i ^ k) for i in range(chan_count)]
-            arrived.append(lax.ppermute(blocks[k], "chan", pairs))
+            arrived[k] = lax.ppermute(blocks[k], "chan", pairs)
         return arrived
 
     target, outgoing = pack(offsets, route[0].reshape(1, rows), amps, chan_count, send, block_rows)
-    blocks = exchange(outgoing)
+    blocks = [exchange(part) for part in outgoing]
+    amps, outgoing = lax.optimization_barrier((amps, outgoing))
+    pick = unpack_matrix(offsets, target.reshape(rows, 1), capacity)
 
     kept = None
     for step in reversed(range(sub_count)):
@@ -259,15 +309,11 @@
         base = base + lax.ppermute(term, "lad", pairs).astype(F32)
 
     operator = cycle_operator(block_index, weight, mixing, block_rows)
-    returned = exchange(apply_cycle(operator, blocks))
-    updated = finish(
-        offsets,
-        target.reshape(rows, 1),
-        base,
-        gap_part[0].reshape(rows, 1),
-        gap_hole.reshape(1, holes),
-        returned,
-    )
+    part_column, hole_row = gap_part[0].reshape(rows, 1), gap_hole.reshape(1, holes)
+    returned = [exchange(apply_cycle(operator, part)) for part in blocks]
+    updated = None
+    for half in range(HALVES):
+        updated = finish(half, pick, base, part_column, hole_row, returned[half], updated)
     return updated[None]
 
 

time: 101 us -> 81.6 us (0.81)
  the two profiles are of different devices: /device:TPU:16 before, /device:TPU:0 now
where the time goes in v2:
time: 81.6 us; the launch traced here: 80.5 us
  starting transfers between devices  31.7 us (39%)
  Pallas kernels  21.5 us (26%)
  waiting for transfers between devices  15.8 us (19%)
  local copies, waits for them, and re-layouts  10.6 us (13%)
    ppermute x12, starting transfers between devices, exchange(): arrived[k] = lax.ppermute(blocks[k], 'chan', pairs)  30.2 us
    ppermute x12, waiting for transfers between devices, exchange(): arrived[k] = lax.ppermute(blocks[k], 'chan', pairs)  15.7 us
    unnamed x34, local copies, waits for them, and re-layouts  10.3 us
    pallas_call x2, Pallas kernels, apply_cycle(): pl.pallas_call(cycle_kernel, out_shape=[jax.ShapeDtypeStruct(b.shape, BF1...  4.89 us
    pallas_call x1, Pallas kernels, cycle_operator(): pl.pallas_call(functools.partial(operator_kernel, group), out_shape=jax.S...  4.37 us
    pallas_call x2, Pallas kernels, finish(): pl.pallas_call(finish_kernel, out_shape=jax.ShapeDtypeStruct((rows, holes...  3.79 us
    pallas_call x2, Pallas kernels, ladder_share(): pl.pallas_call(ladder_kernel, out_shape=jax.ShapeDtypeStruct((lad_count,...  3.11 us
    pallas_call x1, Pallas kernels, pack(): pl.pallas_call(functools.partial(rest_kernel, HALVES, near), out_shape=[b...  2.3 us
  transfers between devices with their start and end apart: 14, of which 4 were waited for; matrix products, arithmetic and copies ran while one was open for 1% of the time, Pallas kernels for 19%

profile of v2, /device:TPU:0, one launch (start us, length us, event | category | flops | bytes accessed | tf_op | source)
XLA Modules:
  0.0 80.5 jit_solution(5086551907408666999)
XLA Ops:
  0.0 0.1 broadcast_multiply_fusion
  0.1 1.1 %copy-done.2 = bf16[1,768,512]{2,1,0:T(8,128)(2,1)S(1)} copy-done((bf16[1,768,512]{2,1,0:T(8,128)(2,1)S(1)}, bf16[1,768,512]{2,1,0:T(8,128)(2,1)}, u32[]{:S(2)}) %copy-start.2) | copy-done | bytes 786456
  1.2 0.7 copy-done.12
  1.9 2.0 %pack_first.1 = (s32[1,768]{1,0:T(1,128)S(1)}, bf16[384,256]{1,0:T(8,128)(2,1)}, bf16[384,256]{1,0:T(8,128)(2,1)}) custom-call(s32[4]{0:T(128)S(1)} %get-tuple-element.41.off_ref, s32[1,768]{1,0:T(1,128)S(1)} %bitcast.30, bf16[768,512]{1,0:T(8,128)(2,1)S(1)} %bitcast.21), custom_call_target="tpu_custom_call" | custom-call | tf_op jit(solution)/shard_map/pack_first/pallas_call | solution.py:72
  3.9 1.1 %copy-done.3 = bf16[1,768,512]{2,1,0:T(8,128)(2,1)S(1)} copy-done((bf16[1,768,512]{2,1,0:T(8,128)(2,1)S(1)}, bf16[1,768,512]{2,1,0:T(8,128)(2,1)}, u32[]{:S(2)}) %copy-start.3) | copy-done | bytes 786456
  5.0 2.3 %pack_rest.1 = (bf16[384,256]{1,0:T(8,128)(2,1)S(1)}, bf16[384,256]{1,0:T(8,128)(2,1)S(1)}, bf16[384,256]{1,0:T(8,128)(2,1)}, bf16[384,256]{1,0:T(8,128)(2,1)}, ...) custom-call(s32[4]{0:T(128)S(1)} %get-tuple-element.41.off_ref, s32[1,768]{1,0:T(1,128)S(1)} %get-tuple-element.23.target_ref, ...), custom_call_target="tpu_custom_call" | custom-call | tf_op jit(solution)/shard_map/pack_rest/pallas_call | solution.py:84
  7.3 0.7 copy-done.13
  8.0 3.0 %collective-permute-start.8 = (bf16[384,256]{1,0:T(8,128)(2,1)}, bf16[384,256]{1,0:T(8,128)(2,1)}, u32[]{:S(2)}, u32[]{:S(2)}) collective-permute-start(bf16[384,256]{1,0:T(8,128)(2,1)} %get-tuple-element.25), channel_id=1, source_target_pairs={{0,4},{4,0},{8,12},{12,8},{1,5},{5,1},{9,13},{13,9},{2,6},{6,2},{1... | collective-permute-start | bytes 589832 | tf_op jit(solution)/shard_map/ppermute | solution.py:284
  11.0 2.5 %collective-permute-start.10 = (bf16[384,256]{1,0:T(8,128)(2,1)}, bf16[384,256]{1,0:T(8,128)(2,1)}, u32[]{:S(2)}, u32[]{:S(2)}) collective-permute-start(bf16[384,256]{1,0:T(8,128)(2,1)} %get-tuple-element.27), channel_id=1, source_target_pairs={{0,12},{4,8},{8,4},{12,0},{1,13},{5,9},{9,5},{13,1},{2,14},{6,10},... | collective-permute-start | bytes 589832 | tf_op jit(solution)/shard_map/ppermute | solution.py:284
  13.5 0.1 collective-permute-start.9
  13.6 1.8 %collective-permute-start.2 = (bf16[384,256]{1,0:T(8,128)(2,1)}, bf16[384,256]{1,0:T(8,128)(2,1)}, u32[]{:S(2)}, u32[]{:S(2)}) collective-permute-start(bf16[384,256]{1,0:T(8,128)(2,1)} %get-tuple-element.29), channel_id=1, source_target_pairs={{0,4},{4,0},{8,12},{12,8},{1,5},{5,1},{9,13},{13,9},{2,6},{6,2},{1... | collective-permute-start | bytes 589832 | tf_op jit(solution)/shard_map/ppermute | solution.py:284
  15.4 1.7 %collective-permute-start.3 = (bf16[384,256]{1,0:T(8,128)(2,1)}, bf16[384,256]{1,0:T(8,128)(2,1)}, u32[]{:S(2)}, u32[]{:S(2)}) collective-permute-start(bf16[384,256]{1,0:T(8,128)(2,1)} %get-tuple-element.30), channel_id=1, source_target_pairs={{0,8},{4,12},{8,0},{12,4},{1,9},{5,13},{9,1},{13,5},{2,10},{6,14},... | collective-permute-start | bytes 589832 | tf_op jit(solution)/shard_map/ppermute | solution.py:284
  17.1 0.0 copy-done.4
  17.1 2.3 %copy-done = bf16[1,3072,768]{2,1,0:T(8,128)(2,1)S(1)} copy-done((bf16[1,3072,768]{2,1,0:T(8,128)(2,1)S(1)}, bf16[1,3072,768]{2,1,0:T(8,128)(2,1)}, u32[]{:S(2)}) %copy-start) | copy-done | bytes 4718616
  19.4 1.6 %ladder_share.2 = bf16[2,768,512]{2,1,0:T(8,128)(2,1)S(1)} custom-call(s32[1]{0:T(128)} %bitcast.7.share_ref, bf16[3072,768]{1,0:T(8,128)(2,1)S(1)} %bitcast.19, bf16[768,512]{1,0:T(8,128)(2,1)S(1)} %bitcast.23), custom_call_target="tpu_custom_call" | custom-call | tf_op jit(solution)/shard_map/ladder_share/pallas_call | solution.py:130
  21.0 0.0 copy-start.8
  21.0 0.8 copy-done.1
  21.8 1.6 %ladder_share.3 = bf16[2,768,512]{2,1,0:T(8,128)(2,1)S(1)} custom-call(s32[1]{0:T(128)} %bitcast.9.share_ref, bf16[3072,768]{1,0:T(8,128)(2,1)S(1)} %bitcast.20, bf16[768,512]{1,0:T(8,128)(2,1)S(1)} %bitcast.24), custom_call_target="tpu_custom_call" | custom-call | tf_op jit(solution)/shard_map/ladder_share/pallas_call | solution.py:130
  23.3 0.0 copy-done.8
  23.3 0.0 copy-start.5
  23.3 1.2 %copy-done.5 = bf16[2,768,512]{2,1,0:T(8,128)(2,1)} copy-done((bf16[2,768,512]{2,1,0:T(8,128)(2,1)}, bf16[2,768,512]{2,1,0:T(8,128)(2,1)S(1)}, u32[]{:S(2)}) %copy-start.5) | copy-done | bytes 1572888
  24.5 0.2 copy.10.target_ref
  24.7 0.0 copy-start.10
  24.7 1.1 %unpack_matrix.1.pick_ref = bf16[768,1536]{1,0:T(8,128)(2,1)S(1)} custom-call(s32[4]{0:T(128)S(1)} %get-tuple-element.41.off_ref, s32[768,1]{1,0:T(8,128)S(1)} %copy.10.target_ref), custom_call_target="tpu_custom_call" | custom-call | tf_op jit(solution)/shard_map/unpack_matrix/pallas_call | solution.py:113
  25.8 0.0 copy-done.16
  25.8 0.2 copy.12.part_ref
  26.0 0.0 copy-done.10
  26.0 0.0 copy-start.7
  26.1 2.3 %copy-done.7 = bf16[1,1,1536,1536]{3,2,1,0:T(8,128)(2,1)S(1)} copy-done((bf16[1,1,1536,1536]{3,2,1,0:T(8,128)(2,1)S(1)}, bf16[1,1,1536,1536]{3,2,1,0:T(8,128)(2,1)}, u32[]{:S(2)}) %copy-start.7) | copy-done | bytes 4718616
  28.4 4.4 %cycle_operator.1.operator_ref = bf16[1536,1536]{1,0:T(8,128)(2,1)S(1)} custom-call(s32[4]{0:T(128)S(1)} %get-tuple-element.42.block_index, bf16[1536,1536]{1,0:T(8,128)(2,1)S(1)} %bitcast.25, bf16[12,128,128]{2,1,0:T(8,128)(2,1)S(1)} %bitcast.26), custom_call_target="tpu_custom_call" | custom-call | tf_op jit(solution)/shard_map/cycle_operator/pallas_call | solution.py:172
  32.8 0.0 copy-start.6
  32.8 0.0 collective-permute-done.8.refs_1_
  32.8 1.0 %collective-permute-start.4 = (bf16[384,256]{1,0:T(8,128)(2,1)S(1)}, bf16[384,256]{1,0:T(8,128)(2,1)S(1)}, u32[]{:S(2)}, u32[]{:S(2)}) collective-permute-start(bf16[384,256]{1,0:T(8,128)(2,1)S(1)} %get-tuple-element.31), channel_id=1, source_target_pairs={{0,12},{4,8},{8,4},{12,0},{1,13},{5,9},{9,5},{13,1},{2,14},{6,10},... | collective-permute-start | bytes 589832 | tf_op jit(solution)/shard_map/ppermute | solution.py:284
  33.8 0.0 collective-permute-done.10.refs_3_
  33.8 0.0 copy-done.9
  33.8 0.0 collective-permute-start
  33.8 7.1 %collective-permute-done.9.refs_2_ = bf16[384,256]{1,0:T(8,128)(2,1)} collective-permute-done((bf16[384,256]{1,0:T(8,128)(2,1)}, bf16[384,256]{1,0:T(8,128)(2,1)}, u32[]{:S(2)}, u32[]{:S(2)}) %collective-permute-start.9) | collective-permute-done | bytes 196640 | tf_op jit(solution)/shard_map/ppermute | solution.py:284
  40.8 0.0 copy-done.14
  40.8 2.5 %apply_cycle.3 = (bf16[384,256]{1,0:T(8,128)(2,1)S(1)}, bf16[384,256]{1,0:T(8,128)(2,1)S(1)}, bf16[384,256]{1,0:T(8,128)(2,1)S(1)}, bf16[384,256]{1,0:T(8,128)(2,1)S(1)}) custom-call(bf16[1536,1536]{1,0:T(8,128)(2,1)S(1)} %cycle_operator.1.operator_ref, bf16[384,256]{1,0:T(8,128)(2,1)S(1)} %copy-done.14, bf16[384,256]{1,0:T(8,128)(2,1)} %collective-permute-done.8.refs_1_, ...), custom_call_target="tpu_custom_call" | custom-call | flops 30000001024 | bytes 1000000 | tf_op jit(solution)/shard_map/apply_cycle/pallas_call | solution.py:204
  43.3 0.1 collective-permute-start.11
  43.5 0.0 collective-permute-done
  43.5 3.5 %collective-permute-start.12 = (bf16[384,256]{1,0:T(8,128)(2,1)S(1)}, bf16[384,256]{1,0:T(8,128)(2,1)S(1)}, u32[]{:S(2)}, u32[]{:S(2)}) collective-permute-start(bf16[384,256]{1,0:T(8,128)(2,1)S(1)} %get-tuple-element.39), channel_id=1, source_target_pairs={{0,8},{4,12},{8,0},{12,4},{1,9},{5,13},{9,1},{13,5},{2,10},{6,14},... | collective-permute-start | bytes 589832 | tf_op jit(solution)/shard_map/ppermute | solution.py:284
  46.9 0.0 copy-done.6
  46.9 0.2 fusion
  47.2 0.0 collective-permute-done.2.refs_1_
  47.2 0.0 copy-start.15
  47.2 0.9 %collective-permute-start.13 = (bf16[384,256]{1,0:T(8,128)(2,1)S(1)}, bf16[384,256]{1,0:T(8,128)(2,1)S(1)}, u32[]{:S(2)}, u32[]{:S(2)}) collective-permute-start(bf16[384,256]{1,0:T(8,128)(2,1)S(1)} %get-tuple-element.40), channel_id=1, source_target_pairs={{0,12},{4,8},{8,4},{12,0},{1,13},{5,9},{9,5},{13,1},{2,14},{6,10},... | collective-permute-start | bytes 589832 | tf_op jit(solution)/shard_map/ppermute | solution.py:284
  48.1 1.1 %collective-permute-done.3.refs_2_ = bf16[384,256]{1,0:T(8,128)(2,1)} collective-permute-done((bf16[384,256]{1,0:T(8,128)(2,1)}, bf16[384,256]{1,0:T(8,128)(2,1)}, u32[]{:S(2)}, u32[]{:S(2)}) %collective-permute-start.3) | collective-permute-done | bytes 196640 | tf_op jit(solution)/shard_map/ppermute | solution.py:284
  49.2 1.5 %collective-permute-start.1 = (bf16[768,512]{1,0:T(8,128)(2,1)S(1)}, bf16[768,512]{1,0:T(8,128)(2,1)S(1)}, u32[]{:S(2)}, u32[]{:S(2)}) collective-permute-start(bf16[768,512]{1,0:T(8,128)(2,1)S(1)} %fusion), channel_id=1, source_target_pairs={{0,2},{2,0},{1,3},{3,1},{4,6},{6,4},{5,7},{7,5},{8,10},{10,8},{9,1... | collective-permute-start | bytes 2359304 | tf_op jit(solution)/shard_map/ppermute | solution.py:309
  50.7 0.0 collective-permute-done.4.refs_3_
  50.7 2.4 %apply_cycle.2 = (bf16[384,256]{1,0:T(8,128)(2,1)S(1)}, bf16[384,256]{1,0:T(8,128)(2,1)S(1)}, bf16[384,256]{1,0:T(8,128)(2,1)S(1)}, bf16[384,256]{1,0:T(8,128)(2,1)S(1)}) custom-call(bf16[1536,1536]{1,0:T(8,128)(2,1)S(1)} %cycle_operator.1.operator_ref, bf16[384,256]{1,0:T(8,128)(2,1)S(1)} %get-tuple-element.28.refs_0_, ...), custom_call_target="tpu_custom_call" | custom-call | flops 30000001024 | bytes 1000000 | tf_op jit(solution)/shard_map/apply_cycle/pallas_call | solution.py:204
  53.1 7.5 %collective-permute-start.5 = (bf16[384,256]{1,0:T(8,128)(2,1)S(1)}, bf16[384,256]{1,0:T(8,128)(2,1)S(1)}, u32[]{:S(2)}, u32[]{:S(2)}) collective-permute-start(bf16[384,256]{1,0:T(8,128)(2,1)S(1)} %get-tuple-element.34), channel_id=1, source_target_pairs={{0,4},{4,0},{8,12},{12,8},{1,5},{5,1},{9,13},{13,9},{2,6},{6,2},{1... | collective-permute-start | bytes 589832 | tf_op jit(solution)/shard_map/ppermute | solution.py:284
  60.6 0.0 collective-permute-done.11.refs_1_
  60.6 1.6 %collective-permute-start.6 = (bf16[384,256]{1,0:T(8,128)(2,1)S(1)}, bf16[384,256]{1,0:T(8,128)(2,1)S(1)}, u32[]{:S(2)}, u32[]{:S(2)}) collective-permute-start(bf16[384,256]{1,0:T(8,128)(2,1)S(1)} %get-tuple-element.35), channel_id=1, source_target_pairs={{0,8},{4,12},{8,0},{12,4},{1,9},{5,13},{9,1},{13,5},{2,10},{6,14},... | collective-permute-start | bytes 589832 | tf_op jit(solution)/shard_map/ppermute | solution.py:284
  62.2 0.1 collective-permute-done.1
  62.3 6.5 %collective-permute-start.7 = (bf16[384,256]{1,0:T(8,128)(2,1)S(1)}, bf16[384,256]{1,0:T(8,128)(2,1)S(1)}, u32[]{:S(2)}, u32[]{:S(2)}) collective-permute-start(bf16[384,256]{1,0:T(8,128)(2,1)S(1)} %get-tuple-element.36), channel_id=1, source_target_pairs={{0,12},{4,8},{8,4},{12,0},{1,13},{5,9},{9,5},{13,1},{2,14},{6,10},... | collective-permute-start | bytes 589832 | tf_op jit(solution)/shard_map/ppermute | solution.py:284
  68.8 0.4 bitcast_add_fusion.base_ref
  69.2 0.0 collective-permute-done.12.refs_2_
  69.2 0.0 collective-permute-done.13.refs_3_
  69.3 1.9 %finish.2.refs_4_ = bf16[768,512]{1,0:T(8,128)(2,1)} custom-call(bf16[768,1536]{1,0:T(8,128)(2,1)S(1)} %unpack_matrix.1.pick_ref, f32[768,512]{1,0:T(8,128)S(1)} %bitcast_add_fusion.base_ref, f32[768,1]{1,0:T(8,128)S(1)} %copy.12.part_ref, f32[1,512]{1,0:T(1,128)S(1)} %bitcast.28, bf16[384,256]{1,0:T(8,128)(2,1)S(1)} %get-tuple-element.37.refs_0_, ...), custom_call_target="tpu_custom_call" | custom-call | tf_op jit(solution)/shard_map/finish/pallas_call | solution.py:244
  71.1 0.0 collective-permute-done.5.refs_1_
  71.1 7.5 %collective-permute-done.6.refs_2_ = bf16[384,256]{1,0:T(8,128)(2,1)S(1)} collective-permute-done((bf16[384,256]{1,0:T(8,128)(2,1)S(1)}, bf16[384,256]{1,0:T(8,128)(2,1)S(1)}, u32[]{:S(2)}, u32[]{:S(2)}) %collective-permute-start.6) | collective-permute-done | bytes 196640 | tf_op jit(solution)/shard_map/ppermute | solution.py:284
  78.6 0.0 collective-permute-done.7.refs_3_
  78.6 1.9 %finish.3 = bf16[768,512]{1,0:T(8,128)(2,1)} custom-call(bf16[768,1536]{1,0:T(8,128)(2,1)S(1)} %unpack_matrix.1.pick_ref, f32[768,512]{1,0:T(8,128)S(1)} %bitcast_add_fusion.base_ref, f32[768,1]{1,0:T(8,128)S(1)} %copy.12.part_ref, f32[1,512]{1,0:T(1,128)S(1)} %bitcast.29, ...), custom_call_target="tpu_custom_call", output_to_operand_aliasing={{}: (8, {})} | custom-call | tf_op jit(solution)/shard_map/finish/pallas_call | solution.py:244
  (13 shorter events, 0.0 us)
Async XLA Ops:
  0.1 1.1 %copy-start.2 = (bf16[1,768,512]{2,1,0:T(8,128)(2,1)S(1)}, bf16[1,768,512]{2,1,0:T(8,128)(2,1)}, u32[]{:S(2)}) copy-start(bf16[1,768,512]{2,1,0:T(8,128)(2,1)} %param.8) | copy-start | bytes 2359300
  1.2 0.7 copy-start.12
  1.9 15.2 %copy-start.4 = (bf16[1,768,512]{2,1,0:T(8,128)(2,1)S(1)}, bf16[1,768,512]{2,1,0:T(8,128)(2,1)}, u32[]{:S(2)}) copy-start(bf16[1,768,512]{2,1,0:T(8,128)(2,1)} %param.8) | copy-start | bytes 2359300
  3.9 1.1 %copy-start.3 = (bf16[1,768,512]{2,1,0:T(8,128)(2,1)S(1)}, bf16[1,768,512]{2,1,0:T(8,128)(2,1)}, u32[]{:S(2)}) copy-start(bf16[1,768,512]{2,1,0:T(8,128)(2,1)} %param.8) | copy-start | bytes 2359300
  7.3 0.7 copy-start.13
  8.0 24.8 %collective-permute-start.8 = (bf16[384,256]{1,0:T(8,128)(2,1)}, bf16[384,256]{1,0:T(8,128)(2,1)}, u32[]{:S(2)}, u32[]{:S(2)}) collective-permute-start(bf16[384,256]{1,0:T(8,128)(2,1)} %get-tuple-element.25), channel_id=1, source_target_pairs={{0,4},{4,0},{8,12},{12,8},{1,5},{5,1},{9,13},{13,9},{2,6},{6,2},{1... | collective-permute-start | bytes 589832 | tf_op jit(solution)/shard_map/ppermute | solution.py:284
  11.0 22.7 %collective-permute-start.10 = (bf16[384,256]{1,0:T(8,128)(2,1)}, bf16[384,256]{1,0:T(8,128)(2,1)}, u32[]{:S(2)}, u32[]{:S(2)}) collective-permute-start(bf16[384,256]{1,0:T(8,128)(2,1)} %get-tuple-element.27), channel_id=1, source_target_pairs={{0,12},{4,8},{8,4},{12,0},{1,13},{5,9},{9,5},{13,1},{2,14},{6,10},... | collective-permute-start | bytes 589832 | tf_op jit(solution)/shard_map/ppermute | solution.py:284
  13.5 27.4 %collective-permute-start.9 = (bf16[384,256]{1,0:T(8,128)(2,1)}, bf16[384,256]{1,0:T(8,128)(2,1)}, u32[]{:S(2)}, u32[]{:S(2)}) collective-permute-start(bf16[384,256]{1,0:T(8,128)(2,1)} %get-tuple-element.26), channel_id=1, source_target_pairs={{0,8},{4,12},{8,0},{12,4},{1,9},{5,13},{9,1},{13,5},{2,10},{6,14},... | collective-permute-start | bytes 589832 | tf_op jit(solution)/shard_map/ppermute | solution.py:284
  13.6 33.6 %collective-permute-start.2 = (bf16[384,256]{1,0:T(8,128)(2,1)}, bf16[384,256]{1,0:T(8,128)(2,1)}, u32[]{:S(2)}, u32[]{:S(2)}) collective-permute-start(bf16[384,256]{1,0:T(8,128)(2,1)} %get-tuple-element.29), channel_id=1, source_target_pairs={{0,4},{4,0},{8,12},{12,8},{1,5},{5,1},{9,13},{13,9},{2,6},{6,2},{1... | collective-permute-start | bytes 589832 | tf_op jit(solution)/shard_map/ppermute | solution.py:284
  15.4 33.8 %collective-permute-start.3 = (bf16[384,256]{1,0:T(8,128)(2,1)}, bf16[384,256]{1,0:T(8,128)(2,1)}, u32[]{:S(2)}, u32[]{:S(2)}) collective-permute-start(bf16[384,256]{1,0:T(8,128)(2,1)} %get-tuple-element.30), channel_id=1, source_target_pairs={{0,8},{4,12},{8,0},{12,4},{1,9},{5,13},{9,1},{13,5},{2,10},{6,14},... | collective-permute-start | bytes 589832 | tf_op jit(solution)/shard_map/ppermute | solution.py:284
  17.1 2.3 %copy-start = (bf16[1,3072,768]{2,1,0:T(8,128)(2,1)S(1)}, bf16[1,3072,768]{2,1,0:T(8,128)(2,1)}, u32[]{:S(2)}) copy-start(bf16[1,3072,768]{2,1,0:T(8,128)(2,1)} %param.11) | copy-start | bytes 14155780
  19.4 2.3 %copy-start.1 = (bf16[1,3072,768]{2,1,0:T(8,128)(2,1)S(1)}, bf16[1,3072,768]{2,1,0:T(8,128)(2,1)}, u32[]{:S(2)}) copy-start(bf16[1,3072,768]{2,1,0:T(8,128)(2,1)} %param.11) | copy-start | bytes 14155780
  21.0 2.3 %copy-start.8 = (bf16[2,768,512]{2,1,0:T(8,128)(2,1)}, bf16[2,768,512]{2,1,0:T(8,128)(2,1)S(1)}, u32[]{:S(2)}) copy-start(bf16[2,768,512]{2,1,0:T(8,128)(2,1)S(1)} %ladder_share.2) | copy-start | bytes 4718596
  23.3 1.2 %copy-start.5 = (bf16[2,768,512]{2,1,0:T(8,128)(2,1)}, bf16[2,768,512]{2,1,0:T(8,128)(2,1)S(1)}, u32[]{:S(2)}) copy-start(bf16[2,768,512]{2,1,0:T(8,128)(2,1)S(1)} %ladder_share.3) | copy-start | bytes 4718596
  24.5 1.3 %copy-start.16 = (f32[1,768]{1,0:T(1,128)S(1)}, f32[1,768]{1,0:T(1,128)}, u32[]{:S(2)}) copy-start(f32[1,768]{1,0:T(1,128)} %param.14) | copy-start | bytes 9220
  24.7 1.3 %copy-start.10 = (bf16[1,1,12,128,128]{4,3,2,1,0:T(8,128)(2,1)S(1)}, bf16[1,1,12,128,128]{4,3,2,1,0:T(8,128)(2,1)}, u32[]{:S(2)}) copy-start(bf16[1,1,12,128,128]{4,3,2,1,0:T(8,128)(2,1)} %param.13) | copy-start | bytes 1179652
  26.0 2.3 %copy-start.7 = (bf16[1,1,1536,1536]{3,2,1,0:T(8,128)(2,1)S(1)}, bf16[1,1,1536,1536]{3,2,1,0:T(8,128)(2,1)}, u32[]{:S(2)}) copy-start(bf16[1,1,1536,1536]{3,2,1,0:T(8,128)(2,1)} %param.12) | copy-start | bytes 14155780
  28.4 5.4 %copy-start.9 = (bf16[2,768,512]{2,1,0:T(8,128)(2,1)S(1)}, bf16[2,768,512]{2,1,0:T(8,128)(2,1)}, u32[]{:S(2)}) copy-start(bf16[2,768,512]{2,1,0:T(8,128)(2,1)} %copy-done.8) | copy-start | bytes 4718596
  28.4 12.5 %copy-start.14 = (bf16[384,256]{1,0:T(8,128)(2,1)S(1)}, bf16[384,256]{1,0:T(8,128)(2,1)}, u32[]{:S(2)}) copy-start(bf16[384,256]{1,0:T(8,128)(2,1)} %copy-done.13) | copy-start | bytes 589828
  32.8 14.2 %copy-start.6 = (bf16[2,768,512]{2,1,0:T(8,128)(2,1)S(1)}, bf16[2,768,512]{2,1,0:T(8,128)(2,1)}, u32[]{:S(2)}) copy-start(bf16[2,768,512]{2,1,0:T(8,128)(2,1)} %copy-done.5) | copy-start | bytes 4718596
  32.8 17.9 %collective-permute-start.4 = (bf16[384,256]{1,0:T(8,128)(2,1)S(1)}, bf16[384,256]{1,0:T(8,128)(2,1)S(1)}, u32[]{:S(2)}, u32[]{:S(2)}) collective-permute-start(bf16[384,256]{1,0:T(8,128)(2,1)S(1)} %get-tuple-element.31), channel_id=1, source_target_pairs={{0,12},{4,8},{8,4},{12,0},{1,13},{5,9},{9,5},{13,1},{2,14},{6,10},... | collective-permute-start | bytes 589832 | tf_op jit(solution)/shard_map/ppermute | solution.py:284
  33.8 9.7 %collective-permute-start = (bf16[2,768,512]{2,1,0:T(8,128)(2,1)S(1)}, bf16[2,768,512]{2,1,0:T(8,128)(2,1)S(1)}, u32[]{:S(2)}, u32[]{:S(2)}) collective-permute-start(bf16[2,768,512]{2,1,0:T(8,128)(2,1)S(1)} %copy-done.9), channel_id=1, source_target_pairs={{0,1},{1,0},{2,3},{3,2},{4,5},{5,4},{6,7},{7,6},{8,9},{9,8},{10,11... | collective-permute-start | bytes 4718600 | tf_op jit(solution)/shard_map/ppermute | solution.py:298
  43.3 17.2 %collective-permute-start.11 = (bf16[384,256]{1,0:T(8,128)(2,1)S(1)}, bf16[384,256]{1,0:T(8,128)(2,1)S(1)}, u32[]{:S(2)}, u32[]{:S(2)}) collective-permute-start(bf16[384,256]{1,0:T(8,128)(2,1)S(1)} %get-tuple-element.38), channel_id=1, source_target_pairs={{0,4},{4,0},{8,12},{12,8},{1,5},{5,1},{9,13},{13,9},{2,6},{6,2},{1... | collective-permute-start | bytes 589832 | tf_op jit(solution)/shard_map/ppermute | solution.py:284
  43.5 25.8 %collective-permute-start.12 = (bf16[384,256]{1,0:T(8,128)(2,1)S(1)}, bf16[384,256]{1,0:T(8,128)(2,1)S(1)}, u32[]{:S(2)}, u32[]{:S(2)}) collective-permute-start(bf16[384,256]{1,0:T(8,128)(2,1)S(1)} %get-tuple-element.39), channel_id=1, source_target_pairs={{0,8},{4,12},{8,0},{12,4},{1,9},{5,13},{9,1},{13,5},{2,10},{6,14},... | collective-permute-start | bytes 589832 | tf_op jit(solution)/shard_map/ppermute | solution.py:284
  47.2 21.6 %copy-start.15 = (bf16[1,768,512]{2,1,0:T(8,128)(2,1)S(1)}, bf16[1,768,512]{2,1,0:T(8,128)(2,1)}, u32[]{:S(2)}) copy-start(bf16[1,768,512]{2,1,0:T(8,128)(2,1)} %param.9) | copy-start | bytes 2359300
  47.2 22.1 %collective-permute-start.13 = (bf16[384,256]{1,0:T(8,128)(2,1)S(1)}, bf16[384,256]{1,0:T(8,128)(2,1)S(1)}, u32[]{:S(2)}, u32[]{:S(2)}) collective-permute-start(bf16[384,256]{1,0:T(8,128)(2,1)S(1)} %get-tuple-element.40), channel_id=1, source_target_pairs={{0,12},{4,8},{8,4},{12,0},{1,13},{5,9},{9,5},{13,1},{2,14},{6,10},... | collective-permute-start | bytes 589832 | tf_op jit(solution)/shard_map/ppermute | solution.py:284
  49.2 13.0 %collective-permute-start.1 = (bf16[768,512]{1,0:T(8,128)(2,1)S(1)}, bf16[768,512]{1,0:T(8,128)(2,1)S(1)}, u32[]{:S(2)}, u32[]{:S(2)}) collective-permute-start(bf16[768,512]{1,0:T(8,128)(2,1)S(1)} %fusion), channel_id=1, source_target_pairs={{0,2},{2,0},{1,3},{3,1},{4,6},{6,4},{5,7},{7,5},{8,10},{10,8},{9,1... | collective-permute-start | bytes 2359304 | tf_op jit(solution)/shard_map/ppermute | solution.py:309
  53.1 18.0 %collective-permute-start.5 = (bf16[384,256]{1,0:T(8,128)(2,1)S(1)}, bf16[384,256]{1,0:T(8,128)(2,1)S(1)}, u32[]{:S(2)}, u32[]{:S(2)}) collective-permute-start(bf16[384,256]{1,0:T(8,128)(2,1)S(1)} %get-tuple-element.34), channel_id=1, source_target_pairs={{0,4},{4,0},{8,12},{12,8},{1,5},{5,1},{9,13},{13,9},{2,6},{6,2},{1... | collective-permute-start | bytes 589832 | tf_op jit(solution)/shard_map/ppermute | solution.py:284
  60.6 18.0 %collective-permute-start.6 = (bf16[384,256]{1,0:T(8,128)(2,1)S(1)}, bf16[384,256]{1,0:T(8,128)(2,1)S(1)}, u32[]{:S(2)}, u32[]{:S(2)}) collective-permute-start(bf16[384,256]{1,0:T(8,128)(2,1)S(1)} %get-tuple-element.35), channel_id=1, source_target_pairs={{0,8},{4,12},{8,0},{12,4},{1,9},{5,13},{9,1},{13,5},{2,10},{6,14},... | collective-permute-start | bytes 589832 | tf_op jit(solution)/shard_map/ppermute | solution.py:284
  62.3 7.0 %copy-start.11 = (f32[512]{0:T(512)S(1)}, f32[512]{0:T(512)}, u32[]{:S(2)}) copy-start(f32[512]{0:T(512)} %param.15) | copy-start | bytes 6148
  62.3 16.3 %collective-permute-start.7 = (bf16[384,256]{1,0:T(8,128)(2,1)S(1)}, bf16[384,256]{1,0:T(8,128)(2,1)S(1)}, u32[]{:S(2)}, u32[]{:S(2)}) collective-permute-start(bf16[384,256]{1,0:T(8,128)(2,1)S(1)} %get-tuple-element.36), channel_id=1, source_target_pairs={{0,12},{4,8},{8,4},{12,0},{1,13},{5,9},{9,5},{13,1},{2,14},{6,10},... | collective-permute-start | bytes 589832 | tf_op jit(solution)/shard_map/ppermute | solution.py:284

commit v3 on v2

--- a/solution.py
+++ b/solution.py
@@ -27,76 +27,70 @@
     return jnp.where(match, 1.0, 0.0).astype(BF16)
 
 
-def place_rows(offset, target, amps, block_refs):
-    slots = lax.broadcasted_iota(jnp.int32, (block_refs[0].shape[0], target.shape[1]), 0)
-    pick = selection(slots == target - offset)
-    for block_ref, columns in zip(block_refs, amps):
-        block_ref[...] = jnp.dot(pick, columns, preferred_element_type=F32).astype(BF16)
-
-
-def first_kernel(chan_count, send, off_ref, route_ref, amps_ref, target_ref, *block_refs):
+def pack_kernel(chan_count, send, off_ref, route_hbm, amps_hbm, target_ref, *refs):
+    block_refs, (route_ref, amps_ref, sems) = refs[:-3], refs[-3:]
+    rows, width = amps_ref.shape[0], amps_ref.shape[1] // HALVES
+    parts = [pl.ds(h * width, width) for h in range(HALVES)]
+    copies = [pltpu.make_async_copy(route_hbm, route_ref, sems.at[0])] + [
+        pltpu.make_async_copy(amps_hbm.at[:, part], amps_ref.at[:, part], sems.at[1 + h])
+        for h, part in enumerate(parts)
+    ]
+    for copy in copies:
+        copy.start()
+    lane = 128
+    pieces = rows // lane
+    before = selection(
+        lax.broadcasted_iota(jnp.int32, (lane, 2 * lane), 0)
+        < lax.broadcasted_iota(jnp.int32, (lane, 2 * lane), 1)
+    )
+    names = max(16, chan_count)
+    copies[0].wait()
     owners = route_ref[...]
-    rows = owners.shape[1]
-    lanes = max(16, chan_count)
-    hot = lax.broadcasted_iota(jnp.int32, (lanes, rows), 0) == owners
-    before = selection(
-        lax.broadcasted_iota(jnp.int32, (rows, rows), 0)
-        < lax.broadcasted_iota(jnp.int32, (rows, rows), 1)
+    hot = [
+        lax.broadcasted_iota(jnp.int32, (names, lane), 0) == owners[:, i * lane : (i + 1) * lane]
+        for i in range(pieces)
+    ]
+    counts = jnp.dot(
+        jnp.concatenate([selection(h) for h in hot], axis=0), before, preferred_element_type=F32
     )
-    earlier = jnp.dot(selection(hot), before, preferred_element_type=F32)
-    slot = jnp.sum(jnp.where(hot, earlier, 0.0), axis=0, keepdims=True)
-    target = owners * send + slot.astype(jnp.int32)
+    passed = jnp.zeros((names, lane), F32)
+    slots = []
+    for i in range(pieces):
+        within = counts[i * names : (i + 1) * names]
+        slots.append(jnp.sum(jnp.where(hot[i], within[:, :lane] + passed, 0.0), axis=0, keepdims=True))
+        passed = passed + within[:, lane:]
+    target = owners * send + jnp.concatenate(slots, axis=1).astype(jnp.int32)
     target_ref[...] = target
-    first = off_ref.shape[0] - len(block_refs)
-    for i, block_ref in enumerate(block_refs):
-        place_rows(off_ref[first + i], target, [amps_ref[:, : block_ref.shape[1]]], [block_ref])
-
-
-def rest_kernel(parts, skipped, off_ref, target_ref, amps_ref, *block_refs):
-    target = target_ref[...]
-    width = amps_ref.shape[1] // parts
-    columns = [amps_ref[:, pl.ds(h * width, width)] for h in range(parts)]
-    left = list(block_refs)
-    for k in range(off_ref.shape[0]):
-        wanted = columns if k < skipped else columns[1:]
-        refs, left = left[: len(wanted)], left[len(wanted) :]
-        place_rows(off_ref[k], target, wanted, refs)
+    count = off_ref.shape[0]
+    slot = lax.broadcasted_iota(jnp.int32, (block_refs[0].shape[0], rows), 0)
+    for k in reversed(range(count)):
+        pick = selection(slot == target - off_ref[k])
+        for h in range(HALVES):
+            if k == count - 1:
+                copies[1 + h].wait()
+            block_refs[k * HALVES + h][...] = jnp.dot(
+                pick, amps_ref[:, parts[h]], preferred_element_type=F32
+            ).astype(BF16)
 
 
 def pack(offsets, route_row, amps, chan_count, send, block_rows):
     rows, holes = amps.shape
     count = offsets.shape[0]
-    far = count // 2 if count > 1 else 1
-    near = count - far
     block = jax.ShapeDtypeStruct((block_rows, holes // HALVES), BF16)
     outs = pl.pallas_call(
-        functools.partial(first_kernel, chan_count, send),
-        out_shape=[jax.ShapeDtypeStruct((1, rows), jnp.int32)] + [block] * far,
-        in_specs=[whole(pltpu.SMEM), whole(), whole()],
-        out_specs=[whole()] * (1 + far),
-        compiler_params=params(),
-        cost_estimate=CHEAP,
-        name="pack_first",
+        functools.partial(pack_kernel, chan_count, send),
+        out_shape=[jax.ShapeDtypeStruct((1, rows), jnp.int32)] + [block] * (count * HALVES),
+        in_specs=[whole(pltpu.SMEM), whole(pltpu.HBM), whole(pltpu.HBM)],
+        out_specs=[whole()] * (1 + count * HALVES),
+        scratch_shapes=[
+            pltpu.VMEM((1, rows), jnp.int32),
+            pltpu.VMEM((rows, holes), BF16),
+            pltpu.SemaphoreType.DMA((1 + HALVES,)),
+        ],
+        compiler_params=params(),
+        name="pack",
     )(offsets, route_row, amps)
-    target, early = outs[0], list(outs[1:])
-    number = near * HALVES + far * (HALVES - 1)
-    late = list(
-        pl.pallas_call(
-            functools.partial(rest_kernel, HALVES, near),
-            out_shape=[block] * number,
-            in_specs=[whole(pltpu.SMEM), whole(), whole()],
-            out_specs=[whole()] * number,
-            compiler_params=params(),
-            name="pack_rest",
-        )(offsets, target, amps)
-    )
-    blocks = [[None] * count for _ in range(HALVES)]
-    for k in range(count):
-        if k >= near:
-            blocks[0][k] = early[k - near]
-        for h in range(0 if k < near else 1, HALVES):
-            blocks[h][k] = late.pop(0)
-    return target, blocks
+    return outs[0], [[outs[1 + k * HALVES + h] for k in range(count)] for h in range(HALVES)]
 
 
 def unpack_kernel(off_ref, target_ref, out_ref):
@@ -193,15 +187,15 @@
     in_refs, out_refs, block_ref = refs[:count], refs[count : 2 * count], refs[2 * count]
     block_rows = in_refs[0].shape[0]
     for j in range(count):
-        block_ref[pl.ds(j * block_rows, block_rows), :] = in_refs[j][...]
+        block_ref[pl.ds(j * block_rows, block_rows), :] = in_refs[count - 1 - j][...]
     for k in reversed(range(count)):
-        out_refs[k][...] = jnp.dot(
+        out_refs[count - 1 - k][...] = jnp.dot(
             operator_ref[pl.ds(k * block_rows, block_rows), :], block_ref[...], preferred_element_type=F32
         ).astype(BF16)
 
 
 def apply_cycle(operator, blocks):
-    return pl.pallas_call(
+    outs = pl.pallas_call(
         cycle_kernel,
         out_shape=[jax.ShapeDtypeStruct(b.shape, BF16) for b in blocks],
         in_specs=[whole()] * (1 + len(blocks)),
@@ -210,43 +204,50 @@
         compiler_params=params(),
         cost_estimate=DEAR,
         name="apply_cycle",
-    )(operator, *blocks)
-
-
-def finish_kernel(pick_ref, base_ref, part_ref, hole_ref, *refs):
-    out_ref = refs[-1]
-    count = (pick_ref.shape[1]) // refs[0].shape[0]
-    block_rows = refs[0].shape[0]
-    total = base_ref[...]
+    )(operator, *reversed(blocks))
+    return list(reversed(outs))
+
+
+def finish_kernel(half, count, tiles, pick_ref, base_ref, part_ref, hole_ref, *refs):
+    in_refs, (out_hbm, block_ref, out_ref, sems) = refs[:count], refs[-4:]
+    block_rows, width = in_refs[0].shape
+    tile = out_ref.shape[0] // tiles
+    columns = pl.ds(half * width, width)
     for k in range(count):
-        total = total + jnp.dot(
-            pick_ref[:, pl.ds(k * block_rows, block_rows)], refs[k][...], preferred_element_type=F32
-        )
-    out_ref[...] = (total / (part_ref[...] + hole_ref[...])).astype(BF16)
+        block_ref[pl.ds(k * block_rows, block_rows), :] = in_refs[count - 1 - k][...]
+    copies = []
+    for t in range(tiles):
+        at = pl.ds(t * tile, tile)
+        back = jnp.dot(pick_ref[at, :], block_ref[...], preferred_element_type=F32)
+        total = base_ref[at, columns] + back
+        out_ref[at, :] = (total / (part_ref[at, :] + hole_ref[:, columns])).astype(BF16)
+        copies.append(pltpu.make_async_copy(out_ref.at[at, :], out_hbm.at[at, columns], sems.at[t]))
+        copies[-1].start()
+    for copy in copies:
+        copy.wait()
 
 
 def finish(half, pick, base, part_column, hole_row, blocks, earlier):
     rows, holes = base.shape
-    tile = rows // 2
-    width = holes // HALVES
-    in_specs = [
-        pl.BlockSpec((tile, pick.shape[1]), lambda i: (i, 0)),
-        pl.BlockSpec((tile, width), lambda i: (i, half)),
-        pl.BlockSpec((tile, 1), lambda i: (i, 0)),
-        pl.BlockSpec((1, width), lambda i: (0, half)),
-    ] + [pl.BlockSpec(b.shape, lambda i: (0, 0)) for b in blocks]
-    operands = [pick, base, part_column, hole_row, *blocks]
+    tiles = 3
+    count, width = len(blocks), blocks[0].shape[1]
+    operands = [pick, base, part_column, hole_row, *reversed(blocks)]
+    in_specs = [whole()] * len(operands)
     aliases = {}
     if earlier is not None:
         aliases = {len(operands): 0}
         operands.append(earlier)
-        in_specs.append(pl.BlockSpec(memory_space=pl.ANY))
+        in_specs.append(whole(pltpu.HBM))
     return pl.pallas_call(
-        finish_kernel,
+        functools.partial(finish_kernel, half, count, tiles),
         out_shape=jax.ShapeDtypeStruct((rows, holes), BF16),
-        grid=(rows // tile,),
         in_specs=in_specs,
-        out_specs=pl.BlockSpec((tile, width), lambda i: (i, half)),
+        out_specs=whole(pltpu.HBM),
+        scratch_shapes=[
+            pltpu.VMEM((pick.shape[1], width), BF16),
+            pltpu.VMEM((rows, width), BF16),
+            pltpu.SemaphoreType.DMA((tiles,)),
+        ],
         input_output_aliases=aliases,
         compiler_params=params(),
         cost_estimate=CHEAP,

time: 81.6 us -> 83.5 us (1.023)
  waiting for transfers between devices: 15.8 us -> 23.3 us
  starting transfers between devices: 31.7 us -> 28.3 us
  Pallas kernels: 21.5 us -> 19.4 us
    ppermute x12, waiting for transfers between devices: 15.7 us -> 23.3 us  [exchange(): arrived[k] = lax.ppermute(blocks[k], 'chan', pairs)]
    ppermute x12, starting transfers between devices: 30.2 us -> 26.7 us  [exchange(): arrived[k] = lax.ppermute(blocks[k], 'chan', pairs)]
    pallas_call x4 -> x3, Pallas kernels: 8.05 us -> 5.94 us  [the longest x2 3.02 us: finish(): pl.pallas_call(functools.partial(finish_kernel, half, count, tiles), out_...]
    unnamed x34 -> x40, local copies, waits for them, and re-layouts: 10.3 us -> 10.9 us
  transfers between devices with their start and end apart: 14 -> 14, of which waited for: 4 -> 4; matrix products, arithmetic and copies ran while one was open for 1% -> 1% of each run, Pallas kernels for 19% -> 18%
where the time goes in v3:
time: 83.5 us; the launch traced here: 83.2 us
  starting transfers between devices  28.3 us (34%)
  waiting for transfers between devices  23.3 us (28%)
  Pallas kernels  19.4 us (23%)
  local copies, waits for them, and re-layouts  11.2 us (13%)
    ppermute x12, starting transfers between devices, exchange(): arrived[k] = lax.ppermute(blocks[k], 'chan', pairs)  26.7 us
    ppermute x12, waiting for transfers between devices, exchange(): arrived[k] = lax.ppermute(blocks[k], 'chan', pairs)  23.3 us
    unnamed x40, local copies, waits for them, and re-layouts  10.9 us
    pallas_call x2, Pallas kernels, apply_cycle(): pl.pallas_call(cycle_kernel, out_shape=[jax.ShapeDtypeStruct(b.shape, BF1...  4.89 us
    pallas_call x1, Pallas kernels, cycle_operator(): pl.pallas_call(functools.partial(operator_kernel, group), out_shape=jax.S...  4.36 us
    pallas_call x2, Pallas kernels, ladder_share(): pl.pallas_call(ladder_kernel, out_shape=jax.ShapeDtypeStruct((lad_count,...  3.11 us
    pallas_call x2, Pallas kernels, finish(): pl.pallas_call(functools.partial(finish_kernel, half, count, tiles), out_...  3.02 us
    pallas_call x1, Pallas kernels, pack(): pl.pallas_call(functools.partial(pack_kernel, chan_count, send), out_shap...  2.91 us
  transfers between devices with their start and end apart: 14, of which 4 were waited for; matrix products, arithmetic and copies ran while one was open for 1% of the time, Pallas kernels for 18%

profile of v3, /device:TPU:0, one launch (start us, length us, event | category | flops | bytes accessed | tf_op | source)
XLA Modules:
  0.0 83.2 jit_solution(7466462373598499112)
XLA Ops:
  0.0 0.1 broadcast_multiply_fusion
  0.1 1.1 %copy-done.2 = bf16[1,768,512]{2,1,0:T(8,128)(2,1)S(1)} copy-done((bf16[1,768,512]{2,1,0:T(8,128)(2,1)S(1)}, bf16[1,768,512]{2,1,0:T(8,128)(2,1)}, u32[]{:S(2)}) %copy-start.2) | copy-done | bytes 786456
  1.2 0.7 copy-done.11
  1.9 2.9 %pack.1 = (s32[1,768]{1,0:T(1,128)S(1)}, bf16[384,256]{1,0:T(8,128)(2,1)S(1)}, bf16[384,256]{1,0:T(8,128)(2,1)S(1)}, bf16[384,256]{1,0:T(8,128)(2,1)}, bf16[384,...) custom-call(s32[4]{0:T(128)S(1)} %get-tuple-element.41.off_ref, ...), custom_call_target="tpu_custom_call" | custom-call | tf_op jit(solution)/shard_map/pack/pallas_call | solution.py:80
  4.8 0.0 copy-start.12
  4.8 0.7 copy-done.12
  5.5 0.7 copy-done.14
  6.2 0.7 copy-done.16
  6.8 5.0 %collective-permute-start.8 = (bf16[384,256]{1,0:T(8,128)(2,1)}, bf16[384,256]{1,0:T(8,128)(2,1)}, u32[]{:S(2)}, u32[]{:S(2)}) collective-permute-start(bf16[384,256]{1,0:T(8,128)(2,1)} %get-tuple-element.27), channel_id=1, source_target_pairs={{0,12},{4,8},{8,4},{12,0},{1,13},{5,9},{9,5},{13,1},{2,14},{6,10},... | collective-permute-start | bytes 589832 | tf_op jit(solution)/shard_map/ppermute | solution.py:285
  11.9 0.0 collective-permute-start.9
  11.9 0.6 collective-permute-start.10
  12.4 3.8 %collective-permute-start.2 = (bf16[384,256]{1,0:T(8,128)(2,1)}, bf16[384,256]{1,0:T(8,128)(2,1)}, u32[]{:S(2)}, u32[]{:S(2)}) collective-permute-start(bf16[384,256]{1,0:T(8,128)(2,1)} %get-tuple-element.31), channel_id=1, source_target_pairs={{0,12},{4,8},{8,4},{12,0},{1,13},{5,9},{9,5},{13,1},{2,14},{6,10},... | collective-permute-start | bytes 589832 | tf_op jit(solution)/shard_map/ppermute | solution.py:285
  16.3 0.0 collective-permute-start.3
  16.3 0.2 copy.10.target_ref
  16.5 1.1 %unpack_matrix.1.pick_ref = bf16[768,1536]{1,0:T(8,128)(2,1)S(1)} custom-call(s32[4]{0:T(128)S(1)} %get-tuple-element.41.off_ref, s32[768,1]{1,0:T(8,128)S(1)} %copy.10.target_ref), custom_call_target="tpu_custom_call" | custom-call | tf_op jit(solution)/shard_map/unpack_matrix/pallas_call | solution.py:107
  17.6 0.0 copy-done.3
  17.6 0.0 copy-start
  17.6 2.3 %copy-done = bf16[1,3072,768]{2,1,0:T(8,128)(2,1)S(1)} copy-done((bf16[1,3072,768]{2,1,0:T(8,128)(2,1)S(1)}, bf16[1,3072,768]{2,1,0:T(8,128)(2,1)}, u32[]{:S(2)}) %copy-start) | copy-done | bytes 4718616
  19.9 1.6 %ladder_share.3 = bf16[2,768,512]{2,1,0:T(8,128)(2,1)S(1)} custom-call(s32[1]{0:T(128)} %bitcast.9.share_ref, bf16[3072,768]{1,0:T(8,128)(2,1)S(1)} %bitcast.19, bf16[768,512]{1,0:T(8,128)(2,1)S(1)} %bitcast.22), custom_call_target="tpu_custom_call" | custom-call | tf_op jit(solution)/shard_map/ladder_share/pallas_call | solution.py:124
  21.5 0.0 copy-start.4
  21.5 1.2 %copy-done.4 = bf16[2,768,512]{2,1,0:T(8,128)(2,1)} copy-done((bf16[2,768,512]{2,1,0:T(8,128)(2,1)}, bf16[2,768,512]{2,1,0:T(8,128)(2,1)S(1)}, u32[]{:S(2)}) %copy-start.4) | copy-done | bytes 1572888
  22.7 0.0 copy-done.1
  22.7 1.6 %ladder_share.2 = bf16[2,768,512]{2,1,0:T(8,128)(2,1)S(1)} custom-call(s32[1]{0:T(128)} %bitcast.7.share_ref, bf16[3072,768]{1,0:T(8,128)(2,1)S(1)} %bitcast.20, bf16[768,512]{1,0:T(8,128)(2,1)S(1)} %bitcast.23), custom_call_target="tpu_custom_call" | custom-call | tf_op jit(solution)/shard_map/ladder_share/pallas_call | solution.py:124
  24.3 0.0 copy-start.7
  24.3 1.1 %copy-done.7 = bf16[2,768,512]{2,1,0:T(8,128)(2,1)} copy-done((bf16[2,768,512]{2,1,0:T(8,128)(2,1)}, bf16[2,768,512]{2,1,0:T(8,128)(2,1)S(1)}, u32[]{:S(2)}) %copy-start.7) | copy-done | bytes 1572888
  25.4 0.0 copy-done.19
  25.4 0.2 copy.12.part_ref
  25.6 0.0 copy-start.6
  25.6 2.3 %copy-done.6 = bf16[1,1,1536,1536]{3,2,1,0:T(8,128)(2,1)S(1)} copy-done((bf16[1,1,1536,1536]{3,2,1,0:T(8,128)(2,1)S(1)}, bf16[1,1,1536,1536]{3,2,1,0:T(8,128)(2,1)}, u32[]{:S(2)}) %copy-start.6) | copy-done | bytes 4718616
  28.0 4.4 %cycle_operator.1.operator_ref = bf16[1536,1536]{1,0:T(8,128)(2,1)S(1)} custom-call(s32[4]{0:T(128)S(1)} %get-tuple-element.42.block_index, bf16[1536,1536]{1,0:T(8,128)(2,1)S(1)} %bitcast.24, bf16[12,128,128]{2,1,0:T(8,128)(2,1)S(1)} %bitcast.25), custom_call_target="tpu_custom_call" | custom-call | tf_op jit(solution)/shard_map/cycle_operator/pallas_call | solution.py:166
  32.3 0.0 collective-permute-done.8.refs_0_
  32.4 0.0 copy-done.15
  32.4 0.6 collective-permute-start.4
  33.0 5.3 %collective-permute-done.9.refs_1_ = bf16[384,256]{1,0:T(8,128)(2,1)} collective-permute-done((bf16[384,256]{1,0:T(8,128)(2,1)}, bf16[384,256]{1,0:T(8,128)(2,1)}, u32[]{:S(2)}, u32[]{:S(2)}) %collective-permute-start.9) | collective-permute-done | bytes 196640 | tf_op jit(solution)/shard_map/ppermute | solution.py:285
  38.3 0.0 copy-done.8
  38.3 0.0 collective-permute-start
  38.3 0.0 collective-permute-done.10.refs_2_
  38.3 2.5 %apply_cycle.3 = (bf16[384,256]{1,0:T(8,128)(2,1)S(1)}, bf16[384,256]{1,0:T(8,128)(2,1)S(1)}, bf16[384,256]{1,0:T(8,128)(2,1)S(1)}, bf16[384,256]{1,0:T(8,128)(2,1)S(1)}) custom-call(bf16[1536,1536]{1,0:T(8,128)(2,1)S(1)} %cycle_operator.1.operator_ref, bf16[384,256]{1,0:T(8,128)(2,1)} %collective-permute-done.8.refs_0_, ...), custom_call_target="tpu_custom_call" | custom-call | flops 30000001024 | bytes 1000000 | tf_op jit(solution)/shard_map/apply_cycle/pallas_call | solution.py:198
  40.8 0.0 copy-start.13
  40.9 2.7 %collective-permute-start.11 = (bf16[384,256]{1,0:T(8,128)(2,1)S(1)}, bf16[384,256]{1,0:T(8,128)(2,1)S(1)}, u32[]{:S(2)}, u32[]{:S(2)}) collective-permute-start(bf16[384,256]{1,0:T(8,128)(2,1)S(1)} %get-tuple-element.37), channel_id=1, source_target_pairs={{0,12},{4,8},{8,4},{12,0},{1,13},{5,9},{9,5},{13,1},{2,14},{6,10},... | collective-permute-start | bytes 589832 | tf_op jit(solution)/shard_map/ppermute | solution.py:285
  43.5 0.0 collective-permute-done
  43.5 0.2 fusion
  43.8 0.0 copy-start.18
  43.8 1.6 %collective-permute-start.1 = (bf16[768,512]{1,0:T(8,128)(2,1)S(1)}, bf16[768,512]{1,0:T(8,128)(2,1)S(1)}, u32[]{:S(2)}, u32[]{:S(2)}) collective-permute-start(bf16[768,512]{1,0:T(8,128)(2,1)S(1)} %fusion), channel_id=1, source_target_pairs={{0,2},{2,0},{1,3},{3,1},{4,6},{6,4},{5,7},{7,5},{8,10},{10,8},{9,1... | collective-permute-start | bytes 2359304 | tf_op jit(solution)/shard_map/ppermute | solution.py:310
  45.3 0.0 collective-permute-done.2.refs_0_
  45.3 5.6 %collective-permute-done.3.refs_1_ = bf16[384,256]{1,0:T(8,128)(2,1)} collective-permute-done((bf16[384,256]{1,0:T(8,128)(2,1)}, bf16[384,256]{1,0:T(8,128)(2,1)}, u32[]{:S(2)}, u32[]{:S(2)}) %collective-permute-start.3) | collective-permute-done | bytes 196640 | tf_op jit(solution)/shard_map/ppermute | solution.py:285
  51.0 0.0 collective-permute-done.4.refs_2_
  51.0 2.4 %apply_cycle.2 = (bf16[384,256]{1,0:T(8,128)(2,1)S(1)}, bf16[384,256]{1,0:T(8,128)(2,1)S(1)}, bf16[384,256]{1,0:T(8,128)(2,1)S(1)}, bf16[384,256]{1,0:T(8,128)(2,1)S(1)}) custom-call(bf16[1536,1536]{1,0:T(8,128)(2,1)S(1)} %cycle_operator.1.operator_ref, bf16[384,256]{1,0:T(8,128)(2,1)} %collective-permute-done.2.refs_0_, ...), custom_call_target="tpu_custom_call" | custom-call | flops 30000001024 | bytes 1000000 | tf_op jit(solution)/shard_map/apply_cycle/pallas_call | solution.py:198
  53.4 2.7 %collective-permute-start.5 = (bf16[384,256]{1,0:T(8,128)(2,1)S(1)}, bf16[384,256]{1,0:T(8,128)(2,1)S(1)}, u32[]{:S(2)}, u32[]{:S(2)}) collective-permute-start(bf16[384,256]{1,0:T(8,128)(2,1)S(1)} %get-tuple-element.33), channel_id=1, source_target_pairs={{0,12},{4,8},{8,4},{12,0},{1,13},{5,9},{9,5},{13,1},{2,14},{6,10},... | collective-permute-start | bytes 589832 | tf_op jit(solution)/shard_map/ppermute | solution.py:285
  56.1 0.0 collective-permute-start.6
  56.1 1.8 %collective-permute-start.7 = (bf16[384,256]{1,0:T(8,128)(2,1)S(1)}, bf16[384,256]{1,0:T(8,128)(2,1)S(1)}, u32[]{:S(2)}, u32[]{:S(2)}) collective-permute-start(bf16[384,256]{1,0:T(8,128)(2,1)S(1)} %get-tuple-element.35), channel_id=1, source_target_pairs={{0,4},{4,0},{8,12},{12,8},{1,5},{5,1},{9,13},{13,9},{2,6},{6,2},{1... | collective-permute-start | bytes 589832 | tf_op jit(solution)/shard_map/ppermute | solution.py:285
  57.8 0.0 collective-permute-done.11.refs_0_
  57.8 9.5 %collective-permute-start.12 = (bf16[384,256]{1,0:T(8,128)(2,1)S(1)}, bf16[384,256]{1,0:T(8,128)(2,1)S(1)}, u32[]{:S(2)}, u32[]{:S(2)}) collective-permute-start(bf16[384,256]{1,0:T(8,128)(2,1)S(1)} %get-tuple-element.38), channel_id=1, source_target_pairs={{0,8},{4,12},{8,0},{12,4},{1,9},{5,13},{9,1},{13,5},{2,10},{6,14},... | collective-permute-start | bytes 589832 | tf_op jit(solution)/shard_map/ppermute | solution.py:285
  67.3 0.0 collective-permute-done.1
  67.3 0.0 collective-permute-start.13
  67.3 0.4 bitcast_add_fusion.base_ref
  67.8 11.7 %collective-permute-done.12.refs_1_ = bf16[384,256]{1,0:T(8,128)(2,1)S(1)} collective-permute-done((bf16[384,256]{1,0:T(8,128)(2,1)S(1)}, bf16[384,256]{1,0:T(8,128)(2,1)S(1)}, u32[]{:S(2)}, u32[]{:S(2)}) %collective-permute-start.12) | collective-permute-done | bytes 196640 | tf_op jit(solution)/shard_map/ppermute | solution.py:285
  79.5 0.6 collective-permute-done.13.refs_2_
  80.1 0.0 copy-done.10
  80.1 1.5 %finish.2.refs_4_ = bf16[768,512]{1,0:T(8,128)(2,1)} custom-call(bf16[768,1536]{1,0:T(8,128)(2,1)S(1)} %unpack_matrix.1.pick_ref, f32[768,512]{1,0:T(8,128)S(1)} %bitcast_add_fusion.base_ref, f32[768,1]{1,0:T(8,128)S(1)} %copy.12.part_ref, f32[1,512]{1,0:T(1,128)S(1)} %bitcast.26, bf16[384,256]{1,0:T(8,128)(2,1)S(1)} %collective-permute-done.11.refs_0_, ...), custom_call_target="tpu_custom_call" | custom-call | tf_op jit(solution)/shard_map/finish/pallas_call | solution.py:241
  81.6 0.0 collective-permute-done.5.refs_0_
  81.6 0.0 collective-permute-done.6.refs_1_
  81.6 0.0 collective-permute-done.7.refs_2_
  81.7 1.5 %finish.3 = bf16[768,512]{1,0:T(8,128)(2,1)} custom-call(bf16[768,1536]{1,0:T(8,128)(2,1)S(1)} %unpack_matrix.1.pick_ref, f32[768,512]{1,0:T(8,128)S(1)} %bitcast_add_fusion.base_ref, f32[768,1]{1,0:T(8,128)S(1)} %copy.12.part_ref, f32[1,512]{1,0:T(1,128)S(1)} %bitcast.27, ...), custom_call_target="tpu_custom_call", output_to_operand_aliasing={{}: (8, {})} | custom-call | tf_op jit(solution)/shard_map/finish/pallas_call | solution.py:241
  (18 shorter events, 0.0 us)
Async XLA Ops:
  0.1 1.1 %copy-start.2 = (bf16[1,768,512]{2,1,0:T(8,128)(2,1)S(1)}, bf16[1,768,512]{2,1,0:T(8,128)(2,1)}, u32[]{:S(2)}) copy-start(bf16[1,768,512]{2,1,0:T(8,128)(2,1)} %param.8) | copy-start | bytes 2359300
  1.2 0.7 copy-start.11
  4.8 0.7 copy-start.12
  5.5 0.7 copy-start.14
  6.2 0.7 copy-start.16
  6.8 25.5 %collective-permute-start.8 = (bf16[384,256]{1,0:T(8,128)(2,1)}, bf16[384,256]{1,0:T(8,128)(2,1)}, u32[]{:S(2)}, u32[]{:S(2)}) collective-permute-start(bf16[384,256]{1,0:T(8,128)(2,1)} %get-tuple-element.27), channel_id=1, source_target_pairs={{0,12},{4,8},{8,4},{12,0},{1,13},{5,9},{9,5},{13,1},{2,14},{6,10},... | collective-permute-start | bytes 589832 | tf_op jit(solution)/shard_map/ppermute | solution.py:285
  11.9 26.4 %collective-permute-start.9 = (bf16[384,256]{1,0:T(8,128)(2,1)}, bf16[384,256]{1,0:T(8,128)(2,1)}, u32[]{:S(2)}, u32[]{:S(2)}) collective-permute-start(bf16[384,256]{1,0:T(8,128)(2,1)} %get-tuple-element.26), channel_id=1, source_target_pairs={{0,8},{4,12},{8,0},{12,4},{1,9},{5,13},{9,1},{13,5},{2,10},{6,14},... | collective-permute-start | bytes 589832 | tf_op jit(solution)/shard_map/ppermute | solution.py:285
  11.9 26.4 %collective-permute-start.10 = (bf16[384,256]{1,0:T(8,128)(2,1)}, bf16[384,256]{1,0:T(8,128)(2,1)}, u32[]{:S(2)}, u32[]{:S(2)}) collective-permute-start(bf16[384,256]{1,0:T(8,128)(2,1)} %get-tuple-element.25), channel_id=1, source_target_pairs={{0,4},{4,0},{8,12},{12,8},{1,5},{5,1},{9,13},{13,9},{2,6},{6,2},{1... | collective-permute-start | bytes 589832 | tf_op jit(solution)/shard_map/ppermute | solution.py:285
  12.4 32.9 %collective-permute-start.2 = (bf16[384,256]{1,0:T(8,128)(2,1)}, bf16[384,256]{1,0:T(8,128)(2,1)}, u32[]{:S(2)}, u32[]{:S(2)}) collective-permute-start(bf16[384,256]{1,0:T(8,128)(2,1)} %get-tuple-element.31), channel_id=1, source_target_pairs={{0,12},{4,8},{8,4},{12,0},{1,13},{5,9},{9,5},{13,1},{2,14},{6,10},... | collective-permute-start | bytes 589832 | tf_op jit(solution)/shard_map/ppermute | solution.py:285
  16.3 34.7 %collective-permute-start.3 = (bf16[384,256]{1,0:T(8,128)(2,1)}, bf16[384,256]{1,0:T(8,128)(2,1)}, u32[]{:S(2)}, u32[]{:S(2)}) collective-permute-start(bf16[384,256]{1,0:T(8,128)(2,1)} %get-tuple-element.30), channel_id=1, source_target_pairs={{0,8},{4,12},{8,0},{12,4},{1,9},{5,13},{9,1},{13,5},{2,10},{6,14},... | collective-permute-start | bytes 589832 | tf_op jit(solution)/shard_map/ppermute | solution.py:285
  16.3 1.3 %copy-start.3 = (bf16[1,768,512]{2,1,0:T(8,128)(2,1)S(1)}, bf16[1,768,512]{2,1,0:T(8,128)(2,1)}, u32[]{:S(2)}) copy-start(bf16[1,768,512]{2,1,0:T(8,128)(2,1)} %param.8) | copy-start | bytes 2359300
  17.6 2.3 %copy-start = (bf16[1,3072,768]{2,1,0:T(8,128)(2,1)S(1)}, bf16[1,3072,768]{2,1,0:T(8,128)(2,1)}, u32[]{:S(2)}) copy-start(bf16[1,3072,768]{2,1,0:T(8,128)(2,1)} %param.11) | copy-start | bytes 14155780
  19.9 2.8 %copy-start.1 = (bf16[1,3072,768]{2,1,0:T(8,128)(2,1)S(1)}, bf16[1,3072,768]{2,1,0:T(8,128)(2,1)}, u32[]{:S(2)}) copy-start(bf16[1,3072,768]{2,1,0:T(8,128)(2,1)} %param.11) | copy-start | bytes 14155780
  21.5 1.2 %copy-start.4 = (bf16[2,768,512]{2,1,0:T(8,128)(2,1)}, bf16[2,768,512]{2,1,0:T(8,128)(2,1)S(1)}, u32[]{:S(2)}) copy-start(bf16[2,768,512]{2,1,0:T(8,128)(2,1)S(1)} %ladder_share.3) | copy-start | bytes 4718596
  22.7 2.7 %copy-start.19 = (f32[1,768]{1,0:T(1,128)S(1)}, f32[1,768]{1,0:T(1,128)}, u32[]{:S(2)}) copy-start(f32[1,768]{1,0:T(1,128)} %param.14) | copy-start | bytes 9220
  22.7 2.9 %copy-start.9 = (bf16[1,1,12,128,128]{4,3,2,1,0:T(8,128)(2,1)S(1)}, bf16[1,1,12,128,128]{4,3,2,1,0:T(8,128)(2,1)}, u32[]{:S(2)}) copy-start(bf16[1,1,12,128,128]{4,3,2,1,0:T(8,128)(2,1)} %param.13) | copy-start | bytes 1179652
  24.3 1.2 %copy-start.7 = (bf16[2,768,512]{2,1,0:T(8,128)(2,1)}, bf16[2,768,512]{2,1,0:T(8,128)(2,1)S(1)}, u32[]{:S(2)}) copy-start(bf16[2,768,512]{2,1,0:T(8,128)(2,1)S(1)} %ladder_share.2) | copy-start | bytes 4718596
  25.6 2.3 %copy-start.6 = (bf16[1,1,1536,1536]{3,2,1,0:T(8,128)(2,1)S(1)}, bf16[1,1,1536,1536]{3,2,1,0:T(8,128)(2,1)}, u32[]{:S(2)}) copy-start(bf16[1,1,1536,1536]{3,2,1,0:T(8,128)(2,1)} %param.12) | copy-start | bytes 14155780
  28.0 4.4 %copy-start.15 = (bf16[384,256]{1,0:T(8,128)(2,1)S(1)}, bf16[384,256]{1,0:T(8,128)(2,1)}, u32[]{:S(2)}) copy-start(bf16[384,256]{1,0:T(8,128)(2,1)} %copy-done.14) | copy-start | bytes 589828
  28.0 10.4 %copy-start.8 = (bf16[2,768,512]{2,1,0:T(8,128)(2,1)S(1)}, bf16[2,768,512]{2,1,0:T(8,128)(2,1)}, u32[]{:S(2)}) copy-start(bf16[2,768,512]{2,1,0:T(8,128)(2,1)} %copy-done.7) | copy-start | bytes 4718596
  28.0 10.4 %copy-start.17 = (bf16[384,256]{1,0:T(8,128)(2,1)S(1)}, bf16[384,256]{1,0:T(8,128)(2,1)}, u32[]{:S(2)}) copy-start(bf16[384,256]{1,0:T(8,128)(2,1)} %copy-done.16) | copy-start | bytes 589828
  32.3 11.2 %copy-start.5 = (bf16[2,768,512]{2,1,0:T(8,128)(2,1)S(1)}, bf16[2,768,512]{2,1,0:T(8,128)(2,1)}, u32[]{:S(2)}) copy-start(bf16[2,768,512]{2,1,0:T(8,128)(2,1)} %copy-done.4) | copy-start | bytes 4718596
  32.4 18.6 %collective-permute-start.4 = (bf16[384,256]{1,0:T(8,128)(2,1)S(1)}, bf16[384,256]{1,0:T(8,128)(2,1)S(1)}, u32[]{:S(2)}, u32[]{:S(2)}) collective-permute-start(bf16[384,256]{1,0:T(8,128)(2,1)S(1)} %copy-done.15), channel_id=1, source_target_pairs={{0,4},{4,0},{8,12},{12,8},{1,5},{5,1},{9,13},{13,9},{2,6},{6,2},{1... | collective-permute-start | bytes 589832 | tf_op jit(solution)/shard_map/ppermute | solution.py:285
  38.3 5.2 %collective-permute-start = (bf16[2,768,512]{2,1,0:T(8,128)(2,1)S(1)}, bf16[2,768,512]{2,1,0:T(8,128)(2,1)S(1)}, u32[]{:S(2)}, u32[]{:S(2)}) collective-permute-start(bf16[2,768,512]{2,1,0:T(8,128)(2,1)S(1)} %copy-done.8), channel_id=1, source_target_pairs={{0,1},{1,0},{2,3},{3,2},{4,5},{5,4},{6,7},{7,6},{8,9},{9,8},{10,11... | collective-permute-start | bytes 4718600 | tf_op jit(solution)/shard_map/ppermute | solution.py:299
  40.8 10.1 %copy-start.13 = (bf16[384,256]{1,0:T(8,128)(2,1)S(1)}, bf16[384,256]{1,0:T(8,128)(2,1)}, u32[]{:S(2)}) copy-start(bf16[384,256]{1,0:T(8,128)(2,1)} %copy-done.12) | copy-start | bytes 589828
  40.9 17.0 %collective-permute-start.11 = (bf16[384,256]{1,0:T(8,128)(2,1)S(1)}, bf16[384,256]{1,0:T(8,128)(2,1)S(1)}, u32[]{:S(2)}, u32[]{:S(2)}) collective-permute-start(bf16[384,256]{1,0:T(8,128)(2,1)S(1)} %get-tuple-element.37), channel_id=1, source_target_pairs={{0,12},{4,8},{8,4},{12,0},{1,13},{5,9},{9,5},{13,1},{2,14},{6,10},... | collective-permute-start | bytes 589832 | tf_op jit(solution)/shard_map/ppermute | solution.py:285
  43.8 23.6 %copy-start.18 = (bf16[1,768,512]{2,1,0:T(8,128)(2,1)S(1)}, bf16[1,768,512]{2,1,0:T(8,128)(2,1)}, u32[]{:S(2)}) copy-start(bf16[1,768,512]{2,1,0:T(8,128)(2,1)} %param.9) | copy-start | bytes 2359300
  43.8 23.6 %collective-permute-start.1 = (bf16[768,512]{1,0:T(8,128)(2,1)S(1)}, bf16[768,512]{1,0:T(8,128)(2,1)S(1)}, u32[]{:S(2)}, u32[]{:S(2)}) collective-permute-start(bf16[768,512]{1,0:T(8,128)(2,1)S(1)} %fusion), channel_id=1, source_target_pairs={{0,2},{2,0},{1,3},{3,1},{4,6},{6,4},{5,7},{7,5},{8,10},{10,8},{9,1... | collective-permute-start | bytes 2359304 | tf_op jit(solution)/shard_map/ppermute | solution.py:310
  53.4 28.3 %collective-permute-start.5 = (bf16[384,256]{1,0:T(8,128)(2,1)S(1)}, bf16[384,256]{1,0:T(8,128)(2,1)S(1)}, u32[]{:S(2)}, u32[]{:S(2)}) collective-permute-start(bf16[384,256]{1,0:T(8,128)(2,1)S(1)} %get-tuple-element.33), channel_id=1, source_target_pairs={{0,12},{4,8},{8,4},{12,0},{1,13},{5,9},{9,5},{13,1},{2,14},{6,10},... | collective-permute-start | bytes 589832 | tf_op jit(solution)/shard_map/ppermute | solution.py:285
  56.1 25.6 %collective-permute-start.6 = (bf16[384,256]{1,0:T(8,128)(2,1)S(1)}, bf16[384,256]{1,0:T(8,128)(2,1)S(1)}, u32[]{:S(2)}, u32[]{:S(2)}) collective-permute-start(bf16[384,256]{1,0:T(8,128)(2,1)S(1)} %get-tuple-element.34), channel_id=1, source_target_pairs={{0,8},{4,12},{8,0},{12,4},{1,9},{5,13},{9,1},{13,5},{2,10},{6,14},... | collective-permute-start | bytes 589832 | tf_op jit(solution)/shard_map/ppermute | solution.py:285
  56.1 25.6 %collective-permute-start.7 = (bf16[384,256]{1,0:T(8,128)(2,1)S(1)}, bf16[384,256]{1,0:T(8,128)(2,1)S(1)}, u32[]{:S(2)}, u32[]{:S(2)}) collective-permute-start(bf16[384,256]{1,0:T(8,128)(2,1)S(1)} %get-tuple-element.35), channel_id=1, source_target_pairs={{0,4},{4,0},{8,12},{12,8},{1,5},{5,1},{9,13},{13,9},{2,6},{6,2},{1... | collective-permute-start | bytes 589832 | tf_op jit(solution)/shard_map/ppermute | solution.py:285
  57.8 21.7 %collective-permute-start.12 = (bf16[384,256]{1,0:T(8,128)(2,1)S(1)}, bf16[384,256]{1,0:T(8,128)(2,1)S(1)}, u32[]{:S(2)}, u32[]{:S(2)}) collective-permute-start(bf16[384,256]{1,0:T(8,128)(2,1)S(1)} %get-tuple-element.38), channel_id=1, source_target_pairs={{0,8},{4,12},{8,0},{12,4},{1,9},{5,13},{9,1},{13,5},{2,10},{6,14},... | collective-permute-start | bytes 589832 | tf_op jit(solution)/shard_map/ppermute | solution.py:285
  67.3 12.8 %copy-start.10 = (f32[512]{0:T(512)S(1)}, f32[512]{0:T(512)}, u32[]{:S(2)}) copy-start(f32[512]{0:T(512)} %param.15) | copy-start | bytes 6148
  67.3 12.8 %collective-permute-start.13 = (bf16[384,256]{1,0:T(8,128)(2,1)S(1)}, bf16[384,256]{1,0:T(8,128)(2,1)S(1)}, u32[]{:S(2)}, u32[]{:S(2)}) collective-permute-start(bf16[384,256]{1,0:T(8,128)(2,1)S(1)} %get-tuple-element.39), channel_id=1, source_target_pairs={{0,4},{4,0},{8,12},{12,8},{1,5},{5,1},{9,13},{13,9},{2,6},{6,2},{1... | collective-permute-start | bytes 589832 | tf_op jit(solution)/shard_map/ppermute | solution.py:285

commit v4 on v3

--- a/solution.py
+++ b/solution.py
@@ -7,7 +7,8 @@
 from jax.experimental.pallas import tpu as pltpu
 from jax.sharding import PartitionSpec as P
 
-VMEM_LIMIT = 20 * 1024 * 1024
+VMEM_LIMIT = 24 * 1024 * 1024
+VMEM_MOST = 60 * 1024 * 1024
 HALVES = 2
 F32 = jnp.float32
 BF16 = jnp.bfloat16
@@ -15,8 +16,8 @@
 DEAR = pl.CostEstimate(flops=3 * 10**10, bytes_accessed=10**6, transcendentals=0)
 
 
-def params():
-    return pltpu.CompilerParams(vmem_limit_bytes=VMEM_LIMIT)
+def params(limit=VMEM_LIMIT):
+    return pltpu.CompilerParams(vmem_limit_bytes=limit)
 
 
 def whole(memory=pltpu.VMEM):
@@ -27,12 +28,25 @@
     return jnp.where(match, 1.0, 0.0).astype(BF16)
 
 
-def pack_kernel(chan_count, send, off_ref, route_hbm, amps_hbm, target_ref, *refs):
-    block_refs, (route_ref, amps_ref, sems) = refs[:-3], refs[-3:]
-    rows, width = amps_ref.shape[0], amps_ref.shape[1] // HALVES
+def parted(k, count):
+    return count > 2 and k >= 2
+
+
+def layout(count):
+    far = [(k, h) for h in range(HALVES) for k in reversed(range(count)) if parted(k, count)]
+    return far + [(k, None) for k in reversed(range(count)) if not parted(k, count)]
+
+
+def pack_kernel(chan_count, send, off_ref, route_hbm, amps_hbm, *refs):
+    items = layout(off_ref.shape[0])
+    outs, (target_ref, route_ref, amps_ref, *kept) = refs[: len(items) + 1], refs[len(items) + 1 :]
+    target_hbm, block_hbm = outs[0], outs[1:]
+    block_refs, (in_sems, out_sems) = kept[: len(items)], kept[len(items) :]
+    rows, holes = amps_ref.shape
+    width = holes // HALVES
     parts = [pl.ds(h * width, width) for h in range(HALVES)]
-    copies = [pltpu.make_async_copy(route_hbm, route_ref, sems.at[0])] + [
-        pltpu.make_async_copy(amps_hbm.at[:, part], amps_ref.at[:, part], sems.at[1 + h])
+    copies = [pltpu.make_async_copy(route_hbm, route_ref, in_sems.at[0])] + [
+        pltpu.make_async_copy(amps_hbm.at[:, part], amps_ref.at[:, part], in_sems.at[1 + h])
         for h, part in enumerate(parts)
     ]
     for copy in copies:
@@ -61,36 +75,44 @@
         passed = passed + within[:, lane:]
     target = owners * send + jnp.concatenate(slots, axis=1).astype(jnp.int32)
     target_ref[...] = target
-    count = off_ref.shape[0]
+    out_copies = [pltpu.make_async_copy(target_ref, target_hbm, out_sems.at[len(items)])]
+    out_copies[0].start()
+    for copy in copies[1:]:
+        copy.wait()
     slot = lax.broadcasted_iota(jnp.int32, (block_refs[0].shape[0], rows), 0)
-    for k in reversed(range(count)):
-        pick = selection(slot == target - off_ref[k])
-        for h in range(HALVES):
-            if k == count - 1:
-                copies[1 + h].wait()
-            block_refs[k * HALVES + h][...] = jnp.dot(
-                pick, amps_ref[:, parts[h]], preferred_element_type=F32
-            ).astype(BF16)
+    picks = {}
+    for i, (k, half) in enumerate(items):
+        if k not in picks:
+            picks[k] = selection(slot == target - off_ref[k])
+        rows_in = amps_ref[...] if half is None else amps_ref[:, parts[half]]
+        block_refs[i][...] = jnp.dot(picks[k], rows_in, preferred_element_type=F32).astype(BF16)
+        out_copies.append(pltpu.make_async_copy(block_refs[i], block_hbm[i], out_sems.at[i]))
+        out_copies[-1].start()
+    for copy in out_copies:
+        copy.wait()
 
 
 def pack(offsets, route_row, amps, chan_count, send, block_rows):
     rows, holes = amps.shape
-    count = offsets.shape[0]
-    block = jax.ShapeDtypeStruct((block_rows, holes // HALVES), BF16)
+    items = layout(offsets.shape[0])
+    shapes = [(block_rows, holes if half is None else holes // HALVES) for _, half in items]
     outs = pl.pallas_call(
         functools.partial(pack_kernel, chan_count, send),
-        out_shape=[jax.ShapeDtypeStruct((1, rows), jnp.int32)] + [block] * (count * HALVES),
-        in_specs=[whole(pltpu.SMEM), whole(pltpu.HBM), whole(pltpu.HBM)],
-        out_specs=[whole()] * (1 + count * HALVES),
+        out_shape=[jax.ShapeDtypeStruct((1, rows), jnp.int32)]
+        + [jax.ShapeDtypeStruct(shape, BF16) for shape in shapes],
+        in_specs=[whole(pltpu.SMEM), whole(pl.ANY), whole(pl.ANY)],
+        out_specs=[whole(pl.ANY)] * (1 + len(items)),
         scratch_shapes=[
             pltpu.VMEM((1, rows), jnp.int32),
+            pltpu.VMEM((1, rows), jnp.int32),
             pltpu.VMEM((rows, holes), BF16),
-            pltpu.SemaphoreType.DMA((1 + HALVES,)),
-        ],
-        compiler_params=params(),
+        ]
+        + [pltpu.VMEM(shape, BF16) for shape in shapes]
+        + [pltpu.SemaphoreType.DMA((1 + HALVES,)), pltpu.SemaphoreType.DMA((1 + len(items),))],
+        compiler_params=params(VMEM_MOST),
         name="pack",
     )(offsets, route_row, amps)
-    return outs[0], [[outs[1 + k * HALVES + h] for k in range(count)] for h in range(HALVES)]
+    return outs[0], dict(zip(items, outs[1:]))
 
 
 def unpack_kernel(off_ref, target_ref, out_ref):
@@ -133,7 +155,7 @@
             ],
             out_specs=pl.BlockSpec((1, rows, holes), lambda i, share: (i, 0, 0)),
         ),
-        compiler_params=params(),
+        compiler_params=params(VMEM_MOST),
         cost_estimate=CHEAP,
         name="ladder_share",
     )(share, weight, amps)
@@ -182,30 +204,29 @@
     )(block_index, weight, mixing)
 
 
-def cycle_kernel(operator_ref, *refs):
+def cycle_kernel(half, operator_ref, *refs):
     count = len(refs) // 2
     in_refs, out_refs, block_ref = refs[:count], refs[count : 2 * count], refs[2 * count]
-    block_rows = in_refs[0].shape[0]
-    for j in range(count):
-        block_ref[pl.ds(j * block_rows, block_rows), :] = in_refs[count - 1 - j][...]
-    for k in reversed(range(count)):
-        out_refs[count - 1 - k][...] = jnp.dot(
-            operator_ref[pl.ds(k * block_rows, block_rows), :], block_ref[...], preferred_element_type=F32
-        ).astype(BF16)
-
-
-def apply_cycle(operator, blocks):
-    outs = pl.pallas_call(
-        cycle_kernel,
-        out_shape=[jax.ShapeDtypeStruct(b.shape, BF16) for b in blocks],
-        in_specs=[whole()] * (1 + len(blocks)),
-        out_specs=[whole()] * len(blocks),
-        scratch_shapes=[pltpu.VMEM((operator.shape[0], blocks[0].shape[1]), BF16)],
+    block_rows, width = out_refs[0].shape
+    for i, in_ref in enumerate(in_refs):
+        at = pl.ds((count - 1 - i) * block_rows, block_rows)
+        block_ref[at, :] = in_ref[...] if in_ref.shape[1] == width else in_ref[:, pl.ds(half * width, width)]
+    for i, out_ref in enumerate(out_refs):
+        at = pl.ds((count - 1 - i) * block_rows, block_rows)
+        out_ref[...] = jnp.dot(operator_ref[at, :], block_ref[...], preferred_element_type=F32).astype(BF16)
+
+
+def apply_cycle(half, operator, arrays, width):
+    return pl.pallas_call(
+        functools.partial(cycle_kernel, half),
+        out_shape=[jax.ShapeDtypeStruct((a.shape[0], width), BF16) for a in arrays],
+        in_specs=[whole()] * (1 + len(arrays)),
+        out_specs=[whole()] * len(arrays),
+        scratch_shapes=[pltpu.VMEM((operator.shape[0], width), BF16)],
         compiler_params=params(),
         cost_estimate=DEAR,
         name="apply_cycle",
-    )(operator, *reversed(blocks))
-    return list(reversed(outs))
+    )(operator, *arrays)
 
 
 def finish_kernel(half, count, tiles, pick_ref, base_ref, part_ref, hole_ref, *refs):
@@ -213,8 +234,8 @@
     block_rows, width = in_refs[0].shape
     tile = out_ref.shape[0] // tiles
     columns = pl.ds(half * width, width)
-    for k in range(count):
-        block_ref[pl.ds(k * block_rows, block_rows), :] = in_refs[count - 1 - k][...]
+    for i, in_ref in enumerate(in_refs):
+        block_ref[pl.ds((count - 1 - i) * block_rows, block_rows), :] = in_ref[...]
     copies = []
     for t in range(tiles):
         at = pl.ds(t * tile, tile)
@@ -227,22 +248,21 @@
         copy.wait()
 
 
-def finish(half, pick, base, part_column, hole_row, blocks, earlier):
+def finish(half, pick, base, part_column, hole_row, arrays, earlier):
     rows, holes = base.shape
-    tiles = 3
-    count, width = len(blocks), blocks[0].shape[1]
-    operands = [pick, base, part_column, hole_row, *reversed(blocks)]
+    tiles, width = 3, holes // HALVES
+    operands = [pick, base, part_column, hole_row, *arrays]
     in_specs = [whole()] * len(operands)
     aliases = {}
     if earlier is not None:
         aliases = {len(operands): 0}
         operands.append(earlier)
-        in_specs.append(whole(pltpu.HBM))
-    return pl.pallas_call(
-        functools.partial(finish_kernel, half, count, tiles),
+        in_specs.append(whole(pl.ANY))
+    return pl.pallas_call(
+        functools.partial(finish_kernel, half, len(arrays), tiles),
         out_shape=jax.ShapeDtypeStruct((rows, holes), BF16),
         in_specs=in_specs,
-        out_specs=whole(pltpu.HBM),
+        out_specs=whole(pl.ANY),
         scratch_shapes=[
             pltpu.VMEM((pick.shape[1], width), BF16),
             pltpu.VMEM((rows, width), BF16),
@@ -274,19 +294,16 @@
         block_index = jnp.zeros((1,), jnp.int32)
     offsets = block_index * block_rows
 
-    def exchange(blocks):
+    def exchange(block, k):
         if not paired:
-            split = blocks[0].reshape(chan_count, send, -1)
+            split = block.reshape(chan_count, send, -1)
             split = lax.all_to_all(split, "chan", split_axis=0, concat_axis=0, tiled=True)
-            return [split.reshape(capacity, -1)]
-        arrived = [blocks[0]] + [None] * (chan_count - 1)
-        for k in reversed(range(1, chan_count)):
-            pairs = [(i, i ^ k) for i in range(chan_count)]
-            arrived[k] = lax.ppermute(blocks[k], "chan", pairs)
-        return arrived
-
+            return split.reshape(capacity, -1)
+        return lax.ppermute(block, "chan", [(i, i ^ k) for i in range(chan_count)]) if k else block
+
+    far_first = list(reversed(range(block_index.shape[0])))
     target, outgoing = pack(offsets, route[0].reshape(1, rows), amps, chan_count, send, block_rows)
-    blocks = [exchange(part) for part in outgoing]
+    arrived = {item: exchange(block, item[0]) for item, block in outgoing.items()}
     amps, outgoing = lax.optimization_barrier((amps, outgoing))
     pick = unpack_matrix(offsets, target.reshape(rows, 1), capacity)
 
@@ -311,7 +328,13 @@
 
     operator = cycle_operator(block_index, weight, mixing, block_rows)
     part_column, hole_row = gap_part[0].reshape(rows, 1), gap_hole.reshape(1, holes)
-    returned = [exchange(apply_cycle(operator, part)) for part in blocks]
+    returned = []
+    for half in range(HALVES):
+        blocks = [arrived[(k, half if parted(k, len(far_first)) else None)] for k in far_first]
+        if returned:
+            blocks, made = lax.optimization_barrier((blocks, made))
+        made = apply_cycle(half, operator, blocks, holes // HALVES)
+        returned.append([exchange(block, k) for k, block in zip(far_first, made)])
     updated = None
     for half in range(HALVES):
         updated = finish(half, pick, base, part_column, hole_row, returned[half], updated)

time: 83.5 us -> 81.4 us (0.975)
  waiting for transfers between devices: 23.3 us -> 13.4 us
  starting transfers between devices: 28.3 us -> 36.6 us
  local copies, waits for them, and re-layouts: 11.2 us -> 4.07 us
  Pallas kernels: 19.4 us -> 25.7 us
    ppermute x12 -> x11, waiting for transfers between devices: 23.3 us -> 13.4 us  [exchange(): lax.ppermute(block, 'chan', [(i, i ^ k) for i in range(chan_count)])]
    unnamed x40 -> x16, local copies, waits for them, and re-layouts: 10.9 us -> 2.36 us
    ppermute x12 -> x11, starting transfers between devices: 26.7 us -> 34.9 us  [exchange(): lax.ppermute(block, 'chan', [(i, i ^ k) for i in range(chan_count)])]
    pallas_call x2, Pallas kernels: 3.11 us -> 7.96 us  [ladder_share(): pl.pallas_call(ladder_kernel, out_shape=jax.ShapeDtypeStruct((lad_count,...]
    pallas_call x1, Pallas kernels: 2.91 us -> 4.03 us  [pack(): pl.pallas_call(functools.partial(pack_kernel, chan_count, send), out_shap...]
  transfers between devices with their start and end apart: 14 -> 13, of which waited for: 4 -> 3; matrix products, arithmetic and copies ran while one was open for 1% -> 3% of each run, Pallas kernels for 18% -> 25%
where the time goes in v4:
time: 81.4 us; the launch traced here: 81.1 us
  starting transfers between devices  36.6 us (45%)
  Pallas kernels  25.7 us (32%)
  waiting for transfers between devices  13.4 us (16%)
  local copies, waits for them, and re-layouts  4.07 us (5%)
  other arithmetic  1.22 us (1%)
    ppermute x11, starting transfers between devices, exchange(): lax.ppermute(block, 'chan', [(i, i ^ k) for i in range(chan_count)])  34.9 us
    ppermute x11, waiting for transfers between devices, exchange(): lax.ppermute(block, 'chan', [(i, i ^ k) for i in range(chan_count)])  13.4 us
    pallas_call x2, Pallas kernels, ladder_share(): pl.pallas_call(ladder_kernel, out_shape=jax.ShapeDtypeStruct((lad_count,...  7.96 us
    pallas_call x2, Pallas kernels, apply_cycle(): pl.pallas_call(functools.partial(cycle_kernel, half), out_shape=[jax.Shap...  5.22 us
    pallas_call x1, Pallas kernels, cycle_operator(): pl.pallas_call(functools.partial(operator_kernel, group), out_shape=jax.S...  4.36 us
    pallas_call x1, Pallas kernels, pack(): pl.pallas_call(functools.partial(pack_kernel, chan_count, send), out_shap...  4.03 us
    pallas_call x2, Pallas kernels, finish(): pl.pallas_call(functools.partial(finish_kernel, half, len(arrays), tiles)...  3.02 us
    unnamed x16, local copies, waits for them, and re-layouts  2.36 us
  transfers between devices with their start and end apart: 13, of which 3 were waited for; matrix products, arithmetic and copies ran while one was open for 3% of the time, Pallas kernels for 25%

profile of v4, /device:TPU:0, one launch (start us, length us, event | category | flops | bytes accessed | tf_op | source)
XLA Modules:
  0.0 81.1 jit_solution(608888586117089461)
XLA Ops:
  0.0 0.6 broadcast_multiply_fusion
  0.6 4.0 %pack.1 = (s32[1,768]{1,0:T(1,128)}, bf16[384,256]{1,0:T(8,128)(2,1)}, bf16[384,256]{1,0:T(8,128)(2,1)}, bf16[384,256]{1,0:T(8,128)(2,1)}, bf16[384,256]{1,0:T(8...) custom-call(s32[4]{0:T(128)} %get-tuple-element.45.off_ref, s32[1,768]{1,0:T(1,128)} %bitcast.28, ...), custom_call_target="tpu_custom_call" | custom-call | tf_op jit(solution)/shard_map/pack/pallas_call | solution.py:99
  4.6 3.1 %collective-permute-start.4 = (bf16[384,512]{1,0:T(8,128)(2,1)}, bf16[384,512]{1,0:T(8,128)(2,1)}, u32[]{:S(2)}, u32[]{:S(2)}) collective-permute-start(bf16[384,512]{1,0:T(8,128)(2,1)} %get-tuple-element.27), channel_id=1, source_target_pairs={{0,4},{4,0},{8,12},{12,8},{1,5},{5,1},{9,13},{13,9},{2,6},{6,2},{1... | collective-permute-start | bytes 1179656 | tf_op jit(solution)/shard_map/ppermute | solution.py:302
  7.7 2.6 %collective-permute-start.6 = (bf16[384,256]{1,0:T(8,128)(2,1)}, bf16[384,256]{1,0:T(8,128)(2,1)}, u32[]{:S(2)}, u32[]{:S(2)}) collective-permute-start(bf16[384,256]{1,0:T(8,128)(2,1)} %get-tuple-element.28), channel_id=1, source_target_pairs={{0,8},{4,12},{8,0},{12,4},{1,9},{5,13},{9,1},{13,5},{2,10},{6,14},... | collective-permute-start | bytes 589832 | tf_op jit(solution)/shard_map/ppermute | solution.py:302
  10.3 0.0 collective-permute-start.5
  10.3 1.9 %collective-permute-start.3 = (bf16[384,256]{1,0:T(8,128)(2,1)}, bf16[384,256]{1,0:T(8,128)(2,1)}, u32[]{:S(2)}, u32[]{:S(2)}) collective-permute-start(bf16[384,256]{1,0:T(8,128)(2,1)} %get-tuple-element.29), channel_id=1, source_target_pairs={{0,8},{4,12},{8,0},{12,4},{1,9},{5,13},{9,1},{13,5},{2,10},{6,14},... | collective-permute-start | bytes 589832 | tf_op jit(solution)/shard_map/ppermute | solution.py:302
  12.2 1.9 %collective-permute-start.2 = (bf16[384,256]{1,0:T(8,128)(2,1)}, bf16[384,256]{1,0:T(8,128)(2,1)}, u32[]{:S(2)}, u32[]{:S(2)}) collective-permute-start(bf16[384,256]{1,0:T(8,128)(2,1)} %get-tuple-element.31), channel_id=1, source_target_pairs={{0,12},{4,8},{8,4},{12,0},{1,13},{5,9},{9,5},{13,1},{2,14},{6,10},... | collective-permute-start | bytes 589832 | tf_op jit(solution)/shard_map/ppermute | solution.py:302
  14.1 0.9 %copy.12.part_ref = f32[768,1]{1,0:T(8,128)S(1)} copy(f32[768,1]{0,1:T(1,128)} %bitcast.29) | data formatting | bytes 6144 | tf_op jit(solution)/shard_map/reshape;squeeze | solution.py:330
  15.0 0.9 %copy.10.target_ref = s32[768,1]{1,0:T(8,128)S(1)} copy(s32[768,1]{0,1:T(1,128)} %bitcast.30) | data formatting | bytes 6144 | tf_op jit(solution)/shard_map/reshape | solution.py:308
  15.9 4.0 %ladder_share.3 = bf16[2,768,512]{2,1,0:T(8,128)(2,1)} custom-call(s32[1]{0:T(128)} %bitcast.9.share_ref, bf16[3072,768]{1,0:T(8,128)(2,1)} %bitcast.23, bf16[768,512]{1,0:T(8,128)(2,1)} %bitcast.26), custom_call_target="tpu_custom_call" | custom-call | tf_op jit(solution)/shard_map/ladder_share/pallas_call | solution.py:146
  19.9 0.0 copy-start.3
  19.9 4.0 %ladder_share.2 = bf16[2,768,512]{2,1,0:T(8,128)(2,1)} custom-call(s32[1]{0:T(128)} %bitcast.7.share_ref, bf16[3072,768]{1,0:T(8,128)(2,1)} %bitcast.24, bf16[768,512]{1,0:T(8,128)(2,1)} %bitcast.27), custom_call_target="tpu_custom_call" | custom-call | tf_op jit(solution)/shard_map/ladder_share/pallas_call | solution.py:146
  23.8 0.0 copy-done.3
  23.8 0.0 copy-start.1
  23.8 1.1 %unpack_matrix.1.pick_ref = bf16[768,1536]{1,0:T(8,128)(2,1)S(1)} custom-call(s32[4]{0:T(128)S(1)} %copy-done.3, s32[768,1]{1,0:T(8,128)S(1)} %copy.10.target_ref), custom_call_target="tpu_custom_call" | custom-call | tf_op jit(solution)/shard_map/unpack_matrix/pallas_call | solution.py:129
  24.9 0.0 copy-done.1
  25.0 0.0 copy-start
  25.0 2.3 %copy-done = bf16[1,1,1536,1536]{3,2,1,0:T(8,128)(2,1)S(1)} copy-done((bf16[1,1,1536,1536]{3,2,1,0:T(8,128)(2,1)S(1)}, bf16[1,1,1536,1536]{3,2,1,0:T(8,128)(2,1)}, u32[]{:S(2)}) %copy-start) | copy-done | bytes 4718616
  27.3 0.0 copy-start.6
  27.3 0.0 copy-start.4
  27.3 4.4 %cycle_operator.1.operator_ref = bf16[1536,1536]{1,0:T(8,128)(2,1)S(1)} custom-call(s32[4]{0:T(128)S(1)} %get-tuple-element.46.block_index, bf16[1536,1536]{1,0:T(8,128)(2,1)S(1)} %bitcast.19, bf16[12,128,128]{2,1,0:T(8,128)(2,1)S(1)} %bitcast.20), custom_call_target="tpu_custom_call" | custom-call | tf_op jit(solution)/shard_map/cycle_operator/pallas_call | solution.py:188
  31.7 0.0 copy-start.5
  31.7 0.0 collective-permute-done.6.refs_1_
  31.7 0.0 copy-done.6
  31.7 0.1 collective-permute-start
  31.8 0.0 collective-permute-done.5.refs_0_
  31.8 0.0 collective-permute-done.4.refs_2_
  31.8 0.0 copy-done.4
  31.8 2.7 %apply_cycle.2 = (bf16[384,256]{1,0:T(8,128)(2,1)S(1)}, bf16[384,256]{1,0:T(8,128)(2,1)S(1)}, bf16[384,256]{1,0:T(8,128)(2,1)S(1)}, bf16[384,256]{1,0:T(8,128)(2,1)S(1)}) custom-call(bf16[1536,1536]{1,0:T(8,128)(2,1)S(1)} %cycle_operator.1.operator_ref, bf16[384,256]{1,0:T(8,128)(2,1)} %collective-permute-done.5.refs_0_, ...), custom_call_target="tpu_custom_call" | custom-call | flops 30000001024 | bytes 1000000 | tf_op jit(solution)/shard_map/apply_cycle/pallas_call | solution.py:220
  34.5 2.0 %collective-permute-start.10 = (bf16[384,256]{1,0:T(8,128)(2,1)S(1)}, bf16[384,256]{1,0:T(8,128)(2,1)S(1)}, u32[]{:S(2)}, u32[]{:S(2)}) collective-permute-start(bf16[384,256]{1,0:T(8,128)(2,1)S(1)} %get-tuple-element.33), channel_id=1, source_target_pairs={{0,12},{4,8},{8,4},{12,0},{1,13},{5,9},{9,5},{13,1},{2,14},{6,10},... | collective-permute-start | bytes 589832 | tf_op jit(solution)/shard_map/ppermute | solution.py:302
  36.4 6.1 %collective-permute-start.11 = (bf16[384,256]{1,0:T(8,128)(2,1)S(1)}, bf16[384,256]{1,0:T(8,128)(2,1)S(1)}, u32[]{:S(2)}, u32[]{:S(2)}) collective-permute-start(bf16[384,256]{1,0:T(8,128)(2,1)S(1)} %get-tuple-element.34), channel_id=1, source_target_pairs={{0,8},{4,12},{8,0},{12,4},{1,9},{5,13},{9,1},{13,5},{2,10},{6,14},... | collective-permute-start | bytes 589832 | tf_op jit(solution)/shard_map/ppermute | solution.py:302
  42.5 8.0 %collective-permute-done.3.refs_1_ = bf16[384,256]{1,0:T(8,128)(2,1)} collective-permute-done((bf16[384,256]{1,0:T(8,128)(2,1)}, bf16[384,256]{1,0:T(8,128)(2,1)}, u32[]{:S(2)}, u32[]{:S(2)}) %collective-permute-start.3) | collective-permute-done | bytes 196640 | tf_op jit(solution)/shard_map/ppermute | solution.py:302
  50.5 0.0 collective-permute-start.12
  50.5 0.0 collective-permute-done.2.refs_0_
  50.5 0.0 collective-permute-done
  50.5 0.0 copy-done.5
  50.5 0.2 fusion
  50.7 0.0 copy-start.7
  50.7 1.6 %collective-permute-start.1 = (bf16[768,512]{1,0:T(8,128)(2,1)S(1)}, bf16[768,512]{1,0:T(8,128)(2,1)S(1)}, u32[]{:S(2)}, u32[]{:S(2)}) collective-permute-start(bf16[768,512]{1,0:T(8,128)(2,1)S(1)} %fusion), channel_id=1, source_target_pairs={{0,2},{2,0},{1,3},{3,1},{4,6},{6,4},{5,7},{7,5},{8,10},{10,8},{9,1... | collective-permute-start | bytes 2359304 | tf_op jit(solution)/shard_map/ppermute | solution.py:327
  52.3 2.6 %apply_cycle.3 = (bf16[384,256]{1,0:T(8,128)(2,1)S(1)}, bf16[384,256]{1,0:T(8,128)(2,1)S(1)}, bf16[384,256]{1,0:T(8,128)(2,1)S(1)}, bf16[384,256]{1,0:T(8,128)(2,1)S(1)}) custom-call(bf16[1536,1536]{1,0:T(8,128)(2,1)S(1)} %cycle_operator.1.operator_ref, bf16[384,256]{1,0:T(8,128)(2,1)} %collective-permute-done.2.refs_0_, ...), custom_call_target="tpu_custom_call" | custom-call | flops 30000001024 | bytes 1000000 | tf_op jit(solution)/shard_map/apply_cycle/pallas_call | solution.py:220
  54.9 2.6 %collective-permute-start.7 = (bf16[384,256]{1,0:T(8,128)(2,1)S(1)}, bf16[384,256]{1,0:T(8,128)(2,1)S(1)}, u32[]{:S(2)}, u32[]{:S(2)}) collective-permute-start(bf16[384,256]{1,0:T(8,128)(2,1)S(1)} %get-tuple-element.41), channel_id=1, source_target_pairs={{0,12},{4,8},{8,4},{12,0},{1,13},{5,9},{9,5},{13,1},{2,14},{6,10},... | collective-permute-start | bytes 589832 | tf_op jit(solution)/shard_map/ppermute | solution.py:302
  57.4 0.0 collective-permute-done.10.refs_0_
  57.4 9.3 %collective-permute-start.8 = (bf16[384,256]{1,0:T(8,128)(2,1)S(1)}, bf16[384,256]{1,0:T(8,128)(2,1)S(1)}, u32[]{:S(2)}, u32[]{:S(2)}) collective-permute-start(bf16[384,256]{1,0:T(8,128)(2,1)S(1)} %get-tuple-element.42), channel_id=1, source_target_pairs={{0,8},{4,12},{8,0},{12,4},{1,9},{5,13},{9,1},{13,5},{2,10},{6,14},... | collective-permute-start | bytes 589832 | tf_op jit(solution)/shard_map/ppermute | solution.py:302
  66.7 0.0 collective-permute-done.1
  66.7 0.0 copy-start.2
  66.7 5.5 %collective-permute-start.9 = (bf16[384,256]{1,0:T(8,128)(2,1)S(1)}, bf16[384,256]{1,0:T(8,128)(2,1)S(1)}, u32[]{:S(2)}, u32[]{:S(2)}) collective-permute-start(bf16[384,256]{1,0:T(8,128)(2,1)S(1)} %get-tuple-element.43), channel_id=1, source_target_pairs={{0,4},{4,0},{8,12},{12,8},{1,5},{5,1},{9,13},{13,9},{2,6},{6,2},{1... | collective-permute-start | bytes 589832 | tf_op jit(solution)/shard_map/ppermute | solution.py:302
  72.3 0.0 copy-done.7
  72.3 0.4 bitcast_add_fusion.base_ref
  72.7 0.0 collective-permute-done.11.refs_1_
  72.7 0.0 collective-permute-done.12.refs_2_
  72.7 0.0 copy-done.2
  72.7 1.5 %finish.2.refs_4_ = bf16[768,512]{1,0:T(8,128)(2,1)} custom-call(bf16[768,1536]{1,0:T(8,128)(2,1)S(1)} %unpack_matrix.1.pick_ref, f32[768,512]{1,0:T(8,128)S(1)} %bitcast_add_fusion.base_ref, f32[768,1]{1,0:T(8,128)S(1)} %copy.12.part_ref, f32[1,512]{1,0:T(1,128)S(1)} %bitcast.21, bf16[384,256]{1,0:T(8,128)(2,1)S(1)} %collective-permute-done.10.refs_0_, ...), custom_call_target="tpu_custom_call" | custom-call | tf_op jit(solution)/shard_map/finish/pallas_call | solution.py:261
  74.2 0.0 collective-permute-done.7.refs_0_
  74.2 4.3 %collective-permute-done.8.refs_1_ = bf16[384,256]{1,0:T(8,128)(2,1)S(1)} collective-permute-done((bf16[384,256]{1,0:T(8,128)(2,1)S(1)}, bf16[384,256]{1,0:T(8,128)(2,1)S(1)}, u32[]{:S(2)}, u32[]{:S(2)}) %collective-permute-start.8) | collective-permute-done | bytes 196640 | tf_op jit(solution)/shard_map/ppermute | solution.py:302
  78.5 1.1 %collective-permute-done.9.refs_2_ = bf16[384,256]{1,0:T(8,128)(2,1)S(1)} collective-permute-done((bf16[384,256]{1,0:T(8,128)(2,1)S(1)}, bf16[384,256]{1,0:T(8,128)(2,1)S(1)}, u32[]{:S(2)}, u32[]{:S(2)}) %collective-permute-start.9) | collective-permute-done | bytes 196640 | tf_op jit(solution)/shard_map/ppermute | solution.py:302
  79.6 1.5 %finish.3 = bf16[768,512]{1,0:T(8,128)(2,1)} custom-call(bf16[768,1536]{1,0:T(8,128)(2,1)S(1)} %unpack_matrix.1.pick_ref, f32[768,512]{1,0:T(8,128)S(1)} %bitcast_add_fusion.base_ref, f32[768,1]{1,0:T(8,128)S(1)} %copy.12.part_ref, f32[1,512]{1,0:T(1,128)S(1)} %bitcast.22, ...), custom_call_target="tpu_custom_call", output_to_operand_aliasing={{}: (8, {})} | custom-call | tf_op jit(solution)/shard_map/finish/pallas_call | solution.py:261
Async XLA Ops:
  4.6 27.2 %collective-permute-start.4 = (bf16[384,512]{1,0:T(8,128)(2,1)}, bf16[384,512]{1,0:T(8,128)(2,1)}, u32[]{:S(2)}, u32[]{:S(2)}) collective-permute-start(bf16[384,512]{1,0:T(8,128)(2,1)} %get-tuple-element.27), channel_id=1, source_target_pairs={{0,4},{4,0},{8,12},{12,8},{1,5},{5,1},{9,13},{13,9},{2,6},{6,2},{1... | collective-permute-start | bytes 1179656 | tf_op jit(solution)/shard_map/ppermute | solution.py:302
  7.7 24.0 %collective-permute-start.6 = (bf16[384,256]{1,0:T(8,128)(2,1)}, bf16[384,256]{1,0:T(8,128)(2,1)}, u32[]{:S(2)}, u32[]{:S(2)}) collective-permute-start(bf16[384,256]{1,0:T(8,128)(2,1)} %get-tuple-element.28), channel_id=1, source_target_pairs={{0,8},{4,12},{8,0},{12,4},{1,9},{5,13},{9,1},{13,5},{2,10},{6,14},... | collective-permute-start | bytes 589832 | tf_op jit(solution)/shard_map/ppermute | solution.py:302
  10.3 21.5 %collective-permute-start.5 = (bf16[384,256]{1,0:T(8,128)(2,1)}, bf16[384,256]{1,0:T(8,128)(2,1)}, u32[]{:S(2)}, u32[]{:S(2)}) collective-permute-start(bf16[384,256]{1,0:T(8,128)(2,1)} %get-tuple-element.30), channel_id=1, source_target_pairs={{0,12},{4,8},{8,4},{12,0},{1,13},{5,9},{9,5},{13,1},{2,14},{6,10},... | collective-permute-start | bytes 589832 | tf_op jit(solution)/shard_map/ppermute | solution.py:302
  10.3 40.2 %collective-permute-start.3 = (bf16[384,256]{1,0:T(8,128)(2,1)}, bf16[384,256]{1,0:T(8,128)(2,1)}, u32[]{:S(2)}, u32[]{:S(2)}) collective-permute-start(bf16[384,256]{1,0:T(8,128)(2,1)} %get-tuple-element.29), channel_id=1, source_target_pairs={{0,8},{4,12},{8,0},{12,4},{1,9},{5,13},{9,1},{13,5},{2,10},{6,14},... | collective-permute-start | bytes 589832 | tf_op jit(solution)/shard_map/ppermute | solution.py:302
  12.2 38.3 %collective-permute-start.2 = (bf16[384,256]{1,0:T(8,128)(2,1)}, bf16[384,256]{1,0:T(8,128)(2,1)}, u32[]{:S(2)}, u32[]{:S(2)}) collective-permute-start(bf16[384,256]{1,0:T(8,128)(2,1)} %get-tuple-element.31), channel_id=1, source_target_pairs={{0,12},{4,8},{8,4},{12,0},{1,13},{5,9},{9,5},{13,1},{2,14},{6,10},... | collective-permute-start | bytes 589832 | tf_op jit(solution)/shard_map/ppermute | solution.py:302
  19.9 4.0 %copy-start.3 = (s32[4]{0:T(128)S(1)}, s32[4]{0:T(128)}, u32[]{:S(2)}) copy-start(s32[4]{0:T(128)} %get-tuple-element.45.off_ref) | copy-start | bytes 52
  23.8 1.1 %copy-start.1 = (bf16[1,1,12,128,128]{4,3,2,1,0:T(8,128)(2,1)S(1)}, bf16[1,1,12,128,128]{4,3,2,1,0:T(8,128)(2,1)}, u32[]{:S(2)}) copy-start(bf16[1,1,12,128,128]{4,3,2,1,0:T(8,128)(2,1)} %param.13) | copy-start | bytes 1179652
  25.0 2.3 %copy-start = (bf16[1,1,1536,1536]{3,2,1,0:T(8,128)(2,1)S(1)}, bf16[1,1,1536,1536]{3,2,1,0:T(8,128)(2,1)}, u32[]{:S(2)}) copy-start(bf16[1,1,1536,1536]{3,2,1,0:T(8,128)(2,1)} %param.12) | copy-start | bytes 14155780
  27.3 4.4 %copy-start.6 = (bf16[2,768,512]{2,1,0:T(8,128)(2,1)S(1)}, bf16[2,768,512]{2,1,0:T(8,128)(2,1)}, u32[]{:S(2)}) copy-start(bf16[2,768,512]{2,1,0:T(8,128)(2,1)} %ladder_share.2) | copy-start | bytes 4718596
  27.3 4.5 %copy-start.4 = (bf16[384,512]{1,0:T(8,128)(2,1)S(1)}, bf16[384,512]{1,0:T(8,128)(2,1)}, u32[]{:S(2)}) copy-start(bf16[384,512]{1,0:T(8,128)(2,1)} %get-tuple-element.40.refs_3_) | copy-start | bytes 1179652
  31.7 18.8 %copy-start.5 = (bf16[2,768,512]{2,1,0:T(8,128)(2,1)S(1)}, bf16[2,768,512]{2,1,0:T(8,128)(2,1)}, u32[]{:S(2)}) copy-start(bf16[2,768,512]{2,1,0:T(8,128)(2,1)} %ladder_share.3) | copy-start | bytes 4718596
  31.7 18.8 %collective-permute-start = (bf16[2,768,512]{2,1,0:T(8,128)(2,1)S(1)}, bf16[2,768,512]{2,1,0:T(8,128)(2,1)S(1)}, u32[]{:S(2)}, u32[]{:S(2)}) collective-permute-start(bf16[2,768,512]{2,1,0:T(8,128)(2,1)S(1)} %copy-done.6), channel_id=1, source_target_pairs={{0,1},{1,0},{2,3},{3,2},{4,5},{5,4},{6,7},{7,6},{8,9},{9,8},{10,11... | collective-permute-start | bytes 4718600 | tf_op jit(solution)/shard_map/ppermute | solution.py:316
  34.5 23.0 %collective-permute-start.10 = (bf16[384,256]{1,0:T(8,128)(2,1)S(1)}, bf16[384,256]{1,0:T(8,128)(2,1)S(1)}, u32[]{:S(2)}, u32[]{:S(2)}) collective-permute-start(bf16[384,256]{1,0:T(8,128)(2,1)S(1)} %get-tuple-element.33), channel_id=1, source_target_pairs={{0,12},{4,8},{8,4},{12,0},{1,13},{5,9},{9,5},{13,1},{2,14},{6,10},... | collective-permute-start | bytes 589832 | tf_op jit(solution)/shard_map/ppermute | solution.py:302
  36.4 36.2 %collective-permute-start.11 = (bf16[384,256]{1,0:T(8,128)(2,1)S(1)}, bf16[384,256]{1,0:T(8,128)(2,1)S(1)}, u32[]{:S(2)}, u32[]{:S(2)}) collective-permute-start(bf16[384,256]{1,0:T(8,128)(2,1)S(1)} %get-tuple-element.34), channel_id=1, source_target_pairs={{0,8},{4,12},{8,0},{12,4},{1,9},{5,13},{9,1},{13,5},{2,10},{6,14},... | collective-permute-start | bytes 589832 | tf_op jit(solution)/shard_map/ppermute | solution.py:302
  50.5 22.2 %collective-permute-start.12 = (bf16[384,256]{1,0:T(8,128)(2,1)S(1)}, bf16[384,256]{1,0:T(8,128)(2,1)S(1)}, u32[]{:S(2)}, u32[]{:S(2)}) collective-permute-start(bf16[384,256]{1,0:T(8,128)(2,1)S(1)} %get-tuple-element.35), channel_id=1, source_target_pairs={{0,4},{4,0},{8,12},{12,8},{1,5},{5,1},{9,13},{13,9},{2,6},{6,2},{1... | collective-permute-start | bytes 589832 | tf_op jit(solution)/shard_map/ppermute | solution.py:302
  50.7 21.5 %copy-start.7 = (bf16[1,768,512]{2,1,0:T(8,128)(2,1)S(1)}, bf16[1,768,512]{2,1,0:T(8,128)(2,1)}, u32[]{:S(2)}) copy-start(bf16[1,768,512]{2,1,0:T(8,128)(2,1)} %param.9) | copy-start | bytes 2359300
  50.7 16.0 %collective-permute-start.1 = (bf16[768,512]{1,0:T(8,128)(2,1)S(1)}, bf16[768,512]{1,0:T(8,128)(2,1)S(1)}, u32[]{:S(2)}, u32[]{:S(2)}) collective-permute-start(bf16[768,512]{1,0:T(8,128)(2,1)S(1)} %fusion), channel_id=1, source_target_pairs={{0,2},{2,0},{1,3},{3,1},{4,6},{6,4},{5,7},{7,5},{8,10},{10,8},{9,1... | collective-permute-start | bytes 2359304 | tf_op jit(solution)/shard_map/ppermute | solution.py:327
  54.9 19.4 %collective-permute-start.7 = (bf16[384,256]{1,0:T(8,128)(2,1)S(1)}, bf16[384,256]{1,0:T(8,128)(2,1)S(1)}, u32[]{:S(2)}, u32[]{:S(2)}) collective-permute-start(bf16[384,256]{1,0:T(8,128)(2,1)S(1)} %get-tuple-element.41), channel_id=1, source_target_pairs={{0,12},{4,8},{8,4},{12,0},{1,13},{5,9},{9,5},{13,1},{2,14},{6,10},... | collective-permute-start | bytes 589832 | tf_op jit(solution)/shard_map/ppermute | solution.py:302
  57.4 21.1 %collective-permute-start.8 = (bf16[384,256]{1,0:T(8,128)(2,1)S(1)}, bf16[384,256]{1,0:T(8,128)(2,1)S(1)}, u32[]{:S(2)}, u32[]{:S(2)}) collective-permute-start(bf16[384,256]{1,0:T(8,128)(2,1)S(1)} %get-tuple-element.42), channel_id=1, source_target_pairs={{0,8},{4,12},{8,0},{12,4},{1,9},{5,13},{9,1},{13,5},{2,10},{6,14},... | collective-permute-start | bytes 589832 | tf_op jit(solution)/shard_map/ppermute | solution.py:302
  66.7 6.0 %copy-start.2 = (f32[512]{0:T(512)S(1)}, f32[512]{0:T(512)}, u32[]{:S(2)}) copy-start(f32[512]{0:T(512)} %param.15) | copy-start | bytes 6148
  66.7 12.9 %collective-permute-start.9 = (bf16[384,256]{1,0:T(8,128)(2,1)S(1)}, bf16[384,256]{1,0:T(8,128)(2,1)S(1)}, u32[]{:S(2)}, u32[]{:S(2)}) collective-permute-start(bf16[384,256]{1,0:T(8,128)(2,1)S(1)} %get-tuple-element.43), channel_id=1, source_target_pairs={{0,4},{4,0},{8,12},{12,8},{1,5},{5,1},{9,13},{13,9},{2,6},{6,2},{1... | collective-permute-start | bytes 589832 | tf_op jit(solution)/shard_map/ppermute | solution.py:302

commit v5 on v4

--- a/solution.py
+++ b/solution.py
@@ -28,38 +28,18 @@
     return jnp.where(match, 1.0, 0.0).astype(BF16)
 
 
-def parted(k, count):
-    return count > 2 and k >= 2
-
-
-def layout(count):
-    far = [(k, h) for h in range(HALVES) for k in reversed(range(count)) if parted(k, count)]
-    return far + [(k, None) for k in reversed(range(count)) if not parted(k, count)]
-
-
-def pack_kernel(chan_count, send, off_ref, route_hbm, amps_hbm, *refs):
-    items = layout(off_ref.shape[0])
-    outs, (target_ref, route_ref, amps_ref, *kept) = refs[: len(items) + 1], refs[len(items) + 1 :]
-    target_hbm, block_hbm = outs[0], outs[1:]
-    block_refs, (in_sems, out_sems) = kept[: len(items)], kept[len(items) :]
-    rows, holes = amps_ref.shape
-    width = holes // HALVES
-    parts = [pl.ds(h * width, width) for h in range(HALVES)]
-    copies = [pltpu.make_async_copy(route_hbm, route_ref, in_sems.at[0])] + [
-        pltpu.make_async_copy(amps_hbm.at[:, part], amps_ref.at[:, part], in_sems.at[1 + h])
-        for h, part in enumerate(parts)
-    ]
-    for copy in copies:
-        copy.start()
+def block_offsets(paired, chan_count, block_rows):
+    chan = lax.axis_index("chan")
+    return [(chan ^ k) * block_rows for k in range(chan_count)] if paired else [0]
+
+
+def slots_of(owners, send, names):
     lane = 128
-    pieces = rows // lane
+    pieces = owners.shape[1] // lane
     before = selection(
         lax.broadcasted_iota(jnp.int32, (lane, 2 * lane), 0)
         < lax.broadcasted_iota(jnp.int32, (lane, 2 * lane), 1)
     )
-    names = max(16, chan_count)
-    copies[0].wait()
-    owners = route_ref[...]
     hot = [
         lax.broadcasted_iota(jnp.int32, (names, lane), 0) == owners[:, i * lane : (i + 1) * lane]
         for i in range(pieces)
@@ -73,46 +53,60 @@
         within = counts[i * names : (i + 1) * names]
         slots.append(jnp.sum(jnp.where(hot[i], within[:, :lane] + passed, 0.0), axis=0, keepdims=True))
         passed = passed + within[:, lane:]
-    target = owners * send + jnp.concatenate(slots, axis=1).astype(jnp.int32)
-    target_ref[...] = target
-    out_copies = [pltpu.make_async_copy(target_ref, target_hbm, out_sems.at[len(items)])]
-    out_copies[0].start()
-    for copy in copies[1:]:
-        copy.wait()
-    slot = lax.broadcasted_iota(jnp.int32, (block_refs[0].shape[0], rows), 0)
-    picks = {}
-    for i, (k, half) in enumerate(items):
-        if k not in picks:
-            picks[k] = selection(slot == target - off_ref[k])
-        rows_in = amps_ref[...] if half is None else amps_ref[:, parts[half]]
-        block_refs[i][...] = jnp.dot(picks[k], rows_in, preferred_element_type=F32).astype(BF16)
+    return owners * send + jnp.concatenate(slots, axis=1).astype(jnp.int32)
+
+
+def pack_kernel(plan, given, route_hbm, amps_hbm, *refs):
+    paired, chan_count, send, block_rows, items = plan
+    extra = 0 if given else 1
+    outs, (route_ref, amps_ref, *kept) = refs[: len(items) + extra], refs[len(items) + extra :]
+    block_hbm, block_refs, (in_sems, out_sems) = outs[extra:], kept[: len(items)], kept[len(items) :]
+    copies = [
+        pltpu.make_async_copy(route_hbm, route_ref, in_sems.at[0]),
+        pltpu.make_async_copy(amps_hbm.at[:, pl.ds(0, amps_ref.shape[1])], amps_ref, in_sems.at[1]),
+    ]
+    for copy in copies:
+        copy.start()
+    copies[0].wait()
+    target = route_ref[...]
+    out_copies = []
+    if not given:
+        target = slots_of(target, send, max(16, chan_count))
+        route_ref[...] = target
+        out_copies.append(pltpu.make_async_copy(route_ref, outs[0], out_sems.at[len(items)]))
+        out_copies[0].start()
+    offsets = block_offsets(paired, chan_count, block_rows)
+    slot = lax.broadcasted_iota(jnp.int32, (block_rows, target.shape[1]), 0)
+    for i, (k, first, width) in enumerate(items):
+        pick = selection(slot == target - offsets[k])
+        if i == 0:
+            copies[1].wait()
+        block_refs[i][...] = jnp.dot(
+            pick, amps_ref[:, pl.ds(first, width)], preferred_element_type=F32
+        ).astype(BF16)
         out_copies.append(pltpu.make_async_copy(block_refs[i], block_hbm[i], out_sems.at[i]))
         out_copies[-1].start()
     for copy in out_copies:
         copy.wait()
 
 
-def pack(offsets, route_row, amps, chan_count, send, block_rows):
-    rows, holes = amps.shape
-    items = layout(offsets.shape[0])
-    shapes = [(block_rows, holes if half is None else holes // HALVES) for _, half in items]
-    outs = pl.pallas_call(
-        functools.partial(pack_kernel, chan_count, send),
-        out_shape=[jax.ShapeDtypeStruct((1, rows), jnp.int32)]
-        + [jax.ShapeDtypeStruct(shape, BF16) for shape in shapes],
-        in_specs=[whole(pltpu.SMEM), whole(pl.ANY), whole(pl.ANY)],
-        out_specs=[whole(pl.ANY)] * (1 + len(items)),
-        scratch_shapes=[
-            pltpu.VMEM((1, rows), jnp.int32),
-            pltpu.VMEM((1, rows), jnp.int32),
-            pltpu.VMEM((rows, holes), BF16),
-        ]
+def pack(plan, given, route_row, amps, name):
+    rows = amps.shape[0]
+    block_rows, items = plan[3], plan[4]
+    columns = max(first + width for _, first, width in items)
+    shapes = [(block_rows, width) for _, _, width in items]
+    extra = [] if given else [jax.ShapeDtypeStruct((1, rows), jnp.int32)]
+    return pl.pallas_call(
+        functools.partial(pack_kernel, plan, given),
+        out_shape=extra + [jax.ShapeDtypeStruct(shape, BF16) for shape in shapes],
+        in_specs=[whole(pl.ANY), whole(pl.ANY)],
+        out_specs=[whole(pl.ANY)] * (len(extra) + len(items)),
+        scratch_shapes=[pltpu.VMEM((1, rows), jnp.int32), pltpu.VMEM((rows, columns), BF16)]
         + [pltpu.VMEM(shape, BF16) for shape in shapes]
-        + [pltpu.SemaphoreType.DMA((1 + HALVES,)), pltpu.SemaphoreType.DMA((1 + len(items),))],
-        compiler_params=params(VMEM_MOST),
-        name="pack",
-    )(offsets, route_row, amps)
-    return outs[0], dict(zip(items, outs[1:]))
+        + [pltpu.SemaphoreType.DMA((2,)), pltpu.SemaphoreType.DMA((1 + len(items),))],
+        compiler_params=params(VMEM_LIMIT if given else VMEM_MOST),
+        name=name,
+    )(route_row, amps)
 
 
 def unpack_kernel(off_ref, target_ref, out_ref):
@@ -156,7 +150,7 @@
             out_specs=pl.BlockSpec((1, rows, holes), lambda i, share: (i, 0, 0)),
         ),
         compiler_params=params(VMEM_MOST),
-        cost_estimate=CHEAP,
+        cost_estimate=DEAR,
         name="ladder_share",
     )(share, weight, amps)
 
@@ -302,10 +296,16 @@
         return lax.ppermute(block, "chan", [(i, i ^ k) for i in range(chan_count)]) if k else block
 
     far_first = list(reversed(range(block_index.shape[0])))
-    target, outgoing = pack(offsets, route[0].reshape(1, rows), amps, chan_count, send, block_rows)
-    arrived = {item: exchange(block, item[0]) for item, block in outgoing.items()}
-    amps, outgoing = lax.optimization_barrier((amps, outgoing))
-    pick = unpack_matrix(offsets, target.reshape(rows, 1), capacity)
+    count = len(far_first)
+    width = holes // HALVES
+    route_row = route[0].reshape(1, rows)
+    plan = (paired, chan_count, send, block_rows)
+    early = [(k, 0, width) for k in far_first if k or not paired]
+    late = [(k, h * width, width) for h in range(1, HALVES) for k in far_first if k or not paired]
+    late += [(0, 0, holes)] if paired else []
+    target, *blocks = pack(plan + (early,), False, route_row, amps, "pack_first")
+    arrived = {(k, 0): exchange(block, k) for (k, _, _), block in zip(early, blocks)}
+    amps, target = lax.optimization_barrier((amps, target))
 
     kept = None
     for step in reversed(range(sub_count)):
@@ -321,16 +321,22 @@
         return sum(p.astype(F32) for p in picked)
 
     base = driving[0].astype(F32) + chip_sum(lad)
-    for step in range(1, lad_count):
+    terms = [chip_sum(lax.rem(lad + step, lad_count)).astype(BF16) for step in range(1, lad_count)]
+    target, terms, weight = lax.optimization_barrier((target, terms, weight))
+    for step, term in enumerate(terms, 1):
         pairs = [(i, (i + step) % lad_count) for i in range(lad_count)]
-        term = chip_sum(lax.rem(lad + step, lad_count)).astype(BF16)
         base = base + lax.ppermute(term, "lad", pairs).astype(F32)
 
+    blocks = pack(plan + (late,), True, target, amps, "pack_rest")
+    for (k, first, _), block in zip(late, blocks):
+        arrived[(k, first // width)] = exchange(block, k)
+
+    pick = unpack_matrix(offsets, target.reshape(rows, 1), capacity)
     operator = cycle_operator(block_index, weight, mixing, block_rows)
     part_column, hole_row = gap_part[0].reshape(rows, 1), gap_hole.reshape(1, holes)
     returned = []
     for half in range(HALVES):
-        blocks = [arrived[(k, half if parted(k, len(far_first)) else None)] for k in far_first]
+        blocks = [arrived[(k, half if k or not paired else 0)] for k in far_first]
         if returned:
             blocks, made = lax.optimization_barrier((blocks, made))
         made = apply_cycle(half, operator, blocks, holes // HALVES)

time: 81.4 us -> 79.2 us (0.973)
  starting transfers between devices: 36.6 us -> 22.9 us
  waiting for transfers between devices: 13.4 us -> 25.4 us
  other arithmetic: 1.22 us -> 3.29 us
  local copies, waits for them, and re-layouts: 4.07 us -> 2.73 us
  Pallas kernels: 25.7 us -> 24.5 us
    ppermute x11 -> x12, starting transfers between devices: 34.9 us -> 21.2 us  [exchange(): lax.ppermute(block, 'chan', [(i, i ^ k) for i in range(chan_count)])]
    ppermute x11 -> x12, waiting for transfers between devices: 13.4 us -> 25.4 us  [exchange(): lax.ppermute(block, 'chan', [(i, i ^ k) for i in range(chan_count)])]
    pallas_call x2, Pallas kernels: 5.22 us -> 2.75 us  [apply_cycle(): pl.pallas_call(functools.partial(cycle_kernel, half), out_shape=[jax.Shap...]
    convert_element_type x1, other arithmetic: 0.22 us -> 1.66 us  [body(): chip_sum(lax.rem(lad + step, lad_count)).astype(BF16)]
    pallas_call x1 -> x2, Pallas kernels: 4.03 us -> 5.34 us  [pack(): pl.pallas_call(functools.partial(pack_kernel, plan, given), out_shape=ext...]
    add x1, other arithmetic: 0.4 us -> 1.55 us  [body(): base = base + lax.ppermute(term, 'lad', pairs).astype(F32)]
  transfers between devices with their start and end apart: 13 -> 14, of which waited for: 3 -> 3; matrix products, arithmetic and copies ran while one was open for 3% -> 5% of each run, Pallas kernels for 25% -> 26%
where the time goes in v5:
time: 79.2 us; the launch traced here: 79 us
  waiting for transfers between devices  25.4 us (32%)
  Pallas kernels  24.5 us (31%)
  starting transfers between devices  22.9 us (29%)
  other arithmetic  3.29 us (4%)
  local copies, waits for them, and re-layouts  2.73 us (3%)
    ppermute x12, waiting for transfers between devices, exchange(): lax.ppermute(block, 'chan', [(i, i ^ k) for i in range(chan_count)])  25.4 us
    ppermute x12, starting transfers between devices, exchange(): lax.ppermute(block, 'chan', [(i, i ^ k) for i in range(chan_count)])  21.2 us
    pallas_call x2, Pallas kernels, ladder_share(): pl.pallas_call(ladder_kernel, out_shape=jax.ShapeDtypeStruct((lad_count,...  7.91 us
    pallas_call x2, Pallas kernels, pack(): pl.pallas_call(functools.partial(pack_kernel, plan, given), out_shape=ext...  5.34 us
    pallas_call x1, Pallas kernels, cycle_operator(): pl.pallas_call(functools.partial(operator_kernel, group), out_shape=jax.S...  4.36 us
    pallas_call x2, Pallas kernels, finish(): pl.pallas_call(functools.partial(finish_kernel, half, len(arrays), tiles)...  3.03 us
    pallas_call x2, Pallas kernels, apply_cycle(): pl.pallas_call(functools.partial(cycle_kernel, half), out_shape=[jax.Shap...  2.75 us
    unnamed x16, local copies, waits for them, and re-layouts  2.37 us
  transfers between devices with their start and end apart: 14, of which 3 were waited for; matrix products, arithmetic and copies ran while one was open for 5% of the time, Pallas kernels for 26%

profile of v5, /device:TPU:0, one launch (start us, length us, event | category | flops | bytes accessed | tf_op | source)
XLA Modules:
  0.0 79.0 jit_solution(10983927096256220858)
XLA Ops:
  0.0 2.4 %pack_first.1 = (s32[1,768]{1,0:T(1,128)}, bf16[384,256]{1,0:T(8,128)(2,1)}, bf16[384,256]{1,0:T(8,128)(2,1)}, bf16[384,256]{1,0:T(8,128)(2,1)}) custom-call(s32[1,768]{1,0:T(1,128)} %bitcast.28, bf16[768,512]{1,0:T(8,128)(2,1)} %bitcast.20), custom_call_target="tpu_custom_call" | custom-call | tf_op jit(solution)/shard_map/pack_first/pallas_call | solution.py:99
  2.4 5.1 %collective-permute-start.5 = (bf16[384,256]{1,0:T(8,128)(2,1)}, bf16[384,256]{1,0:T(8,128)(2,1)S(1)}, u32[]{:S(2)}, u32[]{:S(2)}) collective-permute-start(bf16[384,256]{1,0:T(8,128)(2,1)} %get-tuple-element.40), channel_id=1, source_target_pairs={{0,12},{4,8},{8,4},{12,0},{1,13},{5,9},{9,5},{13,1},{2,14},{6,10},... | collective-permute-start | bytes 589832 | tf_op jit(solution)/shard_map/ppermute | solution.py:296
  7.5 0.0 collective-permute-start.6
  7.5 0.6 collective-permute-start.7
  8.2 0.0 copy-start.7
  8.2 4.0 %ladder_share.2 = bf16[2,768,512]{2,1,0:T(8,128)(2,1)} custom-call(s32[1]{0:T(128)} %bitcast.6.share_ref, bf16[3072,768]{1,0:T(8,128)(2,1)} %bitcast.30, bf16[768,512]{1,0:T(8,128)(2,1)} %bitcast.21), custom_call_target="tpu_custom_call" | custom-call | flops 30000001024 | bytes 1000000 | tf_op jit(solution)/shard_map/ladder_share/pallas_call | solution.py:140
  12.2 0.0 collective-permute-start
  12.2 0.0 copy-done.7
  12.2 0.2 copy.12.part_ref
  12.4 4.0 %ladder_share.3 = bf16[2,768,512]{2,1,0:T(8,128)(2,1)} custom-call(s32[1]{0:T(128)} %bitcast.8.share_ref, bf16[3072,768]{1,0:T(8,128)(2,1)} %bitcast.31, bf16[768,512]{1,0:T(8,128)(2,1)} %bitcast.22), custom_call_target="tpu_custom_call" | custom-call | flops 30000001024 | bytes 1000000 | tf_op jit(solution)/shard_map/ladder_share/pallas_call | solution.py:140
  16.3 0.0 copy-start.1
  16.3 0.0 copy-start.3
  16.3 0.1 broadcast_multiply_fusion
  16.4 0.0 copy-start.2
  16.4 0.0 collective-permute-done
  16.4 1.7 %fusion = bf16[768,512]{1,0:T(8,128)(2,1)S(1)} fusion(bf16[2,768,512]{2,1,0:T(8,128)(2,1)} %ladder_share.3, s32[]{:T(128)S(6)} %select_n.9, bf16[2,768,512]{2,1,0:T(8,128)(2,1)} %collective-permute-done), kind=kLoop, calls=%fused_computation.2 | loop fusion | flops 1572864 | bytes 2359300 | tf_op jit(solution)/shard_map/convert_element_type | solution.py:324
  18.1 0.0 copy-done.1
  18.1 0.0 copy-done.3
  18.1 2.9 %pack_rest.1 = (bf16[384,256]{1,0:T(8,128)(2,1)S(1)}, bf16[384,256]{1,0:T(8,128)(2,1)S(1)}, bf16[384,256]{1,0:T(8,128)(2,1)S(1)}, bf16[384,512]{1,0:T(8,128)(2,1)S(1)}) custom-call(s32[1,768]{1,0:T(1,128)S(1)} %copy-done.3, bf16[768,512]{1,0:T(8,128)(2,1)S(1)} %bitcast.23), custom_call_target="tpu_custom_call" | custom-call | tf_op jit(solution)/shard_map/pack_rest/pallas_call | solution.py:99
  21.0 0.2 copy.10.target_ref
  21.2 1.7 %collective-permute-start.1 = (bf16[768,512]{1,0:T(8,128)(2,1)S(1)}, bf16[768,512]{1,0:T(8,128)(2,1)S(1)}, u32[]{:S(2)}, u32[]{:S(2)}) collective-permute-start(bf16[768,512]{1,0:T(8,128)(2,1)S(1)} %fusion), channel_id=1, source_target_pairs={{0,2},{2,0},{1,3},{3,1},{4,6},{6,4},{5,7},{7,5},{8,10},{10,8},{9,1... | collective-permute-start | bytes 2359304 | tf_op jit(solution)/shard_map/ppermute | solution.py:328
  22.9 3.6 %collective-permute-start.2 = (bf16[384,256]{1,0:T(8,128)(2,1)S(1)}, bf16[384,256]{1,0:T(8,128)(2,1)S(1)}, u32[]{:S(2)}, u32[]{:S(2)}) collective-permute-start(bf16[384,256]{1,0:T(8,128)(2,1)S(1)} %get-tuple-element.36), channel_id=1, source_target_pairs={{0,12},{4,8},{8,4},{12,0},{1,13},{5,9},{9,5},{13,1},{2,14},{6,10},... | collective-permute-start | bytes 589832 | tf_op jit(solution)/shard_map/ppermute | solution.py:296
  26.5 0.0 copy-done.2
  26.5 0.0 copy-start
  26.5 2.3 %copy-done = bf16[1,1,1536,1536]{3,2,1,0:T(8,128)(2,1)S(1)} copy-done((bf16[1,1,1536,1536]{3,2,1,0:T(8,128)(2,1)S(1)}, bf16[1,1,1536,1536]{3,2,1,0:T(8,128)(2,1)}, u32[]{:S(2)}) %copy-start) | copy-done | bytes 4718616
  28.8 4.4 %cycle_operator.1.operator_ref = bf16[1536,1536]{1,0:T(8,128)(2,1)S(1)} custom-call(s32[4]{0:T(128)S(1)} %get-tuple-element.56.block_index, bf16[1536,1536]{1,0:T(8,128)(2,1)S(1)} %bitcast.19, bf16[12,128,128]{2,1,0:T(8,128)(2,1)S(1)} %bitcast.24), custom_call_target="tpu_custom_call" | custom-call | tf_op jit(solution)/shard_map/cycle_operator/pallas_call | solution.py:182
  33.2 0.0 collective-permute-done.5.refs_0_
  33.2 0.1 collective-permute-start.3
  33.3 0.0 collective-permute-done.6.refs_1_
  33.3 0.8 collective-permute-start.4
  34.1 0.0 collective-permute-done.7.refs_2_
  34.1 1.4 %apply_cycle.2 = (bf16[384,256]{1,0:T(8,128)(2,1)S(1)}, bf16[384,256]{1,0:T(8,128)(2,1)S(1)}, bf16[384,256]{1,0:T(8,128)(2,1)S(1)}, bf16[384,256]{1,0:T(8,128)(2,1)S(1)}) custom-call(bf16[1536,1536]{1,0:T(8,128)(2,1)S(1)} %cycle_operator.1.operator_ref, bf16[384,256]{1,0:T(8,128)(2,1)S(1)} %collective-permute-done.5.refs_0_, ...), custom_call_target="tpu_custom_call" | custom-call | flops 30000001024 | bytes 1000000 | tf_op jit(solution)/shard_map/apply_cycle/pallas_call | solution.py:214
  35.4 3.7 %collective-permute-start.11 = (bf16[384,256]{1,0:T(8,128)(2,1)S(1)}, bf16[384,256]{1,0:T(8,128)(2,1)S(1)}, u32[]{:S(2)}, u32[]{:S(2)}) collective-permute-start(bf16[384,256]{1,0:T(8,128)(2,1)S(1)} %get-tuple-element.43), channel_id=1, source_target_pairs={{0,12},{4,8},{8,4},{12,0},{1,13},{5,9},{9,5},{13,1},{2,14},{6,10},... | collective-permute-start | bytes 589832 | tf_op jit(solution)/shard_map/ppermute | solution.py:296
  39.1 1.1 %unpack_matrix.1.pick_ref = bf16[768,1536]{1,0:T(8,128)(2,1)S(1)} custom-call(s32[4]{0:T(128)S(1)} %get-tuple-element.55.off_ref, s32[768,1]{1,0:T(8,128)S(1)} %copy.10.target_ref), custom_call_target="tpu_custom_call" | custom-call | tf_op jit(solution)/shard_map/unpack_matrix/pallas_call | solution.py:123
  40.2 0.0 collective-permute-done.2.refs_0_
  40.2 0.1 collective-permute-start.12
  40.3 11.0 %collective-permute-done.3.refs_1_ = bf16[384,256]{1,0:T(8,128)(2,1)S(1)} collective-permute-done((bf16[384,256]{1,0:T(8,128)(2,1)S(1)}, bf16[384,256]{1,0:T(8,128)(2,1)S(1)}, u32[]{:S(2)}, u32[]{:S(2)}) %collective-permute-start.3) | collective-permute-done | bytes 196640 | tf_op jit(solution)/shard_map/ppermute | solution.py:296
  51.3 0.0 collective-permute-start.13
  51.3 0.0 collective-permute-done.4.refs_2_
  51.3 0.0 copy-start.5
  51.3 0.0 copy-start.6
  51.3 1.4 %apply_cycle.3 = (bf16[384,256]{1,0:T(8,128)(2,1)S(1)}, bf16[384,256]{1,0:T(8,128)(2,1)S(1)}, bf16[384,256]{1,0:T(8,128)(2,1)S(1)}, bf16[384,256]{1,0:T(8,128)(2,1)S(1)}) custom-call(bf16[1536,1536]{1,0:T(8,128)(2,1)S(1)} %cycle_operator.1.operator_ref, bf16[384,256]{1,0:T(8,128)(2,1)S(1)} %collective-permute-done.2.refs_0_, ...), custom_call_target="tpu_custom_call" | custom-call | flops 30000001024 | bytes 1000000 | tf_op jit(solution)/shard_map/apply_cycle/pallas_call | solution.py:214
  52.7 0.1 collective-permute-start.8
  52.8 0.0 collective-permute-done.11.refs_0_
  52.8 7.2 %collective-permute-start.9 = (bf16[384,256]{1,0:T(8,128)(2,1)S(1)}, bf16[384,256]{1,0:T(8,128)(2,1)S(1)}, u32[]{:S(2)}, u32[]{:S(2)}) collective-permute-start(bf16[384,256]{1,0:T(8,128)(2,1)S(1)} %get-tuple-element.52), channel_id=1, source_target_pairs={{0,8},{4,12},{8,0},{12,4},{1,9},{5,13},{9,1},{13,5},{2,10},{6,14},... | collective-permute-start | bytes 589832 | tf_op jit(solution)/shard_map/ppermute | solution.py:296
  60.0 0.0 collective-permute-done.1
  60.0 0.0 copy-start.4
  60.0 0.0 collective-permute-start.10
  60.0 0.0 copy-done.5
  60.0 0.0 copy-done.6
  60.0 1.6 %bitcast_add_fusion.base_ref = f32[768,512]{1,0:T(8,128)S(1)} fusion(bf16[768,512]{1,0:T(8,128)(2,1)S(1)} %collective-permute-done.1, bf16[1,768,512]{2,1,0:T(8,128)(2,1)S(1)} %copy-done.6, bf16[2,768,512]{2,1,0:T(8,128)(2,1)S(1)} %copy-done.5, s32[]{:T(128)S(6)} %select_n.10, bf16[2,768,512]{2,1,0:T(8,128)(2,1)} %collective-permute-done), kind=kLoop, calls=%fused_computation | loop fusion | flops 2752512 | bytes 4718596 | tf_op jit(solution)/shard_map/add | solution.py:328
  61.6 7.6 %collective-permute-done.12.refs_1_ = bf16[384,256]{1,0:T(8,128)(2,1)S(1)} collective-permute-done((bf16[384,256]{1,0:T(8,128)(2,1)S(1)}, bf16[384,256]{1,0:T(8,128)(2,1)S(1)}, u32[]{:S(2)}, u32[]{:S(2)}) %collective-permute-start.12) | collective-permute-done | bytes 196640 | tf_op jit(solution)/shard_map/ppermute | solution.py:296
  69.2 0.0 collective-permute-done.13.refs_2_
  69.2 0.0 copy-done.4
  69.2 1.5 %finish.2.refs_4_ = bf16[768,512]{1,0:T(8,128)(2,1)} custom-call(bf16[768,1536]{1,0:T(8,128)(2,1)S(1)} %unpack_matrix.1.pick_ref, f32[768,512]{1,0:T(8,128)S(1)} %bitcast_add_fusion.base_ref, f32[768,1]{1,0:T(8,128)S(1)} %copy.12.part_ref, f32[1,512]{1,0:T(1,128)S(1)} %bitcast.26, bf16[384,256]{1,0:T(8,128)(2,1)S(1)} %collective-permute-done.11.refs_0_, ...), custom_call_target="tpu_custom_call" | custom-call | tf_op jit(solution)/shard_map/finish/pallas_call | solution.py:255
  70.7 0.0 collective-permute-done.8.refs_0_
  70.7 6.8 %collective-permute-done.9.refs_1_ = bf16[384,256]{1,0:T(8,128)(2,1)S(1)} collective-permute-done((bf16[384,256]{1,0:T(8,128)(2,1)S(1)}, bf16[384,256]{1,0:T(8,128)(2,1)S(1)}, u32[]{:S(2)}, u32[]{:S(2)}) %collective-permute-start.9) | collective-permute-done | bytes 196640 | tf_op jit(solution)/shard_map/ppermute | solution.py:296
  77.5 0.0 collective-permute-done.10.refs_2_
  77.5 1.5 %finish.3 = bf16[768,512]{1,0:T(8,128)(2,1)} custom-call(bf16[768,1536]{1,0:T(8,128)(2,1)S(1)} %unpack_matrix.1.pick_ref, f32[768,512]{1,0:T(8,128)S(1)} %bitcast_add_fusion.base_ref, f32[768,1]{1,0:T(8,128)S(1)} %copy.12.part_ref, f32[1,512]{1,0:T(1,128)S(1)} %bitcast.27, ...), custom_call_target="tpu_custom_call", output_to_operand_aliasing={{}: (8, {})} | custom-call | tf_op jit(solution)/shard_map/finish/pallas_call | solution.py:255
Async XLA Ops:
  2.4 30.8 %collective-permute-start.5 = (bf16[384,256]{1,0:T(8,128)(2,1)}, bf16[384,256]{1,0:T(8,128)(2,1)S(1)}, u32[]{:S(2)}, u32[]{:S(2)}) collective-permute-start(bf16[384,256]{1,0:T(8,128)(2,1)} %get-tuple-element.40), channel_id=1, source_target_pairs={{0,12},{4,8},{8,4},{12,0},{1,13},{5,9},{9,5},{13,1},{2,14},{6,10},... | collective-permute-start | bytes 589832 | tf_op jit(solution)/shard_map/ppermute | solution.py:296
  7.5 25.7 %collective-permute-start.6 = (bf16[384,256]{1,0:T(8,128)(2,1)}, bf16[384,256]{1,0:T(8,128)(2,1)S(1)}, u32[]{:S(2)}, u32[]{:S(2)}) collective-permute-start(bf16[384,256]{1,0:T(8,128)(2,1)} %get-tuple-element.41), channel_id=1, source_target_pairs={{0,8},{4,12},{8,0},{12,4},{1,9},{5,13},{9,1},{13,5},{2,10},{6,14},... | collective-permute-start | bytes 589832 | tf_op jit(solution)/shard_map/ppermute | solution.py:296
  7.5 26.5 %collective-permute-start.7 = (bf16[384,256]{1,0:T(8,128)(2,1)}, bf16[384,256]{1,0:T(8,128)(2,1)S(1)}, u32[]{:S(2)}, u32[]{:S(2)}) collective-permute-start(bf16[384,256]{1,0:T(8,128)(2,1)} %get-tuple-element.42), channel_id=1, source_target_pairs={{0,4},{4,0},{8,12},{12,8},{1,5},{5,1},{9,13},{13,9},{2,6},{6,2},{1... | collective-permute-start | bytes 589832 | tf_op jit(solution)/shard_map/ppermute | solution.py:296
  8.2 4.0 %copy-start.7 = (f32[1,768]{1,0:T(1,128)S(1)}, f32[1,768]{1,0:T(1,128)}, u32[]{:S(2)}) copy-start(f32[1,768]{1,0:T(1,128)} %param.14) | copy-start | bytes 9220
  12.2 4.2 %collective-permute-start = (bf16[2,768,512]{2,1,0:T(8,128)(2,1)}, bf16[2,768,512]{2,1,0:T(8,128)(2,1)}, u32[]{:S(2)}, u32[]{:S(2)}) collective-permute-start(bf16[2,768,512]{2,1,0:T(8,128)(2,1)} %ladder_share.2), channel_id=1, source_target_pairs={{0,1},{1,0},{2,3},{3,2},{4,5},{5,4},{6,7},{7,6},{8,9},{9,8},{10,11... | collective-permute-start | bytes 4718600 | tf_op jit(solution)/shard_map/ppermute | solution.py:316
  16.3 1.8 %copy-start.1 = (bf16[1,768,512]{2,1,0:T(8,128)(2,1)S(1)}, bf16[1,768,512]{2,1,0:T(8,128)(2,1)}, u32[]{:S(2)}) copy-start(bf16[1,768,512]{2,1,0:T(8,128)(2,1)} %param.8) | copy-start | bytes 2359300
  16.3 1.8 %copy-start.3 = (s32[1,768]{1,0:T(1,128)S(1)}, s32[1,768]{1,0:T(1,128)}, u32[]{:S(2)}) copy-start(s32[1,768]{1,0:T(1,128)} %get-tuple-element.33.route_hbm) | copy-start | bytes 9220
  16.4 10.1 %copy-start.2 = (bf16[1,1,12,128,128]{4,3,2,1,0:T(8,128)(2,1)S(1)}, bf16[1,1,12,128,128]{4,3,2,1,0:T(8,128)(2,1)}, u32[]{:S(2)}) copy-start(bf16[1,1,12,128,128]{4,3,2,1,0:T(8,128)(2,1)} %param.13) | copy-start | bytes 1179652
  21.2 38.8 %collective-permute-start.1 = (bf16[768,512]{1,0:T(8,128)(2,1)S(1)}, bf16[768,512]{1,0:T(8,128)(2,1)S(1)}, u32[]{:S(2)}, u32[]{:S(2)}) collective-permute-start(bf16[768,512]{1,0:T(8,128)(2,1)S(1)} %fusion), channel_id=1, source_target_pairs={{0,2},{2,0},{1,3},{3,1},{4,6},{6,4},{5,7},{7,5},{8,10},{10,8},{9,1... | collective-permute-start | bytes 2359304 | tf_op jit(solution)/shard_map/ppermute | solution.py:328
  22.9 17.3 %collective-permute-start.2 = (bf16[384,256]{1,0:T(8,128)(2,1)S(1)}, bf16[384,256]{1,0:T(8,128)(2,1)S(1)}, u32[]{:S(2)}, u32[]{:S(2)}) collective-permute-start(bf16[384,256]{1,0:T(8,128)(2,1)S(1)} %get-tuple-element.36), channel_id=1, source_target_pairs={{0,12},{4,8},{8,4},{12,0},{1,13},{5,9},{9,5},{13,1},{2,14},{6,10},... | collective-permute-start | bytes 589832 | tf_op jit(solution)/shard_map/ppermute | solution.py:296
  26.5 2.3 %copy-start = (bf16[1,1,1536,1536]{3,2,1,0:T(8,128)(2,1)S(1)}, bf16[1,1,1536,1536]{3,2,1,0:T(8,128)(2,1)}, u32[]{:S(2)}) copy-start(bf16[1,1,1536,1536]{3,2,1,0:T(8,128)(2,1)} %param.12) | copy-start | bytes 14155780
  33.2 18.1 %collective-permute-start.3 = (bf16[384,256]{1,0:T(8,128)(2,1)S(1)}, bf16[384,256]{1,0:T(8,128)(2,1)S(1)}, u32[]{:S(2)}, u32[]{:S(2)}) collective-permute-start(bf16[384,256]{1,0:T(8,128)(2,1)S(1)} %get-tuple-element.37), channel_id=1, source_target_pairs={{0,8},{4,12},{8,0},{12,4},{1,9},{5,13},{9,1},{13,5},{2,10},{6,14},... | collective-permute-start | bytes 589832 | tf_op jit(solution)/shard_map/ppermute | solution.py:296
  33.3 18.0 %collective-permute-start.4 = (bf16[384,256]{1,0:T(8,128)(2,1)S(1)}, bf16[384,256]{1,0:T(8,128)(2,1)S(1)}, u32[]{:S(2)}, u32[]{:S(2)}) collective-permute-start(bf16[384,256]{1,0:T(8,128)(2,1)S(1)} %get-tuple-element.38), channel_id=1, source_target_pairs={{0,4},{4,0},{8,12},{12,8},{1,5},{5,1},{9,13},{13,9},{2,6},{6,2},{1... | collective-permute-start | bytes 589832 | tf_op jit(solution)/shard_map/ppermute | solution.py:296
  35.4 17.4 %collective-permute-start.11 = (bf16[384,256]{1,0:T(8,128)(2,1)S(1)}, bf16[384,256]{1,0:T(8,128)(2,1)S(1)}, u32[]{:S(2)}, u32[]{:S(2)}) collective-permute-start(bf16[384,256]{1,0:T(8,128)(2,1)S(1)} %get-tuple-element.43), channel_id=1, source_target_pairs={{0,12},{4,8},{8,4},{12,0},{1,13},{5,9},{9,5},{13,1},{2,14},{6,10},... | collective-permute-start | bytes 589832 | tf_op jit(solution)/shard_map/ppermute | solution.py:296
  40.2 28.9 %collective-permute-start.12 = (bf16[384,256]{1,0:T(8,128)(2,1)S(1)}, bf16[384,256]{1,0:T(8,128)(2,1)S(1)}, u32[]{:S(2)}, u32[]{:S(2)}) collective-permute-start(bf16[384,256]{1,0:T(8,128)(2,1)S(1)} %get-tuple-element.44), channel_id=1, source_target_pairs={{0,8},{4,12},{8,0},{12,4},{1,9},{5,13},{9,1},{13,5},{2,10},{6,14},... | collective-permute-start | bytes 589832 | tf_op jit(solution)/shard_map/ppermute | solution.py:296
  51.3 17.9 %collective-permute-start.13 = (bf16[384,256]{1,0:T(8,128)(2,1)S(1)}, bf16[384,256]{1,0:T(8,128)(2,1)S(1)}, u32[]{:S(2)}, u32[]{:S(2)}) collective-permute-start(bf16[384,256]{1,0:T(8,128)(2,1)S(1)} %get-tuple-element.45), channel_id=1, source_target_pairs={{0,4},{4,0},{8,12},{12,8},{1,5},{5,1},{9,13},{13,9},{2,6},{6,2},{1... | collective-permute-start | bytes 589832 | tf_op jit(solution)/shard_map/ppermute | solution.py:296
  51.3 8.7 %copy-start.5 = (bf16[2,768,512]{2,1,0:T(8,128)(2,1)S(1)}, bf16[2,768,512]{2,1,0:T(8,128)(2,1)}, u32[]{:S(2)}) copy-start(bf16[2,768,512]{2,1,0:T(8,128)(2,1)} %ladder_share.3) | copy-start | bytes 4718596
  51.3 8.7 %copy-start.6 = (bf16[1,768,512]{2,1,0:T(8,128)(2,1)S(1)}, bf16[1,768,512]{2,1,0:T(8,128)(2,1)}, u32[]{:S(2)}) copy-start(bf16[1,768,512]{2,1,0:T(8,128)(2,1)} %param.9) | copy-start | bytes 2359300
  52.7 18.0 %collective-permute-start.8 = (bf16[384,256]{1,0:T(8,128)(2,1)S(1)}, bf16[384,256]{1,0:T(8,128)(2,1)S(1)}, u32[]{:S(2)}, u32[]{:S(2)}) collective-permute-start(bf16[384,256]{1,0:T(8,128)(2,1)S(1)} %get-tuple-element.51), channel_id=1, source_target_pairs={{0,12},{4,8},{8,4},{12,0},{1,13},{5,9},{9,5},{13,1},{2,14},{6,10},... | collective-permute-start | bytes 589832 | tf_op jit(solution)/shard_map/ppermute | solution.py:296
  52.8 24.7 %collective-permute-start.9 = (bf16[384,256]{1,0:T(8,128)(2,1)S(1)}, bf16[384,256]{1,0:T(8,128)(2,1)S(1)}, u32[]{:S(2)}, u32[]{:S(2)}) collective-permute-start(bf16[384,256]{1,0:T(8,128)(2,1)S(1)} %get-tuple-element.52), channel_id=1, source_target_pairs={{0,8},{4,12},{8,0},{12,4},{1,9},{5,13},{9,1},{13,5},{2,10},{6,14},... | collective-permute-start | bytes 589832 | tf_op jit(solution)/shard_map/ppermute | solution.py:296
  60.0 9.2 %copy-start.4 = (f32[512]{0:T(512)S(1)}, f32[512]{0:T(512)}, u32[]{:S(2)}) copy-start(f32[512]{0:T(512)} %param.15) | copy-start | bytes 6148
  60.0 17.5 %collective-permute-start.10 = (bf16[384,256]{1,0:T(8,128)(2,1)S(1)}, bf16[384,256]{1,0:T(8,128)(2,1)S(1)}, u32[]{:S(2)}, u32[]{:S(2)}) collective-permute-start(bf16[384,256]{1,0:T(8,128)(2,1)S(1)} %get-tuple-element.53), channel_id=1, source_target_pairs={{0,4},{4,0},{8,12},{12,8},{1,5},{5,1},{9,13},{13,9},{2,6},{6,2},{1... | collective-permute-start | bytes 589832 | tf_op jit(solution)/shard_map/ppermute | solution.py:296

commit v6 on v5

--- a/solution.py
+++ b/solution.py
@@ -9,6 +9,8 @@
 
 VMEM_LIMIT = 24 * 1024 * 1024
 VMEM_MOST = 60 * 1024 * 1024
+VMEM_LADDER = 49 * 1024 * 1024
+VMEM_OPERATOR = 44 * 1024 * 1024
 HALVES = 2
 F32 = jnp.float32
 BF16 = jnp.bfloat16
@@ -137,19 +139,21 @@
 
 def ladder_share(share, weight, amps, lad_count, sub_count):
     rows, holes = amps.shape
+    tile = 256 if rows % 256 == 0 else 128
+    steps = rows // tile
     return pl.pallas_call(
         ladder_kernel,
         out_shape=jax.ShapeDtypeStruct((lad_count, rows, holes), BF16),
         grid_spec=pltpu.PrefetchScalarGridSpec(
             num_scalar_prefetch=1,
-            grid=(lad_count,),
+            grid=(lad_count, steps),
             in_specs=[
-                pl.BlockSpec((rows, rows), lambda i, share: (i * sub_count + share[0], 0)),
-                pl.BlockSpec((rows, holes), lambda i, share: (0, 0)),
+                pl.BlockSpec((tile, rows), lambda i, t, share: ((i * sub_count + share[0]) * steps + t, 0)),
+                pl.BlockSpec((rows, holes), lambda i, t, share: (0, 0)),
             ],
-            out_specs=pl.BlockSpec((1, rows, holes), lambda i, share: (i, 0, 0)),
+            out_specs=pl.BlockSpec((1, tile, holes), lambda i, t, share: (i, t, 0)),
         ),
-        compiler_params=params(VMEM_MOST),
+        compiler_params=params(VMEM_LADDER),
         cost_estimate=DEAR,
         name="ladder_share",
     )(share, weight, amps)
@@ -192,7 +196,7 @@
             out_specs=pl.BlockSpec((block_rows, capacity), lambda k, index: (k, 0)),
             scratch_shapes=[pltpu.VMEM((block_rows, capacity), BF16)],
         ),
-        compiler_params=params(),
+        compiler_params=params(VMEM_OPERATOR),
         cost_estimate=CHEAP,
         name="cycle_operator",
     )(block_index, weight, mixing)
@@ -332,6 +336,9 @@
         arrived[(k, first // width)] = exchange(block, k)
 
     pick = unpack_matrix(offsets, target.reshape(rows, 1), capacity)
+    if paired:
+        near = (1, 0)
+        weight, arrived[near] = lax.optimization_barrier((weight, arrived[near]))
     operator = cycle_operator(block_index, weight, mixing, block_rows)
     part_column, hole_row = gap_part[0].reshape(rows, 1), gap_hole.reshape(1, holes)
     returned = []

time: 79.2 us -> 86.5 us (1.092)
  local copies, waits for them, and re-layouts: 2.73 us -> 6.59 us
  Pallas kernels: 24.5 us -> 28 us
  starting transfers between devices: 22.9 us -> 20.6 us
  waiting for transfers between devices: 25.4 us -> 26.8 us
    unnamed x16 -> x28, local copies, waits for them, and re-layouts: 2.37 us -> 6.23 us
    pallas_call x2, Pallas kernels: 7.91 us -> 10.4 us  [ladder_share(): pl.pallas_call(ladder_kernel, out_shape=jax.ShapeDtypeStruct((lad_count,...]
    ppermute x12, starting transfers between devices: 21.2 us -> 19.1 us  [exchange(): lax.ppermute(block, 'chan', [(i, i ^ k) for i in range(chan_count)])]
    ppermute x12, waiting for transfers between devices: 25.4 us -> 26.8 us  [exchange(): lax.ppermute(block, 'chan', [(i, i ^ k) for i in range(chan_count)])]
    pallas_call x2, Pallas kernels: 2.75 us -> 3.77 us  [apply_cycle(): pl.pallas_call(functools.partial(cycle_kernel, half), out_shape=[jax.Shap...]
  transfers between devices with their start and end apart: 14 -> 14, of which waited for: 3 -> 3; matrix products, arithmetic and copies ran while one was open for 5% -> 5% of each run, Pallas kernels for 26% -> 28%
where the time goes in v6:
time: 86.5 us; the launch traced here: 86 us
  Pallas kernels  28 us (32%)
  waiting for transfers between devices  26.8 us (31%)
  starting transfers between devices  20.6 us (24%)
  local copies, waits for them, and re-layouts  6.59 us (8%)
  other arithmetic  3.88 us (4%)
    ppermute x12, waiting for transfers between devices, exchange(): lax.ppermute(block, 'chan', [(i, i ^ k) for i in range(chan_count)])  26.8 us
    ppermute x12, starting transfers between devices, exchange(): lax.ppermute(block, 'chan', [(i, i ^ k) for i in range(chan_count)])  19.1 us
    pallas_call x2, Pallas kernels, ladder_share(): pl.pallas_call(ladder_kernel, out_shape=jax.ShapeDtypeStruct((lad_count,...  10.4 us
    unnamed x28, local copies, waits for them, and re-layouts  6.23 us
    pallas_call x2, Pallas kernels, pack(): pl.pallas_call(functools.partial(pack_kernel, plan, given), out_shape=ext...  5.33 us
    pallas_call x1, Pallas kernels, cycle_operator(): pl.pallas_call(functools.partial(operator_kernel, group), out_shape=jax.S...  4.36 us
    pallas_call x2, Pallas kernels, apply_cycle(): pl.pallas_call(functools.partial(cycle_kernel, half), out_shape=[jax.Shap...  3.77 us
    pallas_call x2, Pallas kernels, finish(): pl.pallas_call(functools.partial(finish_kernel, half, len(arrays), tiles)...  3.02 us
  transfers between devices with their start and end apart: 14, of which 3 were waited for; matrix products, arithmetic and copies ran while one was open for 5% of the time, Pallas kernels for 28%

profile of v6, /device:TPU:0, one launch (start us, length us, event | category | flops | bytes accessed | tf_op | source)
XLA Modules:
  0.0 86.0 jit_solution(10160066119969966217)
XLA Ops:
  0.0 2.4 %pack_first.1 = (s32[1,768]{1,0:T(1,128)}, bf16[384,256]{1,0:T(8,128)(2,1)}, bf16[384,256]{1,0:T(8,128)(2,1)}, bf16[384,256]{1,0:T(8,128)(2,1)}) custom-call(s32[1,768]{1,0:T(1,128)} %bitcast.28, bf16[768,512]{1,0:T(8,128)(2,1)} %bitcast.20), custom_call_target="tpu_custom_call" | custom-call | tf_op jit(solution)/shard_map/pack_first/pallas_call | solution.py:101
  2.4 3.1 %collective-permute-start.2 = (bf16[384,256]{1,0:T(8,128)(2,1)}, bf16[384,256]{1,0:T(8,128)(2,1)S(1)}, u32[]{:S(2)}, u32[]{:S(2)}) collective-permute-start(bf16[384,256]{1,0:T(8,128)(2,1)} %get-tuple-element.38), channel_id=1, source_target_pairs={{0,4},{4,0},{8,12},{12,8},{1,5},{5,1},{9,13},{13,9},{2,6},{6,2},{1... | collective-permute-start | bytes 589832 | tf_op jit(solution)/shard_map/ppermute | solution.py:300
  5.5 2.5 %collective-permute-start.6 = (bf16[384,256]{1,0:T(8,128)(2,1)}, bf16[384,256]{1,0:T(8,128)(2,1)}, u32[]{:S(2)}, u32[]{:S(2)}) collective-permute-start(bf16[384,256]{1,0:T(8,128)(2,1)} %get-tuple-element.44), channel_id=1, source_target_pairs={{0,12},{4,8},{8,4},{12,0},{1,13},{5,9},{9,5},{13,1},{2,14},{6,10},... | collective-permute-start | bytes 589832 | tf_op jit(solution)/shard_map/ppermute | solution.py:300
  8.0 0.1 collective-permute-start.7
  8.1 0.0 copy-start.1
  8.1 1.1 %copy-done.1 = bf16[1,768,512]{2,1,0:T(8,128)(2,1)S(1)} copy-done((bf16[1,768,512]{2,1,0:T(8,128)(2,1)S(1)}, bf16[1,768,512]{2,1,0:T(8,128)(2,1)}, u32[]{:S(2)}) %copy-start.1) | copy-done | bytes 786456
  9.2 0.0 copy-start.13
  9.2 0.0 copy-start.2
  9.2 5.8 %ladder_share.2 = bf16[2,768,512]{2,1,0:T(8,128)(2,1)} custom-call(s32[1]{0:T(128)} %bitcast.6.share_ref, bf16[3072,768]{1,0:T(8,128)(2,1)} %bitcast.30, bf16[768,512]{1,0:T(8,128)(2,1)S(1)} %bitcast.21), custom_call_target="tpu_custom_call" | custom-call | flops 30000001024 | bytes 1000000 | tf_op jit(solution)/shard_map/ladder_share/pallas_call | solution.py:144
  15.0 0.0 collective-permute-start
  15.0 0.0 copy-done.13
  15.0 0.2 copy.12.part_ref
  15.2 0.0 copy-done.2
  15.2 4.6 %ladder_share.3 = bf16[2,768,512]{2,1,0:T(8,128)(2,1)S(1)} custom-call(s32[1]{0:T(128)} %bitcast.8.share_ref, bf16[3072,768]{1,0:T(8,128)(2,1)} %bitcast.31, bf16[768,512]{1,0:T(8,128)(2,1)S(1)} %bitcast.22), custom_call_target="tpu_custom_call" | custom-call | flops 30000001024 | bytes 1000000 | tf_op jit(solution)/shard_map/ladder_share/pallas_call | solution.py:144
  19.8 0.0 copy-start.4
  19.8 0.1 broadcast_multiply_fusion
  19.9 0.0 copy-start.3
  19.9 0.0 collective-permute-done
  19.9 2.3 %fusion = bf16[768,512]{1,0:T(8,128)(2,1)} fusion(bf16[2,768,512]{2,1,0:T(8,128)(2,1)S(1)} %ladder_share.3, s32[]{:T(128)S(6)} %select_n.9, bf16[2,768,512]{2,1,0:T(8,128)(2,1)} %collective-permute-done), kind=kLoop, calls=%fused_computation.2 | loop fusion | flops 1572864 | bytes 2359300 | tf_op jit(solution)/shard_map/convert_element_type | solution.py:328
  22.2 0.0 collective-permute-done.2.refs_2_
  22.2 0.7 copy-done.6
  22.9 0.0 copy-done.4
  22.9 2.9 %pack_rest.1 = (bf16[384,256]{1,0:T(8,128)(2,1)S(1)}, bf16[384,256]{1,0:T(8,128)(2,1)S(1)}, bf16[384,256]{1,0:T(8,128)(2,1)S(1)}, bf16[384,512]{1,0:T(8,128)(2,1)S(1)}) custom-call(s32[1,768]{1,0:T(1,128)S(1)} %copy-done.4, bf16[768,512]{1,0:T(8,128)(2,1)S(1)} %bitcast.23), custom_call_target="tpu_custom_call" | custom-call | tf_op jit(solution)/shard_map/pack_rest/pallas_call | solution.py:101
  25.8 0.0 copy-start.8
  25.8 0.7 copy-done.8
  26.5 0.0 copy-start.10
  26.5 0.7 copy-done.10
  27.2 0.7 copy-done.11
  27.9 0.2 copy.10.target_ref
  28.1 1.6 %collective-permute-start.1 = (bf16[768,512]{1,0:T(8,128)(2,1)}, bf16[768,512]{1,0:T(8,128)(2,1)S(1)}, u32[]{:S(2)}, u32[]{:S(2)}) collective-permute-start(bf16[768,512]{1,0:T(8,128)(2,1)} %fusion), channel_id=1, source_target_pairs={{0,2},{2,0},{1,3},{3,1},{4,6},{6,4},{5,7},{7,5},{8,10},{10,8},{9,1... | collective-permute-start | bytes 2359304 | tf_op jit(solution)/shard_map/ppermute | solution.py:332
  29.6 2.9 %collective-permute-start.3 = (bf16[384,256]{1,0:T(8,128)(2,1)}, bf16[384,256]{1,0:T(8,128)(2,1)S(1)}, u32[]{:S(2)}, u32[]{:S(2)}) collective-permute-start(bf16[384,256]{1,0:T(8,128)(2,1)} %copy-done.11), channel_id=1, source_target_pairs={{0,12},{4,8},{8,4},{12,0},{1,13},{5,9},{9,5},{13,1},{2,14},{6,10},... | collective-permute-start | bytes 589832 | tf_op jit(solution)/shard_map/ppermute | solution.py:300
  32.5 0.3 collective-permute-start.4
  32.9 0.0 copy-done.3
  32.9 2.3 %copy-done = bf16[1,1,1536,1536]{3,2,1,0:T(8,128)(2,1)S(1)} copy-done((bf16[1,1,1536,1536]{3,2,1,0:T(8,128)(2,1)S(1)}, bf16[1,1,1536,1536]{3,2,1,0:T(8,128)(2,1)}, u32[]{:S(2)}) %copy-start) | copy-done | bytes 4718616
  35.2 4.4 %cycle_operator.1.operator_ref = bf16[1536,1536]{1,0:T(8,128)(2,1)S(1)} custom-call(s32[4]{0:T(128)S(1)} %get-tuple-element.60.block_index, bf16[1536,1536]{1,0:T(8,128)(2,1)S(1)} %bitcast.19, bf16[12,128,128]{2,1,0:T(8,128)(2,1)S(1)} %bitcast.24), custom_call_target="tpu_custom_call" | custom-call | tf_op jit(solution)/shard_map/cycle_operator/pallas_call | solution.py:186
  39.6 0.0 collective-permute-done.6.refs_0_
  39.6 0.0 copy-done.9
  39.6 1.2 %collective-permute-start.5 = (bf16[384,256]{1,0:T(8,128)(2,1)S(1)}, bf16[384,256]{1,0:T(8,128)(2,1)S(1)}, u32[]{:S(2)}, u32[]{:S(2)}) collective-permute-start(bf16[384,256]{1,0:T(8,128)(2,1)S(1)} %copy-done.9), channel_id=1, source_target_pairs={{0,4},{4,0},{8,12},{12,8},{1,5},{5,1},{9,13},{13,9},{2,6},{6,2},{1... | collective-permute-start | bytes 589832 | tf_op jit(solution)/shard_map/ppermute | solution.py:300
  40.8 0.0 collective-permute-done.7.refs_1_
  40.8 0.0 copy-done.7
  40.8 2.4 %apply_cycle.2 = (bf16[384,256]{1,0:T(8,128)(2,1)S(1)}, bf16[384,256]{1,0:T(8,128)(2,1)S(1)}, bf16[384,256]{1,0:T(8,128)(2,1)S(1)}, bf16[384,256]{1,0:T(8,128)(2,1)S(1)}) custom-call(bf16[1536,1536]{1,0:T(8,128)(2,1)S(1)} %cycle_operator.1.operator_ref, bf16[384,256]{1,0:T(8,128)(2,1)} %collective-permute-done.6.refs_0_, ...), custom_call_target="tpu_custom_call" | custom-call | flops 30000001024 | bytes 1000000 | tf_op jit(solution)/shard_map/apply_cycle/pallas_call | solution.py:218
  43.2 3.0 %collective-permute-start.11 = (bf16[384,256]{1,0:T(8,128)(2,1)S(1)}, bf16[384,256]{1,0:T(8,128)(2,1)S(1)}, u32[]{:S(2)}, u32[]{:S(2)}) collective-permute-start(bf16[384,256]{1,0:T(8,128)(2,1)S(1)} %get-tuple-element.47), channel_id=1, source_target_pairs={{0,12},{4,8},{8,4},{12,0},{1,13},{5,9},{9,5},{13,1},{2,14},{6,10},... | collective-permute-start | bytes 589832 | tf_op jit(solution)/shard_map/ppermute | solution.py:300
  46.2 1.1 %unpack_matrix.1.pick_ref = bf16[768,1536]{1,0:T(8,128)(2,1)S(1)} custom-call(s32[4]{0:T(128)S(1)} %get-tuple-element.59.off_ref, s32[768,1]{1,0:T(8,128)S(1)} %copy.10.target_ref), custom_call_target="tpu_custom_call" | custom-call | tf_op jit(solution)/shard_map/unpack_matrix/pallas_call | solution.py:125
  47.3 0.0 collective-permute-done.3.refs_0_
  47.3 1.5 %collective-permute-start.12 = (bf16[384,256]{1,0:T(8,128)(2,1)S(1)}, bf16[384,256]{1,0:T(8,128)(2,1)S(1)}, u32[]{:S(2)}, u32[]{:S(2)}) collective-permute-start(bf16[384,256]{1,0:T(8,128)(2,1)S(1)} %get-tuple-element.48), channel_id=1, source_target_pairs={{0,8},{4,12},{8,0},{12,4},{1,9},{5,13},{9,1},{13,5},{2,10},{6,14},... | collective-permute-start | bytes 589832 | tf_op jit(solution)/shard_map/ppermute | solution.py:300
  48.8 11.0 %collective-permute-done.4.refs_1_ = bf16[384,256]{1,0:T(8,128)(2,1)S(1)} collective-permute-done((bf16[384,256]{1,0:T(8,128)(2,1)}, bf16[384,256]{1,0:T(8,128)(2,1)S(1)}, u32[]{:S(2)}, u32[]{:S(2)}) %collective-permute-start.4) | collective-permute-done | bytes 196640 | tf_op jit(solution)/shard_map/ppermute | solution.py:300
  59.8 0.0 collective-permute-start.13
  59.8 0.0 collective-permute-done.5.refs_2_
  59.8 1.4 %apply_cycle.3 = (bf16[384,256]{1,0:T(8,128)(2,1)S(1)}, bf16[384,256]{1,0:T(8,128)(2,1)S(1)}, bf16[384,256]{1,0:T(8,128)(2,1)S(1)}, bf16[384,256]{1,0:T(8,128)(2,1)S(1)}) custom-call(bf16[1536,1536]{1,0:T(8,128)(2,1)S(1)} %cycle_operator.1.operator_ref, bf16[384,256]{1,0:T(8,128)(2,1)S(1)} %collective-permute-done.3.refs_0_, ...), custom_call_target="tpu_custom_call" | custom-call | flops 30000001024 | bytes 1000000 | tf_op jit(solution)/shard_map/apply_cycle/pallas_call | solution.py:218
  61.2 2.6 %collective-permute-start.8 = (bf16[384,256]{1,0:T(8,128)(2,1)S(1)}, bf16[384,256]{1,0:T(8,128)(2,1)S(1)}, u32[]{:S(2)}, u32[]{:S(2)}) collective-permute-start(bf16[384,256]{1,0:T(8,128)(2,1)S(1)} %get-tuple-element.55), channel_id=1, source_target_pairs={{0,12},{4,8},{8,4},{12,0},{1,13},{5,9},{9,5},{13,1},{2,14},{6,10},... | collective-permute-start | bytes 589832 | tf_op jit(solution)/shard_map/ppermute | solution.py:300
  63.8 0.0 collective-permute-done.11.refs_0_
  63.8 1.8 %collective-permute-start.9 = (bf16[384,256]{1,0:T(8,128)(2,1)S(1)}, bf16[384,256]{1,0:T(8,128)(2,1)S(1)}, u32[]{:S(2)}, u32[]{:S(2)}) collective-permute-start(bf16[384,256]{1,0:T(8,128)(2,1)S(1)} %get-tuple-element.56), channel_id=1, source_target_pairs={{0,8},{4,12},{8,0},{12,4},{1,9},{5,13},{9,1},{13,5},{2,10},{6,14},... | collective-permute-start | bytes 589832 | tf_op jit(solution)/shard_map/ppermute | solution.py:300
  65.7 0.0 collective-permute-done.1
  65.7 0.0 collective-permute-start.10
  65.7 0.0 copy-done.12
  65.7 1.5 %bitcast_add_fusion.base_ref = f32[768,512]{1,0:T(8,128)S(1)} fusion(bf16[768,512]{1,0:T(8,128)(2,1)S(1)} %collective-permute-done.1, bf16[1,768,512]{2,1,0:T(8,128)(2,1)S(1)} %copy-done.12, bf16[2,768,512]{2,1,0:T(8,128)(2,1)S(1)} %ladder_share.3, s32[]{:T(128)S(6)} %select_n.10, bf16[2,768,512]{2,1,0:T(8,128)(2,1)} %collective-permute-done), kind=kLoop, calls=%fused_computation | loop fusion | flops 2752512 | bytes 4718596 | tf_op jit(solution)/shard_map/add | solution.py:332
  67.2 9.5 %collective-permute-done.12.refs_1_ = bf16[384,256]{1,0:T(8,128)(2,1)S(1)} collective-permute-done((bf16[384,256]{1,0:T(8,128)(2,1)S(1)}, bf16[384,256]{1,0:T(8,128)(2,1)S(1)}, u32[]{:S(2)}, u32[]{:S(2)}) %collective-permute-start.12) | collective-permute-done | bytes 196640 | tf_op jit(solution)/shard_map/ppermute | solution.py:300
  76.7 0.0 collective-permute-done.13.refs_2_
  76.7 0.0 copy-done.5
  76.7 1.5 %finish.2.refs_4_ = bf16[768,512]{1,0:T(8,128)(2,1)} custom-call(bf16[768,1536]{1,0:T(8,128)(2,1)S(1)} %unpack_matrix.1.pick_ref, f32[768,512]{1,0:T(8,128)S(1)} %bitcast_add_fusion.base_ref, f32[768,1]{1,0:T(8,128)S(1)} %copy.12.part_ref, f32[1,512]{1,0:T(1,128)S(1)} %bitcast.26, bf16[384,256]{1,0:T(8,128)(2,1)S(1)} %collective-permute-done.11.refs_0_, ...), custom_call_target="tpu_custom_call" | custom-call | tf_op jit(solution)/shard_map/finish/pallas_call | solution.py:259
  78.2 0.0 collective-permute-done.8.refs_0_
  78.2 6.3 %collective-permute-done.9.refs_1_ = bf16[384,256]{1,0:T(8,128)(2,1)S(1)} collective-permute-done((bf16[384,256]{1,0:T(8,128)(2,1)S(1)}, bf16[384,256]{1,0:T(8,128)(2,1)S(1)}, u32[]{:S(2)}, u32[]{:S(2)}) %collective-permute-start.9) | collective-permute-done | bytes 196640 | tf_op jit(solution)/shard_map/ppermute | solution.py:300
  84.5 0.0 collective-permute-done.10.refs_2_
  84.5 1.5 %finish.3 = bf16[768,512]{1,0:T(8,128)(2,1)} custom-call(bf16[768,1536]{1,0:T(8,128)(2,1)S(1)} %unpack_matrix.1.pick_ref, f32[768,512]{1,0:T(8,128)S(1)} %bitcast_add_fusion.base_ref, f32[768,1]{1,0:T(8,128)S(1)} %copy.12.part_ref, f32[1,512]{1,0:T(1,128)S(1)} %bitcast.27, ...), custom_call_target="tpu_custom_call", output_to_operand_aliasing={{}: (8, {})} | custom-call | tf_op jit(solution)/shard_map/finish/pallas_call | solution.py:259
  (7 shorter events, 0.0 us)
Async XLA Ops:
  2.4 19.8 %collective-permute-start.2 = (bf16[384,256]{1,0:T(8,128)(2,1)}, bf16[384,256]{1,0:T(8,128)(2,1)S(1)}, u32[]{:S(2)}, u32[]{:S(2)}) collective-permute-start(bf16[384,256]{1,0:T(8,128)(2,1)} %get-tuple-element.38), channel_id=1, source_target_pairs={{0,4},{4,0},{8,12},{12,8},{1,5},{5,1},{9,13},{13,9},{2,6},{6,2},{1... | collective-permute-start | bytes 589832 | tf_op jit(solution)/shard_map/ppermute | solution.py:300
  5.5 34.1 %collective-permute-start.6 = (bf16[384,256]{1,0:T(8,128)(2,1)}, bf16[384,256]{1,0:T(8,128)(2,1)}, u32[]{:S(2)}, u32[]{:S(2)}) collective-permute-start(bf16[384,256]{1,0:T(8,128)(2,1)} %get-tuple-element.44), channel_id=1, source_target_pairs={{0,12},{4,8},{8,4},{12,0},{1,13},{5,9},{9,5},{13,1},{2,14},{6,10},... | collective-permute-start | bytes 589832 | tf_op jit(solution)/shard_map/ppermute | solution.py:300
  8.0 32.8 %collective-permute-start.7 = (bf16[384,256]{1,0:T(8,128)(2,1)}, bf16[384,256]{1,0:T(8,128)(2,1)}, u32[]{:S(2)}, u32[]{:S(2)}) collective-permute-start(bf16[384,256]{1,0:T(8,128)(2,1)} %get-tuple-element.45), channel_id=1, source_target_pairs={{0,8},{4,12},{8,0},{12,4},{1,9},{5,13},{9,1},{13,5},{2,10},{6,14},... | collective-permute-start | bytes 589832 | tf_op jit(solution)/shard_map/ppermute | solution.py:300
  8.1 1.1 %copy-start.1 = (bf16[1,768,512]{2,1,0:T(8,128)(2,1)S(1)}, bf16[1,768,512]{2,1,0:T(8,128)(2,1)}, u32[]{:S(2)}) copy-start(bf16[1,768,512]{2,1,0:T(8,128)(2,1)} %param.8) | copy-start | bytes 2359300
  9.2 5.8 %copy-start.13 = (f32[1,768]{1,0:T(1,128)S(1)}, f32[1,768]{1,0:T(1,128)}, u32[]{:S(2)}) copy-start(f32[1,768]{1,0:T(1,128)} %param.14) | copy-start | bytes 9220
  9.2 6.0 %copy-start.2 = (bf16[1,768,512]{2,1,0:T(8,128)(2,1)S(1)}, bf16[1,768,512]{2,1,0:T(8,128)(2,1)}, u32[]{:S(2)}) copy-start(bf16[1,768,512]{2,1,0:T(8,128)(2,1)} %param.8) | copy-start | bytes 2359300
  15.0 4.9 %collective-permute-start = (bf16[2,768,512]{2,1,0:T(8,128)(2,1)}, bf16[2,768,512]{2,1,0:T(8,128)(2,1)}, u32[]{:S(2)}, u32[]{:S(2)}) collective-permute-start(bf16[2,768,512]{2,1,0:T(8,128)(2,1)} %ladder_share.2), channel_id=1, source_target_pairs={{0,1},{1,0},{2,3},{3,2},{4,5},{5,4},{6,7},{7,6},{8,9},{9,8},{10,11... | collective-permute-start | bytes 4718600 | tf_op jit(solution)/shard_map/ppermute | solution.py:320
  19.8 3.1 %copy-start.4 = (s32[1,768]{1,0:T(1,128)S(1)}, s32[1,768]{1,0:T(1,128)}, u32[]{:S(2)}) copy-start(s32[1,768]{1,0:T(1,128)} %get-tuple-element.35.route_hbm) | copy-start | bytes 9220
  19.9 13.0 %copy-start.3 = (bf16[1,1,12,128,128]{4,3,2,1,0:T(8,128)(2,1)S(1)}, bf16[1,1,12,128,128]{4,3,2,1,0:T(8,128)(2,1)}, u32[]{:S(2)}) copy-start(bf16[1,1,12,128,128]{4,3,2,1,0:T(8,128)(2,1)} %param.13) | copy-start | bytes 1179652
  22.2 0.7 copy-start.6
  25.8 0.7 copy-start.8
  26.5 0.7 copy-start.10
  27.2 0.7 copy-start.11
  28.1 37.6 %collective-permute-start.1 = (bf16[768,512]{1,0:T(8,128)(2,1)}, bf16[768,512]{1,0:T(8,128)(2,1)S(1)}, u32[]{:S(2)}, u32[]{:S(2)}) collective-permute-start(bf16[768,512]{1,0:T(8,128)(2,1)} %fusion), channel_id=1, source_target_pairs={{0,2},{2,0},{1,3},{3,1},{4,6},{6,4},{5,7},{7,5},{8,10},{10,8},{9,1... | collective-permute-start | bytes 2359304 | tf_op jit(solution)/shard_map/ppermute | solution.py:332
  29.6 17.7 %collective-permute-start.3 = (bf16[384,256]{1,0:T(8,128)(2,1)}, bf16[384,256]{1,0:T(8,128)(2,1)S(1)}, u32[]{:S(2)}, u32[]{:S(2)}) collective-permute-start(bf16[384,256]{1,0:T(8,128)(2,1)} %copy-done.11), channel_id=1, source_target_pairs={{0,12},{4,8},{8,4},{12,0},{1,13},{5,9},{9,5},{13,1},{2,14},{6,10},... | collective-permute-start | bytes 589832 | tf_op jit(solution)/shard_map/ppermute | solution.py:300
  32.5 27.2 %collective-permute-start.4 = (bf16[384,256]{1,0:T(8,128)(2,1)}, bf16[384,256]{1,0:T(8,128)(2,1)S(1)}, u32[]{:S(2)}, u32[]{:S(2)}) collective-permute-start(bf16[384,256]{1,0:T(8,128)(2,1)} %copy-done.10), channel_id=1, source_target_pairs={{0,8},{4,12},{8,0},{12,4},{1,9},{5,13},{9,1},{13,5},{2,10},{6,14},... | collective-permute-start | bytes 589832 | tf_op jit(solution)/shard_map/ppermute | solution.py:300
  32.9 2.3 %copy-start = (bf16[1,1,1536,1536]{3,2,1,0:T(8,128)(2,1)S(1)}, bf16[1,1,1536,1536]{3,2,1,0:T(8,128)(2,1)}, u32[]{:S(2)}) copy-start(bf16[1,1,1536,1536]{3,2,1,0:T(8,128)(2,1)} %param.12) | copy-start | bytes 14155780
  35.2 4.4 %copy-start.9 = (bf16[384,256]{1,0:T(8,128)(2,1)S(1)}, bf16[384,256]{1,0:T(8,128)(2,1)}, u32[]{:S(2)}) copy-start(bf16[384,256]{1,0:T(8,128)(2,1)} %copy-done.8) | copy-start | bytes 589828
  35.2 5.6 %copy-start.7 = (bf16[384,256]{1,0:T(8,128)(2,1)S(1)}, bf16[384,256]{1,0:T(8,128)(2,1)}, u32[]{:S(2)}) copy-start(bf16[384,256]{1,0:T(8,128)(2,1)} %copy-done.6) | copy-start | bytes 589828
  39.6 20.2 %collective-permute-start.5 = (bf16[384,256]{1,0:T(8,128)(2,1)S(1)}, bf16[384,256]{1,0:T(8,128)(2,1)S(1)}, u32[]{:S(2)}, u32[]{:S(2)}) collective-permute-start(bf16[384,256]{1,0:T(8,128)(2,1)S(1)} %copy-done.9), channel_id=1, source_target_pairs={{0,4},{4,0},{8,12},{12,8},{1,5},{5,1},{9,13},{13,9},{2,6},{6,2},{1... | collective-permute-start | bytes 589832 | tf_op jit(solution)/shard_map/ppermute | solution.py:300
  43.2 20.6 %collective-permute-start.11 = (bf16[384,256]{1,0:T(8,128)(2,1)S(1)}, bf16[384,256]{1,0:T(8,128)(2,1)S(1)}, u32[]{:S(2)}, u32[]{:S(2)}) collective-permute-start(bf16[384,256]{1,0:T(8,128)(2,1)S(1)} %get-tuple-element.47), channel_id=1, source_target_pairs={{0,12},{4,8},{8,4},{12,0},{1,13},{5,9},{9,5},{13,1},{2,14},{6,10},... | collective-permute-start | bytes 589832 | tf_op jit(solution)/shard_map/ppermute | solution.py:300
  47.3 29.3 %collective-permute-start.12 = (bf16[384,256]{1,0:T(8,128)(2,1)S(1)}, bf16[384,256]{1,0:T(8,128)(2,1)S(1)}, u32[]{:S(2)}, u32[]{:S(2)}) collective-permute-start(bf16[384,256]{1,0:T(8,128)(2,1)S(1)} %get-tuple-element.48), channel_id=1, source_target_pairs={{0,8},{4,12},{8,0},{12,4},{1,9},{5,13},{9,1},{13,5},{2,10},{6,14},... | collective-permute-start | bytes 589832 | tf_op jit(solution)/shard_map/ppermute | solution.py:300
  59.8 16.9 %collective-permute-start.13 = (bf16[384,256]{1,0:T(8,128)(2,1)S(1)}, bf16[384,256]{1,0:T(8,128)(2,1)S(1)}, u32[]{:S(2)}, u32[]{:S(2)}) collective-permute-start(bf16[384,256]{1,0:T(8,128)(2,1)S(1)} %get-tuple-element.49), channel_id=1, source_target_pairs={{0,4},{4,0},{8,12},{12,8},{1,5},{5,1},{9,13},{13,9},{2,6},{6,2},{1... | collective-permute-start | bytes 589832 | tf_op jit(solution)/shard_map/ppermute | solution.py:300
  59.8 5.9 %copy-start.12 = (bf16[1,768,512]{2,1,0:T(8,128)(2,1)S(1)}, bf16[1,768,512]{2,1,0:T(8,128)(2,1)}, u32[]{:S(2)}) copy-start(bf16[1,768,512]{2,1,0:T(8,128)(2,1)} %param.9) | copy-start | bytes 2359300
  61.2 17.0 %collective-permute-start.8 = (bf16[384,256]{1,0:T(8,128)(2,1)S(1)}, bf16[384,256]{1,0:T(8,128)(2,1)S(1)}, u32[]{:S(2)}, u32[]{:S(2)}) collective-permute-start(bf16[384,256]{1,0:T(8,128)(2,1)S(1)} %get-tuple-element.55), channel_id=1, source_target_pairs={{0,12},{4,8},{8,4},{12,0},{1,13},{5,9},{9,5},{13,1},{2,14},{6,10},... | collective-permute-start | bytes 589832 | tf_op jit(solution)/shard_map/ppermute | solution.py:300
  63.8 20.7 %collective-permute-start.9 = (bf16[384,256]{1,0:T(8,128)(2,1)S(1)}, bf16[384,256]{1,0:T(8,128)(2,1)S(1)}, u32[]{:S(2)}, u32[]{:S(2)}) collective-permute-start(bf16[384,256]{1,0:T(8,128)(2,1)S(1)} %get-tuple-element.56), channel_id=1, source_target_pairs={{0,8},{4,12},{8,0},{12,4},{1,9},{5,13},{9,1},{13,5},{2,10},{6,14},... | collective-permute-start | bytes 589832 | tf_op jit(solution)/shard_map/ppermute | solution.py:300
  65.7 11.0 %copy-start.5 = (f32[512]{0:T(512)S(1)}, f32[512]{0:T(512)}, u32[]{:S(2)}) copy-start(f32[512]{0:T(512)} %param.15) | copy-start | bytes 6148
  65.7 18.8 %collective-permute-start.10 = (bf16[384,256]{1,0:T(8,128)(2,1)S(1)}, bf16[384,256]{1,0:T(8,128)(2,1)S(1)}, u32[]{:S(2)}, u32[]{:S(2)}) collective-permute-start(bf16[384,256]{1,0:T(8,128)(2,1)S(1)} %get-tuple-element.57), channel_id=1, source_target_pairs={{0,4},{4,0},{8,12},{12,8},{1,5},{5,1},{9,13},{13,9},{2,6},{6,2},{1... | collective-permute-start | bytes 589832 | tf_op jit(solution)/shard_map/ppermute | solution.py:300

commit v7 on v5

v7 whole, which is shorter than its diff:
```python
import functools

import jax
import jax.numpy as jnp
from jax import lax
from jax.experimental import pallas as pl
from jax.experimental.pallas import tpu as pltpu
from jax.sharding import PartitionSpec as P

VMEM_LIMIT = 32 * 1024 * 1024
HALVES = 2
F32 = jnp.float32
BF16 = jnp.bfloat16
CHEAP = pl.CostEstimate(flops=0, bytes_accessed=0, transcendentals=0)
DEAR = pl.CostEstimate(flops=3 * 10**10, bytes_accessed=10**6, transcendentals=0)


def params():
    return pltpu.CompilerParams(vmem_limit_bytes=VMEM_LIMIT)


def in_hbm(*arrays):
    return [pltpu.with_memory_space_constraint(a, pltpu.HBM) for a in arrays]


def whole(memory=pltpu.VMEM):
    return pl.BlockSpec(memory_space=memory)


def selection(match):
    return jnp.where(match, 1.0, 0.0).astype(BF16)


def block_offsets(paired, chan_count, block_rows):
    chan = lax.axis_index("chan")
    return [(chan ^ k) * block_rows for k in range(chan_count)] if paired else [0]


def slots_of(owners, send, names):
    lane = 128
    pieces = owners.shape[1] // lane
    before = selection(
        lax.broadcasted_iota(jnp.int32, (lane, 2 * lane), 0)
        < lax.broadcasted_iota(jnp.int32, (lane, 2 * lane), 1)
    )
    hot = [
        lax.broadcasted_iota(jnp.int32, (names, lane), 0) == owners[:, i * lane : (i + 1) * lane]
        for i in range(pieces)
    ]
    counts = jnp.dot(
        jnp.concatenate([selection(h) for h in hot], axis=0), before, preferred_element_type=F32
    )
    passed = jnp.zeros((names, lane), F32)
    slots = []
    for i in range(pieces):
        within = counts[i * names : (i + 1) * names]
        slots.append(jnp.sum(jnp.where(hot[i], within[:, :lane] + passed, 0.0), axis=0, keepdims=True))
        passed = passed + within[:, lane:]
    return owners * send + jnp.concatenate(slots, axis=1).astype(jnp.int32)


def pack_kernel(plan, given, route_hbm, amps_hbm, *refs):
    paired, chan_count, send, block_rows, items = plan
    outs, (route_ref, amps_ref, sems) = refs[:-3], refs[-3:]
    block_refs = outs if given else outs[1:]
    copies = [
        pltpu.make_async_copy(route_hbm, route_ref, sems.at[0]),
        pltpu.make_async_copy(amps_hbm.at[:, pl.ds(0, amps_ref.shape[1])], amps_ref, sems.at[1]),
    ]
    for copy in copies:
        copy.start()
    copies[0].wait()
    target = route_ref[...]
    if not given:
        target = slots_of(target, send, max(16, chan_count))
        outs[0][...] = target
    offsets = block_offsets(paired, chan_count, block_rows)
    slot = lax.broadcasted_iota(jnp.int32, (block_rows, target.shape[1]), 0)
    for i, (k, first, width) in enumerate(items):
        pick = selection(slot == target - offsets[k])
        if i == 0:
            copies[1].wait()
        block_refs[i][...] = jnp.dot(
            pick, amps_ref[:, pl.ds(first, width)], preferred_element_type=F32
        ).astype(BF16)


def pack(plan, given, route_row, amps, name):
    rows = amps.shape[0]
    block_rows, items = plan[3], plan[4]
    columns = max(first + width for _, first, width in items)
    extra = [] if given else [pltpu.VMEM((1, rows), jnp.int32)]
    return pl.pallas_call(
        functools.partial(pack_kernel, plan, given),
        out_shape=extra + [pltpu.VMEM((block_rows, width), BF16) for _, _, width in items],
        in_specs=[whole(pl.ANY), whole(pl.ANY)],
        out_specs=[whole()] * (len(extra) + len(items)),
        scratch_shapes=[
            pltpu.VMEM((1, rows), jnp.int32),
            pltpu.VMEM((rows, columns), BF16),
            pltpu.SemaphoreType.DMA((2,)),
        ],
        compiler_params=params(),
        name=name,
    )(*in_hbm(route_row, amps))


def unpack_kernel(off_ref, target_ref, out_ref):
    count = off_ref.shape[0]
    rows, capacity = out_ref.shape
    block_rows = capacity // count
    target = target_ref[...]
    slots = lax.broadcasted_iota(jnp.int32, (rows, block_rows), 1)
    for k in range(count):
        out_ref[:, pl.ds(k * block_rows, block_rows)] = selection(slots == target - off_ref[k])


def unpack_matrix(offsets, target_column, capacity):
    return pl.pallas_call(
        unpack_kernel,
        out_shape=jax.ShapeDtypeStruct((target_column.shape[0], capacity), BF16),
        in_specs=[whole(pltpu.SMEM), whole()],
        out_specs=whole(),
        compiler_params=params(),
        cost_estimate=CHEAP,
        name="unpack_matrix",
    )(offsets, target_column)


def ladder_kernel(step, sub_count, weight_hbm, amps_hbm, *refs):
    moved = (len(refs) - 4) // 2
    source_refs, part_ref, held_refs = refs[:moved], refs[moved], refs[moved + 1 : 2 * moved + 1]
    weight_ref, amps_ref, sems = refs[2 * moved + 1 :]
    rows, lad_count = amps_ref.shape[0], part_ref.shape[0]
    share = lax.rem(lax.axis_index("sub") + step, sub_count)
    copies = [pltpu.make_async_copy(amps_hbm, amps_ref, sems.at[0])]
    for i in range(lad_count):
        start = pl.multiple_of((i * sub_count + share) * rows, rows)
        copies.append(pltpu.make_async_copy(weight_hbm.at[pl.ds(start, rows), :], weight_ref.at[i], sems.at[1 + i]))
    for n, (source, held) in enumerate(zip(source_refs, held_refs)):
        copies.append(pltpu.make_async_copy(source, held, sems.at[1 + lad_count + n]))
    for copy in copies:
        copy.start()
    copies[0].wait()
    for i in range(lad_count):
        copies[1 + i].wait()
        part_ref[i] = jnp.dot(weight_ref[i], amps_ref[...], preferred_element_type=F32).astype(BF16)
    for copy in copies[1 + lad_count :]:
        copy.wait()


def ladder_part(step, weight, amps, lad_count, sub_count, moved):
    rows, holes = amps.shape
    return pl.pallas_call(
        functools.partial(ladder_kernel, step, sub_count),
        out_shape=[pltpu.VMEM((lad_count, rows, holes), BF16)] + [pltpu.VMEM(m.shape, BF16) for m in moved],
        in_specs=[whole(pl.ANY)] * (2 + len(moved)),
        out_specs=[whole()] * (1 + len(moved)),
        scratch_shapes=[
            pltpu.VMEM((lad_count, rows, rows), BF16),
            pltpu.VMEM((rows, holes), BF16),
            pltpu.SemaphoreType.DMA((1 + lad_count + len(moved),)),
        ],
        compiler_params=params(),
        cost_estimate=DEAR,
        name="ladder_part",
    )(*in_hbm(weight, amps, *moved))


def cycle_kernel(half, plan, weight_ref, mixing_ref, *refs):
    paired, chan_count, _, _ = plan
    count = len(refs) // 2 - 1
    in_refs, out_refs, (mixed_ref, back_ref) = refs[:count], refs[count : 2 * count], refs[2 * count :]
    block_rows, width = out_refs[0].shape
    group = mixing_ref.shape[1]
    offsets = block_offsets(paired, chan_count, block_rows)
    for i, in_ref in enumerate(in_refs):
        start = pl.multiple_of(offsets[count - 1 - i], block_rows)
        for a in range(block_rows // group):
            at = pl.ds(a * group, group)
            part = in_ref[at, :] if in_ref.shape[1] == width else in_ref[at, pl.ds(half * width, width)]
            mix = mixing_ref[lax.div(start, group) + a]
            mixed_ref[pl.ds(pl.multiple_of(start + a * group, group), group), :] = jnp.dot(
                mix, part, preferred_element_type=F32
            ).astype(BF16)
    for i, out_ref in enumerate(out_refs):
        start = pl.multiple_of(offsets[count - 1 - i], block_rows)
        back_ref[...] = jnp.dot(
            weight_ref[pl.ds(start, block_rows), :], mixed_ref[...], preferred_element_type=F32
        ).astype(BF16)
        for a in range(block_rows // group):
            at = pl.ds(a * group, group)
            mix = mixing_ref[lax.div(start, group) + a]
            out_ref[at, :] = lax.dot_general(
                mix, back_ref[at, :], (((0,), (0,)), ((), ())), preferred_element_type=F32
            ).astype(BF16)


def apply_cycle(half, plan, weight, mixing, arrays, width):
    return pl.pallas_call(
        functools.partial(cycle_kernel, half, plan),
        out_shape=[jax.ShapeDtypeStruct((a.shape[0], width), BF16) for a in arrays],
        in_specs=[whole()] * (2 + len(arrays)),
        out_specs=[whole()] * len(arrays),
        scratch_shapes=[pltpu.VMEM((weight.shape[0], width), BF16), pltpu.VMEM((arrays[0].shape[0], width), BF16)],
        compiler_params=params(),
        cost_estimate=DEAR,
        name="apply_cycle",
    )(weight, mixing, *arrays)


def finish_kernel(half, count, tiles, pick_ref, base_ref, part_ref, hole_ref, *refs):
    in_refs, (out_hbm, block_ref, out_ref, sems) = refs[:count], refs[-4:]
    block_rows, width = in_refs[0].shape
    tile = out_ref.shape[0] // tiles
    columns = pl.ds(half * width, width)
    for i, in_ref in enumerate(in_refs):
        block_ref[pl.ds((count - 1 - i) * block_rows, block_rows), :] = in_ref[...]
    copies = []
    for t in range(tiles):
        at = pl.ds(t * tile, tile)
        back = jnp.dot(pick_ref[at, :], block_ref[...], preferred_element_type=F32)
        total = base_ref[at, columns] + back
        out_ref[at, :] = (total / (part_ref[at, :] + hole_ref[:, columns])).astype(BF16)
        copies.append(pltpu.make_async_copy(out_ref.at[at, :], out_hbm.at[at, columns], sems.at[t]))
        copies[-1].start()
    for copy in copies:
        copy.wait()


def finish(half, pick, base, part_column, hole_row, arrays, earlier):
    rows, holes = base.shape
    tiles, width = 3, holes // HALVES
    operands = [pick, base, part_column, hole_row, *arrays]
    in_specs = [whole()] * len(operands)
    aliases = {}
    if earlier is not None:
        aliases = {len(operands): 0}
        operands.append(earlier)
        in_specs.append(whole(pl.ANY))
    return pl.pallas_call(
        functools.partial(finish_kernel, half, len(arrays), tiles),
        out_shape=jax.ShapeDtypeStruct((rows, holes), BF16),
        in_specs=in_specs,
        out_specs=whole(pl.ANY),
        scratch_shapes=[
            pltpu.VMEM((pick.shape[1], width), BF16),
            pltpu.VMEM((rows, width), BF16),
            pltpu.SemaphoreType.DMA((tiles,)),
        ],
        input_output_aliases=aliases,
        compiler_params=params(),
        cost_estimate=CHEAP,
        name="finish",
    )(*operands)


def body(amplitudes, driving, route, ladder_weight, ph_weight, recouple, gap_part, gap_hole):
    amps = amplitudes[0]
    rows, holes = amps.shape
    chan_count = lax.axis_size("chan")
    lad_count = lax.axis_size("lad")
    sub_count = lax.axis_size("sub")
    chan, lad, sub = lax.axis_index("chan"), lax.axis_index("lad"), lax.axis_index("sub")
    weight, mixing = ph_weight[0, 0], recouple[0, 0]
    capacity = weight.shape[0]
    send = capacity // chan_count
    paired = send % mixing.shape[1] == 0 and chan_count & (chan_count - 1) == 0
    if paired:
        block_rows = send
        block_index = jnp.stack([chan ^ k for k in range(chan_count)]).astype(jnp.int32)
    else:
        block_rows = capacity
        block_index = jnp.zeros((1,), jnp.int32)
    offsets = block_index * block_rows

    def exchange(block, k):
        if not paired:
            split = block.reshape(chan_count, send, -1)
            split = lax.all_to_all(split, "chan", split_axis=0, concat_axis=0, tiled=True)
            return split.reshape(capacity, -1)
        return lax.ppermute(block, "chan", [(i, i ^ k) for i in range(chan_count)]) if k else block

    far_first = list(reversed(range(block_index.shape[0])))
    count = len(far_first)
    width = holes // HALVES
    route_row = route[0].reshape(1, rows)
    plan = (paired, chan_count, send, block_rows)
    early = [(k, 0, width) for k in far_first if k or not paired]
    late = [(k, h * width, width) for h in range(1, HALVES) for k in far_first if k or not paired]
    late += [(0, 0, holes)] if paired else []
    target, *blocks = pack(plan + (early,), False, route_row, amps, "pack_first")
    arrived = {(k, 0): exchange(block, k) for (k, _, _), block in zip(early, blocks)}
    if paired:
        near = (1, 0)
        target, arrived[near] = lax.optimization_barrier((target, arrived[near]))
    blocks = pack(plan + (late,), True, target, amps, "pack_rest")
    for (k, first, _), block in zip(late, blocks):
        arrived[(k, first // width)] = exchange(block, k)

    part_column, hole_row = gap_part[0].reshape(rows, 1), gap_hole.reshape(1, holes)
    amps, blocks = lax.optimization_barrier((amps, blocks))
    pick = unpack_matrix(offsets, target.reshape(rows, 1), capacity)

    kept = []
    for step in reversed(range(sub_count)):
        moved = [] if step else [mixing, weight]
        part, *moved = ladder_part(step, ladder_weight[0], amps, lad_count, sub_count, moved)
        if step:
            part = lax.ppermute(part, "sub", [(i, (i + step) % sub_count) for i in range(sub_count)])
        else:
            mixing, weight = moved
        kept.append(part)

    def chip_sum(position):
        picked = [lax.dynamic_index_in_dim(p, position, 0, keepdims=False) for p in kept]
        return sum(p.astype(F32) for p in picked)

    base = driving[0].astype(F32) + chip_sum(lad)
    terms = [chip_sum(lax.rem(lad + step, lad_count)).astype(BF16) for step in range(1, lad_count)]
    returned = []
    for half in range(HALVES):
        blocks = [arrived[(k, half if k or not paired else 0)] for k in far_first]
        if returned:
            blocks, made = lax.optimization_barrier((blocks, made))
        made = apply_cycle(half, plan, weight, mixing, blocks, width)
        if not half:
            behind, terms = lax.optimization_barrier((made[1:], terms))
            made = [made[0], *behind]
        returned.append([exchange(block, k) for k, block in zip(far_first, made)])
    for step, term in enumerate(terms, 1):
        pairs = [(i, (i + step) % lad_count) for i in range(lad_count)]
        base = base + lax.ppermute(term, "lad", pairs).astype(F32)
    updated = None
    for half in range(HALVES):
        updated = finish(half, pick, base, part_column, hole_row, returned[half], updated)
    return updated[None]


def solution(mesh):
    placed = (
        P(("parts", "chan"), ("lad", "sub"), None),
        P(("parts", "chan"), ("lad", "sub"), None),
        P("chan", ("lad", "sub"), None),
        P("chan", None, ("lad", "sub")),
        P("chan", ("lad", "sub"), None, None),
        P("chan", ("lad", "sub"), None, None, None),
        P(("parts", "chan"), ("lad", "sub")),
        P("parts"),
    )
    return jax.shard_map(
        body,
        mesh=mesh,
        in_specs=placed,
        out_specs=P(("parts", "chan"), ("lad", "sub"), None),
        check_vma=False,
    )
```

time: 79.2 us -> 77.5 us (0.979)
  waiting for transfers between devices: 25.4 us -> 23.4 us
    ppermute x12, waiting for transfers between devices: 25.4 us -> 22.8 us  [exchange(): lax.ppermute(block, 'chan', [(i, i ^ k) for i in range(chan_count)])]
    pallas_call x2, Pallas kernels: 5.34 us -> 4.27 us  [pack(): pl.pallas_call(functools.partial(pack_kernel, plan, given), out_shape=ext...]
    pallas_call x5 -> x4, Pallas kernels: 15 us -> 16 us  [the longest x2 8.25 us: apply_cycle(): pl.pallas_call(functools.partial(cycle_kernel, half, plan), out_shape=[ja...]
    unnamed x16 -> x20, local copies, waits for them, and re-layouts: 2.37 us -> 2.29 us
  transfers between devices with their start and end apart: 14 -> 14, of which waited for: 3 -> 7; matrix products, arithmetic and copies ran while one was open for 5% -> 6% of each run, Pallas kernels for 26% -> 27%
where the time goes in v7:
time: 77.5 us; the launch traced here: 77.3 us
  Pallas kernels  24.4 us (31%)
  waiting for transfers between devices  23.4 us (30%)
  starting transfers between devices  22.7 us (29%)
  local copies, waits for them, and re-layouts  3.33 us (4%)
  other arithmetic  3.3 us (4%)
    ppermute x12, waiting for transfers between devices, exchange(): lax.ppermute(block, 'chan', [(i, i ^ k) for i in range(chan_count)])  22.8 us
    ppermute x12, starting transfers between devices, exchange(): lax.ppermute(block, 'chan', [(i, i ^ k) for i in range(chan_count)])  21 us
    pallas_call x2, Pallas kernels, apply_cycle(): pl.pallas_call(functools.partial(cycle_kernel, half, plan), out_shape=[ja...  8.25 us
    pallas_call x2, Pallas kernels, ladder_part(): pl.pallas_call(functools.partial(ladder_kernel, step, sub_count), out_sha...  7.72 us
    pallas_call x2, Pallas kernels, pack(): pl.pallas_call(functools.partial(pack_kernel, plan, given), out_shape=ext...  4.27 us
    pallas_call x2, Pallas kernels, finish(): pl.pallas_call(functools.partial(finish_kernel, half, len(arrays), tiles)...  3.03 us
    unnamed x20, local copies, waits for them, and re-layouts  2.29 us
    convert_element_type x1, other arithmetic, body(): chip_sum(lax.rem(lad + step, lad_count)).astype(BF16)  1.69 us
  transfers between devices with their start and end apart: 14, of which 7 were waited for; matrix products, arithmetic and copies ran while one was open for 6% of the time, Pallas kernels for 27%

profile of v7, /device:TPU:0, one launch (start us, length us, event | category | flops | bytes accessed | tf_op | source)
XLA Modules:
  0.0 77.3 jit_solution(13708429705588914378)
XLA Ops:
  0.0 1.7 %pack_first.1 = (s32[1,768]{1,0:T(1,128)S(1)}, bf16[384,256]{1,0:T(8,128)(2,1)S(1)}, bf16[384,256]{1,0:T(8,128)(2,1)S(1)}, bf16[384,256]{1,0:T(8,128)(2,1)S(1)}) custom-call(s32[1,768]{1,0:T(1,128)} %bitcast.24, bf16[768,512]{1,0:T(8,128)(2,1)} %bitcast.20), custom_call_target="tpu_custom_call" | custom-call | tf_op jit(solution)/shard_map/pack_first/pallas_call | solution.py:93
  1.7 0.0 copy-start
  1.7 0.6 copy-done
  2.3 3.0 %collective-permute-start = (bf16[384,256]{1,0:T(8,128)(2,1)S(1)}, bf16[384,256]{1,0:T(8,128)(2,1)S(1)}, u32[]{:S(2)}, u32[]{:S(2)}) collective-permute-start(bf16[384,256]{1,0:T(8,128)(2,1)S(1)} %get-tuple-element.36), channel_id=1, source_target_pairs={{0,4},{4,0},{8,12},{12,8},{1,5},{5,1},{9,13},{13,9},{2,6},{6,2},{1... | collective-permute-start | bytes 589832 | tf_op jit(solution)/shard_map/ppermute | solution.py:282
  5.3 2.5 %collective-permute-start.2 = (bf16[384,256]{1,0:T(8,128)(2,1)S(1)}, bf16[384,256]{1,0:T(8,128)(2,1)S(1)}, u32[]{:S(2)}, u32[]{:S(2)}) collective-permute-start(bf16[384,256]{1,0:T(8,128)(2,1)S(1)} %get-tuple-element.46), channel_id=1, source_target_pairs={{0,12},{4,8},{8,4},{12,0},{1,13},{5,9},{9,5},{13,1},{2,14},{6,10},... | collective-permute-start | bytes 589832 | tf_op jit(solution)/shard_map/ppermute | solution.py:282
  7.8 0.1 collective-permute-start.3
  7.9 0.9 %copy.12.part_ref = f32[768,1]{1,0:T(8,128)S(1)} copy(f32[768,1]{0,1:T(1,128)} %bitcast.25) | data formatting | bytes 6144 | tf_op jit(solution)/shard_map/reshape;squeeze | solution.py:301
  8.8 0.1 add_multiply_fusion.off_ref
  8.8 1.8 %collective-permute-done.refs_2_ = bf16[384,256]{1,0:T(8,128)(2,1)S(1)} collective-permute-done((bf16[384,256]{1,0:T(8,128)(2,1)S(1)}, bf16[384,256]{1,0:T(8,128)(2,1)S(1)}, u32[]{:S(2)}, u32[]{:S(2)}) %collective-permute-start) | collective-permute-done | bytes 196640 | tf_op jit(solution)/shard_map/ppermute | solution.py:282
  10.6 2.6 %pack_rest.1 = (bf16[384,256]{1,0:T(8,128)(2,1)}, bf16[384,256]{1,0:T(8,128)(2,1)}, bf16[384,256]{1,0:T(8,128)(2,1)}, bf16[384,512]{1,0:T(8,128)(2,1)S(1)}) custom-call(s32[1,768]{1,0:T(1,128)} %copy-done, bf16[768,512]{1,0:T(8,128)(2,1)} %bitcast.21), custom_call_target="tpu_custom_call" | custom-call | tf_op jit(solution)/shard_map/pack_rest/pallas_call | solution.py:93
  13.2 6.8 %collective-permute-start.5 = (bf16[384,256]{1,0:T(8,128)(2,1)}, bf16[384,256]{1,0:T(8,128)(2,1)}, u32[]{:S(2)}, u32[]{:S(2)}) collective-permute-start(bf16[384,256]{1,0:T(8,128)(2,1)} %get-tuple-element.38), channel_id=1, source_target_pairs={{0,12},{4,8},{8,4},{12,0},{1,13},{5,9},{9,5},{13,1},{2,14},{6,10},... | collective-permute-start | bytes 589832 | tf_op jit(solution)/shard_map/ppermute | solution.py:282
  20.0 0.0 collective-permute-start.6
  20.0 0.6 collective-permute-start.7
  20.6 4.2 %ladder_part.2 = bf16[2,768,512]{2,1,0:T(8,128)(2,1)} custom-call(bf16[3072,768]{1,0:T(8,128)(2,1)} %bitcast.26, bf16[768,512]{1,0:T(8,128)(2,1)} %bitcast.22), custom_call_target="tpu_custom_call" | custom-call | flops 30000001024 | bytes 1000000 | tf_op jit(solution)/shard_map/ladder_part/pallas_call | solution.py:154
  24.9 3.5 %ladder_part.3 = (bf16[2,768,512]{2,1,0:T(8,128)(2,1)S(1)}, bf16[12,128,128]{2,1,0:T(8,128)(2,1)S(1)}, bf16[1536,1536]{1,0:T(8,128)(2,1)S(1)}) custom-call(bf16[3072,768]{1,0:T(8,128)(2,1)} %bitcast.27, bf16[768,512]{1,0:T(8,128)(2,1)} %bitcast.23, bf16[12,128,128]{2,1,0:T(8,128)(2,1)} %bitcast.29, bf16[1536,1536]{1,0:T(8,128)(2,1)} %bitcast.28), custom_call_target="tpu_custom_call" | custom-call | flops 30000001024 | bytes 1000000 | tf_op jit(solution)/shard_map/ladder_part/pallas_call | solution.py:154
  28.3 0.0 copy-start.5
  28.4 0.0 copy-start.7
  28.4 0.0 collective-permute-done.2.refs_0_
  28.4 0.1 collective-permute-start.1
  28.5 6.2 %collective-permute-done.3.refs_1_ = bf16[384,256]{1,0:T(8,128)(2,1)S(1)} collective-permute-done((bf16[384,256]{1,0:T(8,128)(2,1)S(1)}, bf16[384,256]{1,0:T(8,128)(2,1)S(1)}, u32[]{:S(2)}, u32[]{:S(2)}) %collective-permute-start.3) | collective-permute-done | bytes 196640 | tf_op jit(solution)/shard_map/ppermute | solution.py:282
  34.7 0.0 copy-start.1
  34.7 3.5 %apply_cycle.2 = (bf16[384,256]{1,0:T(8,128)(2,1)}, bf16[384,256]{1,0:T(8,128)(2,1)S(1)}, bf16[384,256]{1,0:T(8,128)(2,1)S(1)}, bf16[384,256]{1,0:T(8,128)(2,1)S(1)}) custom-call(bf16[1536,1536]{1,0:T(8,128)(2,1)S(1)} %get-tuple-element.44.weight_ref, bf16[12,128,128]{2,1,0:T(8,128)(2,1)S(1)} %get-tuple-element.45.mixing_ref, ...), custom_call_target="tpu_custom_call" | custom-call | flops 30000001024 | bytes 1000000 | tf_op jit(solution)/shard_map/apply_cycle/pallas_call | solution.py:200
  38.3 0.0 copy-done.5
  38.3 0.0 copy-done.7
  38.3 0.0 copy-start.3
  38.3 0.7 copy-done.3
  39.0 3.0 %collective-permute-start.11 = (bf16[384,256]{1,0:T(8,128)(2,1)}, bf16[384,256]{1,0:T(8,128)(2,1)S(1)}, u32[]{:S(2)}, u32[]{:S(2)}) collective-permute-start(bf16[384,256]{1,0:T(8,128)(2,1)} %get-tuple-element.53), channel_id=1, source_target_pairs={{0,12},{4,8},{8,4},{12,0},{1,13},{5,9},{9,5},{13,1},{2,14},{6,10},... | collective-permute-start | bytes 589832 | tf_op jit(solution)/shard_map/ppermute | solution.py:282
  41.9 0.0 copy-done.1
  41.9 0.2 copy.10.target_ref
  42.1 0.0 copy-start.6
  42.1 1.1 %unpack_matrix.1.pick_ref = bf16[768,1536]{1,0:T(8,128)(2,1)S(1)} custom-call(s32[4]{0:T(128)S(1)} %add_multiply_fusion.off_ref, s32[768,1]{1,0:T(8,128)S(1)} %copy.10.target_ref), custom_call_target="tpu_custom_call" | custom-call | tf_op jit(solution)/shard_map/unpack_matrix/pallas_call | solution.py:119
  43.2 0.0 copy-start.4
  43.2 0.0 collective-permute-done.1
  43.3 1.7 %fusion = bf16[768,512]{1,0:T(8,128)(2,1)S(1)} fusion(bf16[2,768,512]{2,1,0:T(8,128)(2,1)S(1)} %get-tuple-element.43, s32[]{:T(128)S(6)} %select_n.10, bf16[2,768,512]{2,1,0:T(8,128)(2,1)} %collective-permute-done.1), kind=kLoop, calls=%fused_computation.2 | loop fusion | flops 1572864 | bytes 2359300 | tf_op jit(solution)/shard_map/convert_element_type | solution.py:320
  45.0 1.6 %collective-permute-start.4 = (bf16[768,512]{1,0:T(8,128)(2,1)S(1)}, bf16[768,512]{1,0:T(8,128)(2,1)S(1)}, u32[]{:S(2)}, u32[]{:S(2)}) collective-permute-start(bf16[768,512]{1,0:T(8,128)(2,1)S(1)} %fusion), channel_id=1, source_target_pairs={{0,2},{2,0},{1,3},{3,1},{4,6},{6,4},{5,7},{7,5},{8,10},{10,8},{9,1... | collective-permute-start | bytes 2359304 | tf_op jit(solution)/shard_map/ppermute | solution.py:333
  46.5 0.0 collective-permute-done.5.refs_0_
  46.5 0.0 copy-done.4
  46.5 0.0 collective-permute-start.12
  46.5 3.5 %collective-permute-done.6.refs_1_ = bf16[384,256]{1,0:T(8,128)(2,1)} collective-permute-done((bf16[384,256]{1,0:T(8,128)(2,1)}, bf16[384,256]{1,0:T(8,128)(2,1)}, u32[]{:S(2)}, u32[]{:S(2)}) %collective-permute-start.6) | collective-permute-done | bytes 196640 | tf_op jit(solution)/shard_map/ppermute | solution.py:282
  50.0 0.0 collective-permute-start.13
  50.0 0.0 collective-permute-done.7.refs_2_
  50.0 0.0 copy-done.6
  50.0 0.0 copy-start.8
  50.1 1.0 %copy-done.8 = bf16[12,128,128]{2,1,0:T(8,128)(2,1)S(1)} copy-done((bf16[12,128,128]{2,1,0:T(8,128)(2,1)S(1)}, bf16[12,128,128]{2,1,0:T(8,128)(2,1)}, u32[]{:S(2)}) %copy-start.8) | copy-done | bytes 393240
  51.0 0.0 copy-start.9
  51.0 4.7 %apply_cycle.3 = (bf16[384,256]{1,0:T(8,128)(2,1)S(1)}, bf16[384,256]{1,0:T(8,128)(2,1)S(1)}, bf16[384,256]{1,0:T(8,128)(2,1)S(1)}, bf16[384,256]{1,0:T(8,128)(2,1)S(1)}) custom-call(bf16[1536,1536]{1,0:T(8,128)(2,1)S(1)} %copy-done.6, bf16[12,128,128]{2,1,0:T(8,128)(2,1)S(1)} %copy-done.8, bf16[384,256]{1,0:T(8,128)(2,1)} %collective-permute-done.5.refs_0_, ...), custom_call_target="tpu_custom_call" | custom-call | flops 30000001024 | bytes 1000000 | tf_op jit(solution)/shard_map/apply_cycle/pallas_call | solution.py:200
  55.8 2.1 %collective-permute-start.10 = (bf16[384,256]{1,0:T(8,128)(2,1)S(1)}, bf16[384,256]{1,0:T(8,128)(2,1)S(1)}, u32[]{:S(2)}, u32[]{:S(2)}) collective-permute-start(bf16[384,256]{1,0:T(8,128)(2,1)S(1)} %get-tuple-element.63), channel_id=1, source_target_pairs={{0,4},{4,0},{8,12},{12,8},{1,5},{5,1},{9,13},{13,9},{2,6},{6,2},{1... | collective-permute-start | bytes 589832 | tf_op jit(solution)/shard_map/ppermute | solution.py:282
  57.8 0.0 collective-permute-done.11.refs_0_
  57.8 3.0 %collective-permute-start.8 = (bf16[384,256]{1,0:T(8,128)(2,1)S(1)}, bf16[384,256]{1,0:T(8,128)(2,1)S(1)}, u32[]{:S(2)}, u32[]{:S(2)}) collective-permute-start(bf16[384,256]{1,0:T(8,128)(2,1)S(1)} %get-tuple-element.61), channel_id=1, source_target_pairs={{0,12},{4,8},{8,4},{12,0},{1,13},{5,9},{9,5},{13,1},{2,14},{6,10},... | collective-permute-start | bytes 589832 | tf_op jit(solution)/shard_map/ppermute | solution.py:282
  60.8 0.6 collective-permute-done.4
  61.4 0.0 copy-start.2
  61.4 0.0 collective-permute-start.9
  61.4 0.0 copy-done.9
  61.4 1.5 %bitcast_add_fusion.base_ref = f32[768,512]{1,0:T(8,128)S(1)} fusion(bf16[768,512]{1,0:T(8,128)(2,1)S(1)} %collective-permute-done.4, bf16[1,768,512]{2,1,0:T(8,128)(2,1)S(1)} %copy-done.9, bf16[2,768,512]{2,1,0:T(8,128)(2,1)S(1)} %get-tuple-element.43, s32[]{:T(128)S(6)} %select_n.9, bf16[2,768,512]{2,1,0:T(8,128)(2,1)} %collective-permute-done.1), kind=kLoop, calls=%fused_computation | loop fusion | flops 2752512 | bytes 4718596 | tf_op jit(solution)/shard_map/add | solution.py:333
  62.9 1.3 %collective-permute-done.12.refs_1_ = bf16[384,256]{1,0:T(8,128)(2,1)S(1)} collective-permute-done((bf16[384,256]{1,0:T(8,128)(2,1)S(1)}, bf16[384,256]{1,0:T(8,128)(2,1)S(1)}, u32[]{:S(2)}, u32[]{:S(2)}) %collective-permute-start.12) | collective-permute-done | bytes 196640 | tf_op jit(solution)/shard_map/ppermute | solution.py:282
  64.2 0.0 collective-permute-done.13.refs_2_
  64.3 0.0 copy-done.2
  64.3 1.5 %finish.2.refs_4_ = bf16[768,512]{1,0:T(8,128)(2,1)} custom-call(bf16[768,1536]{1,0:T(8,128)(2,1)S(1)} %unpack_matrix.1.pick_ref, f32[768,512]{1,0:T(8,128)S(1)} %bitcast_add_fusion.base_ref, f32[768,1]{1,0:T(8,128)S(1)} %copy.12.part_ref, f32[1,512]{1,0:T(1,128)S(1)} %bitcast.18, bf16[384,256]{1,0:T(8,128)(2,1)S(1)} %collective-permute-done.11.refs_0_, ...), custom_call_target="tpu_custom_call" | custom-call | tf_op jit(solution)/shard_map/finish/pallas_call | solution.py:241
  65.8 2.0 %collective-permute-done.10.refs_2_ = bf16[384,256]{1,0:T(8,128)(2,1)S(1)} collective-permute-done((bf16[384,256]{1,0:T(8,128)(2,1)S(1)}, bf16[384,256]{1,0:T(8,128)(2,1)S(1)}, u32[]{:S(2)}, u32[]{:S(2)}) %collective-permute-start.10) | collective-permute-done | bytes 196640 | tf_op jit(solution)/shard_map/ppermute | solution.py:282
  67.8 0.0 collective-permute-done.8.refs_0_
  67.8 7.9 %collective-permute-done.9.refs_1_ = bf16[384,256]{1,0:T(8,128)(2,1)S(1)} collective-permute-done((bf16[384,256]{1,0:T(8,128)(2,1)S(1)}, bf16[384,256]{1,0:T(8,128)(2,1)S(1)}, u32[]{:S(2)}, u32[]{:S(2)}) %collective-permute-start.9) | collective-permute-done | bytes 196640 | tf_op jit(solution)/shard_map/ppermute | solution.py:282
  75.7 1.5 %finish.3 = bf16[768,512]{1,0:T(8,128)(2,1)} custom-call(bf16[768,1536]{1,0:T(8,128)(2,1)S(1)} %unpack_matrix.1.pick_ref, f32[768,512]{1,0:T(8,128)S(1)} %bitcast_add_fusion.base_ref, f32[768,1]{1,0:T(8,128)S(1)} %copy.12.part_ref, f32[1,512]{1,0:T(1,128)S(1)} %bitcast.19, ...), custom_call_target="tpu_custom_call", output_to_operand_aliasing={{}: (8, {})} | custom-call | tf_op jit(solution)/shard_map/finish/pallas_call | solution.py:241
Async XLA Ops:
  1.7 0.6 copy-start
  2.3 8.3 %collective-permute-start = (bf16[384,256]{1,0:T(8,128)(2,1)S(1)}, bf16[384,256]{1,0:T(8,128)(2,1)S(1)}, u32[]{:S(2)}, u32[]{:S(2)}) collective-permute-start(bf16[384,256]{1,0:T(8,128)(2,1)S(1)} %get-tuple-element.36), channel_id=1, source_target_pairs={{0,4},{4,0},{8,12},{12,8},{1,5},{5,1},{9,13},{13,9},{2,6},{6,2},{1... | collective-permute-start | bytes 589832 | tf_op jit(solution)/shard_map/ppermute | solution.py:282
  5.3 23.1 %collective-permute-start.2 = (bf16[384,256]{1,0:T(8,128)(2,1)S(1)}, bf16[384,256]{1,0:T(8,128)(2,1)S(1)}, u32[]{:S(2)}, u32[]{:S(2)}) collective-permute-start(bf16[384,256]{1,0:T(8,128)(2,1)S(1)} %get-tuple-element.46), channel_id=1, source_target_pairs={{0,12},{4,8},{8,4},{12,0},{1,13},{5,9},{9,5},{13,1},{2,14},{6,10},... | collective-permute-start | bytes 589832 | tf_op jit(solution)/shard_map/ppermute | solution.py:282
  7.8 26.9 %collective-permute-start.3 = (bf16[384,256]{1,0:T(8,128)(2,1)S(1)}, bf16[384,256]{1,0:T(8,128)(2,1)S(1)}, u32[]{:S(2)}, u32[]{:S(2)}) collective-permute-start(bf16[384,256]{1,0:T(8,128)(2,1)S(1)} %get-tuple-element.47), channel_id=1, source_target_pairs={{0,8},{4,12},{8,0},{12,4},{1,9},{5,13},{9,1},{13,5},{2,10},{6,14},... | collective-permute-start | bytes 589832 | tf_op jit(solution)/shard_map/ppermute | solution.py:282
  13.2 33.3 %collective-permute-start.5 = (bf16[384,256]{1,0:T(8,128)(2,1)}, bf16[384,256]{1,0:T(8,128)(2,1)}, u32[]{:S(2)}, u32[]{:S(2)}) collective-permute-start(bf16[384,256]{1,0:T(8,128)(2,1)} %get-tuple-element.38), channel_id=1, source_target_pairs={{0,12},{4,8},{8,4},{12,0},{1,13},{5,9},{9,5},{13,1},{2,14},{6,10},... | collective-permute-start | bytes 589832 | tf_op jit(solution)/shard_map/ppermute | solution.py:282
  20.0 30.1 %collective-permute-start.6 = (bf16[384,256]{1,0:T(8,128)(2,1)}, bf16[384,256]{1,0:T(8,128)(2,1)}, u32[]{:S(2)}, u32[]{:S(2)}) collective-permute-start(bf16[384,256]{1,0:T(8,128)(2,1)} %get-tuple-element.39), channel_id=1, source_target_pairs={{0,8},{4,12},{8,0},{12,4},{1,9},{5,13},{9,1},{13,5},{2,10},{6,14},... | collective-permute-start | bytes 589832 | tf_op jit(solution)/shard_map/ppermute | solution.py:282
  20.0 30.1 %collective-permute-start.7 = (bf16[384,256]{1,0:T(8,128)(2,1)}, bf16[384,256]{1,0:T(8,128)(2,1)}, u32[]{:S(2)}, u32[]{:S(2)}) collective-permute-start(bf16[384,256]{1,0:T(8,128)(2,1)} %get-tuple-element.40), channel_id=1, source_target_pairs={{0,4},{4,0},{8,12},{12,8},{1,5},{5,1},{9,13},{13,9},{2,6},{6,2},{1... | collective-permute-start | bytes 589832 | tf_op jit(solution)/shard_map/ppermute | solution.py:282
  28.3 9.9 %copy-start.5 = (bf16[1536,1536]{1,0:T(8,128)(2,1)}, bf16[1536,1536]{1,0:T(8,128)(2,1)S(1)}, u32[]{:S(2)}) copy-start(bf16[1536,1536]{1,0:T(8,128)(2,1)S(1)} %get-tuple-element.44.weight_ref) | copy-start | bytes 14155780
  28.4 9.9 %copy-start.7 = (bf16[12,128,128]{2,1,0:T(8,128)(2,1)}, bf16[12,128,128]{2,1,0:T(8,128)(2,1)S(1)}, u32[]{:S(2)}) copy-start(bf16[12,128,128]{2,1,0:T(8,128)(2,1)S(1)} %get-tuple-element.45.mixing_ref) | copy-start | bytes 1179652
  28.4 14.9 %collective-permute-start.1 = (bf16[2,768,512]{2,1,0:T(8,128)(2,1)}, bf16[2,768,512]{2,1,0:T(8,128)(2,1)}, u32[]{:S(2)}, u32[]{:S(2)}) collective-permute-start(bf16[2,768,512]{2,1,0:T(8,128)(2,1)} %ladder_part.2), channel_id=1, source_target_pairs={{0,1},{1,0},{2,3},{3,2},{4,5},{5,4},{6,7},{7,6},{8,9},{9,8},{10,11... | collective-permute-start | bytes 4718600 | tf_op jit(solution)/shard_map/ppermute | solution.py:310
  34.7 7.2 %copy-start.1 = (s32[1,768]{1,0:T(1,128)S(1)}, s32[1,768]{1,0:T(1,128)}, u32[]{:S(2)}) copy-start(s32[1,768]{1,0:T(1,128)} %copy-done) | copy-start | bytes 9220
  38.3 0.7 copy-start.3
  39.0 18.9 %collective-permute-start.11 = (bf16[384,256]{1,0:T(8,128)(2,1)}, bf16[384,256]{1,0:T(8,128)(2,1)S(1)}, u32[]{:S(2)}, u32[]{:S(2)}) collective-permute-start(bf16[384,256]{1,0:T(8,128)(2,1)} %get-tuple-element.53), channel_id=1, source_target_pairs={{0,12},{4,8},{8,4},{12,0},{1,13},{5,9},{9,5},{13,1},{2,14},{6,10},... | collective-permute-start | bytes 589832 | tf_op jit(solution)/shard_map/ppermute | solution.py:282
  42.1 7.9 %copy-start.6 = (bf16[1536,1536]{1,0:T(8,128)(2,1)S(1)}, bf16[1536,1536]{1,0:T(8,128)(2,1)}, u32[]{:S(2)}) copy-start(bf16[1536,1536]{1,0:T(8,128)(2,1)} %copy-done.5) | copy-start | bytes 14155780
  43.2 3.3 %copy-start.4 = (bf16[384,256]{1,0:T(8,128)(2,1)S(1)}, bf16[384,256]{1,0:T(8,128)(2,1)}, u32[]{:S(2)}) copy-start(bf16[384,256]{1,0:T(8,128)(2,1)} %copy-done.3) | copy-start | bytes 589828
  45.0 16.4 %collective-permute-start.4 = (bf16[768,512]{1,0:T(8,128)(2,1)S(1)}, bf16[768,512]{1,0:T(8,128)(2,1)S(1)}, u32[]{:S(2)}, u32[]{:S(2)}) collective-permute-start(bf16[768,512]{1,0:T(8,128)(2,1)S(1)} %fusion), channel_id=1, source_target_pairs={{0,2},{2,0},{1,3},{3,1},{4,6},{6,4},{5,7},{7,5},{8,10},{10,8},{9,1... | collective-permute-start | bytes 2359304 | tf_op jit(solution)/shard_map/ppermute | solution.py:333
  46.5 17.7 %collective-permute-start.12 = (bf16[384,256]{1,0:T(8,128)(2,1)S(1)}, bf16[384,256]{1,0:T(8,128)(2,1)S(1)}, u32[]{:S(2)}, u32[]{:S(2)}) collective-permute-start(bf16[384,256]{1,0:T(8,128)(2,1)S(1)} %copy-done.4), channel_id=1, source_target_pairs={{0,8},{4,12},{8,0},{12,4},{1,9},{5,13},{9,1},{13,5},{2,10},{6,14},... | collective-permute-start | bytes 589832 | tf_op jit(solution)/shard_map/ppermute | solution.py:282
  50.0 14.2 %collective-permute-start.13 = (bf16[384,256]{1,0:T(8,128)(2,1)S(1)}, bf16[384,256]{1,0:T(8,128)(2,1)S(1)}, u32[]{:S(2)}, u32[]{:S(2)}) collective-permute-start(bf16[384,256]{1,0:T(8,128)(2,1)S(1)} %get-tuple-element.55), channel_id=1, source_target_pairs={{0,4},{4,0},{8,12},{12,8},{1,5},{5,1},{9,13},{13,9},{2,6},{6,2},{1... | collective-permute-start | bytes 589832 | tf_op jit(solution)/shard_map/ppermute | solution.py:282
  50.0 1.0 %copy-start.8 = (bf16[12,128,128]{2,1,0:T(8,128)(2,1)S(1)}, bf16[12,128,128]{2,1,0:T(8,128)(2,1)}, u32[]{:S(2)}) copy-start(bf16[12,128,128]{2,1,0:T(8,128)(2,1)} %copy-done.7) | copy-start | bytes 1179652
  51.0 10.3 %copy-start.9 = (bf16[1,768,512]{2,1,0:T(8,128)(2,1)S(1)}, bf16[1,768,512]{2,1,0:T(8,128)(2,1)}, u32[]{:S(2)}) copy-start(bf16[1,768,512]{2,1,0:T(8,128)(2,1)} %param.9) | copy-start | bytes 2359300
  55.8 12.0 %collective-permute-start.10 = (bf16[384,256]{1,0:T(8,128)(2,1)S(1)}, bf16[384,256]{1,0:T(8,128)(2,1)S(1)}, u32[]{:S(2)}, u32[]{:S(2)}) collective-permute-start(bf16[384,256]{1,0:T(8,128)(2,1)S(1)} %get-tuple-element.63), channel_id=1, source_target_pairs={{0,4},{4,0},{8,12},{12,8},{1,5},{5,1},{9,13},{13,9},{2,6},{6,2},{1... | collective-permute-start | bytes 589832 | tf_op jit(solution)/shard_map/ppermute | solution.py:282
  57.8 10.0 %collective-permute-start.8 = (bf16[384,256]{1,0:T(8,128)(2,1)S(1)}, bf16[384,256]{1,0:T(8,128)(2,1)S(1)}, u32[]{:S(2)}, u32[]{:S(2)}) collective-permute-start(bf16[384,256]{1,0:T(8,128)(2,1)S(1)} %get-tuple-element.61), channel_id=1, source_target_pairs={{0,12},{4,8},{8,4},{12,0},{1,13},{5,9},{9,5},{13,1},{2,14},{6,10},... | collective-permute-start | bytes 589832 | tf_op jit(solution)/shard_map/ppermute | solution.py:282
  61.4 2.9 %copy-start.2 = (f32[512]{0:T(512)S(1)}, f32[512]{0:T(512)}, u32[]{:S(2)}) copy-start(f32[512]{0:T(512)} %param.15) | copy-start | bytes 6148
  61.4 14.4 %collective-permute-start.9 = (bf16[384,256]{1,0:T(8,128)(2,1)S(1)}, bf16[384,256]{1,0:T(8,128)(2,1)S(1)}, u32[]{:S(2)}, u32[]{:S(2)}) collective-permute-start(bf16[384,256]{1,0:T(8,128)(2,1)S(1)} %get-tuple-element.62), channel_id=1, source_target_pairs={{0,8},{4,12},{8,0},{12,4},{1,9},{5,13},{9,1},{13,5},{2,10},{6,14},... | collective-permute-start | bytes 589832 | tf_op jit(solution)/shard_map/ppermute | solution.py:282

commit v8 on v7

--- a/solution.py
+++ b/solution.py
@@ -7,7 +7,7 @@
 from jax.experimental.pallas import tpu as pltpu
 from jax.sharding import PartitionSpec as P
 
-VMEM_LIMIT = 32 * 1024 * 1024
+VMEM_LIMIT = 16 * 1024 * 1024
 HALVES = 2
 F32 = jnp.float32
 BF16 = jnp.bfloat16
@@ -59,27 +59,27 @@
     return owners * send + jnp.concatenate(slots, axis=1).astype(jnp.int32)
 
 
-def pack_kernel(plan, given, route_hbm, amps_hbm, *refs):
+def pack_kernel(plan, given, route_in, amps_hbm, *refs):
     paired, chan_count, send, block_rows, items = plan
     outs, (route_ref, amps_ref, sems) = refs[:-3], refs[-3:]
     block_refs = outs if given else outs[1:]
-    copies = [
-        pltpu.make_async_copy(route_hbm, route_ref, sems.at[0]),
-        pltpu.make_async_copy(amps_hbm.at[:, pl.ds(0, amps_ref.shape[1])], amps_ref, sems.at[1]),
-    ]
-    for copy in copies:
-        copy.start()
-    copies[0].wait()
-    target = route_ref[...]
-    if not given:
-        target = slots_of(target, send, max(16, chan_count))
+    amps_copy = pltpu.make_async_copy(amps_hbm.at[:, pl.ds(0, amps_ref.shape[1])], amps_ref, sems.at[1])
+    if given:
+        amps_copy.start()
+        target = route_in[...]
+    else:
+        route_copy = pltpu.make_async_copy(route_in, route_ref, sems.at[0])
+        route_copy.start()
+        amps_copy.start()
+        route_copy.wait()
+        target = slots_of(route_ref[...], send, max(16, chan_count))
         outs[0][...] = target
     offsets = block_offsets(paired, chan_count, block_rows)
     slot = lax.broadcasted_iota(jnp.int32, (block_rows, target.shape[1]), 0)
     for i, (k, first, width) in enumerate(items):
         pick = selection(slot == target - offsets[k])
         if i == 0:
-            copies[1].wait()
+            amps_copy.wait()
         block_refs[i][...] = jnp.dot(
             pick, amps_ref[:, pl.ds(first, width)], preferred_element_type=F32
         ).astype(BF16)
@@ -93,7 +93,7 @@
     return pl.pallas_call(
         functools.partial(pack_kernel, plan, given),
         out_shape=extra + [pltpu.VMEM((block_rows, width), BF16) for _, _, width in items],
-        in_specs=[whole(pl.ANY), whole(pl.ANY)],
+        in_specs=[whole() if given else whole(pl.ANY), whole(pl.ANY)],
         out_specs=[whole()] * (len(extra) + len(items)),
         scratch_shapes=[
             pltpu.VMEM((1, rows), jnp.int32),
@@ -102,7 +102,7 @@
         ],
         compiler_params=params(),
         name=name,
-    )(*in_hbm(route_row, amps))
+    )(*([route_row] if given else in_hbm(route_row)), *in_hbm(amps))
 
 
 def unpack_kernel(off_ref, target_ref, out_ref):
@@ -127,55 +127,57 @@
     )(offsets, target_column)
 
 
-def ladder_kernel(step, sub_count, weight_hbm, amps_hbm, *refs):
-    moved = (len(refs) - 4) // 2
-    source_refs, part_ref, held_refs = refs[:moved], refs[moved], refs[moved + 1 : 2 * moved + 1]
-    weight_ref, amps_ref, sems = refs[2 * moved + 1 :]
+def ladder_kernel(step, sub_count, weight_hbm, amps_hbm, part_ref, weight_ref, amps_ref, sems):
     rows, lad_count = amps_ref.shape[0], part_ref.shape[0]
     share = lax.rem(lax.axis_index("sub") + step, sub_count)
     copies = [pltpu.make_async_copy(amps_hbm, amps_ref, sems.at[0])]
     for i in range(lad_count):
         start = pl.multiple_of((i * sub_count + share) * rows, rows)
         copies.append(pltpu.make_async_copy(weight_hbm.at[pl.ds(start, rows), :], weight_ref.at[i], sems.at[1 + i]))
-    for n, (source, held) in enumerate(zip(source_refs, held_refs)):
-        copies.append(pltpu.make_async_copy(source, held, sems.at[1 + lad_count + n]))
     for copy in copies:
         copy.start()
     copies[0].wait()
     for i in range(lad_count):
         copies[1 + i].wait()
         part_ref[i] = jnp.dot(weight_ref[i], amps_ref[...], preferred_element_type=F32).astype(BF16)
-    for copy in copies[1 + lad_count :]:
-        copy.wait()
-
-
-def ladder_part(step, weight, amps, lad_count, sub_count, moved):
+
+
+def ladder_part(step, weight, amps, lad_count, sub_count):
     rows, holes = amps.shape
     return pl.pallas_call(
         functools.partial(ladder_kernel, step, sub_count),
-        out_shape=[pltpu.VMEM((lad_count, rows, holes), BF16)] + [pltpu.VMEM(m.shape, BF16) for m in moved],
-        in_specs=[whole(pl.ANY)] * (2 + len(moved)),
-        out_specs=[whole()] * (1 + len(moved)),
+        out_shape=pltpu.VMEM((lad_count, rows, holes), BF16),
+        in_specs=[whole(pl.ANY)] * 2,
+        out_specs=whole(),
         scratch_shapes=[
             pltpu.VMEM((lad_count, rows, rows), BF16),
             pltpu.VMEM((rows, holes), BF16),
-            pltpu.SemaphoreType.DMA((1 + lad_count + len(moved),)),
+            pltpu.SemaphoreType.DMA((1 + lad_count,)),
         ],
         compiler_params=params(),
         cost_estimate=DEAR,
         name="ladder_part",
-    )(*in_hbm(weight, amps, *moved))
-
-
-def cycle_kernel(half, plan, weight_ref, mixing_ref, *refs):
+    )(*in_hbm(weight, amps))
+
+
+def cycle_kernel(half, plan, weight_hbm, mixing_hbm, *refs):
     paired, chan_count, _, _ = plan
-    count = len(refs) // 2 - 1
-    in_refs, out_refs, (mixed_ref, back_ref) = refs[:count], refs[count : 2 * count], refs[2 * count :]
+    count = (len(refs) - 5) // 2
+    in_refs, out_refs = refs[:count], refs[count : 2 * count]
+    weight_ref, mixing_ref, mixed_ref, back_ref, sems = refs[2 * count :]
     block_rows, width = out_refs[0].shape
     group = mixing_ref.shape[1]
     offsets = block_offsets(paired, chan_count, block_rows)
-    for i, in_ref in enumerate(in_refs):
-        start = pl.multiple_of(offsets[count - 1 - i], block_rows)
+    starts = [pl.multiple_of(offsets[count - 1 - i], block_rows) for i in range(count)]
+    mixing_copy = pltpu.make_async_copy(mixing_hbm, mixing_ref, sems.at[0])
+    copies = [
+        pltpu.make_async_copy(weight_hbm.at[pl.ds(start, block_rows), :], weight_ref.at[i], sems.at[1 + i])
+        for i, start in enumerate(starts)
+    ]
+    for copy in [mixing_copy] + copies:
+        copy.start()
+    mixing_copy.wait()
+    for in_ref, start in zip(in_refs, starts):
         for a in range(block_rows // group):
             at = pl.ds(a * group, group)
             part = in_ref[at, :] if in_ref.shape[1] == width else in_ref[at, pl.ds(half * width, width)]
@@ -183,11 +185,9 @@
             mixed_ref[pl.ds(pl.multiple_of(start + a * group, group), group), :] = jnp.dot(
                 mix, part, preferred_element_type=F32
             ).astype(BF16)
-    for i, out_ref in enumerate(out_refs):
-        start = pl.multiple_of(offsets[count - 1 - i], block_rows)
-        back_ref[...] = jnp.dot(
-            weight_ref[pl.ds(start, block_rows), :], mixed_ref[...], preferred_element_type=F32
-        ).astype(BF16)
+    for i, (out_ref, start) in enumerate(zip(out_refs, starts)):
+        copies[i].wait()
+        back_ref[...] = jnp.dot(weight_ref[i], mixed_ref[...], preferred_element_type=F32).astype(BF16)
         for a in range(block_rows // group):
             at = pl.ds(a * group, group)
             mix = mixing_ref[lax.div(start, group) + a]
@@ -197,16 +197,24 @@
 
 
 def apply_cycle(half, plan, weight, mixing, arrays, width):
+    count, block_rows = len(arrays), arrays[0].shape[0]
+    capacity = weight.shape[0]
     return pl.pallas_call(
         functools.partial(cycle_kernel, half, plan),
-        out_shape=[jax.ShapeDtypeStruct((a.shape[0], width), BF16) for a in arrays],
-        in_specs=[whole()] * (2 + len(arrays)),
-        out_specs=[whole()] * len(arrays),
-        scratch_shapes=[pltpu.VMEM((weight.shape[0], width), BF16), pltpu.VMEM((arrays[0].shape[0], width), BF16)],
+        out_shape=[pltpu.VMEM((block_rows, width), BF16)] * count,
+        in_specs=[whole(pl.ANY)] * 2 + [whole()] * count,
+        out_specs=[whole()] * count,
+        scratch_shapes=[
+            pltpu.VMEM((count, block_rows, capacity), BF16),
+            pltpu.VMEM(mixing.shape, BF16),
+            pltpu.VMEM((capacity, width), BF16),
+            pltpu.VMEM((block_rows, width), BF16),
+            pltpu.SemaphoreType.DMA((1 + count,)),
+        ],
         compiler_params=params(),
         cost_estimate=DEAR,
         name="apply_cycle",
-    )(weight, mixing, *arrays)
+    )(*in_hbm(weight, mixing), *arrays)
 
 
 def finish_kernel(half, count, tiles, pick_ref, base_ref, part_ref, hole_ref, *refs):
@@ -304,12 +312,9 @@
 
     kept = []
     for step in reversed(range(sub_count)):
-        moved = [] if step else [mixing, weight]
-        part, *moved = ladder_part(step, ladder_weight[0], amps, lad_count, sub_count, moved)
+        part = ladder_part(step, ladder_weight[0], amps, lad_count, sub_count)
         if step:
             part = lax.ppermute(part, "sub", [(i, (i + step) % sub_count) for i in range(sub_count)])
-        else:
-            mixing, weight = moved
         kept.append(part)
 
     def chip_sum(position):

time: 77.5 us -> 77 us (level)
  Pallas kernels: 24.4 us -> 27.2 us
  local copies, waits for them, and re-layouts: 3.33 us -> 1.73 us
  waiting for transfers between devices: 23.4 us -> 22.2 us
    pallas_call x2, Pallas kernels: 8.25 us -> 11.6 us  [apply_cycle(): pl.pallas_call(functools.partial(cycle_kernel, half, plan), out_shape=[pl...]
    unnamed x20 -> x8, local copies, waits for them, and re-layouts: 2.29 us -> 0.69 us
  transfers between devices with their start and end apart: 14 -> 14, of which waited for: 7 -> 5; matrix products, arithmetic and copies ran while one was open for 6% -> 5% of each run, Pallas kernels for 27% -> 31%
where the time goes in v8:
time: 77 us; the launch traced here: 76.7 us
  Pallas kernels  27.2 us (35%)
  starting transfers between devices  22.4 us (29%)
  waiting for transfers between devices  22.2 us (29%)
  other arithmetic  3 us (4%)
  local copies, waits for them, and re-layouts  1.73 us (2%)
    ppermute x12, waiting for transfers between devices, exchange(): lax.ppermute(block, 'chan', [(i, i ^ k) for i in range(chan_count)])  22.2 us
    ppermute x12, starting transfers between devices, exchange(): lax.ppermute(block, 'chan', [(i, i ^ k) for i in range(chan_count)])  20.8 us
    pallas_call x2, Pallas kernels, apply_cycle(): pl.pallas_call(functools.partial(cycle_kernel, half, plan), out_shape=[pl...  11.6 us
    pallas_call x2, Pallas kernels, ladder_part(): pl.pallas_call(functools.partial(ladder_kernel, step, sub_count), out_sha...  7.31 us
    pallas_call x2, Pallas kernels, pack(): pl.pallas_call(functools.partial(pack_kernel, plan, given), out_shape=ext...  4.18 us
    pallas_call x2, Pallas kernels, finish(): pl.pallas_call(functools.partial(finish_kernel, half, len(arrays), tiles)...  3.04 us
    ppermute x1, starting transfers between devices, body(): base = base + lax.ppermute(term, 'lad', pairs).astype(F32)  1.56 us
  transfers between devices with their start and end apart: 14, of which 5 were waited for; matrix products, arithmetic and copies ran while one was open for 5% of the time, Pallas kernels for 31%

profile of v8, /device:TPU:0, one launch (start us, length us, event | category | flops | bytes accessed | tf_op | source)
XLA Modules:
  0.0 76.7 jit_solution(3758358737173659336)
XLA Ops:
  0.0 1.7 %pack_first.1 = (s32[1,768]{1,0:T(1,128)S(1)}, bf16[384,256]{1,0:T(8,128)(2,1)S(1)}, bf16[384,256]{1,0:T(8,128)(2,1)S(1)}, bf16[384,256]{1,0:T(8,128)(2,1)S(1)}) custom-call(s32[1,768]{1,0:T(1,128)} %bitcast.24, bf16[768,512]{1,0:T(8,128)(2,1)} %bitcast.20), custom_call_target="tpu_custom_call" | custom-call | tf_op jit(solution)/shard_map/pack_first/pallas_call | solution.py:93
  1.7 3.1 %collective-permute-start = (bf16[384,256]{1,0:T(8,128)(2,1)S(1)}, bf16[384,256]{1,0:T(8,128)(2,1)S(1)}, u32[]{:S(2)}, u32[]{:S(2)}) collective-permute-start(bf16[384,256]{1,0:T(8,128)(2,1)S(1)} %get-tuple-element.33), channel_id=1, source_target_pairs={{0,4},{4,0},{8,12},{12,8},{1,5},{5,1},{9,13},{13,9},{2,6},{6,2},{1... | collective-permute-start | bytes 589832 | tf_op jit(solution)/shard_map/ppermute | solution.py:290
  4.8 2.5 %collective-permute-start.2 = (bf16[384,256]{1,0:T(8,128)(2,1)S(1)}, bf16[384,256]{1,0:T(8,128)(2,1)S(1)}, u32[]{:S(2)}, u32[]{:S(2)}) collective-permute-start(bf16[384,256]{1,0:T(8,128)(2,1)S(1)} %get-tuple-element.40), channel_id=1, source_target_pairs={{0,12},{4,8},{8,4},{12,0},{1,13},{5,9},{9,5},{13,1},{2,14},{6,10},... | collective-permute-start | bytes 589832 | tf_op jit(solution)/shard_map/ppermute | solution.py:290
  7.2 0.1 collective-permute-start.3
  7.4 0.9 %copy.12.part_ref = f32[768,1]{1,0:T(8,128)S(1)} copy(f32[768,1]{0,1:T(1,128)} %bitcast.25) | data formatting | bytes 6144 | tf_op jit(solution)/shard_map/reshape;squeeze | solution.py:309
  8.2 0.1 add_multiply_fusion.off_ref
  8.3 1.8 %collective-permute-done.refs_2_ = bf16[384,256]{1,0:T(8,128)(2,1)S(1)} collective-permute-done((bf16[384,256]{1,0:T(8,128)(2,1)S(1)}, bf16[384,256]{1,0:T(8,128)(2,1)S(1)}, u32[]{:S(2)}, u32[]{:S(2)}) %collective-permute-start) | collective-permute-done | bytes 196640 | tf_op jit(solution)/shard_map/ppermute | solution.py:290
  10.1 2.5 %pack_rest.1 = (bf16[384,256]{1,0:T(8,128)(2,1)}, bf16[384,256]{1,0:T(8,128)(2,1)}, bf16[384,256]{1,0:T(8,128)(2,1)}, bf16[384,512]{1,0:T(8,128)(2,1)S(1)}) custom-call(s32[1,768]{1,0:T(1,128)S(1)} %get-tuple-element.34.route_in, bf16[768,512]{1,0:T(8,128)(2,1)} %bitcast.21), custom_call_target="tpu_custom_call" | custom-call | tf_op jit(solution)/shard_map/pack_rest/pallas_call | solution.py:93
  12.6 4.2 %ladder_part.2 = bf16[2,768,512]{2,1,0:T(8,128)(2,1)} custom-call(bf16[3072,768]{1,0:T(8,128)(2,1)} %bitcast.26, bf16[768,512]{1,0:T(8,128)(2,1)} %bitcast.22), custom_call_target="tpu_custom_call" | custom-call | flops 30000001024 | bytes 1000000 | tf_op jit(solution)/shard_map/ladder_part/pallas_call | solution.py:147
  16.8 3.1 %ladder_part.3 = bf16[2,768,512]{2,1,0:T(8,128)(2,1)S(1)} custom-call(bf16[3072,768]{1,0:T(8,128)(2,1)} %bitcast.27, bf16[768,512]{1,0:T(8,128)(2,1)} %bitcast.23), custom_call_target="tpu_custom_call" | custom-call | flops 30000001024 | bytes 1000000 | tf_op jit(solution)/shard_map/ladder_part/pallas_call | solution.py:147
  19.9 6.8 %collective-permute-start.5 = (bf16[384,256]{1,0:T(8,128)(2,1)}, bf16[384,256]{1,0:T(8,128)(2,1)}, u32[]{:S(2)}, u32[]{:S(2)}) collective-permute-start(bf16[384,256]{1,0:T(8,128)(2,1)} %get-tuple-element.35), channel_id=1, source_target_pairs={{0,12},{4,8},{8,4},{12,0},{1,13},{5,9},{9,5},{13,1},{2,14},{6,10},... | collective-permute-start | bytes 589832 | tf_op jit(solution)/shard_map/ppermute | solution.py:290
  26.7 0.0 collective-permute-start.6
  26.7 0.6 collective-permute-start.7
  27.3 0.0 collective-permute-done.2.refs_0_
  27.3 0.0 collective-permute-start.1
  27.3 4.1 %collective-permute-done.3.refs_1_ = bf16[384,256]{1,0:T(8,128)(2,1)S(1)} collective-permute-done((bf16[384,256]{1,0:T(8,128)(2,1)S(1)}, bf16[384,256]{1,0:T(8,128)(2,1)S(1)}, u32[]{:S(2)}, u32[]{:S(2)}) %collective-permute-start.3) | collective-permute-done | bytes 196640 | tf_op jit(solution)/shard_map/ppermute | solution.py:290
  31.4 5.4 %apply_cycle.2 = (bf16[384,256]{1,0:T(8,128)(2,1)}, bf16[384,256]{1,0:T(8,128)(2,1)S(1)}, bf16[384,256]{1,0:T(8,128)(2,1)S(1)}, bf16[384,256]{1,0:T(8,128)(2,1)S(1)}) custom-call(bf16[1536,1536]{1,0:T(8,128)(2,1)} %bitcast.28, bf16[12,128,128]{2,1,0:T(8,128)(2,1)} %bitcast.30, bf16[384,256]{1,0:T(8,128)(2,1)S(1)} %collective-permute-done.2.refs_0_, ...), custom_call_target="tpu_custom_call" | custom-call | flops 30000001024 | bytes 1000000 | tf_op jit(solution)/shard_map/apply_cycle/pallas_call | solution.py:202
  36.8 0.0 copy-start.1
  36.8 0.7 copy-done.1
  37.5 2.2 %collective-permute-start.11 = (bf16[384,256]{1,0:T(8,128)(2,1)}, bf16[384,256]{1,0:T(8,128)(2,1)S(1)}, u32[]{:S(2)}, u32[]{:S(2)}) collective-permute-start(bf16[384,256]{1,0:T(8,128)(2,1)} %get-tuple-element.47), channel_id=1, source_target_pairs={{0,12},{4,8},{8,4},{12,0},{1,13},{5,9},{9,5},{13,1},{2,14},{6,10},... | collective-permute-start | bytes 589832 | tf_op jit(solution)/shard_map/ppermute | solution.py:290
  39.7 0.2 copy.10.target_ref
  39.9 1.1 %unpack_matrix.1.pick_ref = bf16[768,1536]{1,0:T(8,128)(2,1)S(1)} custom-call(s32[4]{0:T(128)S(1)} %add_multiply_fusion.off_ref, s32[768,1]{1,0:T(8,128)S(1)} %copy.10.target_ref), custom_call_target="tpu_custom_call" | custom-call | tf_op jit(solution)/shard_map/unpack_matrix/pallas_call | solution.py:119
  41.0 0.0 copy-start.2
  41.0 0.0 collective-permute-done.1
  41.0 1.4 %fusion = bf16[768,512]{1,0:T(8,128)(2,1)S(1)} fusion(bf16[2,768,512]{2,1,0:T(8,128)(2,1)S(1)} %ladder_part.3, s32[]{:T(128)S(6)} %select_n.10, bf16[2,768,512]{2,1,0:T(8,128)(2,1)} %collective-permute-done.1), kind=kLoop, calls=%fused_computation.2 | loop fusion | flops 1572864 | bytes 2359300 | tf_op jit(solution)/shard_map/convert_element_type | solution.py:325
  42.4 0.0 copy-start.3
  42.4 1.6 %collective-permute-start.4 = (bf16[768,512]{1,0:T(8,128)(2,1)S(1)}, bf16[768,512]{1,0:T(8,128)(2,1)S(1)}, u32[]{:S(2)}, u32[]{:S(2)}) collective-permute-start(bf16[768,512]{1,0:T(8,128)(2,1)S(1)} %fusion), channel_id=1, source_target_pairs={{0,2},{2,0},{1,3},{3,1},{4,6},{6,4},{5,7},{7,5},{8,10},{10,8},{9,1... | collective-permute-start | bytes 2359304 | tf_op jit(solution)/shard_map/ppermute | solution.py:338
  44.0 0.0 collective-permute-done.5.refs_0_
  44.0 0.0 copy-done.2
  44.0 0.0 collective-permute-start.12
  44.0 6.7 %collective-permute-done.6.refs_1_ = bf16[384,256]{1,0:T(8,128)(2,1)} collective-permute-done((bf16[384,256]{1,0:T(8,128)(2,1)}, bf16[384,256]{1,0:T(8,128)(2,1)}, u32[]{:S(2)}, u32[]{:S(2)}) %collective-permute-start.6) | collective-permute-done | bytes 196640 | tf_op jit(solution)/shard_map/ppermute | solution.py:290
  50.7 0.5 collective-permute-start.13
  51.2 0.0 collective-permute-done.7.refs_2_
  51.2 6.2 %apply_cycle.3 = (bf16[384,256]{1,0:T(8,128)(2,1)S(1)}, bf16[384,256]{1,0:T(8,128)(2,1)S(1)}, bf16[384,256]{1,0:T(8,128)(2,1)S(1)}, bf16[384,256]{1,0:T(8,128)(2,1)S(1)}) custom-call(bf16[1536,1536]{1,0:T(8,128)(2,1)} %bitcast.29, bf16[12,128,128]{2,1,0:T(8,128)(2,1)} %bitcast.31, bf16[384,256]{1,0:T(8,128)(2,1)} %collective-permute-done.5.refs_0_, ...), custom_call_target="tpu_custom_call" | custom-call | flops 30000001024 | bytes 1000000 | tf_op jit(solution)/shard_map/apply_cycle/pallas_call | solution.py:202
  57.4 1.6 %collective-permute-start.10 = (bf16[384,256]{1,0:T(8,128)(2,1)S(1)}, bf16[384,256]{1,0:T(8,128)(2,1)S(1)}, u32[]{:S(2)}, u32[]{:S(2)}) collective-permute-start(bf16[384,256]{1,0:T(8,128)(2,1)S(1)} %get-tuple-element.57), channel_id=1, source_target_pairs={{0,4},{4,0},{8,12},{12,8},{1,5},{5,1},{9,13},{13,9},{2,6},{6,2},{1... | collective-permute-start | bytes 589832 | tf_op jit(solution)/shard_map/ppermute | solution.py:290
  59.0 0.0 collective-permute-done.11.refs_0_
  59.0 3.4 %collective-permute-start.8 = (bf16[384,256]{1,0:T(8,128)(2,1)S(1)}, bf16[384,256]{1,0:T(8,128)(2,1)S(1)}, u32[]{:S(2)}, u32[]{:S(2)}) collective-permute-start(bf16[384,256]{1,0:T(8,128)(2,1)S(1)} %get-tuple-element.55), channel_id=1, source_target_pairs={{0,12},{4,8},{8,4},{12,0},{1,13},{5,9},{9,5},{13,1},{2,14},{6,10},... | collective-permute-start | bytes 589832 | tf_op jit(solution)/shard_map/ppermute | solution.py:290
  62.4 0.0 collective-permute-done.4
  62.4 0.0 copy-start
  62.4 0.0 collective-permute-start.9
  62.5 0.0 copy-done.3
  62.5 1.5 %bitcast_add_fusion.base_ref = f32[768,512]{1,0:T(8,128)S(1)} fusion(bf16[768,512]{1,0:T(8,128)(2,1)S(1)} %collective-permute-done.4, bf16[1,768,512]{2,1,0:T(8,128)(2,1)S(1)} %copy-done.3, bf16[2,768,512]{2,1,0:T(8,128)(2,1)S(1)} %ladder_part.3, s32[]{:T(128)S(6)} %select_n.9, bf16[2,768,512]{2,1,0:T(8,128)(2,1)} %collective-permute-done.1), kind=kLoop, calls=%fused_computation | loop fusion | flops 2752512 | bytes 4718596 | tf_op jit(solution)/shard_map/add | solution.py:338
  64.0 0.0 collective-permute-done.12.refs_1_
  64.0 0.0 collective-permute-done.13.refs_2_
  64.0 0.0 copy-done
  64.0 1.5 %finish.2.refs_4_ = bf16[768,512]{1,0:T(8,128)(2,1)} custom-call(bf16[768,1536]{1,0:T(8,128)(2,1)S(1)} %unpack_matrix.1.pick_ref, f32[768,512]{1,0:T(8,128)S(1)} %bitcast_add_fusion.base_ref, f32[768,1]{1,0:T(8,128)S(1)} %copy.12.part_ref, f32[1,512]{1,0:T(1,128)S(1)} %bitcast.18, bf16[384,256]{1,0:T(8,128)(2,1)S(1)} %collective-permute-done.11.refs_0_, ...), custom_call_target="tpu_custom_call" | custom-call | tf_op jit(solution)/shard_map/finish/pallas_call | solution.py:249
  65.6 0.0 collective-permute-done.10.refs_2_
  65.6 2.7 %collective-permute-done.8.refs_0_ = bf16[384,256]{1,0:T(8,128)(2,1)S(1)} collective-permute-done((bf16[384,256]{1,0:T(8,128)(2,1)S(1)}, bf16[384,256]{1,0:T(8,128)(2,1)S(1)}, u32[]{:S(2)}, u32[]{:S(2)}) %collective-permute-start.8) | collective-permute-done | bytes 196640 | tf_op jit(solution)/shard_map/ppermute | solution.py:290
  68.3 6.9 %collective-permute-done.9.refs_1_ = bf16[384,256]{1,0:T(8,128)(2,1)S(1)} collective-permute-done((bf16[384,256]{1,0:T(8,128)(2,1)S(1)}, bf16[384,256]{1,0:T(8,128)(2,1)S(1)}, u32[]{:S(2)}, u32[]{:S(2)}) %collective-permute-start.9) | collective-permute-done | bytes 196640 | tf_op jit(solution)/shard_map/ppermute | solution.py:290
  75.2 1.5 %finish.3 = bf16[768,512]{1,0:T(8,128)(2,1)} custom-call(bf16[768,1536]{1,0:T(8,128)(2,1)S(1)} %unpack_matrix.1.pick_ref, f32[768,512]{1,0:T(8,128)S(1)} %bitcast_add_fusion.base_ref, f32[768,1]{1,0:T(8,128)S(1)} %copy.12.part_ref, f32[1,512]{1,0:T(1,128)S(1)} %bitcast.19, ...), custom_call_target="tpu_custom_call", output_to_operand_aliasing={{}: (8, {})} | custom-call | tf_op jit(solution)/shard_map/finish/pallas_call | solution.py:249
Async XLA Ops:
  1.7 8.4 %collective-permute-start = (bf16[384,256]{1,0:T(8,128)(2,1)S(1)}, bf16[384,256]{1,0:T(8,128)(2,1)S(1)}, u32[]{:S(2)}, u32[]{:S(2)}) collective-permute-start(bf16[384,256]{1,0:T(8,128)(2,1)S(1)} %get-tuple-element.33), channel_id=1, source_target_pairs={{0,4},{4,0},{8,12},{12,8},{1,5},{5,1},{9,13},{13,9},{2,6},{6,2},{1... | collective-permute-start | bytes 589832 | tf_op jit(solution)/shard_map/ppermute | solution.py:290
  4.8 22.6 %collective-permute-start.2 = (bf16[384,256]{1,0:T(8,128)(2,1)S(1)}, bf16[384,256]{1,0:T(8,128)(2,1)S(1)}, u32[]{:S(2)}, u32[]{:S(2)}) collective-permute-start(bf16[384,256]{1,0:T(8,128)(2,1)S(1)} %get-tuple-element.40), channel_id=1, source_target_pairs={{0,12},{4,8},{8,4},{12,0},{1,13},{5,9},{9,5},{13,1},{2,14},{6,10},... | collective-permute-start | bytes 589832 | tf_op jit(solution)/shard_map/ppermute | solution.py:290
  7.2 24.2 %collective-permute-start.3 = (bf16[384,256]{1,0:T(8,128)(2,1)S(1)}, bf16[384,256]{1,0:T(8,128)(2,1)S(1)}, u32[]{:S(2)}, u32[]{:S(2)}) collective-permute-start(bf16[384,256]{1,0:T(8,128)(2,1)S(1)} %get-tuple-element.41), channel_id=1, source_target_pairs={{0,8},{4,12},{8,0},{12,4},{1,9},{5,13},{9,1},{13,5},{2,10},{6,14},... | collective-permute-start | bytes 589832 | tf_op jit(solution)/shard_map/ppermute | solution.py:290
  19.9 24.1 %collective-permute-start.5 = (bf16[384,256]{1,0:T(8,128)(2,1)}, bf16[384,256]{1,0:T(8,128)(2,1)}, u32[]{:S(2)}, u32[]{:S(2)}) collective-permute-start(bf16[384,256]{1,0:T(8,128)(2,1)} %get-tuple-element.35), channel_id=1, source_target_pairs={{0,12},{4,8},{8,4},{12,0},{1,13},{5,9},{9,5},{13,1},{2,14},{6,10},... | collective-permute-start | bytes 589832 | tf_op jit(solution)/shard_map/ppermute | solution.py:290
  26.7 24.0 %collective-permute-start.6 = (bf16[384,256]{1,0:T(8,128)(2,1)}, bf16[384,256]{1,0:T(8,128)(2,1)}, u32[]{:S(2)}, u32[]{:S(2)}) collective-permute-start(bf16[384,256]{1,0:T(8,128)(2,1)} %get-tuple-element.36), channel_id=1, source_target_pairs={{0,8},{4,12},{8,0},{12,4},{1,9},{5,13},{9,1},{13,5},{2,10},{6,14},... | collective-permute-start | bytes 589832 | tf_op jit(solution)/shard_map/ppermute | solution.py:290
  26.7 24.5 %collective-permute-start.7 = (bf16[384,256]{1,0:T(8,128)(2,1)}, bf16[384,256]{1,0:T(8,128)(2,1)}, u32[]{:S(2)}, u32[]{:S(2)}) collective-permute-start(bf16[384,256]{1,0:T(8,128)(2,1)} %get-tuple-element.37), channel_id=1, source_target_pairs={{0,4},{4,0},{8,12},{12,8},{1,5},{5,1},{9,13},{13,9},{2,6},{6,2},{1... | collective-permute-start | bytes 589832 | tf_op jit(solution)/shard_map/ppermute | solution.py:290
  27.3 13.7 %collective-permute-start.1 = (bf16[2,768,512]{2,1,0:T(8,128)(2,1)}, bf16[2,768,512]{2,1,0:T(8,128)(2,1)}, u32[]{:S(2)}, u32[]{:S(2)}) collective-permute-start(bf16[2,768,512]{2,1,0:T(8,128)(2,1)} %ladder_part.2), channel_id=1, source_target_pairs={{0,1},{1,0},{2,3},{3,2},{4,5},{5,4},{6,7},{7,6},{8,9},{9,8},{10,11... | collective-permute-start | bytes 4718600 | tf_op jit(solution)/shard_map/ppermute | solution.py:317
  36.8 0.7 copy-start.1
  37.5 21.5 %collective-permute-start.11 = (bf16[384,256]{1,0:T(8,128)(2,1)}, bf16[384,256]{1,0:T(8,128)(2,1)S(1)}, u32[]{:S(2)}, u32[]{:S(2)}) collective-permute-start(bf16[384,256]{1,0:T(8,128)(2,1)} %get-tuple-element.47), channel_id=1, source_target_pairs={{0,12},{4,8},{8,4},{12,0},{1,13},{5,9},{9,5},{13,1},{2,14},{6,10},... | collective-permute-start | bytes 589832 | tf_op jit(solution)/shard_map/ppermute | solution.py:290
  41.0 3.0 %copy-start.2 = (bf16[384,256]{1,0:T(8,128)(2,1)S(1)}, bf16[384,256]{1,0:T(8,128)(2,1)}, u32[]{:S(2)}) copy-start(bf16[384,256]{1,0:T(8,128)(2,1)} %copy-done.1) | copy-start | bytes 589828
  42.4 20.0 %copy-start.3 = (bf16[1,768,512]{2,1,0:T(8,128)(2,1)S(1)}, bf16[1,768,512]{2,1,0:T(8,128)(2,1)}, u32[]{:S(2)}) copy-start(bf16[1,768,512]{2,1,0:T(8,128)(2,1)} %param.9) | copy-start | bytes 2359300
  42.4 20.0 %collective-permute-start.4 = (bf16[768,512]{1,0:T(8,128)(2,1)S(1)}, bf16[768,512]{1,0:T(8,128)(2,1)S(1)}, u32[]{:S(2)}, u32[]{:S(2)}) collective-permute-start(bf16[768,512]{1,0:T(8,128)(2,1)S(1)} %fusion), channel_id=1, source_target_pairs={{0,2},{2,0},{1,3},{3,1},{4,6},{6,4},{5,7},{7,5},{8,10},{10,8},{9,1... | collective-permute-start | bytes 2359304 | tf_op jit(solution)/shard_map/ppermute | solution.py:338
  44.0 20.0 %collective-permute-start.12 = (bf16[384,256]{1,0:T(8,128)(2,1)S(1)}, bf16[384,256]{1,0:T(8,128)(2,1)S(1)}, u32[]{:S(2)}, u32[]{:S(2)}) collective-permute-start(bf16[384,256]{1,0:T(8,128)(2,1)S(1)} %copy-done.2), channel_id=1, source_target_pairs={{0,8},{4,12},{8,0},{12,4},{1,9},{5,13},{9,1},{13,5},{2,10},{6,14},... | collective-permute-start | bytes 589832 | tf_op jit(solution)/shard_map/ppermute | solution.py:290
  50.7 13.3 %collective-permute-start.13 = (bf16[384,256]{1,0:T(8,128)(2,1)S(1)}, bf16[384,256]{1,0:T(8,128)(2,1)S(1)}, u32[]{:S(2)}, u32[]{:S(2)}) collective-permute-start(bf16[384,256]{1,0:T(8,128)(2,1)S(1)} %get-tuple-element.49), channel_id=1, source_target_pairs={{0,4},{4,0},{8,12},{12,8},{1,5},{5,1},{9,13},{13,9},{2,6},{6,2},{1... | collective-permute-start | bytes 589832 | tf_op jit(solution)/shard_map/ppermute | solution.py:290
  57.4 8.2 %collective-permute-start.10 = (bf16[384,256]{1,0:T(8,128)(2,1)S(1)}, bf16[384,256]{1,0:T(8,128)(2,1)S(1)}, u32[]{:S(2)}, u32[]{:S(2)}) collective-permute-start(bf16[384,256]{1,0:T(8,128)(2,1)S(1)} %get-tuple-element.57), channel_id=1, source_target_pairs={{0,4},{4,0},{8,12},{12,8},{1,5},{5,1},{9,13},{13,9},{2,6},{6,2},{1... | collective-permute-start | bytes 589832 | tf_op jit(solution)/shard_map/ppermute | solution.py:290
  59.0 9.3 %collective-permute-start.8 = (bf16[384,256]{1,0:T(8,128)(2,1)S(1)}, bf16[384,256]{1,0:T(8,128)(2,1)S(1)}, u32[]{:S(2)}, u32[]{:S(2)}) collective-permute-start(bf16[384,256]{1,0:T(8,128)(2,1)S(1)} %get-tuple-element.55), channel_id=1, source_target_pairs={{0,12},{4,8},{8,4},{12,0},{1,13},{5,9},{9,5},{13,1},{2,14},{6,10},... | collective-permute-start | bytes 589832 | tf_op jit(solution)/shard_map/ppermute | solution.py:290
  62.4 1.6 %copy-start = (f32[512]{0:T(512)S(1)}, f32[512]{0:T(512)}, u32[]{:S(2)}) copy-start(f32[512]{0:T(512)} %param.15) | copy-start | bytes 6148
  62.4 12.8 %collective-permute-start.9 = (bf16[384,256]{1,0:T(8,128)(2,1)S(1)}, bf16[384,256]{1,0:T(8,128)(2,1)S(1)}, u32[]{:S(2)}, u32[]{:S(2)}) collective-permute-start(bf16[384,256]{1,0:T(8,128)(2,1)S(1)} %get-tuple-element.56), channel_id=1, source_target_pairs={{0,8},{4,12},{8,0},{12,4},{1,9},{5,13},{9,1},{13,5},{2,10},{6,14},... | collective-permute-start | bytes 589832 | tf_op jit(solution)/shard_map/ppermute | solution.py:290

commit v9 on v8

--- a/solution.py
+++ b/solution.py
@@ -7,7 +7,7 @@
 from jax.experimental.pallas import tpu as pltpu
 from jax.sharding import PartitionSpec as P
 
-VMEM_LIMIT = 16 * 1024 * 1024
+VMEM_LIMIT = 28 * 1024 * 1024
 HALVES = 2
 F32 = jnp.float32
 BF16 = jnp.bfloat16
@@ -127,94 +127,106 @@
     )(offsets, target_column)
 
 
-def ladder_kernel(step, sub_count, weight_hbm, amps_hbm, part_ref, weight_ref, amps_ref, sems):
-    rows, lad_count = amps_ref.shape[0], part_ref.shape[0]
-    share = lax.rem(lax.axis_index("sub") + step, sub_count)
-    copies = [pltpu.make_async_copy(amps_hbm, amps_ref, sems.at[0])]
-    for i in range(lad_count):
-        start = pl.multiple_of((i * sub_count + share) * rows, rows)
-        copies.append(pltpu.make_async_copy(weight_hbm.at[pl.ds(start, rows), :], weight_ref.at[i], sems.at[1 + i]))
+def prepare_kernel(sub_count, weight_hbm, amps_hbm, cycle_hbm, mixing_hbm, *refs):
+    part_refs, out_ref = refs[:sub_count], refs[sub_count]
+    weight_ref, amps_ref, cycle_ref, half_ref, mixing_ref, pair_ref, sems = refs[sub_count + 1 :]
+    rows, lad_count = amps_ref.shape[0], part_refs[0].shape[0]
+    chunks, chunk, capacity = cycle_ref.shape
+    group = mixing_ref.shape[1]
+    pairs, wide = pair_ref.shape[0], pair_ref.shape[1]
+    sub = lax.axis_index("sub")
+    moves, ladder = [(amps_hbm, amps_ref)], []
+    for n in range(sub_count):
+        share = lax.rem(sub + sub_count - 1 - n, sub_count)
+        for i in range(lad_count):
+            start = pl.multiple_of((i * sub_count + share) * rows, rows)
+            moves.append((weight_hbm.at[pl.ds(start, rows), :], weight_ref.at[len(ladder)]))
+            ladder.append((n, i))
+    moves.append((mixing_hbm, mixing_ref))
+    moves += [(cycle_hbm.at[pl.ds(i * chunk, chunk), :], cycle_ref.at[i]) for i in range(chunks)]
+    copies = [pltpu.make_async_copy(source, held, sems.at[n]) for n, (source, held) in enumerate(moves)]
     for copy in copies:
         copy.start()
+    pair_ref[...] = jnp.zeros(pair_ref.shape, BF16)
     copies[0].wait()
-    for i in range(lad_count):
-        copies[1 + i].wait()
-        part_ref[i] = jnp.dot(weight_ref[i], amps_ref[...], preferred_element_type=F32).astype(BF16)
-
-
-def ladder_part(step, weight, amps, lad_count, sub_count):
+    for m, (n, i) in enumerate(ladder):
+        copies[1 + m].wait()
+        part_refs[n][i] = jnp.dot(weight_ref[m], amps_ref[...], preferred_element_type=F32).astype(BF16)
+    copies[1 + len(ladder)].wait()
+    for q in range(capacity // group):
+        at = pl.ds(q * group % wide, group)
+        pair_ref[q * group // wide, at, at] = mixing_ref[q]
+    for i in range(chunks):
+        copies[2 + len(ladder) + i].wait()
+        for a in range(chunk // group):
+            at = pl.ds(a * group, group)
+            half_ref[pl.ds(i * chunk + a * group, group), :] = lax.dot_general(
+                mixing_ref[i * chunk // group + a],
+                cycle_ref[i, at, :],
+                (((0,), (0,)), ((), ())),
+                preferred_element_type=F32,
+            ).astype(BF16)
+    for j in range(pairs):
+        at = pl.ds(j * wide, wide)
+        out_ref[:, at] = jnp.dot(half_ref[:, at], pair_ref[j], preferred_element_type=F32).astype(BF16)
+
+
+def prepare(weight, amps, cycle_weight, mixing, lad_count, sub_count):
     rows, holes = amps.shape
-    return pl.pallas_call(
-        functools.partial(ladder_kernel, step, sub_count),
-        out_shape=pltpu.VMEM((lad_count, rows, holes), BF16),
-        in_specs=[whole(pl.ANY)] * 2,
-        out_specs=whole(),
+    capacity = cycle_weight.shape[0]
+    groups, group = mixing.shape[0], mixing.shape[1]
+    wide = group * (2 if groups % 2 == 0 else 1)
+    chunks = groups // 3 if groups % 3 == 0 else 1
+    outs = pl.pallas_call(
+        functools.partial(prepare_kernel, sub_count),
+        out_shape=[jax.ShapeDtypeStruct((lad_count, rows, holes), BF16)] * sub_count
+        + [jax.ShapeDtypeStruct((capacity, capacity), BF16)],
+        in_specs=[whole(pl.ANY)] * 4,
+        out_specs=[whole()] * (sub_count + 1),
         scratch_shapes=[
-            pltpu.VMEM((lad_count, rows, rows), BF16),
+            pltpu.VMEM((lad_count * sub_count, rows, rows), BF16),
             pltpu.VMEM((rows, holes), BF16),
-            pltpu.SemaphoreType.DMA((1 + lad_count,)),
+            pltpu.VMEM((chunks, capacity // chunks, capacity), BF16),
+            pltpu.VMEM((capacity, capacity), BF16),
+            pltpu.VMEM(mixing.shape, BF16),
+            pltpu.VMEM((capacity // wide, wide, wide), BF16),
+            pltpu.SemaphoreType.DMA((2 + lad_count * sub_count + chunks,)),
         ],
         compiler_params=params(),
         cost_estimate=DEAR,
-        name="ladder_part",
-    )(*in_hbm(weight, amps))
-
-
-def cycle_kernel(half, plan, weight_hbm, mixing_hbm, *refs):
+        name="prepare",
+    )(*in_hbm(weight, amps, cycle_weight, mixing))
+    return outs[:sub_count], outs[sub_count]
+
+
+def cycle_kernel(half, plan, operator_ref, *refs):
     paired, chan_count, _, _ = plan
-    count = (len(refs) - 5) // 2
-    in_refs, out_refs = refs[:count], refs[count : 2 * count]
-    weight_ref, mixing_ref, mixed_ref, back_ref, sems = refs[2 * count :]
+    count = len(refs) // 2
+    in_refs, out_refs, block_ref = refs[:count], refs[count : 2 * count], refs[2 * count]
     block_rows, width = out_refs[0].shape
-    group = mixing_ref.shape[1]
     offsets = block_offsets(paired, chan_count, block_rows)
     starts = [pl.multiple_of(offsets[count - 1 - i], block_rows) for i in range(count)]
-    mixing_copy = pltpu.make_async_copy(mixing_hbm, mixing_ref, sems.at[0])
-    copies = [
-        pltpu.make_async_copy(weight_hbm.at[pl.ds(start, block_rows), :], weight_ref.at[i], sems.at[1 + i])
-        for i, start in enumerate(starts)
-    ]
-    for copy in [mixing_copy] + copies:
-        copy.start()
-    mixing_copy.wait()
     for in_ref, start in zip(in_refs, starts):
-        for a in range(block_rows // group):
-            at = pl.ds(a * group, group)
-            part = in_ref[at, :] if in_ref.shape[1] == width else in_ref[at, pl.ds(half * width, width)]
-            mix = mixing_ref[lax.div(start, group) + a]
-            mixed_ref[pl.ds(pl.multiple_of(start + a * group, group), group), :] = jnp.dot(
-                mix, part, preferred_element_type=F32
-            ).astype(BF16)
-    for i, (out_ref, start) in enumerate(zip(out_refs, starts)):
-        copies[i].wait()
-        back_ref[...] = jnp.dot(weight_ref[i], mixed_ref[...], preferred_element_type=F32).astype(BF16)
-        for a in range(block_rows // group):
-            at = pl.ds(a * group, group)
-            mix = mixing_ref[lax.div(start, group) + a]
-            out_ref[at, :] = lax.dot_general(
-                mix, back_ref[at, :], (((0,), (0,)), ((), ())), preferred_element_type=F32
-            ).astype(BF16)
-
-
-def apply_cycle(half, plan, weight, mixing, arrays, width):
-    count, block_rows = len(arrays), arrays[0].shape[0]
-    capacity = weight.shape[0]
+        part = in_ref[...] if in_ref.shape[1] == width else in_ref[:, pl.ds(half * width, width)]
+        block_ref[pl.ds(start, block_rows), :] = part
+    for out_ref, start in zip(out_refs, starts):
+        out_ref[...] = jnp.dot(
+            operator_ref[pl.ds(start, block_rows), :], block_ref[...], preferred_element_type=F32
+        ).astype(BF16)
+
+
+def apply_cycle(half, plan, operator, arrays, width):
+    block_rows = arrays[0].shape[0]
     return pl.pallas_call(
         functools.partial(cycle_kernel, half, plan),
-        out_shape=[pltpu.VMEM((block_rows, width), BF16)] * count,
-        in_specs=[whole(pl.ANY)] * 2 + [whole()] * count,
-        out_specs=[whole()] * count,
-        scratch_shapes=[
-            pltpu.VMEM((count, block_rows, capacity), BF16),
-            pltpu.VMEM(mixing.shape, BF16),
-            pltpu.VMEM((capacity, width), BF16),
-            pltpu.VMEM((block_rows, width), BF16),
-            pltpu.SemaphoreType.DMA((1 + count,)),
-        ],
+        out_shape=[jax.ShapeDtypeStruct((block_rows, width), BF16)] * len(arrays),
+        in_specs=[whole()] * (1 + len(arrays)),
+        out_specs=[whole()] * len(arrays),
+        scratch_shapes=[pltpu.VMEM((operator.shape[0], width), BF16)],
         compiler_params=params(),
         cost_estimate=DEAR,
         name="apply_cycle",
-    )(*in_hbm(weight, mixing), *arrays)
+    )(operator, *arrays)
 
 
 def finish_kernel(half, count, tiles, pick_ref, base_ref, part_ref, hole_ref, *refs):
@@ -310,12 +322,11 @@
     amps, blocks = lax.optimization_barrier((amps, blocks))
     pick = unpack_matrix(offsets, target.reshape(rows, 1), capacity)
 
-    kept = []
-    for step in reversed(range(sub_count)):
-        part = ladder_part(step, ladder_weight[0], amps, lad_count, sub_count)
-        if step:
-            part = lax.ppermute(part, "sub", [(i, (i + step) % sub_count) for i in range(sub_count)])
-        kept.append(part)
+    parts, operator = prepare(ladder_weight[0], amps, weight, mixing, lad_count, sub_count)
+    kept = [parts[-1]]
+    for step in range(1, sub_count):
+        pairs = [(i, (i + step) % sub_count) for i in range(sub_count)]
+        kept.append(lax.ppermute(parts[sub_count - 1 - step], "sub", pairs))
 
     def chip_sum(position):
         picked = [lax.dynamic_index_in_dim(p, position, 0, keepdims=False) for p in kept]
@@ -328,7 +339,7 @@
         blocks = [arrived[(k, half if k or not paired else 0)] for k in far_first]
         if returned:
             blocks, made = lax.optimization_barrier((blocks, made))
-        made = apply_cycle(half, plan, weight, mixing, blocks, width)
+        made = apply_cycle(half, plan, operator, blocks, width)
         if not half:
             behind, terms = lax.optimization_barrier((made[1:], terms))
             made = [made[0], *behind]

time: 77 us -> 77 us (level)
  Pallas kernels: 27.2 us -> 20.8 us
  waiting for transfers between devices: 22.2 us -> 26.5 us
  starting transfers between devices: 22.4 us -> 24.2 us
    pallas_call x4 -> x3, Pallas kernels: 18.9 us -> 12.4 us  [the longest x1 7.96 us: prepare(): pl.pallas_call(functools.partial(prepare_kernel, sub_count), out_shape=[j...]
    ppermute x12, waiting for transfers between devices: 22.2 us -> 26 us  [exchange(): lax.ppermute(block, 'chan', [(i, i ^ k) for i in range(chan_count)])]
    ppermute x12, starting transfers between devices: 20.8 us -> 22.6 us  [exchange(): lax.ppermute(block, 'chan', [(i, i ^ k) for i in range(chan_count)])]
  transfers between devices with their start and end apart: 14 -> 14, of which waited for: 5 -> 6; matrix products, arithmetic and copies ran while one was open for 5% -> 6% of each run, Pallas kernels for 31% -> 23%
where the time goes in v9:
time: 77 us; the launch traced here: 76.7 us
  waiting for transfers between devices  26.5 us (34%)
  starting transfers between devices  24.2 us (31%)
  Pallas kernels  20.8 us (27%)
  other arithmetic  3.29 us (4%)
  local copies, waits for them, and re-layouts  1.75 us (2%)
    ppermute x12, waiting for transfers between devices, exchange(): lax.ppermute(block, 'chan', [(i, i ^ k) for i in range(chan_count)])  26 us
    ppermute x12, starting transfers between devices, exchange(): lax.ppermute(block, 'chan', [(i, i ^ k) for i in range(chan_count)])  22.6 us
    pallas_call x1, Pallas kernels, prepare(): pl.pallas_call(functools.partial(prepare_kernel, sub_count), out_shape=[j...  7.96 us
    pallas_call x2, Pallas kernels, apply_cycle(): pl.pallas_call(functools.partial(cycle_kernel, half, plan), out_shape=[ja...  4.49 us
    pallas_call x2, Pallas kernels, pack(): pl.pallas_call(functools.partial(pack_kernel, plan, given), out_shape=ext...  4.21 us
    pallas_call x2, Pallas kernels, finish(): pl.pallas_call(functools.partial(finish_kernel, half, len(arrays), tiles)...  3.02 us
    convert_element_type x1, other arithmetic, body(): chip_sum(lax.rem(lad + step, lad_count)).astype(BF16)  1.69 us
    ppermute x1, starting transfers between devices, body(): base = base + lax.ppermute(term, 'lad', pairs).astype(F32)  1.56 us
  transfers between devices with their start and end apart: 14, of which 6 were waited for; matrix products, arithmetic and copies ran while one was open for 6% of the time, Pallas kernels for 23%

profile of v9, /device:TPU:0, one launch (start us, length us, event | category | flops | bytes accessed | tf_op | source)
XLA Modules:
  0.0 76.7 jit_solution(15206518548716403997)
XLA Ops:
  0.0 1.7 %pack_first.1 = (s32[1,768]{1,0:T(1,128)S(1)}, bf16[384,256]{1,0:T(8,128)(2,1)S(1)}, bf16[384,256]{1,0:T(8,128)(2,1)S(1)}, bf16[384,256]{1,0:T(8,128)(2,1)S(1)}) custom-call(s32[1,768]{1,0:T(1,128)} %bitcast.23, bf16[768,512]{1,0:T(8,128)(2,1)} %bitcast.20), custom_call_target="tpu_custom_call" | custom-call | tf_op jit(solution)/shard_map/pack_first/pallas_call | solution.py:93
  1.7 3.1 %collective-permute-start = (bf16[384,256]{1,0:T(8,128)(2,1)S(1)}, bf16[384,256]{1,0:T(8,128)(2,1)S(1)}, u32[]{:S(2)}, u32[]{:S(2)}) collective-permute-start(bf16[384,256]{1,0:T(8,128)(2,1)S(1)} %get-tuple-element.36), channel_id=1, source_target_pairs={{0,4},{4,0},{8,12},{12,8},{1,5},{5,1},{9,13},{13,9},{2,6},{6,2},{1... | collective-permute-start | bytes 589832 | tf_op jit(solution)/shard_map/ppermute | solution.py:302
  4.8 2.5 %collective-permute-start.2 = (bf16[384,256]{1,0:T(8,128)(2,1)S(1)}, bf16[384,256]{1,0:T(8,128)(2,1)S(1)}, u32[]{:S(2)}, u32[]{:S(2)}) collective-permute-start(bf16[384,256]{1,0:T(8,128)(2,1)S(1)} %get-tuple-element.46), channel_id=1, source_target_pairs={{0,12},{4,8},{8,4},{12,0},{1,13},{5,9},{9,5},{13,1},{2,14},{6,10},... | collective-permute-start | bytes 589832 | tf_op jit(solution)/shard_map/ppermute | solution.py:302
  7.2 0.1 collective-permute-start.3
  7.4 0.9 %copy.12.part_ref = f32[768,1]{1,0:T(8,128)S(1)} copy(f32[768,1]{0,1:T(1,128)} %bitcast.24) | data formatting | bytes 6144 | tf_op jit(solution)/shard_map/reshape;squeeze | solution.py:321
  8.2 0.1 add_multiply_fusion.off_ref
  8.3 1.8 %collective-permute-done.refs_2_ = bf16[384,256]{1,0:T(8,128)(2,1)S(1)} collective-permute-done((bf16[384,256]{1,0:T(8,128)(2,1)S(1)}, bf16[384,256]{1,0:T(8,128)(2,1)S(1)}, u32[]{:S(2)}, u32[]{:S(2)}) %collective-permute-start) | collective-permute-done | bytes 196640 | tf_op jit(solution)/shard_map/ppermute | solution.py:302
  10.1 2.5 %pack_rest.1 = (bf16[384,256]{1,0:T(8,128)(2,1)}, bf16[384,256]{1,0:T(8,128)(2,1)}, bf16[384,256]{1,0:T(8,128)(2,1)}, bf16[384,512]{1,0:T(8,128)(2,1)S(1)}) custom-call(s32[1,768]{1,0:T(1,128)S(1)} %get-tuple-element.37.route_in, bf16[768,512]{1,0:T(8,128)(2,1)} %bitcast.21), custom_call_target="tpu_custom_call" | custom-call | tf_op jit(solution)/shard_map/pack_rest/pallas_call | solution.py:93
  12.6 6.8 %collective-permute-start.5 = (bf16[384,256]{1,0:T(8,128)(2,1)}, bf16[384,256]{1,0:T(8,128)(2,1)}, u32[]{:S(2)}, u32[]{:S(2)}) collective-permute-start(bf16[384,256]{1,0:T(8,128)(2,1)} %get-tuple-element.38), channel_id=1, source_target_pairs={{0,12},{4,8},{8,4},{12,0},{1,13},{5,9},{9,5},{13,1},{2,14},{6,10},... | collective-permute-start | bytes 589832 | tf_op jit(solution)/shard_map/ppermute | solution.py:302
  19.4 0.0 collective-permute-start.6
  19.4 0.6 collective-permute-start.7
  20.0 8.0 %prepare.1 = (bf16[2,768,512]{2,1,0:T(8,128)(2,1)}, bf16[2,768,512]{2,1,0:T(8,128)(2,1)S(1)}, bf16[1536,1536]{1,0:T(8,128)(2,1)S(1)}) custom-call(bf16[3072,768]{1,0:T(8,128)(2,1)} %bitcast.25, bf16[768,512]{1,0:T(8,128)(2,1)} %bitcast.22, bf16[1536,1536]{1,0:T(8,128)(2,1)} %bitcast.26, bf16[12,128,128]{2,1,0:T(8,128)(2,1)} %bitcast.27), custom_call_target="tpu_custom_call" | custom-call | flops 30000001024 | bytes 1000000 | tf_op jit(solution)/shard_map/prepare/pallas_call | solution.py:180
  28.0 0.0 copy-start.3
  28.0 0.0 collective-permute-done.2.refs_0_
  28.0 0.1 collective-permute-start.1
  28.1 6.1 %collective-permute-done.3.refs_1_ = bf16[384,256]{1,0:T(8,128)(2,1)S(1)} collective-permute-done((bf16[384,256]{1,0:T(8,128)(2,1)S(1)}, bf16[384,256]{1,0:T(8,128)(2,1)S(1)}, u32[]{:S(2)}, u32[]{:S(2)}) %collective-permute-start.3) | collective-permute-done | bytes 196640 | tf_op jit(solution)/shard_map/ppermute | solution.py:302
  34.2 1.9 %apply_cycle.2 = (bf16[384,256]{1,0:T(8,128)(2,1)}, bf16[384,256]{1,0:T(8,128)(2,1)S(1)}, bf16[384,256]{1,0:T(8,128)(2,1)S(1)}, bf16[384,256]{1,0:T(8,128)(2,1)S(1)}) custom-call(bf16[1536,1536]{1,0:T(8,128)(2,1)S(1)} %get-tuple-element.45.operator_ref, bf16[384,256]{1,0:T(8,128)(2,1)S(1)} %collective-permute-done.2.refs_0_, ...), custom_call_target="tpu_custom_call" | custom-call | flops 30000001024 | bytes 1000000 | tf_op jit(solution)/shard_map/apply_cycle/pallas_call | solution.py:220
  36.1 0.0 copy-done.3
  36.1 0.0 copy-start.1
  36.1 0.7 copy-done.1
  36.8 3.0 %collective-permute-start.11 = (bf16[384,256]{1,0:T(8,128)(2,1)}, bf16[384,256]{1,0:T(8,128)(2,1)S(1)}, u32[]{:S(2)}, u32[]{:S(2)}) collective-permute-start(bf16[384,256]{1,0:T(8,128)(2,1)} %get-tuple-element.53), channel_id=1, source_target_pairs={{0,12},{4,8},{8,4},{12,0},{1,13},{5,9},{9,5},{13,1},{2,14},{6,10},... | collective-permute-start | bytes 589832 | tf_op jit(solution)/shard_map/ppermute | solution.py:302
  39.8 0.2 copy.10.target_ref
  40.0 0.0 copy-start.4
  40.0 1.1 %unpack_matrix.1.pick_ref = bf16[768,1536]{1,0:T(8,128)(2,1)S(1)} custom-call(s32[4]{0:T(128)S(1)} %add_multiply_fusion.off_ref, s32[768,1]{1,0:T(8,128)S(1)} %copy.10.target_ref), custom_call_target="tpu_custom_call" | custom-call | tf_op jit(solution)/shard_map/unpack_matrix/pallas_call | solution.py:119
  41.1 0.0 copy-start.2
  41.1 0.0 collective-permute-done.1
  41.1 1.7 %fusion = bf16[768,512]{1,0:T(8,128)(2,1)S(1)} fusion(bf16[2,768,512]{2,1,0:T(8,128)(2,1)} %collective-permute-done.1, s32[]{:T(128)S(6)} %select_n.10, bf16[2,768,512]{2,1,0:T(8,128)(2,1)S(1)} %get-tuple-element.43), kind=kLoop, calls=%fused_computation.2 | loop fusion | flops 1572864 | bytes 2359300 | tf_op jit(solution)/shard_map/convert_element_type | solution.py:336
  42.8 0.0 copy-start.5
  42.8 1.6 %collective-permute-start.4 = (bf16[768,512]{1,0:T(8,128)(2,1)S(1)}, bf16[768,512]{1,0:T(8,128)(2,1)S(1)}, u32[]{:S(2)}, u32[]{:S(2)}) collective-permute-start(bf16[768,512]{1,0:T(8,128)(2,1)S(1)} %fusion), channel_id=1, source_target_pairs={{0,2},{2,0},{1,3},{3,1},{4,6},{6,4},{5,7},{7,5},{8,10},{10,8},{9,1... | collective-permute-start | bytes 2359304 | tf_op jit(solution)/shard_map/ppermute | solution.py:349
  44.4 0.0 collective-permute-done.5.refs_0_
  44.4 0.0 copy-done.2
  44.4 0.0 collective-permute-start.12
  44.4 6.7 %collective-permute-done.6.refs_1_ = bf16[384,256]{1,0:T(8,128)(2,1)} collective-permute-done((bf16[384,256]{1,0:T(8,128)(2,1)}, bf16[384,256]{1,0:T(8,128)(2,1)}, u32[]{:S(2)}, u32[]{:S(2)}) %collective-permute-start.6) | collective-permute-done | bytes 196640 | tf_op jit(solution)/shard_map/ppermute | solution.py:302
  51.1 0.0 collective-permute-start.13
  51.1 0.0 collective-permute-done.7.refs_2_
  51.1 0.0 copy-done.4
  51.1 2.6 %apply_cycle.3 = (bf16[384,256]{1,0:T(8,128)(2,1)S(1)}, bf16[384,256]{1,0:T(8,128)(2,1)S(1)}, bf16[384,256]{1,0:T(8,128)(2,1)S(1)}, bf16[384,256]{1,0:T(8,128)(2,1)S(1)}) custom-call(bf16[1536,1536]{1,0:T(8,128)(2,1)S(1)} %copy-done.4, bf16[384,256]{1,0:T(8,128)(2,1)} %collective-permute-done.5.refs_0_, bf16[384,256]{1,0:T(8,128)(2,1)} %collective-permute-done.6.refs_1_, ...), custom_call_target="tpu_custom_call" | custom-call | flops 30000001024 | bytes 1000000 | tf_op jit(solution)/shard_map/apply_cycle/pallas_call | solution.py:220
  53.7 2.1 %collective-permute-start.10 = (bf16[384,256]{1,0:T(8,128)(2,1)S(1)}, bf16[384,256]{1,0:T(8,128)(2,1)S(1)}, u32[]{:S(2)}, u32[]{:S(2)}) collective-permute-start(bf16[384,256]{1,0:T(8,128)(2,1)S(1)} %get-tuple-element.63), channel_id=1, source_target_pairs={{0,4},{4,0},{8,12},{12,8},{1,5},{5,1},{9,13},{13,9},{2,6},{6,2},{1... | collective-permute-start | bytes 589832 | tf_op jit(solution)/shard_map/ppermute | solution.py:302
  55.8 0.0 collective-permute-done.11.refs_0_
  55.8 3.0 %collective-permute-start.8 = (bf16[384,256]{1,0:T(8,128)(2,1)S(1)}, bf16[384,256]{1,0:T(8,128)(2,1)S(1)}, u32[]{:S(2)}, u32[]{:S(2)}) collective-permute-start(bf16[384,256]{1,0:T(8,128)(2,1)S(1)} %get-tuple-element.61), channel_id=1, source_target_pairs={{0,12},{4,8},{8,4},{12,0},{1,13},{5,9},{9,5},{13,1},{2,14},{6,10},... | collective-permute-start | bytes 589832 | tf_op jit(solution)/shard_map/ppermute | solution.py:302
  58.7 0.5 collective-permute-done.4
  59.2 0.0 copy-start
  59.2 1.5 %collective-permute-start.9 = (bf16[384,256]{1,0:T(8,128)(2,1)S(1)}, bf16[384,256]{1,0:T(8,128)(2,1)S(1)}, u32[]{:S(2)}, u32[]{:S(2)}) collective-permute-start(bf16[384,256]{1,0:T(8,128)(2,1)S(1)} %get-tuple-element.62), channel_id=1, source_target_pairs={{0,8},{4,12},{8,0},{12,4},{1,9},{5,13},{9,1},{13,5},{2,10},{6,14},... | collective-permute-start | bytes 589832 | tf_op jit(solution)/shard_map/ppermute | solution.py:302
  60.7 0.0 copy-done.5
  60.7 1.5 %bitcast_add_fusion.base_ref = f32[768,512]{1,0:T(8,128)S(1)} fusion(bf16[768,512]{1,0:T(8,128)(2,1)S(1)} %collective-permute-done.4, bf16[1,768,512]{2,1,0:T(8,128)(2,1)S(1)} %copy-done.5, bf16[2,768,512]{2,1,0:T(8,128)(2,1)} %collective-permute-done.1, s32[]{:T(128)S(6)} %select_n.9, bf16[2,768,512]{2,1,0:T(8,128)(2,1)S(1)} %get-tuple-element.43), kind=kLoop, calls=%fused_computation | loop fusion | flops 2752512 | bytes 4718596 | tf_op jit(solution)/shard_map/add | solution.py:349
  62.2 5.7 %collective-permute-done.12.refs_1_ = bf16[384,256]{1,0:T(8,128)(2,1)S(1)} collective-permute-done((bf16[384,256]{1,0:T(8,128)(2,1)S(1)}, bf16[384,256]{1,0:T(8,128)(2,1)S(1)}, u32[]{:S(2)}, u32[]{:S(2)}) %collective-permute-start.12) | collective-permute-done | bytes 196640 | tf_op jit(solution)/shard_map/ppermute | solution.py:302
  67.9 0.0 collective-permute-done.13.refs_2_
  67.9 0.0 copy-done
  67.9 1.5 %finish.2.refs_4_ = bf16[768,512]{1,0:T(8,128)(2,1)} custom-call(bf16[768,1536]{1,0:T(8,128)(2,1)S(1)} %unpack_matrix.1.pick_ref, f32[768,512]{1,0:T(8,128)S(1)} %bitcast_add_fusion.base_ref, f32[768,1]{1,0:T(8,128)S(1)} %copy.12.part_ref, f32[1,512]{1,0:T(1,128)S(1)} %bitcast.18, bf16[384,256]{1,0:T(8,128)(2,1)S(1)} %collective-permute-done.11.refs_0_, ...), custom_call_target="tpu_custom_call" | custom-call | tf_op jit(solution)/shard_map/finish/pallas_call | solution.py:261
  69.4 0.0 collective-permute-done.10.refs_2_
  69.4 0.0 collective-permute-done.8.refs_0_
  69.4 5.7 %collective-permute-done.9.refs_1_ = bf16[384,256]{1,0:T(8,128)(2,1)S(1)} collective-permute-done((bf16[384,256]{1,0:T(8,128)(2,1)S(1)}, bf16[384,256]{1,0:T(8,128)(2,1)S(1)}, u32[]{:S(2)}, u32[]{:S(2)}) %collective-permute-start.9) | collective-permute-done | bytes 196640 | tf_op jit(solution)/shard_map/ppermute | solution.py:302
  75.2 1.5 %finish.3 = bf16[768,512]{1,0:T(8,128)(2,1)} custom-call(bf16[768,1536]{1,0:T(8,128)(2,1)S(1)} %unpack_matrix.1.pick_ref, f32[768,512]{1,0:T(8,128)S(1)} %bitcast_add_fusion.base_ref, f32[768,1]{1,0:T(8,128)S(1)} %copy.12.part_ref, f32[1,512]{1,0:T(1,128)S(1)} %bitcast.19, ...), custom_call_target="tpu_custom_call", output_to_operand_aliasing={{}: (8, {})} | custom-call | tf_op jit(solution)/shard_map/finish/pallas_call | solution.py:261
Async XLA Ops:
  1.7 8.4 %collective-permute-start = (bf16[384,256]{1,0:T(8,128)(2,1)S(1)}, bf16[384,256]{1,0:T(8,128)(2,1)S(1)}, u32[]{:S(2)}, u32[]{:S(2)}) collective-permute-start(bf16[384,256]{1,0:T(8,128)(2,1)S(1)} %get-tuple-element.36), channel_id=1, source_target_pairs={{0,4},{4,0},{8,12},{12,8},{1,5},{5,1},{9,13},{13,9},{2,6},{6,2},{1... | collective-permute-start | bytes 589832 | tf_op jit(solution)/shard_map/ppermute | solution.py:302
  4.8 23.3 %collective-permute-start.2 = (bf16[384,256]{1,0:T(8,128)(2,1)S(1)}, bf16[384,256]{1,0:T(8,128)(2,1)S(1)}, u32[]{:S(2)}, u32[]{:S(2)}) collective-permute-start(bf16[384,256]{1,0:T(8,128)(2,1)S(1)} %get-tuple-element.46), channel_id=1, source_target_pairs={{0,12},{4,8},{8,4},{12,0},{1,13},{5,9},{9,5},{13,1},{2,14},{6,10},... | collective-permute-start | bytes 589832 | tf_op jit(solution)/shard_map/ppermute | solution.py:302
  7.2 26.9 %collective-permute-start.3 = (bf16[384,256]{1,0:T(8,128)(2,1)S(1)}, bf16[384,256]{1,0:T(8,128)(2,1)S(1)}, u32[]{:S(2)}, u32[]{:S(2)}) collective-permute-start(bf16[384,256]{1,0:T(8,128)(2,1)S(1)} %get-tuple-element.47), channel_id=1, source_target_pairs={{0,8},{4,12},{8,0},{12,4},{1,9},{5,13},{9,1},{13,5},{2,10},{6,14},... | collective-permute-start | bytes 589832 | tf_op jit(solution)/shard_map/ppermute | solution.py:302
  12.6 31.7 %collective-permute-start.5 = (bf16[384,256]{1,0:T(8,128)(2,1)}, bf16[384,256]{1,0:T(8,128)(2,1)}, u32[]{:S(2)}, u32[]{:S(2)}) collective-permute-start(bf16[384,256]{1,0:T(8,128)(2,1)} %get-tuple-element.38), channel_id=1, source_target_pairs={{0,12},{4,8},{8,4},{12,0},{1,13},{5,9},{9,5},{13,1},{2,14},{6,10},... | collective-permute-start | bytes 589832 | tf_op jit(solution)/shard_map/ppermute | solution.py:302
  19.4 31.7 %collective-permute-start.6 = (bf16[384,256]{1,0:T(8,128)(2,1)}, bf16[384,256]{1,0:T(8,128)(2,1)}, u32[]{:S(2)}, u32[]{:S(2)}) collective-permute-start(bf16[384,256]{1,0:T(8,128)(2,1)} %get-tuple-element.39), channel_id=1, source_target_pairs={{0,8},{4,12},{8,0},{12,4},{1,9},{5,13},{9,1},{13,5},{2,10},{6,14},... | collective-permute-start | bytes 589832 | tf_op jit(solution)/shard_map/ppermute | solution.py:302
  19.4 31.7 %collective-permute-start.7 = (bf16[384,256]{1,0:T(8,128)(2,1)}, bf16[384,256]{1,0:T(8,128)(2,1)}, u32[]{:S(2)}, u32[]{:S(2)}) collective-permute-start(bf16[384,256]{1,0:T(8,128)(2,1)} %get-tuple-element.40), channel_id=1, source_target_pairs={{0,4},{4,0},{8,12},{12,8},{1,5},{5,1},{9,13},{13,9},{2,6},{6,2},{1... | collective-permute-start | bytes 589832 | tf_op jit(solution)/shard_map/ppermute | solution.py:302
  28.0 8.1 %copy-start.3 = (bf16[1536,1536]{1,0:T(8,128)(2,1)}, bf16[1536,1536]{1,0:T(8,128)(2,1)S(1)}, u32[]{:S(2)}) copy-start(bf16[1536,1536]{1,0:T(8,128)(2,1)S(1)} %get-tuple-element.45.operator_ref) | copy-start | bytes 14155780
  28.0 13.1 %collective-permute-start.1 = (bf16[2,768,512]{2,1,0:T(8,128)(2,1)}, bf16[2,768,512]{2,1,0:T(8,128)(2,1)}, u32[]{:S(2)}, u32[]{:S(2)}) collective-permute-start(bf16[2,768,512]{2,1,0:T(8,128)(2,1)} %get-tuple-element.44), channel_id=1, source_target_pairs={{0,1},{1,0},{2,3},{3,2},{4,5},{5,4},{6,7},{7,6},{8,9},{9,8},{10,11... | collective-permute-start | bytes 4718600 | tf_op jit(solution)/shard_map/ppermute | solution.py:329
  36.1 0.7 copy-start.1
  36.8 19.0 %collective-permute-start.11 = (bf16[384,256]{1,0:T(8,128)(2,1)}, bf16[384,256]{1,0:T(8,128)(2,1)S(1)}, u32[]{:S(2)}, u32[]{:S(2)}) collective-permute-start(bf16[384,256]{1,0:T(8,128)(2,1)} %get-tuple-element.53), channel_id=1, source_target_pairs={{0,12},{4,8},{8,4},{12,0},{1,13},{5,9},{9,5},{13,1},{2,14},{6,10},... | collective-permute-start | bytes 589832 | tf_op jit(solution)/shard_map/ppermute | solution.py:302
  40.0 11.2 %copy-start.4 = (bf16[1536,1536]{1,0:T(8,128)(2,1)S(1)}, bf16[1536,1536]{1,0:T(8,128)(2,1)}, u32[]{:S(2)}) copy-start(bf16[1536,1536]{1,0:T(8,128)(2,1)} %copy-done.3) | copy-start | bytes 14155780
  41.1 3.3 %copy-start.2 = (bf16[384,256]{1,0:T(8,128)(2,1)S(1)}, bf16[384,256]{1,0:T(8,128)(2,1)}, u32[]{:S(2)}) copy-start(bf16[384,256]{1,0:T(8,128)(2,1)} %copy-done.1) | copy-start | bytes 589828
  42.8 17.9 %copy-start.5 = (bf16[1,768,512]{2,1,0:T(8,128)(2,1)S(1)}, bf16[1,768,512]{2,1,0:T(8,128)(2,1)}, u32[]{:S(2)}) copy-start(bf16[1,768,512]{2,1,0:T(8,128)(2,1)} %param.9) | copy-start | bytes 2359300
  42.8 16.4 %collective-permute-start.4 = (bf16[768,512]{1,0:T(8,128)(2,1)S(1)}, bf16[768,512]{1,0:T(8,128)(2,1)S(1)}, u32[]{:S(2)}, u32[]{:S(2)}) collective-permute-start(bf16[768,512]{1,0:T(8,128)(2,1)S(1)} %fusion), channel_id=1, source_target_pairs={{0,2},{2,0},{1,3},{3,1},{4,6},{6,4},{5,7},{7,5},{8,10},{10,8},{9,1... | collective-permute-start | bytes 2359304 | tf_op jit(solution)/shard_map/ppermute | solution.py:349
  44.4 23.5 %collective-permute-start.12 = (bf16[384,256]{1,0:T(8,128)(2,1)S(1)}, bf16[384,256]{1,0:T(8,128)(2,1)S(1)}, u32[]{:S(2)}, u32[]{:S(2)}) collective-permute-start(bf16[384,256]{1,0:T(8,128)(2,1)S(1)} %copy-done.2), channel_id=1, source_target_pairs={{0,8},{4,12},{8,0},{12,4},{1,9},{5,13},{9,1},{13,5},{2,10},{6,14},... | collective-permute-start | bytes 589832 | tf_op jit(solution)/shard_map/ppermute | solution.py:302
  51.1 16.8 %collective-permute-start.13 = (bf16[384,256]{1,0:T(8,128)(2,1)S(1)}, bf16[384,256]{1,0:T(8,128)(2,1)S(1)}, u32[]{:S(2)}, u32[]{:S(2)}) collective-permute-start(bf16[384,256]{1,0:T(8,128)(2,1)S(1)} %get-tuple-element.55), channel_id=1, source_target_pairs={{0,4},{4,0},{8,12},{12,8},{1,5},{5,1},{9,13},{13,9},{2,6},{6,2},{1... | collective-permute-start | bytes 589832 | tf_op jit(solution)/shard_map/ppermute | solution.py:302
  53.7 15.7 %collective-permute-start.10 = (bf16[384,256]{1,0:T(8,128)(2,1)S(1)}, bf16[384,256]{1,0:T(8,128)(2,1)S(1)}, u32[]{:S(2)}, u32[]{:S(2)}) collective-permute-start(bf16[384,256]{1,0:T(8,128)(2,1)S(1)} %get-tuple-element.63), channel_id=1, source_target_pairs={{0,4},{4,0},{8,12},{12,8},{1,5},{5,1},{9,13},{13,9},{2,6},{6,2},{1... | collective-permute-start | bytes 589832 | tf_op jit(solution)/shard_map/ppermute | solution.py:302
  55.8 13.6 %collective-permute-start.8 = (bf16[384,256]{1,0:T(8,128)(2,1)S(1)}, bf16[384,256]{1,0:T(8,128)(2,1)S(1)}, u32[]{:S(2)}, u32[]{:S(2)}) collective-permute-start(bf16[384,256]{1,0:T(8,128)(2,1)S(1)} %get-tuple-element.61), channel_id=1, source_target_pairs={{0,12},{4,8},{8,4},{12,0},{1,13},{5,9},{9,5},{13,1},{2,14},{6,10},... | collective-permute-start | bytes 589832 | tf_op jit(solution)/shard_map/ppermute | solution.py:302
  59.2 8.7 %copy-start = (f32[512]{0:T(512)S(1)}, f32[512]{0:T(512)}, u32[]{:S(2)}) copy-start(f32[512]{0:T(512)} %param.15) | copy-start | bytes 6148
  59.2 15.9 %collective-permute-start.9 = (bf16[384,256]{1,0:T(8,128)(2,1)S(1)}, bf16[384,256]{1,0:T(8,128)(2,1)S(1)}, u32[]{:S(2)}, u32[]{:S(2)}) collective-permute-start(bf16[384,256]{1,0:T(8,128)(2,1)S(1)} %get-tuple-element.62), channel_id=1, source_target_pairs={{0,8},{4,12},{8,0},{12,4},{1,9},{5,13},{9,1},{13,5},{2,10},{6,14},... | collective-permute-start | bytes 589832 | tf_op jit(solution)/shard_map/ppermute | solution.py:302

commit v10 on v9

--- a/solution.py
+++ b/solution.py
@@ -8,7 +8,6 @@
 from jax.sharding import PartitionSpec as P
 
 VMEM_LIMIT = 28 * 1024 * 1024
-HALVES = 2
 F32 = jnp.float32
 BF16 = jnp.bfloat16
 CHEAP = pl.CostEstimate(flops=0, bytes_accessed=0, transcendentals=0)
@@ -31,9 +30,9 @@
     return jnp.where(match, 1.0, 0.0).astype(BF16)
 
 
-def block_offsets(paired, chan_count, block_rows):
+def block_offsets(paired, chan_count, send):
     chan = lax.axis_index("chan")
-    return [(chan ^ k) * block_rows for k in range(chan_count)] if paired else [0]
+    return [(chan ^ k) * send for k in range(chan_count)] if paired else [0]
 
 
 def slots_of(owners, send, names):
@@ -56,14 +55,14 @@
         within = counts[i * names : (i + 1) * names]
         slots.append(jnp.sum(jnp.where(hot[i], within[:, :lane] + passed, 0.0), axis=0, keepdims=True))
         passed = passed + within[:, lane:]
-    return owners * send + jnp.concatenate(slots, axis=1).astype(jnp.int32)
+    return owners * send + jnp.concatenate(slots, axis=1).astype(jnp.int32), passed
 
 
 def pack_kernel(plan, given, route_in, amps_hbm, *refs):
-    paired, chan_count, send, block_rows, items = plan
+    paired, chan_count, send, items = plan
     outs, (route_ref, amps_ref, sems) = refs[:-3], refs[-3:]
-    block_refs = outs if given else outs[1:]
-    amps_copy = pltpu.make_async_copy(amps_hbm.at[:, pl.ds(0, amps_ref.shape[1])], amps_ref, sems.at[1])
+    block_refs = outs if given else outs[2:]
+    amps_copy = pltpu.make_async_copy(amps_hbm, amps_ref, sems.at[1])
     if given:
         amps_copy.start()
         target = route_in[...]
@@ -72,32 +71,30 @@
         route_copy.start()
         amps_copy.start()
         route_copy.wait()
-        target = slots_of(route_ref[...], send, max(16, chan_count))
+        target, counts = slots_of(route_ref[...], send, outs[1].shape[0])
         outs[0][...] = target
-    offsets = block_offsets(paired, chan_count, block_rows)
-    slot = lax.broadcasted_iota(jnp.int32, (block_rows, target.shape[1]), 0)
-    for i, (k, first, width) in enumerate(items):
-        pick = selection(slot == target - offsets[k])
+        outs[1][...] = counts
+    offsets = block_offsets(paired, chan_count, send)
+    for i, (k, first, size) in enumerate(items):
+        slot = lax.broadcasted_iota(jnp.int32, (size, target.shape[1]), 0)
+        pick = selection(slot == target - (offsets[k] + first))
         if i == 0:
             amps_copy.wait()
-        block_refs[i][...] = jnp.dot(
-            pick, amps_ref[:, pl.ds(first, width)], preferred_element_type=F32
-        ).astype(BF16)
+        block_refs[i][...] = jnp.dot(pick, amps_ref[...], preferred_element_type=F32).astype(BF16)
 
 
 def pack(plan, given, route_row, amps, name):
-    rows = amps.shape[0]
-    block_rows, items = plan[3], plan[4]
-    columns = max(first + width for _, first, width in items)
-    extra = [] if given else [pltpu.VMEM((1, rows), jnp.int32)]
+    rows, holes = amps.shape
+    items = plan[3]
+    extra = [] if given else [pltpu.VMEM((1, rows), jnp.int32), pltpu.VMEM((max(16, plan[1]), 128), F32)]
     return pl.pallas_call(
         functools.partial(pack_kernel, plan, given),
-        out_shape=extra + [pltpu.VMEM((block_rows, width), BF16) for _, _, width in items],
+        out_shape=extra + [pltpu.VMEM((size, holes), BF16) for _, _, size in items],
         in_specs=[whole() if given else whole(pl.ANY), whole(pl.ANY)],
         out_specs=[whole()] * (len(extra) + len(items)),
         scratch_shapes=[
             pltpu.VMEM((1, rows), jnp.int32),
-            pltpu.VMEM((rows, columns), BF16),
+            pltpu.VMEM((rows, holes), BF16),
             pltpu.SemaphoreType.DMA((2,)),
         ],
         compiler_params=params(),
@@ -199,76 +196,63 @@
     return outs[:sub_count], outs[sub_count]
 
 
-def cycle_kernel(half, plan, operator_ref, *refs):
-    paired, chan_count, _, _ = plan
-    count = len(refs) // 2
-    in_refs, out_refs, block_ref = refs[:count], refs[count : 2 * count], refs[2 * count]
-    block_rows, width = out_refs[0].shape
-    offsets = block_offsets(paired, chan_count, block_rows)
-    starts = [pl.multiple_of(offsets[count - 1 - i], block_rows) for i in range(count)]
-    for in_ref, start in zip(in_refs, starts):
-        part = in_ref[...] if in_ref.shape[1] == width else in_ref[:, pl.ds(half * width, width)]
-        block_ref[pl.ds(start, block_rows), :] = part
-    for out_ref, start in zip(out_refs, starts):
-        out_ref[...] = jnp.dot(
-            operator_ref[pl.ds(start, block_rows), :], block_ref[...], preferred_element_type=F32
-        ).astype(BF16)
-
-
-def apply_cycle(half, plan, operator, arrays, width):
-    block_rows = arrays[0].shape[0]
+def cycle_kernel(plan, operator_ref, *refs):
+    paired, chan_count, send, items = plan
+    in_refs, out_refs, block_ref = refs[: len(items)], refs[len(items) : -1], refs[-1]
+    offsets = block_offsets(paired, chan_count, send)
+    align = 128 if paired else block_ref.shape[0]
+    places = [pl.ds(pl.multiple_of(offsets[k] + first, align), size) for k, first, size in items]
+    for in_ref, at in zip(in_refs, places):
+        block_ref[at, :] = in_ref[...]
+    for out_ref, at in zip(out_refs, places):
+        out_ref[...] = jnp.dot(operator_ref[at, :], block_ref[...], preferred_element_type=F32).astype(BF16)
+
+
+def apply_cycle(plan, operator, arrays):
     return pl.pallas_call(
-        functools.partial(cycle_kernel, half, plan),
-        out_shape=[jax.ShapeDtypeStruct((block_rows, width), BF16)] * len(arrays),
+        functools.partial(cycle_kernel, plan),
+        out_shape=[jax.ShapeDtypeStruct(a.shape, BF16) for a in arrays],
         in_specs=[whole()] * (1 + len(arrays)),
         out_specs=[whole()] * len(arrays),
-        scratch_shapes=[pltpu.VMEM((operator.shape[0], width), BF16)],
+        scratch_shapes=[pltpu.VMEM((operator.shape[0], arrays[0].shape[1]), BF16)],
         compiler_params=params(),
         cost_estimate=DEAR,
         name="apply_cycle",
     )(operator, *arrays)
 
 
-def finish_kernel(half, count, tiles, pick_ref, base_ref, part_ref, hole_ref, *refs):
-    in_refs, (out_hbm, block_ref, out_ref, sems) = refs[:count], refs[-4:]
-    block_rows, width = in_refs[0].shape
+def finish_kernel(plan, tiles, pick_ref, base_ref, part_ref, hole_ref, *refs):
+    _, _, send, items = plan
+    in_refs, (out_hbm, block_ref, out_ref, sems) = refs[: len(items)], refs[len(items) :]
     tile = out_ref.shape[0] // tiles
-    columns = pl.ds(half * width, width)
-    for i, in_ref in enumerate(in_refs):
-        block_ref[pl.ds((count - 1 - i) * block_rows, block_rows), :] = in_ref[...]
+    for (k, first, size), in_ref in zip(items, in_refs):
+        block_ref[pl.ds(k * send + first, size), :] = in_ref[...]
     copies = []
     for t in range(tiles):
         at = pl.ds(t * tile, tile)
         back = jnp.dot(pick_ref[at, :], block_ref[...], preferred_element_type=F32)
-        total = base_ref[at, columns] + back
-        out_ref[at, :] = (total / (part_ref[at, :] + hole_ref[:, columns])).astype(BF16)
-        copies.append(pltpu.make_async_copy(out_ref.at[at, :], out_hbm.at[at, columns], sems.at[t]))
+        total = base_ref[at, :] + back
+        out_ref[at, :] = (total / (part_ref[at, :] + hole_ref[...])).astype(BF16)
+        copies.append(pltpu.make_async_copy(out_ref.at[at, :], out_hbm.at[at, :], sems.at[t]))
         copies[-1].start()
     for copy in copies:
         copy.wait()
 
 
-def finish(half, pick, base, part_column, hole_row, arrays, earlier):
+def finish(plan, pick, base, part_column, hole_row, arrays):
     rows, holes = base.shape
-    tiles, width = 3, holes // HALVES
+    tiles = 3
     operands = [pick, base, part_column, hole_row, *arrays]
-    in_specs = [whole()] * len(operands)
-    aliases = {}
-    if earlier is not None:
-        aliases = {len(operands): 0}
-        operands.append(earlier)
-        in_specs.append(whole(pl.ANY))
     return pl.pallas_call(
-        functools.partial(finish_kernel, half, len(arrays), tiles),
+        functools.partial(finish_kernel, plan, tiles),
         out_shape=jax.ShapeDtypeStruct((rows, holes), BF16),
-        in_specs=in_specs,
+        in_specs=[whole()] * len(operands),
         out_specs=whole(pl.ANY),
         scratch_shapes=[
-            pltpu.VMEM((pick.shape[1], width), BF16),
-            pltpu.VMEM((rows, width), BF16),
+            pltpu.VMEM((pick.shape[1], holes), BF16),
+            pltpu.VMEM((rows, holes), BF16),
             pltpu.SemaphoreType.DMA((tiles,)),
         ],
-        input_output_aliases=aliases,
         compiler_params=params(),
         cost_estimate=CHEAP,
         name="finish",
@@ -287,69 +271,93 @@
     send = capacity // chan_count
     paired = send % mixing.shape[1] == 0 and chan_count & (chan_count - 1) == 0
     if paired:
-        block_rows = send
-        block_index = jnp.stack([chan ^ k for k in range(chan_count)]).astype(jnp.int32)
+        offsets = jnp.stack([(chan ^ k) * send for k in range(chan_count)]).astype(jnp.int32)
+        first = send - mixing.shape[1] if send > mixing.shape[1] else send
+        early = [(k, 0, first) for k in reversed(range(1, chan_count))]
+        late = [(k, first, send - first) for k in reversed(range(1, chan_count)) if send > first]
+        own = [(0, 0, send)]
     else:
-        block_rows = capacity
-        block_index = jnp.zeros((1,), jnp.int32)
-    offsets = block_index * block_rows
-
-    def exchange(block, k):
+        offsets = jnp.zeros((1,), jnp.int32)
+        early, late, own = [(0, 0, capacity)], [], []
+    items = early + late + own
+    plan = (paired, chan_count, send)
+
+    def exchange(arrays):
         if not paired:
-            split = block.reshape(chan_count, send, -1)
+            split = arrays[0].reshape(chan_count, send, holes)
             split = lax.all_to_all(split, "chan", split_axis=0, concat_axis=0, tiled=True)
-            return split.reshape(capacity, -1)
-        return lax.ppermute(block, "chan", [(i, i ^ k) for i in range(chan_count)]) if k else block
-
-    far_first = list(reversed(range(block_index.shape[0])))
-    count = len(far_first)
-    width = holes // HALVES
+            return [split.reshape(capacity, holes)]
+        return [
+            lax.ppermute(a, "chan", [(i, i ^ k) for i in range(chan_count)]) for (k, _, _), a in zip(early, arrays)
+        ]
+
+    def crowded(counts):
+        others = chan_count * lad_count * sub_count
+        lines = -(-chan_count // 8) * 8
+        sent = jnp.broadcast_to(counts[:lines][None], (others, lines, 128))
+        every = lax.all_to_all(sent, ("chan", "lad", "sub"), split_axis=0, concat_axis=0, tiled=True)
+        over = (jnp.max(every, axis=(0, 2))[:chan_count] > first).astype(jnp.int32)
+        which = jnp.sum(over * (1 + jnp.arange(chan_count, dtype=jnp.int32)))
+        return jnp.where(jnp.sum(over) > 1, chan_count + 1, which)
+
+    def along(axis, arrays):
+        size = lax.axis_size(axis)
+        return [
+            lax.ppermute(a, axis, [(i, (i + step) % size) for i in range(size)]) for step, a in enumerate(arrays, 1)
+        ]
+
+    def exchange_late(index, before, axis, terms, arrays, back):
+        def case(pairs_of, before, terms, arrays):
+            sent = exchange(before) if before else []
+            moved = [
+                lax.ppermute(a, "chan", pairs_of(k)) if pairs_of else jnp.zeros_like(a)
+                for (k, _, _), a in zip(late, arrays)
+            ]
+            return sent, along(axis, terms), moved
+
+        def single(d, k):
+            return [(d, d ^ k) if back else (d ^ k, d)]
+
+        def several(k):
+            return [(i, i ^ k) for i in range(chan_count)]
+
+        if not late:
+            return case(None, before, terms, arrays)
+        kinds = [None] + [functools.partial(single, d) for d in range(chan_count)] + [several]
+        return lax.switch(index, [functools.partial(case, kind) for kind in kinds], before, terms, arrays)
+
     route_row = route[0].reshape(1, rows)
-    plan = (paired, chan_count, send, block_rows)
-    early = [(k, 0, width) for k in far_first if k or not paired]
-    late = [(k, h * width, width) for h in range(1, HALVES) for k in far_first if k or not paired]
-    late += [(0, 0, holes)] if paired else []
-    target, *blocks = pack(plan + (early,), False, route_row, amps, "pack_first")
-    arrived = {(k, 0): exchange(block, k) for (k, _, _), block in zip(early, blocks)}
+    target, counts, *blocks = pack(plan + (early,), False, route_row, amps, "pack_first")
+    arrived = exchange(blocks)
+    amps, target, counts = lax.optimization_barrier((amps, target, counts))
     if paired:
-        near = (1, 0)
-        target, arrived[near] = lax.optimization_barrier((target, arrived[near]))
-    blocks = pack(plan + (late,), True, target, amps, "pack_rest")
-    for (k, first, _), block in zip(late, blocks):
-        arrived[(k, first // width)] = exchange(block, k)
-
-    part_column, hole_row = gap_part[0].reshape(rows, 1), gap_hole.reshape(1, holes)
-    amps, blocks = lax.optimization_barrier((amps, blocks))
+        amps, target, arrived[-1] = lax.optimization_barrier((amps, target, arrived[-1]))
+    index = crowded(counts) if late else None
+    packed = []
+    if late or own:
+        packed = pack(plan + (late + own,), True, target, amps, "pack_rest")
+        amps, packed = lax.optimization_barrier((amps, packed))
+    extra, mine = packed[: len(late)], packed[len(late) :]
     pick = unpack_matrix(offsets, target.reshape(rows, 1), capacity)
-
+    amps, pick = lax.optimization_barrier((amps, pick))
     parts, operator = prepare(ladder_weight[0], amps, weight, mixing, lad_count, sub_count)
-    kept = [parts[-1]]
-    for step in range(1, sub_count):
-        pairs = [(i, (i + step) % sub_count) for i in range(sub_count)]
-        kept.append(lax.ppermute(parts[sub_count - 1 - step], "sub", pairs))
+    _, _, extra = exchange_late(index, [], "sub", [], extra, False)
+    extra, parts = lax.optimization_barrier((extra, parts))
+    kept = [parts[-1], *along("sub", list(reversed(parts[:-1])))]
 
     def chip_sum(position):
         picked = [lax.dynamic_index_in_dim(p, position, 0, keepdims=False) for p in kept]
         return sum(p.astype(F32) for p in picked)
 
+    part_column, hole_row = gap_part[0].reshape(rows, 1), gap_hole.reshape(1, holes)
     base = driving[0].astype(F32) + chip_sum(lad)
     terms = [chip_sum(lax.rem(lad + step, lad_count)).astype(BF16) for step in range(1, lad_count)]
-    returned = []
-    for half in range(HALVES):
-        blocks = [arrived[(k, half if k or not paired else 0)] for k in far_first]
-        if returned:
-            blocks, made = lax.optimization_barrier((blocks, made))
-        made = apply_cycle(half, plan, operator, blocks, width)
-        if not half:
-            behind, terms = lax.optimization_barrier((made[1:], terms))
-            made = [made[0], *behind]
-        returned.append([exchange(block, k) for k, block in zip(far_first, made)])
-    for step, term in enumerate(terms, 1):
-        pairs = [(i, (i + step) % lad_count) for i in range(lad_count)]
-        base = base + lax.ppermute(term, "lad", pairs).astype(F32)
-    updated = None
-    for half in range(HALVES):
-        updated = finish(half, pick, base, part_column, hole_row, returned[half], updated)
+    made = apply_cycle(plan + (items,), operator, [*arrived, *extra, *mine])
+    made_early, made_late, made_own = made[: len(early)], made[len(early) : len(early + late)], made[len(early + late) :]
+    returned, arrived_terms, returned_late = exchange_late(index, made_early, "lad", terms, made_late, True)
+    for term in arrived_terms:
+        base = base + term.astype(F32)
+    updated = finish(plan + (items,), pick, base, part_column, hole_row, [*returned, *returned_late, *made_own])
     return updated[None]
 
 

time: 77 us -> 101 us (1.31)
  starting transfers between devices: 24.2 us -> 36.7 us
  local copies, waits for them, and re-layouts: 1.75 us -> 11.6 us
  between operations: 0.17 us -> 1.7 us
    unnamed x12 -> x30, local copies, waits for them, and re-layouts: 0.71 us -> 9.97 us
    all_to_all x0 -> x1, starting transfers between devices: none -> 7.36 us  [crowded(): lax.all_to_all(sent, ('chan', 'lad', 'sub'), split_axis=0, concat_axis=0,...]
    ppermute x14, starting transfers between devices: 24.2 us -> 29.4 us  [the longest x6 16.5 us: case(): lax.ppermute(a, 'chan', pairs_of(k))]
    ppermute x14, waiting for transfers between devices: 26.5 us -> 24.3 us  [the longest x6 21.8 us: exchange(): lax.ppermute(a, 'chan', [(i, i ^ k) for i in range(chan_count)])]
    all_to_all x0 -> x1, waiting for transfers between devices: none -> 2.19 us  [crowded(): lax.all_to_all(sent, ('chan', 'lad', 'sub'), split_axis=0, concat_axis=0,...]
    convert_element_type x1, other arithmetic: 1.69 us -> 0.22 us  [body(): chip_sum(lax.rem(lad + step, lad_count)).astype(BF16)]
    pallas_call x4 -> x2, Pallas kernels: 7.51 us -> 7.35 us  [the longest x1 3.99 us: apply_cycle(): pl.pallas_call(functools.partial(cycle_kernel, plan), out_shape=[jax.Shap...]
  transfers between devices with their start and end apart: 14 -> 15, of which waited for: 6 -> 5; matrix products, arithmetic and copies ran while one was open for 6% -> 2% of each run, Pallas kernels for 23% -> 15%
where the time goes in v10:
time: 101 us
  starting transfers between devices  36.7 us (36%)
  waiting for transfers between devices  26.5 us (26%)
  Pallas kernels  20.9 us (21%)
  local copies, waits for them, and re-layouts  11.6 us (11%)
  other arithmetic  3.32 us (3%)
  between operations  1.7 us (2%)
    ppermute x6, waiting for transfers between devices, exchange(): lax.ppermute(a, 'chan', [(i, i ^ k) for i in range(chan_count)])  21.8 us
    ppermute x6, starting transfers between devices, case(): lax.ppermute(a, 'chan', pairs_of(k))  16.5 us
    ppermute x6, starting transfers between devices, exchange(): lax.ppermute(a, 'chan', [(i, i ^ k) for i in range(chan_count)])  11.2 us
    unnamed x30, local copies, waits for them, and re-layouts  9.97 us
    pallas_call x1, Pallas kernels, prepare(): pl.pallas_call(functools.partial(prepare_kernel, sub_count), out_shape=[j...  8.01 us
    all_to_all x1, starting transfers between devices, crowded(): lax.all_to_all(sent, ('chan', 'lad', 'sub'), split_axis=0, concat_axis=0,...  7.36 us
    pallas_call x2, Pallas kernels, pack(): pl.pallas_call(functools.partial(pack_kernel, plan, given), out_shape=ext...  4.48 us
    pallas_call x1, Pallas kernels, apply_cycle(): pl.pallas_call(functools.partial(cycle_kernel, plan), out_shape=[jax.Shap...  3.99 us
  transfers between devices with their start and end apart: 15, of which 5 were waited for; matrix products, arithmetic and copies ran while one was open for 2% of the time, Pallas kernels for 15%

profile of v10, /device:TPU:0, one launch (start us, length us, event | category | flops | bytes accessed | tf_op | source)
XLA Modules:
  0.0 100.8 jit_solution(7699837526398369413)
XLA Ops:
  0.0 2.5 %pack_first.1 = (s32[1,768]{1,0:T(1,128)S(1)}, f32[16,128]{1,0:T(8,128)S(1)}, bf16[256,512]{1,0:T(8,128)(2,1)}, bf16[256,512]{1,0:T(8,128)(2,1)}, bf16[256,512]{1,0:T(8,128)(2,1)S(1)}) custom-call(s32[1,768]{1,0:T(1,128)} %bitcast.22, bf16[768,512]{1,0:T(8,128)(2,1)} %bitcast.19), custom_call_target="tpu_custom_call" | custom-call | tf_op jit(solution)/shard_map/pack_first/pallas_call | solution.py:90
  2.5 0.6 broadcast_in_dim.4
  3.1 7.4 %all-to-all-start = ((f32[16,8,128]{2,1,0:T(8,128)}), f32[16,8,128]{2,1,0:T(8,128)S(1)}, u32[]{:S(2)}, u32[]{:S(2)}) async-start(f32[16,8,128]{2,1,0:T(8,128)} %broadcast_in_dim.4), calls=%async_computation | async-start | bytes 131072 | tf_op jit(solution)/shard_map/all_to_all | solution.py:298
  10.5 1.9 %collective-permute-start.54 = (bf16[256,512]{1,0:T(8,128)(2,1)S(1)}, bf16[256,512]{1,0:T(8,128)(2,1)S(1)}, u32[]{:S(2)}, u32[]{:S(2)}) collective-permute-start(bf16[256,512]{1,0:T(8,128)(2,1)S(1)} %get-tuple-element.236), channel_id=1, source_target_pairs={{0,4},{4,0},{8,12},{12,8},{1,5},{5,1},{9,13},{13,9},{2,6},{6,2},{1... | collective-permute-start | bytes 786440 | tf_op jit(solution)/shard_map/ppermute | solution.py:291
  12.4 2.4 %collective-permute-start.56 = (bf16[256,512]{1,0:T(8,128)(2,1)}, bf16[256,512]{1,0:T(8,128)(2,1)}, u32[]{:S(2)}, u32[]{:S(2)}) collective-permute-start(bf16[256,512]{1,0:T(8,128)(2,1)} %get-tuple-element.258), channel_id=1, source_target_pairs={{0,12},{4,8},{8,4},{12,0},{1,13},{5,9},{9,5},{13,1},{2,14},{6,10},... | collective-permute-start | bytes 786440 | tf_op jit(solution)/shard_map/ppermute | solution.py:291
  14.8 0.0 collective-permute-start.57
  14.8 0.9 copy.12.part_ref
  15.6 2.2 %all-to-all-done = f32[16,8,128]{2,1,0:T(8,128)S(1)} async-done(((f32[16,8,128]{2,1,0:T(8,128)}), f32[16,8,128]{2,1,0:T(8,128)S(1)}, u32[]{:S(2)}, u32[]{:S(2)}) %all-to-all-start) | async-done | bytes 65568 | tf_op jit(solution)/shard_map/all_to_all | solution.py:298
  17.8 0.1 reduce_max.9
  18.0 0.7 fusion.2
  20.0 0.3 collective-permute-done.54.refs_2_
  20.3 2.0 %pack_rest.1 = (bf16[128,512]{1,0:T(8,128)(2,1)S(1)}, bf16[128,512]{1,0:T(8,128)(2,1)S(1)}, bf16[128,512]{1,0:T(8,128)(2,1)S(1)}, bf16[384,512]{1,0:T(8,128)(2,1)S(1)}) custom-call(s32[1,768]{1,0:T(1,128)S(1)} %get-tuple-element.238.route_in, bf16[768,512]{1,0:T(8,128)(2,1)} %bitcast.20), custom_call_target="tpu_custom_call" | custom-call | tf_op jit(solution)/shard_map/pack_rest/pallas_call | solution.py:90
  22.3 0.0 copy-start.10
  22.3 0.7 copy-done.10
  23.0 0.2 copy.11.target_ref
  23.2 0.0 copy-done.4
  23.2 0.4 copy-done.6
  23.6 0.1 copy-done.8
  23.7 1.1 %unpack_matrix.1.pick_ref = bf16[768,1536]{1,0:T(8,128)(2,1)S(1)} custom-call(s32[4]{0:T(128)S(1)} %get-tuple-element.290.off_ref, s32[768,1]{1,0:T(8,128)S(1)} %copy.11.target_ref), custom_call_target="tpu_custom_call" | custom-call | tf_op jit(solution)/shard_map/unpack_matrix/pallas_call | solution.py:116
  24.8 0.0 copy-start.7
  24.8 0.0 copy-start.9
  24.8 0.0 copy-start.11
  24.8 8.0 %prepare.1 = (bf16[2,768,512]{2,1,0:T(8,128)(2,1)S(1)}, bf16[2,768,512]{2,1,0:T(8,128)(2,1)S(1)}, bf16[1536,1536]{1,0:T(8,128)(2,1)S(1)}) custom-call(bf16[3072,768]{1,0:T(8,128)(2,1)} %bitcast.24, bf16[768,512]{1,0:T(8,128)(2,1)} %bitcast.21, bf16[1536,1536]{1,0:T(8,128)(2,1)} %bitcast.25, bf16[12,128,128]{2,1,0:T(8,128)(2,1)} %bitcast.26), custom_call_target="tpu_custom_call" | custom-call | flops 30000001024 | bytes 1000000 | tf_op jit(solution)/shard_map/prepare/pallas_call | solution.py:177
  32.8 0.0 copy-start
  32.8 1.2 %copy-done = bf16[2,768,512]{2,1,0:T(8,128)(2,1)} copy-done((bf16[2,768,512]{2,1,0:T(8,128)(2,1)}, bf16[2,768,512]{2,1,0:T(8,128)(2,1)S(1)}, u32[]{:S(2)}) %copy-start) | copy-done | bytes 1572888
  34.0 1.2 %copy-done.3 = bf16[2,768,512]{2,1,0:T(8,128)(2,1)} copy-done((bf16[2,768,512]{2,1,0:T(8,128)(2,1)}, bf16[2,768,512]{2,1,0:T(8,128)(2,1)S(1)}, u32[]{:S(2)}) %copy-start.3) | copy-done | bytes 1572888
  35.2 2.2 %copy-done.12 = bf16[1536,1536]{1,0:T(8,128)(2,1)} copy-done((bf16[1536,1536]{1,0:T(8,128)(2,1)}, bf16[1536,1536]{1,0:T(8,128)(2,1)S(1)}, u32[]{:S(2)}) %copy-start.12) | copy-done | bytes 4718616
  37.4 0.0 copy-done.7
  37.4 0.0 copy-done.9
  37.4 0.0 copy-done.11
  37.4 12.7 %conditional.4 = (bf16[128,512]{1,0:T(8,128)(2,1)}, bf16[128,512]{1,0:T(8,128)(2,1)}, bf16[128,512]{1,0:T(8,128)(2,1)}) conditional(s32[]{:T(128)} %clamp.4, () %tuple.88, (bf16[128,512]{1,0:T(8,128)(2,1)S(1)}, bf16[128,512]{1,0:T(8,128)(2,1)S(1)}, bf16[128,512]{1,0:T(8,128)(2,1)S(1)}) %tuple.130, ...), branch_computations={%region_3.4_spmd, %region_4.5_spmd, %region_5.6_spmd, %region_6.7_... | conditional | bytes 1573008 | solution.py:327
  37.5 10.0 %collective-permute-start.9 = (bf16[128,512]{1,0:T(8,128)(2,1)S(1)}, bf16[128,512]{1,0:T(8,128)(2,1)}, u32[]{:S(2)}, u32[]{:S(2)}) collective-permute-start(bf16[128,512]{1,0:T(8,128)(2,1)S(1)} %get-tuple-element.140), channel_id=1, source_target_pairs={{0,12},{1,13},{2,14},{3,15},{16,28},{17,29},{18,30},{19,31}} | collective-permute-start | bytes 393224 | tf_op jit(solution)/shard_map/cond/branch_4_fun/ppermute | solution.py:313
  47.4 1.3 %collective-permute-start.10 = (bf16[128,512]{1,0:T(8,128)(2,1)S(1)}, bf16[128,512]{1,0:T(8,128)(2,1)}, u32[]{:S(2)}, u32[]{:S(2)}) collective-permute-start(bf16[128,512]{1,0:T(8,128)(2,1)S(1)} %get-tuple-element.141), channel_id=1, source_target_pairs={{4,12},{5,13},{6,14},{7,15},{20,28},{21,29},{22,30},{23,31}} | collective-permute-start | bytes 393224 | tf_op jit(solution)/shard_map/cond/branch_4_fun/ppermute | solution.py:313
  48.8 1.3 %collective-permute-start.11 = (bf16[128,512]{1,0:T(8,128)(2,1)S(1)}, bf16[128,512]{1,0:T(8,128)(2,1)}, u32[]{:S(2)}, u32[]{:S(2)}) collective-permute-start(bf16[128,512]{1,0:T(8,128)(2,1)S(1)} %get-tuple-element.142), channel_id=1, source_target_pairs={{8,12},{9,13},{10,14},{11,15},{24,28},{25,29},{26,30},{27,31}} | collective-permute-start | bytes 393224 | tf_op jit(solution)/shard_map/cond/branch_4_fun/ppermute | solution.py:313
  50.1 0.0 collective-permute-done.9
  50.1 0.0 collective-permute-done.10
  50.1 0.0 collective-permute-done.11
  50.1 0.1 collective-permute-start.55
  50.2 0.0 collective-permute-done.56.refs_0_
  50.2 0.0 collective-permute-done.57.refs_1_
  50.2 0.0 copy-start.5
  50.2 0.9 copy-done.5
  51.1 2.3 %copy-done.13 = bf16[1536,1536]{1,0:T(8,128)(2,1)S(1)} copy-done((bf16[1536,1536]{1,0:T(8,128)(2,1)S(1)}, bf16[1536,1536]{1,0:T(8,128)(2,1)}, u32[]{:S(2)}) %copy-start.13) | copy-done | bytes 4718616
  53.5 4.0 %apply_cycle.1 = (bf16[256,512]{1,0:T(8,128)(2,1)S(1)}, bf16[256,512]{1,0:T(8,128)(2,1)S(1)}, bf16[256,512]{1,0:T(8,128)(2,1)S(1)}, bf16[128,512]{1,0:T(8,128)(2...) custom-call(bf16[1536,1536]{1,0:T(8,128)(2,1)S(1)} %copy-done.13, ...), custom_call_target="tpu_custom_call" | custom-call | flops 30000001024 | bytes 1000000 | tf_op jit(solution)/shard_map/apply_cycle/pallas_call | solution.py:212
  57.5 0.0 collective-permute-done.55
  57.5 0.2 fusion
  57.7 0.9 copy-done.14
  58.7 36.4 %conditional.6 = (bf16[256,512]{1,0:T(8,128)(2,1)}, bf16[256,512]{1,0:T(8,128)(2,1)}, bf16[256,512]{1,0:T(8,128)(2,1)}, bf16[128,512]{1,0:T(8,128)(2,1)}, bf16[1...) conditional(s32[]{:T(128)} %clamp.4, ...), branch_computations={%region_9.10_spmd, %region_10.11_spmd, %region_11.12_spmd, %region... | conditional | bytes 7864656
  58.7 1.5 %collective-permute-start.46 = (bf16[768,512]{1,0:T(8,128)(2,1)S(1)}, bf16[768,512]{1,0:T(8,128)(2,1)}, u32[]{:S(2)}, u32[]{:S(2)}) collective-permute-start(bf16[768,512]{1,0:T(8,128)(2,1)S(1)} %get-tuple-element.177), channel_id=1, source_target_pairs={{0,2},{2,0},{1,3},{3,1},{4,6},{6,4},{5,7},{7,5},{8,10},{10,8},{9,1... | collective-permute-start | bytes 2359304 | tf_op jit(solution)/shard_map/cond/branch_4_fun/ppermute | solution.py:306
  60.2 1.3 %collective-permute-start.43 = (bf16[128,512]{1,0:T(8,128)(2,1)S(1)}, bf16[128,512]{1,0:T(8,128)(2,1)}, u32[]{:S(2)}, u32[]{:S(2)}) collective-permute-start(bf16[128,512]{1,0:T(8,128)(2,1)S(1)} %get-tuple-element.174), channel_id=1, source_target_pairs={{12,0},{13,1},{14,2},{15,3},{28,16},{29,17},{30,18},{31,19}} | collective-permute-start | bytes 393224 | tf_op jit(solution)/shard_map/cond/branch_4_fun/ppermute | solution.py:313
  61.5 6.9 %collective-permute-start.40 = (bf16[256,512]{1,0:T(8,128)(2,1)S(1)}, bf16[256,512]{1,0:T(8,128)(2,1)}, u32[]{:S(2)}, u32[]{:S(2)}) collective-permute-start(bf16[256,512]{1,0:T(8,128)(2,1)S(1)} %get-tuple-element.171), channel_id=1, source_target_pairs={{0,12},{4,8},{8,4},{12,0},{1,13},{5,9},{9,5},{13,1},{2,14},{6,10},... | collective-permute-start | bytes 786440 | tf_op jit(solution)/shard_map/cond/branch_4_fun/ppermute | solution.py:291
  68.4 1.3 %collective-permute-start.44 = (bf16[128,512]{1,0:T(8,128)(2,1)S(1)}, bf16[128,512]{1,0:T(8,128)(2,1)}, u32[]{:S(2)}, u32[]{:S(2)}) collective-permute-start(bf16[128,512]{1,0:T(8,128)(2,1)S(1)} %get-tuple-element.175), channel_id=1, source_target_pairs={{12,4},{13,5},{14,6},{15,7},{28,20},{29,21},{30,22},{31,23}} | collective-permute-start | bytes 393224 | tf_op jit(solution)/shard_map/cond/branch_4_fun/ppermute | solution.py:313
  69.7 0.0 collective-permute-start.41
  69.7 2.5 %collective-permute-done.43 = bf16[128,512]{1,0:T(8,128)(2,1)} collective-permute-done((bf16[128,512]{1,0:T(8,128)(2,1)S(1)}, bf16[128,512]{1,0:T(8,128)(2,1)}, u32[]{:S(2)}, u32[]{:S(2)}) %collective-permute-start.43) | collective-permute-done | bytes 131104 | tf_op jit(solution)/shard_map/cond/branch_4_fun/ppermute | solution.py:313
  72.2 0.0 collective-permute-start.42
  72.2 0.0 collective-permute-done.44
  72.2 1.3 %collective-permute-start.45 = (bf16[128,512]{1,0:T(8,128)(2,1)S(1)}, bf16[128,512]{1,0:T(8,128)(2,1)}, u32[]{:S(2)}, u32[]{:S(2)}) collective-permute-start(bf16[128,512]{1,0:T(8,128)(2,1)S(1)} %get-tuple-element.176), channel_id=1, source_target_pairs={{12,8},{13,9},{14,10},{15,11},{28,24},{29,25},{30,26},{31,27}} | collective-permute-start | bytes 393224 | tf_op jit(solution)/shard_map/cond/branch_4_fun/ppermute | solution.py:313
  73.5 0.0 collective-permute-done.45
  73.5 4.3 %collective-permute-done.40 = bf16[256,512]{1,0:T(8,128)(2,1)} collective-permute-done((bf16[256,512]{1,0:T(8,128)(2,1)S(1)}, bf16[256,512]{1,0:T(8,128)(2,1)}, u32[]{:S(2)}, u32[]{:S(2)}) %collective-permute-start.40) | collective-permute-done | bytes 262176 | tf_op jit(solution)/shard_map/cond/branch_4_fun/ppermute | solution.py:291
  77.9 17.2 %collective-permute-done.41 = bf16[256,512]{1,0:T(8,128)(2,1)} collective-permute-done((bf16[256,512]{1,0:T(8,128)(2,1)S(1)}, bf16[256,512]{1,0:T(8,128)(2,1)}, u32[]{:S(2)}, u32[]{:S(2)}) %collective-permute-start.41) | collective-permute-done | bytes 262176 | tf_op jit(solution)/shard_map/cond/branch_4_fun/ppermute | solution.py:291
  95.0 0.0 collective-permute-done.42
  95.0 0.0 collective-permute-done.46
  95.0 2.3 %bitcast_add_fusion.base_ref = f32[768,512]{1,0:T(8,128)S(1)} fusion(bf16[768,512]{1,0:T(8,128)(2,1)} %get-tuple-element.287, bf16[1,768,512]{2,1,0:T(8,128)(2,1)} %param.21, bf16[2,768,512]{2,1,0:T(8,128)(2,1)} %copy-done.14, s32[]{:T(128)S(6)} %select_n.14, bf16[2,768,512]{2,1,0:T(8,128)(2,1)} %copy-done), kind=kLoop, calls=%fused_computation | loop fusion | flops 2752512 | bytes 4718596 | tf_op jit(solution)/shard_map/add | solution.py:359
  97.3 3.4 %finish.1 = bf16[768,512]{1,0:T(8,128)(2,1)} custom-call(bf16[768,1536]{1,0:T(8,128)(2,1)S(1)} %unpack_matrix.1.pick_ref, f32[768,512]{1,0:T(8,128)S(1)} %bitcast_add_fusion.base_ref, f32[768,1]{1,0:T(8,128)S(1)} %copy.12.part_ref, f32[1,512]{1,0:T(1,128)S(1)} %bitcast.18, bf16[256,512]{1,0:T(8,128)(2,1)} %get-tuple-element.272.refs_0_, ...), custom_call_target="tpu_custom_call" | custom-call | tf_op jit(solution)/shard_map/finish/pallas_call | solution.py:246
  (12 shorter events, 0.0 us)
Async XLA Ops:
  3.1 14.7 %all-to-all-start = ((f32[16,8,128]{2,1,0:T(8,128)}), f32[16,8,128]{2,1,0:T(8,128)S(1)}, u32[]{:S(2)}, u32[]{:S(2)}) async-start(f32[16,8,128]{2,1,0:T(8,128)} %broadcast_in_dim.4), calls=%async_computation | async-start | bytes 131072 | tf_op jit(solution)/shard_map/all_to_all | solution.py:298
  10.5 9.8 %collective-permute-start.54 = (bf16[256,512]{1,0:T(8,128)(2,1)S(1)}, bf16[256,512]{1,0:T(8,128)(2,1)S(1)}, u32[]{:S(2)}, u32[]{:S(2)}) collective-permute-start(bf16[256,512]{1,0:T(8,128)(2,1)S(1)} %get-tuple-element.236), channel_id=1, source_target_pairs={{0,4},{4,0},{8,12},{12,8},{1,5},{5,1},{9,13},{13,9},{2,6},{6,2},{1... | collective-permute-start | bytes 786440 | tf_op jit(solution)/shard_map/ppermute | solution.py:291
  12.4 37.8 %collective-permute-start.56 = (bf16[256,512]{1,0:T(8,128)(2,1)}, bf16[256,512]{1,0:T(8,128)(2,1)}, u32[]{:S(2)}, u32[]{:S(2)}) collective-permute-start(bf16[256,512]{1,0:T(8,128)(2,1)} %get-tuple-element.258), channel_id=1, source_target_pairs={{0,12},{4,8},{8,4},{12,0},{1,13},{5,9},{9,5},{13,1},{2,14},{6,10},... | collective-permute-start | bytes 786440 | tf_op jit(solution)/shard_map/ppermute | solution.py:291
  14.8 35.4 %collective-permute-start.57 = (bf16[256,512]{1,0:T(8,128)(2,1)}, bf16[256,512]{1,0:T(8,128)(2,1)}, u32[]{:S(2)}, u32[]{:S(2)}) collective-permute-start(bf16[256,512]{1,0:T(8,128)(2,1)} %get-tuple-element.259), channel_id=1, source_target_pairs={{0,8},{4,12},{8,0},{12,4},{1,9},{5,13},{9,1},{13,5},{2,10},{6,14},... | collective-permute-start | bytes 786440 | tf_op jit(solution)/shard_map/ppermute | solution.py:291
  20.3 2.9 %copy-start.4 = (bf16[256,512]{1,0:T(8,128)(2,1)}, bf16[256,512]{1,0:T(8,128)(2,1)S(1)}, u32[]{:S(2)}) copy-start(bf16[256,512]{1,0:T(8,128)(2,1)S(1)} %collective-permute-done.54.refs_2_) | copy-start | bytes 786436
  22.3 0.7 copy-start.10
  23.0 0.7 copy-start.6
  23.0 0.7 copy-start.8
  24.8 12.6 %copy-start.7 = (bf16[128,512]{1,0:T(8,128)(2,1)S(1)}, bf16[128,512]{1,0:T(8,128)(2,1)}, u32[]{:S(2)}) copy-start(bf16[128,512]{1,0:T(8,128)(2,1)} %copy-done.6) | copy-start | bytes 393220
  24.8 12.6 %copy-start.9 = (bf16[128,512]{1,0:T(8,128)(2,1)S(1)}, bf16[128,512]{1,0:T(8,128)(2,1)}, u32[]{:S(2)}) copy-start(bf16[128,512]{1,0:T(8,128)(2,1)} %copy-done.8) | copy-start | bytes 393220
  24.8 12.6 %copy-start.11 = (bf16[128,512]{1,0:T(8,128)(2,1)S(1)}, bf16[128,512]{1,0:T(8,128)(2,1)}, u32[]{:S(2)}) copy-start(bf16[128,512]{1,0:T(8,128)(2,1)} %copy-done.10) | copy-start | bytes 393220
  32.8 1.2 %copy-start = (bf16[2,768,512]{2,1,0:T(8,128)(2,1)}, bf16[2,768,512]{2,1,0:T(8,128)(2,1)S(1)}, u32[]{:S(2)}) copy-start(bf16[2,768,512]{2,1,0:T(8,128)(2,1)S(1)} %get-tuple-element.255) | copy-start | bytes 4718596
  34.0 1.2 %copy-start.3 = (bf16[2,768,512]{2,1,0:T(8,128)(2,1)}, bf16[2,768,512]{2,1,0:T(8,128)(2,1)S(1)}, u32[]{:S(2)}) copy-start(bf16[2,768,512]{2,1,0:T(8,128)(2,1)S(1)} %get-tuple-element.256) | copy-start | bytes 4718596
  35.2 2.2 %copy-start.12 = (bf16[1536,1536]{1,0:T(8,128)(2,1)}, bf16[1536,1536]{1,0:T(8,128)(2,1)S(1)}, u32[]{:S(2)}) copy-start(bf16[1536,1536]{1,0:T(8,128)(2,1)S(1)} %get-tuple-element.257.operator_ref) | copy-start | bytes 14155780
  37.5 12.6 %collective-permute-start.9 = (bf16[128,512]{1,0:T(8,128)(2,1)S(1)}, bf16[128,512]{1,0:T(8,128)(2,1)}, u32[]{:S(2)}, u32[]{:S(2)}) collective-permute-start(bf16[128,512]{1,0:T(8,128)(2,1)S(1)} %get-tuple-element.140), channel_id=1, source_target_pairs={{0,12},{1,13},{2,14},{3,15},{16,28},{17,29},{18,30},{19,31}} | collective-permute-start | bytes 393224 | tf_op jit(solution)/shard_map/cond/branch_4_fun/ppermute | solution.py:313
  47.4 2.6 %collective-permute-start.10 = (bf16[128,512]{1,0:T(8,128)(2,1)S(1)}, bf16[128,512]{1,0:T(8,128)(2,1)}, u32[]{:S(2)}, u32[]{:S(2)}) collective-permute-start(bf16[128,512]{1,0:T(8,128)(2,1)S(1)} %get-tuple-element.141), channel_id=1, source_target_pairs={{4,12},{5,13},{6,14},{7,15},{20,28},{21,29},{22,30},{23,31}} | collective-permute-start | bytes 393224 | tf_op jit(solution)/shard_map/cond/branch_4_fun/ppermute | solution.py:313
  48.8 1.3 %collective-permute-start.11 = (bf16[128,512]{1,0:T(8,128)(2,1)S(1)}, bf16[128,512]{1,0:T(8,128)(2,1)}, u32[]{:S(2)}, u32[]{:S(2)}) collective-permute-start(bf16[128,512]{1,0:T(8,128)(2,1)S(1)} %get-tuple-element.142), channel_id=1, source_target_pairs={{8,12},{9,13},{10,14},{11,15},{24,28},{25,29},{26,30},{27,31}} | collective-permute-start | bytes 393224 | tf_op jit(solution)/shard_map/cond/branch_4_fun/ppermute | solution.py:313
  50.1 7.4 %collective-permute-start.55 = (bf16[2,768,512]{2,1,0:T(8,128)(2,1)}, bf16[2,768,512]{2,1,0:T(8,128)(2,1)S(1)}, u32[]{:S(2)}, u32[]{:S(2)}) collective-permute-start(bf16[2,768,512]{2,1,0:T(8,128)(2,1)} %copy-done.3), channel_id=1, source_target_pairs={{0,1},{1,0},{2,3},{3,2},{4,5},{5,4},{6,7},{7,6},{8,9},{9,8},{10,11... | collective-permute-start | bytes 4718600 | tf_op jit(solution)/shard_map/ppermute | solution.py:306
  50.2 1.0 copy-start.5
  51.1 2.3 %copy-start.13 = (bf16[1536,1536]{1,0:T(8,128)(2,1)S(1)}, bf16[1536,1536]{1,0:T(8,128)(2,1)}, u32[]{:S(2)}) copy-start(bf16[1536,1536]{1,0:T(8,128)(2,1)} %copy-done.12) | copy-start | bytes 14155780
  53.5 4.0 %copy-start.1 = (bf16[2,768,512]{2,1,0:T(8,128)(2,1)S(1)}, bf16[2,768,512]{2,1,0:T(8,128)(2,1)}, u32[]{:S(2)}) copy-start(bf16[2,768,512]{2,1,0:T(8,128)(2,1)} %copy-done) | copy-start | bytes 4718596
  57.5 1.2 %copy-start.14 = (bf16[2,768,512]{2,1,0:T(8,128)(2,1)}, bf16[2,768,512]{2,1,0:T(8,128)(2,1)S(1)}, u32[]{:S(2)}) copy-start(bf16[2,768,512]{2,1,0:T(8,128)(2,1)S(1)} %collective-permute-done.55) | copy-start | bytes 4718596
  58.7 36.4 %collective-permute-start.46 = (bf16[768,512]{1,0:T(8,128)(2,1)S(1)}, bf16[768,512]{1,0:T(8,128)(2,1)}, u32[]{:S(2)}, u32[]{:S(2)}) collective-permute-start(bf16[768,512]{1,0:T(8,128)(2,1)S(1)} %get-tuple-element.177), channel_id=1, source_target_pairs={{0,2},{2,0},{1,3},{3,1},{4,6},{6,4},{5,7},{7,5},{8,10},{10,8},{9,1... | collective-permute-start | bytes 2359304 | tf_op jit(solution)/shard_map/cond/branch_4_fun/ppermute | solution.py:306
  60.2 12.0 %collective-permute-start.43 = (bf16[128,512]{1,0:T(8,128)(2,1)S(1)}, bf16[128,512]{1,0:T(8,128)(2,1)}, u32[]{:S(2)}, u32[]{:S(2)}) collective-permute-start(bf16[128,512]{1,0:T(8,128)(2,1)S(1)} %get-tuple-element.174), channel_id=1, source_target_pairs={{12,0},{13,1},{14,2},{15,3},{28,16},{29,17},{30,18},{31,19}} | collective-permute-start | bytes 393224 | tf_op jit(solution)/shard_map/cond/branch_4_fun/ppermute | solution.py:313
  61.5 16.4 %collective-permute-start.40 = (bf16[256,512]{1,0:T(8,128)(2,1)S(1)}, bf16[256,512]{1,0:T(8,128)(2,1)}, u32[]{:S(2)}, u32[]{:S(2)}) collective-permute-start(bf16[256,512]{1,0:T(8,128)(2,1)S(1)} %get-tuple-element.171), channel_id=1, source_target_pairs={{0,12},{4,8},{8,4},{12,0},{1,13},{5,9},{9,5},{13,1},{2,14},{6,10},... | collective-permute-start | bytes 786440 | tf_op jit(solution)/shard_map/cond/branch_4_fun/ppermute | solution.py:291
  68.4 3.8 %collective-permute-start.44 = (bf16[128,512]{1,0:T(8,128)(2,1)S(1)}, bf16[128,512]{1,0:T(8,128)(2,1)}, u32[]{:S(2)}, u32[]{:S(2)}) collective-permute-start(bf16[128,512]{1,0:T(8,128)(2,1)S(1)} %get-tuple-element.175), channel_id=1, source_target_pairs={{12,4},{13,5},{14,6},{15,7},{28,20},{29,21},{30,22},{31,23}} | collective-permute-start | bytes 393224 | tf_op jit(solution)/shard_map/cond/branch_4_fun/ppermute | solution.py:313
  69.7 25.3 %collective-permute-start.41 = (bf16[256,512]{1,0:T(8,128)(2,1)S(1)}, bf16[256,512]{1,0:T(8,128)(2,1)}, u32[]{:S(2)}, u32[]{:S(2)}) collective-permute-start(bf16[256,512]{1,0:T(8,128)(2,1)S(1)} %get-tuple-element.172), channel_id=1, source_target_pairs={{0,8},{4,12},{8,0},{12,4},{1,9},{5,13},{9,1},{13,5},{2,10},{6,14},... | collective-permute-start | bytes 786440 | tf_op jit(solution)/shard_map/cond/branch_4_fun/ppermute | solution.py:291
  72.2 22.8 %collective-permute-start.42 = (bf16[256,512]{1,0:T(8,128)(2,1)S(1)}, bf16[256,512]{1,0:T(8,128)(2,1)}, u32[]{:S(2)}, u32[]{:S(2)}) collective-permute-start(bf16[256,512]{1,0:T(8,128)(2,1)S(1)} %get-tuple-element.173), channel_id=1, source_target_pairs={{0,4},{4,0},{8,12},{12,8},{1,5},{5,1},{9,13},{13,9},{2,6},{6,2},{1... | collective-permute-start | bytes 786440 | tf_op jit(solution)/shard_map/cond/branch_4_fun/ppermute | solution.py:291
  72.2 1.3 %collective-permute-start.45 = (bf16[128,512]{1,0:T(8,128)(2,1)S(1)}, bf16[128,512]{1,0:T(8,128)(2,1)}, u32[]{:S(2)}, u32[]{:S(2)}) collective-permute-start(bf16[128,512]{1,0:T(8,128)(2,1)S(1)} %get-tuple-element.176), channel_id=1, source_target_pairs={{12,8},{13,9},{14,10},{15,11},{28,24},{29,25},{30,26},{31,27}} | collective-permute-start | bytes 393224 | tf_op jit(solution)/shard_map/cond/branch_4_fun/ppermute | solution.py:313
  95.0 2.3 %copy-start.2 = (f32[512]{0:T(512)S(1)}, f32[512]{0:T(512)}, u32[]{:S(2)}) copy-start(f32[512]{0:T(512)} %param.27) | copy-start | bytes 6148

commit v11 on v9

--- a/solution.py
+++ b/solution.py
@@ -306,8 +306,8 @@
     width = holes // HALVES
     route_row = route[0].reshape(1, rows)
     plan = (paired, chan_count, send, block_rows)
-    early = [(k, 0, width) for k in far_first if k or not paired]
-    late = [(k, h * width, width) for h in range(1, HALVES) for k in far_first if k or not paired]
+    early = [(k, 0, holes if k == 1 else width) for k in far_first if k or not paired]
+    late = [(k, h * width, width) for h in range(1, HALVES) for k in far_first if k > 1 or not paired]
     late += [(0, 0, holes)] if paired else []
     target, *blocks = pack(plan + (early,), False, route_row, amps, "pack_first")
     arrived = {(k, 0): exchange(block, k) for (k, _, _), block in zip(early, blocks)}
@@ -336,13 +336,13 @@
     terms = [chip_sum(lax.rem(lad + step, lad_count)).astype(BF16) for step in range(1, lad_count)]
     returned = []
     for half in range(HALVES):
-        blocks = [arrived[(k, half if k or not paired else 0)] for k in far_first]
+        blocks = [arrived[(k, half if k > 1 or not paired else 0)] for k in far_first]
         if returned:
             blocks, made = lax.optimization_barrier((blocks, made))
         made = apply_cycle(half, plan, operator, blocks, width)
         if not half:
-            behind, terms = lax.optimization_barrier((made[1:], terms))
-            made = [made[0], *behind]
+            behind, terms = lax.optimization_barrier((made[2:], terms))
+            made = [*made[:2], *behind]
         returned.append([exchange(block, k) for k, block in zip(far_first, made)])
     for step, term in enumerate(terms, 1):
         pairs = [(i, (i + step) % lad_count) for i in range(lad_count)]

time: 77 us -> 78.1 us (1.014)
  local copies, waits for them, and re-layouts: 1.75 us -> 4.16 us
  starting transfers between devices: 24.2 us -> 22.2 us
    ppermute x1, waiting for transfers between devices: 0.48 us -> 4.37 us  [body(): base = base + lax.ppermute(term, 'lad', pairs).astype(F32)]
    ppermute x12 -> x11, waiting for transfers between devices: 26 us -> 22.7 us  [exchange(): lax.ppermute(block, 'chan', [(i, i ^ k) for i in range(chan_count)])]
    unnamed x12 -> x16, local copies, waits for them, and re-layouts: 0.71 us -> 3.12 us
    ppermute x12 -> x11, starting transfers between devices: 22.6 us -> 20.4 us  [exchange(): lax.ppermute(block, 'chan', [(i, i ^ k) for i in range(chan_count)])]
  transfers between devices with their start and end apart: 14 -> 13, of which waited for: 6 -> 4; matrix products, arithmetic and copies ran while one was open for 6% -> 5% of each run, Pallas kernels for 23% -> 23%
where the time goes in v11:
time: 78.1 us; the launch traced here: 77.8 us
  waiting for transfers between devices  27.1 us (35%)
  starting transfers between devices  22.2 us (28%)
  Pallas kernels  21 us (27%)
  local copies, waits for them, and re-layouts  4.16 us (5%)
  other arithmetic  3.05 us (4%)
    ppermute x11, waiting for transfers between devices, exchange(): lax.ppermute(block, 'chan', [(i, i ^ k) for i in range(chan_count)])  22.7 us
    ppermute x11, starting transfers between devices, exchange(): lax.ppermute(block, 'chan', [(i, i ^ k) for i in range(chan_count)])  20.4 us
    pallas_call x1, Pallas kernels, prepare(): pl.pallas_call(functools.partial(prepare_kernel, sub_count), out_shape=[j...  7.97 us
    pallas_call x2, Pallas kernels, apply_cycle(): pl.pallas_call(functools.partial(cycle_kernel, half, plan), out_shape=[ja...  4.59 us
    ppermute x1, waiting for transfers between devices, body(): base = base + lax.ppermute(term, 'lad', pairs).astype(F32)  4.37 us
    pallas_call x2, Pallas kernels, pack(): pl.pallas_call(functools.partial(pack_kernel, plan, given), out_shape=ext...  4.34 us
    unnamed x16, local copies, waits for them, and re-layouts  3.12 us
    pallas_call x2, Pallas kernels, finish(): pl.pallas_call(functools.partial(finish_kernel, half, len(arrays), tiles)...  3.02 us
  transfers between devices with their start and end apart: 13, of which 4 were waited for; matrix products, arithmetic and copies ran while one was open for 5% of the time, Pallas kernels for 23%

profile of v11, /device:TPU:0, one launch (start us, length us, event | category | flops | bytes accessed | tf_op | source)
XLA Modules:
  0.0 77.8 jit_solution(11384116598191941617)
XLA Ops:
  0.0 2.0 %pack_first.1 = (s32[1,768]{1,0:T(1,128)S(1)}, bf16[384,256]{1,0:T(8,128)(2,1)S(1)}, bf16[384,256]{1,0:T(8,128)(2,1)S(1)}, bf16[384,512]{1,0:T(8,128)(2,1)S(1)}) custom-call(s32[1,768]{1,0:T(1,128)} %bitcast.23, bf16[768,512]{1,0:T(8,128)(2,1)} %bitcast.20), custom_call_target="tpu_custom_call" | custom-call | tf_op jit(solution)/shard_map/pack_first/pallas_call | solution.py:93
  2.0 3.1 %collective-permute-start = (bf16[384,512]{1,0:T(8,128)(2,1)S(1)}, bf16[384,512]{1,0:T(8,128)(2,1)S(1)}, u32[]{:S(2)}, u32[]{:S(2)}) collective-permute-start(bf16[384,512]{1,0:T(8,128)(2,1)S(1)} %get-tuple-element.34), channel_id=1, source_target_pairs={{0,4},{4,0},{8,12},{12,8},{1,5},{5,1},{9,13},{13,9},{2,6},{6,2},{1... | collective-permute-start | bytes 1179656 | tf_op jit(solution)/shard_map/ppermute | solution.py:302
  5.1 2.5 %collective-permute-start.2 = (bf16[384,256]{1,0:T(8,128)(2,1)S(1)}, bf16[384,256]{1,0:T(8,128)(2,1)S(1)}, u32[]{:S(2)}, u32[]{:S(2)}) collective-permute-start(bf16[384,256]{1,0:T(8,128)(2,1)S(1)} %get-tuple-element.43), channel_id=1, source_target_pairs={{0,12},{4,8},{8,4},{12,0},{1,13},{5,9},{9,5},{13,1},{2,14},{6,10},... | collective-permute-start | bytes 589832 | tf_op jit(solution)/shard_map/ppermute | solution.py:302
  7.5 0.1 collective-permute-start.3
  7.6 0.9 %copy.12.part_ref = f32[768,1]{1,0:T(8,128)S(1)} copy(f32[768,1]{0,1:T(1,128)} %bitcast.24) | data formatting | bytes 6144 | tf_op jit(solution)/shard_map/reshape;squeeze | solution.py:321
  8.5 0.1 add_multiply_fusion.off_ref
  8.6 13.9 %collective-permute-done.refs_2_ = bf16[384,512]{1,0:T(8,128)(2,1)S(1)} collective-permute-done((bf16[384,512]{1,0:T(8,128)(2,1)S(1)}, bf16[384,512]{1,0:T(8,128)(2,1)S(1)}, u32[]{:S(2)}, u32[]{:S(2)}) %collective-permute-start) | collective-permute-done | bytes 393248 | tf_op jit(solution)/shard_map/ppermute | solution.py:302
  22.5 2.4 %pack_rest.1 = (bf16[384,256]{1,0:T(8,128)(2,1)}, bf16[384,256]{1,0:T(8,128)(2,1)}, bf16[384,512]{1,0:T(8,128)(2,1)S(1)}) custom-call(s32[1,768]{1,0:T(1,128)S(1)} %get-tuple-element.35.route_in, bf16[768,512]{1,0:T(8,128)(2,1)} %bitcast.21), custom_call_target="tpu_custom_call" | custom-call | tf_op jit(solution)/shard_map/pack_rest/pallas_call | solution.py:93
  24.9 0.0 copy-start.1
  24.9 2.4 %collective-permute-start.5 = (bf16[384,256]{1,0:T(8,128)(2,1)}, bf16[384,256]{1,0:T(8,128)(2,1)}, u32[]{:S(2)}, u32[]{:S(2)}) collective-permute-start(bf16[384,256]{1,0:T(8,128)(2,1)} %get-tuple-element.36), channel_id=1, source_target_pairs={{0,12},{4,8},{8,4},{12,0},{1,13},{5,9},{9,5},{13,1},{2,14},{6,10},... | collective-permute-start | bytes 589832 | tf_op jit(solution)/shard_map/ppermute | solution.py:302
  27.4 0.0 collective-permute-start.6
  27.4 8.0 %prepare.1 = (bf16[2,768,512]{2,1,0:T(8,128)(2,1)}, bf16[2,768,512]{2,1,0:T(8,128)(2,1)S(1)}, bf16[1536,1536]{1,0:T(8,128)(2,1)S(1)}) custom-call(bf16[3072,768]{1,0:T(8,128)(2,1)} %bitcast.25, bf16[768,512]{1,0:T(8,128)(2,1)} %bitcast.22, bf16[1536,1536]{1,0:T(8,128)(2,1)} %bitcast.26, bf16[12,128,128]{2,1,0:T(8,128)(2,1)} %bitcast.27), custom_call_target="tpu_custom_call" | custom-call | flops 30000001024 | bytes 1000000 | tf_op jit(solution)/shard_map/prepare/pallas_call | solution.py:180
  35.4 0.0 copy-start.5
  35.4 0.1 collective-permute-start.1
  35.4 0.0 collective-permute-done.2.refs_0_
  35.5 0.0 collective-permute-done.3.refs_1_
  35.5 0.0 copy-done.1
  35.5 2.1 %apply_cycle.2 = (bf16[384,256]{1,0:T(8,128)(2,1)}, bf16[384,256]{1,0:T(8,128)(2,1)}, bf16[384,256]{1,0:T(8,128)(2,1)S(1)}, bf16[384,256]{1,0:T(8,128)(2,1)S(1)}) custom-call(bf16[1536,1536]{1,0:T(8,128)(2,1)S(1)} %get-tuple-element.42.operator_ref, bf16[384,256]{1,0:T(8,128)(2,1)S(1)} %collective-permute-done.2.refs_0_, ...), custom_call_target="tpu_custom_call" | custom-call | flops 30000001024 | bytes 1000000 | tf_op jit(solution)/shard_map/apply_cycle/pallas_call | solution.py:220
  37.6 0.1 copy-done.5
  37.7 0.0 copy-start.3
  37.7 0.7 copy-done.3
  38.4 1.4 %collective-permute-start.10 = (bf16[384,256]{1,0:T(8,128)(2,1)}, bf16[384,256]{1,0:T(8,128)(2,1)S(1)}, u32[]{:S(2)}, u32[]{:S(2)}) collective-permute-start(bf16[384,256]{1,0:T(8,128)(2,1)} %get-tuple-element.49), channel_id=1, source_target_pairs={{0,12},{4,8},{8,4},{12,0},{1,13},{5,9},{9,5},{13,1},{2,14},{6,10},... | collective-permute-start | bytes 589832 | tf_op jit(solution)/shard_map/ppermute | solution.py:302
  39.8 2.0 %collective-permute-start.11 = (bf16[384,256]{1,0:T(8,128)(2,1)}, bf16[384,256]{1,0:T(8,128)(2,1)S(1)}, u32[]{:S(2)}, u32[]{:S(2)}) collective-permute-start(bf16[384,256]{1,0:T(8,128)(2,1)} %get-tuple-element.50), channel_id=1, source_target_pairs={{0,8},{4,12},{8,0},{12,4},{1,9},{5,13},{9,1},{13,5},{2,10},{6,14},... | collective-permute-start | bytes 589832 | tf_op jit(solution)/shard_map/ppermute | solution.py:302
  41.8 0.2 copy.10.target_ref
  42.0 1.1 %unpack_matrix.1.pick_ref = bf16[768,1536]{1,0:T(8,128)(2,1)S(1)} custom-call(s32[4]{0:T(128)S(1)} %add_multiply_fusion.off_ref, s32[768,1]{1,0:T(8,128)S(1)} %copy.10.target_ref), custom_call_target="tpu_custom_call" | custom-call | tf_op jit(solution)/shard_map/unpack_matrix/pallas_call | solution.py:119
  43.1 0.0 copy-start.4
  43.2 0.0 copy-start.2
  43.2 0.0 collective-permute-done.1
  43.2 0.0 copy-start.7
  43.2 1.4 %fusion = bf16[768,512]{1,0:T(8,128)(2,1)S(1)} fusion(bf16[2,768,512]{2,1,0:T(8,128)(2,1)} %collective-permute-done.1, s32[]{:T(128)S(6)} %select_n.10, bf16[2,768,512]{2,1,0:T(8,128)(2,1)S(1)} %get-tuple-element.40), kind=kLoop, calls=%fused_computation.2 | loop fusion | flops 1572864 | bytes 2359300 | tf_op jit(solution)/shard_map/convert_element_type | solution.py:336
  44.6 1.7 %collective-permute-start.4 = (bf16[768,512]{1,0:T(8,128)(2,1)S(1)}, bf16[768,512]{1,0:T(8,128)(2,1)S(1)}, u32[]{:S(2)}, u32[]{:S(2)}) collective-permute-start(bf16[768,512]{1,0:T(8,128)(2,1)S(1)} %fusion), channel_id=1, source_target_pairs={{0,2},{2,0},{1,3},{3,1},{4,6},{6,4},{5,7},{7,5},{8,10},{10,8},{9,1... | collective-permute-start | bytes 2359304 | tf_op jit(solution)/shard_map/ppermute | solution.py:349
  46.4 0.0 collective-permute-done.5.refs_0_
  46.4 0.0 copy-done.4
  46.4 0.8 collective-permute-start.12
  47.1 0.0 collective-permute-done.6.refs_1_
  47.1 0.0 copy-done.2
  47.1 0.0 copy-start.6
  47.1 2.3 %copy-done.6 = bf16[1536,1536]{1,0:T(8,128)(2,1)S(1)} copy-done((bf16[1536,1536]{1,0:T(8,128)(2,1)S(1)}, bf16[1536,1536]{1,0:T(8,128)(2,1)}, u32[]{:S(2)}) %copy-start.6) | copy-done | bytes 4718616
  49.5 2.5 %apply_cycle.3 = (bf16[384,256]{1,0:T(8,128)(2,1)S(1)}, bf16[384,256]{1,0:T(8,128)(2,1)S(1)}, bf16[384,256]{1,0:T(8,128)(2,1)S(1)}, bf16[384,256]{1,0:T(8,128)(2,1)S(1)}) custom-call(bf16[1536,1536]{1,0:T(8,128)(2,1)S(1)} %copy-done.6, bf16[384,256]{1,0:T(8,128)(2,1)} %collective-permute-done.5.refs_0_, bf16[384,256]{1,0:T(8,128)(2,1)} %collective-permute-done.6.refs_1_, ...), custom_call_target="tpu_custom_call" | custom-call | flops 30000001024 | bytes 1000000 | tf_op jit(solution)/shard_map/apply_cycle/pallas_call | solution.py:220
  51.9 6.6 %collective-permute-start.7 = (bf16[384,256]{1,0:T(8,128)(2,1)S(1)}, bf16[384,256]{1,0:T(8,128)(2,1)S(1)}, u32[]{:S(2)}, u32[]{:S(2)}) collective-permute-start(bf16[384,256]{1,0:T(8,128)(2,1)S(1)} %get-tuple-element.57), channel_id=1, source_target_pairs={{0,12},{4,8},{8,4},{12,0},{1,13},{5,9},{9,5},{13,1},{2,14},{6,10},... | collective-permute-start | bytes 589832 | tf_op jit(solution)/shard_map/ppermute | solution.py:302
  58.6 0.0 collective-permute-done.10.refs_0_
  58.6 0.6 collective-permute-start.8
  59.1 4.4 %collective-permute-done.4 = bf16[768,512]{1,0:T(8,128)(2,1)S(1)} collective-permute-done((bf16[768,512]{1,0:T(8,128)(2,1)S(1)}, bf16[768,512]{1,0:T(8,128)(2,1)S(1)}, u32[]{:S(2)}, u32[]{:S(2)}) %collective-permute-start.4) | collective-permute-done | bytes 786464 | tf_op jit(solution)/shard_map/ppermute | solution.py:349
  63.5 0.0 copy-start
  63.5 0.9 %collective-permute-start.9 = (bf16[384,256]{1,0:T(8,128)(2,1)S(1)}, bf16[384,256]{1,0:T(8,128)(2,1)S(1)}, u32[]{:S(2)}, u32[]{:S(2)}) collective-permute-start(bf16[384,256]{1,0:T(8,128)(2,1)S(1)} %get-tuple-element.59), channel_id=1, source_target_pairs={{0,4},{4,0},{8,12},{12,8},{1,5},{5,1},{9,13},{13,9},{2,6},{6,2},{1... | collective-permute-start | bytes 589832 | tf_op jit(solution)/shard_map/ppermute | solution.py:302
  64.4 0.0 copy-done.7
  64.4 1.5 %bitcast_add_fusion.base_ref = f32[768,512]{1,0:T(8,128)S(1)} fusion(bf16[768,512]{1,0:T(8,128)(2,1)S(1)} %collective-permute-done.4, bf16[1,768,512]{2,1,0:T(8,128)(2,1)S(1)} %copy-done.7, bf16[2,768,512]{2,1,0:T(8,128)(2,1)} %collective-permute-done.1, s32[]{:T(128)S(6)} %select_n.9, bf16[2,768,512]{2,1,0:T(8,128)(2,1)S(1)} %get-tuple-element.40), kind=kLoop, calls=%fused_computation | loop fusion | flops 2752512 | bytes 4718596 | tf_op jit(solution)/shard_map/add | solution.py:349
  65.9 2.4 %collective-permute-done.11.refs_1_ = bf16[384,256]{1,0:T(8,128)(2,1)S(1)} collective-permute-done((bf16[384,256]{1,0:T(8,128)(2,1)}, bf16[384,256]{1,0:T(8,128)(2,1)S(1)}, u32[]{:S(2)}, u32[]{:S(2)}) %collective-permute-start.11) | collective-permute-done | bytes 196640 | tf_op jit(solution)/shard_map/ppermute | solution.py:302
  68.3 0.0 collective-permute-done.12.refs_2_
  68.3 0.0 copy-done
  68.3 1.5 %finish.2.refs_4_ = bf16[768,512]{1,0:T(8,128)(2,1)} custom-call(bf16[768,1536]{1,0:T(8,128)(2,1)S(1)} %unpack_matrix.1.pick_ref, f32[768,512]{1,0:T(8,128)S(1)} %bitcast_add_fusion.base_ref, f32[768,1]{1,0:T(8,128)S(1)} %copy.12.part_ref, f32[1,512]{1,0:T(1,128)S(1)} %bitcast.18, bf16[384,256]{1,0:T(8,128)(2,1)S(1)} %collective-permute-done.10.refs_0_, ...), custom_call_target="tpu_custom_call" | custom-call | tf_op jit(solution)/shard_map/finish/pallas_call | solution.py:261
  69.8 0.0 collective-permute-done.7.refs_0_
  69.8 6.4 %collective-permute-done.8.refs_1_ = bf16[384,256]{1,0:T(8,128)(2,1)S(1)} collective-permute-done((bf16[384,256]{1,0:T(8,128)(2,1)S(1)}, bf16[384,256]{1,0:T(8,128)(2,1)S(1)}, u32[]{:S(2)}, u32[]{:S(2)}) %collective-permute-start.8) | collective-permute-done | bytes 196640 | tf_op jit(solution)/shard_map/ppermute | solution.py:302
  76.3 0.0 collective-permute-done.9.refs_2_
  76.3 1.5 %finish.3 = bf16[768,512]{1,0:T(8,128)(2,1)} custom-call(bf16[768,1536]{1,0:T(8,128)(2,1)S(1)} %unpack_matrix.1.pick_ref, f32[768,512]{1,0:T(8,128)S(1)} %bitcast_add_fusion.base_ref, f32[768,1]{1,0:T(8,128)S(1)} %copy.12.part_ref, f32[1,512]{1,0:T(1,128)S(1)} %bitcast.19, ...), custom_call_target="tpu_custom_call", output_to_operand_aliasing={{}: (8, {})} | custom-call | tf_op jit(solution)/shard_map/finish/pallas_call | solution.py:261
Async XLA Ops:
  2.0 20.6 %collective-permute-start = (bf16[384,512]{1,0:T(8,128)(2,1)S(1)}, bf16[384,512]{1,0:T(8,128)(2,1)S(1)}, u32[]{:S(2)}, u32[]{:S(2)}) collective-permute-start(bf16[384,512]{1,0:T(8,128)(2,1)S(1)} %get-tuple-element.34), channel_id=1, source_target_pairs={{0,4},{4,0},{8,12},{12,8},{1,5},{5,1},{9,13},{13,9},{2,6},{6,2},{1... | collective-permute-start | bytes 1179656 | tf_op jit(solution)/shard_map/ppermute | solution.py:302
  5.1 30.4 %collective-permute-start.2 = (bf16[384,256]{1,0:T(8,128)(2,1)S(1)}, bf16[384,256]{1,0:T(8,128)(2,1)S(1)}, u32[]{:S(2)}, u32[]{:S(2)}) collective-permute-start(bf16[384,256]{1,0:T(8,128)(2,1)S(1)} %get-tuple-element.43), channel_id=1, source_target_pairs={{0,12},{4,8},{8,4},{12,0},{1,13},{5,9},{9,5},{13,1},{2,14},{6,10},... | collective-permute-start | bytes 589832 | tf_op jit(solution)/shard_map/ppermute | solution.py:302
  7.5 27.9 %collective-permute-start.3 = (bf16[384,256]{1,0:T(8,128)(2,1)S(1)}, bf16[384,256]{1,0:T(8,128)(2,1)S(1)}, u32[]{:S(2)}, u32[]{:S(2)}) collective-permute-start(bf16[384,256]{1,0:T(8,128)(2,1)S(1)} %get-tuple-element.44), channel_id=1, source_target_pairs={{0,8},{4,12},{8,0},{12,4},{1,9},{5,13},{9,1},{13,5},{2,10},{6,14},... | collective-permute-start | bytes 589832 | tf_op jit(solution)/shard_map/ppermute | solution.py:302
  24.9 10.5 %copy-start.1 = (bf16[384,512]{1,0:T(8,128)(2,1)}, bf16[384,512]{1,0:T(8,128)(2,1)S(1)}, u32[]{:S(2)}) copy-start(bf16[384,512]{1,0:T(8,128)(2,1)S(1)} %get-tuple-element.56.refs_3_) | copy-start | bytes 1179652
  24.9 21.4 %collective-permute-start.5 = (bf16[384,256]{1,0:T(8,128)(2,1)}, bf16[384,256]{1,0:T(8,128)(2,1)}, u32[]{:S(2)}, u32[]{:S(2)}) collective-permute-start(bf16[384,256]{1,0:T(8,128)(2,1)} %get-tuple-element.36), channel_id=1, source_target_pairs={{0,12},{4,8},{8,4},{12,0},{1,13},{5,9},{9,5},{13,1},{2,14},{6,10},... | collective-permute-start | bytes 589832 | tf_op jit(solution)/shard_map/ppermute | solution.py:302
  27.4 19.8 %collective-permute-start.6 = (bf16[384,256]{1,0:T(8,128)(2,1)}, bf16[384,256]{1,0:T(8,128)(2,1)}, u32[]{:S(2)}, u32[]{:S(2)}) collective-permute-start(bf16[384,256]{1,0:T(8,128)(2,1)} %get-tuple-element.37), channel_id=1, source_target_pairs={{0,8},{4,12},{8,0},{12,4},{1,9},{5,13},{9,1},{13,5},{2,10},{6,14},... | collective-permute-start | bytes 589832 | tf_op jit(solution)/shard_map/ppermute | solution.py:302
  35.4 2.3 %copy-start.5 = (bf16[1536,1536]{1,0:T(8,128)(2,1)}, bf16[1536,1536]{1,0:T(8,128)(2,1)S(1)}, u32[]{:S(2)}) copy-start(bf16[1536,1536]{1,0:T(8,128)(2,1)S(1)} %get-tuple-element.42.operator_ref) | copy-start | bytes 14155780
  35.4 7.8 %collective-permute-start.1 = (bf16[2,768,512]{2,1,0:T(8,128)(2,1)}, bf16[2,768,512]{2,1,0:T(8,128)(2,1)}, u32[]{:S(2)}, u32[]{:S(2)}) collective-permute-start(bf16[2,768,512]{2,1,0:T(8,128)(2,1)} %get-tuple-element.41), channel_id=1, source_target_pairs={{0,1},{1,0},{2,3},{3,2},{4,5},{5,4},{6,7},{7,6},{8,9},{9,8},{10,11... | collective-permute-start | bytes 4718600 | tf_op jit(solution)/shard_map/ppermute | solution.py:329
  37.7 0.7 copy-start.3
  38.4 20.2 %collective-permute-start.10 = (bf16[384,256]{1,0:T(8,128)(2,1)}, bf16[384,256]{1,0:T(8,128)(2,1)S(1)}, u32[]{:S(2)}, u32[]{:S(2)}) collective-permute-start(bf16[384,256]{1,0:T(8,128)(2,1)} %get-tuple-element.49), channel_id=1, source_target_pairs={{0,12},{4,8},{8,4},{12,0},{1,13},{5,9},{9,5},{13,1},{2,14},{6,10},... | collective-permute-start | bytes 589832 | tf_op jit(solution)/shard_map/ppermute | solution.py:302
  39.8 28.5 %collective-permute-start.11 = (bf16[384,256]{1,0:T(8,128)(2,1)}, bf16[384,256]{1,0:T(8,128)(2,1)S(1)}, u32[]{:S(2)}, u32[]{:S(2)}) collective-permute-start(bf16[384,256]{1,0:T(8,128)(2,1)} %get-tuple-element.50), channel_id=1, source_target_pairs={{0,8},{4,12},{8,0},{12,4},{1,9},{5,13},{9,1},{13,5},{2,10},{6,14},... | collective-permute-start | bytes 589832 | tf_op jit(solution)/shard_map/ppermute | solution.py:302
  43.1 3.2 %copy-start.4 = (bf16[384,256]{1,0:T(8,128)(2,1)S(1)}, bf16[384,256]{1,0:T(8,128)(2,1)}, u32[]{:S(2)}) copy-start(bf16[384,256]{1,0:T(8,128)(2,1)} %copy-done.3) | copy-start | bytes 589828
  43.2 4.0 %copy-start.2 = (bf16[384,512]{1,0:T(8,128)(2,1)S(1)}, bf16[384,512]{1,0:T(8,128)(2,1)}, u32[]{:S(2)}) copy-start(bf16[384,512]{1,0:T(8,128)(2,1)} %copy-done.1) | copy-start | bytes 1179652
  43.2 21.2 %copy-start.7 = (bf16[1,768,512]{2,1,0:T(8,128)(2,1)S(1)}, bf16[1,768,512]{2,1,0:T(8,128)(2,1)}, u32[]{:S(2)}) copy-start(bf16[1,768,512]{2,1,0:T(8,128)(2,1)} %param.9) | copy-start | bytes 2359300
  44.6 18.8 %collective-permute-start.4 = (bf16[768,512]{1,0:T(8,128)(2,1)S(1)}, bf16[768,512]{1,0:T(8,128)(2,1)S(1)}, u32[]{:S(2)}, u32[]{:S(2)}) collective-permute-start(bf16[768,512]{1,0:T(8,128)(2,1)S(1)} %fusion), channel_id=1, source_target_pairs={{0,2},{2,0},{1,3},{3,1},{4,6},{6,4},{5,7},{7,5},{8,10},{10,8},{9,1... | collective-permute-start | bytes 2359304 | tf_op jit(solution)/shard_map/ppermute | solution.py:349
  46.4 21.9 %collective-permute-start.12 = (bf16[384,256]{1,0:T(8,128)(2,1)S(1)}, bf16[384,256]{1,0:T(8,128)(2,1)S(1)}, u32[]{:S(2)}, u32[]{:S(2)}) collective-permute-start(bf16[384,256]{1,0:T(8,128)(2,1)S(1)} %copy-done.4), channel_id=1, source_target_pairs={{0,4},{4,0},{8,12},{12,8},{1,5},{5,1},{9,13},{13,9},{2,6},{6,2},{1... | collective-permute-start | bytes 589832 | tf_op jit(solution)/shard_map/ppermute | solution.py:302
  47.1 2.3 %copy-start.6 = (bf16[1536,1536]{1,0:T(8,128)(2,1)S(1)}, bf16[1536,1536]{1,0:T(8,128)(2,1)}, u32[]{:S(2)}) copy-start(bf16[1536,1536]{1,0:T(8,128)(2,1)} %copy-done.5) | copy-start | bytes 14155780
  51.9 17.9 %collective-permute-start.7 = (bf16[384,256]{1,0:T(8,128)(2,1)S(1)}, bf16[384,256]{1,0:T(8,128)(2,1)S(1)}, u32[]{:S(2)}, u32[]{:S(2)}) collective-permute-start(bf16[384,256]{1,0:T(8,128)(2,1)S(1)} %get-tuple-element.57), channel_id=1, source_target_pairs={{0,12},{4,8},{8,4},{12,0},{1,13},{5,9},{9,5},{13,1},{2,14},{6,10},... | collective-permute-start | bytes 589832 | tf_op jit(solution)/shard_map/ppermute | solution.py:302
  58.6 17.7 %collective-permute-start.8 = (bf16[384,256]{1,0:T(8,128)(2,1)S(1)}, bf16[384,256]{1,0:T(8,128)(2,1)S(1)}, u32[]{:S(2)}, u32[]{:S(2)}) collective-permute-start(bf16[384,256]{1,0:T(8,128)(2,1)S(1)} %get-tuple-element.58), channel_id=1, source_target_pairs={{0,8},{4,12},{8,0},{12,4},{1,9},{5,13},{9,1},{13,5},{2,10},{6,14},... | collective-permute-start | bytes 589832 | tf_op jit(solution)/shard_map/ppermute | solution.py:302
  63.5 4.8 %copy-start = (f32[512]{0:T(512)S(1)}, f32[512]{0:T(512)}, u32[]{:S(2)}) copy-start(f32[512]{0:T(512)} %param.15) | copy-start | bytes 6148
  63.5 12.8 %collective-permute-start.9 = (bf16[384,256]{1,0:T(8,128)(2,1)S(1)}, bf16[384,256]{1,0:T(8,128)(2,1)S(1)}, u32[]{:S(2)}, u32[]{:S(2)}) collective-permute-start(bf16[384,256]{1,0:T(8,128)(2,1)S(1)} %get-tuple-element.59), channel_id=1, source_target_pairs={{0,4},{4,0},{8,12},{12,8},{1,5},{5,1},{9,13},{13,9},{2,6},{6,2},{1... | collective-permute-start | bytes 589832 | tf_op jit(solution)/shard_map/ppermute | solution.py:302

commit v12 on v11

--- a/solution.py
+++ b/solution.py
@@ -8,7 +8,6 @@
 from jax.sharding import PartitionSpec as P
 
 VMEM_LIMIT = 28 * 1024 * 1024
-HALVES = 2
 F32 = jnp.float32
 BF16 = jnp.bfloat16
 CHEAP = pl.CostEstimate(flops=0, bytes_accessed=0, transcendentals=0)
@@ -199,7 +198,7 @@
     return outs[:sub_count], outs[sub_count]
 
 
-def cycle_kernel(half, plan, operator_ref, *refs):
+def cycle_kernel(start_column, plan, operator_ref, *refs):
     paired, chan_count, _, _ = plan
     count = len(refs) // 2
     in_refs, out_refs, block_ref = refs[:count], refs[count : 2 * count], refs[2 * count]
@@ -207,7 +206,7 @@
     offsets = block_offsets(paired, chan_count, block_rows)
     starts = [pl.multiple_of(offsets[count - 1 - i], block_rows) for i in range(count)]
     for in_ref, start in zip(in_refs, starts):
-        part = in_ref[...] if in_ref.shape[1] == width else in_ref[:, pl.ds(half * width, width)]
+        part = in_ref[...] if in_ref.shape[1] == width else in_ref[:, pl.ds(start_column, width)]
         block_ref[pl.ds(start, block_rows), :] = part
     for out_ref, start in zip(out_refs, starts):
         out_ref[...] = jnp.dot(
@@ -215,10 +214,11 @@
         ).astype(BF16)
 
 
-def apply_cycle(half, plan, operator, arrays, width):
+def apply_cycle(part, plan, operator, arrays):
+    start_column, width = part
     block_rows = arrays[0].shape[0]
     return pl.pallas_call(
-        functools.partial(cycle_kernel, half, plan),
+        functools.partial(cycle_kernel, start_column, plan),
         out_shape=[jax.ShapeDtypeStruct((block_rows, width), BF16)] * len(arrays),
         in_specs=[whole()] * (1 + len(arrays)),
         out_specs=[whole()] * len(arrays),
@@ -229,11 +229,11 @@
     )(operator, *arrays)
 
 
-def finish_kernel(half, count, tiles, pick_ref, base_ref, part_ref, hole_ref, *refs):
+def finish_kernel(start_column, count, tiles, pick_ref, base_ref, part_ref, hole_ref, *refs):
     in_refs, (out_hbm, block_ref, out_ref, sems) = refs[:count], refs[-4:]
     block_rows, width = in_refs[0].shape
     tile = out_ref.shape[0] // tiles
-    columns = pl.ds(half * width, width)
+    columns = pl.ds(start_column, width)
     for i, in_ref in enumerate(in_refs):
         block_ref[pl.ds((count - 1 - i) * block_rows, block_rows), :] = in_ref[...]
     copies = []
@@ -248,9 +248,9 @@
         copy.wait()
 
 
-def finish(half, pick, base, part_column, hole_row, arrays, earlier):
+def finish(part, pick, base, part_column, hole_row, arrays, earlier):
     rows, holes = base.shape
-    tiles, width = 3, holes // HALVES
+    tiles, (start_column, width) = 3, part
     operands = [pick, base, part_column, hole_row, *arrays]
     in_specs = [whole()] * len(operands)
     aliases = {}
@@ -259,7 +259,7 @@
         operands.append(earlier)
         in_specs.append(whole(pl.ANY))
     return pl.pallas_call(
-        functools.partial(finish_kernel, half, len(arrays), tiles),
+        functools.partial(finish_kernel, start_column, len(arrays), tiles),
         out_shape=jax.ShapeDtypeStruct((rows, holes), BF16),
         in_specs=in_specs,
         out_specs=whole(pl.ANY),
@@ -303,23 +303,25 @@
 
     far_first = list(reversed(range(block_index.shape[0])))
     count = len(far_first)
-    width = holes // HALVES
+    wide = holes * 3 // 512 * 128
+    columns = [(0, wide), (wide, holes - wide)] if paired else [(0, holes)]
     route_row = route[0].reshape(1, rows)
     plan = (paired, chan_count, send, block_rows)
-    early = [(k, 0, holes if k == 1 else width) for k in far_first if k or not paired]
-    late = [(k, h * width, width) for h in range(1, HALVES) for k in far_first if k > 1 or not paired]
-    late += [(0, 0, holes)] if paired else []
+    early = [(k, *columns[0]) for k in far_first if k or not paired]
+    late = [(k, *part) for part in columns[1:] for k in far_first if k] + ([(0, 0, holes)] if paired else [])
     target, *blocks = pack(plan + (early,), False, route_row, amps, "pack_first")
-    arrived = {(k, 0): exchange(block, k) for (k, _, _), block in zip(early, blocks)}
+    arrived = {(k, start): exchange(block, k) for (k, start, _), block in zip(early, blocks)}
     if paired:
         near = (1, 0)
         target, arrived[near] = lax.optimization_barrier((target, arrived[near]))
-    blocks = pack(plan + (late,), True, target, amps, "pack_rest")
-    for (k, first, _), block in zip(late, blocks):
-        arrived[(k, first // width)] = exchange(block, k)
+    blocks = []
+    if late:
+        blocks = pack(plan + (late,), True, target, amps, "pack_rest")
+        for (k, start, _), block in zip(late, blocks):
+            arrived[(k, start)] = exchange(block, k)
+        amps, blocks = lax.optimization_barrier((amps, blocks))
 
     part_column, hole_row = gap_part[0].reshape(rows, 1), gap_hole.reshape(1, holes)
-    amps, blocks = lax.optimization_barrier((amps, blocks))
     pick = unpack_matrix(offsets, target.reshape(rows, 1), capacity)
 
     parts, operator = prepare(ladder_weight[0], amps, weight, mixing, lad_count, sub_count)
@@ -335,12 +337,12 @@
     base = driving[0].astype(F32) + chip_sum(lad)
     terms = [chip_sum(lax.rem(lad + step, lad_count)).astype(BF16) for step in range(1, lad_count)]
     returned = []
-    for half in range(HALVES):
-        blocks = [arrived[(k, half if k > 1 or not paired else 0)] for k in far_first]
+    for part in columns:
+        blocks = [arrived[(k, part[0] if k or not paired else 0)] for k in far_first]
         if returned:
             blocks, made = lax.optimization_barrier((blocks, made))
-        made = apply_cycle(half, plan, operator, blocks, width)
-        if not half:
+        made = apply_cycle(part, plan, operator, blocks)
+        if not returned:
             behind, terms = lax.optimization_barrier((made[2:], terms))
             made = [*made[:2], *behind]
         returned.append([exchange(block, k) for k, block in zip(far_first, made)])
@@ -348,8 +350,8 @@
         pairs = [(i, (i + step) % lad_count) for i in range(lad_count)]
         base = base + lax.ppermute(term, "lad", pairs).astype(F32)
     updated = None
-    for half in range(HALVES):
-        updated = finish(half, pick, base, part_column, hole_row, returned[half], updated)
+    for part, arrays in zip(columns, returned):
+        updated = finish(part, pick, base, part_column, hole_row, arrays, updated)
     return updated[None]
 
 

time: 78.1 us -> 79.5 us (1.018)
  waiting for transfers between devices: 27.1 us -> 20.9 us
  starting transfers between devices: 22.2 us -> 26.8 us
  Pallas kernels: 21 us -> 23.3 us
    ppermute x11 -> x12, waiting for transfers between devices: 22.7 us -> 15.2 us  [exchange(): lax.ppermute(block, 'chan', [(i, i ^ k) for i in range(chan_count)])]
    ppermute x11 -> x12, starting transfers between devices: 20.4 us -> 25.2 us  [exchange(): lax.ppermute(block, 'chan', [(i, i ^ k) for i in range(chan_count)])]
    pallas_call x4, Pallas kernels: 7.61 us -> 9.53 us  [the longest x2 5.97 us: apply_cycle(): pl.pallas_call(functools.partial(cycle_kernel, start_column, plan), out_s...]
    ppermute x1, waiting for transfers between devices: 4.37 us -> 5.68 us  [body(): base = base + lax.ppermute(term, 'lad', pairs).astype(F32)]
  transfers between devices with their start and end apart: 13 -> 14, of which waited for: 4 -> 4; matrix products, arithmetic and copies ran while one was open for 5% -> 5% of each run, Pallas kernels for 23% -> 25%
where the time goes in v12:
time: 79.5 us; the launch traced here: 79.2 us
  starting transfers between devices  26.8 us (34%)
  Pallas kernels  23.3 us (29%)
  waiting for transfers between devices  20.9 us (26%)
  local copies, waits for them, and re-layouts  4.87 us (6%)
  other arithmetic  3.02 us (4%)
    ppermute x12, starting transfers between devices, exchange(): lax.ppermute(block, 'chan', [(i, i ^ k) for i in range(chan_count)])  25.2 us
    ppermute x12, waiting for transfers between devices, exchange(): lax.ppermute(block, 'chan', [(i, i ^ k) for i in range(chan_count)])  15.2 us
    pallas_call x1, Pallas kernels, prepare(): pl.pallas_call(functools.partial(prepare_kernel, sub_count), out_shape=[j...  7.96 us
    pallas_call x2, Pallas kernels, apply_cycle(): pl.pallas_call(functools.partial(cycle_kernel, start_column, plan), out_s...  5.97 us
    ppermute x1, waiting for transfers between devices, body(): base = base + lax.ppermute(term, 'lad', pairs).astype(F32)  5.68 us
    pallas_call x2, Pallas kernels, pack(): pl.pallas_call(functools.partial(pack_kernel, plan, given), out_shape=ext...  4.75 us
    unnamed x16, local copies, waits for them, and re-layouts  3.83 us
    pallas_call x2, Pallas kernels, finish(): pl.pallas_call(functools.partial(finish_kernel, start_column, len(arrays)...  3.56 us
  transfers between devices with their start and end apart: 14, of which 4 were waited for; matrix products, arithmetic and copies ran while one was open for 5% of the time, Pallas kernels for 25%

profile of v12, /device:TPU:0, one launch (start us, length us, event | category | flops | bytes accessed | tf_op | source)
XLA Modules:
  0.0 79.2 jit_solution(10610517467810732164)
XLA Ops:
  0.0 2.3 %pack_first.1 = (s32[1,768]{1,0:T(1,128)S(1)}, bf16[384,384]{1,0:T(8,128)(2,1)}, bf16[384,384]{1,0:T(8,128)(2,1)S(1)}, bf16[384,384]{1,0:T(8,128)(2,1)S(1)}) custom-call(s32[1,768]{1,0:T(1,128)} %bitcast.23, bf16[768,512]{1,0:T(8,128)(2,1)} %bitcast.20), custom_call_target="tpu_custom_call" | custom-call | tf_op jit(solution)/shard_map/pack_first/pallas_call | solution.py:92
  2.3 3.1 %collective-permute-start = (bf16[384,384]{1,0:T(8,128)(2,1)S(1)}, bf16[384,384]{1,0:T(8,128)(2,1)S(1)}, u32[]{:S(2)}, u32[]{:S(2)}) collective-permute-start(bf16[384,384]{1,0:T(8,128)(2,1)S(1)} %get-tuple-element.35), channel_id=1, source_target_pairs={{0,4},{4,0},{8,12},{12,8},{1,5},{5,1},{9,13},{13,9},{2,6},{6,2},{1... | collective-permute-start | bytes 884744 | tf_op jit(solution)/shard_map/ppermute | solution.py:302
  5.4 2.5 %collective-permute-start.2 = (bf16[384,384]{1,0:T(8,128)(2,1)}, bf16[384,384]{1,0:T(8,128)(2,1)S(1)}, u32[]{:S(2)}, u32[]{:S(2)}) collective-permute-start(bf16[384,384]{1,0:T(8,128)(2,1)} %get-tuple-element.45), channel_id=1, source_target_pairs={{0,12},{4,8},{8,4},{12,0},{1,13},{5,9},{9,5},{13,1},{2,14},{6,10},... | collective-permute-start | bytes 884744 | tf_op jit(solution)/shard_map/ppermute | solution.py:302
  7.9 0.1 collective-permute-start.3
  8.0 0.9 %copy.12.part_ref = f32[768,1]{1,0:T(8,128)S(1)} copy(f32[768,1]{0,1:T(1,128)} %bitcast.24) | data formatting | bytes 6144 | tf_op jit(solution)/shard_map/reshape;squeeze | solution.py:324
  8.8 0.1 add_multiply_fusion.off_ref
  8.9 3.9 %collective-permute-done.refs_2_ = bf16[384,384]{1,0:T(8,128)(2,1)S(1)} collective-permute-done((bf16[384,384]{1,0:T(8,128)(2,1)S(1)}, bf16[384,384]{1,0:T(8,128)(2,1)S(1)}, u32[]{:S(2)}, u32[]{:S(2)}) %collective-permute-start) | collective-permute-done | bytes 294944 | tf_op jit(solution)/shard_map/ppermute | solution.py:302
  12.8 2.5 %pack_rest.1 = (bf16[384,128]{1,0:T(8,128)(2,1)}, bf16[384,128]{1,0:T(8,128)(2,1)}, bf16[384,128]{1,0:T(8,128)(2,1)}, bf16[384,512]{1,0:T(8,128)(2,1)S(1)}) custom-call(s32[1,768]{1,0:T(1,128)S(1)} %get-tuple-element.36.route_in, bf16[768,512]{1,0:T(8,128)(2,1)} %bitcast.21), custom_call_target="tpu_custom_call" | custom-call | tf_op jit(solution)/shard_map/pack_rest/pallas_call | solution.py:92
  15.3 8.7 %collective-permute-start.5 = (bf16[384,128]{1,0:T(8,128)(2,1)}, bf16[384,128]{1,0:T(8,128)(2,1)S(1)}, u32[]{:S(2)}, u32[]{:S(2)}) collective-permute-start(bf16[384,128]{1,0:T(8,128)(2,1)} %get-tuple-element.37), channel_id=1, source_target_pairs={{0,12},{4,8},{8,4},{12,0},{1,13},{5,9},{9,5},{13,1},{2,14},{6,10},... | collective-permute-start | bytes 294920 | tf_op jit(solution)/shard_map/ppermute | solution.py:302
  24.0 0.0 collective-permute-start.6
  24.0 0.6 collective-permute-start.7
  24.6 8.0 %prepare.1 = (bf16[2,768,512]{2,1,0:T(8,128)(2,1)}, bf16[2,768,512]{2,1,0:T(8,128)(2,1)S(1)}, bf16[1536,1536]{1,0:T(8,128)(2,1)S(1)}) custom-call(bf16[3072,768]{1,0:T(8,128)(2,1)} %bitcast.25, bf16[768,512]{1,0:T(8,128)(2,1)} %bitcast.22, bf16[1536,1536]{1,0:T(8,128)(2,1)} %bitcast.26, bf16[12,128,128]{2,1,0:T(8,128)(2,1)} %bitcast.27), custom_call_target="tpu_custom_call" | custom-call | flops 30000001024 | bytes 1000000 | tf_op jit(solution)/shard_map/prepare/pallas_call | solution.py:179
  32.6 0.0 copy-start.5
  32.6 0.0 collective-permute-done.2.refs_0_
  32.6 0.1 collective-permute-start.1
  32.7 6.6 %collective-permute-done.3.refs_1_ = bf16[384,384]{1,0:T(8,128)(2,1)} collective-permute-done((bf16[384,384]{1,0:T(8,128)(2,1)S(1)}, bf16[384,384]{1,0:T(8,128)(2,1)}, u32[]{:S(2)}, u32[]{:S(2)}) %collective-permute-start.3) | collective-permute-done | bytes 294944 | tf_op jit(solution)/shard_map/ppermute | solution.py:302
  39.3 3.7 %apply_cycle.2 = (bf16[384,384]{1,0:T(8,128)(2,1)}, bf16[384,384]{1,0:T(8,128)(2,1)S(1)}, bf16[384,384]{1,0:T(8,128)(2,1)S(1)}, bf16[384,384]{1,0:T(8,128)(2,1)S(1)}) custom-call(bf16[1536,1536]{1,0:T(8,128)(2,1)S(1)} %get-tuple-element.44.operator_ref, bf16[384,384]{1,0:T(8,128)(2,1)S(1)} %collective-permute-done.2.refs_0_, ...), custom_call_target="tpu_custom_call" | custom-call | flops 30000001024 | bytes 1000000 | tf_op jit(solution)/shard_map/apply_cycle/pallas_call | solution.py:220
  43.0 0.0 copy-done.5
  43.0 0.0 copy-start.1
  43.0 0.7 copy-done.1
  43.8 0.0 copy-start.3
  43.8 0.7 copy-done.3
  44.5 3.0 %collective-permute-start.11 = (bf16[384,384]{1,0:T(8,128)(2,1)}, bf16[384,384]{1,0:T(8,128)(2,1)S(1)}, u32[]{:S(2)}, u32[]{:S(2)}) collective-permute-start(bf16[384,384]{1,0:T(8,128)(2,1)} %get-tuple-element.51), channel_id=1, source_target_pairs={{0,12},{4,8},{8,4},{12,0},{1,13},{5,9},{9,5},{13,1},{2,14},{6,10},... | collective-permute-start | bytes 884744 | tf_op jit(solution)/shard_map/ppermute | solution.py:302
  47.4 0.2 copy.10.target_ref
  47.6 0.0 copy-start.4
  47.6 1.1 %unpack_matrix.1.pick_ref = bf16[768,1536]{1,0:T(8,128)(2,1)S(1)} custom-call(s32[4]{0:T(128)S(1)} %add_multiply_fusion.off_ref, s32[768,1]{1,0:T(8,128)S(1)} %copy.10.target_ref), custom_call_target="tpu_custom_call" | custom-call | tf_op jit(solution)/shard_map/unpack_matrix/pallas_call | solution.py:118
  48.8 0.0 copy-start.2
  48.8 0.0 collective-permute-done.1
  48.8 0.0 copy-done.4
  48.8 0.1 collective-permute-start.12
  48.9 0.0 copy-start.7
  48.9 1.4 %fusion = bf16[768,512]{1,0:T(8,128)(2,1)S(1)} fusion(bf16[2,768,512]{2,1,0:T(8,128)(2,1)} %collective-permute-done.1, s32[]{:T(128)S(6)} %select_n.10, bf16[2,768,512]{2,1,0:T(8,128)(2,1)S(1)} %get-tuple-element.42), kind=kLoop, calls=%fused_computation.2 | loop fusion | flops 1572864 | bytes 2359300 | tf_op jit(solution)/shard_map/convert_element_type | solution.py:338
  50.3 0.0 collective-permute-done.5.refs_0_
  50.3 1.6 %collective-permute-start.4 = (bf16[768,512]{1,0:T(8,128)(2,1)S(1)}, bf16[768,512]{1,0:T(8,128)(2,1)S(1)}, u32[]{:S(2)}, u32[]{:S(2)}) collective-permute-start(bf16[768,512]{1,0:T(8,128)(2,1)S(1)} %fusion), channel_id=1, source_target_pairs={{0,2},{2,0},{1,3},{3,1},{4,6},{6,4},{5,7},{7,5},{8,10},{10,8},{9,1... | collective-permute-start | bytes 2359304 | tf_op jit(solution)/shard_map/ppermute | solution.py:351
  51.9 0.0 collective-permute-done.6.refs_1_
  51.9 0.0 copy-done.2
  51.9 1.4 %collective-permute-start.13 = (bf16[384,384]{1,0:T(8,128)(2,1)S(1)}, bf16[384,384]{1,0:T(8,128)(2,1)S(1)}, u32[]{:S(2)}, u32[]{:S(2)}) collective-permute-start(bf16[384,384]{1,0:T(8,128)(2,1)S(1)} %copy-done.2), channel_id=1, source_target_pairs={{0,4},{4,0},{8,12},{12,8},{1,5},{5,1},{9,13},{13,9},{2,6},{6,2},{1... | collective-permute-start | bytes 884744 | tf_op jit(solution)/shard_map/ppermute | solution.py:302
  53.3 0.0 collective-permute-done.7.refs_2_
  53.3 0.0 copy-start.6
  53.3 2.3 %copy-done.6 = bf16[1536,1536]{1,0:T(8,128)(2,1)S(1)} copy-done((bf16[1536,1536]{1,0:T(8,128)(2,1)S(1)}, bf16[1536,1536]{1,0:T(8,128)(2,1)}, u32[]{:S(2)}) %copy-start.6) | copy-done | bytes 4718616
  55.6 2.3 %apply_cycle.3 = (bf16[384,128]{1,0:T(8,128)(2,1)S(1)}, bf16[384,128]{1,0:T(8,128)(2,1)S(1)}, bf16[384,128]{1,0:T(8,128)(2,1)S(1)}, bf16[384,128]{1,0:T(8,128)(2,1)S(1)}) custom-call(bf16[1536,1536]{1,0:T(8,128)(2,1)S(1)} %copy-done.6, bf16[384,128]{1,0:T(8,128)(2,1)S(1)} %collective-permute-done.5.refs_0_, ...), custom_call_target="tpu_custom_call" | custom-call | flops 30000001024 | bytes 1000000 | tf_op jit(solution)/shard_map/apply_cycle/pallas_call | solution.py:220
  57.9 0.7 collective-permute-start.10
  58.6 0.0 collective-permute-done.11.refs_0_
  58.6 2.4 %collective-permute-start.8 = (bf16[384,128]{1,0:T(8,128)(2,1)S(1)}, bf16[384,128]{1,0:T(8,128)(2,1)S(1)}, u32[]{:S(2)}, u32[]{:S(2)}) collective-permute-start(bf16[384,128]{1,0:T(8,128)(2,1)S(1)} %get-tuple-element.59), channel_id=1, source_target_pairs={{0,12},{4,8},{8,4},{12,0},{1,13},{5,9},{9,5},{13,1},{2,14},{6,10},... | collective-permute-start | bytes 294920 | tf_op jit(solution)/shard_map/ppermute | solution.py:302
  61.0 5.7 %collective-permute-done.4 = bf16[768,512]{1,0:T(8,128)(2,1)S(1)} collective-permute-done((bf16[768,512]{1,0:T(8,128)(2,1)S(1)}, bf16[768,512]{1,0:T(8,128)(2,1)S(1)}, u32[]{:S(2)}, u32[]{:S(2)}) %collective-permute-start.4) | collective-permute-done | bytes 786464 | tf_op jit(solution)/shard_map/ppermute | solution.py:351
  66.7 0.0 copy-start
  66.7 2.6 %collective-permute-start.9 = (bf16[384,128]{1,0:T(8,128)(2,1)S(1)}, bf16[384,128]{1,0:T(8,128)(2,1)S(1)}, u32[]{:S(2)}, u32[]{:S(2)}) collective-permute-start(bf16[384,128]{1,0:T(8,128)(2,1)S(1)} %get-tuple-element.60), channel_id=1, source_target_pairs={{0,8},{4,12},{8,0},{12,4},{1,9},{5,13},{9,1},{13,5},{2,10},{6,14},... | collective-permute-start | bytes 294920 | tf_op jit(solution)/shard_map/ppermute | solution.py:302
  69.4 0.0 copy-done.7
  69.4 1.5 %bitcast_add_fusion.base_ref = f32[768,512]{1,0:T(8,128)S(1)} fusion(bf16[768,512]{1,0:T(8,128)(2,1)S(1)} %collective-permute-done.4, bf16[1,768,512]{2,1,0:T(8,128)(2,1)S(1)} %copy-done.7, bf16[2,768,512]{2,1,0:T(8,128)(2,1)} %collective-permute-done.1, s32[]{:T(128)S(6)} %select_n.9, bf16[2,768,512]{2,1,0:T(8,128)(2,1)S(1)} %get-tuple-element.42), kind=kLoop, calls=%fused_computation | loop fusion | flops 2752512 | bytes 4718596 | tf_op jit(solution)/shard_map/add | solution.py:351
  70.9 4.7 %collective-permute-done.12.refs_1_ = bf16[384,384]{1,0:T(8,128)(2,1)S(1)} collective-permute-done((bf16[384,384]{1,0:T(8,128)(2,1)S(1)}, bf16[384,384]{1,0:T(8,128)(2,1)S(1)}, u32[]{:S(2)}, u32[]{:S(2)}) %collective-permute-start.12) | collective-permute-done | bytes 294944 | tf_op jit(solution)/shard_map/ppermute | solution.py:302
  75.6 0.0 collective-permute-done.13.refs_2_
  75.6 0.0 copy-done
  75.6 2.1 %finish.2.refs_4_ = bf16[768,512]{1,0:T(8,128)(2,1)} custom-call(bf16[768,1536]{1,0:T(8,128)(2,1)S(1)} %unpack_matrix.1.pick_ref, f32[768,512]{1,0:T(8,128)S(1)} %bitcast_add_fusion.base_ref, f32[768,1]{1,0:T(8,128)S(1)} %copy.12.part_ref, f32[1,512]{1,0:T(1,128)S(1)} %bitcast.18, bf16[384,384]{1,0:T(8,128)(2,1)S(1)} %collective-permute-done.11.refs_0_, ...), custom_call_target="tpu_custom_call" | custom-call | tf_op jit(solution)/shard_map/finish/pallas_call | solution.py:261
  77.7 0.0 collective-permute-done.10.refs_2_
  77.7 0.0 collective-permute-done.8.refs_0_
  77.7 0.0 collective-permute-done.9.refs_1_
  77.7 1.5 %finish.3 = bf16[768,512]{1,0:T(8,128)(2,1)} custom-call(bf16[768,1536]{1,0:T(8,128)(2,1)S(1)} %unpack_matrix.1.pick_ref, f32[768,512]{1,0:T(8,128)S(1)} %bitcast_add_fusion.base_ref, f32[768,1]{1,0:T(8,128)S(1)} %copy.12.part_ref, f32[1,512]{1,0:T(1,128)S(1)} %bitcast.19, ...), custom_call_target="tpu_custom_call", output_to_operand_aliasing={{}: (8, {})} | custom-call | tf_op jit(solution)/shard_map/finish/pallas_call | solution.py:261
Async XLA Ops:
  2.3 10.5 %collective-permute-start = (bf16[384,384]{1,0:T(8,128)(2,1)S(1)}, bf16[384,384]{1,0:T(8,128)(2,1)S(1)}, u32[]{:S(2)}, u32[]{:S(2)}) collective-permute-start(bf16[384,384]{1,0:T(8,128)(2,1)S(1)} %get-tuple-element.35), channel_id=1, source_target_pairs={{0,4},{4,0},{8,12},{12,8},{1,5},{5,1},{9,13},{13,9},{2,6},{6,2},{1... | collective-permute-start | bytes 884744 | tf_op jit(solution)/shard_map/ppermute | solution.py:302
  5.4 27.2 %collective-permute-start.2 = (bf16[384,384]{1,0:T(8,128)(2,1)}, bf16[384,384]{1,0:T(8,128)(2,1)S(1)}, u32[]{:S(2)}, u32[]{:S(2)}) collective-permute-start(bf16[384,384]{1,0:T(8,128)(2,1)} %get-tuple-element.45), channel_id=1, source_target_pairs={{0,12},{4,8},{8,4},{12,0},{1,13},{5,9},{9,5},{13,1},{2,14},{6,10},... | collective-permute-start | bytes 884744 | tf_op jit(solution)/shard_map/ppermute | solution.py:302
  7.9 31.5 %collective-permute-start.3 = (bf16[384,384]{1,0:T(8,128)(2,1)S(1)}, bf16[384,384]{1,0:T(8,128)(2,1)}, u32[]{:S(2)}, u32[]{:S(2)}) collective-permute-start(bf16[384,384]{1,0:T(8,128)(2,1)S(1)} %get-tuple-element.46), channel_id=1, source_target_pairs={{0,8},{4,12},{8,0},{12,4},{1,9},{5,13},{9,1},{13,5},{2,10},{6,14},... | collective-permute-start | bytes 884744 | tf_op jit(solution)/shard_map/ppermute | solution.py:302
  15.3 35.0 %collective-permute-start.5 = (bf16[384,128]{1,0:T(8,128)(2,1)}, bf16[384,128]{1,0:T(8,128)(2,1)S(1)}, u32[]{:S(2)}, u32[]{:S(2)}) collective-permute-start(bf16[384,128]{1,0:T(8,128)(2,1)} %get-tuple-element.37), channel_id=1, source_target_pairs={{0,12},{4,8},{8,4},{12,0},{1,13},{5,9},{9,5},{13,1},{2,14},{6,10},... | collective-permute-start | bytes 294920 | tf_op jit(solution)/shard_map/ppermute | solution.py:302
  24.0 27.9 %collective-permute-start.6 = (bf16[384,128]{1,0:T(8,128)(2,1)}, bf16[384,128]{1,0:T(8,128)(2,1)S(1)}, u32[]{:S(2)}, u32[]{:S(2)}) collective-permute-start(bf16[384,128]{1,0:T(8,128)(2,1)} %get-tuple-element.38), channel_id=1, source_target_pairs={{0,8},{4,12},{8,0},{12,4},{1,9},{5,13},{9,1},{13,5},{2,10},{6,14},... | collective-permute-start | bytes 294920 | tf_op jit(solution)/shard_map/ppermute | solution.py:302
  24.0 29.3 %collective-permute-start.7 = (bf16[384,128]{1,0:T(8,128)(2,1)}, bf16[384,128]{1,0:T(8,128)(2,1)}, u32[]{:S(2)}, u32[]{:S(2)}) collective-permute-start(bf16[384,128]{1,0:T(8,128)(2,1)} %get-tuple-element.39), channel_id=1, source_target_pairs={{0,4},{4,0},{8,12},{12,8},{1,5},{5,1},{9,13},{13,9},{2,6},{6,2},{1... | collective-permute-start | bytes 294920 | tf_op jit(solution)/shard_map/ppermute | solution.py:302
  32.6 10.4 %copy-start.5 = (bf16[1536,1536]{1,0:T(8,128)(2,1)}, bf16[1536,1536]{1,0:T(8,128)(2,1)S(1)}, u32[]{:S(2)}) copy-start(bf16[1536,1536]{1,0:T(8,128)(2,1)S(1)} %get-tuple-element.44.operator_ref) | copy-start | bytes 14155780
  32.6 16.2 %collective-permute-start.1 = (bf16[2,768,512]{2,1,0:T(8,128)(2,1)}, bf16[2,768,512]{2,1,0:T(8,128)(2,1)}, u32[]{:S(2)}, u32[]{:S(2)}) collective-permute-start(bf16[2,768,512]{2,1,0:T(8,128)(2,1)} %get-tuple-element.43), channel_id=1, source_target_pairs={{0,1},{1,0},{2,3},{3,2},{4,5},{5,4},{6,7},{7,6},{8,9},{9,8},{10,11... | collective-permute-start | bytes 4718600 | tf_op jit(solution)/shard_map/ppermute | solution.py:331
  43.0 0.7 copy-start.1
  43.8 0.7 copy-start.3
  44.5 14.1 %collective-permute-start.11 = (bf16[384,384]{1,0:T(8,128)(2,1)}, bf16[384,384]{1,0:T(8,128)(2,1)S(1)}, u32[]{:S(2)}, u32[]{:S(2)}) collective-permute-start(bf16[384,384]{1,0:T(8,128)(2,1)} %get-tuple-element.51), channel_id=1, source_target_pairs={{0,12},{4,8},{8,4},{12,0},{1,13},{5,9},{9,5},{13,1},{2,14},{6,10},... | collective-permute-start | bytes 884744 | tf_op jit(solution)/shard_map/ppermute | solution.py:302
  47.6 1.1 %copy-start.4 = (bf16[384,384]{1,0:T(8,128)(2,1)S(1)}, bf16[384,384]{1,0:T(8,128)(2,1)}, u32[]{:S(2)}) copy-start(bf16[384,384]{1,0:T(8,128)(2,1)} %copy-done.3) | copy-start | bytes 884740
  48.8 3.1 %copy-start.2 = (bf16[384,384]{1,0:T(8,128)(2,1)S(1)}, bf16[384,384]{1,0:T(8,128)(2,1)}, u32[]{:S(2)}) copy-start(bf16[384,384]{1,0:T(8,128)(2,1)} %copy-done.1) | copy-start | bytes 884740
  48.8 26.8 %collective-permute-start.12 = (bf16[384,384]{1,0:T(8,128)(2,1)S(1)}, bf16[384,384]{1,0:T(8,128)(2,1)S(1)}, u32[]{:S(2)}, u32[]{:S(2)}) collective-permute-start(bf16[384,384]{1,0:T(8,128)(2,1)S(1)} %copy-done.4), channel_id=1, source_target_pairs={{0,8},{4,12},{8,0},{12,4},{1,9},{5,13},{9,1},{13,5},{2,10},{6,14},... | collective-permute-start | bytes 884744 | tf_op jit(solution)/shard_map/ppermute | solution.py:302
  48.9 20.5 %copy-start.7 = (bf16[1,768,512]{2,1,0:T(8,128)(2,1)S(1)}, bf16[1,768,512]{2,1,0:T(8,128)(2,1)}, u32[]{:S(2)}) copy-start(bf16[1,768,512]{2,1,0:T(8,128)(2,1)} %param.9) | copy-start | bytes 2359300
  50.3 16.4 %collective-permute-start.4 = (bf16[768,512]{1,0:T(8,128)(2,1)S(1)}, bf16[768,512]{1,0:T(8,128)(2,1)S(1)}, u32[]{:S(2)}, u32[]{:S(2)}) collective-permute-start(bf16[768,512]{1,0:T(8,128)(2,1)S(1)} %fusion), channel_id=1, source_target_pairs={{0,2},{2,0},{1,3},{3,1},{4,6},{6,4},{5,7},{7,5},{8,10},{10,8},{9,1... | collective-permute-start | bytes 2359304 | tf_op jit(solution)/shard_map/ppermute | solution.py:351
  51.9 23.7 %collective-permute-start.13 = (bf16[384,384]{1,0:T(8,128)(2,1)S(1)}, bf16[384,384]{1,0:T(8,128)(2,1)S(1)}, u32[]{:S(2)}, u32[]{:S(2)}) collective-permute-start(bf16[384,384]{1,0:T(8,128)(2,1)S(1)} %copy-done.2), channel_id=1, source_target_pairs={{0,4},{4,0},{8,12},{12,8},{1,5},{5,1},{9,13},{13,9},{2,6},{6,2},{1... | collective-permute-start | bytes 884744 | tf_op jit(solution)/shard_map/ppermute | solution.py:302
  53.3 2.3 %copy-start.6 = (bf16[1536,1536]{1,0:T(8,128)(2,1)S(1)}, bf16[1536,1536]{1,0:T(8,128)(2,1)}, u32[]{:S(2)}) copy-start(bf16[1536,1536]{1,0:T(8,128)(2,1)} %copy-done.5) | copy-start | bytes 14155780
  57.9 19.7 %collective-permute-start.10 = (bf16[384,128]{1,0:T(8,128)(2,1)S(1)}, bf16[384,128]{1,0:T(8,128)(2,1)S(1)}, u32[]{:S(2)}, u32[]{:S(2)}) collective-permute-start(bf16[384,128]{1,0:T(8,128)(2,1)S(1)} %get-tuple-element.61), channel_id=1, source_target_pairs={{0,4},{4,0},{8,12},{12,8},{1,5},{5,1},{9,13},{13,9},{2,6},{6,2},{1... | collective-permute-start | bytes 294920 | tf_op jit(solution)/shard_map/ppermute | solution.py:302
  58.6 19.1 %collective-permute-start.8 = (bf16[384,128]{1,0:T(8,128)(2,1)S(1)}, bf16[384,128]{1,0:T(8,128)(2,1)S(1)}, u32[]{:S(2)}, u32[]{:S(2)}) collective-permute-start(bf16[384,128]{1,0:T(8,128)(2,1)S(1)} %get-tuple-element.59), channel_id=1, source_target_pairs={{0,12},{4,8},{8,4},{12,0},{1,13},{5,9},{9,5},{13,1},{2,14},{6,10},... | collective-permute-start | bytes 294920 | tf_op jit(solution)/shard_map/ppermute | solution.py:302
  66.7 8.8 %copy-start = (f32[512]{0:T(512)S(1)}, f32[512]{0:T(512)}, u32[]{:S(2)}) copy-start(f32[512]{0:T(512)} %param.15) | copy-start | bytes 6148
  66.7 11.0 %collective-permute-start.9 = (bf16[384,128]{1,0:T(8,128)(2,1)S(1)}, bf16[384,128]{1,0:T(8,128)(2,1)S(1)}, u32[]{:S(2)}, u32[]{:S(2)}) collective-permute-start(bf16[384,128]{1,0:T(8,128)(2,1)S(1)} %get-tuple-element.60), channel_id=1, source_target_pairs={{0,8},{4,12},{8,0},{12,4},{1,9},{5,13},{9,1},{13,5},{2,10},{6,14},... | collective-permute-start | bytes 294920 | tf_op jit(solution)/shard_map/ppermute | solution.py:302

commit v13 on v9

--- a/solution.py
+++ b/solution.py
@@ -320,7 +320,6 @@
 
     part_column, hole_row = gap_part[0].reshape(rows, 1), gap_hole.reshape(1, holes)
     amps, blocks = lax.optimization_barrier((amps, blocks))
-    pick = unpack_matrix(offsets, target.reshape(rows, 1), capacity)
 
     parts, operator = prepare(ladder_weight[0], amps, weight, mixing, lad_count, sub_count)
     kept = [parts[-1]]
@@ -341,12 +340,14 @@
             blocks, made = lax.optimization_barrier((blocks, made))
         made = apply_cycle(half, plan, operator, blocks, width)
         if not half:
-            behind, terms = lax.optimization_barrier((made[1:], terms))
-            made = [made[0], *behind]
+            behind, terms = lax.optimization_barrier((made[2:], terms))
+            made = [*made[:2], *behind]
         returned.append([exchange(block, k) for k, block in zip(far_first, made)])
     for step, term in enumerate(terms, 1):
         pairs = [(i, (i + step) % lad_count) for i in range(lad_count)]
         base = base + lax.ppermute(term, "lad", pairs).astype(F32)
+    target, made = lax.optimization_barrier((target, made))
+    pick = unpack_matrix(offsets, target.reshape(rows, 1), capacity)
     updated = None
     for half in range(HALVES):
         updated = finish(half, pick, base, part_column, hole_row, returned[half], updated)

time: 77 us -> 80.6 us (1.047)
  waiting for transfers between devices: 26.5 us -> 34.4 us
  starting transfers between devices: 24.2 us -> 22.1 us
  Pallas kernels: 20.8 us -> 19.1 us
    ppermute x1, waiting for transfers between devices: 0.48 us -> 7.96 us  [body(): base = base + lax.ppermute(term, 'lad', pairs).astype(F32)]
    ppermute x12, starting transfers between devices: 22.6 us -> 20.5 us  [exchange(): lax.ppermute(block, 'chan', [(i, i ^ k) for i in range(chan_count)])]
    pallas_call x2, Pallas kernels: 4.49 us -> 3.22 us  [apply_cycle(): pl.pallas_call(functools.partial(cycle_kernel, half, plan), out_shape=[ja...]
  transfers between devices with their start and end apart: 14 -> 14, of which waited for: 6 -> 5; matrix products, arithmetic and copies ran while one was open for 6% -> 5% of each run, Pallas kernels for 23% -> 20%
where the time goes in v13:
time: 80.6 us; the launch traced here: 80.4 us
  waiting for transfers between devices  34.4 us (43%)
  starting transfers between devices  22.1 us (27%)
  Pallas kernels  19.1 us (24%)
  other arithmetic  2.89 us (4%)
  local copies, waits for them, and re-layouts  1.76 us (2%)
    ppermute x12, waiting for transfers between devices, exchange(): lax.ppermute(block, 'chan', [(i, i ^ k) for i in range(chan_count)])  26.4 us
    ppermute x12, starting transfers between devices, exchange(): lax.ppermute(block, 'chan', [(i, i ^ k) for i in range(chan_count)])  20.5 us
    ppermute x1, waiting for transfers between devices, body(): base = base + lax.ppermute(term, 'lad', pairs).astype(F32)  7.96 us
    pallas_call x1, Pallas kernels, prepare(): pl.pallas_call(functools.partial(prepare_kernel, sub_count), out_shape=[j...  7.96 us
    pallas_call x2, Pallas kernels, pack(): pl.pallas_call(functools.partial(pack_kernel, plan, given), out_shape=ext...  3.75 us
    pallas_call x2, Pallas kernels, apply_cycle(): pl.pallas_call(functools.partial(cycle_kernel, half, plan), out_shape=[ja...  3.22 us
    pallas_call x2, Pallas kernels, finish(): pl.pallas_call(functools.partial(finish_kernel, half, len(arrays), tiles)...  3.04 us
  transfers between devices with their start and end apart: 14, of which 5 were waited for; matrix products, arithmetic and copies ran while one was open for 5% of the time, Pallas kernels for 20%

profile of v13, /device:TPU:0, one launch (start us, length us, event | category | flops | bytes accessed | tf_op | source)
XLA Modules:
  0.0 80.4 jit_solution(6677167194304524027)
XLA Ops:
  0.0 1.7 %pack_first.1 = (s32[1,768]{1,0:T(1,128)S(1)}, bf16[384,256]{1,0:T(8,128)(2,1)S(1)}, bf16[384,256]{1,0:T(8,128)(2,1)S(1)}, bf16[384,256]{1,0:T(8,128)(2,1)S(1)}) custom-call(s32[1,768]{1,0:T(1,128)} %bitcast.23, bf16[768,512]{1,0:T(8,128)(2,1)} %bitcast.20), custom_call_target="tpu_custom_call" | custom-call | tf_op jit(solution)/shard_map/pack_first/pallas_call | solution.py:93
  1.7 3.1 %collective-permute-start = (bf16[384,256]{1,0:T(8,128)(2,1)S(1)}, bf16[384,256]{1,0:T(8,128)(2,1)S(1)}, u32[]{:S(2)}, u32[]{:S(2)}) collective-permute-start(bf16[384,256]{1,0:T(8,128)(2,1)S(1)} %get-tuple-element.36), channel_id=1, source_target_pairs={{0,4},{4,0},{8,12},{12,8},{1,5},{5,1},{9,13},{13,9},{2,6},{6,2},{1... | collective-permute-start | bytes 589832 | tf_op jit(solution)/shard_map/ppermute | solution.py:302
  4.8 2.5 %collective-permute-start.4 = (bf16[384,256]{1,0:T(8,128)(2,1)S(1)}, bf16[384,256]{1,0:T(8,128)(2,1)S(1)}, u32[]{:S(2)}, u32[]{:S(2)}) collective-permute-start(bf16[384,256]{1,0:T(8,128)(2,1)S(1)} %get-tuple-element.44), channel_id=1, source_target_pairs={{0,12},{4,8},{8,4},{12,0},{1,13},{5,9},{9,5},{13,1},{2,14},{6,10},... | collective-permute-start | bytes 589832 | tf_op jit(solution)/shard_map/ppermute | solution.py:302
  7.2 0.1 collective-permute-start.5
  7.4 0.9 %copy.12.part_ref = f32[768,1]{1,0:T(8,128)S(1)} copy(f32[768,1]{0,1:T(1,128)} %bitcast.24) | data formatting | bytes 6144 | tf_op jit(solution)/shard_map/reshape;squeeze | solution.py:321
  8.2 0.1 add_multiply_fusion.off_ref
  8.3 1.8 %collective-permute-done.refs_2_ = bf16[384,256]{1,0:T(8,128)(2,1)S(1)} collective-permute-done((bf16[384,256]{1,0:T(8,128)(2,1)S(1)}, bf16[384,256]{1,0:T(8,128)(2,1)S(1)}, u32[]{:S(2)}, u32[]{:S(2)}) %collective-permute-start) | collective-permute-done | bytes 196640 | tf_op jit(solution)/shard_map/ppermute | solution.py:302
  10.1 2.1 %pack_rest.1 = (bf16[384,256]{1,0:T(8,128)(2,1)S(1)}, bf16[384,256]{1,0:T(8,128)(2,1)S(1)}, bf16[384,256]{1,0:T(8,128)(2,1)S(1)}, bf16[384,512]{1,0:T(8,128)(2,1)S(1)}) custom-call(s32[1,768]{1,0:T(1,128)S(1)} %get-tuple-element.63.route_in, bf16[768,512]{1,0:T(8,128)(2,1)} %bitcast.21), custom_call_target="tpu_custom_call" | custom-call | tf_op jit(solution)/shard_map/pack_rest/pallas_call | solution.py:93
  12.2 6.8 %collective-permute-start.1 = (bf16[384,256]{1,0:T(8,128)(2,1)S(1)}, bf16[384,256]{1,0:T(8,128)(2,1)S(1)}, u32[]{:S(2)}, u32[]{:S(2)}) collective-permute-start(bf16[384,256]{1,0:T(8,128)(2,1)S(1)} %get-tuple-element.38), channel_id=1, source_target_pairs={{0,12},{4,8},{8,4},{12,0},{1,13},{5,9},{9,5},{13,1},{2,14},{6,10},... | collective-permute-start | bytes 589832 | tf_op jit(solution)/shard_map/ppermute | solution.py:302
  18.9 0.0 collective-permute-start.2
  18.9 0.6 collective-permute-start.3
  19.6 8.0 %prepare.1 = (bf16[2,768,512]{2,1,0:T(8,128)(2,1)S(1)}, bf16[2,768,512]{2,1,0:T(8,128)(2,1)S(1)}, bf16[1536,1536]{1,0:T(8,128)(2,1)S(1)}) custom-call(bf16[3072,768]{1,0:T(8,128)(2,1)} %bitcast.25, bf16[768,512]{1,0:T(8,128)(2,1)} %bitcast.22, bf16[1536,1536]{1,0:T(8,128)(2,1)} %bitcast.26, bf16[12,128,128]{2,1,0:T(8,128)(2,1)} %bitcast.27), custom_call_target="tpu_custom_call" | custom-call | flops 30000001024 | bytes 1000000 | tf_op jit(solution)/shard_map/prepare/pallas_call | solution.py:180
  27.5 0.0 collective-permute-done.4.refs_0_
  27.6 0.1 collective-permute-start.6
  27.6 6.6 %collective-permute-done.5.refs_1_ = bf16[384,256]{1,0:T(8,128)(2,1)S(1)} collective-permute-done((bf16[384,256]{1,0:T(8,128)(2,1)S(1)}, bf16[384,256]{1,0:T(8,128)(2,1)S(1)}, u32[]{:S(2)}, u32[]{:S(2)}) %collective-permute-start.5) | collective-permute-done | bytes 196640 | tf_op jit(solution)/shard_map/ppermute | solution.py:302
  34.2 1.6 %apply_cycle.2 = (bf16[384,256]{1,0:T(8,128)(2,1)}, bf16[384,256]{1,0:T(8,128)(2,1)}, bf16[384,256]{1,0:T(8,128)(2,1)S(1)}, bf16[384,256]{1,0:T(8,128)(2,1)S(1)}) custom-call(bf16[1536,1536]{1,0:T(8,128)(2,1)S(1)} %get-tuple-element.43.operator_ref, bf16[384,256]{1,0:T(8,128)(2,1)S(1)} %collective-permute-done.4.refs_0_, ...), custom_call_target="tpu_custom_call" | custom-call | flops 30000001024 | bytes 1000000 | tf_op jit(solution)/shard_map/apply_cycle/pallas_call | solution.py:220
  35.8 0.0 copy-start.1
  35.8 3.0 %collective-permute-start.11 = (bf16[384,256]{1,0:T(8,128)(2,1)}, bf16[384,256]{1,0:T(8,128)(2,1)S(1)}, u32[]{:S(2)}, u32[]{:S(2)}) collective-permute-start(bf16[384,256]{1,0:T(8,128)(2,1)} %get-tuple-element.47), channel_id=1, source_target_pairs={{0,12},{4,8},{8,4},{12,0},{1,13},{5,9},{9,5},{13,1},{2,14},{6,10},... | collective-permute-start | bytes 589832 | tf_op jit(solution)/shard_map/ppermute | solution.py:302
  38.8 0.0 collective-permute-done.6
  38.8 0.0 copy-start.5
  38.8 0.0 collective-permute-start.12
  38.8 1.3 %fusion = bf16[768,512]{1,0:T(8,128)(2,1)} fusion(bf16[2,768,512]{2,1,0:T(8,128)(2,1)S(1)} %collective-permute-done.6, s32[]{:T(128)S(6)} %select_n.9, bf16[2,768,512]{2,1,0:T(8,128)(2,1)S(1)} %get-tuple-element.51), kind=kLoop, calls=%fused_computation.2 | loop fusion | flops 1572864 | bytes 2359300 | tf_op jit(solution)/shard_map/convert_element_type | solution.py:335
  40.1 0.0 collective-permute-done.1.refs_0_
  40.1 11.0 %collective-permute-done.2.refs_1_ = bf16[384,256]{1,0:T(8,128)(2,1)S(1)} collective-permute-done((bf16[384,256]{1,0:T(8,128)(2,1)S(1)}, bf16[384,256]{1,0:T(8,128)(2,1)S(1)}, u32[]{:S(2)}, u32[]{:S(2)}) %collective-permute-start.2) | collective-permute-done | bytes 196640 | tf_op jit(solution)/shard_map/ppermute | solution.py:302
  51.0 0.0 collective-permute-done.3.refs_2_
  51.0 1.5 %collective-permute-start.7 = (bf16[768,512]{1,0:T(8,128)(2,1)}, bf16[768,512]{1,0:T(8,128)(2,1)}, u32[]{:S(2)}, u32[]{:S(2)}) collective-permute-start(bf16[768,512]{1,0:T(8,128)(2,1)} %fusion), channel_id=1, source_target_pairs={{0,2},{2,0},{1,3},{3,1},{4,6},{6,4},{5,7},{7,5},{8,10},{10,8},{9,1... | collective-permute-start | bytes 2359304 | tf_op jit(solution)/shard_map/ppermute | solution.py:348
  52.5 1.6 %apply_cycle.3 = (bf16[384,256]{1,0:T(8,128)(2,1)}, bf16[384,256]{1,0:T(8,128)(2,1)}, bf16[384,256]{1,0:T(8,128)(2,1)S(1)}, bf16[384,256]{1,0:T(8,128)(2,1)S(1)}) custom-call(bf16[1536,1536]{1,0:T(8,128)(2,1)S(1)} %get-tuple-element.43.operator_ref, bf16[384,256]{1,0:T(8,128)(2,1)S(1)} %collective-permute-done.1.refs_0_, ...), custom_call_target="tpu_custom_call" | custom-call | flops 30000001024 | bytes 1000000 | tf_op jit(solution)/shard_map/apply_cycle/pallas_call | solution.py:220
  54.1 0.0 copy-done.1
  54.1 0.0 copy-done.5
  54.1 0.0 copy-start.3
  54.1 0.7 copy-done.3
  54.8 3.0 %collective-permute-start.8 = (bf16[384,256]{1,0:T(8,128)(2,1)}, bf16[384,256]{1,0:T(8,128)(2,1)S(1)}, u32[]{:S(2)}, u32[]{:S(2)}) collective-permute-start(bf16[384,256]{1,0:T(8,128)(2,1)} %get-tuple-element.59), channel_id=1, source_target_pairs={{0,12},{4,8},{8,4},{12,0},{1,13},{5,9},{9,5},{13,1},{2,14},{6,10},... | collective-permute-start | bytes 589832 | tf_op jit(solution)/shard_map/ppermute | solution.py:302
  57.8 0.0 collective-permute-start.9
  57.8 0.2 copy.10.target_ref
  58.0 0.0 copy-start.4
  58.0 0.0 copy-start.2
  58.0 0.0 copy-start.6
  58.0 0.0 copy-start.7
  58.0 1.1 %unpack_matrix.1.pick_ref = bf16[768,1536]{1,0:T(8,128)(2,1)S(1)} custom-call(s32[4]{0:T(128)S(1)} %add_multiply_fusion.off_ref, s32[768,1]{1,0:T(8,128)S(1)} %copy.10.target_ref), custom_call_target="tpu_custom_call" | custom-call | tf_op jit(solution)/shard_map/unpack_matrix/pallas_call | solution.py:119
  59.1 0.0 copy-start
  59.2 0.0 collective-permute-done.11.refs_0_
  59.2 0.0 copy-done.4
  59.2 1.5 %collective-permute-start.10 = (bf16[384,256]{1,0:T(8,128)(2,1)S(1)}, bf16[384,256]{1,0:T(8,128)(2,1)S(1)}, u32[]{:S(2)}, u32[]{:S(2)}) collective-permute-start(bf16[384,256]{1,0:T(8,128)(2,1)S(1)} %copy-done.4), channel_id=1, source_target_pairs={{0,4},{4,0},{8,12},{12,8},{1,5},{5,1},{9,13},{13,9},{2,6},{6,2},{1... | collective-permute-start | bytes 589832 | tf_op jit(solution)/shard_map/ppermute | solution.py:302
  60.7 8.0 %collective-permute-done.7 = bf16[768,512]{1,0:T(8,128)(2,1)} collective-permute-done((bf16[768,512]{1,0:T(8,128)(2,1)}, bf16[768,512]{1,0:T(8,128)(2,1)}, u32[]{:S(2)}, u32[]{:S(2)}) %collective-permute-start.7) | collective-permute-done | bytes 786464 | tf_op jit(solution)/shard_map/ppermute | solution.py:348
  68.6 0.0 copy-done.2
  68.6 0.0 collective-permute-start.13
  68.6 0.0 copy-done.6
  68.6 0.0 copy-done.7
  68.6 1.5 %bitcast_add_fusion.base_ref = f32[768,512]{1,0:T(8,128)S(1)} fusion(bf16[768,512]{1,0:T(8,128)(2,1)} %collective-permute-done.7, bf16[1,768,512]{2,1,0:T(8,128)(2,1)S(1)} %copy-done.7, bf16[2,768,512]{2,1,0:T(8,128)(2,1)S(1)} %copy-done.6, s32[]{:T(128)S(6)} %select_n.10, bf16[2,768,512]{2,1,0:T(8,128)(2,1)S(1)} %get-tuple-element.51), kind=kLoop, calls=%fused_computation | loop fusion | flops 2752512 | bytes 4718596 | tf_op jit(solution)/shard_map/add | solution.py:348
  70.2 0.0 collective-permute-done.12.refs_1_
  70.2 7.1 %collective-permute-done.13.refs_2_ = bf16[384,256]{1,0:T(8,128)(2,1)S(1)} collective-permute-done((bf16[384,256]{1,0:T(8,128)(2,1)S(1)}, bf16[384,256]{1,0:T(8,128)(2,1)S(1)}, u32[]{:S(2)}, u32[]{:S(2)}) %collective-permute-start.13) | collective-permute-done | bytes 196640 | tf_op jit(solution)/shard_map/ppermute | solution.py:302
  77.3 0.0 copy-done
  77.3 1.5 %finish.2.refs_4_ = bf16[768,512]{1,0:T(8,128)(2,1)} custom-call(bf16[768,1536]{1,0:T(8,128)(2,1)S(1)} %unpack_matrix.1.pick_ref, f32[768,512]{1,0:T(8,128)S(1)} %bitcast_add_fusion.base_ref, f32[768,1]{1,0:T(8,128)S(1)} %copy.12.part_ref, f32[1,512]{1,0:T(1,128)S(1)} %bitcast.18, bf16[384,256]{1,0:T(8,128)(2,1)S(1)} %collective-permute-done.11.refs_0_, ...), custom_call_target="tpu_custom_call" | custom-call | tf_op jit(solution)/shard_map/finish/pallas_call | solution.py:261
  78.8 0.0 collective-permute-done.8.refs_0_
  78.8 0.0 collective-permute-done.9.refs_1_
  78.8 0.0 collective-permute-done.10.refs_2_
  78.8 1.5 %finish.3 = bf16[768,512]{1,0:T(8,128)(2,1)} custom-call(bf16[768,1536]{1,0:T(8,128)(2,1)S(1)} %unpack_matrix.1.pick_ref, f32[768,512]{1,0:T(8,128)S(1)} %bitcast_add_fusion.base_ref, f32[768,1]{1,0:T(8,128)S(1)} %copy.12.part_ref, f32[1,512]{1,0:T(1,128)S(1)} %bitcast.19, ...), custom_call_target="tpu_custom_call", output_to_operand_aliasing={{}: (8, {})} | custom-call | tf_op jit(solution)/shard_map/finish/pallas_call | solution.py:261
Async XLA Ops:
  1.7 8.4 %collective-permute-start = (bf16[384,256]{1,0:T(8,128)(2,1)S(1)}, bf16[384,256]{1,0:T(8,128)(2,1)S(1)}, u32[]{:S(2)}, u32[]{:S(2)}) collective-permute-start(bf16[384,256]{1,0:T(8,128)(2,1)S(1)} %get-tuple-element.36), channel_id=1, source_target_pairs={{0,4},{4,0},{8,12},{12,8},{1,5},{5,1},{9,13},{13,9},{2,6},{6,2},{1... | collective-permute-start | bytes 589832 | tf_op jit(solution)/shard_map/ppermute | solution.py:302
  4.8 22.8 %collective-permute-start.4 = (bf16[384,256]{1,0:T(8,128)(2,1)S(1)}, bf16[384,256]{1,0:T(8,128)(2,1)S(1)}, u32[]{:S(2)}, u32[]{:S(2)}) collective-permute-start(bf16[384,256]{1,0:T(8,128)(2,1)S(1)} %get-tuple-element.44), channel_id=1, source_target_pairs={{0,12},{4,8},{8,4},{12,0},{1,13},{5,9},{9,5},{13,1},{2,14},{6,10},... | collective-permute-start | bytes 589832 | tf_op jit(solution)/shard_map/ppermute | solution.py:302
  7.2 26.9 %collective-permute-start.5 = (bf16[384,256]{1,0:T(8,128)(2,1)S(1)}, bf16[384,256]{1,0:T(8,128)(2,1)S(1)}, u32[]{:S(2)}, u32[]{:S(2)}) collective-permute-start(bf16[384,256]{1,0:T(8,128)(2,1)S(1)} %get-tuple-element.45), channel_id=1, source_target_pairs={{0,8},{4,12},{8,0},{12,4},{1,9},{5,13},{9,1},{13,5},{2,10},{6,14},... | collective-permute-start | bytes 589832 | tf_op jit(solution)/shard_map/ppermute | solution.py:302
  12.2 27.9 %collective-permute-start.1 = (bf16[384,256]{1,0:T(8,128)(2,1)S(1)}, bf16[384,256]{1,0:T(8,128)(2,1)S(1)}, u32[]{:S(2)}, u32[]{:S(2)}) collective-permute-start(bf16[384,256]{1,0:T(8,128)(2,1)S(1)} %get-tuple-element.38), channel_id=1, source_target_pairs={{0,12},{4,8},{8,4},{12,0},{1,13},{5,9},{9,5},{13,1},{2,14},{6,10},... | collective-permute-start | bytes 589832 | tf_op jit(solution)/shard_map/ppermute | solution.py:302
  18.9 32.1 %collective-permute-start.2 = (bf16[384,256]{1,0:T(8,128)(2,1)S(1)}, bf16[384,256]{1,0:T(8,128)(2,1)S(1)}, u32[]{:S(2)}, u32[]{:S(2)}) collective-permute-start(bf16[384,256]{1,0:T(8,128)(2,1)S(1)} %get-tuple-element.39), channel_id=1, source_target_pairs={{0,8},{4,12},{8,0},{12,4},{1,9},{5,13},{9,1},{13,5},{2,10},{6,14},... | collective-permute-start | bytes 589832 | tf_op jit(solution)/shard_map/ppermute | solution.py:302
  18.9 32.1 %collective-permute-start.3 = (bf16[384,256]{1,0:T(8,128)(2,1)S(1)}, bf16[384,256]{1,0:T(8,128)(2,1)S(1)}, u32[]{:S(2)}, u32[]{:S(2)}) collective-permute-start(bf16[384,256]{1,0:T(8,128)(2,1)S(1)} %get-tuple-element.40), channel_id=1, source_target_pairs={{0,4},{4,0},{8,12},{12,8},{1,5},{5,1},{9,13},{13,9},{2,6},{6,2},{1... | collective-permute-start | bytes 589832 | tf_op jit(solution)/shard_map/ppermute | solution.py:302
  27.6 11.2 %collective-permute-start.6 = (bf16[2,768,512]{2,1,0:T(8,128)(2,1)S(1)}, bf16[2,768,512]{2,1,0:T(8,128)(2,1)S(1)}, u32[]{:S(2)}, u32[]{:S(2)}) collective-permute-start(bf16[2,768,512]{2,1,0:T(8,128)(2,1)S(1)} %get-tuple-element.52), channel_id=1, source_target_pairs={{0,1},{1,0},{2,3},{3,2},{4,5},{5,4},{6,7},{7,6},{8,9},{9,8},{10,11... | collective-permute-start | bytes 4718600 | tf_op jit(solution)/shard_map/ppermute | solution.py:328
  35.8 18.3 %copy-start.1 = (bf16[384,256]{1,0:T(8,128)(2,1)}, bf16[384,256]{1,0:T(8,128)(2,1)S(1)}, u32[]{:S(2)}) copy-start(bf16[384,256]{1,0:T(8,128)(2,1)S(1)} %get-tuple-element.53) | copy-start | bytes 589828
  35.8 23.4 %collective-permute-start.11 = (bf16[384,256]{1,0:T(8,128)(2,1)}, bf16[384,256]{1,0:T(8,128)(2,1)S(1)}, u32[]{:S(2)}, u32[]{:S(2)}) collective-permute-start(bf16[384,256]{1,0:T(8,128)(2,1)} %get-tuple-element.47), channel_id=1, source_target_pairs={{0,12},{4,8},{8,4},{12,0},{1,13},{5,9},{9,5},{13,1},{2,14},{6,10},... | collective-permute-start | bytes 589832 | tf_op jit(solution)/shard_map/ppermute | solution.py:302
  38.8 15.4 %copy-start.5 = (bf16[2,768,512]{2,1,0:T(8,128)(2,1)}, bf16[2,768,512]{2,1,0:T(8,128)(2,1)S(1)}, u32[]{:S(2)}) copy-start(bf16[2,768,512]{2,1,0:T(8,128)(2,1)S(1)} %collective-permute-done.6) | copy-start | bytes 4718596
  38.8 31.4 %collective-permute-start.12 = (bf16[384,256]{1,0:T(8,128)(2,1)}, bf16[384,256]{1,0:T(8,128)(2,1)S(1)}, u32[]{:S(2)}, u32[]{:S(2)}) collective-permute-start(bf16[384,256]{1,0:T(8,128)(2,1)} %get-tuple-element.48), channel_id=1, source_target_pairs={{0,8},{4,12},{8,0},{12,4},{1,9},{5,13},{9,1},{13,5},{2,10},{6,14},... | collective-permute-start | bytes 589832 | tf_op jit(solution)/shard_map/ppermute | solution.py:302
  51.0 17.6 %collective-permute-start.7 = (bf16[768,512]{1,0:T(8,128)(2,1)}, bf16[768,512]{1,0:T(8,128)(2,1)}, u32[]{:S(2)}, u32[]{:S(2)}) collective-permute-start(bf16[768,512]{1,0:T(8,128)(2,1)} %fusion), channel_id=1, source_target_pairs={{0,2},{2,0},{1,3},{3,1},{4,6},{6,4},{5,7},{7,5},{8,10},{10,8},{9,1... | collective-permute-start | bytes 2359304 | tf_op jit(solution)/shard_map/ppermute | solution.py:348
  54.1 0.7 copy-start.3
  54.8 24.0 %collective-permute-start.8 = (bf16[384,256]{1,0:T(8,128)(2,1)}, bf16[384,256]{1,0:T(8,128)(2,1)S(1)}, u32[]{:S(2)}, u32[]{:S(2)}) collective-permute-start(bf16[384,256]{1,0:T(8,128)(2,1)} %get-tuple-element.59), channel_id=1, source_target_pairs={{0,12},{4,8},{8,4},{12,0},{1,13},{5,9},{9,5},{13,1},{2,14},{6,10},... | collective-permute-start | bytes 589832 | tf_op jit(solution)/shard_map/ppermute | solution.py:302
  57.8 21.0 %collective-permute-start.9 = (bf16[384,256]{1,0:T(8,128)(2,1)}, bf16[384,256]{1,0:T(8,128)(2,1)S(1)}, u32[]{:S(2)}, u32[]{:S(2)}) collective-permute-start(bf16[384,256]{1,0:T(8,128)(2,1)} %get-tuple-element.60), channel_id=1, source_target_pairs={{0,8},{4,12},{8,0},{12,4},{1,9},{5,13},{9,1},{13,5},{2,10},{6,14},... | collective-permute-start | bytes 589832 | tf_op jit(solution)/shard_map/ppermute | solution.py:302
  58.0 1.2 %copy-start.4 = (bf16[384,256]{1,0:T(8,128)(2,1)S(1)}, bf16[384,256]{1,0:T(8,128)(2,1)}, u32[]{:S(2)}) copy-start(bf16[384,256]{1,0:T(8,128)(2,1)} %copy-done.3) | copy-start | bytes 589828
  58.0 10.6 %copy-start.2 = (bf16[384,256]{1,0:T(8,128)(2,1)S(1)}, bf16[384,256]{1,0:T(8,128)(2,1)}, u32[]{:S(2)}) copy-start(bf16[384,256]{1,0:T(8,128)(2,1)} %copy-done.1) | copy-start | bytes 589828
  58.0 10.6 %copy-start.6 = (bf16[2,768,512]{2,1,0:T(8,128)(2,1)S(1)}, bf16[2,768,512]{2,1,0:T(8,128)(2,1)}, u32[]{:S(2)}) copy-start(bf16[2,768,512]{2,1,0:T(8,128)(2,1)} %copy-done.5) | copy-start | bytes 4718596
  58.0 10.6 %copy-start.7 = (bf16[1,768,512]{2,1,0:T(8,128)(2,1)S(1)}, bf16[1,768,512]{2,1,0:T(8,128)(2,1)}, u32[]{:S(2)}) copy-start(bf16[1,768,512]{2,1,0:T(8,128)(2,1)} %param.9) | copy-start | bytes 2359300
  59.1 18.1 %copy-start = (f32[512]{0:T(512)S(1)}, f32[512]{0:T(512)}, u32[]{:S(2)}) copy-start(f32[512]{0:T(512)} %param.15) | copy-start | bytes 6148
  59.2 19.7 %collective-permute-start.10 = (bf16[384,256]{1,0:T(8,128)(2,1)S(1)}, bf16[384,256]{1,0:T(8,128)(2,1)S(1)}, u32[]{:S(2)}, u32[]{:S(2)}) collective-permute-start(bf16[384,256]{1,0:T(8,128)(2,1)S(1)} %copy-done.4), channel_id=1, source_target_pairs={{0,4},{4,0},{8,12},{12,8},{1,5},{5,1},{9,13},{13,9},{2,6},{6,2},{1... | collective-permute-start | bytes 589832 | tf_op jit(solution)/shard_map/ppermute | solution.py:302
  68.6 8.7 %collective-permute-start.13 = (bf16[384,256]{1,0:T(8,128)(2,1)S(1)}, bf16[384,256]{1,0:T(8,128)(2,1)S(1)}, u32[]{:S(2)}, u32[]{:S(2)}) collective-permute-start(bf16[384,256]{1,0:T(8,128)(2,1)S(1)} %copy-done.2), channel_id=1, source_target_pairs={{0,4},{4,0},{8,12},{12,8},{1,5},{5,1},{9,13},{13,9},{2,6},{6,2},{1... | collective-permute-start | bytes 589832 | tf_op jit(solution)/shard_map/ppermute | solution.py:302

commit v14 on v9

--- a/solution.py
+++ b/solution.py
@@ -334,19 +334,23 @@
 
     base = driving[0].astype(F32) + chip_sum(lad)
     terms = [chip_sum(lax.rem(lad + step, lad_count)).astype(BF16) for step in range(1, lad_count)]
-    returned = []
+    returned, crossed = [], []
     for half in range(HALVES):
         blocks = [arrived[(k, half if k or not paired else 0)] for k in far_first]
         if returned:
             blocks, made = lax.optimization_barrier((blocks, made))
         made = apply_cycle(half, plan, operator, blocks, width)
-        if not half:
-            behind, terms = lax.optimization_barrier((made[1:], terms))
-            made = [made[0], *behind]
+        if not returned:
+            behind, terms = lax.optimization_barrier((made[2:], terms))
+            for step, term in enumerate(terms, 1):
+                pairs = [(i, (i + step) % lad_count) for i in range(lad_count)]
+                crossed.append(lax.ppermute(term, "lad", pairs))
+        else:
+            behind, crossed = lax.optimization_barrier((made[2:], crossed))
+        made = [*made[:2], *behind]
         returned.append([exchange(block, k) for k, block in zip(far_first, made)])
-    for step, term in enumerate(terms, 1):
-        pairs = [(i, (i + step) % lad_count) for i in range(lad_count)]
-        base = base + lax.ppermute(term, "lad", pairs).astype(F32)
+    for term in crossed:
+        base = base + term.astype(F32)
     updated = None
     for half in range(HALVES):
         updated = finish(half, pick, base, part_column, hole_row, returned[half], updated)

time: 77 us -> 77 us (level)
  waiting for transfers between devices: 26.5 us -> 27.6 us
  starting transfers between devices: 24.2 us -> 23.2 us
    ppermute x1, waiting for transfers between devices: 0.48 us -> 2.42 us  [body(): crossed.append(lax.ppermute(term, 'lad', pairs))]
    ppermute x12, starting transfers between devices: 22.6 us -> 21.6 us  [exchange(): lax.ppermute(block, 'chan', [(i, i ^ k) for i in range(chan_count)])]
  transfers between devices with their start and end apart: 14 -> 14, of which waited for: 6 -> 6; matrix products, arithmetic and copies ran while one was open for 6% -> 5% of each run, Pallas kernels for 23% -> 23%
where the time goes in v14:
time: 77 us; the launch traced here: 76.7 us
  waiting for transfers between devices  27.6 us (36%)
  starting transfers between devices  23.2 us (30%)
  Pallas kernels  20.8 us (27%)
  other arithmetic  3.15 us (4%)
  local copies, waits for them, and re-layouts  1.75 us (2%)
    ppermute x12, waiting for transfers between devices, exchange(): lax.ppermute(block, 'chan', [(i, i ^ k) for i in range(chan_count)])  25.2 us
    ppermute x12, starting transfers between devices, exchange(): lax.ppermute(block, 'chan', [(i, i ^ k) for i in range(chan_count)])  21.6 us
    pallas_call x1, Pallas kernels, prepare(): pl.pallas_call(functools.partial(prepare_kernel, sub_count), out_shape=[j...  7.96 us
    pallas_call x2, Pallas kernels, apply_cycle(): pl.pallas_call(functools.partial(cycle_kernel, half, plan), out_shape=[ja...  4.49 us
    pallas_call x2, Pallas kernels, pack(): pl.pallas_call(functools.partial(pack_kernel, plan, given), out_shape=ext...  4.21 us
    pallas_call x2, Pallas kernels, finish(): pl.pallas_call(functools.partial(finish_kernel, half, len(arrays), tiles)...  3.02 us
    ppermute x1, waiting for transfers between devices, body(): crossed.append(lax.ppermute(term, 'lad', pairs))  2.42 us
    ppermute x1, starting transfers between devices, body(): crossed.append(lax.ppermute(term, 'lad', pairs))  1.56 us
  transfers between devices with their start and end apart: 14, of which 6 were waited for; matrix products, arithmetic and copies ran while one was open for 5% of the time, Pallas kernels for 23%

profile of v14, /device:TPU:0, one launch (start us, length us, event | category | flops | bytes accessed | tf_op | source)
XLA Modules:
  0.0 76.7 jit_solution(17422855063233573459)
XLA Ops:
  0.0 1.7 %pack_first.1 = (s32[1,768]{1,0:T(1,128)S(1)}, bf16[384,256]{1,0:T(8,128)(2,1)S(1)}, bf16[384,256]{1,0:T(8,128)(2,1)S(1)}, bf16[384,256]{1,0:T(8,128)(2,1)S(1)}) custom-call(s32[1,768]{1,0:T(1,128)} %bitcast.23, bf16[768,512]{1,0:T(8,128)(2,1)} %bitcast.20), custom_call_target="tpu_custom_call" | custom-call | tf_op jit(solution)/shard_map/pack_first/pallas_call | solution.py:93
  1.7 3.1 %collective-permute-start = (bf16[384,256]{1,0:T(8,128)(2,1)S(1)}, bf16[384,256]{1,0:T(8,128)(2,1)S(1)}, u32[]{:S(2)}, u32[]{:S(2)}) collective-permute-start(bf16[384,256]{1,0:T(8,128)(2,1)S(1)} %get-tuple-element.38), channel_id=1, source_target_pairs={{0,4},{4,0},{8,12},{12,8},{1,5},{5,1},{9,13},{13,9},{2,6},{6,2},{1... | collective-permute-start | bytes 589832 | tf_op jit(solution)/shard_map/ppermute | solution.py:302
  4.8 2.5 %collective-permute-start.5 = (bf16[384,256]{1,0:T(8,128)(2,1)S(1)}, bf16[384,256]{1,0:T(8,128)(2,1)S(1)}, u32[]{:S(2)}, u32[]{:S(2)}) collective-permute-start(bf16[384,256]{1,0:T(8,128)(2,1)S(1)} %get-tuple-element.48), channel_id=1, source_target_pairs={{0,12},{4,8},{8,4},{12,0},{1,13},{5,9},{9,5},{13,1},{2,14},{6,10},... | collective-permute-start | bytes 589832 | tf_op jit(solution)/shard_map/ppermute | solution.py:302
  7.2 0.1 collective-permute-start.6
  7.4 0.9 %copy.12.part_ref = f32[768,1]{1,0:T(8,128)S(1)} copy(f32[768,1]{0,1:T(1,128)} %bitcast.24) | data formatting | bytes 6144 | tf_op jit(solution)/shard_map/reshape;squeeze | solution.py:321
  8.2 0.1 add_multiply_fusion.off_ref
  8.3 1.8 %collective-permute-done.refs_2_ = bf16[384,256]{1,0:T(8,128)(2,1)S(1)} collective-permute-done((bf16[384,256]{1,0:T(8,128)(2,1)S(1)}, bf16[384,256]{1,0:T(8,128)(2,1)S(1)}, u32[]{:S(2)}, u32[]{:S(2)}) %collective-permute-start) | collective-permute-done | bytes 196640 | tf_op jit(solution)/shard_map/ppermute | solution.py:302
  10.1 2.5 %pack_rest.1 = (bf16[384,256]{1,0:T(8,128)(2,1)}, bf16[384,256]{1,0:T(8,128)(2,1)}, bf16[384,256]{1,0:T(8,128)(2,1)}, bf16[384,512]{1,0:T(8,128)(2,1)S(1)}) custom-call(s32[1,768]{1,0:T(1,128)S(1)} %get-tuple-element.39.route_in, bf16[768,512]{1,0:T(8,128)(2,1)} %bitcast.21), custom_call_target="tpu_custom_call" | custom-call | tf_op jit(solution)/shard_map/pack_rest/pallas_call | solution.py:93
  12.6 6.8 %collective-permute-start.2 = (bf16[384,256]{1,0:T(8,128)(2,1)}, bf16[384,256]{1,0:T(8,128)(2,1)}, u32[]{:S(2)}, u32[]{:S(2)}) collective-permute-start(bf16[384,256]{1,0:T(8,128)(2,1)} %get-tuple-element.40), channel_id=1, source_target_pairs={{0,12},{4,8},{8,4},{12,0},{1,13},{5,9},{9,5},{13,1},{2,14},{6,10},... | collective-permute-start | bytes 589832 | tf_op jit(solution)/shard_map/ppermute | solution.py:302
  19.4 0.0 collective-permute-start.3
  19.4 0.6 collective-permute-start.4
  20.0 8.0 %prepare.1 = (bf16[2,768,512]{2,1,0:T(8,128)(2,1)}, bf16[2,768,512]{2,1,0:T(8,128)(2,1)S(1)}, bf16[1536,1536]{1,0:T(8,128)(2,1)S(1)}) custom-call(bf16[3072,768]{1,0:T(8,128)(2,1)} %bitcast.25, bf16[768,512]{1,0:T(8,128)(2,1)} %bitcast.22, bf16[1536,1536]{1,0:T(8,128)(2,1)} %bitcast.26, bf16[12,128,128]{2,1,0:T(8,128)(2,1)} %bitcast.27), custom_call_target="tpu_custom_call" | custom-call | flops 30000001024 | bytes 1000000 | tf_op jit(solution)/shard_map/prepare/pallas_call | solution.py:180
  28.0 0.0 copy-start.3
  28.0 0.0 collective-permute-done.5.refs_0_
  28.0 0.1 collective-permute-start.1
  28.1 6.1 %collective-permute-done.6.refs_1_ = bf16[384,256]{1,0:T(8,128)(2,1)S(1)} collective-permute-done((bf16[384,256]{1,0:T(8,128)(2,1)S(1)}, bf16[384,256]{1,0:T(8,128)(2,1)S(1)}, u32[]{:S(2)}, u32[]{:S(2)}) %collective-permute-start.6) | collective-permute-done | bytes 196640 | tf_op jit(solution)/shard_map/ppermute | solution.py:302
  34.2 1.9 %apply_cycle.2 = (bf16[384,256]{1,0:T(8,128)(2,1)}, bf16[384,256]{1,0:T(8,128)(2,1)S(1)}, bf16[384,256]{1,0:T(8,128)(2,1)S(1)}, bf16[384,256]{1,0:T(8,128)(2,1)S(1)}) custom-call(bf16[1536,1536]{1,0:T(8,128)(2,1)S(1)} %get-tuple-element.47.operator_ref, bf16[384,256]{1,0:T(8,128)(2,1)S(1)} %collective-permute-done.5.refs_0_, ...), custom_call_target="tpu_custom_call" | custom-call | flops 30000001024 | bytes 1000000 | tf_op jit(solution)/shard_map/apply_cycle/pallas_call | solution.py:220
  36.1 0.0 copy-done.3
  36.1 0.0 copy-start.1
  36.1 0.7 copy-done.1
  36.8 3.0 %collective-permute-start.11 = (bf16[384,256]{1,0:T(8,128)(2,1)}, bf16[384,256]{1,0:T(8,128)(2,1)S(1)}, u32[]{:S(2)}, u32[]{:S(2)}) collective-permute-start(bf16[384,256]{1,0:T(8,128)(2,1)} %get-tuple-element.51), channel_id=1, source_target_pairs={{0,12},{4,8},{8,4},{12,0},{1,13},{5,9},{9,5},{13,1},{2,14},{6,10},... | collective-permute-start | bytes 589832 | tf_op jit(solution)/shard_map/ppermute | solution.py:302
  39.8 0.0 copy-start.2
  39.8 0.2 copy.10.target_ref
  40.0 0.0 copy-start.4
  40.0 1.1 %unpack_matrix.1.pick_ref = bf16[768,1536]{1,0:T(8,128)(2,1)S(1)} custom-call(s32[4]{0:T(128)S(1)} %add_multiply_fusion.off_ref, s32[768,1]{1,0:T(8,128)S(1)} %copy.10.target_ref), custom_call_target="tpu_custom_call" | custom-call | tf_op jit(solution)/shard_map/unpack_matrix/pallas_call | solution.py:119
  41.1 0.0 collective-permute-done.1
  41.1 0.0 copy-done.2
  41.1 0.1 collective-permute-start.12
  41.2 1.5 %fusion = bf16[768,512]{1,0:T(8,128)(2,1)S(1)} fusion(bf16[2,768,512]{2,1,0:T(8,128)(2,1)} %collective-permute-done.1, s32[]{:T(128)S(6)} %select_n.10, bf16[2,768,512]{2,1,0:T(8,128)(2,1)S(1)} %get-tuple-element.45), kind=kLoop, calls=%fused_computation.2 | loop fusion | flops 1572864 | bytes 2359300 | tf_op jit(solution)/shard_map/convert_element_type | solution.py:336
  42.7 0.0 copy-start.5
  42.7 0.0 collective-permute-done.2.refs_0_
  42.7 1.6 %collective-permute-start.7 = (bf16[768,512]{1,0:T(8,128)(2,1)S(1)}, bf16[768,512]{1,0:T(8,128)(2,1)S(1)}, u32[]{:S(2)}, u32[]{:S(2)}) collective-permute-start(bf16[768,512]{1,0:T(8,128)(2,1)S(1)} %fusion), channel_id=1, source_target_pairs={{0,2},{2,0},{1,3},{3,1},{4,6},{6,4},{5,7},{7,5},{8,10},{10,8},{9,1... | collective-permute-start | bytes 2359304 | tf_op jit(solution)/shard_map/ppermute | solution.py:347
  44.3 6.8 %collective-permute-done.3.refs_1_ = bf16[384,256]{1,0:T(8,128)(2,1)} collective-permute-done((bf16[384,256]{1,0:T(8,128)(2,1)}, bf16[384,256]{1,0:T(8,128)(2,1)}, u32[]{:S(2)}, u32[]{:S(2)}) %collective-permute-start.3) | collective-permute-done | bytes 196640 | tf_op jit(solution)/shard_map/ppermute | solution.py:302
  51.1 0.1 collective-permute-start.13
  51.3 0.0 collective-permute-done.4.refs_2_
  51.3 0.0 copy-done.4
  51.3 2.6 %apply_cycle.3 = (bf16[384,256]{1,0:T(8,128)(2,1)S(1)}, bf16[384,256]{1,0:T(8,128)(2,1)S(1)}, bf16[384,256]{1,0:T(8,128)(2,1)S(1)}, bf16[384,256]{1,0:T(8,128)(2,1)S(1)}) custom-call(bf16[1536,1536]{1,0:T(8,128)(2,1)S(1)} %copy-done.4, bf16[384,256]{1,0:T(8,128)(2,1)} %collective-permute-done.2.refs_0_, bf16[384,256]{1,0:T(8,128)(2,1)} %collective-permute-done.3.refs_1_, ...), custom_call_target="tpu_custom_call" | custom-call | flops 30000001024 | bytes 1000000 | tf_op jit(solution)/shard_map/apply_cycle/pallas_call | solution.py:220
  53.9 2.9 %collective-permute-start.8 = (bf16[384,256]{1,0:T(8,128)(2,1)S(1)}, bf16[384,256]{1,0:T(8,128)(2,1)S(1)}, u32[]{:S(2)}, u32[]{:S(2)}) collective-permute-start(bf16[384,256]{1,0:T(8,128)(2,1)S(1)} %get-tuple-element.65), channel_id=1, source_target_pairs={{0,12},{4,8},{8,4},{12,0},{1,13},{5,9},{9,5},{13,1},{2,14},{6,10},... | collective-permute-start | bytes 589832 | tf_op jit(solution)/shard_map/ppermute | solution.py:302
  56.7 2.4 %collective-permute-done.7 = bf16[768,512]{1,0:T(8,128)(2,1)S(1)} collective-permute-done((bf16[768,512]{1,0:T(8,128)(2,1)S(1)}, bf16[768,512]{1,0:T(8,128)(2,1)S(1)}, u32[]{:S(2)}, u32[]{:S(2)}) %collective-permute-start.7) | collective-permute-done | bytes 786464 | tf_op jit(solution)/shard_map/ppermute | solution.py:347
  59.2 2.4 %collective-permute-start.9 = (bf16[384,256]{1,0:T(8,128)(2,1)S(1)}, bf16[384,256]{1,0:T(8,128)(2,1)S(1)}, u32[]{:S(2)}, u32[]{:S(2)}) collective-permute-start(bf16[384,256]{1,0:T(8,128)(2,1)S(1)} %get-tuple-element.66), channel_id=1, source_target_pairs={{0,8},{4,12},{8,0},{12,4},{1,9},{5,13},{9,1},{13,5},{2,10},{6,14},... | collective-permute-start | bytes 589832 | tf_op jit(solution)/shard_map/ppermute | solution.py:302
  61.6 0.0 copy-start
  61.6 0.0 collective-permute-done.11.refs_0_
  61.6 0.0 collective-permute-start.10
  61.6 0.0 copy-done.5
  61.6 1.5 %bitcast_add_fusion.base_ref = f32[768,512]{1,0:T(8,128)S(1)} fusion(bf16[768,512]{1,0:T(8,128)(2,1)S(1)} %collective-permute-done.7, bf16[1,768,512]{2,1,0:T(8,128)(2,1)S(1)} %copy-done.5, bf16[2,768,512]{2,1,0:T(8,128)(2,1)} %collective-permute-done.1, s32[]{:T(128)S(6)} %select_n.9, bf16[2,768,512]{2,1,0:T(8,128)(2,1)S(1)} %get-tuple-element.45), kind=kLoop, calls=%fused_computation | loop fusion | flops 2752512 | bytes 4718596 | tf_op jit(solution)/shard_map/add | solution.py:353
  63.1 3.8 %collective-permute-done.12.refs_1_ = bf16[384,256]{1,0:T(8,128)(2,1)S(1)} collective-permute-done((bf16[384,256]{1,0:T(8,128)(2,1)S(1)}, bf16[384,256]{1,0:T(8,128)(2,1)S(1)}, u32[]{:S(2)}, u32[]{:S(2)}) %collective-permute-start.12) | collective-permute-done | bytes 196640 | tf_op jit(solution)/shard_map/ppermute | solution.py:302
  66.9 0.0 collective-permute-done.13.refs_2_
  67.0 0.0 copy-done
  67.0 1.5 %finish.2.refs_4_ = bf16[768,512]{1,0:T(8,128)(2,1)} custom-call(bf16[768,1536]{1,0:T(8,128)(2,1)S(1)} %unpack_matrix.1.pick_ref, f32[768,512]{1,0:T(8,128)S(1)} %bitcast_add_fusion.base_ref, f32[768,1]{1,0:T(8,128)S(1)} %copy.12.part_ref, f32[1,512]{1,0:T(1,128)S(1)} %bitcast.18, bf16[384,256]{1,0:T(8,128)(2,1)S(1)} %collective-permute-done.11.refs_0_, ...), custom_call_target="tpu_custom_call" | custom-call | tf_op jit(solution)/shard_map/finish/pallas_call | solution.py:261
  68.5 0.0 collective-permute-done.8.refs_0_
  68.5 6.7 %collective-permute-done.9.refs_1_ = bf16[384,256]{1,0:T(8,128)(2,1)S(1)} collective-permute-done((bf16[384,256]{1,0:T(8,128)(2,1)S(1)}, bf16[384,256]{1,0:T(8,128)(2,1)S(1)}, u32[]{:S(2)}, u32[]{:S(2)}) %collective-permute-start.9) | collective-permute-done | bytes 196640 | tf_op jit(solution)/shard_map/ppermute | solution.py:302
  75.2 0.0 collective-permute-done.10.refs_2_
  75.2 1.5 %finish.3 = bf16[768,512]{1,0:T(8,128)(2,1)} custom-call(bf16[768,1536]{1,0:T(8,128)(2,1)S(1)} %unpack_matrix.1.pick_ref, f32[768,512]{1,0:T(8,128)S(1)} %bitcast_add_fusion.base_ref, f32[768,1]{1,0:T(8,128)S(1)} %copy.12.part_ref, f32[1,512]{1,0:T(1,128)S(1)} %bitcast.19, ...), custom_call_target="tpu_custom_call", output_to_operand_aliasing={{}: (8, {})} | custom-call | tf_op jit(solution)/shard_map/finish/pallas_call | solution.py:261
Async XLA Ops:
  1.7 8.4 %collective-permute-start = (bf16[384,256]{1,0:T(8,128)(2,1)S(1)}, bf16[384,256]{1,0:T(8,128)(2,1)S(1)}, u32[]{:S(2)}, u32[]{:S(2)}) collective-permute-start(bf16[384,256]{1,0:T(8,128)(2,1)S(1)} %get-tuple-element.38), channel_id=1, source_target_pairs={{0,4},{4,0},{8,12},{12,8},{1,5},{5,1},{9,13},{13,9},{2,6},{6,2},{1... | collective-permute-start | bytes 589832 | tf_op jit(solution)/shard_map/ppermute | solution.py:302
  4.8 23.3 %collective-permute-start.5 = (bf16[384,256]{1,0:T(8,128)(2,1)S(1)}, bf16[384,256]{1,0:T(8,128)(2,1)S(1)}, u32[]{:S(2)}, u32[]{:S(2)}) collective-permute-start(bf16[384,256]{1,0:T(8,128)(2,1)S(1)} %get-tuple-element.48), channel_id=1, source_target_pairs={{0,12},{4,8},{8,4},{12,0},{1,13},{5,9},{9,5},{13,1},{2,14},{6,10},... | collective-permute-start | bytes 589832 | tf_op jit(solution)/shard_map/ppermute | solution.py:302
  7.2 26.9 %collective-permute-start.6 = (bf16[384,256]{1,0:T(8,128)(2,1)S(1)}, bf16[384,256]{1,0:T(8,128)(2,1)S(1)}, u32[]{:S(2)}, u32[]{:S(2)}) collective-permute-start(bf16[384,256]{1,0:T(8,128)(2,1)S(1)} %get-tuple-element.49), channel_id=1, source_target_pairs={{0,8},{4,12},{8,0},{12,4},{1,9},{5,13},{9,1},{13,5},{2,10},{6,14},... | collective-permute-start | bytes 589832 | tf_op jit(solution)/shard_map/ppermute | solution.py:302
  12.6 30.1 %collective-permute-start.2 = (bf16[384,256]{1,0:T(8,128)(2,1)}, bf16[384,256]{1,0:T(8,128)(2,1)}, u32[]{:S(2)}, u32[]{:S(2)}) collective-permute-start(bf16[384,256]{1,0:T(8,128)(2,1)} %get-tuple-element.40), channel_id=1, source_target_pairs={{0,12},{4,8},{8,4},{12,0},{1,13},{5,9},{9,5},{13,1},{2,14},{6,10},... | collective-permute-start | bytes 589832 | tf_op jit(solution)/shard_map/ppermute | solution.py:302
  19.4 31.7 %collective-permute-start.3 = (bf16[384,256]{1,0:T(8,128)(2,1)}, bf16[384,256]{1,0:T(8,128)(2,1)}, u32[]{:S(2)}, u32[]{:S(2)}) collective-permute-start(bf16[384,256]{1,0:T(8,128)(2,1)} %get-tuple-element.41), channel_id=1, source_target_pairs={{0,8},{4,12},{8,0},{12,4},{1,9},{5,13},{9,1},{13,5},{2,10},{6,14},... | collective-permute-start | bytes 589832 | tf_op jit(solution)/shard_map/ppermute | solution.py:302
  19.4 31.9 %collective-permute-start.4 = (bf16[384,256]{1,0:T(8,128)(2,1)}, bf16[384,256]{1,0:T(8,128)(2,1)}, u32[]{:S(2)}, u32[]{:S(2)}) collective-permute-start(bf16[384,256]{1,0:T(8,128)(2,1)} %get-tuple-element.42), channel_id=1, source_target_pairs={{0,4},{4,0},{8,12},{12,8},{1,5},{5,1},{9,13},{13,9},{2,6},{6,2},{1... | collective-permute-start | bytes 589832 | tf_op jit(solution)/shard_map/ppermute | solution.py:302
  28.0 8.1 %copy-start.3 = (bf16[1536,1536]{1,0:T(8,128)(2,1)}, bf16[1536,1536]{1,0:T(8,128)(2,1)S(1)}, u32[]{:S(2)}) copy-start(bf16[1536,1536]{1,0:T(8,128)(2,1)S(1)} %get-tuple-element.47.operator_ref) | copy-start | bytes 14155780
  28.0 13.1 %collective-permute-start.1 = (bf16[2,768,512]{2,1,0:T(8,128)(2,1)}, bf16[2,768,512]{2,1,0:T(8,128)(2,1)}, u32[]{:S(2)}, u32[]{:S(2)}) collective-permute-start(bf16[2,768,512]{2,1,0:T(8,128)(2,1)} %get-tuple-element.46), channel_id=1, source_target_pairs={{0,1},{1,0},{2,3},{3,2},{4,5},{5,4},{6,7},{7,6},{8,9},{9,8},{10,11... | collective-permute-start | bytes 4718600 | tf_op jit(solution)/shard_map/ppermute | solution.py:329
  36.1 0.7 copy-start.1
  36.8 24.8 %collective-permute-start.11 = (bf16[384,256]{1,0:T(8,128)(2,1)}, bf16[384,256]{1,0:T(8,128)(2,1)S(1)}, u32[]{:S(2)}, u32[]{:S(2)}) collective-permute-start(bf16[384,256]{1,0:T(8,128)(2,1)} %get-tuple-element.51), channel_id=1, source_target_pairs={{0,12},{4,8},{8,4},{12,0},{1,13},{5,9},{9,5},{13,1},{2,14},{6,10},... | collective-permute-start | bytes 589832 | tf_op jit(solution)/shard_map/ppermute | solution.py:302
  39.8 1.3 %copy-start.2 = (bf16[384,256]{1,0:T(8,128)(2,1)S(1)}, bf16[384,256]{1,0:T(8,128)(2,1)}, u32[]{:S(2)}) copy-start(bf16[384,256]{1,0:T(8,128)(2,1)} %copy-done.1) | copy-start | bytes 589828
  40.0 11.3 %copy-start.4 = (bf16[1536,1536]{1,0:T(8,128)(2,1)S(1)}, bf16[1536,1536]{1,0:T(8,128)(2,1)}, u32[]{:S(2)}) copy-start(bf16[1536,1536]{1,0:T(8,128)(2,1)} %copy-done.3) | copy-start | bytes 14155780
  41.1 25.8 %collective-permute-start.12 = (bf16[384,256]{1,0:T(8,128)(2,1)S(1)}, bf16[384,256]{1,0:T(8,128)(2,1)S(1)}, u32[]{:S(2)}, u32[]{:S(2)}) collective-permute-start(bf16[384,256]{1,0:T(8,128)(2,1)S(1)} %copy-done.2), channel_id=1, source_target_pairs={{0,8},{4,12},{8,0},{12,4},{1,9},{5,13},{9,1},{13,5},{2,10},{6,14},... | collective-permute-start | bytes 589832 | tf_op jit(solution)/shard_map/ppermute | solution.py:302
  42.7 18.9 %copy-start.5 = (bf16[1,768,512]{2,1,0:T(8,128)(2,1)S(1)}, bf16[1,768,512]{2,1,0:T(8,128)(2,1)}, u32[]{:S(2)}) copy-start(bf16[1,768,512]{2,1,0:T(8,128)(2,1)} %param.9) | copy-start | bytes 2359300
  42.7 16.4 %collective-permute-start.7 = (bf16[768,512]{1,0:T(8,128)(2,1)S(1)}, bf16[768,512]{1,0:T(8,128)(2,1)S(1)}, u32[]{:S(2)}, u32[]{:S(2)}) collective-permute-start(bf16[768,512]{1,0:T(8,128)(2,1)S(1)} %fusion), channel_id=1, source_target_pairs={{0,2},{2,0},{1,3},{3,1},{4,6},{6,4},{5,7},{7,5},{8,10},{10,8},{9,1... | collective-permute-start | bytes 2359304 | tf_op jit(solution)/shard_map/ppermute | solution.py:347
  51.1 15.8 %collective-permute-start.13 = (bf16[384,256]{1,0:T(8,128)(2,1)S(1)}, bf16[384,256]{1,0:T(8,128)(2,1)S(1)}, u32[]{:S(2)}, u32[]{:S(2)}) collective-permute-start(bf16[384,256]{1,0:T(8,128)(2,1)S(1)} %get-tuple-element.55), channel_id=1, source_target_pairs={{0,4},{4,0},{8,12},{12,8},{1,5},{5,1},{9,13},{13,9},{2,6},{6,2},{1... | collective-permute-start | bytes 589832 | tf_op jit(solution)/shard_map/ppermute | solution.py:302
  53.9 14.6 %collective-permute-start.8 = (bf16[384,256]{1,0:T(8,128)(2,1)S(1)}, bf16[384,256]{1,0:T(8,128)(2,1)S(1)}, u32[]{:S(2)}, u32[]{:S(2)}) collective-permute-start(bf16[384,256]{1,0:T(8,128)(2,1)S(1)} %get-tuple-element.65), channel_id=1, source_target_pairs={{0,12},{4,8},{8,4},{12,0},{1,13},{5,9},{9,5},{13,1},{2,14},{6,10},... | collective-permute-start | bytes 589832 | tf_op jit(solution)/shard_map/ppermute | solution.py:302
  59.2 16.1 %collective-permute-start.9 = (bf16[384,256]{1,0:T(8,128)(2,1)S(1)}, bf16[384,256]{1,0:T(8,128)(2,1)S(1)}, u32[]{:S(2)}, u32[]{:S(2)}) collective-permute-start(bf16[384,256]{1,0:T(8,128)(2,1)S(1)} %get-tuple-element.66), channel_id=1, source_target_pairs={{0,8},{4,12},{8,0},{12,4},{1,9},{5,13},{9,1},{13,5},{2,10},{6,14},... | collective-permute-start | bytes 589832 | tf_op jit(solution)/shard_map/ppermute | solution.py:302
  61.6 5.4 %copy-start = (f32[512]{0:T(512)S(1)}, f32[512]{0:T(512)}, u32[]{:S(2)}) copy-start(f32[512]{0:T(512)} %param.15) | copy-start | bytes 6148
  61.6 13.6 %collective-permute-start.10 = (bf16[384,256]{1,0:T(8,128)(2,1)S(1)}, bf16[384,256]{1,0:T(8,128)(2,1)S(1)}, u32[]{:S(2)}, u32[]{:S(2)}) collective-permute-start(bf16[384,256]{1,0:T(8,128)(2,1)S(1)} %get-tuple-element.67), channel_id=1, source_target_pairs={{0,4},{4,0},{8,12},{12,8},{1,5},{5,1},{9,13},{13,9},{2,6},{6,2},{1... | collective-permute-start | bytes 589832 | tf_op jit(solution)/shard_map/ppermute | solution.py:302

commit v15 on v14

--- a/solution.py
+++ b/solution.py
@@ -105,7 +105,7 @@
     )(*([route_row] if given else in_hbm(route_row)), *in_hbm(amps))
 
 
-def unpack_kernel(off_ref, target_ref, out_ref):
+def unpack_kernel(off_ref, target_ref, part_ref, hole_ref, out_ref, inverse_ref):
     count = off_ref.shape[0]
     rows, capacity = out_ref.shape
     block_rows = capacity // count
@@ -113,18 +113,20 @@
     slots = lax.broadcasted_iota(jnp.int32, (rows, block_rows), 1)
     for k in range(count):
         out_ref[:, pl.ds(k * block_rows, block_rows)] = selection(slots == target - off_ref[k])
-
-
-def unpack_matrix(offsets, target_column, capacity):
+    inverse_ref[...] = 1.0 / (part_ref[...] + hole_ref[...])
+
+
+def unpack_matrix(offsets, target_column, part_column, hole_row, capacity):
+    rows, holes = part_column.shape[0], hole_row.shape[1]
     return pl.pallas_call(
         unpack_kernel,
-        out_shape=jax.ShapeDtypeStruct((target_column.shape[0], capacity), BF16),
-        in_specs=[whole(pltpu.SMEM), whole()],
-        out_specs=whole(),
+        out_shape=[jax.ShapeDtypeStruct((rows, capacity), BF16), jax.ShapeDtypeStruct((rows, holes), F32)],
+        in_specs=[whole(pltpu.SMEM), whole(), whole(), whole()],
+        out_specs=[whole()] * 2,
         compiler_params=params(),
-        cost_estimate=CHEAP,
+        cost_estimate=DEAR,
         name="unpack_matrix",
-    )(offsets, target_column)
+    )(offsets, target_column, part_column, hole_row)
 
 
 def prepare_kernel(sub_count, weight_hbm, amps_hbm, cycle_hbm, mixing_hbm, *refs):
@@ -229,29 +231,64 @@
     )(operator, *arrays)
 
 
-def finish_kernel(half, count, tiles, pick_ref, base_ref, part_ref, hole_ref, *refs):
-    in_refs, (out_hbm, block_ref, out_ref, sems) = refs[:count], refs[-4:]
-    block_rows, width = in_refs[0].shape
-    tile = out_ref.shape[0] // tiles
-    columns = pl.ds(half * width, width)
-    for i, in_ref in enumerate(in_refs):
-        block_ref[pl.ds((count - 1 - i) * block_rows, block_rows), :] = in_ref[...]
+def gathered(blocks, block_ref):
+    block_rows = blocks[0][1].shape[0]
+    for n, (_, ref) in enumerate(blocks):
+        block_ref[pl.ds(n * block_rows, block_rows), :] = ref[...]
+
+
+def picked(blocks, pick_ref, rows_at):
+    block_rows = blocks[0][1].shape[0]
+    return jnp.concatenate([pick_ref[rows_at, pl.ds(k * block_rows, block_rows)] for k, _ in blocks], axis=1)
+
+
+def partial_kernel(start_column, places, tiles, pick_ref, base_ref, *refs):
+    blocks, (out_ref, block_ref) = list(zip(places, refs[:-2])), refs[-2:]
+    tile, columns = out_ref.shape[0] // tiles, pl.ds(start_column, out_ref.shape[1])
+    gathered(blocks, block_ref)
+    for t in range(tiles):
+        at = pl.ds(t * tile, tile)
+        back = jnp.dot(picked(blocks, pick_ref, at), block_ref[...], preferred_element_type=F32)
+        out_ref[at, :] = base_ref[at, columns] + back
+
+
+def finish_kernel(start_column, places, tiles, pick_ref, base_ref, inverse_ref, *refs):
+    blocks, (out_hbm, block_ref, out_ref, sems) = list(zip(places, refs)), refs[-4:]
+    tile, width = out_ref.shape[0] // tiles, out_ref.shape[1]
+    columns = pl.ds(start_column, width)
+    base_columns = columns if base_ref.shape[1] > width else pl.ds(0, width)
+    gathered(blocks, block_ref)
     copies = []
     for t in range(tiles):
         at = pl.ds(t * tile, tile)
-        back = jnp.dot(pick_ref[at, :], block_ref[...], preferred_element_type=F32)
-        total = base_ref[at, columns] + back
-        out_ref[at, :] = (total / (part_ref[at, :] + hole_ref[:, columns])).astype(BF16)
+        back = jnp.dot(picked(blocks, pick_ref, at), block_ref[...], preferred_element_type=F32)
+        out_ref[at, :] = ((base_ref[at, base_columns] + back) * inverse_ref[at, columns]).astype(BF16)
         copies.append(pltpu.make_async_copy(out_ref.at[at, :], out_hbm.at[at, columns], sems.at[t]))
         copies[-1].start()
     for copy in copies:
         copy.wait()
 
 
-def finish(half, pick, base, part_column, hole_row, arrays, earlier):
-    rows, holes = base.shape
+def finish(half, pick, base, inverse, arrays, earlier):
+    rows, holes = inverse.shape
     tiles, width = 3, holes // HALVES
-    operands = [pick, base, part_column, hole_row, *arrays]
+    block_rows = arrays[0].shape[0]
+    places = list(range(len(arrays)))
+    if earlier is not None and len(arrays) > 1:
+        last = min(2, len(arrays) - 1)
+        places.remove(last)
+        base = pl.pallas_call(
+            functools.partial(partial_kernel, half * width, tuple(places), tiles),
+            out_shape=jax.ShapeDtypeStruct((rows, width), F32),
+            in_specs=[whole()] * (2 + len(places)),
+            out_specs=whole(),
+            scratch_shapes=[pltpu.VMEM((block_rows * len(places), width), BF16)],
+            compiler_params=params(),
+            cost_estimate=CHEAP,
+            name="partial",
+        )(pick, base, *[arrays[k] for k in places])
+        places = [last]
+    operands = [pick, base, inverse] + [arrays[k] for k in places]
     in_specs = [whole()] * len(operands)
     aliases = {}
     if earlier is not None:
@@ -259,12 +296,12 @@
         operands.append(earlier)
         in_specs.append(whole(pl.ANY))
     return pl.pallas_call(
-        functools.partial(finish_kernel, half, len(arrays), tiles),
+        functools.partial(finish_kernel, half * width, tuple(places), tiles),
         out_shape=jax.ShapeDtypeStruct((rows, holes), BF16),
         in_specs=in_specs,
         out_specs=whole(pl.ANY),
         scratch_shapes=[
-            pltpu.VMEM((pick.shape[1], width), BF16),
+            pltpu.VMEM((block_rows * len(places), width), BF16),
             pltpu.VMEM((rows, width), BF16),
             pltpu.SemaphoreType.DMA((tiles,)),
         ],
@@ -320,7 +357,7 @@
 
     part_column, hole_row = gap_part[0].reshape(rows, 1), gap_hole.reshape(1, holes)
     amps, blocks = lax.optimization_barrier((amps, blocks))
-    pick = unpack_matrix(offsets, target.reshape(rows, 1), capacity)
+    pick, inverse = unpack_matrix(offsets, target.reshape(rows, 1), part_column, hole_row, capacity)
 
     parts, operator = prepare(ladder_weight[0], amps, weight, mixing, lad_count, sub_count)
     kept = [parts[-1]]
@@ -353,7 +390,7 @@
         base = base + term.astype(F32)
     updated = None
     for half in range(HALVES):
-        updated = finish(half, pick, base, part_column, hole_row, returned[half], updated)
+        updated = finish(half, pick, base, inverse, list(reversed(returned[half])), updated)
     return updated[None]
 
 

time: 77 us -> 76.6 us (level)
    pallas_call x3 -> x4, Pallas kernels: 4.12 us -> 4.59 us  [the longest x2 2.6 us: finish(): pl.pallas_call(functools.partial(finish_kernel, half * width, tuple(place...]
  transfers between devices with their start and end apart: 14 -> 14, of which waited for: 6 -> 6; matrix products, arithmetic and copies ran while one was open for 5% -> 5% of each run, Pallas kernels for 23% -> 24%
where the time goes in v15:
time: 76.6 us; the launch traced here: 76.3 us
  waiting for transfers between devices  27 us (35%)
  starting transfers between devices  23.1 us (30%)
  Pallas kernels  21.2 us (28%)
  other arithmetic  2.94 us (4%)
  local copies, waits for them, and re-layouts  1.74 us (2%)
    ppermute x12, waiting for transfers between devices, exchange(): lax.ppermute(block, 'chan', [(i, i ^ k) for i in range(chan_count)])  24.6 us
    ppermute x12, starting transfers between devices, exchange(): lax.ppermute(block, 'chan', [(i, i ^ k) for i in range(chan_count)])  21.5 us
    pallas_call x1, Pallas kernels, prepare(): pl.pallas_call(functools.partial(prepare_kernel, sub_count), out_shape=[j...  7.96 us
    pallas_call x2, Pallas kernels, apply_cycle(): pl.pallas_call(functools.partial(cycle_kernel, half, plan), out_shape=[ja...  4.49 us
    pallas_call x2, Pallas kernels, pack(): pl.pallas_call(functools.partial(pack_kernel, plan, given), out_shape=ext...  4.2 us
    pallas_call x2, Pallas kernels, finish(): pl.pallas_call(functools.partial(finish_kernel, half * width, tuple(place...  2.6 us
    ppermute x1, waiting for transfers between devices, body(): crossed.append(lax.ppermute(term, 'lad', pairs))  2.41 us
    ppermute x1, starting transfers between devices, body(): crossed.append(lax.ppermute(term, 'lad', pairs))  1.56 us
  transfers between devices with their start and end apart: 14, of which 6 were waited for; matrix products, arithmetic and copies ran while one was open for 5% of the time, Pallas kernels for 24%

profile of v15, /device:TPU:0, one launch (start us, length us, event | category | flops | bytes accessed | tf_op | source)
XLA Modules:
  0.0 76.3 jit_solution(17228907913564808134)
XLA Ops:
  0.0 1.7 %pack_first.1 = (s32[1,768]{1,0:T(1,128)S(1)}, bf16[384,256]{1,0:T(8,128)(2,1)S(1)}, bf16[384,256]{1,0:T(8,128)(2,1)S(1)}, bf16[384,256]{1,0:T(8,128)(2,1)S(1)}) custom-call(s32[1,768]{1,0:T(1,128)} %bitcast.24, bf16[768,512]{1,0:T(8,128)(2,1)} %bitcast.21), custom_call_target="tpu_custom_call" | custom-call | tf_op jit(solution)/shard_map/pack_first/pallas_call | solution.py:93
  1.7 3.1 %collective-permute-start = (bf16[384,256]{1,0:T(8,128)(2,1)S(1)}, bf16[384,256]{1,0:T(8,128)(2,1)S(1)}, u32[]{:S(2)}, u32[]{:S(2)}) collective-permute-start(bf16[384,256]{1,0:T(8,128)(2,1)S(1)} %get-tuple-element.40), channel_id=1, source_target_pairs={{0,4},{4,0},{8,12},{12,8},{1,5},{5,1},{9,13},{13,9},{2,6},{6,2},{1... | collective-permute-start | bytes 589832 | tf_op jit(solution)/shard_map/ppermute | solution.py:339
  4.8 2.5 %collective-permute-start.5 = (bf16[384,256]{1,0:T(8,128)(2,1)S(1)}, bf16[384,256]{1,0:T(8,128)(2,1)S(1)}, u32[]{:S(2)}, u32[]{:S(2)}) collective-permute-start(bf16[384,256]{1,0:T(8,128)(2,1)S(1)} %get-tuple-element.51), channel_id=1, source_target_pairs={{0,12},{4,8},{8,4},{12,0},{1,13},{5,9},{9,5},{13,1},{2,14},{6,10},... | collective-permute-start | bytes 589832 | tf_op jit(solution)/shard_map/ppermute | solution.py:339
  7.2 0.1 collective-permute-start.6
  7.4 0.9 %copy.11.part_ref = f32[768,1]{1,0:T(8,128)S(1)} copy(f32[768,1]{0,1:T(1,128)} %bitcast.25) | data formatting | bytes 6144 | tf_op jit(solution)/shard_map/reshape;squeeze | solution.py:358
  8.2 0.1 add_multiply_fusion.off_ref
  8.3 1.8 %collective-permute-done.refs_2_ = bf16[384,256]{1,0:T(8,128)(2,1)S(1)} collective-permute-done((bf16[384,256]{1,0:T(8,128)(2,1)S(1)}, bf16[384,256]{1,0:T(8,128)(2,1)S(1)}, u32[]{:S(2)}, u32[]{:S(2)}) %collective-permute-start) | collective-permute-done | bytes 196640 | tf_op jit(solution)/shard_map/ppermute | solution.py:339
  10.1 2.5 %pack_rest.1 = (bf16[384,256]{1,0:T(8,128)(2,1)}, bf16[384,256]{1,0:T(8,128)(2,1)}, bf16[384,256]{1,0:T(8,128)(2,1)}, bf16[384,512]{1,0:T(8,128)(2,1)S(1)}) custom-call(s32[1,768]{1,0:T(1,128)S(1)} %get-tuple-element.41.route_in, bf16[768,512]{1,0:T(8,128)(2,1)} %bitcast.22), custom_call_target="tpu_custom_call" | custom-call | tf_op jit(solution)/shard_map/pack_rest/pallas_call | solution.py:93
  12.6 6.8 %collective-permute-start.2 = (bf16[384,256]{1,0:T(8,128)(2,1)}, bf16[384,256]{1,0:T(8,128)(2,1)}, u32[]{:S(2)}, u32[]{:S(2)}) collective-permute-start(bf16[384,256]{1,0:T(8,128)(2,1)} %get-tuple-element.43), channel_id=1, source_target_pairs={{0,12},{4,8},{8,4},{12,0},{1,13},{5,9},{9,5},{13,1},{2,14},{6,10},... | collective-permute-start | bytes 589832 | tf_op jit(solution)/shard_map/ppermute | solution.py:339
  19.4 0.0 collective-permute-start.3
  19.4 0.6 collective-permute-start.4
  20.0 8.0 %prepare.1 = (bf16[2,768,512]{2,1,0:T(8,128)(2,1)}, bf16[2,768,512]{2,1,0:T(8,128)(2,1)S(1)}, bf16[1536,1536]{1,0:T(8,128)(2,1)S(1)}) custom-call(bf16[3072,768]{1,0:T(8,128)(2,1)} %bitcast.26, bf16[768,512]{1,0:T(8,128)(2,1)} %bitcast.23, bf16[1536,1536]{1,0:T(8,128)(2,1)} %bitcast.27, bf16[12,128,128]{2,1,0:T(8,128)(2,1)} %bitcast.28), custom_call_target="tpu_custom_call" | custom-call | flops 30000001024 | bytes 1000000 | tf_op jit(solution)/shard_map/prepare/pallas_call | solution.py:182
  28.0 0.0 copy-start.3
  28.0 0.0 collective-permute-done.5.refs_0_
  28.0 0.1 collective-permute-start.1
  28.1 6.1 %collective-permute-done.6.refs_1_ = bf16[384,256]{1,0:T(8,128)(2,1)S(1)} collective-permute-done((bf16[384,256]{1,0:T(8,128)(2,1)S(1)}, bf16[384,256]{1,0:T(8,128)(2,1)S(1)}, u32[]{:S(2)}, u32[]{:S(2)}) %collective-permute-start.6) | collective-permute-done | bytes 196640 | tf_op jit(solution)/shard_map/ppermute | solution.py:339
  34.2 0.0 copy-start.2
  34.2 1.9 %apply_cycle.2 = (bf16[384,256]{1,0:T(8,128)(2,1)S(1)}, bf16[384,256]{1,0:T(8,128)(2,1)}, bf16[384,256]{1,0:T(8,128)(2,1)S(1)}, bf16[384,256]{1,0:T(8,128)(2,1)S(1)}) custom-call(bf16[1536,1536]{1,0:T(8,128)(2,1)S(1)} %get-tuple-element.50.operator_ref, bf16[384,256]{1,0:T(8,128)(2,1)S(1)} %collective-permute-done.5.refs_0_, ...), custom_call_target="tpu_custom_call" | custom-call | flops 30000001024 | bytes 1000000 | tf_op jit(solution)/shard_map/apply_cycle/pallas_call | solution.py:222
  36.1 0.0 copy-done.3
  36.1 0.0 copy-start
  36.1 0.7 copy-done
  36.8 0.0 collective-permute-start.12
  36.8 0.2 copy.10.target_ref
  37.0 0.0 slice-start
  37.0 0.0 copy-done.2
  37.0 0.0 copy-start.1
  37.0 0.0 slice-start.1
  37.0 1.3 %unpack_matrix.1 = (bf16[768,1536]{1,0:T(8,128)(2,1)S(1)}, f32[768,512]{1,0:T(8,128)S(1)}) custom-call(s32[4]{0:T(128)S(1)} %add_multiply_fusion.off_ref, s32[768,1]{1,0:T(8,128)S(1)} %copy.10.target_ref, f32[768,1]{1,0:T(8,128)S(1)} %copy.11.part_ref, f32[1,512]{1,0:T(1,128)S(1)} %bitcast.18), custom_call_target="tpu_custom_call" | custom-call | flops 30000001024 | bytes 1000000 | tf_op jit(solution)/shard_map/unpack_matrix/pallas_call | solution.py:121
  38.4 0.0 collective-permute-done.1
  38.4 0.0 copy-done.1
  38.4 3.0 %collective-permute-start.13 = (bf16[384,256]{1,0:T(8,128)(2,1)S(1)}, bf16[384,256]{1,0:T(8,128)(2,1)S(1)}, u32[]{:S(2)}, u32[]{:S(2)}) collective-permute-start(bf16[384,256]{1,0:T(8,128)(2,1)S(1)} %copy-done.1), channel_id=1, source_target_pairs={{0,12},{4,8},{8,4},{12,0},{1,13},{5,9},{9,5},{13,1},{2,14},{6,10},... | collective-permute-start | bytes 589832 | tf_op jit(solution)/shard_map/ppermute | solution.py:339
  41.4 1.3 %fusion = bf16[768,512]{1,0:T(8,128)(2,1)S(1)} fusion(bf16[2,768,512]{2,1,0:T(8,128)(2,1)} %collective-permute-done.1, s32[]{:T(128)S(6)} %select_n.10, bf16[2,768,512]{2,1,0:T(8,128)(2,1)S(1)} %get-tuple-element.48), kind=kLoop, calls=%fused_computation.2 | loop fusion | flops 1572864 | bytes 2359300 | tf_op jit(solution)/shard_map/convert_element_type | solution.py:373
  42.7 0.0 copy-start.4
  42.8 0.0 collective-permute-done.2.refs_0_
  42.8 1.6 %collective-permute-start.7 = (bf16[768,512]{1,0:T(8,128)(2,1)S(1)}, bf16[768,512]{1,0:T(8,128)(2,1)S(1)}, u32[]{:S(2)}, u32[]{:S(2)}) collective-permute-start(bf16[768,512]{1,0:T(8,128)(2,1)S(1)} %fusion), channel_id=1, source_target_pairs={{0,2},{2,0},{1,3},{3,1},{4,6},{6,4},{5,7},{7,5},{8,10},{10,8},{9,1... | collective-permute-start | bytes 2359304 | tf_op jit(solution)/shard_map/ppermute | solution.py:384
  44.3 6.8 %collective-permute-done.3.refs_1_ = bf16[384,256]{1,0:T(8,128)(2,1)} collective-permute-done((bf16[384,256]{1,0:T(8,128)(2,1)}, bf16[384,256]{1,0:T(8,128)(2,1)}, u32[]{:S(2)}, u32[]{:S(2)}) %collective-permute-start.3) | collective-permute-done | bytes 196640 | tf_op jit(solution)/shard_map/ppermute | solution.py:339
  51.1 0.1 collective-permute-start.11
  51.3 0.0 collective-permute-done.4.refs_2_
  51.3 0.0 slice-done
  51.3 0.0 slice-done.1
  51.3 2.6 %apply_cycle.3 = (bf16[384,256]{1,0:T(8,128)(2,1)S(1)}, bf16[384,256]{1,0:T(8,128)(2,1)S(1)}, bf16[384,256]{1,0:T(8,128)(2,1)S(1)}, bf16[384,256]{1,0:T(8,128)(2,1)S(1)}) custom-call(bf16[1536,1536]{1,0:T(8,128)(2,1)S(1)} %bitcast.20, bf16[384,256]{1,0:T(8,128)(2,1)} %collective-permute-done.2.refs_0_, bf16[384,256]{1,0:T(8,128)(2,1)} %collective-permute-done.3.refs_1_, ...), custom_call_target="tpu_custom_call" | custom-call | flops 30000001024 | bytes 1000000 | tf_op jit(solution)/shard_map/apply_cycle/pallas_call | solution.py:222
  53.9 2.9 %collective-permute-start.9 = (bf16[384,256]{1,0:T(8,128)(2,1)S(1)}, bf16[384,256]{1,0:T(8,128)(2,1)S(1)}, u32[]{:S(2)}, u32[]{:S(2)}) collective-permute-start(bf16[384,256]{1,0:T(8,128)(2,1)S(1)} %get-tuple-element.70), channel_id=1, source_target_pairs={{0,12},{4,8},{8,4},{12,0},{1,13},{5,9},{9,5},{13,1},{2,14},{6,10},... | collective-permute-start | bytes 589832 | tf_op jit(solution)/shard_map/ppermute | solution.py:339
  56.8 2.4 %collective-permute-done.7 = bf16[768,512]{1,0:T(8,128)(2,1)S(1)} collective-permute-done((bf16[768,512]{1,0:T(8,128)(2,1)S(1)}, bf16[768,512]{1,0:T(8,128)(2,1)S(1)}, u32[]{:S(2)}, u32[]{:S(2)}) %collective-permute-start.7) | collective-permute-done | bytes 786464 | tf_op jit(solution)/shard_map/ppermute | solution.py:384
  59.2 1.8 %collective-permute-start.10 = (bf16[384,256]{1,0:T(8,128)(2,1)S(1)}, bf16[384,256]{1,0:T(8,128)(2,1)S(1)}, u32[]{:S(2)}, u32[]{:S(2)}) collective-permute-start(bf16[384,256]{1,0:T(8,128)(2,1)S(1)} %get-tuple-element.72), channel_id=1, source_target_pairs={{0,8},{4,12},{8,0},{12,4},{1,9},{5,13},{9,1},{13,5},{2,10},{6,14},... | collective-permute-start | bytes 589832 | tf_op jit(solution)/shard_map/ppermute | solution.py:339
  61.0 0.0 collective-permute-done.12.refs_2_
  61.0 0.5 collective-permute-start.8
  61.5 0.0 copy-done.4
  61.5 1.5 %bitcast_add_fusion.base_ref = f32[768,512]{1,0:T(8,128)S(1)} fusion(bf16[768,512]{1,0:T(8,128)(2,1)S(1)} %collective-permute-done.7, bf16[1,768,512]{2,1,0:T(8,128)(2,1)S(1)} %copy-done.4, bf16[2,768,512]{2,1,0:T(8,128)(2,1)} %collective-permute-done.1, s32[]{:T(128)S(6)} %select_n.9, bf16[2,768,512]{2,1,0:T(8,128)(2,1)S(1)} %get-tuple-element.48), kind=kLoop, calls=%fused_computation | loop fusion | flops 2752512 | bytes 4718596 | tf_op jit(solution)/shard_map/add | solution.py:390
  63.0 0.0 collective-permute-done.13.refs_3_
  63.1 0.0 collective-permute-done.11.refs_1_
  63.1 1.5 %finish.2.refs_1_ = bf16[768,512]{1,0:T(8,128)(2,1)} custom-call(bf16[768,1536]{1,0:T(8,128)(2,1)S(1)} %get-tuple-element.42.pick_ref, f32[768,512]{1,0:T(8,128)S(1)} %bitcast_add_fusion.base_ref, f32[768,512]{1,0:T(8,128)S(1)} %get-tuple-element.71.inverse_ref, bf16[384,256]{1,0:T(8,128)(2,1)S(1)} %get-tuple-element.59.refs_0_, ...), custom_call_target="tpu_custom_call" | custom-call | tf_op jit(solution)/shard_map/finish/pallas_call | solution.py:298
  64.6 0.0 collective-permute-done.9.refs_2_
  64.6 2.6 %collective-permute-done.8.refs_1_ = bf16[384,256]{1,0:T(8,128)(2,1)S(1)} collective-permute-done((bf16[384,256]{1,0:T(8,128)(2,1)S(1)}, bf16[384,256]{1,0:T(8,128)(2,1)S(1)}, u32[]{:S(2)}, u32[]{:S(2)}) %collective-permute-start.8) | collective-permute-done | bytes 196640 | tf_op jit(solution)/shard_map/ppermute | solution.py:339
  67.2 0.7 partial.1.base_ref
  67.8 7.3 %collective-permute-done.10.refs_0_ = bf16[384,256]{1,0:T(8,128)(2,1)S(1)} collective-permute-done((bf16[384,256]{1,0:T(8,128)(2,1)S(1)}, bf16[384,256]{1,0:T(8,128)(2,1)S(1)}, u32[]{:S(2)}, u32[]{:S(2)}) %collective-permute-start.10) | collective-permute-done | bytes 196640 | tf_op jit(solution)/shard_map/ppermute | solution.py:339
  75.2 1.1 %finish.3 = bf16[768,512]{1,0:T(8,128)(2,1)} custom-call(bf16[768,1536]{1,0:T(8,128)(2,1)S(1)} %get-tuple-element.42.pick_ref, f32[768,256]{1,0:T(8,128)S(1)} %partial.1.base_ref, f32[768,512]{1,0:T(8,128)S(1)} %get-tuple-element.71.inverse_ref, bf16[384,256]{1,0:T(8,128)(2,1)S(1)} %collective-permute-done.10.refs_0_, ...), custom_call_target="tpu_custom_call", output_to_operand_aliasing={{}: (4, {})} | custom-call | tf_op jit(solution)/shard_map/finish/pallas_call | solution.py:298
  (1 shorter events, 0.0 us)
Async XLA Ops:
  1.7 8.4 %collective-permute-start = (bf16[384,256]{1,0:T(8,128)(2,1)S(1)}, bf16[384,256]{1,0:T(8,128)(2,1)S(1)}, u32[]{:S(2)}, u32[]{:S(2)}) collective-permute-start(bf16[384,256]{1,0:T(8,128)(2,1)S(1)} %get-tuple-element.40), channel_id=1, source_target_pairs={{0,4},{4,0},{8,12},{12,8},{1,5},{5,1},{9,13},{13,9},{2,6},{6,2},{1... | collective-permute-start | bytes 589832 | tf_op jit(solution)/shard_map/ppermute | solution.py:339
  4.8 23.2 %collective-permute-start.5 = (bf16[384,256]{1,0:T(8,128)(2,1)S(1)}, bf16[384,256]{1,0:T(8,128)(2,1)S(1)}, u32[]{:S(2)}, u32[]{:S(2)}) collective-permute-start(bf16[384,256]{1,0:T(8,128)(2,1)S(1)} %get-tuple-element.51), channel_id=1, source_target_pairs={{0,12},{4,8},{8,4},{12,0},{1,13},{5,9},{9,5},{13,1},{2,14},{6,10},... | collective-permute-start | bytes 589832 | tf_op jit(solution)/shard_map/ppermute | solution.py:339
  7.2 26.9 %collective-permute-start.6 = (bf16[384,256]{1,0:T(8,128)(2,1)S(1)}, bf16[384,256]{1,0:T(8,128)(2,1)S(1)}, u32[]{:S(2)}, u32[]{:S(2)}) collective-permute-start(bf16[384,256]{1,0:T(8,128)(2,1)S(1)} %get-tuple-element.52), channel_id=1, source_target_pairs={{0,8},{4,12},{8,0},{12,4},{1,9},{5,13},{9,1},{13,5},{2,10},{6,14},... | collective-permute-start | bytes 589832 | tf_op jit(solution)/shard_map/ppermute | solution.py:339
  12.6 30.1 %collective-permute-start.2 = (bf16[384,256]{1,0:T(8,128)(2,1)}, bf16[384,256]{1,0:T(8,128)(2,1)}, u32[]{:S(2)}, u32[]{:S(2)}) collective-permute-start(bf16[384,256]{1,0:T(8,128)(2,1)} %get-tuple-element.43), channel_id=1, source_target_pairs={{0,12},{4,8},{8,4},{12,0},{1,13},{5,9},{9,5},{13,1},{2,14},{6,10},... | collective-permute-start | bytes 589832 | tf_op jit(solution)/shard_map/ppermute | solution.py:339
  19.4 31.8 %collective-permute-start.3 = (bf16[384,256]{1,0:T(8,128)(2,1)}, bf16[384,256]{1,0:T(8,128)(2,1)}, u32[]{:S(2)}, u32[]{:S(2)}) collective-permute-start(bf16[384,256]{1,0:T(8,128)(2,1)} %get-tuple-element.44), channel_id=1, source_target_pairs={{0,8},{4,12},{8,0},{12,4},{1,9},{5,13},{9,1},{13,5},{2,10},{6,14},... | collective-permute-start | bytes 589832 | tf_op jit(solution)/shard_map/ppermute | solution.py:339
  19.4 31.9 %collective-permute-start.4 = (bf16[384,256]{1,0:T(8,128)(2,1)}, bf16[384,256]{1,0:T(8,128)(2,1)}, u32[]{:S(2)}, u32[]{:S(2)}) collective-permute-start(bf16[384,256]{1,0:T(8,128)(2,1)} %get-tuple-element.45), channel_id=1, source_target_pairs={{0,4},{4,0},{8,12},{12,8},{1,5},{5,1},{9,13},{13,9},{2,6},{6,2},{1... | collective-permute-start | bytes 589832 | tf_op jit(solution)/shard_map/ppermute | solution.py:339
  28.0 8.1 %copy-start.3 = (bf16[1536,1536]{1,0:T(8,128)(2,1)}, bf16[1536,1536]{1,0:T(8,128)(2,1)S(1)}, u32[]{:S(2)}) copy-start(bf16[1536,1536]{1,0:T(8,128)(2,1)S(1)} %get-tuple-element.50.operator_ref) | copy-start | bytes 14155780
  28.0 10.3 %collective-permute-start.1 = (bf16[2,768,512]{2,1,0:T(8,128)(2,1)}, bf16[2,768,512]{2,1,0:T(8,128)(2,1)}, u32[]{:S(2)}, u32[]{:S(2)}) collective-permute-start(bf16[2,768,512]{2,1,0:T(8,128)(2,1)} %get-tuple-element.49), channel_id=1, source_target_pairs={{0,1},{1,0},{2,3},{3,2},{4,5},{5,4},{6,7},{7,6},{8,9},{9,8},{10,11... | collective-permute-start | bytes 4718600 | tf_op jit(solution)/shard_map/ppermute | solution.py:366
  34.2 2.8 %copy-start.2 = (f32[512]{0:T(512)S(1)}, f32[512]{0:T(512)}, u32[]{:S(2)}) copy-start(f32[512]{0:T(512)} %param.15) | copy-start | bytes 6148
  36.1 0.7 copy-start
  36.8 24.2 %collective-permute-start.12 = (bf16[384,256]{1,0:T(8,128)(2,1)}, bf16[384,256]{1,0:T(8,128)(2,1)S(1)}, u32[]{:S(2)}, u32[]{:S(2)}) collective-permute-start(bf16[384,256]{1,0:T(8,128)(2,1)} %get-tuple-element.55), channel_id=1, source_target_pairs={{0,8},{4,12},{8,0},{12,4},{1,9},{5,13},{9,1},{13,5},{2,10},{6,14},... | collective-permute-start | bytes 589832 | tf_op jit(solution)/shard_map/ppermute | solution.py:339
  37.0 14.3 %slice-start = ((s8[4718592]{0:T(1024)(128)(4,1)}), s8[4194304]{0:T(1024)(128)(4,1)S(1)}, s32[]{:S(2)}) async-start(s8[4718592]{0:T(1024)(128)(4,1)} %bitcast.19), calls=%async_computation | async-start | bytes 8388608
  37.0 1.4 %copy-start.1 = (bf16[384,256]{1,0:T(8,128)(2,1)S(1)}, bf16[384,256]{1,0:T(8,128)(2,1)}, u32[]{:S(2)}) copy-start(bf16[384,256]{1,0:T(8,128)(2,1)} %copy-done) | copy-start | bytes 589828
  37.0 14.3 %slice-start.1 = ((s8[4718592]{0:T(1024)(128)(4,1)}), s8[524288]{0:T(1024)(128)(4,1)S(1)}, s32[]{:S(2)}) async-start(s8[4718592]{0:T(1024)(128)(4,1)} %bitcast.19), calls=%async_computation.1 | async-start | bytes 1048576
  38.4 24.7 %collective-permute-start.13 = (bf16[384,256]{1,0:T(8,128)(2,1)S(1)}, bf16[384,256]{1,0:T(8,128)(2,1)S(1)}, u32[]{:S(2)}, u32[]{:S(2)}) collective-permute-start(bf16[384,256]{1,0:T(8,128)(2,1)S(1)} %copy-done.1), channel_id=1, source_target_pairs={{0,12},{4,8},{8,4},{12,0},{1,13},{5,9},{9,5},{13,1},{2,14},{6,10},... | collective-permute-start | bytes 589832 | tf_op jit(solution)/shard_map/ppermute | solution.py:339
  42.7 18.8 %copy-start.4 = (bf16[1,768,512]{2,1,0:T(8,128)(2,1)S(1)}, bf16[1,768,512]{2,1,0:T(8,128)(2,1)}, u32[]{:S(2)}) copy-start(bf16[1,768,512]{2,1,0:T(8,128)(2,1)} %param.9) | copy-start | bytes 2359300
  42.8 16.4 %collective-permute-start.7 = (bf16[768,512]{1,0:T(8,128)(2,1)S(1)}, bf16[768,512]{1,0:T(8,128)(2,1)S(1)}, u32[]{:S(2)}, u32[]{:S(2)}) collective-permute-start(bf16[768,512]{1,0:T(8,128)(2,1)S(1)} %fusion), channel_id=1, source_target_pairs={{0,2},{2,0},{1,3},{3,1},{4,6},{6,4},{5,7},{7,5},{8,10},{10,8},{9,1... | collective-permute-start | bytes 2359304 | tf_op jit(solution)/shard_map/ppermute | solution.py:384
  51.1 11.9 %collective-permute-start.11 = (bf16[384,256]{1,0:T(8,128)(2,1)S(1)}, bf16[384,256]{1,0:T(8,128)(2,1)S(1)}, u32[]{:S(2)}, u32[]{:S(2)}) collective-permute-start(bf16[384,256]{1,0:T(8,128)(2,1)S(1)} %get-tuple-element.58), channel_id=1, source_target_pairs={{0,4},{4,0},{8,12},{12,8},{1,5},{5,1},{9,13},{13,9},{2,6},{6,2},{1... | collective-permute-start | bytes 589832 | tf_op jit(solution)/shard_map/ppermute | solution.py:339
  53.9 10.7 %collective-permute-start.9 = (bf16[384,256]{1,0:T(8,128)(2,1)S(1)}, bf16[384,256]{1,0:T(8,128)(2,1)S(1)}, u32[]{:S(2)}, u32[]{:S(2)}) collective-permute-start(bf16[384,256]{1,0:T(8,128)(2,1)S(1)} %get-tuple-element.70), channel_id=1, source_target_pairs={{0,12},{4,8},{8,4},{12,0},{1,13},{5,9},{9,5},{13,1},{2,14},{6,10},... | collective-permute-start | bytes 589832 | tf_op jit(solution)/shard_map/ppermute | solution.py:339
  59.2 16.0 %collective-permute-start.10 = (bf16[384,256]{1,0:T(8,128)(2,1)S(1)}, bf16[384,256]{1,0:T(8,128)(2,1)S(1)}, u32[]{:S(2)}, u32[]{:S(2)}) collective-permute-start(bf16[384,256]{1,0:T(8,128)(2,1)S(1)} %get-tuple-element.72), channel_id=1, source_target_pairs={{0,8},{4,12},{8,0},{12,4},{1,9},{5,13},{9,1},{13,5},{2,10},{6,14},... | collective-permute-start | bytes 589832 | tf_op jit(solution)/shard_map/ppermute | solution.py:339
  61.0 6.2 %collective-permute-start.8 = (bf16[384,256]{1,0:T(8,128)(2,1)S(1)}, bf16[384,256]{1,0:T(8,128)(2,1)S(1)}, u32[]{:S(2)}, u32[]{:S(2)}) collective-permute-start(bf16[384,256]{1,0:T(8,128)(2,1)S(1)} %get-tuple-element.69), channel_id=1, source_target_pairs={{0,4},{4,0},{8,12},{12,8},{1,5},{5,1},{9,13},{13,9},{2,6},{6,2},{1... | collective-permute-start | bytes 589832 | tf_op jit(solution)/shard_map/ppermute | solution.py:339

commit v16 on v15

--- a/solution.py
+++ b/solution.py
@@ -1,4 +1,5 @@
 import functools
+import math
 
 import jax
 import jax.numpy as jnp
@@ -75,9 +76,9 @@
         target = slots_of(route_ref[...], send, max(16, chan_count))
         outs[0][...] = target
     offsets = block_offsets(paired, chan_count, block_rows)
-    slot = lax.broadcasted_iota(jnp.int32, (block_rows, target.shape[1]), 0)
-    for i, (k, first, width) in enumerate(items):
-        pick = selection(slot == target - offsets[k])
+    for i, (k, low, slots, first, width) in enumerate(items):
+        slot = lax.broadcasted_iota(jnp.int32, (slots, target.shape[1]), 0)
+        pick = selection(slot == target - (offsets[k] + low))
         if i == 0:
             amps_copy.wait()
         block_refs[i][...] = jnp.dot(
@@ -87,12 +88,12 @@
 
 def pack(plan, given, route_row, amps, name):
     rows = amps.shape[0]
-    block_rows, items = plan[3], plan[4]
-    columns = max(first + width for _, first, width in items)
+    items = plan[4]
+    columns = max(first + width for *_, first, width in items)
     extra = [] if given else [pltpu.VMEM((1, rows), jnp.int32)]
     return pl.pallas_call(
         functools.partial(pack_kernel, plan, given),
-        out_shape=extra + [pltpu.VMEM((block_rows, width), BF16) for _, _, width in items],
+        out_shape=extra + [pltpu.VMEM((slots, width), BF16) for _, _, slots, _, width in items],
         in_specs=[whole() if given else whole(pl.ANY), whole(pl.ANY)],
         out_specs=[whole()] * (len(extra) + len(items)),
         scratch_shapes=[
@@ -201,29 +202,30 @@
     return outs[:sub_count], outs[sub_count]
 
 
-def cycle_kernel(half, plan, operator_ref, *refs):
-    paired, chan_count, _, _ = plan
-    count = len(refs) // 2
-    in_refs, out_refs, block_ref = refs[:count], refs[count : 2 * count], refs[2 * count]
-    block_rows, width = out_refs[0].shape
+def cycle_kernel(half, plan, places, operator_ref, *refs):
+    paired, chan_count, _, block_rows = plan
+    in_refs, out_refs, block_ref = refs[: len(places)], refs[len(places) : -1], refs[-1]
+    width = out_refs[0].shape[1]
     offsets = block_offsets(paired, chan_count, block_rows)
-    starts = [pl.multiple_of(offsets[count - 1 - i], block_rows) for i in range(count)]
-    for in_ref, start in zip(in_refs, starts):
+    starts = [pl.multiple_of(offset, block_rows) for offset in reversed(offsets)]
+    for in_ref, (k, low) in zip(in_refs, places):
         part = in_ref[...] if in_ref.shape[1] == width else in_ref[:, pl.ds(half * width, width)]
-        block_ref[pl.ds(start, block_rows), :] = part
+        start = pl.multiple_of(offsets[k] + low, math.gcd(low, block_rows))
+        block_ref[pl.ds(start, in_ref.shape[0]), :] = part
     for out_ref, start in zip(out_refs, starts):
         out_ref[...] = jnp.dot(
             operator_ref[pl.ds(start, block_rows), :], block_ref[...], preferred_element_type=F32
         ).astype(BF16)
 
 
-def apply_cycle(half, plan, operator, arrays, width):
-    block_rows = arrays[0].shape[0]
+def apply_cycle(half, plan, operator, places, arrays, width):
+    block_rows = plan[3]
+    count = operator.shape[0] // block_rows
     return pl.pallas_call(
-        functools.partial(cycle_kernel, half, plan),
-        out_shape=[jax.ShapeDtypeStruct((block_rows, width), BF16)] * len(arrays),
+        functools.partial(cycle_kernel, half, plan, places),
+        out_shape=[jax.ShapeDtypeStruct((block_rows, width), BF16)] * count,
         in_specs=[whole()] * (1 + len(arrays)),
-        out_specs=[whole()] * len(arrays),
+        out_specs=[whole()] * count,
         scratch_shapes=[pltpu.VMEM((operator.shape[0], width), BF16)],
         compiler_params=params(),
         cost_estimate=DEAR,
@@ -343,17 +345,19 @@
     width = holes // HALVES
     route_row = route[0].reshape(1, rows)
     plan = (paired, chan_count, send, block_rows)
-    early = [(k, 0, width) for k in far_first if k or not paired]
-    late = [(k, h * width, width) for h in range(1, HALVES) for k in far_first if k or not paired]
-    late += [(0, 0, holes)] if paired else []
+    leading = 128 if paired and count > 2 and block_rows > 128 else block_rows
+    early = [(k, 0, block_rows, 0, width) for k in far_first if k or not paired]
+    if leading < block_rows:
+        early[:1] = [(early[0][0], 0, leading, 0, width), (early[0][0], leading, block_rows - leading, 0, width)]
+    late = [(k, 0, block_rows, h * width, width) for h in range(1, HALVES) for k in far_first if k or not paired]
+    late += [(0, 0, block_rows, 0, holes)] if paired else []
     target, *blocks = pack(plan + (early,), False, route_row, amps, "pack_first")
-    arrived = {(k, 0): exchange(block, k) for (k, _, _), block in zip(early, blocks)}
+    arrived = {item: exchange(block, item[0]) for item, block in zip(early, blocks)}
     if paired:
-        near = (1, 0)
-        target, arrived[near] = lax.optimization_barrier((target, arrived[near]))
+        first = early[0]
+        target, arrived[first] = lax.optimization_barrier((target, arrived[first]))
     blocks = pack(plan + (late,), True, target, amps, "pack_rest")
-    for (k, first, _), block in zip(late, blocks):
-        arrived[(k, first // width)] = exchange(block, k)
+    arrived.update({item: exchange(block, item[0]) for item, block in zip(late, blocks)})
 
     part_column, hole_row = gap_part[0].reshape(rows, 1), gap_hole.reshape(1, holes)
     amps, blocks = lax.optimization_barrier((amps, blocks))
@@ -373,10 +377,11 @@
     terms = [chip_sum(lax.rem(lad + step, lad_count)).astype(BF16) for step in range(1, lad_count)]
     returned, crossed = [], []
     for half in range(HALVES):
-        blocks = [arrived[(k, half if k or not paired else 0)] for k in far_first]
+        here = [item for item in early + late if item[3] == half * width or item[4] > width]
+        blocks = [arrived[item] for item in here]
         if returned:
             blocks, made = lax.optimization_barrier((blocks, made))
-        made = apply_cycle(half, plan, operator, blocks, width)
+        made = apply_cycle(half, plan, operator, [item[:2] for item in here], blocks, width)
         if not returned:
             behind, terms = lax.optimization_barrier((made[2:], terms))
             for step, term in enumerate(terms, 1):

time: 76.6 us -> 75.6 us (0.987)
  starting transfers between devices: 23.1 us -> 29.4 us
  other arithmetic: 2.94 us -> 0.7 us
  waiting for transfers between devices: 27 us -> 24.8 us
  Pallas kernels: 21.2 us -> 19.2 us
    ppermute x12 -> x13, starting transfers between devices: 21.5 us -> 27.9 us  [exchange(): lax.ppermute(block, 'chan', [(i, i ^ k) for i in range(chan_count)])]
    ppermute x12 -> x13, waiting for transfers between devices: 24.6 us -> 19.3 us  [exchange(): lax.ppermute(block, 'chan', [(i, i ^ k) for i in range(chan_count)])]
    ppermute x1, waiting for transfers between devices: 2.41 us -> 5.16 us  [body(): crossed.append(lax.ppermute(term, 'lad', pairs))]
    pallas_call x2, Pallas kernels: 4.49 us -> 2.88 us  [apply_cycle(): pl.pallas_call(functools.partial(cycle_kernel, half, plan, places), out_s...]
    convert_element_type x1, other arithmetic: 1.34 us -> 0.21 us  [body(): chip_sum(lax.rem(lad + step, lad_count)).astype(BF16)]
    add x1, other arithmetic: 1.52 us -> 0.41 us  [body(): base = base + term.astype(F32)]
  transfers between devices with their start and end apart: 14 -> 15, of which waited for: 6 -> 6; matrix products, arithmetic and copies ran while one was open for 5% -> 2% of each run, Pallas kernels for 24% -> 22%
where the time goes in v16:
time: 75.6 us; the launch traced here: 75.3 us
  starting transfers between devices  29.4 us (39%)
  waiting for transfers between devices  24.8 us (33%)
  Pallas kernels  19.2 us (25%)
  local copies, waits for them, and re-layouts  1.05 us (1%)
    ppermute x13, starting transfers between devices, exchange(): lax.ppermute(block, 'chan', [(i, i ^ k) for i in range(chan_count)])  27.9 us
    ppermute x13, waiting for transfers between devices, exchange(): lax.ppermute(block, 'chan', [(i, i ^ k) for i in range(chan_count)])  19.3 us
    pallas_call x1, Pallas kernels, prepare(): pl.pallas_call(functools.partial(prepare_kernel, sub_count), out_shape=[j...  7.97 us
    ppermute x1, waiting for transfers between devices, body(): crossed.append(lax.ppermute(term, 'lad', pairs))  5.16 us
    pallas_call x2, Pallas kernels, pack(): pl.pallas_call(functools.partial(pack_kernel, plan, given), out_shape=ext...  3.76 us
    pallas_call x2, Pallas kernels, apply_cycle(): pl.pallas_call(functools.partial(cycle_kernel, half, plan, places), out_s...  2.88 us
    pallas_call x2, Pallas kernels, finish(): pl.pallas_call(functools.partial(finish_kernel, half * width, tuple(place...  2.6 us
    ppermute x1, starting transfers between devices, body(): crossed.append(lax.ppermute(term, 'lad', pairs))  1.56 us
  transfers between devices with their start and end apart: 15, of which 6 were waited for; matrix products, arithmetic and copies ran while one was open for 2% of the time, Pallas kernels for 22%

profile of v16, /device:TPU:0, one launch (start us, length us, event | category | flops | bytes accessed | tf_op | source)
XLA Modules:
  0.0 75.3 jit_solution(5545778499093032622)
XLA Ops:
  0.0 1.7 %pack_first.1 = (s32[1,768]{1,0:T(1,128)S(1)}, bf16[128,256]{1,0:T(8,128)(2,1)S(1)}, bf16[256,256]{1,0:T(8,128)(2,1)S(1)}, bf16[384,256]{1,0:T(8,128)(2,1)S(1)}, bf16[384,256]{1,0:T(8,128)(2,1)S(1)}) custom-call(s32[1,768]{1,0:T(1,128)} %bitcast.22, bf16[768,512]{1,0:T(8,128)(2,1)} %bitcast.19), custom_call_target="tpu_custom_call" | custom-call | tf_op jit(solution)/shard_map/pack_first/pallas_call | solution.py:94
  1.7 5.1 %collective-permute-start = (bf16[128,256]{1,0:T(8,128)(2,1)S(1)}, bf16[128,256]{1,0:T(8,128)(2,1)S(1)}, u32[]{:S(2)}, u32[]{:S(2)}) collective-permute-start(bf16[128,256]{1,0:T(8,128)(2,1)S(1)} %get-tuple-element.41), channel_id=1, source_target_pairs={{0,12},{4,8},{8,4},{12,0},{1,13},{5,9},{9,5},{13,1},{2,14},{6,10},... | collective-permute-start | bytes 196616 | tf_op jit(solution)/shard_map/ppermute | solution.py:341
  6.8 0.0 collective-permute-start.6
  6.8 0.6 collective-permute-start.7
  7.4 3.7 %collective-permute-start.5 = (bf16[256,256]{1,0:T(8,128)(2,1)S(1)}, bf16[256,256]{1,0:T(8,128)(2,1)S(1)}, u32[]{:S(2)}, u32[]{:S(2)}) collective-permute-start(bf16[256,256]{1,0:T(8,128)(2,1)S(1)} %get-tuple-element.53), channel_id=1, source_target_pairs={{0,12},{4,8},{8,4},{12,0},{1,13},{5,9},{9,5},{13,1},{2,14},{6,10},... | collective-permute-start | bytes 393224 | tf_op jit(solution)/shard_map/ppermute | solution.py:341
  11.2 0.9 %copy.11.part_ref = f32[768,1]{1,0:T(8,128)S(1)} copy(f32[768,1]{0,1:T(1,128)} %bitcast.23) | data formatting | bytes 6144 | tf_op jit(solution)/shard_map/reshape;squeeze | solution.py:362
  12.1 0.1 add_multiply_fusion.off_ref
  12.1 0.0 collective-permute-done.refs_0_
  12.1 2.1 %pack_rest.1 = (bf16[384,256]{1,0:T(8,128)(2,1)S(1)}, bf16[384,256]{1,0:T(8,128)(2,1)S(1)}, bf16[384,256]{1,0:T(8,128)(2,1)S(1)}, bf16[384,512]{1,0:T(8,128)(2,1)S(1)}) custom-call(s32[1,768]{1,0:T(1,128)S(1)} %get-tuple-element.42.route_in, bf16[768,512]{1,0:T(8,128)(2,1)} %bitcast.20), custom_call_target="tpu_custom_call" | custom-call | tf_op jit(solution)/shard_map/pack_rest/pallas_call | solution.py:94
  14.2 1.5 %collective-permute-start.2 = (bf16[384,256]{1,0:T(8,128)(2,1)S(1)}, bf16[384,256]{1,0:T(8,128)(2,1)S(1)}, u32[]{:S(2)}, u32[]{:S(2)}) collective-permute-start(bf16[384,256]{1,0:T(8,128)(2,1)S(1)} %get-tuple-element.44), channel_id=1, source_target_pairs={{0,12},{4,8},{8,4},{12,0},{1,13},{5,9},{9,5},{13,1},{2,14},{6,10},... | collective-permute-start | bytes 589832 | tf_op jit(solution)/shard_map/ppermute | solution.py:341
  15.8 2.5 %collective-permute-start.3 = (bf16[384,256]{1,0:T(8,128)(2,1)S(1)}, bf16[384,256]{1,0:T(8,128)(2,1)S(1)}, u32[]{:S(2)}, u32[]{:S(2)}) collective-permute-start(bf16[384,256]{1,0:T(8,128)(2,1)S(1)} %get-tuple-element.45), channel_id=1, source_target_pairs={{0,8},{4,12},{8,0},{12,4},{1,9},{5,13},{9,1},{13,5},{2,10},{6,14},... | collective-permute-start | bytes 589832 | tf_op jit(solution)/shard_map/ppermute | solution.py:341
  18.3 0.2 copy.10.target_ref
  18.5 0.0 copy-start
  18.5 8.0 %prepare.1 = (bf16[2,768,512]{2,1,0:T(8,128)(2,1)S(1)}, bf16[2,768,512]{2,1,0:T(8,128)(2,1)S(1)}, bf16[1536,1536]{1,0:T(8,128)(2,1)S(1)}) custom-call(bf16[3072,768]{1,0:T(8,128)(2,1)} %bitcast.24, bf16[768,512]{1,0:T(8,128)(2,1)} %bitcast.21, bf16[1536,1536]{1,0:T(8,128)(2,1)} %bitcast.25, bf16[12,128,128]{2,1,0:T(8,128)(2,1)} %bitcast.26), custom_call_target="tpu_custom_call" | custom-call | flops 30000001024 | bytes 1000000 | tf_op jit(solution)/shard_map/prepare/pallas_call | solution.py:183
  26.4 0.0 copy-done
  26.5 1.3 %unpack_matrix.1 = (bf16[768,1536]{1,0:T(8,128)(2,1)S(1)}, f32[768,512]{1,0:T(8,128)S(1)}) custom-call(s32[4]{0:T(128)S(1)} %add_multiply_fusion.off_ref, s32[768,1]{1,0:T(8,128)S(1)} %copy.10.target_ref, f32[768,1]{1,0:T(8,128)S(1)} %copy.11.part_ref, f32[1,512]{1,0:T(1,128)S(1)} %bitcast.18), custom_call_target="tpu_custom_call" | custom-call | flops 30000001024 | bytes 1000000 | tf_op jit(solution)/shard_map/unpack_matrix/pallas_call | solution.py:122
  27.8 0.0 collective-permute-done.5.refs_1_
  27.8 5.3 %collective-permute-start.4 = (bf16[384,256]{1,0:T(8,128)(2,1)S(1)}, bf16[384,256]{1,0:T(8,128)(2,1)S(1)}, u32[]{:S(2)}, u32[]{:S(2)}) collective-permute-start(bf16[384,256]{1,0:T(8,128)(2,1)S(1)} %get-tuple-element.46), channel_id=1, source_target_pairs={{0,4},{4,0},{8,12},{12,8},{1,5},{5,1},{9,13},{13,9},{2,6},{6,2},{1... | collective-permute-start | bytes 589832 | tf_op jit(solution)/shard_map/ppermute | solution.py:341
  33.1 0.0 collective-permute-done.6.refs_2_
  33.1 0.0 collective-permute-start.1
  33.1 0.0 collective-permute-done.7.refs_3_
  33.1 1.4 %apply_cycle.2 = (bf16[384,256]{1,0:T(8,128)(2,1)S(1)}, bf16[384,256]{1,0:T(8,128)(2,1)S(1)}, bf16[384,256]{1,0:T(8,128)(2,1)S(1)}, bf16[384,256]{1,0:T(8,128)(2,1)S(1)}) custom-call(bf16[1536,1536]{1,0:T(8,128)(2,1)S(1)} %get-tuple-element.51.operator_ref, bf16[128,256]{1,0:T(8,128)(2,1)S(1)} %collective-permute-done.refs_0_, ...), custom_call_target="tpu_custom_call" | custom-call | flops 30000001024 | bytes 1000000 | tf_op jit(solution)/shard_map/apply_cycle/pallas_call | solution.py:224
  34.6 1.6 %collective-permute-start.13 = (bf16[384,256]{1,0:T(8,128)(2,1)S(1)}, bf16[384,256]{1,0:T(8,128)(2,1)S(1)}, u32[]{:S(2)}, u32[]{:S(2)}) collective-permute-start(bf16[384,256]{1,0:T(8,128)(2,1)S(1)} %get-tuple-element.57), channel_id=1, source_target_pairs={{0,8},{4,12},{8,0},{12,4},{1,9},{5,13},{9,1},{13,5},{2,10},{6,14},... | collective-permute-start | bytes 589832 | tf_op jit(solution)/shard_map/ppermute | solution.py:341
  36.2 0.4 collective-permute-done.1
  36.5 3.0 %collective-permute-start.14 = (bf16[384,256]{1,0:T(8,128)(2,1)S(1)}, bf16[384,256]{1,0:T(8,128)(2,1)S(1)}, u32[]{:S(2)}, u32[]{:S(2)}) collective-permute-start(bf16[384,256]{1,0:T(8,128)(2,1)S(1)} %get-tuple-element.56), channel_id=1, source_target_pairs={{0,12},{4,8},{8,4},{12,0},{1,13},{5,9},{9,5},{13,1},{2,14},{6,10},... | collective-permute-start | bytes 589832 | tf_op jit(solution)/shard_map/ppermute | solution.py:341
  39.5 0.2 fusion
  39.7 0.0 copy-start.1
  39.7 0.0 collective-permute-done.2.refs_0_
  39.7 1.6 %collective-permute-start.8 = (bf16[768,512]{1,0:T(8,128)(2,1)S(1)}, bf16[768,512]{1,0:T(8,128)(2,1)S(1)}, u32[]{:S(2)}, u32[]{:S(2)}) collective-permute-start(bf16[768,512]{1,0:T(8,128)(2,1)S(1)} %fusion), channel_id=1, source_target_pairs={{0,2},{2,0},{1,3},{3,1},{4,6},{6,4},{5,7},{7,5},{8,10},{10,8},{9,1... | collective-permute-start | bytes 2359304 | tf_op jit(solution)/shard_map/ppermute | solution.py:389
  41.3 8.2 %collective-permute-done.3.refs_1_ = bf16[384,256]{1,0:T(8,128)(2,1)S(1)} collective-permute-done((bf16[384,256]{1,0:T(8,128)(2,1)S(1)}, bf16[384,256]{1,0:T(8,128)(2,1)S(1)}, u32[]{:S(2)}, u32[]{:S(2)}) %collective-permute-start.3) | collective-permute-done | bytes 196640 | tf_op jit(solution)/shard_map/ppermute | solution.py:341
  49.5 0.1 collective-permute-start.12
  49.6 0.0 collective-permute-done.4.refs_2_
  49.6 1.4 %apply_cycle.3 = (bf16[384,256]{1,0:T(8,128)(2,1)S(1)}, bf16[384,256]{1,0:T(8,128)(2,1)S(1)}, bf16[384,256]{1,0:T(8,128)(2,1)S(1)}, bf16[384,256]{1,0:T(8,128)(2,1)S(1)}) custom-call(bf16[1536,1536]{1,0:T(8,128)(2,1)S(1)} %get-tuple-element.51.operator_ref, bf16[384,256]{1,0:T(8,128)(2,1)S(1)} %collective-permute-done.2.refs_0_, ...), custom_call_target="tpu_custom_call" | custom-call | flops 30000001024 | bytes 1000000 | tf_op jit(solution)/shard_map/apply_cycle/pallas_call | solution.py:224
  51.1 2.9 %collective-permute-start.10 = (bf16[384,256]{1,0:T(8,128)(2,1)S(1)}, bf16[384,256]{1,0:T(8,128)(2,1)S(1)}, u32[]{:S(2)}, u32[]{:S(2)}) collective-permute-start(bf16[384,256]{1,0:T(8,128)(2,1)S(1)} %get-tuple-element.72), channel_id=1, source_target_pairs={{0,12},{4,8},{8,4},{12,0},{1,13},{5,9},{9,5},{13,1},{2,14},{6,10},... | collective-permute-start | bytes 589832 | tf_op jit(solution)/shard_map/ppermute | solution.py:341
  53.9 5.2 %collective-permute-done.8 = bf16[768,512]{1,0:T(8,128)(2,1)S(1)} collective-permute-done((bf16[768,512]{1,0:T(8,128)(2,1)S(1)}, bf16[768,512]{1,0:T(8,128)(2,1)S(1)}, u32[]{:S(2)}, u32[]{:S(2)}) %collective-permute-start.8) | collective-permute-done | bytes 786464 | tf_op jit(solution)/shard_map/ppermute | solution.py:389
  59.1 0.2 collective-permute-start.11
  59.3 0.0 collective-permute-done.13.refs_2_
  59.3 1.2 %collective-permute-start.9 = (bf16[384,256]{1,0:T(8,128)(2,1)S(1)}, bf16[384,256]{1,0:T(8,128)(2,1)S(1)}, u32[]{:S(2)}, u32[]{:S(2)}) collective-permute-start(bf16[384,256]{1,0:T(8,128)(2,1)S(1)} %get-tuple-element.71), channel_id=1, source_target_pairs={{0,4},{4,0},{8,12},{12,8},{1,5},{5,1},{9,13},{13,9},{2,6},{6,2},{1... | collective-permute-start | bytes 589832 | tf_op jit(solution)/shard_map/ppermute | solution.py:341
  60.5 0.0 copy-done.1
  60.5 0.4 bitcast_add_fusion.base_ref
  61.0 0.0 collective-permute-done.14.refs_3_
  61.0 0.8 %collective-permute-done.12.refs_1_ = bf16[384,256]{1,0:T(8,128)(2,1)S(1)} collective-permute-done((bf16[384,256]{1,0:T(8,128)(2,1)S(1)}, bf16[384,256]{1,0:T(8,128)(2,1)S(1)}, u32[]{:S(2)}, u32[]{:S(2)}) %collective-permute-start.12) | collective-permute-done | bytes 196640 | tf_op jit(solution)/shard_map/ppermute | solution.py:341
  61.8 1.5 %finish.2.refs_1_ = bf16[768,512]{1,0:T(8,128)(2,1)} custom-call(bf16[768,1536]{1,0:T(8,128)(2,1)S(1)} %get-tuple-element.43.pick_ref, f32[768,512]{1,0:T(8,128)S(1)} %bitcast_add_fusion.base_ref, f32[768,512]{1,0:T(8,128)S(1)} %get-tuple-element.73.inverse_ref, bf16[384,256]{1,0:T(8,128)(2,1)S(1)} %get-tuple-element.61.refs_0_, ...), custom_call_target="tpu_custom_call" | custom-call | tf_op jit(solution)/shard_map/finish/pallas_call | solution.py:300
  63.3 0.0 collective-permute-done.10.refs_2_
  63.3 3.7 %collective-permute-done.9.refs_1_ = bf16[384,256]{1,0:T(8,128)(2,1)S(1)} collective-permute-done((bf16[384,256]{1,0:T(8,128)(2,1)S(1)}, bf16[384,256]{1,0:T(8,128)(2,1)S(1)}, u32[]{:S(2)}, u32[]{:S(2)}) %collective-permute-start.9) | collective-permute-done | bytes 196640 | tf_op jit(solution)/shard_map/ppermute | solution.py:341
  67.0 0.7 partial.1.base_ref
  67.7 6.6 %collective-permute-done.11.refs_0_ = bf16[384,256]{1,0:T(8,128)(2,1)S(1)} collective-permute-done((bf16[384,256]{1,0:T(8,128)(2,1)S(1)}, bf16[384,256]{1,0:T(8,128)(2,1)S(1)}, u32[]{:S(2)}, u32[]{:S(2)}) %collective-permute-start.11) | collective-permute-done | bytes 196640 | tf_op jit(solution)/shard_map/ppermute | solution.py:341
  74.2 1.1 %finish.3 = bf16[768,512]{1,0:T(8,128)(2,1)} custom-call(bf16[768,1536]{1,0:T(8,128)(2,1)S(1)} %get-tuple-element.43.pick_ref, f32[768,256]{1,0:T(8,128)S(1)} %partial.1.base_ref, f32[768,512]{1,0:T(8,128)S(1)} %get-tuple-element.73.inverse_ref, bf16[384,256]{1,0:T(8,128)(2,1)S(1)} %collective-permute-done.11.refs_0_, ...), custom_call_target="tpu_custom_call", output_to_operand_aliasing={{}: (4, {})} | custom-call | tf_op jit(solution)/shard_map/finish/pallas_call | solution.py:300
Async XLA Ops:
  1.7 10.5 %collective-permute-start = (bf16[128,256]{1,0:T(8,128)(2,1)S(1)}, bf16[128,256]{1,0:T(8,128)(2,1)S(1)}, u32[]{:S(2)}, u32[]{:S(2)}) collective-permute-start(bf16[128,256]{1,0:T(8,128)(2,1)S(1)} %get-tuple-element.41), channel_id=1, source_target_pairs={{0,12},{4,8},{8,4},{12,0},{1,13},{5,9},{9,5},{13,1},{2,14},{6,10},... | collective-permute-start | bytes 196616 | tf_op jit(solution)/shard_map/ppermute | solution.py:341
  6.8 26.3 %collective-permute-start.6 = (bf16[384,256]{1,0:T(8,128)(2,1)S(1)}, bf16[384,256]{1,0:T(8,128)(2,1)S(1)}, u32[]{:S(2)}, u32[]{:S(2)}) collective-permute-start(bf16[384,256]{1,0:T(8,128)(2,1)S(1)} %get-tuple-element.54), channel_id=1, source_target_pairs={{0,8},{4,12},{8,0},{12,4},{1,9},{5,13},{9,1},{13,5},{2,10},{6,14},... | collective-permute-start | bytes 589832 | tf_op jit(solution)/shard_map/ppermute | solution.py:341
  6.8 26.3 %collective-permute-start.7 = (bf16[384,256]{1,0:T(8,128)(2,1)S(1)}, bf16[384,256]{1,0:T(8,128)(2,1)S(1)}, u32[]{:S(2)}, u32[]{:S(2)}) collective-permute-start(bf16[384,256]{1,0:T(8,128)(2,1)S(1)} %get-tuple-element.55), channel_id=1, source_target_pairs={{0,4},{4,0},{8,12},{12,8},{1,5},{5,1},{9,13},{13,9},{2,6},{6,2},{1... | collective-permute-start | bytes 589832 | tf_op jit(solution)/shard_map/ppermute | solution.py:341
  7.4 20.3 %collective-permute-start.5 = (bf16[256,256]{1,0:T(8,128)(2,1)S(1)}, bf16[256,256]{1,0:T(8,128)(2,1)S(1)}, u32[]{:S(2)}, u32[]{:S(2)}) collective-permute-start(bf16[256,256]{1,0:T(8,128)(2,1)S(1)} %get-tuple-element.53), channel_id=1, source_target_pairs={{0,12},{4,8},{8,4},{12,0},{1,13},{5,9},{9,5},{13,1},{2,14},{6,10},... | collective-permute-start | bytes 393224 | tf_op jit(solution)/shard_map/ppermute | solution.py:341
  14.2 25.5 %collective-permute-start.2 = (bf16[384,256]{1,0:T(8,128)(2,1)S(1)}, bf16[384,256]{1,0:T(8,128)(2,1)S(1)}, u32[]{:S(2)}, u32[]{:S(2)}) collective-permute-start(bf16[384,256]{1,0:T(8,128)(2,1)S(1)} %get-tuple-element.44), channel_id=1, source_target_pairs={{0,12},{4,8},{8,4},{12,0},{1,13},{5,9},{9,5},{13,1},{2,14},{6,10},... | collective-permute-start | bytes 589832 | tf_op jit(solution)/shard_map/ppermute | solution.py:341
  15.8 33.7 %collective-permute-start.3 = (bf16[384,256]{1,0:T(8,128)(2,1)S(1)}, bf16[384,256]{1,0:T(8,128)(2,1)S(1)}, u32[]{:S(2)}, u32[]{:S(2)}) collective-permute-start(bf16[384,256]{1,0:T(8,128)(2,1)S(1)} %get-tuple-element.45), channel_id=1, source_target_pairs={{0,8},{4,12},{8,0},{12,4},{1,9},{5,13},{9,1},{13,5},{2,10},{6,14},... | collective-permute-start | bytes 589832 | tf_op jit(solution)/shard_map/ppermute | solution.py:341
  18.5 8.0 %copy-start = (f32[512]{0:T(512)S(1)}, f32[512]{0:T(512)}, u32[]{:S(2)}) copy-start(f32[512]{0:T(512)} %param.15) | copy-start | bytes 6148
  27.8 21.8 %collective-permute-start.4 = (bf16[384,256]{1,0:T(8,128)(2,1)S(1)}, bf16[384,256]{1,0:T(8,128)(2,1)S(1)}, u32[]{:S(2)}, u32[]{:S(2)}) collective-permute-start(bf16[384,256]{1,0:T(8,128)(2,1)S(1)} %get-tuple-element.46), channel_id=1, source_target_pairs={{0,4},{4,0},{8,12},{12,8},{1,5},{5,1},{9,13},{13,9},{2,6},{6,2},{1... | collective-permute-start | bytes 589832 | tf_op jit(solution)/shard_map/ppermute | solution.py:341
  33.1 3.4 %collective-permute-start.1 = (bf16[2,768,512]{2,1,0:T(8,128)(2,1)S(1)}, bf16[2,768,512]{2,1,0:T(8,128)(2,1)S(1)}, u32[]{:S(2)}, u32[]{:S(2)}) collective-permute-start(bf16[2,768,512]{2,1,0:T(8,128)(2,1)S(1)} %get-tuple-element.50), channel_id=1, source_target_pairs={{0,1},{1,0},{2,3},{3,2},{4,5},{5,4},{6,7},{7,6},{8,9},{9,8},{10,11... | collective-permute-start | bytes 4718600 | tf_op jit(solution)/shard_map/ppermute | solution.py:370
  34.6 24.7 %collective-permute-start.13 = (bf16[384,256]{1,0:T(8,128)(2,1)S(1)}, bf16[384,256]{1,0:T(8,128)(2,1)S(1)}, u32[]{:S(2)}, u32[]{:S(2)}) collective-permute-start(bf16[384,256]{1,0:T(8,128)(2,1)S(1)} %get-tuple-element.57), channel_id=1, source_target_pairs={{0,8},{4,12},{8,0},{12,4},{1,9},{5,13},{9,1},{13,5},{2,10},{6,14},... | collective-permute-start | bytes 589832 | tf_op jit(solution)/shard_map/ppermute | solution.py:341
  36.5 24.4 %collective-permute-start.14 = (bf16[384,256]{1,0:T(8,128)(2,1)S(1)}, bf16[384,256]{1,0:T(8,128)(2,1)S(1)}, u32[]{:S(2)}, u32[]{:S(2)}) collective-permute-start(bf16[384,256]{1,0:T(8,128)(2,1)S(1)} %get-tuple-element.56), channel_id=1, source_target_pairs={{0,12},{4,8},{8,4},{12,0},{1,13},{5,9},{9,5},{13,1},{2,14},{6,10},... | collective-permute-start | bytes 589832 | tf_op jit(solution)/shard_map/ppermute | solution.py:341
  39.7 20.8 %copy-start.1 = (bf16[1,768,512]{2,1,0:T(8,128)(2,1)S(1)}, bf16[1,768,512]{2,1,0:T(8,128)(2,1)}, u32[]{:S(2)}) copy-start(bf16[1,768,512]{2,1,0:T(8,128)(2,1)} %param.9) | copy-start | bytes 2359300
  39.7 19.4 %collective-permute-start.8 = (bf16[768,512]{1,0:T(8,128)(2,1)S(1)}, bf16[768,512]{1,0:T(8,128)(2,1)S(1)}, u32[]{:S(2)}, u32[]{:S(2)}) collective-permute-start(bf16[768,512]{1,0:T(8,128)(2,1)S(1)} %fusion), channel_id=1, source_target_pairs={{0,2},{2,0},{1,3},{3,1},{4,6},{6,4},{5,7},{7,5},{8,10},{10,8},{9,1... | collective-permute-start | bytes 2359304 | tf_op jit(solution)/shard_map/ppermute | solution.py:389
  49.5 12.3 %collective-permute-start.12 = (bf16[384,256]{1,0:T(8,128)(2,1)S(1)}, bf16[384,256]{1,0:T(8,128)(2,1)S(1)}, u32[]{:S(2)}, u32[]{:S(2)}) collective-permute-start(bf16[384,256]{1,0:T(8,128)(2,1)S(1)} %get-tuple-element.60), channel_id=1, source_target_pairs={{0,4},{4,0},{8,12},{12,8},{1,5},{5,1},{9,13},{13,9},{2,6},{6,2},{1... | collective-permute-start | bytes 589832 | tf_op jit(solution)/shard_map/ppermute | solution.py:341
  51.1 12.2 %collective-permute-start.10 = (bf16[384,256]{1,0:T(8,128)(2,1)S(1)}, bf16[384,256]{1,0:T(8,128)(2,1)S(1)}, u32[]{:S(2)}, u32[]{:S(2)}) collective-permute-start(bf16[384,256]{1,0:T(8,128)(2,1)S(1)} %get-tuple-element.72), channel_id=1, source_target_pairs={{0,12},{4,8},{8,4},{12,0},{1,13},{5,9},{9,5},{13,1},{2,14},{6,10},... | collective-permute-start | bytes 589832 | tf_op jit(solution)/shard_map/ppermute | solution.py:341
  59.1 15.1 %collective-permute-start.11 = (bf16[384,256]{1,0:T(8,128)(2,1)S(1)}, bf16[384,256]{1,0:T(8,128)(2,1)S(1)}, u32[]{:S(2)}, u32[]{:S(2)}) collective-permute-start(bf16[384,256]{1,0:T(8,128)(2,1)S(1)} %get-tuple-element.74), channel_id=1, source_target_pairs={{0,8},{4,12},{8,0},{12,4},{1,9},{5,13},{9,1},{13,5},{2,10},{6,14},... | collective-permute-start | bytes 589832 | tf_op jit(solution)/shard_map/ppermute | solution.py:341
  59.3 7.7 %collective-permute-start.9 = (bf16[384,256]{1,0:T(8,128)(2,1)S(1)}, bf16[384,256]{1,0:T(8,128)(2,1)S(1)}, u32[]{:S(2)}, u32[]{:S(2)}) collective-permute-start(bf16[384,256]{1,0:T(8,128)(2,1)S(1)} %get-tuple-element.71), channel_id=1, source_target_pairs={{0,4},{4,0},{8,12},{12,8},{1,5},{5,1},{9,13},{13,9},{2,6},{6,2},{1... | collective-permute-start | bytes 589832 | tf_op jit(solution)/shard_map/ppermute | solution.py:341

commit v17 on v16

--- a/solution.py
+++ b/solution.py
@@ -346,10 +346,12 @@
     route_row = route[0].reshape(1, rows)
     plan = (paired, chan_count, send, block_rows)
     leading = 128 if paired and count > 2 and block_rows > 128 else block_rows
-    early = [(k, 0, block_rows, 0, width) for k in far_first if k or not paired]
+    soon = count > 2 and paired
+    early = [(k, 0, block_rows, 0, width) for k in far_first if k > soon or not paired]
     if leading < block_rows:
         early[:1] = [(early[0][0], 0, leading, 0, width), (early[0][0], leading, block_rows - leading, 0, width)]
-    late = [(k, 0, block_rows, h * width, width) for h in range(1, HALVES) for k in far_first if k or not paired]
+    late = [(1, 0, block_rows, 0, width)] if soon else []
+    late += [(k, 0, block_rows, h * width, width) for h in range(1, HALVES) for k in far_first if k or not paired]
     late += [(0, 0, block_rows, 0, holes)] if paired else []
     target, *blocks = pack(plan + (early,), False, route_row, amps, "pack_first")
     arrived = {item: exchange(block, item[0]) for item, block in zip(early, blocks)}

time: 75.6 us -> 75.5 us (level)
    ppermute x13, waiting for transfers between devices: 19.3 us -> 18.4 us  [exchange(): lax.ppermute(block, 'chan', [(i, i ^ k) for i in range(chan_count)])]
where the time goes in v17:
time: 75.5 us; the launch traced here: 75.3 us
  starting transfers between devices  29.6 us (39%)
  waiting for transfers between devices  24.6 us (33%)
  Pallas kernels  19.2 us (25%)
  local copies, waits for them, and re-layouts  1.05 us (1%)
    ppermute x13, starting transfers between devices, exchange(): lax.ppermute(block, 'chan', [(i, i ^ k) for i in range(chan_count)])  28 us
    ppermute x13, waiting for transfers between devices, exchange(): lax.ppermute(block, 'chan', [(i, i ^ k) for i in range(chan_count)])  18.4 us
    pallas_call x1, Pallas kernels, prepare(): pl.pallas_call(functools.partial(prepare_kernel, sub_count), out_shape=[j...  7.96 us
    ppermute x1, waiting for transfers between devices, body(): crossed.append(lax.ppermute(term, 'lad', pairs))  5.47 us
    pallas_call x2, Pallas kernels, pack(): pl.pallas_call(functools.partial(pack_kernel, plan, given), out_shape=ext...  3.75 us
    pallas_call x2, Pallas kernels, apply_cycle(): pl.pallas_call(functools.partial(cycle_kernel, half, plan, places), out_s...  2.88 us
    pallas_call x2, Pallas kernels, finish(): pl.pallas_call(functools.partial(finish_kernel, half * width, tuple(place...  2.6 us
    ppermute x1, starting transfers between devices, body(): crossed.append(lax.ppermute(term, 'lad', pairs))  1.56 us
  transfers between devices with their start and end apart: 15, of which 6 were waited for; matrix products, arithmetic and copies ran while one was open for 2% of the time, Pallas kernels for 22%

profile of v17, /device:TPU:0, one launch (start us, length us, event | category | flops | bytes accessed | tf_op | source)
XLA Modules:
  0.0 75.3 jit_solution(2589359415114390304)
XLA Ops:
  0.0 1.5 %pack_first.1 = (s32[1,768]{1,0:T(1,128)S(1)}, bf16[128,256]{1,0:T(8,128)(2,1)S(1)}, bf16[256,256]{1,0:T(8,128)(2,1)S(1)}, bf16[384,256]{1,0:T(8,128)(2,1)S(1)}) custom-call(s32[1,768]{1,0:T(1,128)} %bitcast.22, bf16[768,512]{1,0:T(8,128)(2,1)} %bitcast.19), custom_call_target="tpu_custom_call" | custom-call | tf_op jit(solution)/shard_map/pack_first/pallas_call | solution.py:94
  1.5 5.1 %collective-permute-start = (bf16[128,256]{1,0:T(8,128)(2,1)S(1)}, bf16[128,256]{1,0:T(8,128)(2,1)S(1)}, u32[]{:S(2)}, u32[]{:S(2)}) collective-permute-start(bf16[128,256]{1,0:T(8,128)(2,1)S(1)} %get-tuple-element.41), channel_id=1, source_target_pairs={{0,12},{4,8},{8,4},{12,0},{1,13},{5,9},{9,5},{13,1},{2,14},{6,10},... | collective-permute-start | bytes 196616 | tf_op jit(solution)/shard_map/ppermute | solution.py:341
  6.6 0.0 collective-permute-start.6
  6.6 1.9 %collective-permute-start.5 = (bf16[256,256]{1,0:T(8,128)(2,1)S(1)}, bf16[256,256]{1,0:T(8,128)(2,1)S(1)}, u32[]{:S(2)}, u32[]{:S(2)}) collective-permute-start(bf16[256,256]{1,0:T(8,128)(2,1)S(1)} %get-tuple-element.54), channel_id=1, source_target_pairs={{0,12},{4,8},{8,4},{12,0},{1,13},{5,9},{9,5},{13,1},{2,14},{6,10},... | collective-permute-start | bytes 393224 | tf_op jit(solution)/shard_map/ppermute | solution.py:341
  8.6 0.9 %copy.11.part_ref = f32[768,1]{1,0:T(8,128)S(1)} copy(f32[768,1]{0,1:T(1,128)} %bitcast.23) | data formatting | bytes 6144 | tf_op jit(solution)/shard_map/reshape;squeeze | solution.py:364
  9.4 0.1 add_multiply_fusion.off_ref
  9.5 0.0 collective-permute-done.refs_0_
  9.5 2.2 %pack_rest.1 = (bf16[384,256]{1,0:T(8,128)(2,1)S(1)}, bf16[384,256]{1,0:T(8,128)(2,1)S(1)}, bf16[384,256]{1,0:T(8,128)(2,1)S(1)}, bf16[384,256]{1,0:T(8,128)(2,1)S(1)}, bf16[384,512]{1,0:T(8,128)(2,1)S(1)}) custom-call(s32[1,768]{1,0:T(1,128)S(1)} %get-tuple-element.42.route_in, bf16[768,512]{1,0:T(8,128)(2,1)} %bitcast.20), custom_call_target="tpu_custom_call" | custom-call | tf_op jit(solution)/shard_map/pack_rest/pallas_call | solution.py:94
  11.8 7.9 %collective-permute-start.7 = (bf16[384,256]{1,0:T(8,128)(2,1)S(1)}, bf16[384,256]{1,0:T(8,128)(2,1)S(1)}, u32[]{:S(2)}, u32[]{:S(2)}) collective-permute-start(bf16[384,256]{1,0:T(8,128)(2,1)S(1)} %get-tuple-element.44), channel_id=1, source_target_pairs={{0,4},{4,0},{8,12},{12,8},{1,5},{5,1},{9,13},{13,9},{2,6},{6,2},{1... | collective-permute-start | bytes 589832 | tf_op jit(solution)/shard_map/ppermute | solution.py:341
  19.7 2.6 %collective-permute-start.2 = (bf16[384,256]{1,0:T(8,128)(2,1)S(1)}, bf16[384,256]{1,0:T(8,128)(2,1)S(1)}, u32[]{:S(2)}, u32[]{:S(2)}) collective-permute-start(bf16[384,256]{1,0:T(8,128)(2,1)S(1)} %get-tuple-element.45), channel_id=1, source_target_pairs={{0,12},{4,8},{8,4},{12,0},{1,13},{5,9},{9,5},{13,1},{2,14},{6,10},... | collective-permute-start | bytes 589832 | tf_op jit(solution)/shard_map/ppermute | solution.py:341
  22.3 0.0 collective-permute-start.3
  22.3 0.2 copy.10.target_ref
  22.4 0.0 copy-start
  22.5 8.0 %prepare.1 = (bf16[2,768,512]{2,1,0:T(8,128)(2,1)S(1)}, bf16[2,768,512]{2,1,0:T(8,128)(2,1)S(1)}, bf16[1536,1536]{1,0:T(8,128)(2,1)S(1)}) custom-call(bf16[3072,768]{1,0:T(8,128)(2,1)} %bitcast.24, bf16[768,512]{1,0:T(8,128)(2,1)} %bitcast.21, bf16[1536,1536]{1,0:T(8,128)(2,1)} %bitcast.25, bf16[12,128,128]{2,1,0:T(8,128)(2,1)} %bitcast.26), custom_call_target="tpu_custom_call" | custom-call | flops 30000001024 | bytes 1000000 | tf_op jit(solution)/shard_map/prepare/pallas_call | solution.py:183
  30.4 0.0 copy-done
  30.4 1.3 %unpack_matrix.1 = (bf16[768,1536]{1,0:T(8,128)(2,1)S(1)}, f32[768,512]{1,0:T(8,128)S(1)}) custom-call(s32[4]{0:T(128)S(1)} %add_multiply_fusion.off_ref, s32[768,1]{1,0:T(8,128)S(1)} %copy.10.target_ref, f32[768,1]{1,0:T(8,128)S(1)} %copy.11.part_ref, f32[1,512]{1,0:T(1,128)S(1)} %bitcast.18), custom_call_target="tpu_custom_call" | custom-call | flops 30000001024 | bytes 1000000 | tf_op jit(solution)/shard_map/unpack_matrix/pallas_call | solution.py:122
  31.8 0.0 collective-permute-done.5.refs_1_
  31.8 1.9 %collective-permute-start.4 = (bf16[384,256]{1,0:T(8,128)(2,1)S(1)}, bf16[384,256]{1,0:T(8,128)(2,1)S(1)}, u32[]{:S(2)}, u32[]{:S(2)}) collective-permute-start(bf16[384,256]{1,0:T(8,128)(2,1)S(1)} %get-tuple-element.47), channel_id=1, source_target_pairs={{0,4},{4,0},{8,12},{12,8},{1,5},{5,1},{9,13},{13,9},{2,6},{6,2},{1... | collective-permute-start | bytes 589832 | tf_op jit(solution)/shard_map/ppermute | solution.py:341
  33.7 0.0 collective-permute-done.6.refs_2_
  33.7 0.0 collective-permute-start.1
  33.7 0.0 collective-permute-done.7.refs_3_
  33.7 1.4 %apply_cycle.2 = (bf16[384,256]{1,0:T(8,128)(2,1)S(1)}, bf16[384,256]{1,0:T(8,128)(2,1)S(1)}, bf16[384,256]{1,0:T(8,128)(2,1)S(1)}, bf16[384,256]{1,0:T(8,128)(2,1)S(1)}) custom-call(bf16[1536,1536]{1,0:T(8,128)(2,1)S(1)} %get-tuple-element.52.operator_ref, bf16[128,256]{1,0:T(8,128)(2,1)S(1)} %collective-permute-done.refs_0_, ...), custom_call_target="tpu_custom_call" | custom-call | flops 30000001024 | bytes 1000000 | tf_op jit(solution)/shard_map/apply_cycle/pallas_call | solution.py:224
  35.1 1.3 %collective-permute-start.13 = (bf16[384,256]{1,0:T(8,128)(2,1)S(1)}, bf16[384,256]{1,0:T(8,128)(2,1)S(1)}, u32[]{:S(2)}, u32[]{:S(2)}) collective-permute-start(bf16[384,256]{1,0:T(8,128)(2,1)S(1)} %get-tuple-element.57), channel_id=1, source_target_pairs={{0,8},{4,12},{8,0},{12,4},{1,9},{5,13},{9,1},{13,5},{2,10},{6,14},... | collective-permute-start | bytes 589832 | tf_op jit(solution)/shard_map/ppermute | solution.py:341
  36.4 0.7 collective-permute-done.1
  37.1 2.6 %collective-permute-start.14 = (bf16[384,256]{1,0:T(8,128)(2,1)S(1)}, bf16[384,256]{1,0:T(8,128)(2,1)S(1)}, u32[]{:S(2)}, u32[]{:S(2)}) collective-permute-start(bf16[384,256]{1,0:T(8,128)(2,1)S(1)} %get-tuple-element.56), channel_id=1, source_target_pairs={{0,12},{4,8},{8,4},{12,0},{1,13},{5,9},{9,5},{13,1},{2,14},{6,10},... | collective-permute-start | bytes 589832 | tf_op jit(solution)/shard_map/ppermute | solution.py:341
  39.6 0.2 fusion
  39.9 0.0 copy-start.1
  39.9 0.0 collective-permute-done.2.refs_0_
  39.9 1.6 %collective-permute-start.8 = (bf16[768,512]{1,0:T(8,128)(2,1)S(1)}, bf16[768,512]{1,0:T(8,128)(2,1)S(1)}, u32[]{:S(2)}, u32[]{:S(2)}) collective-permute-start(bf16[768,512]{1,0:T(8,128)(2,1)S(1)} %fusion), channel_id=1, source_target_pairs={{0,2},{2,0},{1,3},{3,1},{4,6},{6,4},{5,7},{7,5},{8,10},{10,8},{9,1... | collective-permute-start | bytes 2359304 | tf_op jit(solution)/shard_map/ppermute | solution.py:391
  41.4 7.9 %collective-permute-done.3.refs_1_ = bf16[384,256]{1,0:T(8,128)(2,1)S(1)} collective-permute-done((bf16[384,256]{1,0:T(8,128)(2,1)S(1)}, bf16[384,256]{1,0:T(8,128)(2,1)S(1)}, u32[]{:S(2)}, u32[]{:S(2)}) %collective-permute-start.3) | collective-permute-done | bytes 196640 | tf_op jit(solution)/shard_map/ppermute | solution.py:341
  49.4 0.1 collective-permute-start.12
  49.4 0.0 collective-permute-done.4.refs_2_
  49.4 1.4 %apply_cycle.3 = (bf16[384,256]{1,0:T(8,128)(2,1)S(1)}, bf16[384,256]{1,0:T(8,128)(2,1)S(1)}, bf16[384,256]{1,0:T(8,128)(2,1)S(1)}, bf16[384,256]{1,0:T(8,128)(2,1)S(1)}) custom-call(bf16[1536,1536]{1,0:T(8,128)(2,1)S(1)} %get-tuple-element.52.operator_ref, bf16[384,256]{1,0:T(8,128)(2,1)S(1)} %collective-permute-done.2.refs_0_, ...), custom_call_target="tpu_custom_call" | custom-call | flops 30000001024 | bytes 1000000 | tf_op jit(solution)/shard_map/apply_cycle/pallas_call | solution.py:224
  50.9 2.9 %collective-permute-start.10 = (bf16[384,256]{1,0:T(8,128)(2,1)S(1)}, bf16[384,256]{1,0:T(8,128)(2,1)S(1)}, u32[]{:S(2)}, u32[]{:S(2)}) collective-permute-start(bf16[384,256]{1,0:T(8,128)(2,1)S(1)} %get-tuple-element.72), channel_id=1, source_target_pairs={{0,12},{4,8},{8,4},{12,0},{1,13},{5,9},{9,5},{13,1},{2,14},{6,10},... | collective-permute-start | bytes 589832 | tf_op jit(solution)/shard_map/ppermute | solution.py:341
  53.8 5.5 %collective-permute-done.8 = bf16[768,512]{1,0:T(8,128)(2,1)S(1)} collective-permute-done((bf16[768,512]{1,0:T(8,128)(2,1)S(1)}, bf16[768,512]{1,0:T(8,128)(2,1)S(1)}, u32[]{:S(2)}, u32[]{:S(2)}) %collective-permute-start.8) | collective-permute-done | bytes 786464 | tf_op jit(solution)/shard_map/ppermute | solution.py:391
  59.2 0.2 collective-permute-start.11
  59.5 0.0 collective-permute-done.13.refs_2_
  59.5 1.6 %collective-permute-start.9 = (bf16[384,256]{1,0:T(8,128)(2,1)S(1)}, bf16[384,256]{1,0:T(8,128)(2,1)S(1)}, u32[]{:S(2)}, u32[]{:S(2)}) collective-permute-start(bf16[384,256]{1,0:T(8,128)(2,1)S(1)} %get-tuple-element.71), channel_id=1, source_target_pairs={{0,4},{4,0},{8,12},{12,8},{1,5},{5,1},{9,13},{13,9},{2,6},{6,2},{1... | collective-permute-start | bytes 589832 | tf_op jit(solution)/shard_map/ppermute | solution.py:341
  61.1 0.0 copy-done.1
  61.1 0.4 bitcast_add_fusion.base_ref
  61.5 0.0 collective-permute-done.14.refs_3_
  61.5 0.2 collective-permute-done.12.refs_1_
  61.7 1.5 %finish.2.refs_1_ = bf16[768,512]{1,0:T(8,128)(2,1)} custom-call(bf16[768,1536]{1,0:T(8,128)(2,1)S(1)} %get-tuple-element.43.pick_ref, f32[768,512]{1,0:T(8,128)S(1)} %bitcast_add_fusion.base_ref, f32[768,512]{1,0:T(8,128)S(1)} %get-tuple-element.73.inverse_ref, bf16[384,256]{1,0:T(8,128)(2,1)S(1)} %get-tuple-element.61.refs_0_, ...), custom_call_target="tpu_custom_call" | custom-call | tf_op jit(solution)/shard_map/finish/pallas_call | solution.py:300
  63.2 0.0 collective-permute-done.10.refs_2_
  63.2 3.9 %collective-permute-done.9.refs_1_ = bf16[384,256]{1,0:T(8,128)(2,1)S(1)} collective-permute-done((bf16[384,256]{1,0:T(8,128)(2,1)S(1)}, bf16[384,256]{1,0:T(8,128)(2,1)S(1)}, u32[]{:S(2)}, u32[]{:S(2)}) %collective-permute-start.9) | collective-permute-done | bytes 196640 | tf_op jit(solution)/shard_map/ppermute | solution.py:341
  67.1 0.7 partial.1.base_ref
  67.8 6.3 %collective-permute-done.11.refs_0_ = bf16[384,256]{1,0:T(8,128)(2,1)S(1)} collective-permute-done((bf16[384,256]{1,0:T(8,128)(2,1)S(1)}, bf16[384,256]{1,0:T(8,128)(2,1)S(1)}, u32[]{:S(2)}, u32[]{:S(2)}) %collective-permute-start.11) | collective-permute-done | bytes 196640 | tf_op jit(solution)/shard_map/ppermute | solution.py:341
  74.2 1.1 %finish.3 = bf16[768,512]{1,0:T(8,128)(2,1)} custom-call(bf16[768,1536]{1,0:T(8,128)(2,1)S(1)} %get-tuple-element.43.pick_ref, f32[768,256]{1,0:T(8,128)S(1)} %partial.1.base_ref, f32[768,512]{1,0:T(8,128)S(1)} %get-tuple-element.73.inverse_ref, bf16[384,256]{1,0:T(8,128)(2,1)S(1)} %collective-permute-done.11.refs_0_, ...), custom_call_target="tpu_custom_call", output_to_operand_aliasing={{}: (4, {})} | custom-call | tf_op jit(solution)/shard_map/finish/pallas_call | solution.py:300
Async XLA Ops:
  1.5 8.0 %collective-permute-start = (bf16[128,256]{1,0:T(8,128)(2,1)S(1)}, bf16[128,256]{1,0:T(8,128)(2,1)S(1)}, u32[]{:S(2)}, u32[]{:S(2)}) collective-permute-start(bf16[128,256]{1,0:T(8,128)(2,1)S(1)} %get-tuple-element.41), channel_id=1, source_target_pairs={{0,12},{4,8},{8,4},{12,0},{1,13},{5,9},{9,5},{13,1},{2,14},{6,10},... | collective-permute-start | bytes 196616 | tf_op jit(solution)/shard_map/ppermute | solution.py:341
  6.6 27.0 %collective-permute-start.6 = (bf16[384,256]{1,0:T(8,128)(2,1)S(1)}, bf16[384,256]{1,0:T(8,128)(2,1)S(1)}, u32[]{:S(2)}, u32[]{:S(2)}) collective-permute-start(bf16[384,256]{1,0:T(8,128)(2,1)S(1)} %get-tuple-element.55), channel_id=1, source_target_pairs={{0,8},{4,12},{8,0},{12,4},{1,9},{5,13},{9,1},{13,5},{2,10},{6,14},... | collective-permute-start | bytes 589832 | tf_op jit(solution)/shard_map/ppermute | solution.py:341
  6.6 25.1 %collective-permute-start.5 = (bf16[256,256]{1,0:T(8,128)(2,1)S(1)}, bf16[256,256]{1,0:T(8,128)(2,1)S(1)}, u32[]{:S(2)}, u32[]{:S(2)}) collective-permute-start(bf16[256,256]{1,0:T(8,128)(2,1)S(1)} %get-tuple-element.54), channel_id=1, source_target_pairs={{0,12},{4,8},{8,4},{12,0},{1,13},{5,9},{9,5},{13,1},{2,14},{6,10},... | collective-permute-start | bytes 393224 | tf_op jit(solution)/shard_map/ppermute | solution.py:341
  11.8 21.9 %collective-permute-start.7 = (bf16[384,256]{1,0:T(8,128)(2,1)S(1)}, bf16[384,256]{1,0:T(8,128)(2,1)S(1)}, u32[]{:S(2)}, u32[]{:S(2)}) collective-permute-start(bf16[384,256]{1,0:T(8,128)(2,1)S(1)} %get-tuple-element.44), channel_id=1, source_target_pairs={{0,4},{4,0},{8,12},{12,8},{1,5},{5,1},{9,13},{13,9},{2,6},{6,2},{1... | collective-permute-start | bytes 589832 | tf_op jit(solution)/shard_map/ppermute | solution.py:341
  19.7 20.2 %collective-permute-start.2 = (bf16[384,256]{1,0:T(8,128)(2,1)S(1)}, bf16[384,256]{1,0:T(8,128)(2,1)S(1)}, u32[]{:S(2)}, u32[]{:S(2)}) collective-permute-start(bf16[384,256]{1,0:T(8,128)(2,1)S(1)} %get-tuple-element.45), channel_id=1, source_target_pairs={{0,12},{4,8},{8,4},{12,0},{1,13},{5,9},{9,5},{13,1},{2,14},{6,10},... | collective-permute-start | bytes 589832 | tf_op jit(solution)/shard_map/ppermute | solution.py:341
  22.3 27.1 %collective-permute-start.3 = (bf16[384,256]{1,0:T(8,128)(2,1)S(1)}, bf16[384,256]{1,0:T(8,128)(2,1)S(1)}, u32[]{:S(2)}, u32[]{:S(2)}) collective-permute-start(bf16[384,256]{1,0:T(8,128)(2,1)S(1)} %get-tuple-element.46), channel_id=1, source_target_pairs={{0,8},{4,12},{8,0},{12,4},{1,9},{5,13},{9,1},{13,5},{2,10},{6,14},... | collective-permute-start | bytes 589832 | tf_op jit(solution)/shard_map/ppermute | solution.py:341
  22.4 8.0 %copy-start = (f32[512]{0:T(512)S(1)}, f32[512]{0:T(512)}, u32[]{:S(2)}) copy-start(f32[512]{0:T(512)} %param.15) | copy-start | bytes 6148
  31.8 17.7 %collective-permute-start.4 = (bf16[384,256]{1,0:T(8,128)(2,1)S(1)}, bf16[384,256]{1,0:T(8,128)(2,1)S(1)}, u32[]{:S(2)}, u32[]{:S(2)}) collective-permute-start(bf16[384,256]{1,0:T(8,128)(2,1)S(1)} %get-tuple-element.47), channel_id=1, source_target_pairs={{0,4},{4,0},{8,12},{12,8},{1,5},{5,1},{9,13},{13,9},{2,6},{6,2},{1... | collective-permute-start | bytes 589832 | tf_op jit(solution)/shard_map/ppermute | solution.py:341
  33.7 3.4 %collective-permute-start.1 = (bf16[2,768,512]{2,1,0:T(8,128)(2,1)S(1)}, bf16[2,768,512]{2,1,0:T(8,128)(2,1)S(1)}, u32[]{:S(2)}, u32[]{:S(2)}) collective-permute-start(bf16[2,768,512]{2,1,0:T(8,128)(2,1)S(1)} %get-tuple-element.51), channel_id=1, source_target_pairs={{0,1},{1,0},{2,3},{3,2},{4,5},{5,4},{6,7},{7,6},{8,9},{9,8},{10,11... | collective-permute-start | bytes 4718600 | tf_op jit(solution)/shard_map/ppermute | solution.py:372
  35.1 24.4 %collective-permute-start.13 = (bf16[384,256]{1,0:T(8,128)(2,1)S(1)}, bf16[384,256]{1,0:T(8,128)(2,1)S(1)}, u32[]{:S(2)}, u32[]{:S(2)}) collective-permute-start(bf16[384,256]{1,0:T(8,128)(2,1)S(1)} %get-tuple-element.57), channel_id=1, source_target_pairs={{0,8},{4,12},{8,0},{12,4},{1,9},{5,13},{9,1},{13,5},{2,10},{6,14},... | collective-permute-start | bytes 589832 | tf_op jit(solution)/shard_map/ppermute | solution.py:341
  37.1 24.4 %collective-permute-start.14 = (bf16[384,256]{1,0:T(8,128)(2,1)S(1)}, bf16[384,256]{1,0:T(8,128)(2,1)S(1)}, u32[]{:S(2)}, u32[]{:S(2)}) collective-permute-start(bf16[384,256]{1,0:T(8,128)(2,1)S(1)} %get-tuple-element.56), channel_id=1, source_target_pairs={{0,12},{4,8},{8,4},{12,0},{1,13},{5,9},{9,5},{13,1},{2,14},{6,10},... | collective-permute-start | bytes 589832 | tf_op jit(solution)/shard_map/ppermute | solution.py:341
  39.9 21.2 %copy-start.1 = (bf16[1,768,512]{2,1,0:T(8,128)(2,1)S(1)}, bf16[1,768,512]{2,1,0:T(8,128)(2,1)}, u32[]{:S(2)}) copy-start(bf16[1,768,512]{2,1,0:T(8,128)(2,1)} %param.9) | copy-start | bytes 2359300
  39.9 19.4 %collective-permute-start.8 = (bf16[768,512]{1,0:T(8,128)(2,1)S(1)}, bf16[768,512]{1,0:T(8,128)(2,1)S(1)}, u32[]{:S(2)}, u32[]{:S(2)}) collective-permute-start(bf16[768,512]{1,0:T(8,128)(2,1)S(1)} %fusion), channel_id=1, source_target_pairs={{0,2},{2,0},{1,3},{3,1},{4,6},{6,4},{5,7},{7,5},{8,10},{10,8},{9,1... | collective-permute-start | bytes 2359304 | tf_op jit(solution)/shard_map/ppermute | solution.py:391
  49.4 12.3 %collective-permute-start.12 = (bf16[384,256]{1,0:T(8,128)(2,1)S(1)}, bf16[384,256]{1,0:T(8,128)(2,1)S(1)}, u32[]{:S(2)}, u32[]{:S(2)}) collective-permute-start(bf16[384,256]{1,0:T(8,128)(2,1)S(1)} %get-tuple-element.60), channel_id=1, source_target_pairs={{0,4},{4,0},{8,12},{12,8},{1,5},{5,1},{9,13},{13,9},{2,6},{6,2},{1... | collective-permute-start | bytes 589832 | tf_op jit(solution)/shard_map/ppermute | solution.py:341
  50.9 12.3 %collective-permute-start.10 = (bf16[384,256]{1,0:T(8,128)(2,1)S(1)}, bf16[384,256]{1,0:T(8,128)(2,1)S(1)}, u32[]{:S(2)}, u32[]{:S(2)}) collective-permute-start(bf16[384,256]{1,0:T(8,128)(2,1)S(1)} %get-tuple-element.72), channel_id=1, source_target_pairs={{0,12},{4,8},{8,4},{12,0},{1,13},{5,9},{9,5},{13,1},{2,14},{6,10},... | collective-permute-start | bytes 589832 | tf_op jit(solution)/shard_map/ppermute | solution.py:341
  59.2 14.9 %collective-permute-start.11 = (bf16[384,256]{1,0:T(8,128)(2,1)S(1)}, bf16[384,256]{1,0:T(8,128)(2,1)S(1)}, u32[]{:S(2)}, u32[]{:S(2)}) collective-permute-start(bf16[384,256]{1,0:T(8,128)(2,1)S(1)} %get-tuple-element.74), channel_id=1, source_target_pairs={{0,8},{4,12},{8,0},{12,4},{1,9},{5,13},{9,1},{13,5},{2,10},{6,14},... | collective-permute-start | bytes 589832 | tf_op jit(solution)/shard_map/ppermute | solution.py:341
  59.5 7.7 %collective-permute-start.9 = (bf16[384,256]{1,0:T(8,128)(2,1)S(1)}, bf16[384,256]{1,0:T(8,128)(2,1)S(1)}, u32[]{:S(2)}, u32[]{:S(2)}) collective-permute-start(bf16[384,256]{1,0:T(8,128)(2,1)S(1)} %get-tuple-element.71), channel_id=1, source_target_pairs={{0,4},{4,0},{8,12},{12,8},{1,5},{5,1},{9,13},{13,9},{2,6},{6,2},{1... | collective-permute-start | bytes 589832 | tf_op jit(solution)/shard_map/ppermute | solution.py:341

commit v18 on v16

--- a/solution.py
+++ b/solution.py
@@ -277,7 +277,7 @@
     block_rows = arrays[0].shape[0]
     places = list(range(len(arrays)))
     if earlier is not None and len(arrays) > 1:
-        last = min(2, len(arrays) - 1)
+        last = len(arrays) - 1
         places.remove(last)
         base = pl.pallas_call(
             functools.partial(partial_kernel, half * width, tuple(places), tiles),

time: 75.6 us -> 75.8 us (level)
    ppermute x13, waiting for transfers between devices: 19.3 us -> 20.1 us  [exchange(): lax.ppermute(block, 'chan', [(i, i ^ k) for i in range(chan_count)])]
  transfers between devices with their start and end apart: 15 -> 15, of which waited for: 6 -> 5; matrix products, arithmetic and copies ran while one was open for 2% -> 2% of each run, Pallas kernels for 22% -> 22%
where the time goes in v18:
time: 75.8 us; the launch traced here: 75.6 us
  starting transfers between devices  29.4 us (39%)
  waiting for transfers between devices  25.1 us (33%)
  Pallas kernels  19.2 us (25%)
  local copies, waits for them, and re-layouts  1.05 us (1%)
    ppermute x13, starting transfers between devices, exchange(): lax.ppermute(block, 'chan', [(i, i ^ k) for i in range(chan_count)])  27.9 us
    ppermute x13, waiting for transfers between devices, exchange(): lax.ppermute(block, 'chan', [(i, i ^ k) for i in range(chan_count)])  20.1 us
    pallas_call x1, Pallas kernels, prepare(): pl.pallas_call(functools.partial(prepare_kernel, sub_count), out_shape=[j...  7.97 us
    ppermute x1, waiting for transfers between devices, body(): crossed.append(lax.ppermute(term, 'lad', pairs))  4.6 us
    pallas_call x2, Pallas kernels, pack(): pl.pallas_call(functools.partial(pack_kernel, plan, given), out_shape=ext...  3.76 us
    pallas_call x2, Pallas kernels, apply_cycle(): pl.pallas_call(functools.partial(cycle_kernel, half, plan, places), out_s...  2.88 us
    pallas_call x2, Pallas kernels, finish(): pl.pallas_call(functools.partial(finish_kernel, half * width, tuple(place...  2.61 us
    ppermute x1, starting transfers between devices, body(): crossed.append(lax.ppermute(term, 'lad', pairs))  1.56 us
  transfers between devices with their start and end apart: 15, of which 5 were waited for; matrix products, arithmetic and copies ran while one was open for 2% of the time, Pallas kernels for 22%

profile of v18, /device:TPU:0, one launch (start us, length us, event | category | flops | bytes accessed | tf_op | source)
XLA Modules:
  0.0 75.6 jit_solution(12946150008781476111)
XLA Ops:
  0.0 1.7 %pack_first.1 = (s32[1,768]{1,0:T(1,128)S(1)}, bf16[128,256]{1,0:T(8,128)(2,1)S(1)}, bf16[256,256]{1,0:T(8,128)(2,1)S(1)}, bf16[384,256]{1,0:T(8,128)(2,1)S(1)}, bf16[384,256]{1,0:T(8,128)(2,1)S(1)}) custom-call(s32[1,768]{1,0:T(1,128)} %bitcast.22, bf16[768,512]{1,0:T(8,128)(2,1)} %bitcast.19), custom_call_target="tpu_custom_call" | custom-call | tf_op jit(solution)/shard_map/pack_first/pallas_call | solution.py:94
  1.7 5.1 %collective-permute-start = (bf16[128,256]{1,0:T(8,128)(2,1)S(1)}, bf16[128,256]{1,0:T(8,128)(2,1)S(1)}, u32[]{:S(2)}, u32[]{:S(2)}) collective-permute-start(bf16[128,256]{1,0:T(8,128)(2,1)S(1)} %get-tuple-element.41), channel_id=1, source_target_pairs={{0,12},{4,8},{8,4},{12,0},{1,13},{5,9},{9,5},{13,1},{2,14},{6,10},... | collective-permute-start | bytes 196616 | tf_op jit(solution)/shard_map/ppermute | solution.py:341
  6.8 0.0 collective-permute-start.6
  6.8 0.6 collective-permute-start.7
  7.4 3.7 %collective-permute-start.5 = (bf16[256,256]{1,0:T(8,128)(2,1)S(1)}, bf16[256,256]{1,0:T(8,128)(2,1)S(1)}, u32[]{:S(2)}, u32[]{:S(2)}) collective-permute-start(bf16[256,256]{1,0:T(8,128)(2,1)S(1)} %get-tuple-element.53), channel_id=1, source_target_pairs={{0,12},{4,8},{8,4},{12,0},{1,13},{5,9},{9,5},{13,1},{2,14},{6,10},... | collective-permute-start | bytes 393224 | tf_op jit(solution)/shard_map/ppermute | solution.py:341
  11.2 0.9 %copy.11.part_ref = f32[768,1]{1,0:T(8,128)S(1)} copy(f32[768,1]{0,1:T(1,128)} %bitcast.23) | data formatting | bytes 6144 | tf_op jit(solution)/shard_map/reshape;squeeze | solution.py:362
  12.1 0.1 add_multiply_fusion.off_ref
  12.1 0.0 collective-permute-done.refs_0_
  12.1 2.1 %pack_rest.1 = (bf16[384,256]{1,0:T(8,128)(2,1)S(1)}, bf16[384,256]{1,0:T(8,128)(2,1)S(1)}, bf16[384,256]{1,0:T(8,128)(2,1)S(1)}, bf16[384,512]{1,0:T(8,128)(2,1)S(1)}) custom-call(s32[1,768]{1,0:T(1,128)S(1)} %get-tuple-element.42.route_in, bf16[768,512]{1,0:T(8,128)(2,1)} %bitcast.20), custom_call_target="tpu_custom_call" | custom-call | tf_op jit(solution)/shard_map/pack_rest/pallas_call | solution.py:94
  14.2 1.5 %collective-permute-start.2 = (bf16[384,256]{1,0:T(8,128)(2,1)S(1)}, bf16[384,256]{1,0:T(8,128)(2,1)S(1)}, u32[]{:S(2)}, u32[]{:S(2)}) collective-permute-start(bf16[384,256]{1,0:T(8,128)(2,1)S(1)} %get-tuple-element.44), channel_id=1, source_target_pairs={{0,12},{4,8},{8,4},{12,0},{1,13},{5,9},{9,5},{13,1},{2,14},{6,10},... | collective-permute-start | bytes 589832 | tf_op jit(solution)/shard_map/ppermute | solution.py:341
  15.8 2.5 %collective-permute-start.3 = (bf16[384,256]{1,0:T(8,128)(2,1)S(1)}, bf16[384,256]{1,0:T(8,128)(2,1)S(1)}, u32[]{:S(2)}, u32[]{:S(2)}) collective-permute-start(bf16[384,256]{1,0:T(8,128)(2,1)S(1)} %get-tuple-element.45), channel_id=1, source_target_pairs={{0,8},{4,12},{8,0},{12,4},{1,9},{5,13},{9,1},{13,5},{2,10},{6,14},... | collective-permute-start | bytes 589832 | tf_op jit(solution)/shard_map/ppermute | solution.py:341
  18.3 0.2 copy.10.target_ref
  18.5 0.0 copy-start
  18.5 8.0 %prepare.1 = (bf16[2,768,512]{2,1,0:T(8,128)(2,1)S(1)}, bf16[2,768,512]{2,1,0:T(8,128)(2,1)S(1)}, bf16[1536,1536]{1,0:T(8,128)(2,1)S(1)}) custom-call(bf16[3072,768]{1,0:T(8,128)(2,1)} %bitcast.24, bf16[768,512]{1,0:T(8,128)(2,1)} %bitcast.21, bf16[1536,1536]{1,0:T(8,128)(2,1)} %bitcast.25, bf16[12,128,128]{2,1,0:T(8,128)(2,1)} %bitcast.26), custom_call_target="tpu_custom_call" | custom-call | flops 30000001024 | bytes 1000000 | tf_op jit(solution)/shard_map/prepare/pallas_call | solution.py:183
  26.4 0.0 copy-done
  26.5 1.3 %unpack_matrix.1 = (bf16[768,1536]{1,0:T(8,128)(2,1)S(1)}, f32[768,512]{1,0:T(8,128)S(1)}) custom-call(s32[4]{0:T(128)S(1)} %add_multiply_fusion.off_ref, s32[768,1]{1,0:T(8,128)S(1)} %copy.10.target_ref, f32[768,1]{1,0:T(8,128)S(1)} %copy.11.part_ref, f32[1,512]{1,0:T(1,128)S(1)} %bitcast.18), custom_call_target="tpu_custom_call" | custom-call | flops 30000001024 | bytes 1000000 | tf_op jit(solution)/shard_map/unpack_matrix/pallas_call | solution.py:122
  27.8 0.0 collective-permute-done.5.refs_1_
  27.8 5.3 %collective-permute-start.4 = (bf16[384,256]{1,0:T(8,128)(2,1)S(1)}, bf16[384,256]{1,0:T(8,128)(2,1)S(1)}, u32[]{:S(2)}, u32[]{:S(2)}) collective-permute-start(bf16[384,256]{1,0:T(8,128)(2,1)S(1)} %get-tuple-element.46), channel_id=1, source_target_pairs={{0,4},{4,0},{8,12},{12,8},{1,5},{5,1},{9,13},{13,9},{2,6},{6,2},{1... | collective-permute-start | bytes 589832 | tf_op jit(solution)/shard_map/ppermute | solution.py:341
  33.1 0.0 collective-permute-done.6.refs_2_
  33.1 0.0 collective-permute-start.1
  33.1 0.0 collective-permute-done.7.refs_3_
  33.1 1.4 %apply_cycle.2 = (bf16[384,256]{1,0:T(8,128)(2,1)S(1)}, bf16[384,256]{1,0:T(8,128)(2,1)S(1)}, bf16[384,256]{1,0:T(8,128)(2,1)S(1)}, bf16[384,256]{1,0:T(8,128)(2,1)S(1)}) custom-call(bf16[1536,1536]{1,0:T(8,128)(2,1)S(1)} %get-tuple-element.51.operator_ref, bf16[128,256]{1,0:T(8,128)(2,1)S(1)} %collective-permute-done.refs_0_, ...), custom_call_target="tpu_custom_call" | custom-call | flops 30000001024 | bytes 1000000 | tf_op jit(solution)/shard_map/apply_cycle/pallas_call | solution.py:224
  34.6 1.6 %collective-permute-start.13 = (bf16[384,256]{1,0:T(8,128)(2,1)S(1)}, bf16[384,256]{1,0:T(8,128)(2,1)S(1)}, u32[]{:S(2)}, u32[]{:S(2)}) collective-permute-start(bf16[384,256]{1,0:T(8,128)(2,1)S(1)} %get-tuple-element.57), channel_id=1, source_target_pairs={{0,8},{4,12},{8,0},{12,4},{1,9},{5,13},{9,1},{13,5},{2,10},{6,14},... | collective-permute-start | bytes 589832 | tf_op jit(solution)/shard_map/ppermute | solution.py:341
  36.2 0.4 collective-permute-done.1
  36.5 3.0 %collective-permute-start.14 = (bf16[384,256]{1,0:T(8,128)(2,1)S(1)}, bf16[384,256]{1,0:T(8,128)(2,1)S(1)}, u32[]{:S(2)}, u32[]{:S(2)}) collective-permute-start(bf16[384,256]{1,0:T(8,128)(2,1)S(1)} %get-tuple-element.56), channel_id=1, source_target_pairs={{0,12},{4,8},{8,4},{12,0},{1,13},{5,9},{9,5},{13,1},{2,14},{6,10},... | collective-permute-start | bytes 589832 | tf_op jit(solution)/shard_map/ppermute | solution.py:341
  39.5 0.2 fusion
  39.7 0.0 copy-start.1
  39.7 0.0 collective-permute-done.2.refs_0_
  39.7 1.6 %collective-permute-start.8 = (bf16[768,512]{1,0:T(8,128)(2,1)S(1)}, bf16[768,512]{1,0:T(8,128)(2,1)S(1)}, u32[]{:S(2)}, u32[]{:S(2)}) collective-permute-start(bf16[768,512]{1,0:T(8,128)(2,1)S(1)} %fusion), channel_id=1, source_target_pairs={{0,2},{2,0},{1,3},{3,1},{4,6},{6,4},{5,7},{7,5},{8,10},{10,8},{9,1... | collective-permute-start | bytes 2359304 | tf_op jit(solution)/shard_map/ppermute | solution.py:389
  41.3 8.2 %collective-permute-done.3.refs_1_ = bf16[384,256]{1,0:T(8,128)(2,1)S(1)} collective-permute-done((bf16[384,256]{1,0:T(8,128)(2,1)S(1)}, bf16[384,256]{1,0:T(8,128)(2,1)S(1)}, u32[]{:S(2)}, u32[]{:S(2)}) %collective-permute-start.3) | collective-permute-done | bytes 196640 | tf_op jit(solution)/shard_map/ppermute | solution.py:341
  49.5 0.1 collective-permute-start.12
  49.6 0.0 collective-permute-done.4.refs_2_
  49.6 1.4 %apply_cycle.3 = (bf16[384,256]{1,0:T(8,128)(2,1)S(1)}, bf16[384,256]{1,0:T(8,128)(2,1)S(1)}, bf16[384,256]{1,0:T(8,128)(2,1)S(1)}, bf16[384,256]{1,0:T(8,128)(2,1)S(1)}) custom-call(bf16[1536,1536]{1,0:T(8,128)(2,1)S(1)} %get-tuple-element.51.operator_ref, bf16[384,256]{1,0:T(8,128)(2,1)S(1)} %collective-permute-done.2.refs_0_, ...), custom_call_target="tpu_custom_call" | custom-call | flops 30000001024 | bytes 1000000 | tf_op jit(solution)/shard_map/apply_cycle/pallas_call | solution.py:224
  51.1 3.4 %collective-permute-start.10 = (bf16[384,256]{1,0:T(8,128)(2,1)S(1)}, bf16[384,256]{1,0:T(8,128)(2,1)S(1)}, u32[]{:S(2)}, u32[]{:S(2)}) collective-permute-start(bf16[384,256]{1,0:T(8,128)(2,1)S(1)} %get-tuple-element.72), channel_id=1, source_target_pairs={{0,8},{4,12},{8,0},{12,4},{1,9},{5,13},{9,1},{13,5},{2,10},{6,14},... | collective-permute-start | bytes 589832 | tf_op jit(solution)/shard_map/ppermute | solution.py:341
  54.5 4.6 %collective-permute-done.8 = bf16[768,512]{1,0:T(8,128)(2,1)S(1)} collective-permute-done((bf16[768,512]{1,0:T(8,128)(2,1)S(1)}, bf16[768,512]{1,0:T(8,128)(2,1)S(1)}, u32[]{:S(2)}, u32[]{:S(2)}) %collective-permute-start.8) | collective-permute-done | bytes 786464 | tf_op jit(solution)/shard_map/ppermute | solution.py:389
  59.1 0.9 %collective-permute-start.11 = (bf16[384,256]{1,0:T(8,128)(2,1)S(1)}, bf16[384,256]{1,0:T(8,128)(2,1)S(1)}, u32[]{:S(2)}, u32[]{:S(2)}) collective-permute-start(bf16[384,256]{1,0:T(8,128)(2,1)S(1)} %get-tuple-element.74), channel_id=1, source_target_pairs={{0,12},{4,8},{8,4},{12,0},{1,13},{5,9},{9,5},{13,1},{2,14},{6,10},... | collective-permute-start | bytes 589832 | tf_op jit(solution)/shard_map/ppermute | solution.py:341
  60.0 0.0 collective-permute-done.13.refs_2_
  60.0 0.0 collective-permute-start.9
  60.0 0.0 copy-done.1
  60.0 0.4 bitcast_add_fusion.base_ref
  60.4 0.0 collective-permute-done.14.refs_3_
  60.4 0.0 collective-permute-done.12.refs_1_
  60.4 1.5 %finish.2.refs_1_ = bf16[768,512]{1,0:T(8,128)(2,1)} custom-call(bf16[768,1536]{1,0:T(8,128)(2,1)S(1)} %get-tuple-element.43.pick_ref, f32[768,512]{1,0:T(8,128)S(1)} %bitcast_add_fusion.base_ref, f32[768,512]{1,0:T(8,128)S(1)} %get-tuple-element.73.inverse_ref, bf16[384,256]{1,0:T(8,128)(2,1)S(1)} %get-tuple-element.61.refs_0_, ...), custom_call_target="tpu_custom_call" | custom-call | tf_op jit(solution)/shard_map/finish/pallas_call | solution.py:300
  61.9 8.6 %collective-permute-done.10.refs_2_ = bf16[384,256]{1,0:T(8,128)(2,1)S(1)} collective-permute-done((bf16[384,256]{1,0:T(8,128)(2,1)S(1)}, bf16[384,256]{1,0:T(8,128)(2,1)S(1)}, u32[]{:S(2)}, u32[]{:S(2)}) %collective-permute-start.10) | collective-permute-done | bytes 196640 | tf_op jit(solution)/shard_map/ppermute | solution.py:341
  70.6 3.3 %collective-permute-done.9.refs_1_ = bf16[384,256]{1,0:T(8,128)(2,1)S(1)} collective-permute-done((bf16[384,256]{1,0:T(8,128)(2,1)S(1)}, bf16[384,256]{1,0:T(8,128)(2,1)S(1)}, u32[]{:S(2)}, u32[]{:S(2)}) %collective-permute-start.9) | collective-permute-done | bytes 196640 | tf_op jit(solution)/shard_map/ppermute | solution.py:341
  73.8 0.7 partial.1.base_ref
  74.5 0.0 collective-permute-done.11.refs_0_
  74.5 1.1 %finish.3 = bf16[768,512]{1,0:T(8,128)(2,1)} custom-call(bf16[768,1536]{1,0:T(8,128)(2,1)S(1)} %get-tuple-element.43.pick_ref, f32[768,256]{1,0:T(8,128)S(1)} %partial.1.base_ref, f32[768,512]{1,0:T(8,128)S(1)} %get-tuple-element.73.inverse_ref, bf16[384,256]{1,0:T(8,128)(2,1)S(1)} %collective-permute-done.11.refs_0_, ...), custom_call_target="tpu_custom_call", output_to_operand_aliasing={{}: (4, {})} | custom-call | tf_op jit(solution)/shard_map/finish/pallas_call | solution.py:300
Async XLA Ops:
  1.7 10.5 %collective-permute-start = (bf16[128,256]{1,0:T(8,128)(2,1)S(1)}, bf16[128,256]{1,0:T(8,128)(2,1)S(1)}, u32[]{:S(2)}, u32[]{:S(2)}) collective-permute-start(bf16[128,256]{1,0:T(8,128)(2,1)S(1)} %get-tuple-element.41), channel_id=1, source_target_pairs={{0,12},{4,8},{8,4},{12,0},{1,13},{5,9},{9,5},{13,1},{2,14},{6,10},... | collective-permute-start | bytes 196616 | tf_op jit(solution)/shard_map/ppermute | solution.py:341
  6.8 26.3 %collective-permute-start.6 = (bf16[384,256]{1,0:T(8,128)(2,1)S(1)}, bf16[384,256]{1,0:T(8,128)(2,1)S(1)}, u32[]{:S(2)}, u32[]{:S(2)}) collective-permute-start(bf16[384,256]{1,0:T(8,128)(2,1)S(1)} %get-tuple-element.54), channel_id=1, source_target_pairs={{0,8},{4,12},{8,0},{12,4},{1,9},{5,13},{9,1},{13,5},{2,10},{6,14},... | collective-permute-start | bytes 589832 | tf_op jit(solution)/shard_map/ppermute | solution.py:341
  6.8 26.3 %collective-permute-start.7 = (bf16[384,256]{1,0:T(8,128)(2,1)S(1)}, bf16[384,256]{1,0:T(8,128)(2,1)S(1)}, u32[]{:S(2)}, u32[]{:S(2)}) collective-permute-start(bf16[384,256]{1,0:T(8,128)(2,1)S(1)} %get-tuple-element.55), channel_id=1, source_target_pairs={{0,4},{4,0},{8,12},{12,8},{1,5},{5,1},{9,13},{13,9},{2,6},{6,2},{1... | collective-permute-start | bytes 589832 | tf_op jit(solution)/shard_map/ppermute | solution.py:341
  7.4 20.3 %collective-permute-start.5 = (bf16[256,256]{1,0:T(8,128)(2,1)S(1)}, bf16[256,256]{1,0:T(8,128)(2,1)S(1)}, u32[]{:S(2)}, u32[]{:S(2)}) collective-permute-start(bf16[256,256]{1,0:T(8,128)(2,1)S(1)} %get-tuple-element.53), channel_id=1, source_target_pairs={{0,12},{4,8},{8,4},{12,0},{1,13},{5,9},{9,5},{13,1},{2,14},{6,10},... | collective-permute-start | bytes 393224 | tf_op jit(solution)/shard_map/ppermute | solution.py:341
  14.2 25.5 %collective-permute-start.2 = (bf16[384,256]{1,0:T(8,128)(2,1)S(1)}, bf16[384,256]{1,0:T(8,128)(2,1)S(1)}, u32[]{:S(2)}, u32[]{:S(2)}) collective-permute-start(bf16[384,256]{1,0:T(8,128)(2,1)S(1)} %get-tuple-element.44), channel_id=1, source_target_pairs={{0,12},{4,8},{8,4},{12,0},{1,13},{5,9},{9,5},{13,1},{2,14},{6,10},... | collective-permute-start | bytes 589832 | tf_op jit(solution)/shard_map/ppermute | solution.py:341
  15.8 33.7 %collective-permute-start.3 = (bf16[384,256]{1,0:T(8,128)(2,1)S(1)}, bf16[384,256]{1,0:T(8,128)(2,1)S(1)}, u32[]{:S(2)}, u32[]{:S(2)}) collective-permute-start(bf16[384,256]{1,0:T(8,128)(2,1)S(1)} %get-tuple-element.45), channel_id=1, source_target_pairs={{0,8},{4,12},{8,0},{12,4},{1,9},{5,13},{9,1},{13,5},{2,10},{6,14},... | collective-permute-start | bytes 589832 | tf_op jit(solution)/shard_map/ppermute | solution.py:341
  18.5 8.0 %copy-start = (f32[512]{0:T(512)S(1)}, f32[512]{0:T(512)}, u32[]{:S(2)}) copy-start(f32[512]{0:T(512)} %param.15) | copy-start | bytes 6148
  27.8 21.8 %collective-permute-start.4 = (bf16[384,256]{1,0:T(8,128)(2,1)S(1)}, bf16[384,256]{1,0:T(8,128)(2,1)S(1)}, u32[]{:S(2)}, u32[]{:S(2)}) collective-permute-start(bf16[384,256]{1,0:T(8,128)(2,1)S(1)} %get-tuple-element.46), channel_id=1, source_target_pairs={{0,4},{4,0},{8,12},{12,8},{1,5},{5,1},{9,13},{13,9},{2,6},{6,2},{1... | collective-permute-start | bytes 589832 | tf_op jit(solution)/shard_map/ppermute | solution.py:341
  33.1 3.4 %collective-permute-start.1 = (bf16[2,768,512]{2,1,0:T(8,128)(2,1)S(1)}, bf16[2,768,512]{2,1,0:T(8,128)(2,1)S(1)}, u32[]{:S(2)}, u32[]{:S(2)}) collective-permute-start(bf16[2,768,512]{2,1,0:T(8,128)(2,1)S(1)} %get-tuple-element.50), channel_id=1, source_target_pairs={{0,1},{1,0},{2,3},{3,2},{4,5},{5,4},{6,7},{7,6},{8,9},{9,8},{10,11... | collective-permute-start | bytes 4718600 | tf_op jit(solution)/shard_map/ppermute | solution.py:370
  34.6 25.4 %collective-permute-start.13 = (bf16[384,256]{1,0:T(8,128)(2,1)S(1)}, bf16[384,256]{1,0:T(8,128)(2,1)S(1)}, u32[]{:S(2)}, u32[]{:S(2)}) collective-permute-start(bf16[384,256]{1,0:T(8,128)(2,1)S(1)} %get-tuple-element.57), channel_id=1, source_target_pairs={{0,8},{4,12},{8,0},{12,4},{1,9},{5,13},{9,1},{13,5},{2,10},{6,14},... | collective-permute-start | bytes 589832 | tf_op jit(solution)/shard_map/ppermute | solution.py:341
  36.5 23.9 %collective-permute-start.14 = (bf16[384,256]{1,0:T(8,128)(2,1)S(1)}, bf16[384,256]{1,0:T(8,128)(2,1)S(1)}, u32[]{:S(2)}, u32[]{:S(2)}) collective-permute-start(bf16[384,256]{1,0:T(8,128)(2,1)S(1)} %get-tuple-element.56), channel_id=1, source_target_pairs={{0,12},{4,8},{8,4},{12,0},{1,13},{5,9},{9,5},{13,1},{2,14},{6,10},... | collective-permute-start | bytes 589832 | tf_op jit(solution)/shard_map/ppermute | solution.py:341
  39.7 20.3 %copy-start.1 = (bf16[1,768,512]{2,1,0:T(8,128)(2,1)S(1)}, bf16[1,768,512]{2,1,0:T(8,128)(2,1)}, u32[]{:S(2)}) copy-start(bf16[1,768,512]{2,1,0:T(8,128)(2,1)} %param.9) | copy-start | bytes 2359300
  39.7 19.4 %collective-permute-start.8 = (bf16[768,512]{1,0:T(8,128)(2,1)S(1)}, bf16[768,512]{1,0:T(8,128)(2,1)S(1)}, u32[]{:S(2)}, u32[]{:S(2)}) collective-permute-start(bf16[768,512]{1,0:T(8,128)(2,1)S(1)} %fusion), channel_id=1, source_target_pairs={{0,2},{2,0},{1,3},{3,1},{4,6},{6,4},{5,7},{7,5},{8,10},{10,8},{9,1... | collective-permute-start | bytes 2359304 | tf_op jit(solution)/shard_map/ppermute | solution.py:389
  49.5 10.9 %collective-permute-start.12 = (bf16[384,256]{1,0:T(8,128)(2,1)S(1)}, bf16[384,256]{1,0:T(8,128)(2,1)S(1)}, u32[]{:S(2)}, u32[]{:S(2)}) collective-permute-start(bf16[384,256]{1,0:T(8,128)(2,1)S(1)} %get-tuple-element.60), channel_id=1, source_target_pairs={{0,4},{4,0},{8,12},{12,8},{1,5},{5,1},{9,13},{13,9},{2,6},{6,2},{1... | collective-permute-start | bytes 589832 | tf_op jit(solution)/shard_map/ppermute | solution.py:341
  51.1 19.5 %collective-permute-start.10 = (bf16[384,256]{1,0:T(8,128)(2,1)S(1)}, bf16[384,256]{1,0:T(8,128)(2,1)S(1)}, u32[]{:S(2)}, u32[]{:S(2)}) collective-permute-start(bf16[384,256]{1,0:T(8,128)(2,1)S(1)} %get-tuple-element.72), channel_id=1, source_target_pairs={{0,8},{4,12},{8,0},{12,4},{1,9},{5,13},{9,1},{13,5},{2,10},{6,14},... | collective-permute-start | bytes 589832 | tf_op jit(solution)/shard_map/ppermute | solution.py:341
  59.1 15.4 %collective-permute-start.11 = (bf16[384,256]{1,0:T(8,128)(2,1)S(1)}, bf16[384,256]{1,0:T(8,128)(2,1)S(1)}, u32[]{:S(2)}, u32[]{:S(2)}) collective-permute-start(bf16[384,256]{1,0:T(8,128)(2,1)S(1)} %get-tuple-element.74), channel_id=1, source_target_pairs={{0,12},{4,8},{8,4},{12,0},{1,13},{5,9},{9,5},{13,1},{2,14},{6,10},... | collective-permute-start | bytes 589832 | tf_op jit(solution)/shard_map/ppermute | solution.py:341
  60.0 13.9 %collective-permute-start.9 = (bf16[384,256]{1,0:T(8,128)(2,1)S(1)}, bf16[384,256]{1,0:T(8,128)(2,1)S(1)}, u32[]{:S(2)}, u32[]{:S(2)}) collective-permute-start(bf16[384,256]{1,0:T(8,128)(2,1)S(1)} %get-tuple-element.71), channel_id=1, source_target_pairs={{0,4},{4,0},{8,12},{12,8},{1,5},{5,1},{9,13},{13,9},{2,6},{6,2},{1... | collective-permute-start | bytes 589832 | tf_op jit(solution)/shard_map/ppermute | solution.py:341

commit v19 on v18

--- a/solution.py
+++ b/solution.py
@@ -277,7 +277,7 @@
     block_rows = arrays[0].shape[0]
     places = list(range(len(arrays)))
     if earlier is not None and len(arrays) > 1:
-        last = len(arrays) - 1
+        last = 1
         places.remove(last)
         base = pl.pallas_call(
             functools.partial(partial_kernel, half * width, tuple(places), tiles),
@@ -384,12 +384,13 @@
         made = apply_cycle(half, plan, operator, [item[:2] for item in here], blocks, width)
         if not returned:
             behind, terms = lax.optimization_barrier((made[2:], terms))
+            made = [*made[:2], *behind]
             for step, term in enumerate(terms, 1):
                 pairs = [(i, (i + step) % lad_count) for i in range(lad_count)]
                 crossed.append(lax.ppermute(term, "lad", pairs))
         else:
-            behind, crossed = lax.optimization_barrier((made[2:], crossed))
-        made = [*made[:2], *behind]
+            behind, crossed = lax.optimization_barrier((made[0], crossed))
+            made = [behind, *made[1:]]
         returned.append([exchange(block, k) for k, block in zip(far_first, made)])
     for term in crossed:
         base = base + term.astype(F32)

time: 75.8 us -> 74.6 us (0.984)
  waiting for transfers between devices: 25.1 us -> 23.1 us
  starting transfers between devices: 29.4 us -> 30.2 us
    ppermute x13, waiting for transfers between devices: 20.1 us -> 18.1 us  [exchange(): lax.ppermute(block, 'chan', [(i, i ^ k) for i in range(chan_count)])]
    ppermute x13, starting transfers between devices: 27.9 us -> 28.7 us  [exchange(): lax.ppermute(block, 'chan', [(i, i ^ k) for i in range(chan_count)])]
where the time goes in v19:
time: 74.6 us; the launch traced here: 74.4 us
  starting transfers between devices  30.2 us (40%)
  waiting for transfers between devices  23.1 us (31%)
  Pallas kernels  19.2 us (26%)
  local copies, waits for them, and re-layouts  1.05 us (1%)
    ppermute x13, starting transfers between devices, exchange(): lax.ppermute(block, 'chan', [(i, i ^ k) for i in range(chan_count)])  28.7 us
    ppermute x13, waiting for transfers between devices, exchange(): lax.ppermute(block, 'chan', [(i, i ^ k) for i in range(chan_count)])  18.1 us
    pallas_call x1, Pallas kernels, prepare(): pl.pallas_call(functools.partial(prepare_kernel, sub_count), out_shape=[j...  7.97 us
    ppermute x1, waiting for transfers between devices, body(): crossed.append(lax.ppermute(term, 'lad', pairs))  4.6 us
    pallas_call x2, Pallas kernels, pack(): pl.pallas_call(functools.partial(pack_kernel, plan, given), out_shape=ext...  3.76 us
    pallas_call x2, Pallas kernels, apply_cycle(): pl.pallas_call(functools.partial(cycle_kernel, half, plan, places), out_s...  2.88 us
    pallas_call x2, Pallas kernels, finish(): pl.pallas_call(functools.partial(finish_kernel, half * width, tuple(place...  2.6 us
    ppermute x1, starting transfers between devices, body(): crossed.append(lax.ppermute(term, 'lad', pairs))  1.56 us
  transfers between devices with their start and end apart: 15, of which 5 were waited for; matrix products, arithmetic and copies ran while one was open for 2% of the time, Pallas kernels for 22%

profile of v19, /device:TPU:0, one launch (start us, length us, event | category | flops | bytes accessed | tf_op | source)
XLA Modules:
  0.0 74.4 jit_solution(9364480302100896282)
XLA Ops:
  0.0 1.7 %pack_first.1 = (s32[1,768]{1,0:T(1,128)S(1)}, bf16[128,256]{1,0:T(8,128)(2,1)S(1)}, bf16[256,256]{1,0:T(8,128)(2,1)S(1)}, bf16[384,256]{1,0:T(8,128)(2,1)S(1)}, bf16[384,256]{1,0:T(8,128)(2,1)S(1)}) custom-call(s32[1,768]{1,0:T(1,128)} %bitcast.22, bf16[768,512]{1,0:T(8,128)(2,1)} %bitcast.19), custom_call_target="tpu_custom_call" | custom-call | tf_op jit(solution)/shard_map/pack_first/pallas_call | solution.py:94
  1.7 5.1 %collective-permute-start = (bf16[128,256]{1,0:T(8,128)(2,1)S(1)}, bf16[128,256]{1,0:T(8,128)(2,1)S(1)}, u32[]{:S(2)}, u32[]{:S(2)}) collective-permute-start(bf16[128,256]{1,0:T(8,128)(2,1)S(1)} %get-tuple-element.40), channel_id=1, source_target_pairs={{0,12},{4,8},{8,4},{12,0},{1,13},{5,9},{9,5},{13,1},{2,14},{6,10},... | collective-permute-start | bytes 196616 | tf_op jit(solution)/shard_map/ppermute | solution.py:341
  6.8 0.0 collective-permute-start.6
  6.8 0.6 collective-permute-start.7
  7.4 3.7 %collective-permute-start.5 = (bf16[256,256]{1,0:T(8,128)(2,1)S(1)}, bf16[256,256]{1,0:T(8,128)(2,1)S(1)}, u32[]{:S(2)}, u32[]{:S(2)}) collective-permute-start(bf16[256,256]{1,0:T(8,128)(2,1)S(1)} %get-tuple-element.52), channel_id=1, source_target_pairs={{0,12},{4,8},{8,4},{12,0},{1,13},{5,9},{9,5},{13,1},{2,14},{6,10},... | collective-permute-start | bytes 393224 | tf_op jit(solution)/shard_map/ppermute | solution.py:341
  11.2 0.9 %copy.11.part_ref = f32[768,1]{1,0:T(8,128)S(1)} copy(f32[768,1]{0,1:T(1,128)} %bitcast.23) | data formatting | bytes 6144 | tf_op jit(solution)/shard_map/reshape;squeeze | solution.py:362
  12.1 0.1 add_multiply_fusion.off_ref
  12.1 0.0 collective-permute-done.refs_0_
  12.1 2.1 %pack_rest.1 = (bf16[384,256]{1,0:T(8,128)(2,1)S(1)}, bf16[384,256]{1,0:T(8,128)(2,1)S(1)}, bf16[384,256]{1,0:T(8,128)(2,1)S(1)}, bf16[384,512]{1,0:T(8,128)(2,1)S(1)}) custom-call(s32[1,768]{1,0:T(1,128)S(1)} %get-tuple-element.41.route_in, bf16[768,512]{1,0:T(8,128)(2,1)} %bitcast.20), custom_call_target="tpu_custom_call" | custom-call | tf_op jit(solution)/shard_map/pack_rest/pallas_call | solution.py:94
  14.2 1.5 %collective-permute-start.2 = (bf16[384,256]{1,0:T(8,128)(2,1)S(1)}, bf16[384,256]{1,0:T(8,128)(2,1)S(1)}, u32[]{:S(2)}, u32[]{:S(2)}) collective-permute-start(bf16[384,256]{1,0:T(8,128)(2,1)S(1)} %get-tuple-element.43), channel_id=1, source_target_pairs={{0,12},{4,8},{8,4},{12,0},{1,13},{5,9},{9,5},{13,1},{2,14},{6,10},... | collective-permute-start | bytes 589832 | tf_op jit(solution)/shard_map/ppermute | solution.py:341
  15.8 2.5 %collective-permute-start.3 = (bf16[384,256]{1,0:T(8,128)(2,1)S(1)}, bf16[384,256]{1,0:T(8,128)(2,1)S(1)}, u32[]{:S(2)}, u32[]{:S(2)}) collective-permute-start(bf16[384,256]{1,0:T(8,128)(2,1)S(1)} %get-tuple-element.44), channel_id=1, source_target_pairs={{0,8},{4,12},{8,0},{12,4},{1,9},{5,13},{9,1},{13,5},{2,10},{6,14},... | collective-permute-start | bytes 589832 | tf_op jit(solution)/shard_map/ppermute | solution.py:341
  18.3 0.2 copy.10.target_ref
  18.5 0.0 copy-start
  18.5 8.0 %prepare.1 = (bf16[2,768,512]{2,1,0:T(8,128)(2,1)S(1)}, bf16[2,768,512]{2,1,0:T(8,128)(2,1)S(1)}, bf16[1536,1536]{1,0:T(8,128)(2,1)S(1)}) custom-call(bf16[3072,768]{1,0:T(8,128)(2,1)} %bitcast.24, bf16[768,512]{1,0:T(8,128)(2,1)} %bitcast.21, bf16[1536,1536]{1,0:T(8,128)(2,1)} %bitcast.25, bf16[12,128,128]{2,1,0:T(8,128)(2,1)} %bitcast.26), custom_call_target="tpu_custom_call" | custom-call | flops 30000001024 | bytes 1000000 | tf_op jit(solution)/shard_map/prepare/pallas_call | solution.py:183
  26.4 0.0 copy-done
  26.5 1.3 %unpack_matrix.1 = (bf16[768,1536]{1,0:T(8,128)(2,1)S(1)}, f32[768,512]{1,0:T(8,128)S(1)}) custom-call(s32[4]{0:T(128)S(1)} %add_multiply_fusion.off_ref, s32[768,1]{1,0:T(8,128)S(1)} %copy.10.target_ref, f32[768,1]{1,0:T(8,128)S(1)} %copy.11.part_ref, f32[1,512]{1,0:T(1,128)S(1)} %bitcast.18), custom_call_target="tpu_custom_call" | custom-call | flops 30000001024 | bytes 1000000 | tf_op jit(solution)/shard_map/unpack_matrix/pallas_call | solution.py:122
  27.8 0.0 collective-permute-done.5.refs_1_
  27.8 5.3 %collective-permute-start.4 = (bf16[384,256]{1,0:T(8,128)(2,1)S(1)}, bf16[384,256]{1,0:T(8,128)(2,1)S(1)}, u32[]{:S(2)}, u32[]{:S(2)}) collective-permute-start(bf16[384,256]{1,0:T(8,128)(2,1)S(1)} %get-tuple-element.45), channel_id=1, source_target_pairs={{0,4},{4,0},{8,12},{12,8},{1,5},{5,1},{9,13},{13,9},{2,6},{6,2},{1... | collective-permute-start | bytes 589832 | tf_op jit(solution)/shard_map/ppermute | solution.py:341
  33.1 0.0 collective-permute-done.6.refs_2_
  33.1 0.0 collective-permute-start.1
  33.1 0.0 collective-permute-done.7.refs_3_
  33.1 1.4 %apply_cycle.2 = (bf16[384,256]{1,0:T(8,128)(2,1)S(1)}, bf16[384,256]{1,0:T(8,128)(2,1)S(1)}, bf16[384,256]{1,0:T(8,128)(2,1)S(1)}, bf16[384,256]{1,0:T(8,128)(2,1)S(1)}) custom-call(bf16[1536,1536]{1,0:T(8,128)(2,1)S(1)} %get-tuple-element.50.operator_ref, bf16[128,256]{1,0:T(8,128)(2,1)S(1)} %collective-permute-done.refs_0_, ...), custom_call_target="tpu_custom_call" | custom-call | flops 30000001024 | bytes 1000000 | tf_op jit(solution)/shard_map/apply_cycle/pallas_call | solution.py:224
  34.6 1.6 %collective-permute-start.13 = (bf16[384,256]{1,0:T(8,128)(2,1)S(1)}, bf16[384,256]{1,0:T(8,128)(2,1)S(1)}, u32[]{:S(2)}, u32[]{:S(2)}) collective-permute-start(bf16[384,256]{1,0:T(8,128)(2,1)S(1)} %get-tuple-element.56), channel_id=1, source_target_pairs={{0,8},{4,12},{8,0},{12,4},{1,9},{5,13},{9,1},{13,5},{2,10},{6,14},... | collective-permute-start | bytes 589832 | tf_op jit(solution)/shard_map/ppermute | solution.py:341
  36.2 0.4 collective-permute-done.1
  36.5 3.0 %collective-permute-start.14 = (bf16[384,256]{1,0:T(8,128)(2,1)S(1)}, bf16[384,256]{1,0:T(8,128)(2,1)S(1)}, u32[]{:S(2)}, u32[]{:S(2)}) collective-permute-start(bf16[384,256]{1,0:T(8,128)(2,1)S(1)} %get-tuple-element.55), channel_id=1, source_target_pairs={{0,12},{4,8},{8,4},{12,0},{1,13},{5,9},{9,5},{13,1},{2,14},{6,10},... | collective-permute-start | bytes 589832 | tf_op jit(solution)/shard_map/ppermute | solution.py:341
  39.5 0.2 fusion
  39.7 0.0 copy-start.1
  39.7 0.0 collective-permute-done.2.refs_0_
  39.7 1.6 %collective-permute-start.8 = (bf16[768,512]{1,0:T(8,128)(2,1)S(1)}, bf16[768,512]{1,0:T(8,128)(2,1)S(1)}, u32[]{:S(2)}, u32[]{:S(2)}) collective-permute-start(bf16[768,512]{1,0:T(8,128)(2,1)S(1)} %fusion), channel_id=1, source_target_pairs={{0,2},{2,0},{1,3},{3,1},{4,6},{6,4},{5,7},{7,5},{8,10},{10,8},{9,1... | collective-permute-start | bytes 2359304 | tf_op jit(solution)/shard_map/ppermute | solution.py:390
  41.3 8.2 %collective-permute-done.3.refs_1_ = bf16[384,256]{1,0:T(8,128)(2,1)S(1)} collective-permute-done((bf16[384,256]{1,0:T(8,128)(2,1)S(1)}, bf16[384,256]{1,0:T(8,128)(2,1)S(1)}, u32[]{:S(2)}, u32[]{:S(2)}) %collective-permute-start.3) | collective-permute-done | bytes 196640 | tf_op jit(solution)/shard_map/ppermute | solution.py:341
  49.5 0.1 collective-permute-start.12
  49.6 0.0 collective-permute-done.4.refs_2_
  49.6 1.4 %apply_cycle.3 = (bf16[384,256]{1,0:T(8,128)(2,1)S(1)}, bf16[384,256]{1,0:T(8,128)(2,1)S(1)}, bf16[384,256]{1,0:T(8,128)(2,1)S(1)}, bf16[384,256]{1,0:T(8,128)(2,1)S(1)}) custom-call(bf16[1536,1536]{1,0:T(8,128)(2,1)S(1)} %get-tuple-element.50.operator_ref, bf16[384,256]{1,0:T(8,128)(2,1)S(1)} %collective-permute-done.2.refs_0_, ...), custom_call_target="tpu_custom_call" | custom-call | flops 30000001024 | bytes 1000000 | tf_op jit(solution)/shard_map/apply_cycle/pallas_call | solution.py:224
  51.1 3.4 %collective-permute-start.9 = (bf16[384,256]{1,0:T(8,128)(2,1)S(1)}, bf16[384,256]{1,0:T(8,128)(2,1)S(1)}, u32[]{:S(2)}, u32[]{:S(2)}) collective-permute-start(bf16[384,256]{1,0:T(8,128)(2,1)S(1)} %get-tuple-element.69), channel_id=1, source_target_pairs={{0,8},{4,12},{8,0},{12,4},{1,9},{5,13},{9,1},{13,5},{2,10},{6,14},... | collective-permute-start | bytes 589832 | tf_op jit(solution)/shard_map/ppermute | solution.py:341
  54.5 4.6 %collective-permute-done.8 = bf16[768,512]{1,0:T(8,128)(2,1)S(1)} collective-permute-done((bf16[768,512]{1,0:T(8,128)(2,1)S(1)}, bf16[768,512]{1,0:T(8,128)(2,1)S(1)}, u32[]{:S(2)}, u32[]{:S(2)}) %collective-permute-start.8) | collective-permute-done | bytes 786464 | tf_op jit(solution)/shard_map/ppermute | solution.py:390
  59.1 0.0 collective-permute-start.11
  59.1 0.0 collective-permute-done.13.refs_2_
  59.1 1.7 %collective-permute-start.10 = (bf16[384,256]{1,0:T(8,128)(2,1)S(1)}, bf16[384,256]{1,0:T(8,128)(2,1)S(1)}, u32[]{:S(2)}, u32[]{:S(2)}) collective-permute-start(bf16[384,256]{1,0:T(8,128)(2,1)S(1)} %get-tuple-element.70), channel_id=1, source_target_pairs={{0,12},{4,8},{8,4},{12,0},{1,13},{5,9},{9,5},{13,1},{2,14},{6,10},... | collective-permute-start | bytes 589832 | tf_op jit(solution)/shard_map/ppermute | solution.py:341
  60.8 0.0 copy-done.1
  60.8 0.4 bitcast_add_fusion.base_ref
  61.2 0.0 collective-permute-done.14.refs_3_
  61.2 0.0 collective-permute-done.12.refs_1_
  61.2 1.5 %finish.2.refs_1_ = bf16[768,512]{1,0:T(8,128)(2,1)} custom-call(bf16[768,1536]{1,0:T(8,128)(2,1)S(1)} %get-tuple-element.42.pick_ref, f32[768,512]{1,0:T(8,128)S(1)} %bitcast_add_fusion.base_ref, f32[768,512]{1,0:T(8,128)S(1)} %get-tuple-element.71.inverse_ref, bf16[384,256]{1,0:T(8,128)(2,1)S(1)} %get-tuple-element.60.refs_0_, ...), custom_call_target="tpu_custom_call" | custom-call | tf_op jit(solution)/shard_map/finish/pallas_call | solution.py:300
  62.7 7.8 %collective-permute-done.9.refs_1_ = bf16[384,256]{1,0:T(8,128)(2,1)S(1)} collective-permute-done((bf16[384,256]{1,0:T(8,128)(2,1)S(1)}, bf16[384,256]{1,0:T(8,128)(2,1)S(1)}, u32[]{:S(2)}, u32[]{:S(2)}) %collective-permute-start.9) | collective-permute-done | bytes 196640 | tf_op jit(solution)/shard_map/ppermute | solution.py:341
  70.6 0.0 collective-permute-done.10.refs_2_
  70.6 0.7 partial.1.base_ref
  71.3 2.1 %collective-permute-done.11.refs_0_ = bf16[384,256]{1,0:T(8,128)(2,1)S(1)} collective-permute-done((bf16[384,256]{1,0:T(8,128)(2,1)S(1)}, bf16[384,256]{1,0:T(8,128)(2,1)S(1)}, u32[]{:S(2)}, u32[]{:S(2)}) %collective-permute-start.11) | collective-permute-done | bytes 196640 | tf_op jit(solution)/shard_map/ppermute | solution.py:341
  73.3 1.1 %finish.3 = bf16[768,512]{1,0:T(8,128)(2,1)} custom-call(bf16[768,1536]{1,0:T(8,128)(2,1)S(1)} %get-tuple-element.42.pick_ref, f32[768,256]{1,0:T(8,128)S(1)} %partial.1.base_ref, f32[768,512]{1,0:T(8,128)S(1)} %get-tuple-element.71.inverse_ref, bf16[384,256]{1,0:T(8,128)(2,1)S(1)} %collective-permute-done.11.refs_0_, ...), custom_call_target="tpu_custom_call", output_to_operand_aliasing={{}: (4, {})} | custom-call | tf_op jit(solution)/shard_map/finish/pallas_call | solution.py:300
Async XLA Ops:
  1.7 10.5 %collective-permute-start = (bf16[128,256]{1,0:T(8,128)(2,1)S(1)}, bf16[128,256]{1,0:T(8,128)(2,1)S(1)}, u32[]{:S(2)}, u32[]{:S(2)}) collective-permute-start(bf16[128,256]{1,0:T(8,128)(2,1)S(1)} %get-tuple-element.40), channel_id=1, source_target_pairs={{0,12},{4,8},{8,4},{12,0},{1,13},{5,9},{9,5},{13,1},{2,14},{6,10},... | collective-permute-start | bytes 196616 | tf_op jit(solution)/shard_map/ppermute | solution.py:341
  6.8 26.3 %collective-permute-start.6 = (bf16[384,256]{1,0:T(8,128)(2,1)S(1)}, bf16[384,256]{1,0:T(8,128)(2,1)S(1)}, u32[]{:S(2)}, u32[]{:S(2)}) collective-permute-start(bf16[384,256]{1,0:T(8,128)(2,1)S(1)} %get-tuple-element.53), channel_id=1, source_target_pairs={{0,8},{4,12},{8,0},{12,4},{1,9},{5,13},{9,1},{13,5},{2,10},{6,14},... | collective-permute-start | bytes 589832 | tf_op jit(solution)/shard_map/ppermute | solution.py:341
  6.8 26.3 %collective-permute-start.7 = (bf16[384,256]{1,0:T(8,128)(2,1)S(1)}, bf16[384,256]{1,0:T(8,128)(2,1)S(1)}, u32[]{:S(2)}, u32[]{:S(2)}) collective-permute-start(bf16[384,256]{1,0:T(8,128)(2,1)S(1)} %get-tuple-element.54), channel_id=1, source_target_pairs={{0,4},{4,0},{8,12},{12,8},{1,5},{5,1},{9,13},{13,9},{2,6},{6,2},{1... | collective-permute-start | bytes 589832 | tf_op jit(solution)/shard_map/ppermute | solution.py:341
  7.4 20.3 %collective-permute-start.5 = (bf16[256,256]{1,0:T(8,128)(2,1)S(1)}, bf16[256,256]{1,0:T(8,128)(2,1)S(1)}, u32[]{:S(2)}, u32[]{:S(2)}) collective-permute-start(bf16[256,256]{1,0:T(8,128)(2,1)S(1)} %get-tuple-element.52), channel_id=1, source_target_pairs={{0,12},{4,8},{8,4},{12,0},{1,13},{5,9},{9,5},{13,1},{2,14},{6,10},... | collective-permute-start | bytes 393224 | tf_op jit(solution)/shard_map/ppermute | solution.py:341
  14.2 25.5 %collective-permute-start.2 = (bf16[384,256]{1,0:T(8,128)(2,1)S(1)}, bf16[384,256]{1,0:T(8,128)(2,1)S(1)}, u32[]{:S(2)}, u32[]{:S(2)}) collective-permute-start(bf16[384,256]{1,0:T(8,128)(2,1)S(1)} %get-tuple-element.43), channel_id=1, source_target_pairs={{0,12},{4,8},{8,4},{12,0},{1,13},{5,9},{9,5},{13,1},{2,14},{6,10},... | collective-permute-start | bytes 589832 | tf_op jit(solution)/shard_map/ppermute | solution.py:341
  15.8 33.7 %collective-permute-start.3 = (bf16[384,256]{1,0:T(8,128)(2,1)S(1)}, bf16[384,256]{1,0:T(8,128)(2,1)S(1)}, u32[]{:S(2)}, u32[]{:S(2)}) collective-permute-start(bf16[384,256]{1,0:T(8,128)(2,1)S(1)} %get-tuple-element.44), channel_id=1, source_target_pairs={{0,8},{4,12},{8,0},{12,4},{1,9},{5,13},{9,1},{13,5},{2,10},{6,14},... | collective-permute-start | bytes 589832 | tf_op jit(solution)/shard_map/ppermute | solution.py:341
  18.5 8.0 %copy-start = (f32[512]{0:T(512)S(1)}, f32[512]{0:T(512)}, u32[]{:S(2)}) copy-start(f32[512]{0:T(512)} %param.15) | copy-start | bytes 6148
  27.8 21.8 %collective-permute-start.4 = (bf16[384,256]{1,0:T(8,128)(2,1)S(1)}, bf16[384,256]{1,0:T(8,128)(2,1)S(1)}, u32[]{:S(2)}, u32[]{:S(2)}) collective-permute-start(bf16[384,256]{1,0:T(8,128)(2,1)S(1)} %get-tuple-element.45), channel_id=1, source_target_pairs={{0,4},{4,0},{8,12},{12,8},{1,5},{5,1},{9,13},{13,9},{2,6},{6,2},{1... | collective-permute-start | bytes 589832 | tf_op jit(solution)/shard_map/ppermute | solution.py:341
  33.1 3.4 %collective-permute-start.1 = (bf16[2,768,512]{2,1,0:T(8,128)(2,1)S(1)}, bf16[2,768,512]{2,1,0:T(8,128)(2,1)S(1)}, u32[]{:S(2)}, u32[]{:S(2)}) collective-permute-start(bf16[2,768,512]{2,1,0:T(8,128)(2,1)S(1)} %get-tuple-element.49), channel_id=1, source_target_pairs={{0,1},{1,0},{2,3},{3,2},{4,5},{5,4},{6,7},{7,6},{8,9},{9,8},{10,11... | collective-permute-start | bytes 4718600 | tf_op jit(solution)/shard_map/ppermute | solution.py:370
  34.6 24.5 %collective-permute-start.13 = (bf16[384,256]{1,0:T(8,128)(2,1)S(1)}, bf16[384,256]{1,0:T(8,128)(2,1)S(1)}, u32[]{:S(2)}, u32[]{:S(2)}) collective-permute-start(bf16[384,256]{1,0:T(8,128)(2,1)S(1)} %get-tuple-element.56), channel_id=1, source_target_pairs={{0,8},{4,12},{8,0},{12,4},{1,9},{5,13},{9,1},{13,5},{2,10},{6,14},... | collective-permute-start | bytes 589832 | tf_op jit(solution)/shard_map/ppermute | solution.py:341
  36.5 24.7 %collective-permute-start.14 = (bf16[384,256]{1,0:T(8,128)(2,1)S(1)}, bf16[384,256]{1,0:T(8,128)(2,1)S(1)}, u32[]{:S(2)}, u32[]{:S(2)}) collective-permute-start(bf16[384,256]{1,0:T(8,128)(2,1)S(1)} %get-tuple-element.55), channel_id=1, source_target_pairs={{0,12},{4,8},{8,4},{12,0},{1,13},{5,9},{9,5},{13,1},{2,14},{6,10},... | collective-permute-start | bytes 589832 | tf_op jit(solution)/shard_map/ppermute | solution.py:341
  39.7 21.1 %copy-start.1 = (bf16[1,768,512]{2,1,0:T(8,128)(2,1)S(1)}, bf16[1,768,512]{2,1,0:T(8,128)(2,1)}, u32[]{:S(2)}) copy-start(bf16[1,768,512]{2,1,0:T(8,128)(2,1)} %param.9) | copy-start | bytes 2359300
  39.7 19.4 %collective-permute-start.8 = (bf16[768,512]{1,0:T(8,128)(2,1)S(1)}, bf16[768,512]{1,0:T(8,128)(2,1)S(1)}, u32[]{:S(2)}, u32[]{:S(2)}) collective-permute-start(bf16[768,512]{1,0:T(8,128)(2,1)S(1)} %fusion), channel_id=1, source_target_pairs={{0,2},{2,0},{1,3},{3,1},{4,6},{6,4},{5,7},{7,5},{8,10},{10,8},{9,1... | collective-permute-start | bytes 2359304 | tf_op jit(solution)/shard_map/ppermute | solution.py:390
  49.5 11.8 %collective-permute-start.12 = (bf16[384,256]{1,0:T(8,128)(2,1)S(1)}, bf16[384,256]{1,0:T(8,128)(2,1)S(1)}, u32[]{:S(2)}, u32[]{:S(2)}) collective-permute-start(bf16[384,256]{1,0:T(8,128)(2,1)S(1)} %get-tuple-element.59), channel_id=1, source_target_pairs={{0,4},{4,0},{8,12},{12,8},{1,5},{5,1},{9,13},{13,9},{2,6},{6,2},{1... | collective-permute-start | bytes 589832 | tf_op jit(solution)/shard_map/ppermute | solution.py:341
  51.1 19.5 %collective-permute-start.9 = (bf16[384,256]{1,0:T(8,128)(2,1)S(1)}, bf16[384,256]{1,0:T(8,128)(2,1)S(1)}, u32[]{:S(2)}, u32[]{:S(2)}) collective-permute-start(bf16[384,256]{1,0:T(8,128)(2,1)S(1)} %get-tuple-element.69), channel_id=1, source_target_pairs={{0,8},{4,12},{8,0},{12,4},{1,9},{5,13},{9,1},{13,5},{2,10},{6,14},... | collective-permute-start | bytes 589832 | tf_op jit(solution)/shard_map/ppermute | solution.py:341
  59.1 14.2 %collective-permute-start.11 = (bf16[384,256]{1,0:T(8,128)(2,1)S(1)}, bf16[384,256]{1,0:T(8,128)(2,1)S(1)}, u32[]{:S(2)}, u32[]{:S(2)}) collective-permute-start(bf16[384,256]{1,0:T(8,128)(2,1)S(1)} %get-tuple-element.72), channel_id=1, source_target_pairs={{0,4},{4,0},{8,12},{12,8},{1,5},{5,1},{9,13},{13,9},{2,6},{6,2},{1... | collective-permute-start | bytes 589832 | tf_op jit(solution)/shard_map/ppermute | solution.py:341
  59.1 11.5 %collective-permute-start.10 = (bf16[384,256]{1,0:T(8,128)(2,1)S(1)}, bf16[384,256]{1,0:T(8,128)(2,1)S(1)}, u32[]{:S(2)}, u32[]{:S(2)}) collective-permute-start(bf16[384,256]{1,0:T(8,128)(2,1)S(1)} %get-tuple-element.70), channel_id=1, source_target_pairs={{0,12},{4,8},{8,4},{12,0},{1,13},{5,9},{9,5},{13,1},{2,14},{6,10},... | collective-permute-start | bytes 589832 | tf_op jit(solution)/shard_map/ppermute | solution.py:341

commit v20 on v19

--- a/solution.py
+++ b/solution.py
@@ -345,11 +345,13 @@
     width = holes // HALVES
     route_row = route[0].reshape(1, rows)
     plan = (paired, chan_count, send, block_rows)
-    leading = 128 if paired and count > 2 and block_rows > 128 else block_rows
-    early = [(k, 0, block_rows, 0, width) for k in far_first if k or not paired]
+    leading = 256 if paired and count > 2 and block_rows > 256 else block_rows
+    soon = count > 2 and paired
+    early = [(k, 0, block_rows, 0, width) for k in far_first if k > soon or not paired]
     if leading < block_rows:
         early[:1] = [(early[0][0], 0, leading, 0, width), (early[0][0], leading, block_rows - leading, 0, width)]
-    late = [(k, 0, block_rows, h * width, width) for h in range(1, HALVES) for k in far_first if k or not paired]
+    late = [(1, 0, block_rows, 0, width)] if soon else []
+    late += [(k, 0, block_rows, h * width, width) for h in range(1, HALVES) for k in far_first if k or not paired]
     late += [(0, 0, block_rows, 0, holes)] if paired else []
     target, *blocks = pack(plan + (early,), False, route_row, amps, "pack_first")
     arrived = {item: exchange(block, item[0]) for item, block in zip(early, blocks)}

time: 74.6 us -> 76.1 us (1.020)
  waiting for transfers between devices: 23.1 us -> 26 us
  starting transfers between devices: 30.2 us -> 28.8 us
    ppermute x1, waiting for transfers between devices: 4.6 us -> 14.6 us  [body(): crossed.append(lax.ppermute(term, 'lad', pairs))]
    ppermute x13, waiting for transfers between devices: 18.1 us -> 10.9 us  [exchange(): lax.ppermute(block, 'chan', [(i, i ^ k) for i in range(chan_count)])]
    ppermute x13, starting transfers between devices: 28.7 us -> 27.2 us  [exchange(): lax.ppermute(block, 'chan', [(i, i ^ k) for i in range(chan_count)])]
  transfers between devices with their start and end apart: 15 -> 15, of which waited for: 5 -> 6; matrix products, arithmetic and copies ran while one was open for 2% -> 2% of each run, Pallas kernels for 22% -> 22%
where the time goes in v20:
time: 76.1 us; the launch traced here: 75.9 us
  starting transfers between devices  28.8 us (38%)
  waiting for transfers between devices  26 us (34%)
  Pallas kernels  19.2 us (25%)
  local copies, waits for them, and re-layouts  1.05 us (1%)
    ppermute x13, starting transfers between devices, exchange(): lax.ppermute(block, 'chan', [(i, i ^ k) for i in range(chan_count)])  27.2 us
    ppermute x1, waiting for transfers between devices, body(): crossed.append(lax.ppermute(term, 'lad', pairs))  14.6 us
    ppermute x13, waiting for transfers between devices, exchange(): lax.ppermute(block, 'chan', [(i, i ^ k) for i in range(chan_count)])  10.9 us
    pallas_call x1, Pallas kernels, prepare(): pl.pallas_call(functools.partial(prepare_kernel, sub_count), out_shape=[j...  7.97 us
    pallas_call x2, Pallas kernels, pack(): pl.pallas_call(functools.partial(pack_kernel, plan, given), out_shape=ext...  3.75 us
    pallas_call x2, Pallas kernels, apply_cycle(): pl.pallas_call(functools.partial(cycle_kernel, half, plan, places), out_s...  2.88 us
    pallas_call x2, Pallas kernels, finish(): pl.pallas_call(functools.partial(finish_kernel, half * width, tuple(place...  2.6 us
    ppermute x1, starting transfers between devices, body(): crossed.append(lax.ppermute(term, 'lad', pairs))  1.56 us
  transfers between devices with their start and end apart: 15, of which 6 were waited for; matrix products, arithmetic and copies ran while one was open for 2% of the time, Pallas kernels for 22%

profile of v20, /device:TPU:0, one launch (start us, length us, event | category | flops | bytes accessed | tf_op | source)
XLA Modules:
  0.0 75.9 jit_solution(849900134399214423)
XLA Ops:
  0.0 1.5 %pack_first.1 = (s32[1,768]{1,0:T(1,128)S(1)}, bf16[256,256]{1,0:T(8,128)(2,1)S(1)}, bf16[128,256]{1,0:T(8,128)(2,1)S(1)}, bf16[384,256]{1,0:T(8,128)(2,1)S(1)}) custom-call(s32[1,768]{1,0:T(1,128)} %bitcast.22, bf16[768,512]{1,0:T(8,128)(2,1)} %bitcast.19), custom_call_target="tpu_custom_call" | custom-call | tf_op jit(solution)/shard_map/pack_first/pallas_call | solution.py:94
  1.5 5.1 %collective-permute-start = (bf16[256,256]{1,0:T(8,128)(2,1)S(1)}, bf16[256,256]{1,0:T(8,128)(2,1)S(1)}, u32[]{:S(2)}, u32[]{:S(2)}) collective-permute-start(bf16[256,256]{1,0:T(8,128)(2,1)S(1)} %get-tuple-element.40), channel_id=1, source_target_pairs={{0,12},{4,8},{8,4},{12,0},{1,13},{5,9},{9,5},{13,1},{2,14},{6,10},... | collective-permute-start | bytes 393224 | tf_op jit(solution)/shard_map/ppermute | solution.py:341
  6.6 0.0 collective-permute-start.6
  6.6 1.9 %collective-permute-start.5 = (bf16[128,256]{1,0:T(8,128)(2,1)S(1)}, bf16[128,256]{1,0:T(8,128)(2,1)S(1)}, u32[]{:S(2)}, u32[]{:S(2)}) collective-permute-start(bf16[128,256]{1,0:T(8,128)(2,1)S(1)} %get-tuple-element.53), channel_id=1, source_target_pairs={{0,12},{4,8},{8,4},{12,0},{1,13},{5,9},{9,5},{13,1},{2,14},{6,10},... | collective-permute-start | bytes 196616 | tf_op jit(solution)/shard_map/ppermute | solution.py:341
  8.6 0.9 %copy.11.part_ref = f32[768,1]{1,0:T(8,128)S(1)} copy(f32[768,1]{0,1:T(1,128)} %bitcast.23) | data formatting | bytes 6144 | tf_op jit(solution)/shard_map/reshape;squeeze | solution.py:364
  9.4 0.1 add_multiply_fusion.off_ref
  9.5 1.6 %collective-permute-done.refs_0_ = bf16[256,256]{1,0:T(8,128)(2,1)S(1)} collective-permute-done((bf16[256,256]{1,0:T(8,128)(2,1)S(1)}, bf16[256,256]{1,0:T(8,128)(2,1)S(1)}, u32[]{:S(2)}, u32[]{:S(2)}) %collective-permute-start) | collective-permute-done | bytes 131104 | tf_op jit(solution)/shard_map/ppermute | solution.py:341
  11.1 2.2 %pack_rest.1 = (bf16[384,256]{1,0:T(8,128)(2,1)S(1)}, bf16[384,256]{1,0:T(8,128)(2,1)S(1)}, bf16[384,256]{1,0:T(8,128)(2,1)S(1)}, bf16[384,256]{1,0:T(8,128)(2,1)S(1)}, bf16[384,512]{1,0:T(8,128)(2,1)S(1)}) custom-call(s32[1,768]{1,0:T(1,128)S(1)} %get-tuple-element.41.route_in, bf16[768,512]{1,0:T(8,128)(2,1)} %bitcast.20), custom_call_target="tpu_custom_call" | custom-call | tf_op jit(solution)/shard_map/pack_rest/pallas_call | solution.py:94
  13.3 8.2 %collective-permute-start.7 = (bf16[384,256]{1,0:T(8,128)(2,1)S(1)}, bf16[384,256]{1,0:T(8,128)(2,1)S(1)}, u32[]{:S(2)}, u32[]{:S(2)}) collective-permute-start(bf16[384,256]{1,0:T(8,128)(2,1)S(1)} %get-tuple-element.43), channel_id=1, source_target_pairs={{0,4},{4,0},{8,12},{12,8},{1,5},{5,1},{9,13},{13,9},{2,6},{6,2},{1... | collective-permute-start | bytes 589832 | tf_op jit(solution)/shard_map/ppermute | solution.py:341
  21.6 2.7 %collective-permute-start.2 = (bf16[384,256]{1,0:T(8,128)(2,1)S(1)}, bf16[384,256]{1,0:T(8,128)(2,1)S(1)}, u32[]{:S(2)}, u32[]{:S(2)}) collective-permute-start(bf16[384,256]{1,0:T(8,128)(2,1)S(1)} %get-tuple-element.44), channel_id=1, source_target_pairs={{0,12},{4,8},{8,4},{12,0},{1,13},{5,9},{9,5},{13,1},{2,14},{6,10},... | collective-permute-start | bytes 589832 | tf_op jit(solution)/shard_map/ppermute | solution.py:341
  24.2 0.0 collective-permute-start.3
  24.2 0.2 copy.10.target_ref
  24.4 0.0 copy-start
  24.4 8.0 %prepare.1 = (bf16[2,768,512]{2,1,0:T(8,128)(2,1)S(1)}, bf16[2,768,512]{2,1,0:T(8,128)(2,1)S(1)}, bf16[1536,1536]{1,0:T(8,128)(2,1)S(1)}) custom-call(bf16[3072,768]{1,0:T(8,128)(2,1)} %bitcast.24, bf16[768,512]{1,0:T(8,128)(2,1)} %bitcast.21, bf16[1536,1536]{1,0:T(8,128)(2,1)} %bitcast.25, bf16[12,128,128]{2,1,0:T(8,128)(2,1)} %bitcast.26), custom_call_target="tpu_custom_call" | custom-call | flops 30000001024 | bytes 1000000 | tf_op jit(solution)/shard_map/prepare/pallas_call | solution.py:183
  32.4 0.0 copy-done
  32.4 1.3 %unpack_matrix.1 = (bf16[768,1536]{1,0:T(8,128)(2,1)S(1)}, f32[768,512]{1,0:T(8,128)S(1)}) custom-call(s32[4]{0:T(128)S(1)} %add_multiply_fusion.off_ref, s32[768,1]{1,0:T(8,128)S(1)} %copy.10.target_ref, f32[768,1]{1,0:T(8,128)S(1)} %copy.11.part_ref, f32[1,512]{1,0:T(1,128)S(1)} %bitcast.18), custom_call_target="tpu_custom_call" | custom-call | flops 30000001024 | bytes 1000000 | tf_op jit(solution)/shard_map/unpack_matrix/pallas_call | solution.py:122
  33.7 0.0 collective-permute-done.5.refs_1_
  33.7 1.8 %collective-permute-start.4 = (bf16[384,256]{1,0:T(8,128)(2,1)S(1)}, bf16[384,256]{1,0:T(8,128)(2,1)S(1)}, u32[]{:S(2)}, u32[]{:S(2)}) collective-permute-start(bf16[384,256]{1,0:T(8,128)(2,1)S(1)} %get-tuple-element.46), channel_id=1, source_target_pairs={{0,4},{4,0},{8,12},{12,8},{1,5},{5,1},{9,13},{13,9},{2,6},{6,2},{1... | collective-permute-start | bytes 589832 | tf_op jit(solution)/shard_map/ppermute | solution.py:341
  35.5 0.0 collective-permute-done.6.refs_2_
  35.5 0.0 collective-permute-start.1
  35.5 0.0 collective-permute-done.7.refs_3_
  35.5 1.4 %apply_cycle.2 = (bf16[384,256]{1,0:T(8,128)(2,1)S(1)}, bf16[384,256]{1,0:T(8,128)(2,1)S(1)}, bf16[384,256]{1,0:T(8,128)(2,1)S(1)}, bf16[384,256]{1,0:T(8,128)(2,1)S(1)}) custom-call(bf16[1536,1536]{1,0:T(8,128)(2,1)S(1)} %get-tuple-element.51.operator_ref, bf16[256,256]{1,0:T(8,128)(2,1)S(1)} %collective-permute-done.refs_0_, ...), custom_call_target="tpu_custom_call" | custom-call | flops 30000001024 | bytes 1000000 | tf_op jit(solution)/shard_map/apply_cycle/pallas_call | solution.py:224
  37.0 1.4 %collective-permute-start.13 = (bf16[384,256]{1,0:T(8,128)(2,1)S(1)}, bf16[384,256]{1,0:T(8,128)(2,1)S(1)}, u32[]{:S(2)}, u32[]{:S(2)}) collective-permute-start(bf16[384,256]{1,0:T(8,128)(2,1)S(1)} %get-tuple-element.56), channel_id=1, source_target_pairs={{0,8},{4,12},{8,0},{12,4},{1,9},{5,13},{9,1},{13,5},{2,10},{6,14},... | collective-permute-start | bytes 589832 | tf_op jit(solution)/shard_map/ppermute | solution.py:341
  38.3 0.6 collective-permute-done.1
  38.9 2.7 %collective-permute-start.14 = (bf16[384,256]{1,0:T(8,128)(2,1)S(1)}, bf16[384,256]{1,0:T(8,128)(2,1)S(1)}, u32[]{:S(2)}, u32[]{:S(2)}) collective-permute-start(bf16[384,256]{1,0:T(8,128)(2,1)S(1)} %get-tuple-element.55), channel_id=1, source_target_pairs={{0,12},{4,8},{8,4},{12,0},{1,13},{5,9},{9,5},{13,1},{2,14},{6,10},... | collective-permute-start | bytes 589832 | tf_op jit(solution)/shard_map/ppermute | solution.py:341
  41.6 0.2 fusion
  41.8 0.0 copy-start.1
  41.8 0.0 collective-permute-done.2.refs_0_
  41.8 1.6 %collective-permute-start.8 = (bf16[768,512]{1,0:T(8,128)(2,1)S(1)}, bf16[768,512]{1,0:T(8,128)(2,1)S(1)}, u32[]{:S(2)}, u32[]{:S(2)}) collective-permute-start(bf16[768,512]{1,0:T(8,128)(2,1)S(1)} %fusion), channel_id=1, source_target_pairs={{0,2},{2,0},{1,3},{3,1},{4,6},{6,4},{5,7},{7,5},{8,10},{10,8},{9,1... | collective-permute-start | bytes 2359304 | tf_op jit(solution)/shard_map/ppermute | solution.py:392
  43.4 0.0 collective-permute-done.3.refs_1_
  43.4 0.0 collective-permute-start.12
  43.4 0.0 collective-permute-done.4.refs_2_
  43.4 1.4 %apply_cycle.3 = (bf16[384,256]{1,0:T(8,128)(2,1)S(1)}, bf16[384,256]{1,0:T(8,128)(2,1)S(1)}, bf16[384,256]{1,0:T(8,128)(2,1)S(1)}, bf16[384,256]{1,0:T(8,128)(2,1)S(1)}) custom-call(bf16[1536,1536]{1,0:T(8,128)(2,1)S(1)} %get-tuple-element.51.operator_ref, bf16[384,256]{1,0:T(8,128)(2,1)S(1)} %collective-permute-done.2.refs_0_, ...), custom_call_target="tpu_custom_call" | custom-call | flops 30000001024 | bytes 1000000 | tf_op jit(solution)/shard_map/apply_cycle/pallas_call | solution.py:224
  44.9 1.8 %collective-permute-start.9 = (bf16[384,256]{1,0:T(8,128)(2,1)S(1)}, bf16[384,256]{1,0:T(8,128)(2,1)S(1)}, u32[]{:S(2)}, u32[]{:S(2)}) collective-permute-start(bf16[384,256]{1,0:T(8,128)(2,1)S(1)} %get-tuple-element.69), channel_id=1, source_target_pairs={{0,8},{4,12},{8,0},{12,4},{1,9},{5,13},{9,1},{13,5},{2,10},{6,14},... | collective-permute-start | bytes 589832 | tf_op jit(solution)/shard_map/ppermute | solution.py:341
  46.6 14.6 %collective-permute-done.8 = bf16[768,512]{1,0:T(8,128)(2,1)S(1)} collective-permute-done((bf16[768,512]{1,0:T(8,128)(2,1)S(1)}, bf16[768,512]{1,0:T(8,128)(2,1)S(1)}, u32[]{:S(2)}, u32[]{:S(2)}) %collective-permute-start.8) | collective-permute-done | bytes 786464 | tf_op jit(solution)/shard_map/ppermute | solution.py:392
  61.2 0.0 collective-permute-start.11
  61.2 0.0 collective-permute-done.13.refs_2_
  61.2 1.7 %collective-permute-start.10 = (bf16[384,256]{1,0:T(8,128)(2,1)S(1)}, bf16[384,256]{1,0:T(8,128)(2,1)S(1)}, u32[]{:S(2)}, u32[]{:S(2)}) collective-permute-start(bf16[384,256]{1,0:T(8,128)(2,1)S(1)} %get-tuple-element.70), channel_id=1, source_target_pairs={{0,12},{4,8},{8,4},{12,0},{1,13},{5,9},{9,5},{13,1},{2,14},{6,10},... | collective-permute-start | bytes 589832 | tf_op jit(solution)/shard_map/ppermute | solution.py:341
  62.9 0.0 copy-done.1
  62.9 0.4 bitcast_add_fusion.base_ref
  63.3 0.0 collective-permute-done.14.refs_3_
  63.3 0.0 collective-permute-done.12.refs_1_
  63.3 1.5 %finish.2.refs_1_ = bf16[768,512]{1,0:T(8,128)(2,1)} custom-call(bf16[768,1536]{1,0:T(8,128)(2,1)S(1)} %get-tuple-element.42.pick_ref, f32[768,512]{1,0:T(8,128)S(1)} %bitcast_add_fusion.base_ref, f32[768,512]{1,0:T(8,128)S(1)} %get-tuple-element.71.inverse_ref, bf16[384,256]{1,0:T(8,128)(2,1)S(1)} %get-tuple-element.60.refs_0_, ...), custom_call_target="tpu_custom_call" | custom-call | tf_op jit(solution)/shard_map/finish/pallas_call | solution.py:300
  64.9 3.7 %collective-permute-done.9.refs_1_ = bf16[384,256]{1,0:T(8,128)(2,1)S(1)} collective-permute-done((bf16[384,256]{1,0:T(8,128)(2,1)S(1)}, bf16[384,256]{1,0:T(8,128)(2,1)S(1)}, u32[]{:S(2)}, u32[]{:S(2)}) %collective-permute-start.9) | collective-permute-done | bytes 196640 | tf_op jit(solution)/shard_map/ppermute | solution.py:341
  68.6 2.6 %collective-permute-done.10.refs_2_ = bf16[384,256]{1,0:T(8,128)(2,1)S(1)} collective-permute-done((bf16[384,256]{1,0:T(8,128)(2,1)S(1)}, bf16[384,256]{1,0:T(8,128)(2,1)S(1)}, u32[]{:S(2)}, u32[]{:S(2)}) %collective-permute-start.10) | collective-permute-done | bytes 196640 | tf_op jit(solution)/shard_map/ppermute | solution.py:341
  71.1 0.7 partial.1.base_ref
  71.8 3.0 %collective-permute-done.11.refs_0_ = bf16[384,256]{1,0:T(8,128)(2,1)S(1)} collective-permute-done((bf16[384,256]{1,0:T(8,128)(2,1)S(1)}, bf16[384,256]{1,0:T(8,128)(2,1)S(1)}, u32[]{:S(2)}, u32[]{:S(2)}) %collective-permute-start.11) | collective-permute-done | bytes 196640 | tf_op jit(solution)/shard_map/ppermute | solution.py:341
  74.8 1.1 %finish.3 = bf16[768,512]{1,0:T(8,128)(2,1)} custom-call(bf16[768,1536]{1,0:T(8,128)(2,1)S(1)} %get-tuple-element.42.pick_ref, f32[768,256]{1,0:T(8,128)S(1)} %partial.1.base_ref, f32[768,512]{1,0:T(8,128)S(1)} %get-tuple-element.71.inverse_ref, bf16[384,256]{1,0:T(8,128)(2,1)S(1)} %collective-permute-done.11.refs_0_, ...), custom_call_target="tpu_custom_call", output_to_operand_aliasing={{}: (4, {})} | custom-call | tf_op jit(solution)/shard_map/finish/pallas_call | solution.py:300
Async XLA Ops:
  1.5 9.5 %collective-permute-start = (bf16[256,256]{1,0:T(8,128)(2,1)S(1)}, bf16[256,256]{1,0:T(8,128)(2,1)S(1)}, u32[]{:S(2)}, u32[]{:S(2)}) collective-permute-start(bf16[256,256]{1,0:T(8,128)(2,1)S(1)} %get-tuple-element.40), channel_id=1, source_target_pairs={{0,12},{4,8},{8,4},{12,0},{1,13},{5,9},{9,5},{13,1},{2,14},{6,10},... | collective-permute-start | bytes 393224 | tf_op jit(solution)/shard_map/ppermute | solution.py:341
  6.6 28.9 %collective-permute-start.6 = (bf16[384,256]{1,0:T(8,128)(2,1)S(1)}, bf16[384,256]{1,0:T(8,128)(2,1)S(1)}, u32[]{:S(2)}, u32[]{:S(2)}) collective-permute-start(bf16[384,256]{1,0:T(8,128)(2,1)S(1)} %get-tuple-element.54), channel_id=1, source_target_pairs={{0,8},{4,12},{8,0},{12,4},{1,9},{5,13},{9,1},{13,5},{2,10},{6,14},... | collective-permute-start | bytes 589832 | tf_op jit(solution)/shard_map/ppermute | solution.py:341
  6.6 27.1 %collective-permute-start.5 = (bf16[128,256]{1,0:T(8,128)(2,1)S(1)}, bf16[128,256]{1,0:T(8,128)(2,1)S(1)}, u32[]{:S(2)}, u32[]{:S(2)}) collective-permute-start(bf16[128,256]{1,0:T(8,128)(2,1)S(1)} %get-tuple-element.53), channel_id=1, source_target_pairs={{0,12},{4,8},{8,4},{12,0},{1,13},{5,9},{9,5},{13,1},{2,14},{6,10},... | collective-permute-start | bytes 196616 | tf_op jit(solution)/shard_map/ppermute | solution.py:341
  13.3 22.2 %collective-permute-start.7 = (bf16[384,256]{1,0:T(8,128)(2,1)S(1)}, bf16[384,256]{1,0:T(8,128)(2,1)S(1)}, u32[]{:S(2)}, u32[]{:S(2)}) collective-permute-start(bf16[384,256]{1,0:T(8,128)(2,1)S(1)} %get-tuple-element.43), channel_id=1, source_target_pairs={{0,4},{4,0},{8,12},{12,8},{1,5},{5,1},{9,13},{13,9},{2,6},{6,2},{1... | collective-permute-start | bytes 589832 | tf_op jit(solution)/shard_map/ppermute | solution.py:341
  21.6 20.3 %collective-permute-start.2 = (bf16[384,256]{1,0:T(8,128)(2,1)S(1)}, bf16[384,256]{1,0:T(8,128)(2,1)S(1)}, u32[]{:S(2)}, u32[]{:S(2)}) collective-permute-start(bf16[384,256]{1,0:T(8,128)(2,1)S(1)} %get-tuple-element.44), channel_id=1, source_target_pairs={{0,12},{4,8},{8,4},{12,0},{1,13},{5,9},{9,5},{13,1},{2,14},{6,10},... | collective-permute-start | bytes 589832 | tf_op jit(solution)/shard_map/ppermute | solution.py:341
  24.2 19.2 %collective-permute-start.3 = (bf16[384,256]{1,0:T(8,128)(2,1)S(1)}, bf16[384,256]{1,0:T(8,128)(2,1)S(1)}, u32[]{:S(2)}, u32[]{:S(2)}) collective-permute-start(bf16[384,256]{1,0:T(8,128)(2,1)S(1)} %get-tuple-element.45), channel_id=1, source_target_pairs={{0,8},{4,12},{8,0},{12,4},{1,9},{5,13},{9,1},{13,5},{2,10},{6,14},... | collective-permute-start | bytes 589832 | tf_op jit(solution)/shard_map/ppermute | solution.py:341
  24.4 8.0 %copy-start = (f32[512]{0:T(512)S(1)}, f32[512]{0:T(512)}, u32[]{:S(2)}) copy-start(f32[512]{0:T(512)} %param.15) | copy-start | bytes 6148
  33.7 9.7 %collective-permute-start.4 = (bf16[384,256]{1,0:T(8,128)(2,1)S(1)}, bf16[384,256]{1,0:T(8,128)(2,1)S(1)}, u32[]{:S(2)}, u32[]{:S(2)}) collective-permute-start(bf16[384,256]{1,0:T(8,128)(2,1)S(1)} %get-tuple-element.46), channel_id=1, source_target_pairs={{0,4},{4,0},{8,12},{12,8},{1,5},{5,1},{9,13},{13,9},{2,6},{6,2},{1... | collective-permute-start | bytes 589832 | tf_op jit(solution)/shard_map/ppermute | solution.py:341
  35.5 3.4 %collective-permute-start.1 = (bf16[2,768,512]{2,1,0:T(8,128)(2,1)S(1)}, bf16[2,768,512]{2,1,0:T(8,128)(2,1)S(1)}, u32[]{:S(2)}, u32[]{:S(2)}) collective-permute-start(bf16[2,768,512]{2,1,0:T(8,128)(2,1)S(1)} %get-tuple-element.50), channel_id=1, source_target_pairs={{0,1},{1,0},{2,3},{3,2},{4,5},{5,4},{6,7},{7,6},{8,9},{9,8},{10,11... | collective-permute-start | bytes 4718600 | tf_op jit(solution)/shard_map/ppermute | solution.py:372
  37.0 24.2 %collective-permute-start.13 = (bf16[384,256]{1,0:T(8,128)(2,1)S(1)}, bf16[384,256]{1,0:T(8,128)(2,1)S(1)}, u32[]{:S(2)}, u32[]{:S(2)}) collective-permute-start(bf16[384,256]{1,0:T(8,128)(2,1)S(1)} %get-tuple-element.56), channel_id=1, source_target_pairs={{0,8},{4,12},{8,0},{12,4},{1,9},{5,13},{9,1},{13,5},{2,10},{6,14},... | collective-permute-start | bytes 589832 | tf_op jit(solution)/shard_map/ppermute | solution.py:341
  38.9 24.4 %collective-permute-start.14 = (bf16[384,256]{1,0:T(8,128)(2,1)S(1)}, bf16[384,256]{1,0:T(8,128)(2,1)S(1)}, u32[]{:S(2)}, u32[]{:S(2)}) collective-permute-start(bf16[384,256]{1,0:T(8,128)(2,1)S(1)} %get-tuple-element.55), channel_id=1, source_target_pairs={{0,12},{4,8},{8,4},{12,0},{1,13},{5,9},{9,5},{13,1},{2,14},{6,10},... | collective-permute-start | bytes 589832 | tf_op jit(solution)/shard_map/ppermute | solution.py:341
  41.8 21.1 %copy-start.1 = (bf16[1,768,512]{2,1,0:T(8,128)(2,1)S(1)}, bf16[1,768,512]{2,1,0:T(8,128)(2,1)}, u32[]{:S(2)}) copy-start(bf16[1,768,512]{2,1,0:T(8,128)(2,1)} %param.9) | copy-start | bytes 2359300
  41.8 19.4 %collective-permute-start.8 = (bf16[768,512]{1,0:T(8,128)(2,1)S(1)}, bf16[768,512]{1,0:T(8,128)(2,1)S(1)}, u32[]{:S(2)}, u32[]{:S(2)}) collective-permute-start(bf16[768,512]{1,0:T(8,128)(2,1)S(1)} %fusion), channel_id=1, source_target_pairs={{0,2},{2,0},{1,3},{3,1},{4,6},{6,4},{5,7},{7,5},{8,10},{10,8},{9,1... | collective-permute-start | bytes 2359304 | tf_op jit(solution)/shard_map/ppermute | solution.py:392
  43.4 19.9 %collective-permute-start.12 = (bf16[384,256]{1,0:T(8,128)(2,1)S(1)}, bf16[384,256]{1,0:T(8,128)(2,1)S(1)}, u32[]{:S(2)}, u32[]{:S(2)}) collective-permute-start(bf16[384,256]{1,0:T(8,128)(2,1)S(1)} %get-tuple-element.59), channel_id=1, source_target_pairs={{0,4},{4,0},{8,12},{12,8},{1,5},{5,1},{9,13},{13,9},{2,6},{6,2},{1... | collective-permute-start | bytes 589832 | tf_op jit(solution)/shard_map/ppermute | solution.py:341
  44.9 23.7 %collective-permute-start.9 = (bf16[384,256]{1,0:T(8,128)(2,1)S(1)}, bf16[384,256]{1,0:T(8,128)(2,1)S(1)}, u32[]{:S(2)}, u32[]{:S(2)}) collective-permute-start(bf16[384,256]{1,0:T(8,128)(2,1)S(1)} %get-tuple-element.69), channel_id=1, source_target_pairs={{0,8},{4,12},{8,0},{12,4},{1,9},{5,13},{9,1},{13,5},{2,10},{6,14},... | collective-permute-start | bytes 589832 | tf_op jit(solution)/shard_map/ppermute | solution.py:341
  61.2 13.6 %collective-permute-start.11 = (bf16[384,256]{1,0:T(8,128)(2,1)S(1)}, bf16[384,256]{1,0:T(8,128)(2,1)S(1)}, u32[]{:S(2)}, u32[]{:S(2)}) collective-permute-start(bf16[384,256]{1,0:T(8,128)(2,1)S(1)} %get-tuple-element.72), channel_id=1, source_target_pairs={{0,4},{4,0},{8,12},{12,8},{1,5},{5,1},{9,13},{13,9},{2,6},{6,2},{1... | collective-permute-start | bytes 589832 | tf_op jit(solution)/shard_map/ppermute | solution.py:341
  61.2 9.9 %collective-permute-start.10 = (bf16[384,256]{1,0:T(8,128)(2,1)S(1)}, bf16[384,256]{1,0:T(8,128)(2,1)S(1)}, u32[]{:S(2)}, u32[]{:S(2)}) collective-permute-start(bf16[384,256]{1,0:T(8,128)(2,1)S(1)} %get-tuple-element.70), channel_id=1, source_target_pairs={{0,12},{4,8},{8,4},{12,0},{1,13},{5,9},{9,5},{13,1},{2,14},{6,10},... | collective-permute-start | bytes 589832 | tf_op jit(solution)/shard_map/ppermute | solution.py:341

commit v21 on v20

--- a/solution.py
+++ b/solution.py
@@ -345,7 +345,7 @@
     width = holes // HALVES
     route_row = route[0].reshape(1, rows)
     plan = (paired, chan_count, send, block_rows)
-    leading = 256 if paired and count > 2 and block_rows > 256 else block_rows
+    leading = 128 if paired and count > 2 and block_rows > 128 else block_rows
     soon = count > 2 and paired
     early = [(k, 0, block_rows, 0, width) for k in far_first if k > soon or not paired]
     if leading < block_rows:

time: 76.1 us -> 74.8 us (0.983)
  waiting for transfers between devices: 26 us -> 23.5 us
  starting transfers between devices: 28.8 us -> 30 us
    ppermute x1, waiting for transfers between devices: 14.6 us -> 4.91 us  [body(): crossed.append(lax.ppermute(term, 'lad', pairs))]
    ppermute x13, waiting for transfers between devices: 10.9 us -> 17.9 us  [exchange(): lax.ppermute(block, 'chan', [(i, i ^ k) for i in range(chan_count)])]
    ppermute x13, starting transfers between devices: 27.2 us -> 28.4 us  [exchange(): lax.ppermute(block, 'chan', [(i, i ^ k) for i in range(chan_count)])]
  transfers between devices with their start and end apart: 15 -> 15, of which waited for: 6 -> 5; matrix products, arithmetic and copies ran while one was open for 2% -> 2% of each run, Pallas kernels for 22% -> 22%
where the time goes in v21:
time: 74.8 us; the launch traced here: 74.6 us
  starting transfers between devices  30 us (40%)
  waiting for transfers between devices  23.5 us (31%)
  Pallas kernels  19.2 us (26%)
  local copies, waits for them, and re-layouts  1.05 us (1%)
    ppermute x13, starting transfers between devices, exchange(): lax.ppermute(block, 'chan', [(i, i ^ k) for i in range(chan_count)])  28.4 us
    ppermute x13, waiting for transfers between devices, exchange(): lax.ppermute(block, 'chan', [(i, i ^ k) for i in range(chan_count)])  17.9 us
    pallas_call x1, Pallas kernels, prepare(): pl.pallas_call(functools.partial(prepare_kernel, sub_count), out_shape=[j...  7.96 us
    ppermute x1, waiting for transfers between devices, body(): crossed.append(lax.ppermute(term, 'lad', pairs))  4.91 us
    pallas_call x2, Pallas kernels, pack(): pl.pallas_call(functools.partial(pack_kernel, plan, given), out_shape=ext...  3.75 us
    pallas_call x2, Pallas kernels, apply_cycle(): pl.pallas_call(functools.partial(cycle_kernel, half, plan, places), out_s...  2.88 us
    pallas_call x2, Pallas kernels, finish(): pl.pallas_call(functools.partial(finish_kernel, half * width, tuple(place...  2.6 us
    ppermute x1, starting transfers between devices, body(): crossed.append(lax.ppermute(term, 'lad', pairs))  1.56 us
  transfers between devices with their start and end apart: 15, of which 5 were waited for; matrix products, arithmetic and copies ran while one was open for 2% of the time, Pallas kernels for 22%

profile of v21, /device:TPU:0, one launch (start us, length us, event | category | flops | bytes accessed | tf_op | source)
XLA Modules:
  0.0 74.6 jit_solution(1446606544135804536)
XLA Ops:
  0.0 1.5 %pack_first.1 = (s32[1,768]{1,0:T(1,128)S(1)}, bf16[128,256]{1,0:T(8,128)(2,1)S(1)}, bf16[256,256]{1,0:T(8,128)(2,1)S(1)}, bf16[384,256]{1,0:T(8,128)(2,1)S(1)}) custom-call(s32[1,768]{1,0:T(1,128)} %bitcast.22, bf16[768,512]{1,0:T(8,128)(2,1)} %bitcast.19), custom_call_target="tpu_custom_call" | custom-call | tf_op jit(solution)/shard_map/pack_first/pallas_call | solution.py:94
  1.5 5.1 %collective-permute-start = (bf16[128,256]{1,0:T(8,128)(2,1)S(1)}, bf16[128,256]{1,0:T(8,128)(2,1)S(1)}, u32[]{:S(2)}, u32[]{:S(2)}) collective-permute-start(bf16[128,256]{1,0:T(8,128)(2,1)S(1)} %get-tuple-element.40), channel_id=1, source_target_pairs={{0,12},{4,8},{8,4},{12,0},{1,13},{5,9},{9,5},{13,1},{2,14},{6,10},... | collective-permute-start | bytes 196616 | tf_op jit(solution)/shard_map/ppermute | solution.py:341
  6.6 0.0 collective-permute-start.6
  6.6 1.9 %collective-permute-start.5 = (bf16[256,256]{1,0:T(8,128)(2,1)S(1)}, bf16[256,256]{1,0:T(8,128)(2,1)S(1)}, u32[]{:S(2)}, u32[]{:S(2)}) collective-permute-start(bf16[256,256]{1,0:T(8,128)(2,1)S(1)} %get-tuple-element.53), channel_id=1, source_target_pairs={{0,12},{4,8},{8,4},{12,0},{1,13},{5,9},{9,5},{13,1},{2,14},{6,10},... | collective-permute-start | bytes 393224 | tf_op jit(solution)/shard_map/ppermute | solution.py:341
  8.6 0.9 %copy.11.part_ref = f32[768,1]{1,0:T(8,128)S(1)} copy(f32[768,1]{0,1:T(1,128)} %bitcast.23) | data formatting | bytes 6144 | tf_op jit(solution)/shard_map/reshape;squeeze | solution.py:364
  9.4 0.1 add_multiply_fusion.off_ref
  9.5 0.0 collective-permute-done.refs_0_
  9.5 2.2 %pack_rest.1 = (bf16[384,256]{1,0:T(8,128)(2,1)S(1)}, bf16[384,256]{1,0:T(8,128)(2,1)S(1)}, bf16[384,256]{1,0:T(8,128)(2,1)S(1)}, bf16[384,256]{1,0:T(8,128)(2,1)S(1)}, bf16[384,512]{1,0:T(8,128)(2,1)S(1)}) custom-call(s32[1,768]{1,0:T(1,128)S(1)} %get-tuple-element.41.route_in, bf16[768,512]{1,0:T(8,128)(2,1)} %bitcast.20), custom_call_target="tpu_custom_call" | custom-call | tf_op jit(solution)/shard_map/pack_rest/pallas_call | solution.py:94
  11.8 7.9 %collective-permute-start.7 = (bf16[384,256]{1,0:T(8,128)(2,1)S(1)}, bf16[384,256]{1,0:T(8,128)(2,1)S(1)}, u32[]{:S(2)}, u32[]{:S(2)}) collective-permute-start(bf16[384,256]{1,0:T(8,128)(2,1)S(1)} %get-tuple-element.43), channel_id=1, source_target_pairs={{0,4},{4,0},{8,12},{12,8},{1,5},{5,1},{9,13},{13,9},{2,6},{6,2},{1... | collective-permute-start | bytes 589832 | tf_op jit(solution)/shard_map/ppermute | solution.py:341
  19.7 2.6 %collective-permute-start.2 = (bf16[384,256]{1,0:T(8,128)(2,1)S(1)}, bf16[384,256]{1,0:T(8,128)(2,1)S(1)}, u32[]{:S(2)}, u32[]{:S(2)}) collective-permute-start(bf16[384,256]{1,0:T(8,128)(2,1)S(1)} %get-tuple-element.44), channel_id=1, source_target_pairs={{0,12},{4,8},{8,4},{12,0},{1,13},{5,9},{9,5},{13,1},{2,14},{6,10},... | collective-permute-start | bytes 589832 | tf_op jit(solution)/shard_map/ppermute | solution.py:341
  22.3 0.0 collective-permute-start.3
  22.3 0.2 copy.10.target_ref
  22.4 0.0 copy-start
  22.5 8.0 %prepare.1 = (bf16[2,768,512]{2,1,0:T(8,128)(2,1)S(1)}, bf16[2,768,512]{2,1,0:T(8,128)(2,1)S(1)}, bf16[1536,1536]{1,0:T(8,128)(2,1)S(1)}) custom-call(bf16[3072,768]{1,0:T(8,128)(2,1)} %bitcast.24, bf16[768,512]{1,0:T(8,128)(2,1)} %bitcast.21, bf16[1536,1536]{1,0:T(8,128)(2,1)} %bitcast.25, bf16[12,128,128]{2,1,0:T(8,128)(2,1)} %bitcast.26), custom_call_target="tpu_custom_call" | custom-call | flops 30000001024 | bytes 1000000 | tf_op jit(solution)/shard_map/prepare/pallas_call | solution.py:183
  30.4 0.0 copy-done
  30.4 1.3 %unpack_matrix.1 = (bf16[768,1536]{1,0:T(8,128)(2,1)S(1)}, f32[768,512]{1,0:T(8,128)S(1)}) custom-call(s32[4]{0:T(128)S(1)} %add_multiply_fusion.off_ref, s32[768,1]{1,0:T(8,128)S(1)} %copy.10.target_ref, f32[768,1]{1,0:T(8,128)S(1)} %copy.11.part_ref, f32[1,512]{1,0:T(1,128)S(1)} %bitcast.18), custom_call_target="tpu_custom_call" | custom-call | flops 30000001024 | bytes 1000000 | tf_op jit(solution)/shard_map/unpack_matrix/pallas_call | solution.py:122
  31.8 0.0 collective-permute-done.5.refs_1_
  31.8 1.9 %collective-permute-start.4 = (bf16[384,256]{1,0:T(8,128)(2,1)S(1)}, bf16[384,256]{1,0:T(8,128)(2,1)S(1)}, u32[]{:S(2)}, u32[]{:S(2)}) collective-permute-start(bf16[384,256]{1,0:T(8,128)(2,1)S(1)} %get-tuple-element.46), channel_id=1, source_target_pairs={{0,4},{4,0},{8,12},{12,8},{1,5},{5,1},{9,13},{13,9},{2,6},{6,2},{1... | collective-permute-start | bytes 589832 | tf_op jit(solution)/shard_map/ppermute | solution.py:341
  33.7 0.0 collective-permute-done.6.refs_2_
  33.7 0.0 collective-permute-start.1
  33.7 0.0 collective-permute-done.7.refs_3_
  33.7 1.4 %apply_cycle.2 = (bf16[384,256]{1,0:T(8,128)(2,1)S(1)}, bf16[384,256]{1,0:T(8,128)(2,1)S(1)}, bf16[384,256]{1,0:T(8,128)(2,1)S(1)}, bf16[384,256]{1,0:T(8,128)(2,1)S(1)}) custom-call(bf16[1536,1536]{1,0:T(8,128)(2,1)S(1)} %get-tuple-element.51.operator_ref, bf16[128,256]{1,0:T(8,128)(2,1)S(1)} %collective-permute-done.refs_0_, ...), custom_call_target="tpu_custom_call" | custom-call | flops 30000001024 | bytes 1000000 | tf_op jit(solution)/shard_map/apply_cycle/pallas_call | solution.py:224
  35.1 1.3 %collective-permute-start.13 = (bf16[384,256]{1,0:T(8,128)(2,1)S(1)}, bf16[384,256]{1,0:T(8,128)(2,1)S(1)}, u32[]{:S(2)}, u32[]{:S(2)}) collective-permute-start(bf16[384,256]{1,0:T(8,128)(2,1)S(1)} %get-tuple-element.56), channel_id=1, source_target_pairs={{0,8},{4,12},{8,0},{12,4},{1,9},{5,13},{9,1},{13,5},{2,10},{6,14},... | collective-permute-start | bytes 589832 | tf_op jit(solution)/shard_map/ppermute | solution.py:341
  36.4 0.7 collective-permute-done.1
  37.1 2.6 %collective-permute-start.14 = (bf16[384,256]{1,0:T(8,128)(2,1)S(1)}, bf16[384,256]{1,0:T(8,128)(2,1)S(1)}, u32[]{:S(2)}, u32[]{:S(2)}) collective-permute-start(bf16[384,256]{1,0:T(8,128)(2,1)S(1)} %get-tuple-element.55), channel_id=1, source_target_pairs={{0,12},{4,8},{8,4},{12,0},{1,13},{5,9},{9,5},{13,1},{2,14},{6,10},... | collective-permute-start | bytes 589832 | tf_op jit(solution)/shard_map/ppermute | solution.py:341
  39.6 0.2 fusion
  39.9 0.0 copy-start.1
  39.9 0.0 collective-permute-done.2.refs_0_
  39.9 1.6 %collective-permute-start.8 = (bf16[768,512]{1,0:T(8,128)(2,1)S(1)}, bf16[768,512]{1,0:T(8,128)(2,1)S(1)}, u32[]{:S(2)}, u32[]{:S(2)}) collective-permute-start(bf16[768,512]{1,0:T(8,128)(2,1)S(1)} %fusion), channel_id=1, source_target_pairs={{0,2},{2,0},{1,3},{3,1},{4,6},{6,4},{5,7},{7,5},{8,10},{10,8},{9,1... | collective-permute-start | bytes 2359304 | tf_op jit(solution)/shard_map/ppermute | solution.py:392
  41.4 7.9 %collective-permute-done.3.refs_1_ = bf16[384,256]{1,0:T(8,128)(2,1)S(1)} collective-permute-done((bf16[384,256]{1,0:T(8,128)(2,1)S(1)}, bf16[384,256]{1,0:T(8,128)(2,1)S(1)}, u32[]{:S(2)}, u32[]{:S(2)}) %collective-permute-start.3) | collective-permute-done | bytes 196640 | tf_op jit(solution)/shard_map/ppermute | solution.py:341
  49.4 0.1 collective-permute-start.12
  49.4 0.0 collective-permute-done.4.refs_2_
  49.4 1.4 %apply_cycle.3 = (bf16[384,256]{1,0:T(8,128)(2,1)S(1)}, bf16[384,256]{1,0:T(8,128)(2,1)S(1)}, bf16[384,256]{1,0:T(8,128)(2,1)S(1)}, bf16[384,256]{1,0:T(8,128)(2,1)S(1)}) custom-call(bf16[1536,1536]{1,0:T(8,128)(2,1)S(1)} %get-tuple-element.51.operator_ref, bf16[384,256]{1,0:T(8,128)(2,1)S(1)} %collective-permute-done.2.refs_0_, ...), custom_call_target="tpu_custom_call" | custom-call | flops 30000001024 | bytes 1000000 | tf_op jit(solution)/shard_map/apply_cycle/pallas_call | solution.py:224
  50.9 3.4 %collective-permute-start.9 = (bf16[384,256]{1,0:T(8,128)(2,1)S(1)}, bf16[384,256]{1,0:T(8,128)(2,1)S(1)}, u32[]{:S(2)}, u32[]{:S(2)}) collective-permute-start(bf16[384,256]{1,0:T(8,128)(2,1)S(1)} %get-tuple-element.69), channel_id=1, source_target_pairs={{0,8},{4,12},{8,0},{12,4},{1,9},{5,13},{9,1},{13,5},{2,10},{6,14},... | collective-permute-start | bytes 589832 | tf_op jit(solution)/shard_map/ppermute | solution.py:341
  54.3 4.9 %collective-permute-done.8 = bf16[768,512]{1,0:T(8,128)(2,1)S(1)} collective-permute-done((bf16[768,512]{1,0:T(8,128)(2,1)S(1)}, bf16[768,512]{1,0:T(8,128)(2,1)S(1)}, u32[]{:S(2)}, u32[]{:S(2)}) %collective-permute-start.8) | collective-permute-done | bytes 786464 | tf_op jit(solution)/shard_map/ppermute | solution.py:392
  59.2 0.0 collective-permute-start.11
  59.3 0.0 collective-permute-done.13.refs_2_
  59.3 1.7 %collective-permute-start.10 = (bf16[384,256]{1,0:T(8,128)(2,1)S(1)}, bf16[384,256]{1,0:T(8,128)(2,1)S(1)}, u32[]{:S(2)}, u32[]{:S(2)}) collective-permute-start(bf16[384,256]{1,0:T(8,128)(2,1)S(1)} %get-tuple-element.70), channel_id=1, source_target_pairs={{0,12},{4,8},{8,4},{12,0},{1,13},{5,9},{9,5},{13,1},{2,14},{6,10},... | collective-permute-start | bytes 589832 | tf_op jit(solution)/shard_map/ppermute | solution.py:341
  60.9 0.0 copy-done.1
  60.9 0.4 bitcast_add_fusion.base_ref
  61.4 0.0 collective-permute-done.14.refs_3_
  61.4 0.0 collective-permute-done.12.refs_1_
  61.4 1.5 %finish.2.refs_1_ = bf16[768,512]{1,0:T(8,128)(2,1)} custom-call(bf16[768,1536]{1,0:T(8,128)(2,1)S(1)} %get-tuple-element.42.pick_ref, f32[768,512]{1,0:T(8,128)S(1)} %bitcast_add_fusion.base_ref, f32[768,512]{1,0:T(8,128)S(1)} %get-tuple-element.71.inverse_ref, bf16[384,256]{1,0:T(8,128)(2,1)S(1)} %get-tuple-element.60.refs_0_, ...), custom_call_target="tpu_custom_call" | custom-call | tf_op jit(solution)/shard_map/finish/pallas_call | solution.py:300
  62.9 7.6 %collective-permute-done.9.refs_1_ = bf16[384,256]{1,0:T(8,128)(2,1)S(1)} collective-permute-done((bf16[384,256]{1,0:T(8,128)(2,1)S(1)}, bf16[384,256]{1,0:T(8,128)(2,1)S(1)}, u32[]{:S(2)}, u32[]{:S(2)}) %collective-permute-start.9) | collective-permute-done | bytes 196640 | tf_op jit(solution)/shard_map/ppermute | solution.py:341
  70.5 0.0 collective-permute-done.10.refs_2_
  70.5 0.7 partial.1.base_ref
  71.2 2.3 %collective-permute-done.11.refs_0_ = bf16[384,256]{1,0:T(8,128)(2,1)S(1)} collective-permute-done((bf16[384,256]{1,0:T(8,128)(2,1)S(1)}, bf16[384,256]{1,0:T(8,128)(2,1)S(1)}, u32[]{:S(2)}, u32[]{:S(2)}) %collective-permute-start.11) | collective-permute-done | bytes 196640 | tf_op jit(solution)/shard_map/ppermute | solution.py:341
  73.5 1.1 %finish.3 = bf16[768,512]{1,0:T(8,128)(2,1)} custom-call(bf16[768,1536]{1,0:T(8,128)(2,1)S(1)} %get-tuple-element.42.pick_ref, f32[768,256]{1,0:T(8,128)S(1)} %partial.1.base_ref, f32[768,512]{1,0:T(8,128)S(1)} %get-tuple-element.71.inverse_ref, bf16[384,256]{1,0:T(8,128)(2,1)S(1)} %collective-permute-done.11.refs_0_, ...), custom_call_target="tpu_custom_call", output_to_operand_aliasing={{}: (4, {})} | custom-call | tf_op jit(solution)/shard_map/finish/pallas_call | solution.py:300
Async XLA Ops:
  1.5 8.0 %collective-permute-start = (bf16[128,256]{1,0:T(8,128)(2,1)S(1)}, bf16[128,256]{1,0:T(8,128)(2,1)S(1)}, u32[]{:S(2)}, u32[]{:S(2)}) collective-permute-start(bf16[128,256]{1,0:T(8,128)(2,1)S(1)} %get-tuple-element.40), channel_id=1, source_target_pairs={{0,12},{4,8},{8,4},{12,0},{1,13},{5,9},{9,5},{13,1},{2,14},{6,10},... | collective-permute-start | bytes 196616 | tf_op jit(solution)/shard_map/ppermute | solution.py:341
  6.6 27.0 %collective-permute-start.6 = (bf16[384,256]{1,0:T(8,128)(2,1)S(1)}, bf16[384,256]{1,0:T(8,128)(2,1)S(1)}, u32[]{:S(2)}, u32[]{:S(2)}) collective-permute-start(bf16[384,256]{1,0:T(8,128)(2,1)S(1)} %get-tuple-element.54), channel_id=1, source_target_pairs={{0,8},{4,12},{8,0},{12,4},{1,9},{5,13},{9,1},{13,5},{2,10},{6,14},... | collective-permute-start | bytes 589832 | tf_op jit(solution)/shard_map/ppermute | solution.py:341
  6.6 25.1 %collective-permute-start.5 = (bf16[256,256]{1,0:T(8,128)(2,1)S(1)}, bf16[256,256]{1,0:T(8,128)(2,1)S(1)}, u32[]{:S(2)}, u32[]{:S(2)}) collective-permute-start(bf16[256,256]{1,0:T(8,128)(2,1)S(1)} %get-tuple-element.53), channel_id=1, source_target_pairs={{0,12},{4,8},{8,4},{12,0},{1,13},{5,9},{9,5},{13,1},{2,14},{6,10},... | collective-permute-start | bytes 393224 | tf_op jit(solution)/shard_map/ppermute | solution.py:341
  11.8 21.9 %collective-permute-start.7 = (bf16[384,256]{1,0:T(8,128)(2,1)S(1)}, bf16[384,256]{1,0:T(8,128)(2,1)S(1)}, u32[]{:S(2)}, u32[]{:S(2)}) collective-permute-start(bf16[384,256]{1,0:T(8,128)(2,1)S(1)} %get-tuple-element.43), channel_id=1, source_target_pairs={{0,4},{4,0},{8,12},{12,8},{1,5},{5,1},{9,13},{13,9},{2,6},{6,2},{1... | collective-permute-start | bytes 589832 | tf_op jit(solution)/shard_map/ppermute | solution.py:341
  19.7 20.2 %collective-permute-start.2 = (bf16[384,256]{1,0:T(8,128)(2,1)S(1)}, bf16[384,256]{1,0:T(8,128)(2,1)S(1)}, u32[]{:S(2)}, u32[]{:S(2)}) collective-permute-start(bf16[384,256]{1,0:T(8,128)(2,1)S(1)} %get-tuple-element.44), channel_id=1, source_target_pairs={{0,12},{4,8},{8,4},{12,0},{1,13},{5,9},{9,5},{13,1},{2,14},{6,10},... | collective-permute-start | bytes 589832 | tf_op jit(solution)/shard_map/ppermute | solution.py:341
  22.3 27.1 %collective-permute-start.3 = (bf16[384,256]{1,0:T(8,128)(2,1)S(1)}, bf16[384,256]{1,0:T(8,128)(2,1)S(1)}, u32[]{:S(2)}, u32[]{:S(2)}) collective-permute-start(bf16[384,256]{1,0:T(8,128)(2,1)S(1)} %get-tuple-element.45), channel_id=1, source_target_pairs={{0,8},{4,12},{8,0},{12,4},{1,9},{5,13},{9,1},{13,5},{2,10},{6,14},... | collective-permute-start | bytes 589832 | tf_op jit(solution)/shard_map/ppermute | solution.py:341
  22.4 8.0 %copy-start = (f32[512]{0:T(512)S(1)}, f32[512]{0:T(512)}, u32[]{:S(2)}) copy-start(f32[512]{0:T(512)} %param.15) | copy-start | bytes 6148
  31.8 17.7 %collective-permute-start.4 = (bf16[384,256]{1,0:T(8,128)(2,1)S(1)}, bf16[384,256]{1,0:T(8,128)(2,1)S(1)}, u32[]{:S(2)}, u32[]{:S(2)}) collective-permute-start(bf16[384,256]{1,0:T(8,128)(2,1)S(1)} %get-tuple-element.46), channel_id=1, source_target_pairs={{0,4},{4,0},{8,12},{12,8},{1,5},{5,1},{9,13},{13,9},{2,6},{6,2},{1... | collective-permute-start | bytes 589832 | tf_op jit(solution)/shard_map/ppermute | solution.py:341
  33.7 3.4 %collective-permute-start.1 = (bf16[2,768,512]{2,1,0:T(8,128)(2,1)S(1)}, bf16[2,768,512]{2,1,0:T(8,128)(2,1)S(1)}, u32[]{:S(2)}, u32[]{:S(2)}) collective-permute-start(bf16[2,768,512]{2,1,0:T(8,128)(2,1)S(1)} %get-tuple-element.50), channel_id=1, source_target_pairs={{0,1},{1,0},{2,3},{3,2},{4,5},{5,4},{6,7},{7,6},{8,9},{9,8},{10,11... | collective-permute-start | bytes 4718600 | tf_op jit(solution)/shard_map/ppermute | solution.py:372
  35.1 24.1 %collective-permute-start.13 = (bf16[384,256]{1,0:T(8,128)(2,1)S(1)}, bf16[384,256]{1,0:T(8,128)(2,1)S(1)}, u32[]{:S(2)}, u32[]{:S(2)}) collective-permute-start(bf16[384,256]{1,0:T(8,128)(2,1)S(1)} %get-tuple-element.56), channel_id=1, source_target_pairs={{0,8},{4,12},{8,0},{12,4},{1,9},{5,13},{9,1},{13,5},{2,10},{6,14},... | collective-permute-start | bytes 589832 | tf_op jit(solution)/shard_map/ppermute | solution.py:341
  37.1 24.3 %collective-permute-start.14 = (bf16[384,256]{1,0:T(8,128)(2,1)S(1)}, bf16[384,256]{1,0:T(8,128)(2,1)S(1)}, u32[]{:S(2)}, u32[]{:S(2)}) collective-permute-start(bf16[384,256]{1,0:T(8,128)(2,1)S(1)} %get-tuple-element.55), channel_id=1, source_target_pairs={{0,12},{4,8},{8,4},{12,0},{1,13},{5,9},{9,5},{13,1},{2,14},{6,10},... | collective-permute-start | bytes 589832 | tf_op jit(solution)/shard_map/ppermute | solution.py:341
  39.9 21.1 %copy-start.1 = (bf16[1,768,512]{2,1,0:T(8,128)(2,1)S(1)}, bf16[1,768,512]{2,1,0:T(8,128)(2,1)}, u32[]{:S(2)}) copy-start(bf16[1,768,512]{2,1,0:T(8,128)(2,1)} %param.9) | copy-start | bytes 2359300
  39.9 19.4 %collective-permute-start.8 = (bf16[768,512]{1,0:T(8,128)(2,1)S(1)}, bf16[768,512]{1,0:T(8,128)(2,1)S(1)}, u32[]{:S(2)}, u32[]{:S(2)}) collective-permute-start(bf16[768,512]{1,0:T(8,128)(2,1)S(1)} %fusion), channel_id=1, source_target_pairs={{0,2},{2,0},{1,3},{3,1},{4,6},{6,4},{5,7},{7,5},{8,10},{10,8},{9,1... | collective-permute-start | bytes 2359304 | tf_op jit(solution)/shard_map/ppermute | solution.py:392
  49.4 12.0 %collective-permute-start.12 = (bf16[384,256]{1,0:T(8,128)(2,1)S(1)}, bf16[384,256]{1,0:T(8,128)(2,1)S(1)}, u32[]{:S(2)}, u32[]{:S(2)}) collective-permute-start(bf16[384,256]{1,0:T(8,128)(2,1)S(1)} %get-tuple-element.59), channel_id=1, source_target_pairs={{0,4},{4,0},{8,12},{12,8},{1,5},{5,1},{9,13},{13,9},{2,6},{6,2},{1... | collective-permute-start | bytes 589832 | tf_op jit(solution)/shard_map/ppermute | solution.py:341
  50.9 19.6 %collective-permute-start.9 = (bf16[384,256]{1,0:T(8,128)(2,1)S(1)}, bf16[384,256]{1,0:T(8,128)(2,1)S(1)}, u32[]{:S(2)}, u32[]{:S(2)}) collective-permute-start(bf16[384,256]{1,0:T(8,128)(2,1)S(1)} %get-tuple-element.69), channel_id=1, source_target_pairs={{0,8},{4,12},{8,0},{12,4},{1,9},{5,13},{9,1},{13,5},{2,10},{6,14},... | collective-permute-start | bytes 589832 | tf_op jit(solution)/shard_map/ppermute | solution.py:341
  59.2 14.2 %collective-permute-start.11 = (bf16[384,256]{1,0:T(8,128)(2,1)S(1)}, bf16[384,256]{1,0:T(8,128)(2,1)S(1)}, u32[]{:S(2)}, u32[]{:S(2)}) collective-permute-start(bf16[384,256]{1,0:T(8,128)(2,1)S(1)} %get-tuple-element.72), channel_id=1, source_target_pairs={{0,4},{4,0},{8,12},{12,8},{1,5},{5,1},{9,13},{13,9},{2,6},{6,2},{1... | collective-permute-start | bytes 589832 | tf_op jit(solution)/shard_map/ppermute | solution.py:341
  59.3 11.3 %collective-permute-start.10 = (bf16[384,256]{1,0:T(8,128)(2,1)S(1)}, bf16[384,256]{1,0:T(8,128)(2,1)S(1)}, u32[]{:S(2)}, u32[]{:S(2)}) collective-permute-start(bf16[384,256]{1,0:T(8,128)(2,1)S(1)} %get-tuple-element.70), channel_id=1, source_target_pairs={{0,12},{4,8},{8,4},{12,0},{1,13},{5,9},{9,5},{13,1},{2,14},{6,10},... | collective-permute-start | bytes 589832 | tf_op jit(solution)/shard_map/ppermute | solution.py:341

commit v22 on v19

--- a/solution.py
+++ b/solution.py
@@ -273,7 +273,7 @@
 
 def finish(half, pick, base, inverse, arrays, earlier):
     rows, holes = inverse.shape
-    tiles, width = 3, holes // HALVES
+    tiles, width = 2, holes // HALVES
     block_rows = arrays[0].shape[0]
     places = list(range(len(arrays)))
     if earlier is not None and len(arrays) > 1:

time: 74.6 us -> 74.7 us (level)
  no operation moved by 1% of the time
where the time goes in v22:
time: 74.7 us; the launch traced here: 74.4 us
  starting transfers between devices  30.2 us (40%)
  waiting for transfers between devices  23 us (31%)
  Pallas kernels  19.3 us (26%)
  local copies, waits for them, and re-layouts  1.05 us (1%)
    ppermute x13, starting transfers between devices, exchange(): lax.ppermute(block, 'chan', [(i, i ^ k) for i in range(chan_count)])  28.7 us
    ppermute x13, waiting for transfers between devices, exchange(): lax.ppermute(block, 'chan', [(i, i ^ k) for i in range(chan_count)])  18.1 us
    pallas_call x1, Pallas kernels, prepare(): pl.pallas_call(functools.partial(prepare_kernel, sub_count), out_shape=[j...  7.97 us
    ppermute x1, waiting for transfers between devices, body(): crossed.append(lax.ppermute(term, 'lad', pairs))  4.6 us
    pallas_call x2, Pallas kernels, pack(): pl.pallas_call(functools.partial(pack_kernel, plan, given), out_shape=ext...  3.76 us
    pallas_call x2, Pallas kernels, apply_cycle(): pl.pallas_call(functools.partial(cycle_kernel, half, plan, places), out_s...  2.88 us
    pallas_call x2, Pallas kernels, finish(): pl.pallas_call(functools.partial(finish_kernel, half * width, tuple(place...  2.66 us
    ppermute x1, starting transfers between devices, body(): crossed.append(lax.ppermute(term, 'lad', pairs))  1.56 us
  transfers between devices with their start and end apart: 15, of which 5 were waited for; matrix products, arithmetic and copies ran while one was open for 2% of the time, Pallas kernels for 22%

profile of v22, /device:TPU:0, one launch (start us, length us, event | category | flops | bytes accessed | tf_op | source)
XLA Modules:
  0.0 74.4 jit_solution(7499812871739562556)
XLA Ops:
  0.0 1.7 %pack_first.1 = (s32[1,768]{1,0:T(1,128)S(1)}, bf16[128,256]{1,0:T(8,128)(2,1)S(1)}, bf16[256,256]{1,0:T(8,128)(2,1)S(1)}, bf16[384,256]{1,0:T(8,128)(2,1)S(1)}, bf16[384,256]{1,0:T(8,128)(2,1)S(1)}) custom-call(s32[1,768]{1,0:T(1,128)} %bitcast.22, bf16[768,512]{1,0:T(8,128)(2,1)} %bitcast.19), custom_call_target="tpu_custom_call" | custom-call | tf_op jit(solution)/shard_map/pack_first/pallas_call | solution.py:94
  1.7 5.1 %collective-permute-start = (bf16[128,256]{1,0:T(8,128)(2,1)S(1)}, bf16[128,256]{1,0:T(8,128)(2,1)S(1)}, u32[]{:S(2)}, u32[]{:S(2)}) collective-permute-start(bf16[128,256]{1,0:T(8,128)(2,1)S(1)} %get-tuple-element.40), channel_id=1, source_target_pairs={{0,12},{4,8},{8,4},{12,0},{1,13},{5,9},{9,5},{13,1},{2,14},{6,10},... | collective-permute-start | bytes 196616 | tf_op jit(solution)/shard_map/ppermute | solution.py:341
  6.8 0.0 collective-permute-start.6
  6.8 0.6 collective-permute-start.7
  7.4 3.7 %collective-permute-start.5 = (bf16[256,256]{1,0:T(8,128)(2,1)S(1)}, bf16[256,256]{1,0:T(8,128)(2,1)S(1)}, u32[]{:S(2)}, u32[]{:S(2)}) collective-permute-start(bf16[256,256]{1,0:T(8,128)(2,1)S(1)} %get-tuple-element.52), channel_id=1, source_target_pairs={{0,12},{4,8},{8,4},{12,0},{1,13},{5,9},{9,5},{13,1},{2,14},{6,10},... | collective-permute-start | bytes 393224 | tf_op jit(solution)/shard_map/ppermute | solution.py:341
  11.2 0.9 %copy.11.part_ref = f32[768,1]{1,0:T(8,128)S(1)} copy(f32[768,1]{0,1:T(1,128)} %bitcast.23) | data formatting | bytes 6144 | tf_op jit(solution)/shard_map/reshape;squeeze | solution.py:362
  12.1 0.1 add_multiply_fusion.off_ref
  12.1 0.0 collective-permute-done.refs_0_
  12.1 2.1 %pack_rest.1 = (bf16[384,256]{1,0:T(8,128)(2,1)S(1)}, bf16[384,256]{1,0:T(8,128)(2,1)S(1)}, bf16[384,256]{1,0:T(8,128)(2,1)S(1)}, bf16[384,512]{1,0:T(8,128)(2,1)S(1)}) custom-call(s32[1,768]{1,0:T(1,128)S(1)} %get-tuple-element.41.route_in, bf16[768,512]{1,0:T(8,128)(2,1)} %bitcast.20), custom_call_target="tpu_custom_call" | custom-call | tf_op jit(solution)/shard_map/pack_rest/pallas_call | solution.py:94
  14.2 1.5 %collective-permute-start.2 = (bf16[384,256]{1,0:T(8,128)(2,1)S(1)}, bf16[384,256]{1,0:T(8,128)(2,1)S(1)}, u32[]{:S(2)}, u32[]{:S(2)}) collective-permute-start(bf16[384,256]{1,0:T(8,128)(2,1)S(1)} %get-tuple-element.43), channel_id=1, source_target_pairs={{0,12},{4,8},{8,4},{12,0},{1,13},{5,9},{9,5},{13,1},{2,14},{6,10},... | collective-permute-start | bytes 589832 | tf_op jit(solution)/shard_map/ppermute | solution.py:341
  15.8 2.5 %collective-permute-start.3 = (bf16[384,256]{1,0:T(8,128)(2,1)S(1)}, bf16[384,256]{1,0:T(8,128)(2,1)S(1)}, u32[]{:S(2)}, u32[]{:S(2)}) collective-permute-start(bf16[384,256]{1,0:T(8,128)(2,1)S(1)} %get-tuple-element.44), channel_id=1, source_target_pairs={{0,8},{4,12},{8,0},{12,4},{1,9},{5,13},{9,1},{13,5},{2,10},{6,14},... | collective-permute-start | bytes 589832 | tf_op jit(solution)/shard_map/ppermute | solution.py:341
  18.3 0.2 copy.10.target_ref
  18.5 0.0 copy-start
  18.5 8.0 %prepare.1 = (bf16[2,768,512]{2,1,0:T(8,128)(2,1)S(1)}, bf16[2,768,512]{2,1,0:T(8,128)(2,1)S(1)}, bf16[1536,1536]{1,0:T(8,128)(2,1)S(1)}) custom-call(bf16[3072,768]{1,0:T(8,128)(2,1)} %bitcast.24, bf16[768,512]{1,0:T(8,128)(2,1)} %bitcast.21, bf16[1536,1536]{1,0:T(8,128)(2,1)} %bitcast.25, bf16[12,128,128]{2,1,0:T(8,128)(2,1)} %bitcast.26), custom_call_target="tpu_custom_call" | custom-call | flops 30000001024 | bytes 1000000 | tf_op jit(solution)/shard_map/prepare/pallas_call | solution.py:183
  26.4 0.0 copy-done
  26.5 1.3 %unpack_matrix.1 = (bf16[768,1536]{1,0:T(8,128)(2,1)S(1)}, f32[768,512]{1,0:T(8,128)S(1)}) custom-call(s32[4]{0:T(128)S(1)} %add_multiply_fusion.off_ref, s32[768,1]{1,0:T(8,128)S(1)} %copy.10.target_ref, f32[768,1]{1,0:T(8,128)S(1)} %copy.11.part_ref, f32[1,512]{1,0:T(1,128)S(1)} %bitcast.18), custom_call_target="tpu_custom_call" | custom-call | flops 30000001024 | bytes 1000000 | tf_op jit(solution)/shard_map/unpack_matrix/pallas_call | solution.py:122
  27.8 0.0 collective-permute-done.5.refs_1_
  27.8 5.3 %collective-permute-start.4 = (bf16[384,256]{1,0:T(8,128)(2,1)S(1)}, bf16[384,256]{1,0:T(8,128)(2,1)S(1)}, u32[]{:S(2)}, u32[]{:S(2)}) collective-permute-start(bf16[384,256]{1,0:T(8,128)(2,1)S(1)} %get-tuple-element.45), channel_id=1, source_target_pairs={{0,4},{4,0},{8,12},{12,8},{1,5},{5,1},{9,13},{13,9},{2,6},{6,2},{1... | collective-permute-start | bytes 589832 | tf_op jit(solution)/shard_map/ppermute | solution.py:341
  33.1 0.0 collective-permute-done.6.refs_2_
  33.1 0.0 collective-permute-start.1
  33.1 0.0 collective-permute-done.7.refs_3_
  33.1 1.4 %apply_cycle.2 = (bf16[384,256]{1,0:T(8,128)(2,1)S(1)}, bf16[384,256]{1,0:T(8,128)(2,1)S(1)}, bf16[384,256]{1,0:T(8,128)(2,1)S(1)}, bf16[384,256]{1,0:T(8,128)(2,1)S(1)}) custom-call(bf16[1536,1536]{1,0:T(8,128)(2,1)S(1)} %get-tuple-element.50.operator_ref, bf16[128,256]{1,0:T(8,128)(2,1)S(1)} %collective-permute-done.refs_0_, ...), custom_call_target="tpu_custom_call" | custom-call | flops 30000001024 | bytes 1000000 | tf_op jit(solution)/shard_map/apply_cycle/pallas_call | solution.py:224
  34.6 1.6 %collective-permute-start.13 = (bf16[384,256]{1,0:T(8,128)(2,1)S(1)}, bf16[384,256]{1,0:T(8,128)(2,1)S(1)}, u32[]{:S(2)}, u32[]{:S(2)}) collective-permute-start(bf16[384,256]{1,0:T(8,128)(2,1)S(1)} %get-tuple-element.56), channel_id=1, source_target_pairs={{0,8},{4,12},{8,0},{12,4},{1,9},{5,13},{9,1},{13,5},{2,10},{6,14},... | collective-permute-start | bytes 589832 | tf_op jit(solution)/shard_map/ppermute | solution.py:341
  36.2 0.4 collective-permute-done.1
  36.5 3.0 %collective-permute-start.14 = (bf16[384,256]{1,0:T(8,128)(2,1)S(1)}, bf16[384,256]{1,0:T(8,128)(2,1)S(1)}, u32[]{:S(2)}, u32[]{:S(2)}) collective-permute-start(bf16[384,256]{1,0:T(8,128)(2,1)S(1)} %get-tuple-element.55), channel_id=1, source_target_pairs={{0,12},{4,8},{8,4},{12,0},{1,13},{5,9},{9,5},{13,1},{2,14},{6,10},... | collective-permute-start | bytes 589832 | tf_op jit(solution)/shard_map/ppermute | solution.py:341
  39.5 0.2 fusion
  39.7 0.0 copy-start.1
  39.7 0.0 collective-permute-done.2.refs_0_
  39.7 1.6 %collective-permute-start.8 = (bf16[768,512]{1,0:T(8,128)(2,1)S(1)}, bf16[768,512]{1,0:T(8,128)(2,1)S(1)}, u32[]{:S(2)}, u32[]{:S(2)}) collective-permute-start(bf16[768,512]{1,0:T(8,128)(2,1)S(1)} %fusion), channel_id=1, source_target_pairs={{0,2},{2,0},{1,3},{3,1},{4,6},{6,4},{5,7},{7,5},{8,10},{10,8},{9,1... | collective-permute-start | bytes 2359304 | tf_op jit(solution)/shard_map/ppermute | solution.py:390
  41.3 8.2 %collective-permute-done.3.refs_1_ = bf16[384,256]{1,0:T(8,128)(2,1)S(1)} collective-permute-done((bf16[384,256]{1,0:T(8,128)(2,1)S(1)}, bf16[384,256]{1,0:T(8,128)(2,1)S(1)}, u32[]{:S(2)}, u32[]{:S(2)}) %collective-permute-start.3) | collective-permute-done | bytes 196640 | tf_op jit(solution)/shard_map/ppermute | solution.py:341
  49.5 0.1 collective-permute-start.12
  49.6 0.0 collective-permute-done.4.refs_2_
  49.6 1.4 %apply_cycle.3 = (bf16[384,256]{1,0:T(8,128)(2,1)S(1)}, bf16[384,256]{1,0:T(8,128)(2,1)S(1)}, bf16[384,256]{1,0:T(8,128)(2,1)S(1)}, bf16[384,256]{1,0:T(8,128)(2,1)S(1)}) custom-call(bf16[1536,1536]{1,0:T(8,128)(2,1)S(1)} %get-tuple-element.50.operator_ref, bf16[384,256]{1,0:T(8,128)(2,1)S(1)} %collective-permute-done.2.refs_0_, ...), custom_call_target="tpu_custom_call" | custom-call | flops 30000001024 | bytes 1000000 | tf_op jit(solution)/shard_map/apply_cycle/pallas_call | solution.py:224
  51.1 3.4 %collective-permute-start.9 = (bf16[384,256]{1,0:T(8,128)(2,1)S(1)}, bf16[384,256]{1,0:T(8,128)(2,1)S(1)}, u32[]{:S(2)}, u32[]{:S(2)}) collective-permute-start(bf16[384,256]{1,0:T(8,128)(2,1)S(1)} %get-tuple-element.69), channel_id=1, source_target_pairs={{0,8},{4,12},{8,0},{12,4},{1,9},{5,13},{9,1},{13,5},{2,10},{6,14},... | collective-permute-start | bytes 589832 | tf_op jit(solution)/shard_map/ppermute | solution.py:341
  54.5 4.6 %collective-permute-done.8 = bf16[768,512]{1,0:T(8,128)(2,1)S(1)} collective-permute-done((bf16[768,512]{1,0:T(8,128)(2,1)S(1)}, bf16[768,512]{1,0:T(8,128)(2,1)S(1)}, u32[]{:S(2)}, u32[]{:S(2)}) %collective-permute-start.8) | collective-permute-done | bytes 786464 | tf_op jit(solution)/shard_map/ppermute | solution.py:390
  59.1 0.0 collective-permute-start.11
  59.1 0.0 collective-permute-done.13.refs_2_
  59.1 1.7 %collective-permute-start.10 = (bf16[384,256]{1,0:T(8,128)(2,1)S(1)}, bf16[384,256]{1,0:T(8,128)(2,1)S(1)}, u32[]{:S(2)}, u32[]{:S(2)}) collective-permute-start(bf16[384,256]{1,0:T(8,128)(2,1)S(1)} %get-tuple-element.70), channel_id=1, source_target_pairs={{0,12},{4,8},{8,4},{12,0},{1,13},{5,9},{9,5},{13,1},{2,14},{6,10},... | collective-permute-start | bytes 589832 | tf_op jit(solution)/shard_map/ppermute | solution.py:341
  60.8 0.0 copy-done.1
  60.8 0.4 bitcast_add_fusion.base_ref
  61.2 0.0 collective-permute-done.14.refs_3_
  61.2 0.0 collective-permute-done.12.refs_1_
  61.2 1.5 %finish.2.refs_1_ = bf16[768,512]{1,0:T(8,128)(2,1)} custom-call(bf16[768,1536]{1,0:T(8,128)(2,1)S(1)} %get-tuple-element.42.pick_ref, f32[768,512]{1,0:T(8,128)S(1)} %bitcast_add_fusion.base_ref, f32[768,512]{1,0:T(8,128)S(1)} %get-tuple-element.71.inverse_ref, bf16[384,256]{1,0:T(8,128)(2,1)S(1)} %get-tuple-element.60.refs_0_, ...), custom_call_target="tpu_custom_call" | custom-call | tf_op jit(solution)/shard_map/finish/pallas_call | solution.py:300
  62.8 7.8 %collective-permute-done.9.refs_1_ = bf16[384,256]{1,0:T(8,128)(2,1)S(1)} collective-permute-done((bf16[384,256]{1,0:T(8,128)(2,1)S(1)}, bf16[384,256]{1,0:T(8,128)(2,1)S(1)}, u32[]{:S(2)}, u32[]{:S(2)}) %collective-permute-start.9) | collective-permute-done | bytes 196640 | tf_op jit(solution)/shard_map/ppermute | solution.py:341
  70.6 0.0 collective-permute-done.10.refs_2_
  70.6 0.7 partial.1.base_ref
  71.3 2.1 %collective-permute-done.11.refs_0_ = bf16[384,256]{1,0:T(8,128)(2,1)S(1)} collective-permute-done((bf16[384,256]{1,0:T(8,128)(2,1)S(1)}, bf16[384,256]{1,0:T(8,128)(2,1)S(1)}, u32[]{:S(2)}, u32[]{:S(2)}) %collective-permute-start.11) | collective-permute-done | bytes 196640 | tf_op jit(solution)/shard_map/ppermute | solution.py:341
  73.3 1.1 %finish.3 = bf16[768,512]{1,0:T(8,128)(2,1)} custom-call(bf16[768,1536]{1,0:T(8,128)(2,1)S(1)} %get-tuple-element.42.pick_ref, f32[768,256]{1,0:T(8,128)S(1)} %partial.1.base_ref, f32[768,512]{1,0:T(8,128)S(1)} %get-tuple-element.71.inverse_ref, bf16[384,256]{1,0:T(8,128)(2,1)S(1)} %collective-permute-done.11.refs_0_, ...), custom_call_target="tpu_custom_call", output_to_operand_aliasing={{}: (4, {})} | custom-call | tf_op jit(solution)/shard_map/finish/pallas_call | solution.py:300
Async XLA Ops:
  1.7 10.5 %collective-permute-start = (bf16[128,256]{1,0:T(8,128)(2,1)S(1)}, bf16[128,256]{1,0:T(8,128)(2,1)S(1)}, u32[]{:S(2)}, u32[]{:S(2)}) collective-permute-start(bf16[128,256]{1,0:T(8,128)(2,1)S(1)} %get-tuple-element.40), channel_id=1, source_target_pairs={{0,12},{4,8},{8,4},{12,0},{1,13},{5,9},{9,5},{13,1},{2,14},{6,10},... | collective-permute-start | bytes 196616 | tf_op jit(solution)/shard_map/ppermute | solution.py:341
  6.8 26.3 %collective-permute-start.6 = (bf16[384,256]{1,0:T(8,128)(2,1)S(1)}, bf16[384,256]{1,0:T(8,128)(2,1)S(1)}, u32[]{:S(2)}, u32[]{:S(2)}) collective-permute-start(bf16[384,256]{1,0:T(8,128)(2,1)S(1)} %get-tuple-element.53), channel_id=1, source_target_pairs={{0,8},{4,12},{8,0},{12,4},{1,9},{5,13},{9,1},{13,5},{2,10},{6,14},... | collective-permute-start | bytes 589832 | tf_op jit(solution)/shard_map/ppermute | solution.py:341
  6.8 26.3 %collective-permute-start.7 = (bf16[384,256]{1,0:T(8,128)(2,1)S(1)}, bf16[384,256]{1,0:T(8,128)(2,1)S(1)}, u32[]{:S(2)}, u32[]{:S(2)}) collective-permute-start(bf16[384,256]{1,0:T(8,128)(2,1)S(1)} %get-tuple-element.54), channel_id=1, source_target_pairs={{0,4},{4,0},{8,12},{12,8},{1,5},{5,1},{9,13},{13,9},{2,6},{6,2},{1... | collective-permute-start | bytes 589832 | tf_op jit(solution)/shard_map/ppermute | solution.py:341
  7.4 20.3 %collective-permute-start.5 = (bf16[256,256]{1,0:T(8,128)(2,1)S(1)}, bf16[256,256]{1,0:T(8,128)(2,1)S(1)}, u32[]{:S(2)}, u32[]{:S(2)}) collective-permute-start(bf16[256,256]{1,0:T(8,128)(2,1)S(1)} %get-tuple-element.52), channel_id=1, source_target_pairs={{0,12},{4,8},{8,4},{12,0},{1,13},{5,9},{9,5},{13,1},{2,14},{6,10},... | collective-permute-start | bytes 393224 | tf_op jit(solution)/shard_map/ppermute | solution.py:341
  14.2 25.5 %collective-permute-start.2 = (bf16[384,256]{1,0:T(8,128)(2,1)S(1)}, bf16[384,256]{1,0:T(8,128)(2,1)S(1)}, u32[]{:S(2)}, u32[]{:S(2)}) collective-permute-start(bf16[384,256]{1,0:T(8,128)(2,1)S(1)} %get-tuple-element.43), channel_id=1, source_target_pairs={{0,12},{4,8},{8,4},{12,0},{1,13},{5,9},{9,5},{13,1},{2,14},{6,10},... | collective-permute-start | bytes 589832 | tf_op jit(solution)/shard_map/ppermute | solution.py:341
  15.8 33.7 %collective-permute-start.3 = (bf16[384,256]{1,0:T(8,128)(2,1)S(1)}, bf16[384,256]{1,0:T(8,128)(2,1)S(1)}, u32[]{:S(2)}, u32[]{:S(2)}) collective-permute-start(bf16[384,256]{1,0:T(8,128)(2,1)S(1)} %get-tuple-element.44), channel_id=1, source_target_pairs={{0,8},{4,12},{8,0},{12,4},{1,9},{5,13},{9,1},{13,5},{2,10},{6,14},... | collective-permute-start | bytes 589832 | tf_op jit(solution)/shard_map/ppermute | solution.py:341
  18.5 8.0 %copy-start = (f32[512]{0:T(512)S(1)}, f32[512]{0:T(512)}, u32[]{:S(2)}) copy-start(f32[512]{0:T(512)} %param.15) | copy-start | bytes 6148
  27.8 21.8 %collective-permute-start.4 = (bf16[384,256]{1,0:T(8,128)(2,1)S(1)}, bf16[384,256]{1,0:T(8,128)(2,1)S(1)}, u32[]{:S(2)}, u32[]{:S(2)}) collective-permute-start(bf16[384,256]{1,0:T(8,128)(2,1)S(1)} %get-tuple-element.45), channel_id=1, source_target_pairs={{0,4},{4,0},{8,12},{12,8},{1,5},{5,1},{9,13},{13,9},{2,6},{6,2},{1... | collective-permute-start | bytes 589832 | tf_op jit(solution)/shard_map/ppermute | solution.py:341
  33.1 3.4 %collective-permute-start.1 = (bf16[2,768,512]{2,1,0:T(8,128)(2,1)S(1)}, bf16[2,768,512]{2,1,0:T(8,128)(2,1)S(1)}, u32[]{:S(2)}, u32[]{:S(2)}) collective-permute-start(bf16[2,768,512]{2,1,0:T(8,128)(2,1)S(1)} %get-tuple-element.49), channel_id=1, source_target_pairs={{0,1},{1,0},{2,3},{3,2},{4,5},{5,4},{6,7},{7,6},{8,9},{9,8},{10,11... | collective-permute-start | bytes 4718600 | tf_op jit(solution)/shard_map/ppermute | solution.py:370
  34.6 24.5 %collective-permute-start.13 = (bf16[384,256]{1,0:T(8,128)(2,1)S(1)}, bf16[384,256]{1,0:T(8,128)(2,1)S(1)}, u32[]{:S(2)}, u32[]{:S(2)}) collective-permute-start(bf16[384,256]{1,0:T(8,128)(2,1)S(1)} %get-tuple-element.56), channel_id=1, source_target_pairs={{0,8},{4,12},{8,0},{12,4},{1,9},{5,13},{9,1},{13,5},{2,10},{6,14},... | collective-permute-start | bytes 589832 | tf_op jit(solution)/shard_map/ppermute | solution.py:341
  36.5 24.7 %collective-permute-start.14 = (bf16[384,256]{1,0:T(8,128)(2,1)S(1)}, bf16[384,256]{1,0:T(8,128)(2,1)S(1)}, u32[]{:S(2)}, u32[]{:S(2)}) collective-permute-start(bf16[384,256]{1,0:T(8,128)(2,1)S(1)} %get-tuple-element.55), channel_id=1, source_target_pairs={{0,12},{4,8},{8,4},{12,0},{1,13},{5,9},{9,5},{13,1},{2,14},{6,10},... | collective-permute-start | bytes 589832 | tf_op jit(solution)/shard_map/ppermute | solution.py:341
  39.7 21.1 %copy-start.1 = (bf16[1,768,512]{2,1,0:T(8,128)(2,1)S(1)}, bf16[1,768,512]{2,1,0:T(8,128)(2,1)}, u32[]{:S(2)}) copy-start(bf16[1,768,512]{2,1,0:T(8,128)(2,1)} %param.9) | copy-start | bytes 2359300
  39.7 19.4 %collective-permute-start.8 = (bf16[768,512]{1,0:T(8,128)(2,1)S(1)}, bf16[768,512]{1,0:T(8,128)(2,1)S(1)}, u32[]{:S(2)}, u32[]{:S(2)}) collective-permute-start(bf16[768,512]{1,0:T(8,128)(2,1)S(1)} %fusion), channel_id=1, source_target_pairs={{0,2},{2,0},{1,3},{3,1},{4,6},{6,4},{5,7},{7,5},{8,10},{10,8},{9,1... | collective-permute-start | bytes 2359304 | tf_op jit(solution)/shard_map/ppermute | solution.py:390
  49.5 11.8 %collective-permute-start.12 = (bf16[384,256]{1,0:T(8,128)(2,1)S(1)}, bf16[384,256]{1,0:T(8,128)(2,1)S(1)}, u32[]{:S(2)}, u32[]{:S(2)}) collective-permute-start(bf16[384,256]{1,0:T(8,128)(2,1)S(1)} %get-tuple-element.59), channel_id=1, source_target_pairs={{0,4},{4,0},{8,12},{12,8},{1,5},{5,1},{9,13},{13,9},{2,6},{6,2},{1... | collective-permute-start | bytes 589832 | tf_op jit(solution)/shard_map/ppermute | solution.py:341
  51.1 19.5 %collective-permute-start.9 = (bf16[384,256]{1,0:T(8,128)(2,1)S(1)}, bf16[384,256]{1,0:T(8,128)(2,1)S(1)}, u32[]{:S(2)}, u32[]{:S(2)}) collective-permute-start(bf16[384,256]{1,0:T(8,128)(2,1)S(1)} %get-tuple-element.69), channel_id=1, source_target_pairs={{0,8},{4,12},{8,0},{12,4},{1,9},{5,13},{9,1},{13,5},{2,10},{6,14},... | collective-permute-start | bytes 589832 | tf_op jit(solution)/shard_map/ppermute | solution.py:341
  59.1 14.2 %collective-permute-start.11 = (bf16[384,256]{1,0:T(8,128)(2,1)S(1)}, bf16[384,256]{1,0:T(8,128)(2,1)S(1)}, u32[]{:S(2)}, u32[]{:S(2)}) collective-permute-start(bf16[384,256]{1,0:T(8,128)(2,1)S(1)} %get-tuple-element.72), channel_id=1, source_target_pairs={{0,4},{4,0},{8,12},{12,8},{1,5},{5,1},{9,13},{13,9},{2,6},{6,2},{1... | collective-permute-start | bytes 589832 | tf_op jit(solution)/shard_map/ppermute | solution.py:341
  59.1 11.5 %collective-permute-start.10 = (bf16[384,256]{1,0:T(8,128)(2,1)S(1)}, bf16[384,256]{1,0:T(8,128)(2,1)S(1)}, u32[]{:S(2)}, u32[]{:S(2)}) collective-permute-start(bf16[384,256]{1,0:T(8,128)(2,1)S(1)} %get-tuple-element.70), channel_id=1, source_target_pairs={{0,12},{4,8},{8,4},{12,0},{1,13},{5,9},{9,5},{13,1},{2,14},{6,10},... | collective-permute-start | bytes 589832 | tf_op jit(solution)/shard_map/ppermute | solution.py:341
